TPU v7x, 32 devices: a whole 2x2x4 slice. The times are simulated.
32 devices in a mesh: groups: 1, dp: 32 (over z, y, x, core).
Axes of the slice: x: 2, y: 2, z: 4, core: 2. Of those that a mesh axis runs over, the one named last changes fastest.
Arguments:
- queries: bfloat16 [256, 64, 576], P(('groups', 'dp')), may hold values from -40 to 40
- latent_cache: bfloat16 [256, 96, 576], P(('groups', 'dp')), may hold values from -6 to 6
- new_latent: bfloat16 [256, 576], P(('groups', 'dp')), may hold values from -6 to 6
- parents: int32 [256], P(('groups', 'dp')), may hold values from 0 to 255, as said below
- lengths: int32 [256], P(('groups', 'dp')), may hold values from 2 to 96, as said below
- expert_input: bfloat16 [256, 7168], P(('groups', 'dp')), may hold values from -6 to 6
- routed_experts: int32 [256, 2], P(('groups', 'dp')), may hold values from 0 to 3, all different within a row; in each aligned block of 8 rows (0 to 7, 8 to 15, ...) at most 8 rows name the same one
- route_weights: float32 [256, 2], P(('groups', 'dp')), may hold values from 0.2 to 2
- gate_weight: bfloat16 [32, 7168, 256], P('dp'), may hold values from -0.0625 to 0.0625
- up_weight: bfloat16 [32, 7168, 256], P('dp'), may hold values from -0.0625 to 0.0625
- down_weight: bfloat16 [32, 256, 7168], P('dp'), may hold values from -0.125 to 0.125
Outputs:
- attention: bfloat16 [256, 64, 512], P(('groups', 'dp'))
- expert_output: bfloat16 [256, 7168], P(('groups', 'dp'))
Inputs may be any that keep to these rules, and one draw needn't show every extreme that they name: `parents`: the parent of survivor g (g counted within its beam-search group) lies within 8 slots of g in the same group. `lengths`: some survivor has length exactly 96. `routed_experts`: each row names 2 different experts; among the rows of one device no expert is named more than 8 times, and that many is reached.
All inputs are finite; a program needn't handle non-finite values.
Results may differ from a plain program's by a relative error of at most 0.0058.
Values may be sent and summed in bfloat16 or wider, within the bound.
No kernel may reach another device: no remote copies, remote signals or barrier semaphores. Data moves between devices by JAX's collectives and lax.ppermute only.
A program may use at most 128 MiB of HBM per device.

v0:
```python
import jax
import jax.numpy as jnp
from jax import lax
from jax.sharding import PartitionSpec as P

FF_E = 2048
KV = 512


score_scale = 192.0 ** (-0.5)


def padded_2(value, sides, width):
    for axis, dim in sides:
        peers, length = (lax.axis_size(axis), value.shape[dim])
        up = [(i, (i + 1) % peers) for i in range(peers - 1)]
        down = [(j, i) for i, j in up]
        last = lax.slice_in_dim(value, length - width, length, axis=dim)
        first = lax.slice_in_dim(value, 0, width, axis=dim)
        before = lax.ppermute(last, axis, up)
        after = lax.ppermute(first, axis, down)
        value = jnp.concatenate([before, value, after], axis=dim)
    return value


def pair_slots(route_rows, expert_count, capacity):
    flat_experts = route_rows.reshape(-1)
    onehot = (flat_experts[:, None] == jnp.arange(expert_count, dtype=jnp.int32)[None, :]).astype(
        jnp.int32
    )
    position = jnp.sum((jnp.cumsum(onehot, axis=0) - onehot) * onehot, axis=1)
    return (flat_experts * capacity + position).astype(jnp.int32)


def body(
    queries,
    latent_cache,
    new_latent,
    parents,
    lengths,
    expert_input,
    routed_experts,
    route_weights,
    gate_weight,
    up_weight,
    down_weight,
):
    beam_count = queries.shape[0]
    my_rank = lax.axis_index("dp")
    devices = lax.axis_size("dp")
    positions = jnp.arange(latent_cache.shape[1], dtype=jnp.int32)
    first_slot = (my_rank - 1) * beam_count
    padded = padded_2(latent_cache, (("dp", 0),), beam_count)
    parent_rows = jnp.take(padded, parents - first_slot, axis=0)
    child_cache = jnp.where(
        (positions[None, :] < lengths[:, None] - 1)[:, :, None],
        parent_rows,
        jnp.zeros_like(parent_rows),
    )
    child_cache = jnp.where(
        (positions[None, :] == lengths[:, None] - 1)[:, :, None],
        new_latent[:, None, :],
        child_cache,
    )
    scores = (
        jnp.einsum("bhc,blc->bhl", queries, child_cache, preferred_element_type=jnp.float32)
        * score_scale
    )
    scores = jnp.where((positions[None, :] < lengths[:, None])[:, None, :], scores, -jnp.inf)
    row_max = jnp.max(scores, axis=2, keepdims=True)
    expons = jnp.exp(scores - row_max)
    probs = (expons / jnp.sum(expons, axis=2, keepdims=True)).astype(jnp.bfloat16)
    mixed = jnp.einsum(
        "bhl,blc->bhc", probs, child_cache[:, :, :KV], preferred_element_type=jnp.float32
    )
    attention = mixed.astype(jnp.bfloat16)
    slices = FF_E // gate_weight.shape[2]
    expert_count = devices // slices
    route_count = routed_experts.shape[1]
    capacity = min(beam_count, max(2, 2 * beam_count * route_count // expert_count))
    width = expert_input.shape[1]
    slot_index = pair_slots(routed_experts, expert_count, capacity)
    every_token, every_route = (
        lax.all_gather(expert_input, "dp", axis=0, tiled=True),
        lax.all_gather(routed_experts, "dp", axis=0, tiled=True),
    )
    mine = my_rank // slices
    source_slots = jax.vmap(lambda route_rows: pair_slots(route_rows, expert_count, capacity))(
        every_route.reshape(devices, beam_count, route_count)
    )
    source_slots = source_slots.reshape(devices, beam_count, route_count)
    wanted = mine * capacity + jnp.arange(capacity, dtype=jnp.int32)
    selector = jnp.sum(
        (source_slots[:, None, :, :] == wanted[None, :, None, None]).astype(jnp.int32), axis=3
    ).astype(jnp.bfloat16)
    incoming = jnp.einsum(
        "scb,sbd->scd",
        selector,
        every_token.reshape(devices, beam_count, width),
        preferred_element_type=jnp.float32,
    ).astype(jnp.bfloat16)
    sources, items, _ = incoming.shape
    flat_rows = incoming.reshape(sources * items, width)
    gate_value = jnp.dot(flat_rows, gate_weight[0], preferred_element_type=jnp.float32)
    up_value = jnp.dot(flat_rows, up_weight[0], preferred_element_type=jnp.float32)
    hidden = (jax.nn.silu(gate_value) * up_value).astype(jnp.bfloat16)
    part = jnp.dot(hidden, down_weight[0], preferred_element_type=jnp.float32).astype(jnp.bfloat16)
    partial_value = part.reshape(sources, items, width)
    returned = lax.all_to_all(partial_value, "dp", split_axis=0, concat_axis=0, tiled=True)
    summed = jnp.sum(
        returned.reshape(expert_count, slices, capacity, width), axis=1, dtype=jnp.float32
    ).reshape(expert_count * capacity, width)
    matches = (
        slot_index.reshape(beam_count, route_count)[:, :, None]
        == jnp.arange(expert_count * capacity, dtype=jnp.int32)[None, None, :]
    ).astype(jnp.float32)
    mixing = jnp.sum(route_weights[:, :, None] * matches, axis=1)
    expert_output = jnp.dot(
        mixing, summed, precision=lax.Precision.HIGHEST, preferred_element_type=jnp.float32
    ).astype(jnp.bfloat16)
    return (attention, expert_output)


def solution(mesh):
    in_specs = (
        P(("groups", "dp"), None, None),
        P(("groups", "dp"), None, None),
        P(("groups", "dp"), None),
        P(("groups", "dp")),
        P(("groups", "dp")),
        P(("groups", "dp"), None),
        P(("groups", "dp"), None),
        P(("groups", "dp"), None),
        P("dp", None, None),
        P("dp", None, None),
        P("dp", None, None),
    )
    out_specs = (P(("groups", "dp"), None, None), P(("groups", "dp"), None))
    return jax.shard_map(body, mesh=mesh, in_specs=in_specs, out_specs=out_specs, check_vma=False)
```

profile of v0, /device:TPU:16, one launch (start us, length us, event | category | flops | bytes accessed | tf_op | source)
XLA Modules:
  0.0 205.2 jit_solution(8154991089582339432)
XLA Ops:
  7.2 0.0 copy-start
  7.2 0.0 all-gather.3.cloned.1.call-start
  7.2 0.7 all-gather.3.cloned.1.call-update
  7.9 31.7 %all-gather = s32[32,8,2]{1,2,0:T(2,128)S(1)} all-gather(s32[1,8,2]{1,2,0:T(2,128)} %bitcast.43), channel_id=1, replica_groups=mesh['groups'=1,'dp'=32] {'dp'}, dimensions={0}, use_global_device_ids=true | all-gather | bytes 2112 | tf_op jit(solution)/shard_map/all_gather | solution.py:85
  39.6 0.1 copy.40
  39.7 0.1 copy.39
  39.8 0.6 fusion.37
  40.4 0.1 convert_reduce_fusion.1
  40.5 0.1 copy.42
  40.6 30.6 %all-gather.3.cloned.1.call-done = bf16[256,7168]{1,0:T(8,128)(2,1)} async-done(((bf16[8,7168]{1,0:T(8,128)(2,1)}), bf16[256,7168]{1,0:T(8,128)(2,1)}) %all-gather.3.cloned.1.call-update) | async-done | bytes 3670032 | tf_op jit(solution)/shard_map/all_gather | solution.py:84
  71.2 0.0 copy-start.7
  71.2 3.3 %fusion.1 = bf16[256,7168]{1,0:T(8,128)(2,1)S(1)} fusion(bf16[32,8,8]{2,1,0:T(8,128)(2,1)S(1)} %copy.42, bf16[256,7168]{1,0:T(8,128)(2,1)} %all-gather.3.cloned.1.call-done), kind=kOutput, calls=%fused_computation.4 | convolution fusion | flops 31195136 | bytes 7344128 | tf_op jit(solution)/shard_map/scb,sbd->scd/dot_general | solution.py:96
  74.5 0.0 copy-start.1
  74.5 1.8 copy-done.1
  76.3 0.0 copy-done.7
  76.3 1.1 fusion.6
  77.4 10.0 %fusion.2 = bf16[32,8,7168]{2,1,0:T(8,128)(2,1)} fusion(bf16[1,256,7168]{2,1,0:T(8,128)(2,1)} %param.21, bf16[256,7168]{1,0:T(8,128)(2,1)} %copy-done.1, bf16[1,7168,256]{2,1,0:T(8,128)(2,1)} %param.20, f32[256,256]{1,0:T(8,128)S(1)} %fusion.6), kind=kOutput, calls=%fused_computation.5 | convolution fusion | flops 1881276416 | bytes 14942208 | tf_op jit(solution)/shard_map/dot_general | solution.py:107
  87.5 0.0 copy-start.8
  87.5 4.9 %all-to-all-start = ((bf16[32,8,7168]{2,1,0:T(8,128)(2,1)}), bf16[32,8,7168]{2,1,0:T(8,128)(2,1)}, u32[]{:S(2)}, u32[]{:S(2)}) async-start(bf16[32,8,7168]{2,1,0:T(8,128)(2,1)} %fusion.2), calls=%async_computation | async-start | bytes 7340032 | tf_op jit(solution)/shard_map/all_to_all | solution.py:109
  92.4 0.0 copy-done.2
  92.4 2.1 %collective-permute-start = (bf16[8,96,576]{2,1,0:T(8,128)(2,1)S(1)}, bf16[8,96,576]{2,1,0:T(8,128)(2,1)S(1)}, u32[]{:S(2)}, u32[]{:S(2)}) collective-permute-start(bf16[8,96,576]{2,1,0:T(8,128)(2,1)S(1)} %copy-done.2), channel_id=1, source_target_pairs={{0,1},{1,2},{2,3},{3,4},{4,5},{5,6},{6,7},{7,8},{8,9},{9,10},{10,1... | collective-permute-start | bytes 2654216 | tf_op jit(solution)/shard_map/ppermute | solution.py:20
  94.5 5.3 %collective-permute-start.1 = (bf16[8,96,576]{2,1,0:T(8,128)(2,1)S(1)}, bf16[8,96,576]{2,1,0:T(8,128)(2,1)}, u32[]{:S(2)}, u32[]{:S(2)}) collective-permute-start(bf16[8,96,576]{2,1,0:T(8,128)(2,1)S(1)} %copy-done.2), channel_id=1, source_target_pairs={{1,0},{2,1},{3,2},{4,3},{5,4},{6,5},{7,6},{8,7},{9,8},{10,9},{11,1... | collective-permute-start | bytes 2654216 | tf_op jit(solution)/shard_map/ppermute | solution.py:21
  99.8 0.0 copy-done.4
  99.8 0.1 copy.36
  99.9 0.1 eq.73
  100.0 0.1 fusion.33
  100.1 0.2 select_reduce_fusion.1
  100.3 0.1 reduce_sum.60
  100.4 0.1 copy.38
  100.4 0.0 copy-done.6
  100.5 0.0 copy-done.5
  100.5 0.1 select_reduce_fusion
  100.6 0.0 copy-done.8
  100.6 0.1 iota_compare_fusion.6
  100.7 0.1 iota_compare_fusion.5
  100.7 84.9 %collective-permute-done = bf16[8,96,576]{2,1,0:T(8,128)(2,1)S(1)} collective-permute-done((bf16[8,96,576]{2,1,0:T(8,128)(2,1)S(1)}, bf16[8,96,576]{2,1,0:T(8,128)(2,1)S(1)}, u32[]{:S(2)}, u32[]{:S(2)}) %collective-permute-start) | collective-permute-done | bytes 884768 | tf_op jit(solution)/shard_map/ppermute | solution.py:20
  185.7 0.0 collective-permute-done.1
  185.7 3.3 %pad_maximum_fusion = bf16[24,96,576]{2,1,0:T(8,128)(2,1)} fusion(bf16[8,96,576]{2,1,0:T(8,128)(2,1)} %collective-permute-done.1, bf16[8,96,576]{2,1,0:T(8,128)(2,1)S(1)} %copy-done.2, bf16[8,96,576]{2,1,0:T(8,128)(2,1)S(1)} %collective-permute-done), kind=kLoop, calls=%fused_computation.14 | loop fusion | flops 2654208 | bytes 5308416 | tf_op jit(solution)/shard_map/concatenate | solution.py:22
  189.0 2.6 %gather_fusion = bf16[8,96,576]{2,1,0:T(8,128)(2,1)S(1)} fusion(bf16[24,96,576]{2,1,0:T(8,128)(2,1)} %pad_maximum_fusion, s32[1024]{0:T(1024)S(1)} %pad_clamp_fusion), kind=kCustom, calls=%fused_computation | custom fusion | bytes 1769504 | tf_op jit(solution)/shard_map/jit(_take)/gather | solution.py:54
  191.5 0.0 copy-done.3
  191.6 0.4 select_select_fusion
  191.9 0.0 copy-done
  191.9 0.5 fusion.15
  192.4 0.2 fusion.36
  192.7 1.8 convolution_convert_fusion.3
  194.5 0.0 all-to-all-done
  194.5 2.7 %convert_reduce_fusion = f32[4,8,7168]{2,1,0:T(8,128)S(1)} fusion(bf16[32,8,7168]{2,1,0:T(8,128)(2,1)} %all-to-all-done), kind=kLoop, calls=%fused_computation.7 | loop fusion | flops 3440640 | bytes 4587520 | tf_op jit(solution)/shard_map/reduce_sum | solution.py:110
  197.2 1.2 convolution_convert_fusion.2
  (13 shorter events, 0.1 us)
Async XLA Ops:
  7.2 184.8 %copy-start = (bf16[8,64,576]{2,1,0:T(8,128)(2,1)S(1)}, bf16[8,64,576]{2,1,0:T(8,128)(2,1)}, u32[]{:S(2)}) copy-start(bf16[8,64,576]{2,1,0:T(8,128)(2,1)} %param.11) | copy-start | bytes 1769476
  7.2 64.0 %all-gather.3.cloned.1.call-start = ((), (), s32[]{:S(2)}) async-start(), calls=%async_computation.1 | async-start | bytes 3784704 | tf_op jit(solution)/shard_map/all_gather | solution.py:84
  71.2 5.1 %copy-start.7 = (bf16[1,7168,256]{2,1,0:T(8,128)(2,1)S(1)}, bf16[1,7168,256]{2,1,0:T(8,128)(2,1)}, u32[]{:S(2)}) copy-start(bf16[1,7168,256]{2,1,0:T(8,128)(2,1)} %param.19) | copy-start | bytes 11010052
  74.5 1.8 copy-start.1
  87.4 5.0 %copy-start.2 = (bf16[8,96,576]{2,1,0:T(8,128)(2,1)S(1)}, bf16[8,96,576]{2,1,0:T(8,128)(2,1)}, u32[]{:S(2)}) copy-start(bf16[8,96,576]{2,1,0:T(8,128)(2,1)} %param.12) | copy-start | bytes 2654212
  87.4 12.4 %copy-start.4 = (s32[8,2]{0,1:T(2,128)S(1)}, s32[8,2]{0,1:T(2,128)}, u32[]{:S(2)}) copy-start(s32[8,2]{0,1:T(2,128)} %param.17) | copy-start | bytes 196
  87.5 13.0 %copy-start.6 = (s32[8]{0:T(128)S(1)}, s32[8]{0:T(128)}, u32[]{:S(2)}) copy-start(s32[8]{0:T(128)} %param.14) | copy-start | bytes 100
  87.5 13.0 %copy-start.5 = (f32[8,2]{0,1:T(2,128)S(1)}, f32[8,2]{0,1:T(2,128)}, u32[]{:S(2)}) copy-start(f32[8,2]{0,1:T(2,128)} %param.18) | copy-start | bytes 196
  87.5 13.1 %copy-start.8 = (s32[8]{0:T(128)S(1)}, s32[8]{0:T(128)}, u32[]{:S(2)}) copy-start(s32[8]{0:T(128)} %param.15) | copy-start | bytes 100
  87.5 107.0 %all-to-all-start = ((bf16[32,8,7168]{2,1,0:T(8,128)(2,1)}), bf16[32,8,7168]{2,1,0:T(8,128)(2,1)}, u32[]{:S(2)}, u32[]{:S(2)}) async-start(bf16[32,8,7168]{2,1,0:T(8,128)(2,1)} %fusion.2), calls=%async_computation | async-start | bytes 7340032 | tf_op jit(solution)/shard_map/all_to_all | solution.py:109
  92.4 93.2 %collective-permute-start = (bf16[8,96,576]{2,1,0:T(8,128)(2,1)S(1)}, bf16[8,96,576]{2,1,0:T(8,128)(2,1)S(1)}, u32[]{:S(2)}, u32[]{:S(2)}) collective-permute-start(bf16[8,96,576]{2,1,0:T(8,128)(2,1)S(1)} %copy-done.2), channel_id=1, source_target_pairs={{0,1},{1,2},{2,3},{3,4},{4,5},{5,6},{6,7},{7,8},{8,9},{9,10},{10,1... | collective-permute-start | bytes 2654216 | tf_op jit(solution)/shard_map/ppermute | solution.py:20
  94.5 91.2 %collective-permute-start.1 = (bf16[8,96,576]{2,1,0:T(8,128)(2,1)S(1)}, bf16[8,96,576]{2,1,0:T(8,128)(2,1)}, u32[]{:S(2)}, u32[]{:S(2)}) collective-permute-start(bf16[8,96,576]{2,1,0:T(8,128)(2,1)S(1)} %copy-done.2), channel_id=1, source_target_pairs={{1,0},{2,1},{3,2},{4,3},{5,4},{6,5},{7,6},{8,7},{9,8},{10,9},{11,1... | collective-permute-start | bytes 2654216 | tf_op jit(solution)/shard_map/ppermute | solution.py:21
  100.7 90.8 %copy-start.3 = (bf16[8,576]{1,0:T(8,128)(2,1)S(1)}, bf16[8,576]{1,0:T(8,128)(2,1)}, u32[]{:S(2)}) copy-start(bf16[8,576]{1,0:T(8,128)(2,1)} %param.13) | copy-start | bytes 27652
Sparse Core Ops, SparseCore 0:
  10.9 60.2 all-gather.2
where the time goes:
time: 206 us; the launch traced here: 205 us
  waiting for transfers between devices  116 us (56%)
  blocking collectives  31.7 us (15%)
  matrix products  17.9 us (9%)
  between operations  14.2 us (7%)
  starting transfers between devices  12.3 us (6%)
  other arithmetic  7.81 us (4%)
  local copies, waits for them, and re-layouts  5.01 us (2%)
    ppermute x1, waiting for transfers between devices, padded_2(): before = lax.ppermute(last, axis, up)  84.9 us
    all_gather x1, blocking collectives, body(): lax.all_gather(routed_experts, 'dp', axis=0, tiled=True)  31.7 us
    all_gather x1, waiting for transfers between devices, body(): lax.all_gather(expert_input, 'dp', axis=0, tiled=True)  30.6 us
    dot_general x1, matrix products, body(): jnp.dot(hidden, down_weight[0], preferred_element_type=jnp.float32)  10 us
    ppermute x1, starting transfers between devices, padded_2(): after = lax.ppermute(first, axis, down)  5.3 us
    all_to_all x1, starting transfers between devices, body(): lax.all_to_all(partial_value, 'dp', split_axis=0, concat_axis=0, tiled=True)  4.94 us
  transfers between devices with their start and end apart: 4, of which 2 were waited for; matrix products, arithmetic and copies ran while one was open for 5% of the time, Pallas kernels for 0%

commit v1 on v0

v1 whole, which is shorter than its diff:
```python
import jax
import jax.numpy as jnp
from jax import lax
from jax.sharding import PartitionSpec as P

FF_E = 2048
KV = 512


score_scale = 192.0 ** (-0.5)


def padded_2(value, sides, width):
    for axis, dim in sides:
        peers, length = (lax.axis_size(axis), value.shape[dim])
        up = [(i, (i + 1) % peers) for i in range(peers - 1)]
        down = [(j, i) for i, j in up]
        last = lax.slice_in_dim(value, length - width, length, axis=dim)
        first = lax.slice_in_dim(value, 0, width, axis=dim)
        before = lax.ppermute(last, axis, up)
        after = lax.ppermute(first, axis, down)
        value = jnp.concatenate([before, value, after], axis=dim)
    return value


def pair_slots(route_rows, expert_count, capacity):
    flat_experts = route_rows.reshape(-1)
    onehot = (flat_experts[:, None] == jnp.arange(expert_count, dtype=jnp.int32)[None, :]).astype(
        jnp.int32
    )
    position = jnp.sum((jnp.cumsum(onehot, axis=0) - onehot) * onehot, axis=1)
    return (flat_experts * capacity + position).astype(jnp.int32).reshape(route_rows.shape)


def attend(queries, latent_cache, new_latent, parents, lengths):
    beam_count = queries.shape[0]
    my_rank = lax.axis_index("dp")
    positions = jnp.arange(latent_cache.shape[1], dtype=jnp.int32)
    first_slot = (my_rank - 1) * beam_count
    padded = padded_2(latent_cache, (("dp", 0),), beam_count)
    parent_rows = jnp.take(padded, parents - first_slot, axis=0)
    child_cache = jnp.where(
        (positions[None, :] < lengths[:, None] - 1)[:, :, None],
        parent_rows,
        jnp.zeros_like(parent_rows),
    )
    child_cache = jnp.where(
        (positions[None, :] == lengths[:, None] - 1)[:, :, None],
        new_latent[:, None, :],
        child_cache,
    )
    scores = (
        jnp.einsum("bhc,blc->bhl", queries, child_cache, preferred_element_type=jnp.float32)
        * score_scale
    )
    scores = jnp.where((positions[None, :] < lengths[:, None])[:, None, :], scores, -jnp.inf)
    row_max = jnp.max(scores, axis=2, keepdims=True)
    expons = jnp.exp(scores - row_max)
    probs = (expons / jnp.sum(expons, axis=2, keepdims=True)).astype(jnp.bfloat16)
    mixed = jnp.einsum(
        "bhl,blc->bhc", probs, child_cache[:, :, :KV], preferred_element_type=jnp.float32
    )
    return mixed.astype(jnp.bfloat16)


def routed(expert_input, routed_experts, route_weights, gate_weight, up_weight, down_weight):
    beam_count, width = expert_input.shape
    devices = lax.axis_size("dp")
    slices = FF_E // gate_weight.shape[2]
    expert_count = devices // slices
    route_count = routed_experts.shape[1]
    capacity = min(beam_count, max(2, 2 * beam_count * route_count // expert_count))
    planes = [[e * slices + s for s in range(slices)] for e in range(expert_count)]
    columns = [[e * slices + s for e in range(expert_count)] for s in range(slices)]
    slots = (
        pair_slots(routed_experts, expert_count, capacity)
        if capacity < beam_count
        else routed_experts * capacity + jnp.arange(beam_count, dtype=jnp.int32)[:, None]
    )
    matches = (
        slots[:, :, None] == jnp.arange(expert_count * capacity, dtype=jnp.int32)
    ).astype(jnp.float32)
    if capacity < beam_count:
        selector = jnp.sum(matches, axis=1).T.astype(jnp.bfloat16)
        chosen = jnp.dot(selector, expert_input, preferred_element_type=jnp.float32)
        chosen = chosen.astype(jnp.bfloat16).reshape(expert_count, capacity, width)
        column = lax.all_to_all(
            chosen, "dp", split_axis=0, concat_axis=0, axis_index_groups=columns, tiled=True
        ).reshape(expert_count * capacity, width)
    else:
        column = lax.all_gather(
            expert_input, "dp", axis=0, axis_index_groups=columns, tiled=True
        )
    rows = lax.all_gather(column, "dp", axis=0, axis_index_groups=planes, tiled=True)
    gate_value = jnp.dot(rows, gate_weight[0], preferred_element_type=jnp.float32)
    up_value = jnp.dot(rows, up_weight[0], preferred_element_type=jnp.float32)
    hidden = (jax.nn.silu(gate_value) * up_value).astype(jnp.bfloat16)
    part = jnp.dot(hidden, down_weight[0], preferred_element_type=jnp.float32).astype(jnp.bfloat16)
    value = lax.psum_scatter(
        part, "dp", scatter_dimension=0, axis_index_groups=planes, tiled=True
    )
    returned = lax.all_to_all(
        value.reshape(expert_count, capacity, width),
        "dp",
        split_axis=0,
        concat_axis=0,
        axis_index_groups=columns,
        tiled=True,
    ).reshape(expert_count * capacity, width)
    mixing = jnp.sum(route_weights[:, :, None] * matches, axis=1)
    return jnp.dot(
        mixing,
        returned.astype(jnp.float32),
        precision=lax.Precision.HIGHEST,
        preferred_element_type=jnp.float32,
    ).astype(jnp.bfloat16)


def body(
    queries,
    latent_cache,
    new_latent,
    parents,
    lengths,
    expert_input,
    routed_experts,
    route_weights,
    gate_weight,
    up_weight,
    down_weight,
):
    attention = attend(queries, latent_cache, new_latent, parents, lengths)
    expert_output = routed(
        expert_input, routed_experts, route_weights, gate_weight, up_weight, down_weight
    )
    return (attention, expert_output)


def solution(mesh):
    in_specs = (
        P(("groups", "dp"), None, None),
        P(("groups", "dp"), None, None),
        P(("groups", "dp"), None),
        P(("groups", "dp")),
        P(("groups", "dp")),
        P(("groups", "dp"), None),
        P(("groups", "dp"), None),
        P(("groups", "dp"), None),
        P("dp", None, None),
        P("dp", None, None),
        P("dp", None, None),
    )
    out_specs = (P(("groups", "dp"), None, None), P(("groups", "dp"), None))
    return jax.shard_map(body, mesh=mesh, in_specs=in_specs, out_specs=out_specs, check_vma=False)
```

time: 206 us -> 154 us (0.75)
  the two profiles are of different devices: /device:TPU:16 before, /device:TPU:0 now
where the time goes in v1:
time: 154 us; the launch traced here: 153 us
  waiting for transfers between devices  86.5 us (56%)
  blocking collectives  18.7 us (12%)
  matrix products  17.5 us (11%)
  between operations  14.2 us (9%)
  starting transfers between devices  8.18 us (5%)
  other arithmetic  4.1 us (3%)
  local copies, waits for them, and re-layouts  3.99 us (3%)
    reduce_scatter x1, waiting for transfers between devices, routed(): lax.psum_scatter(part, 'dp', scatter_dimension=0, axis_index_groups=plane...  37.9 us
    all_gather x1, waiting for transfers between devices, routed(): lax.all_gather(column, 'dp', axis=0, axis_index_groups=planes, tiled=True)  34.8 us
    all_gather x1, blocking collectives, routed(): lax.all_gather(expert_input, 'dp', axis=0, axis_index_groups=columns, til...  18.7 us
    all_to_all x1, waiting for transfers between devices, routed(): lax.all_to_all(value.reshape(expert_count, capacity, width), 'dp', split_...  10.1 us
    dot_general x1, matrix products, routed(): jnp.dot(hidden, down_weight[0], preferred_element_type=jnp.float32)  10 us
    all_to_all x1, starting transfers between devices, routed(): lax.all_to_all(value.reshape(expert_count, capacity, width), 'dp', split_...  4.6 us
    dot_general x1, matrix products, routed(): jnp.dot(rows, gate_weight[0], preferred_element_type=jnp.float32)  4.26 us
    concatenate x1, other arithmetic, padded_2(): value = jnp.concatenate([before, value, after], axis=dim)  3.26 us
  transfers between devices with their start and end apart: 5, of which 5 were waited for; matrix products, arithmetic and copies ran while one was open for 6% of the time, Pallas kernels for 0%

profile of v1, /device:TPU:0, one launch (start us, length us, event | category | flops | bytes accessed | tf_op | source)
XLA Modules:
  0.0 153.2 jit_solution(3093421447811070320)
XLA Ops:
  7.2 0.0 copy-start
  7.2 0.0 all-gather.2.cloned.1.call-start
  7.2 18.7 %all_gather.6 = bf16[32,7168]{1,0:T(8,128)(2,1)} all-gather(bf16[8,7168]{1,0:T(8,128)(2,1)} %param.16), channel_id=1, replica_groups={{0,8,16,24},{1,9,17,25},{2,10,18,26},{3,11,19,27},{4,12,20,28},{5,13,21..., dimensions={0}, use_global_device_ids=true | all-gather | bytes 573440 | tf_op jit(solution)/shard_map/all_gather | solution.py:91
  25.9 0.0 all-gather.2.cloned.1.call-update
  25.9 0.0 reduce-scatter.2.cloned.1.call-start
  26.0 34.8 %all-gather.2.cloned.1.call-done = bf16[256,7168]{1,0:T(8,128)(2,1)} async-done(((bf16[32,7168]{1,0:T(8,128)(2,1)}), bf16[256,7168]{1,0:T(8,128)(2,1)}) %all-gather.2.cloned.1.call-update) | async-done | bytes 3670032 | tf_op jit(solution)/shard_map/all_gather | solution.py:94
  60.8 4.3 %fusion.4 = f32[256,256]{1,0:T(8,128)S(1)} fusion(bf16[256,7168]{1,0:T(8,128)(2,1)} %all-gather.2.cloned.1.call-done, bf16[1,7168,256]{2,1,0:T(8,128)(2,1)} %param.19), kind=kOutput, calls=%fused_computation.7 | convolution fusion | flops 939524096 | bytes 7602176 | tf_op jit(solution)/shard_map/dot_general | solution.py:95
  65.0 10.0 %convolution_convert_fusion = bf16[256,7168]{1,0:T(8,128)(2,1)} fusion(bf16[1,256,7168]{2,1,0:T(8,128)(2,1)} %param.21, bf16[256,7168]{1,0:T(8,128)(2,1)} %all-gather.2.cloned.1.call-done, bf16[1,7168,256]{2,1,0:T(8,128)(2,1)} %param.20, f32[256,256]{1,0:T(8,128)S(1)} %fusion.4), kind=kOutput, calls=%fused_computation.2 | convolution fusion | flops 1881276416 | bytes 14942208 | tf_op jit(solution)/shard_map/dot_general | solution.py:98
  75.0 0.0 copy-start.1
  75.0 0.0 copy-start.5
  75.0 0.0 copy-start.3
  75.0 0.0 copy-start.4
  75.0 0.0 copy-start.6
  75.1 0.0 reduce-scatter.2.cloned.1.call-update
  75.1 1.2 copy-done.1
  76.2 2.2 %collective-permute-start = (bf16[8,96,576]{2,1,0:T(8,128)(2,1)S(1)}, bf16[8,96,576]{2,1,0:T(8,128)(2,1)S(1)}, u32[]{:S(2)}, u32[]{:S(2)}) collective-permute-start(bf16[8,96,576]{2,1,0:T(8,128)(2,1)S(1)} %copy-done.1), channel_id=1, source_target_pairs={{0,1},{1,2},{2,3},{3,4},{4,5},{5,6},{6,7},{7,8},{8,9},{9,10},{10,1... | collective-permute-start | bytes 2654216 | tf_op jit(solution)/shard_map/ppermute | solution.py:20
  78.4 1.3 collective-permute-start.1
  79.8 0.0 copy-done.5
  79.8 0.0 copy-done.3
  79.8 0.0 copy-done.4
  79.8 0.1 select_reduce_fusion
  79.9 0.0 copy-done.6
  79.9 0.1 iota_compare_fusion.3
  80.0 0.1 iota_compare_fusion.2
  80.1 0.0 copy-start.2
  80.1 0.5 collective-permute-done
  80.6 3.2 %collective-permute-done.1 = bf16[8,96,576]{2,1,0:T(8,128)(2,1)} collective-permute-done((bf16[8,96,576]{2,1,0:T(8,128)(2,1)S(1)}, bf16[8,96,576]{2,1,0:T(8,128)(2,1)}, u32[]{:S(2)}, u32[]{:S(2)}) %collective-permute-start.1) | collective-permute-done | bytes 884768 | tf_op jit(solution)/shard_map/ppermute | solution.py:21
  83.8 3.3 %pad_maximum_fusion = bf16[24,96,576]{2,1,0:T(8,128)(2,1)} fusion(bf16[8,96,576]{2,1,0:T(8,128)(2,1)} %collective-permute-done.1, bf16[8,96,576]{2,1,0:T(8,128)(2,1)S(1)} %copy-done.1, bf16[8,96,576]{2,1,0:T(8,128)(2,1)S(1)} %collective-permute-done), kind=kLoop, calls=%fused_computation.9 | loop fusion | flops 2654208 | bytes 5308416 | tf_op jit(solution)/shard_map/concatenate | solution.py:22
  87.1 2.8 %gather_fusion = bf16[8,96,576]{2,1,0:T(8,128)(2,1)S(1)} fusion(bf16[24,96,576]{2,1,0:T(8,128)(2,1)} %pad_maximum_fusion, s32[1024]{0:T(1024)S(1)} %pad_clamp_fusion), kind=kCustom, calls=%fused_computation | custom fusion | bytes 1769504 | tf_op jit(solution)/shard_map/jit(_take)/gather | solution.py:41
  89.9 37.9 %reduce-scatter.2.cloned.1.call-done = bf16[32,7168]{1,0:T(8,128)(2,1)} async-done(((bf16[256,7168]{1,0:T(8,128)(2,1)}), bf16[32,7168]{1,0:T(8,128)(2,1)}) %reduce-scatter.2.cloned.1.call-update) | async-done | bytes 458768 | tf_op jit(solution)/shard_map/reduce_scatter | solution.py:99
  127.7 4.6 %all-to-all-start = ((bf16[4,8,7168]{2,1,0:T(8,128)(2,1)}), bf16[4,8,7168]{2,1,0:T(8,128)(2,1)S(1)}, u32[]{:S(2)}, u32[]{:S(2)}) async-start(bf16[4,8,7168]{2,1,0:T(8,128)(2,1)} %bitcast.28), calls=%async_computation.1 | async-start | bytes 917504 | tf_op jit(solution)/shard_map/all_to_all | solution.py:102
  132.3 0.0 copy-done.2
  132.3 0.4 select_select_fusion
  132.7 0.0 copy-done
  132.7 0.5 fusion.11
  133.2 0.2 fusion.29
  133.5 1.8 %convolution_convert_fusion.2 = bf16[8,64,512]{2,1,0:T(8,128)(2,1)} fusion(bf16[8,96,576]{2,1,0:T(8,128)(2,1)S(1)} %select_select_fusion, f32[8,64]{1,0:T(8,128)S(1)} %fusion.29, f32[8,64,96]{2,1,0:T(8,128)S(1)} %fusion.11), kind=kOutput, calls=%fused_computation.10 | convolution fusion | flops 50741856 | bytes 1839104 | tf_op jit(solution)/shard_map/bhl,blc->bhc/dot_general | solution.py:60
  135.3 10.1 %all-to-all-done = bf16[4,8,7168]{2,1,0:T(8,128)(2,1)S(1)} async-done(((bf16[4,8,7168]{2,1,0:T(8,128)(2,1)}), bf16[4,8,7168]{2,1,0:T(8,128)(2,1)S(1)}, u32[]{:S(2)}, u32[]{:S(2)}) %all-to-all-start) | async-done | bytes 458784 | tf_op jit(solution)/shard_map/all_to_all | solution.py:102
  145.4 0.9 convolution_convert_fusion.1
  (4 shorter events, 0.0 us)
Async XLA Ops:
  7.2 125.5 %copy-start = (bf16[8,64,576]{2,1,0:T(8,128)(2,1)S(1)}, bf16[8,64,576]{2,1,0:T(8,128)(2,1)}, u32[]{:S(2)}) copy-start(bf16[8,64,576]{2,1,0:T(8,128)(2,1)} %param.11) | copy-start | bytes 1769476
  7.2 53.6 %all-gather.2.cloned.1.call-start = ((), (), s32[]{:S(2)}) async-start(), calls=%async_computation.2 | async-start | bytes 4128768 | tf_op jit(solution)/shard_map/all_gather | solution.py:94
  25.9 101.8 %reduce-scatter.2.cloned.1.call-start = ((), (), s32[]{:S(2)}) async-start(), calls=%async_computation.3 | async-start | bytes 4128768 | tf_op jit(solution)/shard_map/reduce_scatter | solution.py:99
  75.0 1.2 copy-start.1
  75.0 4.7 %copy-start.5 = (s32[8]{0:T(128)S(1)}, s32[8]{0:T(128)}, u32[]{:S(2)}) copy-start(s32[8]{0:T(128)} %param.14) | copy-start | bytes 100
  75.0 4.8 %copy-start.3 = (s32[8,2]{0,1:T(2,128)S(1)}, s32[8,2]{0,1:T(2,128)}, u32[]{:S(2)}) copy-start(s32[8,2]{0,1:T(2,128)} %param.17) | copy-start | bytes 196
  75.0 4.8 %copy-start.4 = (f32[8,2]{0,1:T(2,128)S(1)}, f32[8,2]{0,1:T(2,128)}, u32[]{:S(2)}) copy-start(f32[8,2]{0,1:T(2,128)} %param.18) | copy-start | bytes 196
  75.0 4.9 %copy-start.6 = (s32[8]{0:T(128)S(1)}, s32[8]{0:T(128)}, u32[]{:S(2)}) copy-start(s32[8]{0:T(128)} %param.15) | copy-start | bytes 100
  76.2 4.3 %collective-permute-start = (bf16[8,96,576]{2,1,0:T(8,128)(2,1)S(1)}, bf16[8,96,576]{2,1,0:T(8,128)(2,1)S(1)}, u32[]{:S(2)}, u32[]{:S(2)}) collective-permute-start(bf16[8,96,576]{2,1,0:T(8,128)(2,1)S(1)} %copy-done.1), channel_id=1, source_target_pairs={{0,1},{1,2},{2,3},{3,4},{4,5},{5,6},{6,7},{7,8},{8,9},{9,10},{10,1... | collective-permute-start | bytes 2654216 | tf_op jit(solution)/shard_map/ppermute | solution.py:20
  78.4 5.4 %collective-permute-start.1 = (bf16[8,96,576]{2,1,0:T(8,128)(2,1)S(1)}, bf16[8,96,576]{2,1,0:T(8,128)(2,1)}, u32[]{:S(2)}, u32[]{:S(2)}) collective-permute-start(bf16[8,96,576]{2,1,0:T(8,128)(2,1)S(1)} %copy-done.1), channel_id=1, source_target_pairs={{1,0},{2,1},{3,2},{4,3},{5,4},{6,5},{7,6},{8,7},{9,8},{10,9},{11,1... | collective-permute-start | bytes 2654216 | tf_op jit(solution)/shard_map/ppermute | solution.py:21
  80.1 52.3 %copy-start.2 = (bf16[8,576]{1,0:T(8,128)(2,1)S(1)}, bf16[8,576]{1,0:T(8,128)(2,1)}, u32[]{:S(2)}) copy-start(bf16[8,576]{1,0:T(8,128)(2,1)} %param.13) | copy-start | bytes 27652
  127.7 17.7 %all-to-all-start = ((bf16[4,8,7168]{2,1,0:T(8,128)(2,1)}), bf16[4,8,7168]{2,1,0:T(8,128)(2,1)S(1)}, u32[]{:S(2)}, u32[]{:S(2)}) async-start(bf16[4,8,7168]{2,1,0:T(8,128)(2,1)} %bitcast.28), calls=%async_computation.1 | async-start | bytes 917504 | tf_op jit(solution)/shard_map/all_to_all | solution.py:102
Sparse Core Ops, SparseCore 0:
  26.1 34.6 all-gather.1
  75.2 52.5 reduce-scatter.1

commit v2 on v1

--- a/solution.py
+++ b/solution.py
@@ -63,57 +63,101 @@
     return mixed.astype(jnp.bfloat16)
 
 
+def swapped(value, partner):
+    peers = lax.axis_size("dp")
+    return lax.ppermute(value, "dp", [(i, partner(i)) for i in range(peers)])
+
+
+def experts(rows, gate_weight, up_weight, down_weight):
+    gate_value = jnp.dot(rows, gate_weight[0], preferred_element_type=jnp.float32)
+    up_value = jnp.dot(rows, up_weight[0], preferred_element_type=jnp.float32)
+    hidden = (jax.nn.silu(gate_value) * up_value).astype(jnp.bfloat16)
+    return jnp.dot(hidden, down_weight[0], preferred_element_type=jnp.float32).astype(jnp.bfloat16)
+
+
+def added(values):
+    total = values[0].astype(jnp.float32)
+    for value in values[1:]:
+        total = total + value.astype(jnp.float32)
+    return total
+
+
 def routed(expert_input, routed_experts, route_weights, gate_weight, up_weight, down_weight):
     beam_count, width = expert_input.shape
     devices = lax.axis_size("dp")
     slices = FF_E // gate_weight.shape[2]
     expert_count = devices // slices
+    chips = slices // 2
     route_count = routed_experts.shape[1]
     capacity = min(beam_count, max(2, 2 * beam_count * route_count // expert_count))
-    planes = [[e * slices + s for s in range(slices)] for e in range(expert_count)]
-    columns = [[e * slices + s for e in range(expert_count)] for s in range(slices)]
-    slots = (
-        pair_slots(routed_experts, expert_count, capacity)
-        if capacity < beam_count
-        else routed_experts * capacity + jnp.arange(beam_count, dtype=jnp.int32)[:, None]
-    )
-    matches = (
-        slots[:, :, None] == jnp.arange(expert_count * capacity, dtype=jnp.int32)
-    ).astype(jnp.float32)
-    if capacity < beam_count:
+    dense = capacity == beam_count
+    mine = lax.axis_index("dp") // slices
+
+    turns = jnp.arange(expert_count, dtype=jnp.int32)
+    targets = (mine + turns) % expert_count
+    if dense:
+        slots = routed_experts * capacity + jnp.arange(beam_count, dtype=jnp.int32)[:, None]
+    else:
+        slots = pair_slots(routed_experts, expert_count, capacity)
+    wanted = targets[:, None] * capacity + jnp.arange(capacity, dtype=jnp.int32)
+    matches = (slots[:, :, None] == wanted.reshape(-1)).astype(jnp.float32)
+    mixing = jnp.sum(route_weights[:, :, None] * matches, axis=1)
+    if dense:
+        blocks = [expert_input] * expert_count
+    else:
         selector = jnp.sum(matches, axis=1).T.astype(jnp.bfloat16)
         chosen = jnp.dot(selector, expert_input, preferred_element_type=jnp.float32)
-        chosen = chosen.astype(jnp.bfloat16).reshape(expert_count, capacity, width)
-        column = lax.all_to_all(
-            chosen, "dp", split_axis=0, concat_axis=0, axis_index_groups=columns, tiled=True
-        ).reshape(expert_count * capacity, width)
+        blocks = list(chosen.astype(jnp.bfloat16).reshape(expert_count, capacity, width))
+
+    def ahead(r):
+        return lambda i: (i + r * slices) % devices
+
+    def beside(j):
+        return lambda i: i ^ (2 * j)
+
+    def twin(i):
+        return i ^ 1
+
+    near = [blocks[0]]
+    far = jnp.concatenate([swapped(blocks[r], ahead(r)) for r in range(1, expert_count)])
+    near = jnp.concatenate(near + [swapped(blocks[0], beside(j)) for j in range(1, chips)])
+    near_twin = swapped(near, twin)
+    far = jnp.concatenate([far] + [swapped(far, beside(j)) for j in range(1, chips)])
+    far_twin = swapped(far, twin)
+    near_rows, far_rows = near.shape[0], far.shape[0]
+    rows = jnp.concatenate([near, near_twin, far, far_twin])
+    part = experts(rows, gate_weight, up_weight, down_weight)
+    at = 2 * near_rows
+    near, near_twin = part[:near_rows], part[near_rows:at]
+    far, far_twin = part[at : at + far_rows], part[at + far_rows :]
+
+    def collected(held, twin_rows):
+        held = added([held, swapped(twin_rows, twin)]).astype(jnp.bfloat16)
+        pieces = held.reshape(chips, held.shape[0] // chips, width)
+        return added(
+            [pieces[0]] + [swapped(pieces[j], beside(j)) for j in range(1, chips)]
+        )
+
+    far = collected(far, far_twin).astype(jnp.bfloat16)
+    far = far.reshape(expert_count - 1, capacity, width)
+    values = [swapped(far[r - 1], ahead(-r)) for r in range(1, expert_count)]
+    values = [collected(near, near_twin)] + values
+    if dense:
+        total = sum(
+            jnp.sum(
+                mixing.reshape(beam_count, expert_count, capacity)[:, r], axis=1, keepdims=True
+            )
+            * values[r].astype(jnp.float32)
+            for r in range(expert_count)
+        )
     else:
-        column = lax.all_gather(
-            expert_input, "dp", axis=0, axis_index_groups=columns, tiled=True
+        total = jnp.dot(
+            mixing,
+            jnp.concatenate(values).astype(jnp.float32),
+            precision=lax.Precision.HIGHEST,
+            preferred_element_type=jnp.float32,
         )
-    rows = lax.all_gather(column, "dp", axis=0, axis_index_groups=planes, tiled=True)
-    gate_value = jnp.dot(rows, gate_weight[0], preferred_element_type=jnp.float32)
-    up_value = jnp.dot(rows, up_weight[0], preferred_element_type=jnp.float32)
-    hidden = (jax.nn.silu(gate_value) * up_value).astype(jnp.bfloat16)
-    part = jnp.dot(hidden, down_weight[0], preferred_element_type=jnp.float32).astype(jnp.bfloat16)
-    value = lax.psum_scatter(
-        part, "dp", scatter_dimension=0, axis_index_groups=planes, tiled=True
-    )
-    returned = lax.all_to_all(
-        value.reshape(expert_count, capacity, width),
-        "dp",
-        split_axis=0,
-        concat_axis=0,
-        axis_index_groups=columns,
-        tiled=True,
-    ).reshape(expert_count * capacity, width)
-    mixing = jnp.sum(route_weights[:, :, None] * matches, axis=1)
-    return jnp.dot(
-        mixing,
-        returned.astype(jnp.float32),
-        precision=lax.Precision.HIGHEST,
-        preferred_element_type=jnp.float32,
-    ).astype(jnp.bfloat16)
+    return total.astype(jnp.bfloat16)
 
 
 def body(

time: 154 us -> 119 us (0.77)
  waiting for transfers between devices: 86.5 us -> 44.7 us
  starting transfers between devices: 8.18 us -> 33.1 us
  blocking collectives: 18.7 us -> 0 us
  between operations: 14.2 us -> 0.9 us
  local copies, waits for them, and re-layouts: 3.99 us -> 16.6 us
  other arithmetic: 4.1 us -> 7.04 us
    ppermute x0 -> x22, waiting for transfers between devices: none -> 44.7 us  [swapped(): return lax.ppermute(value, 'dp', [(i, partner(i)) for i in range(peers)])]
    reduce_scatter x1 -> x0, waiting for transfers between devices: 37.9 us -> none  [routed(): lax.psum_scatter(part, 'dp', scatter_dimension=0, axis_index_groups=plane...]
    all_gather x1 -> x0, waiting for transfers between devices: 34.8 us -> none  [routed(): lax.all_gather(column, 'dp', axis=0, axis_index_groups=planes, tiled=True)]
    ppermute x0 -> x22, starting transfers between devices: none -> 30.5 us  [swapped(): return lax.ppermute(value, 'dp', [(i, partner(i)) for i in range(peers)])]
    all_gather x1 -> x0, blocking collectives: 18.7 us -> none  [routed(): lax.all_gather(expert_input, 'dp', axis=0, axis_index_groups=columns, til...]
    all_to_all x1 -> x0, waiting for transfers between devices: 10.1 us -> none  [routed(): lax.all_to_all(value.reshape(expert_count, capacity, width), 'dp', split_...]
    unnamed x14 -> x26, local copies, waits for them, and re-layouts: 1.18 us -> 8.37 us
    all_to_all x1 -> x0, starting transfers between devices: 4.6 us -> none  [routed(): lax.all_to_all(value.reshape(expert_count, capacity, width), 'dp', split_...]
  transfers between devices with their start and end apart: 5 -> 24, of which waited for: 5 -> 7; matrix products, arithmetic and copies ran while one was open for 6% -> 18% of each run, Pallas kernels for 0% -> 0%
where the time goes in v2:
time: 119 us
  waiting for transfers between devices  44.7 us (38%)
  starting transfers between devices  33.1 us (28%)
  matrix products  16.7 us (14%)
  local copies, waits for them, and re-layouts  16.6 us (14%)
  other arithmetic  7.04 us (6%)
    ppermute x22, waiting for transfers between devices, swapped(): return lax.ppermute(value, 'dp', [(i, partner(i)) for i in range(peers)])  44.7 us
    ppermute x22, starting transfers between devices, swapped(): return lax.ppermute(value, 'dp', [(i, partner(i)) for i in range(peers)])  30.5 us
    dot_general x1, matrix products, experts(): jnp.dot(hidden, down_weight[0], preferred_element_type=jnp.float32)  10.1 us
    unnamed x26, local copies, waits for them, and re-layouts  8.37 us
    dot_general x1, matrix products, experts(): up_value = jnp.dot(rows, up_weight[0], preferred_element_type=jnp.float32)  4.26 us
    concatenate x1, other arithmetic, padded_2(): value = jnp.concatenate([before, value, after], axis=dim)  3.31 us
    gather x1, local copies, waits for them, and re-layouts, attend(): parent_rows = jnp.take(padded, parents - first_slot, axis=0)  2.56 us
    concatenate x1, local copies, waits for them, and re-layouts, routed(): rows = jnp.concatenate([near, near_twin, far, far_twin])  2.51 us
  transfers between devices with their start and end apart: 24, of which 7 were waited for; matrix products, arithmetic and copies ran while one was open for 18% of the time, Pallas kernels for 0%

profile of v2, /device:TPU:0, one launch (start us, length us, event | category | flops | bytes accessed | tf_op | source)
XLA Modules:
  0.0 119.0 jit_solution(14430703180579634581)
XLA Ops:
  0.7 3.0 %collective-permute-start.2 = (bf16[8,7168]{1,0:T(8,128)(2,1)}, bf16[8,7168]{1,0:T(8,128)(2,1)S(1)}, u32[]{:S(2)}, u32[]{:S(2)}) collective-permute-start(bf16[8,7168]{1,0:T(8,128)(2,1)} %param.16), channel_id=1, source_target_pairs={{0,2},{1,3},{2,0},{3,1},{4,6},{5,7},{6,4},{7,5},{8,10},{9,11},{10,... | collective-permute-start | bytes 344072 | tf_op jit(solution)/shard_map/ppermute | solution.py:68
  3.7 1.5 %collective-permute-start.3 = (bf16[8,7168]{1,0:T(8,128)(2,1)}, bf16[8,7168]{1,0:T(8,128)(2,1)S(1)}, u32[]{:S(2)}, u32[]{:S(2)}) collective-permute-start(bf16[8,7168]{1,0:T(8,128)(2,1)} %param.16), channel_id=1, source_target_pairs={{0,4},{1,5},{2,6},{3,7},{4,0},{5,1},{6,2},{7,3},{8,12},{9,13},{10,... | collective-permute-start | bytes 344072 | tf_op jit(solution)/shard_map/ppermute | solution.py:68
  5.2 2.0 %collective-permute-start.6 = (bf16[8,7168]{1,0:T(8,128)(2,1)}, bf16[8,7168]{1,0:T(8,128)(2,1)S(1)}, u32[]{:S(2)}, u32[]{:S(2)}) collective-permute-start(bf16[8,7168]{1,0:T(8,128)(2,1)} %param.16), channel_id=1, source_target_pairs={{0,8},{1,9},{2,10},{3,11},{4,12},{5,13},{6,14},{7,15},{8,16},{9,17... | collective-permute-start | bytes 344072 | tf_op jit(solution)/shard_map/ppermute | solution.py:68
  7.3 2.6 %collective-permute-start.7 = (bf16[8,7168]{1,0:T(8,128)(2,1)}, bf16[8,7168]{1,0:T(8,128)(2,1)S(1)}, u32[]{:S(2)}, u32[]{:S(2)}) collective-permute-start(bf16[8,7168]{1,0:T(8,128)(2,1)} %param.16), channel_id=1, source_target_pairs={{0,16},{1,17},{2,18},{3,19},{4,20},{5,21},{6,22},{7,23},{8,24},{9,... | collective-permute-start | bytes 344072 | tf_op jit(solution)/shard_map/ppermute | solution.py:68
  9.9 1.6 %constant_dynamic-update-slice_fusion.20 = bf16[256,7168]{1,0:T(8,128)(2,1)} fusion(bf16[8,7168]{1,0:T(8,128)(2,1)} %param.16), kind=kLoop, calls=%fused_computation.46 | loop fusion | bytes 229376
  11.5 1.4 %collective-permute-start.8 = (bf16[8,7168]{1,0:T(8,128)(2,1)}, bf16[8,7168]{1,0:T(8,128)(2,1)S(1)}, u32[]{:S(2)}, u32[]{:S(2)}) collective-permute-start(bf16[8,7168]{1,0:T(8,128)(2,1)} %param.16), channel_id=1, source_target_pairs={{0,24},{1,25},{2,26},{3,27},{4,28},{5,29},{6,30},{7,31},{8,0},{9,1... | collective-permute-start | bytes 344072 | tf_op jit(solution)/shard_map/ppermute | solution.py:68
  12.9 1.3 %collective-permute-start = (bf16[8,96,576]{2,1,0:T(8,128)(2,1)}, bf16[8,96,576]{2,1,0:T(8,128)(2,1)S(1)}, u32[]{:S(2)}, u32[]{:S(2)}) collective-permute-start(bf16[8,96,576]{2,1,0:T(8,128)(2,1)} %param.12), channel_id=1, source_target_pairs={{0,1},{1,2},{2,3},{3,4},{4,5},{5,6},{6,7},{7,8},{8,9},{9,10},{10,1... | collective-permute-start | bytes 2654216 | tf_op jit(solution)/shard_map/ppermute | solution.py:20
  14.2 0.9 pad_maximum_fusion.1
  15.2 2.2 %collective-permute-start.5 = (bf16[32,7168]{1,0:T(8,128)(2,1)S(1)}, bf16[32,7168]{1,0:T(8,128)(2,1)S(1)}, u32[]{:S(2)}, u32[]{:S(2)}) collective-permute-start(bf16[32,7168]{1,0:T(8,128)(2,1)S(1)} %pad_maximum_fusion.1), channel_id=1, source_target_pairs={{0,1},{1,0},{2,3},{3,2},{4,5},{5,4},{6,7},{7,6},{8,9},{9,8},{10,11... | collective-permute-start | bytes 1376264 | tf_op jit(solution)/shard_map/ppermute | solution.py:68
  17.4 0.7 constant_dynamic-update-slice_fusion.19
  18.1 0.6 constant_dynamic-update-slice_fusion.18
  18.7 0.7 constant_dynamic-update-slice_fusion.17
  19.4 1.3 %collective-permute-start.1 = (bf16[8,96,576]{2,1,0:T(8,128)(2,1)}, bf16[8,96,576]{2,1,0:T(8,128)(2,1)}, u32[]{:S(2)}, u32[]{:S(2)}) collective-permute-start(bf16[8,96,576]{2,1,0:T(8,128)(2,1)} %param.12), channel_id=1, source_target_pairs={{1,0},{2,1},{3,2},{4,3},{5,4},{6,5},{7,6},{8,7},{9,8},{10,9},{11,1... | collective-permute-start | bytes 2654216 | tf_op jit(solution)/shard_map/ppermute | solution.py:21
  20.6 0.8 constant_dynamic-update-slice_fusion.16
  21.5 0.7 constant_dynamic-update-slice_fusion.8
  22.2 0.7 constant_dynamic-update-slice_fusion.7
  22.9 0.7 constant_dynamic-update-slice_fusion.6
  23.6 2.3 %collective-permute-start.9 = (bf16[24,7168]{1,0:T(8,128)(2,1)S(1)}, bf16[24,7168]{1,0:T(8,128)(2,1)S(1)}, u32[]{:S(2)}, u32[]{:S(2)}) collective-permute-start(bf16[24,7168]{1,0:T(8,128)(2,1)S(1)} %get-tuple-element.21), channel_id=1, source_target_pairs={{0,2},{1,3},{2,0},{3,1},{4,6},{5,7},{6,4},{7,5},{8,10},{9,11},{10,... | collective-permute-start | bytes 1032200 | tf_op jit(solution)/shard_map/ppermute | solution.py:68
  26.2 1.5 %collective-permute-start.10 = (bf16[24,7168]{1,0:T(8,128)(2,1)S(1)}, bf16[24,7168]{1,0:T(8,128)(2,1)S(1)}, u32[]{:S(2)}, u32[]{:S(2)}) collective-permute-start(bf16[24,7168]{1,0:T(8,128)(2,1)S(1)} %get-tuple-element.21), channel_id=1, source_target_pairs={{0,4},{1,5},{2,6},{3,7},{4,0},{5,1},{6,2},{7,3},{8,12},{9,13},{10,... | collective-permute-start | bytes 1032200 | tf_op jit(solution)/shard_map/ppermute | solution.py:68
  27.7 0.9 collective-permute-start.11
  28.7 22.4 %collective-permute-done.9 = bf16[24,7168]{1,0:T(8,128)(2,1)S(1)} collective-permute-done((bf16[24,7168]{1,0:T(8,128)(2,1)S(1)}, bf16[24,7168]{1,0:T(8,128)(2,1)S(1)}, u32[]{:S(2)}, u32[]{:S(2)}) %collective-permute-start.9) | collective-permute-done | bytes 344096 | tf_op jit(solution)/shard_map/ppermute | solution.py:68
  51.0 0.9 constant_dynamic-update-slice_fusion.5
  52.0 0.9 constant_dynamic-update-slice_fusion.4
  52.9 0.9 constant_dynamic-update-slice_fusion.3
  54.5 3.3 %pad_maximum_fusion = bf16[24,96,576]{2,1,0:T(8,128)(2,1)} fusion(bf16[8,96,576]{2,1,0:T(8,128)(2,1)} %collective-permute-done.1, bf16[8,96,576]{2,1,0:T(8,128)(2,1)S(1)} %copy-done.2, bf16[8,96,576]{2,1,0:T(8,128)(2,1)S(1)} %collective-permute-done), kind=kLoop, calls=%fused_computation.8 | loop fusion | flops 2654208 | bytes 5308416 | tf_op jit(solution)/shard_map/concatenate | solution.py:22
  57.8 2.6 %gather_fusion = bf16[8,96,576]{2,1,0:T(8,128)(2,1)S(1)} fusion(bf16[24,96,576]{2,1,0:T(8,128)(2,1)} %pad_maximum_fusion, s32[1024]{0:T(1024)S(1)} %pad_clamp_fusion), kind=kCustom, calls=%fused_computation | custom fusion | bytes 1769504 | tf_op jit(solution)/shard_map/jit(_take)/gather | solution.py:41
  60.4 2.5 %constant_dynamic-update-slice_fusion.9 = bf16[256,7168]{1,0:T(8,128)(2,1)} fusion(bf16[256,7168]{1,0:T(8,128)(2,1)} %get-tuple-element.14, bf16[96,7168]{1,0:T(8,128)(2,1)} %collective-permute-done.12), kind=kLoop, calls=%fused_computation.35 | loop fusion | bytes 2752512 | tf_op jit(solution)/shard_map/concatenate | solution.py:128
  62.9 4.3 %fusion.2 = f32[256,256]{1,0:T(8,128)S(1)} fusion(bf16[256,7168]{1,0:T(8,128)(2,1)} %constant_dynamic-update-slice_fusion.9, bf16[1,7168,256]{2,1,0:T(8,128)(2,1)} %param.20), kind=kOutput, calls=%fused_computation.4 | convolution fusion | flops 939524096 | bytes 7602176 | tf_op jit(solution)/shard_map/dot_general | solution.py:73
  67.2 10.1 %convolution_convert_fusion = bf16[256,7168]{1,0:T(8,128)(2,1)} fusion(bf16[1,256,7168]{2,1,0:T(8,128)(2,1)} %param.21, f32[256,256]{1,0:T(8,128)S(1)} %fusion.2, bf16[256,7168]{1,0:T(8,128)(2,1)} %constant_dynamic-update-slice_fusion.9, bf16[1,7168,256]{2,1,0:T(8,128)(2,1)} %param.19), kind=kOutput, calls=%fused_computation.2 | convolution fusion | flops 1881276416 | bytes 14942208 | tf_op jit(solution)/shard_map/dot_general | solution.py:75
  77.3 1.2 %slice.96 = bf16[32,7168]{1,0:T(8,128)(2,1)S(1)} slice(bf16[256,7168]{1,0:T(8,128)(2,1)} %convolution_convert_fusion), slice={[32:64], [0:7168]} | slice | bytes 917504 | tf_op jit(solution)/shard_map/slice | solution.py:131
  78.5 0.6 collective-permute-start.13
  79.1 0.4 select_select_fusion
  79.4 0.5 fusion.8
  80.6 2.9 %collective-permute-done.17 = bf16[96,7168]{1,0:T(8,128)(2,1)S(1)} collective-permute-done((bf16[96,7168]{1,0:T(8,128)(2,1)S(1)}, bf16[96,7168]{1,0:T(8,128)(2,1)S(1)}, u32[]{:S(2)}, u32[]{:S(2)}) %collective-permute-start.17) | collective-permute-done | bytes 1376288 | tf_op jit(solution)/shard_map/ppermute | solution.py:68
  83.5 0.3 add_convert_fusion
  83.9 3.4 %collective-permute-start.18 = (bf16[24,7168]{1,0:T(8,128)(2,1)S(1)}, bf16[24,7168]{1,0:T(8,128)(2,1)S(1)}, u32[]{:S(2)}, u32[]{:S(2)}) collective-permute-start(bf16[24,7168]{1,0:T(8,128)(2,1)S(1)} %get-tuple-element.4), channel_id=1, source_target_pairs={{0,2},{1,3},{2,0},{3,1},{4,6},{5,7},{6,4},{7,5},{8,10},{9,11},{10,... | collective-permute-start | bytes 1032200 | tf_op jit(solution)/shard_map/ppermute | solution.py:68
  87.4 1.5 %collective-permute-start.20 = (bf16[24,7168]{1,0:T(8,128)(2,1)S(1)}, bf16[24,7168]{1,0:T(8,128)(2,1)S(1)}, u32[]{:S(2)}, u32[]{:S(2)}) collective-permute-start(bf16[24,7168]{1,0:T(8,128)(2,1)S(1)} %get-tuple-element.5), channel_id=1, source_target_pairs={{0,6},{1,7},{2,4},{3,5},{4,2},{5,3},{6,0},{7,1},{8,14},{9,15},{10,... | collective-permute-start | bytes 1032200 | tf_op jit(solution)/shard_map/ppermute | solution.py:68
  88.9 2.0 %collective-permute-start.14 = (bf16[8,7168]{1,0:T(8,128)(2,1)S(1)}, bf16[8,7168]{1,0:T(8,128)(2,1)S(1)}, u32[]{:S(2)}, u32[]{:S(2)}) collective-permute-start(bf16[8,7168]{1,0:T(8,128)(2,1)S(1)} %get-tuple-element.7), channel_id=1, source_target_pairs={{0,2},{1,3},{2,0},{3,1},{4,6},{5,7},{6,4},{7,5},{8,10},{9,11},{10,... | collective-permute-start | bytes 344072 | tf_op jit(solution)/shard_map/ppermute | solution.py:68
  90.9 5.3 %collective-permute-done.18 = bf16[24,7168]{1,0:T(8,128)(2,1)S(1)} collective-permute-done((bf16[24,7168]{1,0:T(8,128)(2,1)S(1)}, bf16[24,7168]{1,0:T(8,128)(2,1)S(1)}, u32[]{:S(2)}, u32[]{:S(2)}) %collective-permute-start.18) | collective-permute-done | bytes 344096 | tf_op jit(solution)/shard_map/ppermute | solution.py:68
  96.2 1.4 %collective-permute-start.16 = (bf16[8,7168]{1,0:T(8,128)(2,1)S(1)}, bf16[8,7168]{1,0:T(8,128)(2,1)S(1)}, u32[]{:S(2)}, u32[]{:S(2)}) collective-permute-start(bf16[8,7168]{1,0:T(8,128)(2,1)S(1)} %get-tuple-element.8), channel_id=1, source_target_pairs={{0,6},{1,7},{2,4},{3,5},{4,2},{5,3},{6,0},{7,1},{8,14},{9,15},{10,... | collective-permute-start | bytes 344072 | tf_op jit(solution)/shard_map/ppermute | solution.py:68
  97.6 8.1 %collective-permute-done.19 = bf16[24,7168]{1,0:T(8,128)(2,1)S(1)} collective-permute-done((bf16[24,7168]{1,0:T(8,128)(2,1)S(1)}, bf16[24,7168]{1,0:T(8,128)(2,1)S(1)}, u32[]{:S(2)}, u32[]{:S(2)}) %collective-permute-start.19) | collective-permute-done | bytes 344096 | tf_op jit(solution)/shard_map/ppermute | solution.py:68
  105.9 0.7 fusion.23
  106.5 2.6 %collective-permute-start.21 = (bf16[8,7168]{1,0:T(8,128)(2,1)}, bf16[8,7168]{1,0:T(8,128)(2,1)S(1)}, u32[]{:S(2)}, u32[]{:S(2)}) collective-permute-start(bf16[8,7168]{1,0:T(8,128)(2,1)} %get-tuple-element.10), channel_id=1, source_target_pairs={{0,24},{1,25},{2,26},{3,27},{4,28},{5,29},{6,30},{7,31},{8,0},{9,1... | collective-permute-start | bytes 344072 | tf_op jit(solution)/shard_map/ppermute | solution.py:68
  109.2 1.2 %collective-permute-start.23 = (bf16[8,7168]{1,0:T(8,128)(2,1)S(1)}, bf16[8,7168]{1,0:T(8,128)(2,1)S(1)}, u32[]{:S(2)}, u32[]{:S(2)}) collective-permute-start(bf16[8,7168]{1,0:T(8,128)(2,1)S(1)} %get-tuple-element.11), channel_id=1, source_target_pairs={{0,8},{1,9},{2,10},{3,11},{4,12},{5,13},{6,14},{7,15},{8,16},{9,17... | collective-permute-start | bytes 344072 | tf_op jit(solution)/shard_map/ppermute | solution.py:68
  110.4 1.8 %convolution_convert_fusion.1 = bf16[8,64,512]{2,1,0:T(8,128)(2,1)} fusion(bf16[8,96,576]{2,1,0:T(8,128)(2,1)S(1)} %select_select_fusion, f32[8,64]{1,0:T(8,128)S(1)} %fusion.25, f32[8,64,96]{2,1,0:T(8,128)S(1)} %fusion.8), kind=kOutput, calls=%fused_computation.10 | convolution fusion | flops 50741856 | bytes 1839104 | tf_op jit(solution)/shard_map/bhl,blc->bhc/dot_general | solution.py:60
  112.2 1.2 collective-permute-done.21
  113.4 4.8 %collective-permute-done.22 = bf16[8,7168]{1,0:T(8,128)(2,1)S(1)} collective-permute-done((bf16[8,7168]{1,0:T(8,128)(2,1)S(1)}, bf16[8,7168]{1,0:T(8,128)(2,1)S(1)}, u32[]{:S(2)}, u32[]{:S(2)}) %collective-permute-start.22) | collective-permute-done | bytes 114720 | tf_op jit(solution)/shard_map/ppermute | solution.py:68
  118.2 0.8 add_convert_fusion.3
  (62 shorter events, 2.0 us)
Async XLA Ops:
  0.6 78.8 %copy-start = (bf16[8,64,576]{2,1,0:T(8,128)(2,1)S(1)}, bf16[8,64,576]{2,1,0:T(8,128)(2,1)}, u32[]{:S(2)}) copy-start(bf16[8,64,576]{2,1,0:T(8,128)(2,1)} %param.11) | copy-start | bytes 1769476
  0.6 53.9 %copy-start.2 = (bf16[8,96,576]{2,1,0:T(8,128)(2,1)S(1)}, bf16[8,96,576]{2,1,0:T(8,128)(2,1)}, u32[]{:S(2)}) copy-start(bf16[8,96,576]{2,1,0:T(8,128)(2,1)} %param.12) | copy-start | bytes 2654212
  0.7 25.4 %copy-start.4 = (s32[8,2]{0,1:T(2,128)S(1)}, s32[8,2]{0,1:T(2,128)}, u32[]{:S(2)}) copy-start(s32[8,2]{0,1:T(2,128)} %param.17) | copy-start | bytes 196
  0.7 25.4 %copy-start.5 = (f32[8,2]{0,1:T(2,128)S(1)}, f32[8,2]{0,1:T(2,128)}, u32[]{:S(2)}) copy-start(f32[8,2]{0,1:T(2,128)} %param.18) | copy-start | bytes 196
  0.7 53.2 %copy-start.6 = (s32[8]{0:T(128)S(1)}, s32[8]{0:T(128)}, u32[]{:S(2)}) copy-start(s32[8]{0:T(128)} %param.14) | copy-start | bytes 100
  0.7 53.7 %copy-start.7 = (s32[8]{0:T(128)S(1)}, s32[8]{0:T(128)}, u32[]{:S(2)}) copy-start(s32[8]{0:T(128)} %param.15) | copy-start | bytes 100
  0.7 10.8 %collective-permute-start.2 = (bf16[8,7168]{1,0:T(8,128)(2,1)}, bf16[8,7168]{1,0:T(8,128)(2,1)S(1)}, u32[]{:S(2)}, u32[]{:S(2)}) collective-permute-start(bf16[8,7168]{1,0:T(8,128)(2,1)} %param.16), channel_id=1, source_target_pairs={{0,2},{1,3},{2,0},{3,1},{4,6},{5,7},{6,4},{7,5},{8,10},{9,11},{10,... | collective-permute-start | bytes 344072 | tf_op jit(solution)/shard_map/ppermute | solution.py:68
  3.7 9.2 %collective-permute-start.3 = (bf16[8,7168]{1,0:T(8,128)(2,1)}, bf16[8,7168]{1,0:T(8,128)(2,1)S(1)}, u32[]{:S(2)}, u32[]{:S(2)}) collective-permute-start(bf16[8,7168]{1,0:T(8,128)(2,1)} %param.16), channel_id=1, source_target_pairs={{0,4},{1,5},{2,6},{3,7},{4,0},{5,1},{6,2},{7,3},{8,12},{9,13},{10,... | collective-permute-start | bytes 344072 | tf_op jit(solution)/shard_map/ppermute | solution.py:68
  5.2 9.0 %collective-permute-start.4 = (bf16[8,7168]{1,0:T(8,128)(2,1)}, bf16[8,7168]{1,0:T(8,128)(2,1)S(1)}, u32[]{:S(2)}, u32[]{:S(2)}) collective-permute-start(bf16[8,7168]{1,0:T(8,128)(2,1)} %param.16), channel_id=1, source_target_pairs={{0,6},{1,7},{2,4},{3,5},{4,2},{5,3},{6,0},{7,1},{8,14},{9,15},{10,... | collective-permute-start | bytes 344072 | tf_op jit(solution)/shard_map/ppermute | solution.py:68
  5.2 16.2 %collective-permute-start.6 = (bf16[8,7168]{1,0:T(8,128)(2,1)}, bf16[8,7168]{1,0:T(8,128)(2,1)S(1)}, u32[]{:S(2)}, u32[]{:S(2)}) collective-permute-start(bf16[8,7168]{1,0:T(8,128)(2,1)} %param.16), channel_id=1, source_target_pairs={{0,8},{1,9},{2,10},{3,11},{4,12},{5,13},{6,14},{7,15},{8,16},{9,17... | collective-permute-start | bytes 344072 | tf_op jit(solution)/shard_map/ppermute | solution.py:68
  7.3 14.9 %collective-permute-start.7 = (bf16[8,7168]{1,0:T(8,128)(2,1)}, bf16[8,7168]{1,0:T(8,128)(2,1)S(1)}, u32[]{:S(2)}, u32[]{:S(2)}) collective-permute-start(bf16[8,7168]{1,0:T(8,128)(2,1)} %param.16), channel_id=1, source_target_pairs={{0,16},{1,17},{2,18},{3,19},{4,20},{5,21},{6,22},{7,23},{8,24},{9,... | collective-permute-start | bytes 344072 | tf_op jit(solution)/shard_map/ppermute | solution.py:68
  11.5 11.4 %collective-permute-start.8 = (bf16[8,7168]{1,0:T(8,128)(2,1)}, bf16[8,7168]{1,0:T(8,128)(2,1)S(1)}, u32[]{:S(2)}, u32[]{:S(2)}) collective-permute-start(bf16[8,7168]{1,0:T(8,128)(2,1)} %param.16), channel_id=1, source_target_pairs={{0,24},{1,25},{2,26},{3,27},{4,28},{5,29},{6,30},{7,31},{8,0},{9,1... | collective-permute-start | bytes 344072 | tf_op jit(solution)/shard_map/ppermute | solution.py:68
  12.9 41.7 %collective-permute-start = (bf16[8,96,576]{2,1,0:T(8,128)(2,1)}, bf16[8,96,576]{2,1,0:T(8,128)(2,1)S(1)}, u32[]{:S(2)}, u32[]{:S(2)}) collective-permute-start(bf16[8,96,576]{2,1,0:T(8,128)(2,1)} %param.12), channel_id=1, source_target_pairs={{0,1},{1,2},{2,3},{3,4},{4,5},{5,6},{6,7},{7,8},{8,9},{9,10},{10,1... | collective-permute-start | bytes 2654216 | tf_op jit(solution)/shard_map/ppermute | solution.py:20
  15.2 4.2 %collective-permute-start.5 = (bf16[32,7168]{1,0:T(8,128)(2,1)S(1)}, bf16[32,7168]{1,0:T(8,128)(2,1)S(1)}, u32[]{:S(2)}, u32[]{:S(2)}) collective-permute-start(bf16[32,7168]{1,0:T(8,128)(2,1)S(1)} %pad_maximum_fusion.1), channel_id=1, source_target_pairs={{0,1},{1,0},{2,3},{3,2},{4,5},{5,4},{6,7},{7,6},{8,9},{9,8},{10,11... | collective-permute-start | bytes 1376264 | tf_op jit(solution)/shard_map/ppermute | solution.py:68
  19.4 35.2 %collective-permute-start.1 = (bf16[8,96,576]{2,1,0:T(8,128)(2,1)}, bf16[8,96,576]{2,1,0:T(8,128)(2,1)}, u32[]{:S(2)}, u32[]{:S(2)}) collective-permute-start(bf16[8,96,576]{2,1,0:T(8,128)(2,1)} %param.12), channel_id=1, source_target_pairs={{1,0},{2,1},{3,2},{4,3},{5,4},{6,5},{7,6},{8,7},{9,8},{10,9},{11,1... | collective-permute-start | bytes 2654216 | tf_op jit(solution)/shard_map/ppermute | solution.py:21
  23.6 27.4 %collective-permute-start.9 = (bf16[24,7168]{1,0:T(8,128)(2,1)S(1)}, bf16[24,7168]{1,0:T(8,128)(2,1)S(1)}, u32[]{:S(2)}, u32[]{:S(2)}) collective-permute-start(bf16[24,7168]{1,0:T(8,128)(2,1)S(1)} %get-tuple-element.21), channel_id=1, source_target_pairs={{0,2},{1,3},{2,0},{3,1},{4,6},{5,7},{6,4},{7,5},{8,10},{9,11},{10,... | collective-permute-start | bytes 1032200 | tf_op jit(solution)/shard_map/ppermute | solution.py:68
  26.2 25.8 %collective-permute-start.10 = (bf16[24,7168]{1,0:T(8,128)(2,1)S(1)}, bf16[24,7168]{1,0:T(8,128)(2,1)S(1)}, u32[]{:S(2)}, u32[]{:S(2)}) collective-permute-start(bf16[24,7168]{1,0:T(8,128)(2,1)S(1)} %get-tuple-element.21), channel_id=1, source_target_pairs={{0,4},{1,5},{2,6},{3,7},{4,0},{5,1},{6,2},{7,3},{8,12},{9,13},{10,... | collective-permute-start | bytes 1032200 | tf_op jit(solution)/shard_map/ppermute | solution.py:68
  27.7 25.2 %collective-permute-start.11 = (bf16[24,7168]{1,0:T(8,128)(2,1)S(1)}, bf16[24,7168]{1,0:T(8,128)(2,1)S(1)}, u32[]{:S(2)}, u32[]{:S(2)}) collective-permute-start(bf16[24,7168]{1,0:T(8,128)(2,1)S(1)} %get-tuple-element.21), channel_id=1, source_target_pairs={{0,6},{1,7},{2,4},{3,5},{4,2},{5,3},{6,0},{7,1},{8,14},{9,15},{10,... | collective-permute-start | bytes 1032200 | tf_op jit(solution)/shard_map/ppermute | solution.py:68
  53.8 6.6 %collective-permute-start.12 = (bf16[96,7168]{1,0:T(8,128)(2,1)}, bf16[96,7168]{1,0:T(8,128)(2,1)}, u32[]{:S(2)}, u32[]{:S(2)}) collective-permute-start(bf16[96,7168]{1,0:T(8,128)(2,1)} %get-tuple-element.13), channel_id=1, source_target_pairs={{0,1},{1,0},{2,3},{3,2},{4,5},{5,4},{6,7},{7,6},{8,9},{9,8},{10,11... | collective-permute-start | bytes 4128776 | tf_op jit(solution)/shard_map/ppermute | solution.py:68
  67.2 11.9 %copy-start.3 = (bf16[8,576]{1,0:T(8,128)(2,1)S(1)}, bf16[8,576]{1,0:T(8,128)(2,1)}, u32[]{:S(2)}) copy-start(bf16[8,576]{1,0:T(8,128)(2,1)} %param.13) | copy-start | bytes 27652
  77.3 2.9 %copy-start.1 = (bf16[256,7168]{1,0:T(8,128)(2,1)S(1)}, bf16[256,7168]{1,0:T(8,128)(2,1)}, u32[]{:S(2)}) copy-start(bf16[256,7168]{1,0:T(8,128)(2,1)} %convolution_convert_fusion) | copy-start | bytes 11010052
  78.5 2.0 %collective-permute-start.13 = (bf16[32,7168]{1,0:T(8,128)(2,1)S(1)}, bf16[32,7168]{1,0:T(8,128)(2,1)S(1)}, u32[]{:S(2)}, u32[]{:S(2)}) collective-permute-start(bf16[32,7168]{1,0:T(8,128)(2,1)S(1)} %slice.96), channel_id=1, source_target_pairs={{0,1},{1,0},{2,3},{3,2},{4,5},{5,4},{6,7},{7,6},{8,9},{9,8},{10,11... | collective-permute-start | bytes 1376264 | tf_op jit(solution)/shard_map/ppermute | solution.py:68
  80.3 3.2 %collective-permute-start.17 = (bf16[96,7168]{1,0:T(8,128)(2,1)S(1)}, bf16[96,7168]{1,0:T(8,128)(2,1)S(1)}, u32[]{:S(2)}, u32[]{:S(2)}) collective-permute-start(bf16[96,7168]{1,0:T(8,128)(2,1)S(1)} %slice.103), channel_id=1, source_target_pairs={{0,1},{1,0},{2,3},{3,2},{4,5},{5,4},{6,7},{7,6},{8,9},{9,8},{10,11... | collective-permute-start | bytes 4128776 | tf_op jit(solution)/shard_map/ppermute | solution.py:68
  83.9 12.3 %collective-permute-start.18 = (bf16[24,7168]{1,0:T(8,128)(2,1)S(1)}, bf16[24,7168]{1,0:T(8,128)(2,1)S(1)}, u32[]{:S(2)}, u32[]{:S(2)}) collective-permute-start(bf16[24,7168]{1,0:T(8,128)(2,1)S(1)} %get-tuple-element.4), channel_id=1, source_target_pairs={{0,2},{1,3},{2,0},{3,1},{4,6},{5,7},{6,4},{7,5},{8,10},{9,11},{10,... | collective-permute-start | bytes 1032200 | tf_op jit(solution)/shard_map/ppermute | solution.py:68
  87.4 18.3 %collective-permute-start.19 = (bf16[24,7168]{1,0:T(8,128)(2,1)S(1)}, bf16[24,7168]{1,0:T(8,128)(2,1)S(1)}, u32[]{:S(2)}, u32[]{:S(2)}) collective-permute-start(bf16[24,7168]{1,0:T(8,128)(2,1)S(1)} %get-tuple-element.6), channel_id=1, source_target_pairs={{0,4},{1,5},{2,6},{3,7},{4,0},{5,1},{6,2},{7,3},{8,12},{9,13},{10,... | collective-permute-start | bytes 1032200 | tf_op jit(solution)/shard_map/ppermute | solution.py:68
  87.4 18.3 %collective-permute-start.20 = (bf16[24,7168]{1,0:T(8,128)(2,1)S(1)}, bf16[24,7168]{1,0:T(8,128)(2,1)S(1)}, u32[]{:S(2)}, u32[]{:S(2)}) collective-permute-start(bf16[24,7168]{1,0:T(8,128)(2,1)S(1)} %get-tuple-element.5), channel_id=1, source_target_pairs={{0,6},{1,7},{2,4},{3,5},{4,2},{5,3},{6,0},{7,1},{8,14},{9,15},{10,... | collective-permute-start | bytes 1032200 | tf_op jit(solution)/shard_map/ppermute | solution.py:68
  88.9 20.3 %collective-permute-start.14 = (bf16[8,7168]{1,0:T(8,128)(2,1)S(1)}, bf16[8,7168]{1,0:T(8,128)(2,1)S(1)}, u32[]{:S(2)}, u32[]{:S(2)}) collective-permute-start(bf16[8,7168]{1,0:T(8,128)(2,1)S(1)} %get-tuple-element.7), channel_id=1, source_target_pairs={{0,2},{1,3},{2,0},{3,1},{4,6},{5,7},{6,4},{7,5},{8,10},{9,11},{10,... | collective-permute-start | bytes 344072 | tf_op jit(solution)/shard_map/ppermute | solution.py:68
  90.9 21.3 %collective-permute-start.15 = (bf16[8,7168]{1,0:T(8,128)(2,1)S(1)}, bf16[8,7168]{1,0:T(8,128)(2,1)S(1)}, u32[]{:S(2)}, u32[]{:S(2)}) collective-permute-start(bf16[8,7168]{1,0:T(8,128)(2,1)S(1)} %get-tuple-element.9), channel_id=1, source_target_pairs={{0,4},{1,5},{2,6},{3,7},{4,0},{5,1},{6,2},{7,3},{8,12},{9,13},{10,... | collective-permute-start | bytes 344072 | tf_op jit(solution)/shard_map/ppermute | solution.py:68
  96.2 16.0 %collective-permute-start.16 = (bf16[8,7168]{1,0:T(8,128)(2,1)S(1)}, bf16[8,7168]{1,0:T(8,128)(2,1)S(1)}, u32[]{:S(2)}, u32[]{:S(2)}) collective-permute-start(bf16[8,7168]{1,0:T(8,128)(2,1)S(1)} %get-tuple-element.8), channel_id=1, source_target_pairs={{0,6},{1,7},{2,4},{3,5},{4,2},{5,3},{6,0},{7,1},{8,14},{9,15},{10,... | collective-permute-start | bytes 344072 | tf_op jit(solution)/shard_map/ppermute | solution.py:68
  106.5 6.9 %collective-permute-start.21 = (bf16[8,7168]{1,0:T(8,128)(2,1)}, bf16[8,7168]{1,0:T(8,128)(2,1)S(1)}, u32[]{:S(2)}, u32[]{:S(2)}) collective-permute-start(bf16[8,7168]{1,0:T(8,128)(2,1)} %get-tuple-element.10), channel_id=1, source_target_pairs={{0,24},{1,25},{2,26},{3,27},{4,28},{5,29},{6,30},{7,31},{8,0},{9,1... | collective-permute-start | bytes 344072 | tf_op jit(solution)/shard_map/ppermute | solution.py:68
  109.2 9.0 %collective-permute-start.22 = (bf16[8,7168]{1,0:T(8,128)(2,1)S(1)}, bf16[8,7168]{1,0:T(8,128)(2,1)S(1)}, u32[]{:S(2)}, u32[]{:S(2)}) collective-permute-start(bf16[8,7168]{1,0:T(8,128)(2,1)S(1)} %get-tuple-element.12), channel_id=1, source_target_pairs={{0,16},{1,17},{2,18},{3,19},{4,20},{5,21},{6,22},{7,23},{8,24},{9,... | collective-permute-start | bytes 344072 | tf_op jit(solution)/shard_map/ppermute | solution.py:68
  109.2 9.0 %collective-permute-start.23 = (bf16[8,7168]{1,0:T(8,128)(2,1)S(1)}, bf16[8,7168]{1,0:T(8,128)(2,1)S(1)}, u32[]{:S(2)}, u32[]{:S(2)}) collective-permute-start(bf16[8,7168]{1,0:T(8,128)(2,1)S(1)} %get-tuple-element.11), channel_id=1, source_target_pairs={{0,8},{1,9},{2,10},{3,11},{4,12},{5,13},{6,14},{7,15},{8,16},{9,17... | collective-permute-start | bytes 344072 | tf_op jit(solution)/shard_map/ppermute | solution.py:68

commit v3 on v2

v3 whole, which is shorter than its diff:
```python
import jax
import jax.numpy as jnp
from jax import lax
from jax.experimental import pallas as pl
from jax.experimental.pallas import tpu as pltpu
from jax.sharding import PartitionSpec as P

FF_E = 2048
KV = 512


score_scale = 192.0 ** (-0.5)


def pair_slots(route_rows, expert_count, capacity):
    flat_experts = route_rows.reshape(-1)
    onehot = (flat_experts[:, None] == jnp.arange(expert_count, dtype=jnp.int32)[None, :]).astype(
        jnp.int32
    )
    position = jnp.sum((jnp.cumsum(onehot, axis=0) - onehot) * onehot, axis=1)
    return (flat_experts * capacity + position).astype(jnp.int32).reshape(route_rows.shape)


def attend(queries, before, latent_cache, after, new_latent, parents, lengths):
    beam_count = queries.shape[0]
    my_rank = lax.axis_index("dp")
    positions = jnp.arange(latent_cache.shape[1], dtype=jnp.int32)
    first_slot = (my_rank - 1) * beam_count
    padded = jnp.concatenate([before, latent_cache, after], axis=0)
    parent_rows = jnp.take(padded, parents - first_slot, axis=0)
    child_cache = jnp.where(
        (positions[None, :] < lengths[:, None] - 1)[:, :, None],
        parent_rows,
        jnp.zeros_like(parent_rows),
    )
    child_cache = jnp.where(
        (positions[None, :] == lengths[:, None] - 1)[:, :, None],
        new_latent[:, None, :],
        child_cache,
    )
    scores = (
        jnp.einsum("bhc,blc->bhl", queries, child_cache, preferred_element_type=jnp.float32)
        * score_scale
    )
    scores = jnp.where((positions[None, :] < lengths[:, None])[:, None, :], scores, -jnp.inf)
    row_max = jnp.max(scores, axis=2, keepdims=True)
    expons = jnp.exp(scores - row_max)
    probs = (expons / jnp.sum(expons, axis=2, keepdims=True)).astype(jnp.bfloat16)
    mixed = jnp.einsum(
        "bhl,blc->bhc", probs, child_cache[:, :, :KV], preferred_element_type=jnp.float32
    )
    return mixed.astype(jnp.bfloat16)


def swapped(value, partner):
    peers = lax.axis_size("dp")
    return lax.ppermute(value, "dp", [(i, partner(i)) for i in range(peers)])


def step_width(width):
    return max(w for w in (128, 256, 512, 1024) if width % w == 0)


def expert_kernel(steps, blocks, *refs):
    rows, refs = refs[:blocks], refs[blocks:]
    gate_ref, up_ref, down_ref = refs[:3]
    out_refs, (gate_sum, up_sum, hidden) = refs[3 : 3 + blocks], refs[3 + blocks :]
    height = rows[0].shape[0]
    step = pl.program_id(0)

    @pl.when(step < steps)
    def _():
        value = jnp.concatenate([ref[...] for ref in rows], axis=0)
        gate = jnp.dot(value, gate_ref[0], preferred_element_type=jnp.float32)
        up = jnp.dot(value, up_ref[0], preferred_element_type=jnp.float32)
        first = step == 0
        gate_sum[...] = gate + jnp.where(first, 0.0, gate_sum[...])
        up_sum[...] = up + jnp.where(first, 0.0, up_sum[...])

    @pl.when(step == steps - 1)
    def _():
        gate = gate_sum[...]
        hidden[...] = (gate / (1.0 + jnp.exp(-gate)) * up_sum[...]).astype(hidden.dtype)

    @pl.when(step >= steps)
    def _():
        part = jnp.dot(hidden[...], down_ref[0], preferred_element_type=jnp.float32)
        for i, ref in enumerate(out_refs):
            ref[...] = part[i * height : (i + 1) * height].astype(ref.dtype)


def experts(rows, gate_weight, up_weight, down_weight):
    height, width = rows[0].shape
    units = gate_weight.shape[2]
    wide = step_width(width)
    steps = width // wide
    total = len(rows) * height

    def inward(k):
        return jnp.minimum(k, steps - 1)

    def outward(k):
        return jnp.maximum(k - steps, 0)

    return pl.pallas_call(
        lambda *refs: expert_kernel(steps, len(rows), *refs),
        grid=(2 * steps,),
        in_specs=[pl.BlockSpec((height, wide), lambda k: (0, inward(k)))] * len(rows)
        + [pl.BlockSpec((1, wide, units), lambda k: (0, inward(k), 0))] * 2
        + [pl.BlockSpec((1, units, wide), lambda k: (0, 0, outward(k)))],
        out_specs=[pl.BlockSpec((height, wide), lambda k: (0, outward(k)))] * len(rows),
        out_shape=[jax.ShapeDtypeStruct((height, width), jnp.bfloat16)] * len(rows),
        scratch_shapes=[
            pltpu.VMEM((total, units), jnp.float32),
            pltpu.VMEM((total, units), jnp.float32),
            pltpu.VMEM((total, units), jnp.bfloat16),
        ],
        compiler_params=pltpu.CompilerParams(vmem_limit_bytes=24 * 2**20),
        cost_estimate=pl.CostEstimate(
            flops=6 * total * width * units,
            bytes_accessed=6 * width * units + 4 * total * width,
            transcendentals=total * units,
        ),
    )(*rows, gate_weight, up_weight, down_weight)


def added(values):
    total = values[0].astype(jnp.float32)
    for value in values[1:]:
        total = total + value.astype(jnp.float32)
    return total


def body(
    queries,
    latent_cache,
    new_latent,
    parents,
    lengths,
    expert_input,
    routed_experts,
    route_weights,
    gate_weight,
    up_weight,
    down_weight,
):
    beam_count, width = expert_input.shape
    devices = lax.axis_size("dp")
    slices = FF_E // gate_weight.shape[2]
    expert_count = devices // slices
    chips = slices // 2
    route_count = routed_experts.shape[1]
    capacity = min(beam_count, max(2, 2 * beam_count * route_count // expert_count))
    dense = capacity == beam_count
    mine = lax.axis_index("dp") // slices

    turns = jnp.arange(expert_count, dtype=jnp.int32)
    targets = (mine + turns) % expert_count
    if dense:
        slots = routed_experts * capacity + jnp.arange(beam_count, dtype=jnp.int32)[:, None]
    else:
        slots = pair_slots(routed_experts, expert_count, capacity)
    wanted = targets[:, None] * capacity + jnp.arange(capacity, dtype=jnp.int32)
    matches = (slots[:, :, None] == wanted.reshape(-1)).astype(jnp.float32)
    mixing = jnp.sum(route_weights[:, :, None] * matches, axis=1)
    if dense:
        blocks = [expert_input] * expert_count
    else:
        selector = jnp.sum(matches, axis=1).T.astype(jnp.bfloat16)
        chosen = jnp.dot(selector, expert_input, preferred_element_type=jnp.float32)
        blocks = list(chosen.astype(jnp.bfloat16).reshape(expert_count, capacity, width))

    def ahead(r):
        return lambda i: (i + r * slices) % devices

    def beside(j):
        return lambda i: i ^ (2 * j)

    def twin(i):
        return i ^ 1

    column = jnp.concatenate(
        [blocks[0]] + [swapped(blocks[r], ahead(r)) for r in range(1, expert_count)]
    )
    before = lax.ppermute(latent_cache, "dp", [(i, i + 1) for i in range(devices - 1)])
    held = [column] + [swapped(column, beside(j)) for j in range(1, chips)]
    *held, latent_again = lax.optimization_barrier((*held, latent_cache))
    after = lax.ppermute(latent_again, "dp", [(i + 1, i) for i in range(devices - 1)])
    held = held + [swapped(value, twin) for value in held]
    parts = experts(held, gate_weight, up_weight, down_weight)

    own, others = parts[:chips], parts[chips:]
    joined = {}
    for j in list(range(1, chips)) + [0]:
        joined[j] = added([own[j], swapped(others[j], twin)]).astype(jnp.bfloat16)
    arrived = [swapped(joined[j], beside(j)) for j in range(1, chips)]
    value = added([joined[0]] + arrived).reshape(expert_count, capacity, width)
    values = [value[0]] + [
        swapped(value[r].astype(jnp.bfloat16), ahead(-r)) for r in range(1, expert_count)
    ]
    if dense:
        weights = jnp.sum(mixing.reshape(beam_count, expert_count, capacity), axis=2)
        total = sum(
            weights[:, r : r + 1] * values[r].astype(jnp.float32) for r in range(expert_count)
        )
    else:
        total = jnp.dot(
            mixing,
            jnp.concatenate([v.astype(jnp.float32) for v in values]),
            precision=lax.Precision.HIGHEST,
            preferred_element_type=jnp.float32,
        )
    attention = attend(queries, before, latent_cache, after, new_latent, parents, lengths)
    return (attention, total.astype(jnp.bfloat16))


def solution(mesh):
    in_specs = (
        P(("groups", "dp"), None, None),
        P(("groups", "dp"), None, None),
        P(("groups", "dp"), None),
        P(("groups", "dp")),
        P(("groups", "dp")),
        P(("groups", "dp"), None),
        P(("groups", "dp"), None),
        P(("groups", "dp"), None),
        P("dp", None, None),
        P("dp", None, None),
        P("dp", None, None),
    )
    out_specs = (P(("groups", "dp"), None, None), P(("groups", "dp"), None))
    return jax.shard_map(body, mesh=mesh, in_specs=in_specs, out_specs=out_specs, check_vma=False)
```

time: 119 us -> 130 us (1.092)
  matrix products: 16.7 us -> 2.33 us
  Pallas kernels: 0 us -> 9.92 us
  other arithmetic: 7.04 us -> 15.4 us
  local copies, waits for them, and re-layouts: 16.6 us -> 20.6 us
    dot_general x2 -> x0, matrix products: 14.3 us -> none  [the longest x1 10.1 us: experts(): jnp.dot(hidden, down_weight[0], preferred_element_type=jnp.float32)]
    pallas_call x0 -> x1, Pallas kernels: none -> 9.92 us  [experts(): pl.pallas_call(lambda *refs: expert_kernel(steps, len(rows), *refs), grid...]
    unnamed x26 -> x53, local copies, waits for them, and re-layouts: 8.37 us -> 17 us
    concatenate x2 -> x1, local copies, waits for them, and re-layouts: 3.45 us -> 0.01 us  [body(): jnp.concatenate([blocks[0]] + [swapped(blocks[r], ahead(r)) for r in rang...]
    convert_element_type x4, other arithmetic: 1.42 us -> 4.17 us  [the longest x3 3.38 us: body(): joined[j] = added([own[j], swapped(others[j], twin)]).astype(jnp.bfloat16)]
    slice x6 -> x2, local copies, waits for them, and re-layouts: 2.07 us -> 0.74 us  [the longest x1 0.67 us: body(): value[r].astype(jnp.bfloat16)]
    another operation x0 -> x1, other arithmetic: none -> 1.31 us
    ppermute x22 -> x20, waiting for transfers between devices: 44.7 us -> 45.9 us  [swapped(): return lax.ppermute(value, 'dp', [(i, partner(i)) for i in range(peers)])]
  transfers between devices with their start and end apart: 24 -> 22, of which waited for: 7 -> 6; matrix products, arithmetic and copies ran while one was open for 18% -> 17% of each run, Pallas kernels for 0% -> 8%
where the time goes in v3:
time: 130 us; the launch traced here: 129 us
  waiting for transfers between devices  45.9 us (35%)
  starting transfers between devices  34.3 us (26%)
  local copies, waits for them, and re-layouts  20.6 us (16%)
  other arithmetic  15.4 us (12%)
  Pallas kernels  9.92 us (8%)
  matrix products  2.33 us (2%)
    ppermute x20, waiting for transfers between devices, swapped(): return lax.ppermute(value, 'dp', [(i, partner(i)) for i in range(peers)])  45.9 us
    ppermute x20, starting transfers between devices, swapped(): return lax.ppermute(value, 'dp', [(i, partner(i)) for i in range(peers)])  30.8 us
    unnamed x53, local copies, waits for them, and re-layouts  17 us
    pallas_call x1, Pallas kernels, experts(): pl.pallas_call(lambda *refs: expert_kernel(steps, len(rows), *refs), grid...  9.92 us
    concatenate x1, other arithmetic, attend(): padded = jnp.concatenate([before, latent_cache, after], axis=0)  3.88 us
    convert_element_type x3, other arithmetic, body(): joined[j] = added([own[j], swapped(others[j], twin)]).astype(jnp.bfloat16)  3.38 us
    gather x1, local copies, waits for them, and re-layouts, attend(): parent_rows = jnp.take(padded, parents - first_slot, axis=0)  2.61 us
  transfers between devices with their start and end apart: 22, of which 6 were waited for; matrix products, arithmetic and copies ran while one was open for 17% of the time, Pallas kernels for 8%

profile of v3, /device:TPU:0, one launch (start us, length us, event | category | flops | bytes accessed | tf_op | source)
XLA Modules:
  0.0 129.3 jit_solution(14790648677278440003)
XLA Ops:
  0.6 3.1 %collective-permute-start.1 = (bf16[8,7168]{1,0:T(8,128)(2,1)}, bf16[8,7168]{1,0:T(8,128)(2,1)S(1)}, u32[]{:S(2)}, u32[]{:S(2)}) collective-permute-start(bf16[8,7168]{1,0:T(8,128)(2,1)} %param.16), channel_id=1, source_target_pairs={{0,8},{1,9},{2,10},{3,11},{4,12},{5,13},{6,14},{7,15},{8,16},{9,17... | collective-permute-start | bytes 344072 | tf_op jit(solution)/shard_map/ppermute | solution.py:57
  3.7 2.6 %collective-permute-start.2 = (bf16[8,7168]{1,0:T(8,128)(2,1)}, bf16[8,7168]{1,0:T(8,128)(2,1)S(1)}, u32[]{:S(2)}, u32[]{:S(2)}) collective-permute-start(bf16[8,7168]{1,0:T(8,128)(2,1)} %param.16), channel_id=1, source_target_pairs={{0,16},{1,17},{2,18},{3,19},{4,20},{5,21},{6,22},{7,23},{8,24},{9,... | collective-permute-start | bytes 344072 | tf_op jit(solution)/shard_map/ppermute | solution.py:57
  6.3 1.3 %collective-permute-start.3 = (bf16[8,7168]{1,0:T(8,128)(2,1)}, bf16[8,7168]{1,0:T(8,128)(2,1)S(1)}, u32[]{:S(2)}, u32[]{:S(2)}) collective-permute-start(bf16[8,7168]{1,0:T(8,128)(2,1)} %param.16), channel_id=1, source_target_pairs={{0,24},{1,25},{2,26},{3,27},{4,28},{5,29},{6,30},{7,31},{8,0},{9,1... | collective-permute-start | bytes 344072 | tf_op jit(solution)/shard_map/ppermute | solution.py:57
  7.7 2.2 %collective-permute-start = (bf16[8,96,576]{2,1,0:T(8,128)(2,1)}, bf16[8,96,576]{2,1,0:T(8,128)(2,1)}, u32[]{:S(2)}, u32[]{:S(2)}) collective-permute-start(bf16[8,96,576]{2,1,0:T(8,128)(2,1)} %param.12), channel_id=1, source_target_pairs={{0,1},{1,2},{2,3},{3,4},{4,5},{5,6},{6,7},{7,8},{8,9},{9,10},{10,1... | collective-permute-start | bytes 2654216 | tf_op jit(solution)/shard_map/ppermute | solution.py:185
  9.9 0.9 constant_dynamic-update-slice_fusion.3
  10.8 3.3 %collective-permute-done.2 = bf16[8,7168]{1,0:T(8,128)(2,1)S(1)} collective-permute-done((bf16[8,7168]{1,0:T(8,128)(2,1)}, bf16[8,7168]{1,0:T(8,128)(2,1)S(1)}, u32[]{:S(2)}, u32[]{:S(2)}) %collective-permute-start.2) | collective-permute-done | bytes 114720 | tf_op jit(solution)/shard_map/ppermute | solution.py:57
  14.2 1.6 %collective-permute-start.4 = (bf16[32,7168]{1,0:T(8,128)(2,1)S(1)}, bf16[32,7168]{1,0:T(8,128)(2,1)S(1)}, u32[]{:S(2)}, u32[]{:S(2)}) collective-permute-start(bf16[32,7168]{1,0:T(8,128)(2,1)S(1)} %constant_dynamic-update-slice_fusion.refs_0_), channel_id=1, source_target_pairs={{0,2},{1,3},{2,0},{3,1},{4,6},{5,7},{6,4},{7,5},{8,10},{9,11},{10,... | collective-permute-start | bytes 1376264 | tf_op jit(solution)/shard_map/ppermute | solution.py:57
  15.8 1.5 %collective-permute-start.5 = (bf16[32,7168]{1,0:T(8,128)(2,1)S(1)}, bf16[32,7168]{1,0:T(8,128)(2,1)S(1)}, u32[]{:S(2)}, u32[]{:S(2)}) collective-permute-start(bf16[32,7168]{1,0:T(8,128)(2,1)S(1)} %constant_dynamic-update-slice_fusion.refs_0_), channel_id=1, source_target_pairs={{0,4},{1,5},{2,6},{3,7},{4,0},{5,1},{6,2},{7,3},{8,12},{9,13},{10,... | collective-permute-start | bytes 1376264 | tf_op jit(solution)/shard_map/ppermute | solution.py:57
  17.7 1.3 %iota_compare_fusion.2 = pred[8,96]{1,0:T(8,128)(4,1)} fusion(s32[8]{0:T(128)} %param.15), kind=kLoop, calls=%fused_computation.31 | loop fusion | flops 768 | bytes 800 | tf_op jit(solution)/shard_map/lt | solution.py:45
  19.1 8.6 %collective-permute-done.4.refs_1_ = bf16[32,7168]{1,0:T(8,128)(2,1)S(1)} collective-permute-done((bf16[32,7168]{1,0:T(8,128)(2,1)S(1)}, bf16[32,7168]{1,0:T(8,128)(2,1)S(1)}, u32[]{:S(2)}, u32[]{:S(2)}) %collective-permute-start.4) | collective-permute-done | bytes 458784 | tf_op jit(solution)/shard_map/ppermute | solution.py:57
  27.7 10.4 %collective-permute-done.5.refs_2_ = bf16[32,7168]{1,0:T(8,128)(2,1)S(1)} collective-permute-done((bf16[32,7168]{1,0:T(8,128)(2,1)S(1)}, bf16[32,7168]{1,0:T(8,128)(2,1)S(1)}, u32[]{:S(2)}, u32[]{:S(2)}) %collective-permute-start.5) | collective-permute-done | bytes 458784 | tf_op jit(solution)/shard_map/ppermute | solution.py:57
  38.1 4.0 %collective-permute-start.10 = (bf16[32,7168]{1,0:T(8,128)(2,1)S(1)}, bf16[32,7168]{1,0:T(8,128)(2,1)S(1)}, u32[]{:S(2)}, u32[]{:S(2)}) collective-permute-start(bf16[32,7168]{1,0:T(8,128)(2,1)S(1)} %collective-permute-done.5.refs_2_), channel_id=1, source_target_pairs={{0,1},{1,0},{2,3},{3,2},{4,5},{5,4},{6,7},{7,6},{8,9},{9,8},{10,11... | collective-permute-start | bytes 1376264 | tf_op jit(solution)/shard_map/ppermute | solution.py:57
  42.1 1.2 compare_and_fusion
  43.4 0.7 iota_add_fusion.1
  45.2 0.8 copy-done.6
  46.0 1.3 collective-permute-start.7
  47.3 0.8 select_reduce_fusion
  48.3 0.8 copy-done.10
  49.1 2.0 %copy-done.1 = bf16[1,7168,256]{2,1,0:T(8,128)(2,1)S(1)} copy-done((bf16[1,7168,256]{2,1,0:T(8,128)(2,1)S(1)}, bf16[1,7168,256]{2,1,0:T(8,128)(2,1)}, u32[]{:S(2)}) %copy-start.1) | copy-done | bytes 3670040
  51.1 2.0 %copy-done.2 = bf16[1,7168,256]{2,1,0:T(8,128)(2,1)S(1)} copy-done((bf16[1,7168,256]{2,1,0:T(8,128)(2,1)S(1)}, bf16[1,7168,256]{2,1,0:T(8,128)(2,1)}, u32[]{:S(2)}) %copy-start.2) | copy-done | bytes 3670040
  53.1 2.0 %copy-done.3 = bf16[1,256,7168]{2,1,0:T(8,128)(2,1)S(1)} copy-done((bf16[1,256,7168]{2,1,0:T(8,128)(2,1)S(1)}, bf16[1,256,7168]{2,1,0:T(8,128)(2,1)}, u32[]{:S(2)}) %copy-start.3) | copy-done | bytes 3670040
  55.2 1.0 copy-done.7
  56.2 1.0 copy-done.11
  57.2 9.9 %shard_map.122 = (bf16[32,7168]{1,0:T(8,128)(2,1)S(1)}, bf16[32,7168]{1,0:T(8,128)(2,1)S(1)}, bf16[32,7168]{1,0:T(8,128)(2,1)S(1)}, bf16[32,7168]{1,0:T(8,128)(2...) custom-call(bf16[32,7168]{1,0:T(8,128)(2,1)S(1)} %constant_dynamic-u, ...), custom_call_target="tpu_custom_call" | custom-call | flops 2818572288 | bytes 18350080 | tf_op jit(solution)/shard_map/pallas_call | solution.py:105
  67.1 0.8 copy-done.4
  67.9 0.8 copy-done.8
  68.7 0.8 copy-done.12
  69.5 0.8 copy-done.13
  70.3 0.8 copy-done.14
  71.1 1.1 collective-permute-start.13
  73.4 0.7 copy.19
  75.9 3.9 %pad_maximum_fusion = bf16[24,96,576]{2,1,0:T(8,128)(2,1)} fusion(bf16[8,96,576]{2,1,0:T(8,128)(2,1)} %collective-permute-done.7, bf16[8,96,576]{2,1,0:T(8,128)(2,1)} %param.12, bf16[8,96,576]{2,1,0:T(8,128)(2,1)} %collective-permute-done), kind=kLoop, calls=%fused_computation.2 | loop fusion | flops 2654208 | bytes 5308416 | tf_op jit(solution)/shard_map/concatenate | solution.py:29
  79.8 2.6 %gather_fusion = bf16[8,96,576]{2,1,0:T(8,128)(2,1)S(1)} fusion(bf16[24,96,576]{2,1,0:T(8,128)(2,1)} %pad_maximum_fusion, s32[1024]{0:T(1024)S(1)} %pad_clamp_fusion), kind=kCustom, calls=%fused_computation | custom fusion | bytes 1769504 | tf_op jit(solution)/shard_map/jit(_take)/gather | solution.py:30
  82.4 1.1 add_convert_fusion.2
  83.6 3.2 %collective-permute-start.14 = (bf16[32,7168]{1,0:T(8,128)(2,1)S(1)}, bf16[32,7168]{1,0:T(8,128)(2,1)S(1)}, u32[]{:S(2)}, u32[]{:S(2)}) collective-permute-start(bf16[32,7168]{1,0:T(8,128)(2,1)S(1)} %add_convert_fusion.2), channel_id=1, source_target_pairs={{0,2},{1,3},{2,0},{3,1},{4,6},{5,7},{6,4},{7,5},{8,10},{9,11},{10,... | collective-permute-start | bytes 1376264 | tf_op jit(solution)/shard_map/ppermute | solution.py:57
  86.8 1.1 add_convert_fusion.1
  87.9 2.2 %collective-permute-start.16 = (bf16[32,7168]{1,0:T(8,128)(2,1)S(1)}, bf16[32,7168]{1,0:T(8,128)(2,1)S(1)}, u32[]{:S(2)}, u32[]{:S(2)}) collective-permute-start(bf16[32,7168]{1,0:T(8,128)(2,1)S(1)} %add_convert_fusion.1), channel_id=1, source_target_pairs={{0,4},{1,5},{2,6},{3,7},{4,0},{5,1},{6,2},{7,3},{8,12},{9,13},{10,... | collective-permute-start | bytes 1376264 | tf_op jit(solution)/shard_map/ppermute | solution.py:57
  90.1 1.1 add_convert_fusion
  91.2 0.9 collective-permute-start.18
  93.3 4.9 %collective-permute-done.14 = bf16[32,7168]{1,0:T(8,128)(2,1)S(1)} collective-permute-done((bf16[32,7168]{1,0:T(8,128)(2,1)S(1)}, bf16[32,7168]{1,0:T(8,128)(2,1)S(1)}, u32[]{:S(2)}, u32[]{:S(2)}) %collective-permute-start.14) | collective-permute-done | bytes 458784 | tf_op jit(solution)/shard_map/ppermute | solution.py:57
  98.2 12.3 %collective-permute-done.16 = bf16[32,7168]{1,0:T(8,128)(2,1)S(1)} collective-permute-done((bf16[32,7168]{1,0:T(8,128)(2,1)S(1)}, bf16[32,7168]{1,0:T(8,128)(2,1)S(1)}, u32[]{:S(2)}, u32[]{:S(2)}) %collective-permute-start.16) | collective-permute-done | bytes 458784 | tf_op jit(solution)/shard_map/ppermute | solution.py:57
  110.4 1.3 %fusion.14 = (bf16[32,7168]{1,0:T(8,128)(2,1)S(1)}, f32[32,7168]{1,0:T(8,128)S(1)}) fusion(bf16[32,7168]{1,0:T(8,128)(2,1)S(1)} %collective-permute-done.18, bf16[32,7168]{1,0:T(8,128)(2,1)S(1)} %collective-permute-done.16, bf16[32,7168]{1,0:T(8,128)(2,1)S(1)} %collective-permute-done.14, bf16[32,7168]{1,0:T(8,128)(2,1)} %collective-permute-done.12, ...), kind=kLoop, calls=%fused_computation.43 | loop fusion | flops 2752512 | bytes 3670016 | tf_op jit(solution)/shard_map/convert.2
  111.8 0.7 fusion.15
  112.4 5.3 %collective-permute-start.19 = (bf16[8,7168]{1,0:T(8,128)(2,1)}, bf16[8,7168]{1,0:T(8,128)(2,1)S(1)}, u32[]{:S(2)}, u32[]{:S(2)}) collective-permute-start(bf16[8,7168]{1,0:T(8,128)(2,1)} %get-tuple-element.32), channel_id=1, source_target_pairs={{0,24},{1,25},{2,26},{3,27},{4,28},{5,29},{6,30},{7,31},{8,0},{9,1... | collective-permute-start | bytes 344072 | tf_op jit(solution)/shard_map/ppermute | solution.py:57
  118.1 2.0 %collective-permute-start.21 = (bf16[8,7168]{1,0:T(8,128)(2,1)S(1)}, bf16[8,7168]{1,0:T(8,128)(2,1)S(1)}, u32[]{:S(2)}, u32[]{:S(2)}) collective-permute-start(bf16[8,7168]{1,0:T(8,128)(2,1)S(1)} %get-tuple-element.33), channel_id=1, source_target_pairs={{0,8},{1,9},{2,10},{3,11},{4,12},{5,13},{6,14},{7,15},{8,16},{9,17... | collective-permute-start | bytes 344072 | tf_op jit(solution)/shard_map/ppermute | solution.py:57
  120.1 1.8 %convolution_convert_fusion = bf16[8,64,512]{2,1,0:T(8,128)(2,1)} fusion(bf16[8,96,576]{2,1,0:T(8,128)(2,1)S(1)} %select_select_fusion, f32[8,64]{1,0:T(8,128)S(1)} %fusion.17, f32[8,64,96]{2,1,0:T(8,128)S(1)} %fusion.3), kind=kOutput, calls=%fused_computation.3 | convolution fusion | flops 50741856 | bytes 1839104 | tf_op jit(solution)/shard_map/bhl,blc->bhc/dot_general | solution.py:49
  122.0 6.5 %collective-permute-done.20 = bf16[8,7168]{1,0:T(8,128)(2,1)S(1)} collective-permute-done((bf16[8,7168]{1,0:T(8,128)(2,1)S(1)}, bf16[8,7168]{1,0:T(8,128)(2,1)S(1)}, u32[]{:S(2)}, u32[]{:S(2)}) %collective-permute-start.20) | collective-permute-done | bytes 114720 | tf_op jit(solution)/shard_map/ppermute | solution.py:57
  128.5 0.8 fusion.9
  (76 shorter events, 6.7 us)
Async XLA Ops:
  0.6 91.9 %copy-start = (bf16[8,64,576]{2,1,0:T(8,128)(2,1)S(1)}, bf16[8,64,576]{2,1,0:T(8,128)(2,1)}, u32[]{:S(2)}) copy-start(bf16[8,64,576]{2,1,0:T(8,128)(2,1)} %param.11) | copy-start | bytes 1769476
  0.6 10.2 %collective-permute-start.1 = (bf16[8,7168]{1,0:T(8,128)(2,1)}, bf16[8,7168]{1,0:T(8,128)(2,1)S(1)}, u32[]{:S(2)}, u32[]{:S(2)}) collective-permute-start(bf16[8,7168]{1,0:T(8,128)(2,1)} %param.16), channel_id=1, source_target_pairs={{0,8},{1,9},{2,10},{3,11},{4,12},{5,13},{6,14},{7,15},{8,16},{9,17... | collective-permute-start | bytes 344072 | tf_op jit(solution)/shard_map/ppermute | solution.py:57
  3.7 10.4 %collective-permute-start.2 = (bf16[8,7168]{1,0:T(8,128)(2,1)}, bf16[8,7168]{1,0:T(8,128)(2,1)S(1)}, u32[]{:S(2)}, u32[]{:S(2)}) collective-permute-start(bf16[8,7168]{1,0:T(8,128)(2,1)} %param.16), channel_id=1, source_target_pairs={{0,16},{1,17},{2,18},{3,19},{4,20},{5,21},{6,22},{7,23},{8,24},{9,... | collective-permute-start | bytes 344072 | tf_op jit(solution)/shard_map/ppermute | solution.py:57
  6.3 7.8 %collective-permute-start.3 = (bf16[8,7168]{1,0:T(8,128)(2,1)}, bf16[8,7168]{1,0:T(8,128)(2,1)S(1)}, u32[]{:S(2)}, u32[]{:S(2)}) collective-permute-start(bf16[8,7168]{1,0:T(8,128)(2,1)} %param.16), channel_id=1, source_target_pairs={{0,24},{1,25},{2,26},{3,27},{4,28},{5,29},{6,30},{7,31},{8,0},{9,1... | collective-permute-start | bytes 344072 | tf_op jit(solution)/shard_map/ppermute | solution.py:57
  7.7 68.2 %collective-permute-start = (bf16[8,96,576]{2,1,0:T(8,128)(2,1)}, bf16[8,96,576]{2,1,0:T(8,128)(2,1)}, u32[]{:S(2)}, u32[]{:S(2)}) collective-permute-start(bf16[8,96,576]{2,1,0:T(8,128)(2,1)} %param.12), channel_id=1, source_target_pairs={{0,1},{1,2},{2,3},{3,4},{4,5},{5,6},{6,7},{7,8},{8,9},{9,10},{10,1... | collective-permute-start | bytes 2654216 | tf_op jit(solution)/shard_map/ppermute | solution.py:185
  14.2 13.5 %collective-permute-start.4 = (bf16[32,7168]{1,0:T(8,128)(2,1)S(1)}, bf16[32,7168]{1,0:T(8,128)(2,1)S(1)}, u32[]{:S(2)}, u32[]{:S(2)}) collective-permute-start(bf16[32,7168]{1,0:T(8,128)(2,1)S(1)} %constant_dynamic-update-slice_fusion.refs_0_), channel_id=1, source_target_pairs={{0,2},{1,3},{2,0},{3,1},{4,6},{5,7},{6,4},{7,5},{8,10},{9,11},{10,... | collective-permute-start | bytes 1376264 | tf_op jit(solution)/shard_map/ppermute | solution.py:57
  15.8 22.3 %collective-permute-start.5 = (bf16[32,7168]{1,0:T(8,128)(2,1)S(1)}, bf16[32,7168]{1,0:T(8,128)(2,1)S(1)}, u32[]{:S(2)}, u32[]{:S(2)}) collective-permute-start(bf16[32,7168]{1,0:T(8,128)(2,1)S(1)} %constant_dynamic-update-slice_fusion.refs_0_), channel_id=1, source_target_pairs={{0,4},{1,5},{2,6},{3,7},{4,0},{5,1},{6,2},{7,3},{8,12},{9,13},{10,... | collective-permute-start | bytes 1376264 | tf_op jit(solution)/shard_map/ppermute | solution.py:57
  17.3 20.8 %collective-permute-start.6 = (bf16[32,7168]{1,0:T(8,128)(2,1)S(1)}, bf16[32,7168]{1,0:T(8,128)(2,1)S(1)}, u32[]{:S(2)}, u32[]{:S(2)}) collective-permute-start(bf16[32,7168]{1,0:T(8,128)(2,1)S(1)} %constant_dynamic-update-slice_fusion.refs_0_), channel_id=1, source_target_pairs={{0,6},{1,7},{2,4},{3,5},{4,2},{5,3},{6,0},{7,1},{8,14},{9,15},{10,... | collective-permute-start | bytes 1376264 | tf_op jit(solution)/shard_map/ppermute | solution.py:57
  38.1 7.2 %collective-permute-start.10 = (bf16[32,7168]{1,0:T(8,128)(2,1)S(1)}, bf16[32,7168]{1,0:T(8,128)(2,1)S(1)}, u32[]{:S(2)}, u32[]{:S(2)}) collective-permute-start(bf16[32,7168]{1,0:T(8,128)(2,1)S(1)} %collective-permute-done.5.refs_2_), channel_id=1, source_target_pairs={{0,1},{1,0},{2,3},{3,2},{4,5},{5,4},{6,7},{7,6},{8,9},{9,8},{10,11... | collective-permute-start | bytes 1376264 | tf_op jit(solution)/shard_map/ppermute | solution.py:57
  44.1 4.2 %collective-permute-start.11 = (bf16[32,7168]{1,0:T(8,128)(2,1)S(1)}, bf16[32,7168]{1,0:T(8,128)(2,1)S(1)}, u32[]{:S(2)}, u32[]{:S(2)}) collective-permute-start(bf16[32,7168]{1,0:T(8,128)(2,1)S(1)} %collective-permute-done.6.refs_3_), channel_id=1, source_target_pairs={{0,1},{1,0},{2,3},{3,2},{4,5},{5,4},{6,7},{7,6},{8,9},{9,8},{10,11... | collective-permute-start | bytes 1376264 | tf_op jit(solution)/shard_map/ppermute | solution.py:57
  44.1 5.0 %collective-permute-start.8 = (bf16[32,7168]{1,0:T(8,128)(2,1)S(1)}, bf16[32,7168]{1,0:T(8,128)(2,1)}, u32[]{:S(2)}, u32[]{:S(2)}) collective-permute-start(bf16[32,7168]{1,0:T(8,128)(2,1)S(1)} %constant_dynamic-update-slice_fusion.refs_0_), channel_id=1, source_target_pairs={{0,1},{1,0},{2,3},{3,2},{4,5},{5,4},{6,7},{7,6},{8,9},{9,8},{10,11... | collective-permute-start | bytes 1376264 | tf_op jit(solution)/shard_map/ppermute | solution.py:57
  44.6 4.5 %collective-permute-start.9 = (bf16[32,7168]{1,0:T(8,128)(2,1)S(1)}, bf16[32,7168]{1,0:T(8,128)(2,1)}, u32[]{:S(2)}, u32[]{:S(2)}) collective-permute-start(bf16[32,7168]{1,0:T(8,128)(2,1)S(1)} %collective-permute-done.4.refs_1_), channel_id=1, source_target_pairs={{0,1},{1,0},{2,3},{3,2},{4,5},{5,4},{6,7},{7,6},{8,9},{9,8},{10,11... | collective-permute-start | bytes 1376264 | tf_op jit(solution)/shard_map/ppermute | solution.py:57
  45.2 0.8 copy-start.6
  46.0 29.9 %collective-permute-start.7 = (bf16[8,96,576]{2,1,0:T(8,128)(2,1)}, bf16[8,96,576]{2,1,0:T(8,128)(2,1)}, u32[]{:S(2)}, u32[]{:S(2)}) collective-permute-start(bf16[8,96,576]{2,1,0:T(8,128)(2,1)} %param.12), channel_id=1, source_target_pairs={{1,0},{2,1},{3,2},{4,3},{5,4},{6,5},{7,6},{8,7},{9,8},{10,9},{11,1... | collective-permute-start | bytes 2654216 | tf_op jit(solution)/shard_map/ppermute | solution.py:188
  48.3 0.8 copy-start.10
  49.1 2.0 %copy-start.1 = (bf16[1,7168,256]{2,1,0:T(8,128)(2,1)S(1)}, bf16[1,7168,256]{2,1,0:T(8,128)(2,1)}, u32[]{:S(2)}) copy-start(bf16[1,7168,256]{2,1,0:T(8,128)(2,1)} %refs_8_.1) | copy-start | bytes 11010052
  51.1 2.0 %copy-start.2 = (bf16[1,7168,256]{2,1,0:T(8,128)(2,1)S(1)}, bf16[1,7168,256]{2,1,0:T(8,128)(2,1)}, u32[]{:S(2)}) copy-start(bf16[1,7168,256]{2,1,0:T(8,128)(2,1)} %refs_9_.1) | copy-start | bytes 11010052
  53.1 2.0 %copy-start.3 = (bf16[1,256,7168]{2,1,0:T(8,128)(2,1)S(1)}, bf16[1,256,7168]{2,1,0:T(8,128)(2,1)}, u32[]{:S(2)}) copy-start(bf16[1,256,7168]{2,1,0:T(8,128)(2,1)} %refs_10_.1) | copy-start | bytes 11010052
  55.2 1.0 copy-start.7
  56.2 1.0 copy-start.11
  67.1 0.8 copy-start.4
  67.9 0.8 copy-start.8
  68.7 0.8 copy-start.12
  69.5 0.8 copy-start.13
  70.3 0.8 copy-start.14
  71.1 11.4 %collective-permute-start.13 = (bf16[32,7168]{1,0:T(8,128)(2,1)}, bf16[32,7168]{1,0:T(8,128)(2,1)}, u32[]{:S(2)}, u32[]{:S(2)}) collective-permute-start(bf16[32,7168]{1,0:T(8,128)(2,1)} %get-tuple-element.23), channel_id=1, source_target_pairs={{0,1},{1,0},{2,3},{3,2},{4,5},{5,4},{6,7},{7,6},{8,9},{9,8},{10,11... | collective-permute-start | bytes 1376264 | tf_op jit(solution)/shard_map/ppermute | solution.py:57
  75.3 11.5 %collective-permute-start.15 = (bf16[32,7168]{1,0:T(8,128)(2,1)}, bf16[32,7168]{1,0:T(8,128)(2,1)}, u32[]{:S(2)}, u32[]{:S(2)}) collective-permute-start(bf16[32,7168]{1,0:T(8,128)(2,1)} %copy-done.14), channel_id=1, source_target_pairs={{0,1},{1,0},{2,3},{3,2},{4,5},{5,4},{6,7},{7,6},{8,9},{9,8},{10,11... | collective-permute-start | bytes 1376264 | tf_op jit(solution)/shard_map/ppermute | solution.py:57
  75.3 14.8 %collective-permute-start.17 = (bf16[32,7168]{1,0:T(8,128)(2,1)}, bf16[32,7168]{1,0:T(8,128)(2,1)}, u32[]{:S(2)}, u32[]{:S(2)}) collective-permute-start(bf16[32,7168]{1,0:T(8,128)(2,1)} %copy-done.13), channel_id=1, source_target_pairs={{0,1},{1,0},{2,3},{3,2},{4,5},{5,4},{6,7},{7,6},{8,9},{9,8},{10,11... | collective-permute-start | bytes 1376264 | tf_op jit(solution)/shard_map/ppermute | solution.py:57
  75.8 6.6 %copy-start.9 = (bf16[32,7168]{1,0:T(8,128)(2,1)S(1)}, bf16[32,7168]{1,0:T(8,128)(2,1)}, u32[]{:S(2)}) copy-start(bf16[32,7168]{1,0:T(8,128)(2,1)} %copy-done.8) | copy-start | bytes 1376260
  75.8 17.5 %collective-permute-start.12 = (bf16[32,7168]{1,0:T(8,128)(2,1)}, bf16[32,7168]{1,0:T(8,128)(2,1)}, u32[]{:S(2)}, u32[]{:S(2)}) collective-permute-start(bf16[32,7168]{1,0:T(8,128)(2,1)} %copy-done.12), channel_id=1, source_target_pairs={{0,1},{1,0},{2,3},{3,2},{4,5},{5,4},{6,7},{7,6},{8,9},{9,8},{10,11... | collective-permute-start | bytes 1376264 | tf_op jit(solution)/shard_map/ppermute | solution.py:57
  79.8 7.0 %copy-start.5 = (bf16[32,7168]{1,0:T(8,128)(2,1)S(1)}, bf16[32,7168]{1,0:T(8,128)(2,1)}, u32[]{:S(2)}) copy-start(bf16[32,7168]{1,0:T(8,128)(2,1)} %copy-done.4) | copy-start | bytes 1376260
  79.8 12.3 %copy-start.15 = (bf16[8,576]{1,0:T(8,128)(2,1)S(1)}, bf16[8,576]{1,0:T(8,128)(2,1)}, u32[]{:S(2)}) copy-start(bf16[8,576]{1,0:T(8,128)(2,1)} %param.13) | copy-start | bytes 27652
  82.4 9.7 %copy-start.16 = (pred[8,96]{1,0:T(8,128)(4,1)S(1)}, pred[8,96]{1,0:T(8,128)(4,1)}, u32[]{:S(2)}) copy-start(pred[8,96]{1,0:T(8,128)(4,1)} %get-tuple-element.40) | copy-start | bytes 2308
  82.4 9.7 %copy-start.17 = (pred[8]{0:T(512)(128)(4,1)S(1)}, pred[8]{0:T(512)(128)(4,1)}, u32[]{:S(2)}) copy-start(pred[8]{0:T(512)(128)(4,1)} %get-tuple-element.30) | copy-start | bytes 28
  82.4 10.1 %copy-start.22 = (pred[8,96]{1,0:T(8,128)(4,1)S(1)}, pred[8,96]{1,0:T(8,128)(4,1)}, u32[]{:S(2)}) copy-start(pred[8,96]{1,0:T(8,128)(4,1)} %iota_compare_fusion.2) | copy-start | bytes 2308
  83.6 14.6 %collective-permute-start.14 = (bf16[32,7168]{1,0:T(8,128)(2,1)S(1)}, bf16[32,7168]{1,0:T(8,128)(2,1)S(1)}, u32[]{:S(2)}, u32[]{:S(2)}) collective-permute-start(bf16[32,7168]{1,0:T(8,128)(2,1)S(1)} %add_convert_fusion.2), channel_id=1, source_target_pairs={{0,2},{1,3},{2,0},{3,1},{4,6},{5,7},{6,4},{7,5},{8,10},{9,11},{10,... | collective-permute-start | bytes 1376264 | tf_op jit(solution)/shard_map/ppermute | solution.py:57
  87.9 22.5 %collective-permute-start.16 = (bf16[32,7168]{1,0:T(8,128)(2,1)S(1)}, bf16[32,7168]{1,0:T(8,128)(2,1)S(1)}, u32[]{:S(2)}, u32[]{:S(2)}) collective-permute-start(bf16[32,7168]{1,0:T(8,128)(2,1)S(1)} %add_convert_fusion.1), channel_id=1, source_target_pairs={{0,4},{1,5},{2,6},{3,7},{4,0},{5,1},{6,2},{7,3},{8,12},{9,13},{10,... | collective-permute-start | bytes 1376264 | tf_op jit(solution)/shard_map/ppermute | solution.py:57
  91.2 19.2 %collective-permute-start.18 = (bf16[32,7168]{1,0:T(8,128)(2,1)S(1)}, bf16[32,7168]{1,0:T(8,128)(2,1)S(1)}, u32[]{:S(2)}, u32[]{:S(2)}) collective-permute-start(bf16[32,7168]{1,0:T(8,128)(2,1)S(1)} %add_convert_fusion), channel_id=1, source_target_pairs={{0,6},{1,7},{2,4},{3,5},{4,2},{5,3},{6,0},{7,1},{8,14},{9,15},{10,... | collective-permute-start | bytes 1376264 | tf_op jit(solution)/shard_map/ppermute | solution.py:57
  110.4 18.0 %copy-start.18 = (f32[8,1]{0,1:T(1,128)S(1)}, f32[8,1]{0,1:T(1,128)}, u32[]{:S(2)}) copy-start(f32[8,1]{0,1:T(1,128)} %copy.17) | copy-start | bytes 100
  110.4 18.0 %copy-start.19 = (f32[8,1]{0,1:T(1,128)S(1)}, f32[8,1]{0,1:T(1,128)}, u32[]{:S(2)}) copy-start(f32[8,1]{0,1:T(1,128)} %copy.18) | copy-start | bytes 100
  110.4 18.0 %copy-start.20 = (f32[8,1]{0,1:T(1,128)S(1)}, f32[8,1]{0,1:T(1,128)}, u32[]{:S(2)}) copy-start(f32[8,1]{0,1:T(1,128)} %copy.19) | copy-start | bytes 100
  110.4 18.0 %copy-start.21 = (f32[8,1]{0,1:T(1,128)S(1)}, f32[8,1]{0,1:T(1,128)}, u32[]{:S(2)}) copy-start(f32[8,1]{0,1:T(1,128)} %copy.20) | copy-start | bytes 100
  112.4 9.5 %collective-permute-start.19 = (bf16[8,7168]{1,0:T(8,128)(2,1)}, bf16[8,7168]{1,0:T(8,128)(2,1)S(1)}, u32[]{:S(2)}, u32[]{:S(2)}) collective-permute-start(bf16[8,7168]{1,0:T(8,128)(2,1)} %get-tuple-element.32), channel_id=1, source_target_pairs={{0,24},{1,25},{2,26},{3,27},{4,28},{5,29},{6,30},{7,31},{8,0},{9,1... | collective-permute-start | bytes 344072 | tf_op jit(solution)/shard_map/ppermute | solution.py:57
  117.7 10.7 %collective-permute-start.20 = (bf16[8,7168]{1,0:T(8,128)(2,1)S(1)}, bf16[8,7168]{1,0:T(8,128)(2,1)S(1)}, u32[]{:S(2)}, u32[]{:S(2)}) collective-permute-start(bf16[8,7168]{1,0:T(8,128)(2,1)S(1)} %get-tuple-element.34), channel_id=1, source_target_pairs={{0,16},{1,17},{2,18},{3,19},{4,20},{5,21},{6,22},{7,23},{8,24},{9,... | collective-permute-start | bytes 344072 | tf_op jit(solution)/shard_map/ppermute | solution.py:57
  118.1 10.4 %collective-permute-start.21 = (bf16[8,7168]{1,0:T(8,128)(2,1)S(1)}, bf16[8,7168]{1,0:T(8,128)(2,1)S(1)}, u32[]{:S(2)}, u32[]{:S(2)}) collective-permute-start(bf16[8,7168]{1,0:T(8,128)(2,1)S(1)} %get-tuple-element.33), channel_id=1, source_target_pairs={{0,8},{1,9},{2,10},{3,11},{4,12},{5,13},{6,14},{7,15},{8,16},{9,17... | collective-permute-start | bytes 344072 | tf_op jit(solution)/shard_map/ppermute | solution.py:57

commit v4 on v3

--- a/solution.py
+++ b/solution.py
@@ -115,7 +115,7 @@
             pltpu.VMEM((total, units), jnp.float32),
             pltpu.VMEM((total, units), jnp.bfloat16),
         ],
-        compiler_params=pltpu.CompilerParams(vmem_limit_bytes=24 * 2**20),
+        compiler_params=pltpu.CompilerParams(vmem_limit_bytes=60 * 2**20),
         cost_estimate=pl.CostEstimate(
             flops=6 * total * width * units,
             bytes_accessed=6 * width * units + 4 * total * width,
@@ -148,11 +148,11 @@
     devices = lax.axis_size("dp")
     slices = FF_E // gate_weight.shape[2]
     expert_count = devices // slices
-    chips = slices // 2
     route_count = routed_experts.shape[1]
     capacity = min(beam_count, max(2, 2 * beam_count * route_count // expert_count))
     dense = capacity == beam_count
     mine = lax.axis_index("dp") // slices
+    assert slices == 8
 
     turns = jnp.arange(expert_count, dtype=jnp.int32)
     targets = (mine + turns) % expert_count
@@ -173,28 +173,39 @@
     def ahead(r):
         return lambda i: (i + r * slices) % devices
 
-    def beside(j):
-        return lambda i: i ^ (2 * j)
-
     def twin(i):
         return i ^ 1
 
+    def first(i):
+        return i ^ (2 if i & 1 else 4)
+
+    def second(i):
+        return i ^ (4 if i & 1 else 2)
+
     column = jnp.concatenate(
         [blocks[0]] + [swapped(blocks[r], ahead(r)) for r in range(1, expert_count)]
     )
     before = lax.ppermute(latent_cache, "dp", [(i, i + 1) for i in range(devices - 1)])
-    held = [column] + [swapped(column, beside(j)) for j in range(1, chips)]
-    *held, latent_again = lax.optimization_barrier((*held, latent_cache))
-    after = lax.ppermute(latent_again, "dp", [(i + 1, i) for i in range(devices - 1)])
+    near = swapped(column, first)
+    side = swapped(column, second)
+    across = swapped(near, second)
+    held = [column, near, side, across]
+    *held, latent_cache, mixing = lax.optimization_barrier((*held, latent_cache, mixing))
+    after = lax.ppermute(latent_cache, "dp", [(i + 1, i) for i in range(devices - 1)])
     held = held + [swapped(value, twin) for value in held]
     parts = experts(held, gate_weight, up_weight, down_weight)
 
-    own, others = parts[:chips], parts[chips:]
-    joined = {}
-    for j in list(range(1, chips)) + [0]:
-        joined[j] = added([own[j], swapped(others[j], twin)]).astype(jnp.bfloat16)
-    arrived = [swapped(joined[j], beside(j)) for j in range(1, chips)]
-    value = added([joined[0]] + arrived).reshape(expert_count, capacity, width)
+    own, others = parts[:4], parts[4:]
+
+    def joined(j):
+        return added([own[j], swapped(others[j], twin)]).astype(jnp.bfloat16)
+
+    across = swapped(joined(3), second)
+    side = swapped(joined(2), second)
+    near = added([own[1], swapped(others[1], twin), across]).astype(jnp.bfloat16)
+    near, before, after = lax.optimization_barrier((near, before, after))
+    near = swapped(near, first)
+    value = added([joined(0), side, near]).reshape(expert_count, capacity, width)
     values = [value[0]] + [
         swapped(value[r].astype(jnp.bfloat16), ahead(-r)) for r in range(1, expert_count)
     ]

time: 130 us -> 112 us (0.86)
  local copies, waits for them, and re-layouts: 20.6 us -> 7.38 us
  starting transfers between devices: 34.3 us -> 25.7 us
  Pallas kernels: 9.92 us -> 13.9 us
  other arithmetic: 15.4 us -> 16.8 us
    unnamed x53 -> x31, local copies, waits for them, and re-layouts: 17 us -> 2.6 us
    ppermute x20, starting transfers between devices: 30.8 us -> 22.9 us  [swapped(): return lax.ppermute(value, 'dp', [(i, partner(i)) for i in range(peers)])]
    pallas_call x1, Pallas kernels: 9.92 us -> 13.9 us  [experts(): pl.pallas_call(lambda *refs: expert_kernel(steps, len(rows), *refs), grid...]
    ppermute x20, waiting for transfers between devices: 45.9 us -> 44.6 us  [swapped(): return lax.ppermute(value, 'dp', [(i, partner(i)) for i in range(peers)])]
  transfers between devices with their start and end apart: 22 -> 22, of which waited for: 6 -> 10; matrix products, arithmetic and copies ran while one was open for 17% -> 21% of each run, Pallas kernels for 8% -> 12%
where the time goes in v4:
time: 112 us
  waiting for transfers between devices  44.6 us (40%)
  starting transfers between devices  25.7 us (23%)
  other arithmetic  16.8 us (15%)
  Pallas kernels  13.9 us (12%)
  local copies, waits for them, and re-layouts  7.38 us (7%)
  matrix products  2.33 us (2%)
    ppermute x20, waiting for transfers between devices, swapped(): return lax.ppermute(value, 'dp', [(i, partner(i)) for i in range(peers)])  44.6 us
    ppermute x20, starting transfers between devices, swapped(): return lax.ppermute(value, 'dp', [(i, partner(i)) for i in range(peers)])  22.9 us
    pallas_call x1, Pallas kernels, experts(): pl.pallas_call(lambda *refs: expert_kernel(steps, len(rows), *refs), grid...  13.9 us
    concatenate x1, other arithmetic, attend(): padded = jnp.concatenate([before, latent_cache, after], axis=0)  3.24 us
    convert_element_type x2, other arithmetic, joined(): return added([own[j], swapped(others[j], twin)]).astype(jnp.bfloat16)  3.02 us
    gather x1, local copies, waits for them, and re-layouts, attend(): parent_rows = jnp.take(padded, parents - first_slot, axis=0)  2.73 us
    unnamed x31, local copies, waits for them, and re-layouts  2.6 us
  transfers between devices with their start and end apart: 22, of which 10 were waited for; matrix products, arithmetic and copies ran while one was open for 21% of the time, Pallas kernels for 12%

profile of v4, /device:TPU:0, one launch (start us, length us, event | category | flops | bytes accessed | tf_op | source)
XLA Modules:
  0.0 111.6 jit_solution(3830612949151782589)
XLA Ops:
  0.6 3.1 %collective-permute-start = (bf16[8,7168]{1,0:T(8,128)(2,1)}, bf16[8,7168]{1,0:T(8,128)(2,1)S(1)}, u32[]{:S(2)}, u32[]{:S(2)}) collective-permute-start(bf16[8,7168]{1,0:T(8,128)(2,1)} %param.16), channel_id=1, source_target_pairs={{0,8},{1,9},{2,10},{3,11},{4,12},{5,13},{6,14},{7,15},{8,16},{9,17... | collective-permute-start | bytes 344072 | tf_op jit(solution)/shard_map/ppermute | solution.py:57
  3.7 2.6 %collective-permute-start.1 = (bf16[8,7168]{1,0:T(8,128)(2,1)}, bf16[8,7168]{1,0:T(8,128)(2,1)S(1)}, u32[]{:S(2)}, u32[]{:S(2)}) collective-permute-start(bf16[8,7168]{1,0:T(8,128)(2,1)} %param.16), channel_id=1, source_target_pairs={{0,16},{1,17},{2,18},{3,19},{4,20},{5,21},{6,22},{7,23},{8,24},{9,... | collective-permute-start | bytes 344072 | tf_op jit(solution)/shard_map/ppermute | solution.py:57
  6.3 1.3 %collective-permute-start.2 = (bf16[8,7168]{1,0:T(8,128)(2,1)}, bf16[8,7168]{1,0:T(8,128)(2,1)S(1)}, u32[]{:S(2)}, u32[]{:S(2)}) collective-permute-start(bf16[8,7168]{1,0:T(8,128)(2,1)} %param.16), channel_id=1, source_target_pairs={{0,24},{1,25},{2,26},{3,27},{4,28},{5,29},{6,30},{7,31},{8,0},{9,1... | collective-permute-start | bytes 344072 | tf_op jit(solution)/shard_map/ppermute | solution.py:57
  7.7 0.9 constant_dynamic-update-slice_fusion.3
  8.6 1.4 %collective-permute-done = bf16[8,7168]{1,0:T(8,128)(2,1)S(1)} collective-permute-done((bf16[8,7168]{1,0:T(8,128)(2,1)}, bf16[8,7168]{1,0:T(8,128)(2,1)S(1)}, u32[]{:S(2)}, u32[]{:S(2)}) %collective-permute-start) | collective-permute-done | bytes 114720 | tf_op jit(solution)/shard_map/ppermute | solution.py:57
  10.0 4.1 %collective-permute-done.1 = bf16[8,7168]{1,0:T(8,128)(2,1)S(1)} collective-permute-done((bf16[8,7168]{1,0:T(8,128)(2,1)}, bf16[8,7168]{1,0:T(8,128)(2,1)S(1)}, u32[]{:S(2)}, u32[]{:S(2)}) %collective-permute-start.1) | collective-permute-done | bytes 114720 | tf_op jit(solution)/shard_map/ppermute | solution.py:57
  14.2 1.6 %collective-permute-start.3 = (bf16[32,7168]{1,0:T(8,128)(2,1)S(1)}, bf16[32,7168]{1,0:T(8,128)(2,1)S(1)}, u32[]{:S(2)}, u32[]{:S(2)}) collective-permute-start(bf16[32,7168]{1,0:T(8,128)(2,1)S(1)} %constant_dynamic-update-slice_fusion.refs_0_), channel_id=1, source_target_pairs={{0,4},{1,3},{2,6},{3,1},{4,0},{5,7},{6,2},{7,5},{8,12},{9,11},{10,... | collective-permute-start | bytes 1376264 | tf_op jit(solution)/shard_map/ppermute | solution.py:57
  15.8 1.6 %collective-permute-start.13 = (bf16[8,96,576]{2,1,0:T(8,128)(2,1)}, bf16[8,96,576]{2,1,0:T(8,128)(2,1)S(1)}, u32[]{:S(2)}, u32[]{:S(2)}) collective-permute-start(bf16[8,96,576]{2,1,0:T(8,128)(2,1)} %param.12), channel_id=1, source_target_pairs={{0,1},{1,2},{2,3},{3,4},{4,5},{5,6},{6,7},{7,8},{8,9},{9,10},{10,1... | collective-permute-start | bytes 2654216 | tf_op jit(solution)/shard_map/ppermute | solution.py:188
  17.4 1.9 %collective-permute-start.4 = (bf16[32,7168]{1,0:T(8,128)(2,1)S(1)}, bf16[32,7168]{1,0:T(8,128)(2,1)}, u32[]{:S(2)}, u32[]{:S(2)}) collective-permute-start(bf16[32,7168]{1,0:T(8,128)(2,1)S(1)} %constant_dynamic-update-slice_fusion.refs_0_), channel_id=1, source_target_pairs={{0,2},{1,5},{2,0},{3,7},{4,6},{5,1},{6,4},{7,3},{8,10},{9,13},{10,... | collective-permute-start | bytes 1376264 | tf_op jit(solution)/shard_map/ppermute | solution.py:57
  19.3 6.0 %collective-permute-done.3.refs_1_ = bf16[32,7168]{1,0:T(8,128)(2,1)S(1)} collective-permute-done((bf16[32,7168]{1,0:T(8,128)(2,1)S(1)}, bf16[32,7168]{1,0:T(8,128)(2,1)S(1)}, u32[]{:S(2)}, u32[]{:S(2)}) %collective-permute-start.3) | collective-permute-done | bytes 458784 | tf_op jit(solution)/shard_map/ppermute | solution.py:57
  25.4 0.7 iota_add_fusion.1
  26.1 0.8 select_reduce_fusion
  26.9 4.1 %collective-permute-done.4.refs_2_ = bf16[32,7168]{1,0:T(8,128)(2,1)} collective-permute-done((bf16[32,7168]{1,0:T(8,128)(2,1)S(1)}, bf16[32,7168]{1,0:T(8,128)(2,1)}, u32[]{:S(2)}, u32[]{:S(2)}) %collective-permute-start.4) | collective-permute-done | bytes 458784 | tf_op jit(solution)/shard_map/ppermute | solution.py:57
  31.0 9.8 %collective-permute-done.5.refs_3_ = bf16[32,7168]{1,0:T(8,128)(2,1)} collective-permute-done((bf16[32,7168]{1,0:T(8,128)(2,1)S(1)}, bf16[32,7168]{1,0:T(8,128)(2,1)}, u32[]{:S(2)}, u32[]{:S(2)}) %collective-permute-start.5) | collective-permute-done | bytes 458784 | tf_op jit(solution)/shard_map/ppermute | solution.py:57
  40.9 1.4 %collective-permute-start.6 = (bf16[32,7168]{1,0:T(8,128)(2,1)S(1)}, bf16[32,7168]{1,0:T(8,128)(2,1)}, u32[]{:S(2)}, u32[]{:S(2)}) collective-permute-start(bf16[32,7168]{1,0:T(8,128)(2,1)S(1)} %constant_dynamic-update-slice_fusion.refs_0_), channel_id=1, source_target_pairs={{0,1},{1,0},{2,3},{3,2},{4,5},{5,4},{6,7},{7,6},{8,9},{9,8},{10,11... | collective-permute-start | bytes 1376264 | tf_op jit(solution)/shard_map/ppermute | solution.py:57
  42.3 0.5 collective-permute-start.8
  42.8 0.7 broadcast_add_fusion
  43.4 1.3 %iota_compare_fusion.2 = pred[8,96]{1,0:T(8,128)(4,1)} fusion(s32[8]{0:T(128)} %param.15), kind=kLoop, calls=%fused_computation.31 | loop fusion | flops 768 | bytes 800 | tf_op jit(solution)/shard_map/lt | solution.py:45
  44.8 1.1 %compare_and_fusion = (pred[8]{0:T(512)(128)(4,1)}, s32[8]{0:T(128)S(1)}) fusion(s32[8]{0:T(128)} %param.14, s32[]{:T(128)S(6)} %mul.69), kind=kLoop, calls=%fused_computation.37 | loop fusion | flops 56 | bytes 76 | tf_op jit(solution)/shard_map/jit(_take)/and | solution.py:30
  46.0 13.9 %shard_map.122 = (bf16[32,7168]{1,0:T(8,128)(2,1)}, bf16[32,7168]{1,0:T(8,128)(2,1)}, bf16[32,7168]{1,0:T(8,128)(2,1)}, bf16[32,7168]{1,0:T(8,128)(2,1)}, bf16[3...) custom-call(bf16[32,7168]{1,0:T(8,128)(2,1)} %copy-done.2, ...), custom_call_target="tpu_custom_call" | custom-call | flops 2818572288 | bytes 18350080 | tf_op jit(solution)/shard_map/pallas_call | solution.py:105
  59.9 0.5 collective-permute-start.11
  60.5 0.6 pad_clamp_fusion
  61.0 0.7 iota_compare_fusion.1
  61.7 1.3 %collective-permute-start.14 = (bf16[8,96,576]{2,1,0:T(8,128)(2,1)S(1)}, bf16[8,96,576]{2,1,0:T(8,128)(2,1)}, u32[]{:S(2)}, u32[]{:S(2)}) collective-permute-start(bf16[8,96,576]{2,1,0:T(8,128)(2,1)S(1)} %copy-done.1), channel_id=1, source_target_pairs={{1,0},{2,1},{3,2},{4,3},{5,4},{6,5},{7,6},{8,7},{9,8},{10,9},{11,1... | collective-permute-start | bytes 2654216 | tf_op jit(solution)/shard_map/ppermute | solution.py:194
  63.0 0.7 reshape.115
  63.7 0.8 reduce_sum.29
  64.5 0.6 fusion.16
  65.1 0.8 copy.17
  65.9 0.7 copy.18
  66.7 1.1 %collective-permute-start.16 = (bf16[32,7168]{1,0:T(8,128)(2,1)}, bf16[32,7168]{1,0:T(8,128)(2,1)S(1)}, u32[]{:S(2)}, u32[]{:S(2)}) collective-permute-start(bf16[32,7168]{1,0:T(8,128)(2,1)} %get-tuple-element.34), channel_id=1, source_target_pairs={{0,1},{1,0},{2,3},{3,2},{4,5},{5,4},{6,7},{7,6},{8,9},{9,8},{10,11... | collective-permute-start | bytes 1376264 | tf_op jit(solution)/shard_map/ppermute | solution.py:57
  68.3 1.1 %add_convert_fusion.3 = bf16[32,7168]{1,0:T(8,128)(2,1)S(1)} fusion(bf16[32,7168]{1,0:T(8,128)(2,1)S(1)} %collective-permute-done.11, bf16[32,7168]{1,0:T(8,128)(2,1)} %get-tuple-element.25), kind=kLoop, calls=%fused_computation.14 | loop fusion | flops 917504 | bytes 1376256 | tf_op jit(solution)/shard_map/convert_element_type | solution.py:201
  69.5 1.6 %collective-permute-start.12 = (bf16[32,7168]{1,0:T(8,128)(2,1)S(1)}, bf16[32,7168]{1,0:T(8,128)(2,1)S(1)}, u32[]{:S(2)}, u32[]{:S(2)}) collective-permute-start(bf16[32,7168]{1,0:T(8,128)(2,1)S(1)} %add_convert_fusion.3), channel_id=1, source_target_pairs={{0,2},{1,5},{2,0},{3,7},{4,6},{5,1},{6,4},{7,3},{8,10},{9,13},{10,... | collective-permute-start | bytes 1376264 | tf_op jit(solution)/shard_map/ppermute | solution.py:57
  71.0 1.9 %add_convert_fusion = bf16[32,7168]{1,0:T(8,128)(2,1)} fusion(bf16[32,7168]{1,0:T(8,128)(2,1)S(1)} %collective-permute-done.16, bf16[32,7168]{1,0:T(8,128)(2,1)} %get-tuple-element.33), kind=kLoop, calls=%fused_computation.11 | loop fusion | flops 917504 | bytes 1376256 | tf_op jit(solution)/shard_map/convert_element_type | solution.py:201
  72.9 0.5 collective-permute-start.17
  73.5 9.8 %collective-permute-done.12 = bf16[32,7168]{1,0:T(8,128)(2,1)S(1)} collective-permute-done((bf16[32,7168]{1,0:T(8,128)(2,1)S(1)}, bf16[32,7168]{1,0:T(8,128)(2,1)S(1)}, u32[]{:S(2)}, u32[]{:S(2)}) %collective-permute-start.12) | collective-permute-done | bytes 458784 | tf_op jit(solution)/shard_map/ppermute | solution.py:57
  83.2 0.9 add_convert_fusion.2
  84.2 1.4 %collective-permute-start.18 = (bf16[32,7168]{1,0:T(8,128)(2,1)}, bf16[32,7168]{1,0:T(8,128)(2,1)}, u32[]{:S(2)}, u32[]{:S(2)}) collective-permute-start(bf16[32,7168]{1,0:T(8,128)(2,1)} %add_convert_fusion.2), channel_id=1, source_target_pairs={{0,4},{1,3},{2,6},{3,1},{4,0},{5,7},{6,2},{7,5},{8,12},{9,11},{10,... | collective-permute-start | bytes 1376264 | tf_op jit(solution)/shard_map/ppermute | solution.py:57
  85.6 3.2 %pad_maximum_fusion = bf16[24,96,576]{2,1,0:T(8,128)(2,1)} fusion(bf16[8,96,576]{2,1,0:T(8,128)(2,1)} %collective-permute-done.14, bf16[8,96,576]{2,1,0:T(8,128)(2,1)S(1)} %copy-done.1, bf16[8,96,576]{2,1,0:T(8,128)(2,1)S(1)} %collective-permute-done.13), kind=kLoop, calls=%fused_computation.2 | loop fusion | flops 2654208 | bytes 5308416 | tf_op jit(solution)/shard_map/concatenate | solution.py:29
  88.8 2.7 %gather_fusion = bf16[8,96,576]{2,1,0:T(8,128)(2,1)S(1)} fusion(bf16[24,96,576]{2,1,0:T(8,128)(2,1)} %pad_maximum_fusion, s32[1024]{0:T(1024)} %pad_clamp_fusion), kind=kCustom, calls=%fused_computation | custom fusion | bytes 1769504 | tf_op jit(solution)/shard_map/jit(_take)/gather | solution.py:30
  92.0 0.5 fusion.3
  93.0 1.5 %fusion.14 = (bf16[32,7168]{1,0:T(8,128)(2,1)S(1)}, f32[32,7168]{1,0:T(8,128)S(1)}) fusion(bf16[32,7168]{1,0:T(8,128)(2,1)} %collective-permute-done.18, bf16[32,7168]{1,0:T(8,128)(2,1)} %collective-permute-done.17, bf16[32,7168]{1,0:T(8,128)(2,1)} %collective-permute-done.15, bf16[32,7168]{1,0:T(8,128)(2,1)S(1)} %copy-done.3), kind=kLoop, calls=%fused_computation.43 | loop fusion | flops 2293760 | bytes 3211264 | tf_op jit(solution)/shard_map/convert.2
  94.6 0.7 fusion.15
  95.2 3.8 %collective-permute-start.19 = (bf16[8,7168]{1,0:T(8,128)(2,1)}, bf16[8,7168]{1,0:T(8,128)(2,1)S(1)}, u32[]{:S(2)}, u32[]{:S(2)}) collective-permute-start(bf16[8,7168]{1,0:T(8,128)(2,1)} %get-tuple-element.40), channel_id=1, source_target_pairs={{0,24},{1,25},{2,26},{3,27},{4,28},{5,29},{6,30},{7,31},{8,0},{9,1... | collective-permute-start | bytes 344072 | tf_op jit(solution)/shard_map/ppermute | solution.py:57
  99.0 1.0 collective-permute-start.20
  100.0 1.8 %convolution_convert_fusion = bf16[8,64,512]{2,1,0:T(8,128)(2,1)} fusion(bf16[8,96,576]{2,1,0:T(8,128)(2,1)S(1)} %select_select_fusion, f32[8,64]{1,0:T(8,128)S(1)} %fusion.17, f32[8,64,96]{2,1,0:T(8,128)S(1)} %fusion.3), kind=kOutput, calls=%fused_computation.3 | convolution fusion | flops 50741856 | bytes 1839104 | tf_op jit(solution)/shard_map/bhl,blc->bhc/dot_general | solution.py:49
  101.8 1.1 collective-permute-done.19
  102.9 7.9 %collective-permute-done.20 = bf16[8,7168]{1,0:T(8,128)(2,1)S(1)} collective-permute-done((bf16[8,7168]{1,0:T(8,128)(2,1)S(1)}, bf16[8,7168]{1,0:T(8,128)(2,1)S(1)}, u32[]{:S(2)}, u32[]{:S(2)}) %collective-permute-start.20) | collective-permute-done | bytes 114720 | tf_op jit(solution)/shard_map/ppermute | solution.py:57
  110.8 0.8 fusion.9
  (54 shorter events, 1.9 us)
Async XLA Ops:
  0.6 91.4 %copy-start = (bf16[8,64,576]{2,1,0:T(8,128)(2,1)S(1)}, bf16[8,64,576]{2,1,0:T(8,128)(2,1)}, u32[]{:S(2)}) copy-start(bf16[8,64,576]{2,1,0:T(8,128)(2,1)} %param.11) | copy-start | bytes 1769476
  0.6 9.4 %collective-permute-start = (bf16[8,7168]{1,0:T(8,128)(2,1)}, bf16[8,7168]{1,0:T(8,128)(2,1)S(1)}, u32[]{:S(2)}, u32[]{:S(2)}) collective-permute-start(bf16[8,7168]{1,0:T(8,128)(2,1)} %param.16), channel_id=1, source_target_pairs={{0,8},{1,9},{2,10},{3,11},{4,12},{5,13},{6,14},{7,15},{8,16},{9,17... | collective-permute-start | bytes 344072 | tf_op jit(solution)/shard_map/ppermute | solution.py:57
  3.7 10.4 %collective-permute-start.1 = (bf16[8,7168]{1,0:T(8,128)(2,1)}, bf16[8,7168]{1,0:T(8,128)(2,1)S(1)}, u32[]{:S(2)}, u32[]{:S(2)}) collective-permute-start(bf16[8,7168]{1,0:T(8,128)(2,1)} %param.16), channel_id=1, source_target_pairs={{0,16},{1,17},{2,18},{3,19},{4,20},{5,21},{6,22},{7,23},{8,24},{9,... | collective-permute-start | bytes 344072 | tf_op jit(solution)/shard_map/ppermute | solution.py:57
  6.3 7.8 %collective-permute-start.2 = (bf16[8,7168]{1,0:T(8,128)(2,1)}, bf16[8,7168]{1,0:T(8,128)(2,1)S(1)}, u32[]{:S(2)}, u32[]{:S(2)}) collective-permute-start(bf16[8,7168]{1,0:T(8,128)(2,1)} %param.16), channel_id=1, source_target_pairs={{0,24},{1,25},{2,26},{3,27},{4,28},{5,29},{6,30},{7,31},{8,0},{9,1... | collective-permute-start | bytes 344072 | tf_op jit(solution)/shard_map/ppermute | solution.py:57
  14.2 31.9 %copy-start.2 = (bf16[32,7168]{1,0:T(8,128)(2,1)}, bf16[32,7168]{1,0:T(8,128)(2,1)S(1)}, u32[]{:S(2)}) copy-start(bf16[32,7168]{1,0:T(8,128)(2,1)S(1)} %constant_dynamic-update-slice_fusion.refs_0_) | copy-start | bytes 1376260
  14.2 11.1 %collective-permute-start.3 = (bf16[32,7168]{1,0:T(8,128)(2,1)S(1)}, bf16[32,7168]{1,0:T(8,128)(2,1)S(1)}, u32[]{:S(2)}, u32[]{:S(2)}) collective-permute-start(bf16[32,7168]{1,0:T(8,128)(2,1)S(1)} %constant_dynamic-update-slice_fusion.refs_0_), channel_id=1, source_target_pairs={{0,4},{1,3},{2,6},{3,1},{4,0},{5,7},{6,2},{7,5},{8,12},{9,11},{10,... | collective-permute-start | bytes 1376264 | tf_op jit(solution)/shard_map/ppermute | solution.py:57
  15.8 68.4 %collective-permute-start.13 = (bf16[8,96,576]{2,1,0:T(8,128)(2,1)}, bf16[8,96,576]{2,1,0:T(8,128)(2,1)S(1)}, u32[]{:S(2)}, u32[]{:S(2)}) collective-permute-start(bf16[8,96,576]{2,1,0:T(8,128)(2,1)} %param.12), channel_id=1, source_target_pairs={{0,1},{1,2},{2,3},{3,4},{4,5},{5,6},{6,7},{7,8},{8,9},{9,10},{10,1... | collective-permute-start | bytes 2654216 | tf_op jit(solution)/shard_map/ppermute | solution.py:188
  17.4 13.6 %collective-permute-start.4 = (bf16[32,7168]{1,0:T(8,128)(2,1)S(1)}, bf16[32,7168]{1,0:T(8,128)(2,1)}, u32[]{:S(2)}, u32[]{:S(2)}) collective-permute-start(bf16[32,7168]{1,0:T(8,128)(2,1)S(1)} %constant_dynamic-update-slice_fusion.refs_0_), channel_id=1, source_target_pairs={{0,2},{1,5},{2,0},{3,7},{4,6},{5,1},{6,4},{7,3},{8,10},{9,13},{10,... | collective-permute-start | bytes 1376264 | tf_op jit(solution)/shard_map/ppermute | solution.py:57
  25.3 20.8 %copy-start.5 = (bf16[32,7168]{1,0:T(8,128)(2,1)}, bf16[32,7168]{1,0:T(8,128)(2,1)S(1)}, u32[]{:S(2)}) copy-start(bf16[32,7168]{1,0:T(8,128)(2,1)S(1)} %collective-permute-done.3.refs_1_) | copy-start | bytes 1376260
  25.3 15.6 %collective-permute-start.5 = (bf16[32,7168]{1,0:T(8,128)(2,1)S(1)}, bf16[32,7168]{1,0:T(8,128)(2,1)}, u32[]{:S(2)}, u32[]{:S(2)}) collective-permute-start(bf16[32,7168]{1,0:T(8,128)(2,1)S(1)} %collective-permute-done.3.refs_1_), channel_id=1, source_target_pairs={{0,2},{1,5},{2,0},{3,7},{4,6},{5,1},{6,4},{7,3},{8,10},{9,13},{10,... | collective-permute-start | bytes 1376264 | tf_op jit(solution)/shard_map/ppermute | solution.py:57
  40.9 5.0 %collective-permute-start.6 = (bf16[32,7168]{1,0:T(8,128)(2,1)S(1)}, bf16[32,7168]{1,0:T(8,128)(2,1)}, u32[]{:S(2)}, u32[]{:S(2)}) collective-permute-start(bf16[32,7168]{1,0:T(8,128)(2,1)S(1)} %constant_dynamic-update-slice_fusion.refs_0_), channel_id=1, source_target_pairs={{0,1},{1,0},{2,3},{3,2},{4,5},{5,4},{6,7},{7,6},{8,9},{9,8},{10,11... | collective-permute-start | bytes 1376264 | tf_op jit(solution)/shard_map/ppermute | solution.py:57
  42.3 3.6 %collective-permute-start.7 = (bf16[32,7168]{1,0:T(8,128)(2,1)S(1)}, bf16[32,7168]{1,0:T(8,128)(2,1)}, u32[]{:S(2)}, u32[]{:S(2)}) collective-permute-start(bf16[32,7168]{1,0:T(8,128)(2,1)S(1)} %collective-permute-done.3.refs_1_), channel_id=1, source_target_pairs={{0,1},{1,0},{2,3},{3,2},{4,5},{5,4},{6,7},{7,6},{8,9},{9,8},{10,11... | collective-permute-start | bytes 1376264 | tf_op jit(solution)/shard_map/ppermute | solution.py:57
  42.3 3.6 %collective-permute-start.8 = (bf16[32,7168]{1,0:T(8,128)(2,1)}, bf16[32,7168]{1,0:T(8,128)(2,1)}, u32[]{:S(2)}, u32[]{:S(2)}) collective-permute-start(bf16[32,7168]{1,0:T(8,128)(2,1)} %collective-permute-done.4.refs_2_), channel_id=1, source_target_pairs={{0,1},{1,0},{2,3},{3,2},{4,5},{5,4},{6,7},{7,6},{8,9},{9,8},{10,11... | collective-permute-start | bytes 1376264 | tf_op jit(solution)/shard_map/ppermute | solution.py:57
  42.8 3.2 %collective-permute-start.9 = (bf16[32,7168]{1,0:T(8,128)(2,1)}, bf16[32,7168]{1,0:T(8,128)(2,1)}, u32[]{:S(2)}, u32[]{:S(2)}) collective-permute-start(bf16[32,7168]{1,0:T(8,128)(2,1)} %collective-permute-done.5.refs_3_), channel_id=1, source_target_pairs={{0,1},{1,0},{2,3},{3,2},{4,5},{5,4},{6,7},{7,6},{8,9},{9,8},{10,11... | collective-permute-start | bytes 1376264 | tf_op jit(solution)/shard_map/ppermute | solution.py:57
  45.9 15.8 %copy-start.1 = (bf16[8,96,576]{2,1,0:T(8,128)(2,1)S(1)}, bf16[8,96,576]{2,1,0:T(8,128)(2,1)}, u32[]{:S(2)}) copy-start(bf16[8,96,576]{2,1,0:T(8,128)(2,1)} %param.12) | copy-start | bytes 2654212
  59.9 23.3 %copy-start.4 = (bf16[32,7168]{1,0:T(8,128)(2,1)S(1)}, bf16[32,7168]{1,0:T(8,128)(2,1)}, u32[]{:S(2)}) copy-start(bf16[32,7168]{1,0:T(8,128)(2,1)} %get-tuple-element.23) | copy-start | bytes 1376260
  59.9 7.9 %collective-permute-start.11 = (bf16[32,7168]{1,0:T(8,128)(2,1)}, bf16[32,7168]{1,0:T(8,128)(2,1)S(1)}, u32[]{:S(2)}, u32[]{:S(2)}) collective-permute-start(bf16[32,7168]{1,0:T(8,128)(2,1)} %get-tuple-element.26), channel_id=1, source_target_pairs={{0,1},{1,0},{2,3},{3,2},{4,5},{5,4},{6,7},{7,6},{8,9},{9,8},{10,11... | collective-permute-start | bytes 1376264 | tf_op jit(solution)/shard_map/ppermute | solution.py:57
  61.7 22.4 %collective-permute-start.14 = (bf16[8,96,576]{2,1,0:T(8,128)(2,1)S(1)}, bf16[8,96,576]{2,1,0:T(8,128)(2,1)}, u32[]{:S(2)}, u32[]{:S(2)}) collective-permute-start(bf16[8,96,576]{2,1,0:T(8,128)(2,1)S(1)} %copy-done.1), channel_id=1, source_target_pairs={{1,0},{2,1},{3,2},{4,3},{5,4},{6,5},{7,6},{8,7},{9,8},{10,9},{11,1... | collective-permute-start | bytes 2654216 | tf_op jit(solution)/shard_map/ppermute | solution.py:194
  66.7 2.8 %collective-permute-start.16 = (bf16[32,7168]{1,0:T(8,128)(2,1)}, bf16[32,7168]{1,0:T(8,128)(2,1)S(1)}, u32[]{:S(2)}, u32[]{:S(2)}) collective-permute-start(bf16[32,7168]{1,0:T(8,128)(2,1)} %get-tuple-element.34), channel_id=1, source_target_pairs={{0,1},{1,0},{2,3},{3,2},{4,5},{5,4},{6,7},{7,6},{8,9},{9,8},{10,11... | collective-permute-start | bytes 1376264 | tf_op jit(solution)/shard_map/ppermute | solution.py:57
  67.8 5.1 %collective-permute-start.10 = (bf16[32,7168]{1,0:T(8,128)(2,1)}, bf16[32,7168]{1,0:T(8,128)(2,1)S(1)}, u32[]{:S(2)}, u32[]{:S(2)}) collective-permute-start(bf16[32,7168]{1,0:T(8,128)(2,1)} %get-tuple-element.24), channel_id=1, source_target_pairs={{0,1},{1,0},{2,3},{3,2},{4,5},{5,4},{6,7},{7,6},{8,9},{9,8},{10,11... | collective-permute-start | bytes 1376264 | tf_op jit(solution)/shard_map/ppermute | solution.py:57
  67.8 25.0 %collective-permute-start.15 = (bf16[32,7168]{1,0:T(8,128)(2,1)}, bf16[32,7168]{1,0:T(8,128)(2,1)}, u32[]{:S(2)}, u32[]{:S(2)}) collective-permute-start(bf16[32,7168]{1,0:T(8,128)(2,1)} %get-tuple-element.32), channel_id=1, source_target_pairs={{0,1},{1,0},{2,3},{3,2},{4,5},{5,4},{6,7},{7,6},{8,9},{9,8},{10,11... | collective-permute-start | bytes 1376264 | tf_op jit(solution)/shard_map/ppermute | solution.py:57
  69.5 13.7 %collective-permute-start.12 = (bf16[32,7168]{1,0:T(8,128)(2,1)S(1)}, bf16[32,7168]{1,0:T(8,128)(2,1)S(1)}, u32[]{:S(2)}, u32[]{:S(2)}) collective-permute-start(bf16[32,7168]{1,0:T(8,128)(2,1)S(1)} %add_convert_fusion.3), channel_id=1, source_target_pairs={{0,2},{1,5},{2,0},{3,7},{4,6},{5,1},{6,4},{7,3},{8,10},{9,13},{10,... | collective-permute-start | bytes 1376264 | tf_op jit(solution)/shard_map/ppermute | solution.py:57
  72.9 19.9 %collective-permute-start.17 = (bf16[32,7168]{1,0:T(8,128)(2,1)}, bf16[32,7168]{1,0:T(8,128)(2,1)}, u32[]{:S(2)}, u32[]{:S(2)}) collective-permute-start(bf16[32,7168]{1,0:T(8,128)(2,1)} %add_convert_fusion), channel_id=1, source_target_pairs={{0,2},{1,5},{2,0},{3,7},{4,6},{5,1},{6,4},{7,3},{8,10},{9,13},{10,... | collective-permute-start | bytes 1376264 | tf_op jit(solution)/shard_map/ppermute | solution.py:57
  84.1 7.5 %copy-start.6 = (bf16[8,576]{1,0:T(8,128)(2,1)S(1)}, bf16[8,576]{1,0:T(8,128)(2,1)}, u32[]{:S(2)}) copy-start(bf16[8,576]{1,0:T(8,128)(2,1)} %param.13) | copy-start | bytes 27652
  84.1 7.5 %copy-start.7 = (pred[8,96]{1,0:T(8,128)(4,1)S(1)}, pred[8,96]{1,0:T(8,128)(4,1)}, u32[]{:S(2)}) copy-start(pred[8,96]{1,0:T(8,128)(4,1)} %get-tuple-element.47) | copy-start | bytes 2308
  84.1 7.5 %copy-start.8 = (pred[8,96]{1,0:T(8,128)(4,1)S(1)}, pred[8,96]{1,0:T(8,128)(4,1)}, u32[]{:S(2)}) copy-start(pred[8,96]{1,0:T(8,128)(4,1)} %get-tuple-element.48) | copy-start | bytes 2308
  84.1 7.5 %copy-start.9 = (pred[8]{0:T(512)(128)(4,1)S(1)}, pred[8]{0:T(512)(128)(4,1)}, u32[]{:S(2)}) copy-start(pred[8]{0:T(512)(128)(4,1)} %get-tuple-element.38) | copy-start | bytes 28
  84.2 8.9 %collective-permute-start.18 = (bf16[32,7168]{1,0:T(8,128)(2,1)}, bf16[32,7168]{1,0:T(8,128)(2,1)}, u32[]{:S(2)}, u32[]{:S(2)}) collective-permute-start(bf16[32,7168]{1,0:T(8,128)(2,1)} %add_convert_fusion.2), channel_id=1, source_target_pairs={{0,4},{1,3},{2,6},{3,1},{4,0},{5,7},{6,2},{7,5},{8,12},{9,11},{10,... | collective-permute-start | bytes 1376264 | tf_op jit(solution)/shard_map/ppermute | solution.py:57
  88.8 3.2 %copy-start.11 = (pred[8,96]{1,0:T(8,128)(4,1)S(1)}, pred[8,96]{1,0:T(8,128)(4,1)}, u32[]{:S(2)}) copy-start(pred[8,96]{1,0:T(8,128)(4,1)} %iota_compare_fusion.2) | copy-start | bytes 2308
  88.8 4.2 %copy-start.3 = (bf16[32,7168]{1,0:T(8,128)(2,1)S(1)}, bf16[32,7168]{1,0:T(8,128)(2,1)}, u32[]{:S(2)}) copy-start(bf16[32,7168]{1,0:T(8,128)(2,1)} %get-tuple-element.31) | copy-start | bytes 1376260
  92.8 18.0 %copy-start.10 = (f32[8,1]{0,1:T(1,128)S(1)}, f32[8,1]{0,1:T(1,128)}, u32[]{:S(2)}) copy-start(f32[8,1]{0,1:T(1,128)} %copy.18) | copy-start | bytes 100
  95.2 7.7 %collective-permute-start.19 = (bf16[8,7168]{1,0:T(8,128)(2,1)}, bf16[8,7168]{1,0:T(8,128)(2,1)S(1)}, u32[]{:S(2)}, u32[]{:S(2)}) collective-permute-start(bf16[8,7168]{1,0:T(8,128)(2,1)} %get-tuple-element.40), channel_id=1, source_target_pairs={{0,24},{1,25},{2,26},{3,27},{4,28},{5,29},{6,30},{7,31},{8,0},{9,1... | collective-permute-start | bytes 344072 | tf_op jit(solution)/shard_map/ppermute | solution.py:57
  99.0 11.8 %collective-permute-start.20 = (bf16[8,7168]{1,0:T(8,128)(2,1)S(1)}, bf16[8,7168]{1,0:T(8,128)(2,1)S(1)}, u32[]{:S(2)}, u32[]{:S(2)}) collective-permute-start(bf16[8,7168]{1,0:T(8,128)(2,1)S(1)} %get-tuple-element.42), channel_id=1, source_target_pairs={{0,16},{1,17},{2,18},{3,19},{4,20},{5,21},{6,22},{7,23},{8,24},{9,... | collective-permute-start | bytes 344072 | tf_op jit(solution)/shard_map/ppermute | solution.py:57
  100.0 10.8 %collective-permute-start.21 = (bf16[8,7168]{1,0:T(8,128)(2,1)S(1)}, bf16[8,7168]{1,0:T(8,128)(2,1)S(1)}, u32[]{:S(2)}, u32[]{:S(2)}) collective-permute-start(bf16[8,7168]{1,0:T(8,128)(2,1)S(1)} %get-tuple-element.41), channel_id=1, source_target_pairs={{0,8},{1,9},{2,10},{3,11},{4,12},{5,13},{6,14},{7,15},{8,16},{9,17... | collective-permute-start | bytes 344072 | tf_op jit(solution)/shard_map/ppermute | solution.py:57

commit v5 on v4

v5 whole, which is shorter than its diff:
```python
import jax
import jax.numpy as jnp
from jax import lax
from jax.experimental import pallas as pl
from jax.experimental.pallas import tpu as pltpu
from jax.sharding import PartitionSpec as P

FF_E = 2048
KV = 512


score_scale = 192.0 ** (-0.5)


def pair_slots(route_rows, expert_count, capacity):
    flat_experts = route_rows.reshape(-1)
    onehot = (flat_experts[:, None] == jnp.arange(expert_count, dtype=jnp.int32)[None, :]).astype(
        jnp.int32
    )
    position = jnp.sum((jnp.cumsum(onehot, axis=0) - onehot) * onehot, axis=1)
    return (flat_experts * capacity + position).astype(jnp.int32).reshape(route_rows.shape)


def swapped(value, partner):
    peers = lax.axis_size("dp")
    return lax.ppermute(value, "dp", [(i, partner(i)) for i in range(peers)])


def added(values):
    total = values[0].astype(jnp.float32)
    for value in values[1:]:
        total = total + value.astype(jnp.float32)
    return total


EARLY = ((1, 2), (3, 4), (5, 6), (6, 5))
LATE = ((2, 1), (4, 3), (7, 8), (8, 7))


def neighbours(value, moves, slices):
    peers = lax.axis_size("dp")
    pairs = [(base + i, base + j) for base in range(0, peers, slices) for i, j in moves]
    return lax.ppermute(value, "dp", [p for p in pairs if max(p) < peers])


def attend_kernel(parents, lengths, query, own, twin, early, late, newest, out):
    beam_count = parents.shape[0]
    beam = pl.program_id(0)
    rank = lax.axis_index("dp")
    holder = parents[beam] // beam_count
    length = lengths[beam]
    place = rank % 8
    arrives_early = (place == 2) | (place == 4) | (place == 5) | (place == 6)
    rows = jnp.where(arrives_early, early[0], late[0])
    rows = jnp.where(holder == (rank ^ 1), twin[0], rows)
    rows = jnp.where(holder == rank, own[0], rows)
    at = lax.broadcasted_iota(jnp.int32, rows.shape, 0)
    rows = jnp.where(at < length - 1, rows, jnp.zeros_like(rows))
    rows = jnp.where(at == length - 1, newest[0], rows)
    scores = lax.dot_general(
        query[0], rows, (((1,), (1,)), ((), ())), preferred_element_type=jnp.float32
    )
    scores = scores * score_scale
    at = lax.broadcasted_iota(jnp.int32, scores.shape, 1)
    scores = jnp.where(at < length, scores, -jnp.inf)
    expons = jnp.exp(scores - jnp.max(scores, axis=1, keepdims=True))
    probs = (expons / jnp.sum(expons, axis=1, keepdims=True)).astype(jnp.bfloat16)
    mixed = jnp.dot(probs, rows[:, :KV], preferred_element_type=jnp.float32)
    out[0] = mixed.astype(out.dtype)


def attend(queries, own, twin, early, late, new_latent, parents, lengths):
    beam_count, heads, width = queries.shape
    positions = own.shape[1]

    def chosen(b, parents, lengths):
        return (parents[b] % beam_count, 0, 0)

    def each(b, parents, lengths):
        return (b, 0, 0)

    return pl.pallas_call(
        attend_kernel,
        grid_spec=pltpu.PrefetchScalarGridSpec(
            num_scalar_prefetch=2,
            grid=(beam_count,),
            in_specs=[pl.BlockSpec((1, heads, width), each)]
            + [pl.BlockSpec((1, positions, width), chosen)] * 4
            + [pl.BlockSpec((1, 1, width), each)],
            out_specs=pl.BlockSpec((1, heads, KV), each),
        ),
        out_shape=jax.ShapeDtypeStruct((beam_count, heads, KV), jnp.bfloat16),
        cost_estimate=pl.CostEstimate(
            flops=2 * beam_count * heads * positions * (width + KV),
            bytes_accessed=2 * beam_count * (4 * positions * width + heads * (width + KV)),
            transcendentals=beam_count * heads * positions,
        ),
    )(parents, lengths, queries, own, twin, early, late, new_latent[:, None, :])


def expert_kernel(wide, *refs):
    rows, refs = refs[:8], refs[8:]
    gate_hbm, up_hbm, down_hbm, own_hbm, high_hbm, low_hbm = refs[:6]
    value, gate, up, down, part, gate_sum, up_sum, row_sem, weight_sem, out_sem = refs[6:]
    height, width = rows[0].shape
    steps = width // wide
    half = 4 * height

    def row_copy(i):
        return pltpu.make_async_copy(
            rows[i], value.at[pl.ds(i * height, height), :], row_sem.at[i]
        )

    def span(k):
        return pl.ds(pl.multiple_of(k * wide, wide), wide)

    def inward(which, k):
        hbm, ref = ((gate_hbm, gate), (up_hbm, up))[which]
        return pltpu.make_async_copy(
            hbm.at[0, span(k), :], ref.at[span(k), :], weight_sem.at[which, k]
        )

    def onward(k):
        return pltpu.make_async_copy(
            down_hbm.at[0, :, span(k)], down.at[:, span(k)], weight_sem.at[2, k]
        )

    def outward(which, k):
        hbm, first, count = (
            (own_hbm, 0, half),
            (high_hbm, half + 2 * height, 2 * height),
            (low_hbm, half, 2 * height),
        )[which]
        return pltpu.make_async_copy(
            part.at[pl.ds(first, count), span(k)], hbm.at[:, span(k)], out_sem.at[which, k]
        )

    for i in range(8):
        row_copy(i).start()
    for k in range(steps):
        inward(0, k).start()
        inward(1, k).start()
    for k in range(steps):
        onward(k).start()
    for i in range(8):
        row_copy(i).wait()
    gate_sum[...] = jnp.zeros_like(gate_sum)
    up_sum[...] = jnp.zeros_like(up_sum)

    @pl.loop(0, steps)
    def _(k):
        inward(0, k).wait()
        inward(1, k).wait()
        piece = value[:, span(k)]
        gate_sum[...] += jnp.dot(piece, gate[span(k), :], preferred_element_type=jnp.float32)
        up_sum[...] += jnp.dot(piece, up[span(k), :], preferred_element_type=jnp.float32)

    total = gate_sum[...]
    hidden = (total / (1.0 + jnp.exp(-total)) * up_sum[...]).astype(jnp.bfloat16)

    @pl.loop(0, steps)
    def _(k):
        onward(k).wait()
        product = jnp.dot(hidden, down[:, span(k)], preferred_element_type=jnp.float32)
        part[:, span(k)] = product.astype(part.dtype)
        for which in range(3):
            outward(which, k).start()

    @pl.loop(0, steps)
    def _(k):
        for which in range(3):
            outward(which, k).wait()


def experts(rows, gate_weight, up_weight, down_weight):
    height, width = rows[0].shape
    units = gate_weight.shape[2]
    wide = max(w for w in (128, 256, 512, 1024) if width % w == 0)
    total = len(rows) * height
    return pl.pallas_call(
        lambda *refs: expert_kernel(wide, *refs),
        in_specs=[pl.BlockSpec(memory_space=pl.ANY)] * (len(rows) + 3),
        out_specs=[pl.BlockSpec(memory_space=pl.ANY)] * 3,
        out_shape=[
            jax.ShapeDtypeStruct((count * height, width), jnp.bfloat16) for count in (4, 2, 2)
        ],
        scratch_shapes=[
            pltpu.VMEM((total, width), jnp.bfloat16),
            pltpu.VMEM((width, units), jnp.bfloat16),
            pltpu.VMEM((width, units), jnp.bfloat16),
            pltpu.VMEM((units, width), jnp.bfloat16),
            pltpu.VMEM((total, width), jnp.bfloat16),
            pltpu.VMEM((total, units), jnp.float32),
            pltpu.VMEM((total, units), jnp.float32),
            pltpu.SemaphoreType.DMA((len(rows),)),
            pltpu.SemaphoreType.DMA((3, width // wide)),
            pltpu.SemaphoreType.DMA((3, width // wide)),
        ],
        compiler_params=pltpu.CompilerParams(vmem_limit_bytes=60 * 2**20),
        cost_estimate=pl.CostEstimate(
            flops=6 * total * width * units,
            bytes_accessed=6 * width * units + 4 * total * width,
            transcendentals=total * units,
        ),
    )(*rows, gate_weight, up_weight, down_weight)


def mix_kernel(expert_count, slices, routes, scales, *refs):
    values, out = refs[:-1], refs[-1]
    top, beam_count = routes.shape
    mine = lax.axis_index("dp") // slices
    at = lax.broadcasted_iota(jnp.int32, (beam_count, 1), 0)
    total = jnp.zeros(out.shape, jnp.float32)
    for r, value in enumerate(values):
        expert = (mine + r) % expert_count
        column = jnp.zeros((beam_count, 1), jnp.float32)
        for b in range(beam_count):
            scale = 0.0
            for k in range(top):
                scale = scale + jnp.where(routes[k, b] == expert, scales[k, b], 0.0)
            column = jnp.where(at == b, scale, column)
        total = total + column * value[...].astype(jnp.float32)
    out[...] = total.astype(out.dtype)


def mixed_rows(values, routed_experts, route_weights, expert_count, slices):
    scalars = pl.BlockSpec(memory_space=pltpu.SMEM)
    whole = pl.BlockSpec(memory_space=pltpu.VMEM)
    return pl.pallas_call(
        lambda *refs: mix_kernel(expert_count, slices, *refs),
        in_specs=[scalars, scalars] + [whole] * len(values),
        out_specs=whole,
        out_shape=jax.ShapeDtypeStruct(values[0].shape, jnp.bfloat16),
        cost_estimate=pl.CostEstimate(
            flops=2 * len(values) * values[0].size,
            bytes_accessed=2 * (len(values) + 2) * values[0].size,
            transcendentals=0,
        ),
    )(routed_experts.T, route_weights.T, *values)


def body(
    queries,
    latent_cache,
    new_latent,
    parents,
    lengths,
    expert_input,
    routed_experts,
    route_weights,
    gate_weight,
    up_weight,
    down_weight,
):
    beam_count, width = expert_input.shape
    devices = lax.axis_size("dp")
    slices = FF_E // gate_weight.shape[2]
    expert_count = devices // slices
    route_count = routed_experts.shape[1]
    capacity = min(beam_count, max(2, 2 * beam_count * route_count // expert_count))
    dense = capacity == beam_count
    assert slices == 8

    if dense:
        blocks = [expert_input] * expert_count
    else:
        mine = lax.axis_index("dp") // slices
        turns = jnp.arange(expert_count, dtype=jnp.int32)
        targets = (mine + turns) % expert_count
        slots = pair_slots(routed_experts, expert_count, capacity)
        wanted = targets[:, None] * capacity + jnp.arange(capacity, dtype=jnp.int32)
        matches = (slots[:, :, None] == wanted.reshape(-1)).astype(jnp.float32)
        mixing = jnp.sum(route_weights[:, :, None] * matches, axis=1)
        selector = jnp.sum(matches, axis=1).T.astype(jnp.bfloat16)
        chosen = jnp.dot(selector, expert_input, preferred_element_type=jnp.float32)
        blocks = list(chosen.astype(jnp.bfloat16).reshape(expert_count, capacity, width))

    def ahead(r):
        return lambda i: (i + r * slices) % devices

    def twin(i):
        return i ^ 1

    def first(i):
        return i ^ (2 if i & 1 else 4)

    def second(i):
        return i ^ (4 if i & 1 else 2)

    blocks = blocks[:1] + [swapped(blocks[r], ahead(r)) for r in range(1, expert_count)]
    early = neighbours(latent_cache, EARLY, slices)
    *blocks, early = lax.optimization_barrier((*blocks, early))
    column = jnp.concatenate(blocks)
    near = swapped(column, first)
    side = swapped(column, second)
    across = swapped(near, second)
    beside = swapped(latent_cache, twin)
    held = [column, near, side, across]
    *held, latent_cache = lax.optimization_barrier((*held, latent_cache))
    late = neighbours(latent_cache, LATE, slices)
    held = held + [swapped(value, twin) for value in held]
    own, high, low = experts(held, gate_weight, up_weight, down_weight)

    high, low = swapped(high, twin), swapped(low, twin)
    height = expert_count * capacity

    def block(value, j):
        return lax.slice_in_dim(value, j * height, (j + 1) * height)

    across = swapped(added([block(own, 3), block(high, 1)]).astype(jnp.bfloat16), second)
    side = swapped(added([block(own, 2), block(high, 0)]).astype(jnp.bfloat16), second)
    near = added([block(own, 1), block(low, 1), across]).astype(jnp.bfloat16)
    near, early, late = lax.optimization_barrier((near, early, late))
    near = swapped(near, first)
    here = [own, low, side, near]

    def share(r):
        return added([v[r * capacity : (r + 1) * capacity] for v in here])

    values = [swapped(share(r).astype(jnp.bfloat16), ahead(-r)) for r in range(1, expert_count)]
    values = [share(0)] + values
    if dense:
        expert_output = mixed_rows(values, routed_experts, route_weights, expert_count, slices)
    else:
        expert_output = jnp.dot(
            mixing,
            jnp.concatenate([v.astype(jnp.float32) for v in values]),
            precision=lax.Precision.HIGHEST,
            preferred_element_type=jnp.float32,
        ).astype(jnp.bfloat16)
    attention = attend(
        queries, latent_cache, beside, early, late, new_latent, parents, lengths
    )
    return (attention, expert_output)


def solution(mesh):
    in_specs = (
        P(("groups", "dp"), None, None),
        P(("groups", "dp"), None, None),
        P(("groups", "dp"), None),
        P(("groups", "dp")),
        P(("groups", "dp")),
        P(("groups", "dp"), None),
        P(("groups", "dp"), None),
        P(("groups", "dp"), None),
        P("dp", None, None),
        P("dp", None, None),
        P("dp", None, None),
    )
    out_specs = (P(("groups", "dp"), None, None), P(("groups", "dp"), None))
    return jax.shard_map(body, mesh=mesh, in_specs=in_specs, out_specs=out_specs, check_vma=False)
```

time: 112 us -> 111 us (level)
  other arithmetic: 16.8 us -> 2.45 us
  Pallas kernels: 13.9 us -> 22.1 us
  starting transfers between devices: 25.7 us -> 33.8 us
  local copies, waits for them, and re-layouts: 7.38 us -> 4.24 us
  waiting for transfers between devices: 44.6 us -> 47.3 us
  matrix products: 2.33 us -> 0 us
    ppermute x20 -> x19, starting transfers between devices: 22.9 us -> 32.3 us  [swapped(): return lax.ppermute(value, 'dp', [(i, partner(i)) for i in range(peers)])]
    pallas_call x1 -> x3, Pallas kernels: 13.9 us -> 22.1 us  [the longest x1 11.7 us: experts(): pl.pallas_call(lambda *refs: expert_kernel(wide, *refs), in_specs=[pl.Blo...]
    concatenate x1 -> x0, other arithmetic: 3.24 us -> none  [attend(): padded = jnp.concatenate([before, latent_cache, after], axis=0)]
    ppermute x20 -> x19, waiting for transfers between devices: 44.6 us -> 47.3 us  [swapped(): return lax.ppermute(value, 'dp', [(i, partner(i)) for i in range(peers)])]
    gather x1 -> x0, local copies, waits for them, and re-layouts: 2.73 us -> none  [attend(): parent_rows = jnp.take(padded, parents - first_slot, axis=0)]
    dot_general x2 -> x0, matrix products: 2.33 us -> none  [the longest x1 1.82 us: attend(): jnp.einsum('bhl,blc->bhc', probs, child_cache[:, :, :KV], preferred_eleme...]
    convert_element_type x4 -> x3, other arithmetic: 4.75 us -> 2.45 us  [the longest x1 1.37 us: body(): added([block(own, 2), block(high, 0)]).astype(jnp.bfloat16)]
    reduce_sum x2 -> x0, other arithmetic: 1.55 us -> none  [the longest x1 0.8 us: body(): jnp.sum(mixing.reshape(beam_count, expert_count, capacity), axis=2)]
  transfers between devices with their start and end apart: 22 -> 21, of which waited for: 10 -> 13; matrix products, arithmetic and copies ran while one was open for 21% -> 3% of each run, Pallas kernels for 12% -> 8%
where the time goes in v5:
time: 111 us
  waiting for transfers between devices  47.3 us (43%)
  starting transfers between devices  33.8 us (30%)
  Pallas kernels  22.1 us (20%)
  local copies, waits for them, and re-layouts  4.24 us (4%)
  other arithmetic  2.45 us (2%)
    ppermute x19, waiting for transfers between devices, swapped(): return lax.ppermute(value, 'dp', [(i, partner(i)) for i in range(peers)])  47.3 us
    ppermute x19, starting transfers between devices, swapped(): return lax.ppermute(value, 'dp', [(i, partner(i)) for i in range(peers)])  32.3 us
    pallas_call x1, Pallas kernels, experts(): pl.pallas_call(lambda *refs: expert_kernel(wide, *refs), in_specs=[pl.Blo...  11.7 us
    pallas_call x1, Pallas kernels, attend(): pl.pallas_call(attend_kernel, grid_spec=pltpu.PrefetchScalarGridSpec(num_...  8.53 us
    unnamed x33, local copies, waits for them, and re-layouts  3.61 us
  transfers between devices with their start and end apart: 21, of which 13 were waited for; matrix products, arithmetic and copies ran while one was open for 3% of the time, Pallas kernels for 8%

profile of v5, /device:TPU:0, one launch (start us, length us, event | category | flops | bytes accessed | tf_op | source)
XLA Modules:
  0.0 110.7 jit_solution(9420437813273550314)
XLA Ops:
  0.6 0.7 collective-permute-start.3
  1.4 3.1 %collective-permute-start = (bf16[8,7168]{1,0:T(8,128)(2,1)}, bf16[8,7168]{1,0:T(8,128)(2,1)S(1)}, u32[]{:S(2)}, u32[]{:S(2)}) collective-permute-start(bf16[8,7168]{1,0:T(8,128)(2,1)} %param.16), channel_id=1, source_target_pairs={{0,8},{1,9},{2,10},{3,11},{4,12},{5,13},{6,14},{7,15},{8,16},{9,17... | collective-permute-start | bytes 344072 | tf_op jit(solution)/shard_map/ppermute | solution.py:26
  4.4 2.6 %collective-permute-start.1 = (bf16[8,7168]{1,0:T(8,128)(2,1)}, bf16[8,7168]{1,0:T(8,128)(2,1)S(1)}, u32[]{:S(2)}, u32[]{:S(2)}) collective-permute-start(bf16[8,7168]{1,0:T(8,128)(2,1)} %param.16), channel_id=1, source_target_pairs={{0,16},{1,17},{2,18},{3,19},{4,20},{5,21},{6,22},{7,23},{8,24},{9,... | collective-permute-start | bytes 344072 | tf_op jit(solution)/shard_map/ppermute | solution.py:26
  7.0 1.3 %collective-permute-start.2 = (bf16[8,7168]{1,0:T(8,128)(2,1)}, bf16[8,7168]{1,0:T(8,128)(2,1)S(1)}, u32[]{:S(2)}, u32[]{:S(2)}) collective-permute-start(bf16[8,7168]{1,0:T(8,128)(2,1)} %param.16), channel_id=1, source_target_pairs={{0,24},{1,25},{2,26},{3,27},{4,28},{5,29},{6,30},{7,31},{8,0},{9,1... | collective-permute-start | bytes 344072 | tf_op jit(solution)/shard_map/ppermute | solution.py:26
  8.4 1.1 collective-permute-done
  9.5 4.7 %collective-permute-done.1 = bf16[8,7168]{1,0:T(8,128)(2,1)S(1)} collective-permute-done((bf16[8,7168]{1,0:T(8,128)(2,1)}, bf16[8,7168]{1,0:T(8,128)(2,1)S(1)}, u32[]{:S(2)}, u32[]{:S(2)}) %collective-permute-start.1) | collective-permute-done | bytes 114720 | tf_op jit(solution)/shard_map/ppermute | solution.py:26
  14.1 0.4 collective-permute-done.2
  14.6 1.0 constant_dynamic-update-slice_fusion.3
  15.6 0.0 copy-start.5
  15.6 5.6 %collective-permute-start.4 = (bf16[32,7168]{1,0:T(8,128)(2,1)S(1)}, bf16[32,7168]{1,0:T(8,128)(2,1)S(1)}, u32[]{:S(2)}, u32[]{:S(2)}) collective-permute-start(bf16[32,7168]{1,0:T(8,128)(2,1)S(1)} %constant_dynamic-update-slice_fusion.refs_0_), channel_id=1, source_target_pairs={{0,4},{1,3},{2,6},{3,1},{4,0},{5,7},{6,2},{7,5},{8,12},{9,11},{10,... | collective-permute-start | bytes 1376264 | tf_op jit(solution)/shard_map/ppermute | solution.py:26
  21.3 0.6 collective-permute-start.5
  21.8 9.9 %collective-permute-done.4.refs_1_ = bf16[32,7168]{1,0:T(8,128)(2,1)S(1)} collective-permute-done((bf16[32,7168]{1,0:T(8,128)(2,1)S(1)}, bf16[32,7168]{1,0:T(8,128)(2,1)S(1)}, u32[]{:S(2)}, u32[]{:S(2)}) %collective-permute-start.4) | collective-permute-done | bytes 458784 | tf_op jit(solution)/shard_map/ppermute | solution.py:26
  31.7 2.0 %collective-permute-start.6 = (bf16[32,7168]{1,0:T(8,128)(2,1)S(1)}, bf16[32,7168]{1,0:T(8,128)(2,1)S(1)}, u32[]{:S(2)}, u32[]{:S(2)}) collective-permute-start(bf16[32,7168]{1,0:T(8,128)(2,1)S(1)} %collective-permute-done.4.refs_1_), channel_id=1, source_target_pairs={{0,2},{1,5},{2,0},{3,7},{4,6},{5,1},{6,4},{7,3},{8,10},{9,13},{10,... | collective-permute-start | bytes 1376264 | tf_op jit(solution)/shard_map/ppermute | solution.py:26
  33.7 6.5 %collective-permute-done.6.refs_3_ = bf16[32,7168]{1,0:T(8,128)(2,1)S(1)} collective-permute-done((bf16[32,7168]{1,0:T(8,128)(2,1)S(1)}, bf16[32,7168]{1,0:T(8,128)(2,1)S(1)}, u32[]{:S(2)}, u32[]{:S(2)}) %collective-permute-start.6) | collective-permute-done | bytes 458784 | tf_op jit(solution)/shard_map/ppermute | solution.py:26
  40.2 0.5 collective-permute-start.11
  40.7 0.0 collective-permute-start.8
  40.7 0.5 collective-permute-start.9
  41.2 0.8 collective-permute-done.10.refs_6_
  42.0 1.3 %collective-permute-done.11.refs_7_ = bf16[32,7168]{1,0:T(8,128)(2,1)S(1)} collective-permute-done((bf16[32,7168]{1,0:T(8,128)(2,1)S(1)}, bf16[32,7168]{1,0:T(8,128)(2,1)S(1)}, u32[]{:S(2)}, u32[]{:S(2)}) %collective-permute-start.11) | collective-permute-done | bytes 458784 | tf_op jit(solution)/shard_map/ppermute | solution.py:26
  43.3 0.7 collective-permute-done.8.refs_4_
  44.0 0.2 copy-done.10
  44.1 0.8 copy-done.11
  44.9 0.0 copy-start.1
  45.0 11.7 %shard_map.122 = (bf16[128,7168]{1,0:T(8,128)(2,1)}, bf16[64,7168]{1,0:T(8,128)(2,1)}, bf16[64,7168]{1,0:T(8,128)(2,1)}) custom-call(bf16[32,7168]{1,0:T(8,128)(2,1)} %copy-done.5, bf16[32,7168]{1,0:T(8,128)(2,1)} %copy-done.6, bf16[32,7168]{1,0:T(8,128)(2,1)} %copy-done.7, bf16[32,7168]{1,0:T(8,128)(2,1)} %copy-done.8, bf16[32,7168]{1,0:T(8,128)(2,1)} %copy-done.11, ...), custom_call_target="tpu_custom_call" | custom-call | flops 2818572288 | bytes 18350080 | tf_op jit(solution)/shard_map/pallas_call | solution.py:180
  56.7 0.2 collective-permute-start.13
  56.9 0.4 collective-permute-start.12
  57.2 2.2 %collective-permute-done.13 = bf16[64,7168]{1,0:T(8,128)(2,1)S(1)} collective-permute-done((bf16[64,7168]{1,0:T(8,128)(2,1)}, bf16[64,7168]{1,0:T(8,128)(2,1)S(1)}, u32[]{:S(2)}, u32[]{:S(2)}) %collective-permute-start.13) | collective-permute-done | bytes 917536 | tf_op jit(solution)/shard_map/ppermute | solution.py:26
  59.4 1.4 %add_convert_fusion = (bf16[32,7168]{1,0:T(8,128)(2,1)S(1)}, bf16[32,7168]{1,0:T(8,128)(2,1)S(1)}) fusion(bf16[64,7168]{1,0:T(8,128)(2,1)S(1)} %collective-permute-done.13, bf16[128,7168]{1,0:T(8,128)(2,1)} %get-tuple-element.27), kind=kLoop, calls=%fused_computation | loop fusion | flops 1835008 | bytes 2752512 | tf_op jit(solution)/shard_map/convert_element_type | solution.py:311
  60.8 2.0 %collective-permute-start.14 = (bf16[32,7168]{1,0:T(8,128)(2,1)S(1)}, bf16[32,7168]{1,0:T(8,128)(2,1)S(1)}, u32[]{:S(2)}, u32[]{:S(2)}) collective-permute-start(bf16[32,7168]{1,0:T(8,128)(2,1)S(1)} %get-tuple-element.39), channel_id=1, source_target_pairs={{0,2},{1,5},{2,0},{3,7},{4,6},{5,1},{6,4},{7,3},{8,10},{9,13},{10,... | collective-permute-start | bytes 1376264 | tf_op jit(solution)/shard_map/ppermute | solution.py:26
  62.8 0.7 collective-permute-start.15
  63.6 0.0 copy-start.14
  63.6 2.3 %collective-permute-start.16 = (bf16[32,7168]{1,0:T(8,128)(2,1)S(1)}, bf16[32,7168]{1,0:T(8,128)(2,1)S(1)}, u32[]{:S(2)}, u32[]{:S(2)}) collective-permute-start(bf16[32,7168]{1,0:T(8,128)(2,1)S(1)} %get-tuple-element.38), channel_id=1, source_target_pairs={{0,2},{1,5},{2,0},{3,7},{4,6},{5,1},{6,4},{7,3},{8,10},{9,13},{10,... | collective-permute-start | bytes 1376264 | tf_op jit(solution)/shard_map/ppermute | solution.py:26
  65.8 13.5 %collective-permute-done.14 = bf16[32,7168]{1,0:T(8,128)(2,1)S(1)} collective-permute-done((bf16[32,7168]{1,0:T(8,128)(2,1)S(1)}, bf16[32,7168]{1,0:T(8,128)(2,1)S(1)}, u32[]{:S(2)}, u32[]{:S(2)}) %collective-permute-start.14) | collective-permute-done | bytes 458784 | tf_op jit(solution)/shard_map/ppermute | solution.py:26
  79.4 0.2 add_convert_fusion.1
  79.6 1.3 %collective-permute-start.17 = (bf16[32,7168]{1,0:T(8,128)(2,1)S(1)}, bf16[32,7168]{1,0:T(8,128)(2,1)S(1)}, u32[]{:S(2)}, u32[]{:S(2)}) collective-permute-start(bf16[32,7168]{1,0:T(8,128)(2,1)S(1)} %add_convert_fusion.1), channel_id=1, source_target_pairs={{0,4},{1,3},{2,6},{3,1},{4,0},{5,7},{6,2},{7,5},{8,12},{9,11},{10,... | collective-permute-start | bytes 1376264 | tf_op jit(solution)/shard_map/ppermute | solution.py:26
  80.9 1.5 %collective-permute-start.7 = (bf16[8,96,576]{2,1,0:T(8,128)(2,1)S(1)}, bf16[8,96,576]{2,1,0:T(8,128)(2,1)S(1)}, u32[]{:S(2)}, u32[]{:S(2)}) collective-permute-start(bf16[8,96,576]{2,1,0:T(8,128)(2,1)S(1)} %copy-done.1), channel_id=1, source_target_pairs={{0,1},{1,0},{2,3},{3,2},{4,5},{5,4},{6,7},{7,6},{8,9},{9,8},{10,11... | collective-permute-start | bytes 2654216 | tf_op jit(solution)/shard_map/ppermute | solution.py:26
  82.4 3.5 %collective-permute-done.16 = bf16[32,7168]{1,0:T(8,128)(2,1)S(1)} collective-permute-done((bf16[32,7168]{1,0:T(8,128)(2,1)S(1)}, bf16[32,7168]{1,0:T(8,128)(2,1)S(1)}, u32[]{:S(2)}, u32[]{:S(2)}) %collective-permute-start.16) | collective-permute-done | bytes 458784 | tf_op jit(solution)/shard_map/ppermute | solution.py:26
  85.9 2.2 %collective-permute-done.17 = bf16[32,7168]{1,0:T(8,128)(2,1)S(1)} collective-permute-done((bf16[32,7168]{1,0:T(8,128)(2,1)S(1)}, bf16[32,7168]{1,0:T(8,128)(2,1)S(1)}, u32[]{:S(2)}, u32[]{:S(2)}) %collective-permute-start.17) | collective-permute-done | bytes 458784 | tf_op jit(solution)/shard_map/ppermute | solution.py:26
  88.1 0.9 add_convert_fusion.3
  89.0 7.8 %collective-permute-start.18 = (bf16[8,7168]{1,0:T(8,128)(2,1)S(1)}, bf16[8,7168]{1,0:T(8,128)(2,1)S(1)}, u32[]{:S(2)}, u32[]{:S(2)}) collective-permute-start(bf16[8,7168]{1,0:T(8,128)(2,1)S(1)} %get-tuple-element.36), channel_id=1, source_target_pairs={{0,24},{1,25},{2,26},{3,27},{4,28},{5,29},{6,30},{7,31},{8,0},{9,1... | collective-permute-start | bytes 344072 | tf_op jit(solution)/shard_map/ppermute | solution.py:26
  96.8 0.6 collective-permute-start.20
  97.4 0.6 copy.13.newest
  98.0 1.0 copy-done.4
  99.0 8.5 %shard_map.123 = bf16[8,64,512]{2,1,0:T(8,128)(2,1)} custom-call(s32[8]{0:T(128)} %parents.1, s32[8]{0:T(128)} %lengths.1, bf16[8,64,576]{2,1,0:T(8,128)(2,1)} %query.1, bf16[8,96,576]{2,1,0:T(8,128)(2,1)} %own, bf16[8,96,576]{2,1,0:T(8,128)(2,1)} %copy-done.4, bf16[8,96,576]{2,1,0:T(8,128)(2,1)} %copy-done.2, bf16[8,96,576]{2,1,0:T(8,128)(2,1)} %copy-done.3, ...), custom_call_target="tpu_custom_call" | custom-call | flops 106954752 | bytes 4653056 | tf_op jit(solution)/shard_map/pallas_call | solution.py:82
  107.5 0.6 collective-permute-done.19.refs_4_
  108.1 0.0 copy-done.12
  108.1 0.6 copy-done.13
  108.8 1.9 %shard_map.124 = bf16[8,7168]{1,0:T(8,128)(2,1)} custom-call(s32[2,8]{1,0:T(2,128)} %bitcast.4, f32[2,8]{1,0:T(2,128)} %bitcast.5, f32[8,7168]{1,0:T(8,128)} %get-tuple-element.37.refs_2_, bf16[8,7168]{1,0:T(8,128)(2,1)} %copy-done.12, bf16[8,7168]{1,0:T(8,128)(2,1)} %copy-done.13, bf16[8,7168]{1,0:T(8,128)(2,1)} %collective-permute-done.20.refs_5_), custom_call_target="tpu_custom_call" | custom-call | flops 458752 | bytes 688128 | tf_op jit(solution)/shard_map/pallas_call | solution.py:229
  (35 shorter events, 0.1 us)
Async XLA Ops:
  0.6 13.9 %collective-permute-start.3 = (bf16[8,96,576]{2,1,0:T(8,128)(2,1)}, bf16[8,96,576]{2,1,0:T(8,128)(2,1)S(1)}, u32[]{:S(2)}, u32[]{:S(2)}) collective-permute-start(bf16[8,96,576]{2,1,0:T(8,128)(2,1)} %own), channel_id=1, source_target_pairs={{1,2},{3,4},{5,6},{6,5},{9,10},{11,12},{13,14},{14,13},{17,18},{19... | collective-permute-start | bytes 2654216 | tf_op jit(solution)/shard_map/ppermute | solution.py:43
  1.4 8.1 %collective-permute-start = (bf16[8,7168]{1,0:T(8,128)(2,1)}, bf16[8,7168]{1,0:T(8,128)(2,1)S(1)}, u32[]{:S(2)}, u32[]{:S(2)}) collective-permute-start(bf16[8,7168]{1,0:T(8,128)(2,1)} %param.16), channel_id=1, source_target_pairs={{0,8},{1,9},{2,10},{3,11},{4,12},{5,13},{6,14},{7,15},{8,16},{9,17... | collective-permute-start | bytes 344072 | tf_op jit(solution)/shard_map/ppermute | solution.py:26
  4.4 9.7 %collective-permute-start.1 = (bf16[8,7168]{1,0:T(8,128)(2,1)}, bf16[8,7168]{1,0:T(8,128)(2,1)S(1)}, u32[]{:S(2)}, u32[]{:S(2)}) collective-permute-start(bf16[8,7168]{1,0:T(8,128)(2,1)} %param.16), channel_id=1, source_target_pairs={{0,16},{1,17},{2,18},{3,19},{4,20},{5,21},{6,22},{7,23},{8,24},{9,... | collective-permute-start | bytes 344072 | tf_op jit(solution)/shard_map/ppermute | solution.py:26
  7.0 7.5 %collective-permute-start.2 = (bf16[8,7168]{1,0:T(8,128)(2,1)}, bf16[8,7168]{1,0:T(8,128)(2,1)S(1)}, u32[]{:S(2)}, u32[]{:S(2)}) collective-permute-start(bf16[8,7168]{1,0:T(8,128)(2,1)} %param.16), channel_id=1, source_target_pairs={{0,24},{1,25},{2,26},{3,27},{4,28},{5,29},{6,30},{7,31},{8,0},{9,1... | collective-permute-start | bytes 344072 | tf_op jit(solution)/shard_map/ppermute | solution.py:26
  14.6 42.1 %copy-start.2 = (bf16[8,96,576]{2,1,0:T(8,128)(2,1)}, bf16[8,96,576]{2,1,0:T(8,128)(2,1)S(1)}, u32[]{:S(2)}) copy-start(bf16[8,96,576]{2,1,0:T(8,128)(2,1)S(1)} %collective-permute-done.3.early) | copy-start | bytes 2654212
  15.6 29.3 %copy-start.5 = (bf16[32,7168]{1,0:T(8,128)(2,1)}, bf16[32,7168]{1,0:T(8,128)(2,1)S(1)}, u32[]{:S(2)}) copy-start(bf16[32,7168]{1,0:T(8,128)(2,1)S(1)} %constant_dynamic-update-slice_fusion.refs_0_) | copy-start | bytes 1376260
  15.6 16.1 %collective-permute-start.4 = (bf16[32,7168]{1,0:T(8,128)(2,1)S(1)}, bf16[32,7168]{1,0:T(8,128)(2,1)S(1)}, u32[]{:S(2)}, u32[]{:S(2)}) collective-permute-start(bf16[32,7168]{1,0:T(8,128)(2,1)S(1)} %constant_dynamic-update-slice_fusion.refs_0_), channel_id=1, source_target_pairs={{0,4},{1,3},{2,6},{3,1},{4,0},{5,7},{6,2},{7,5},{8,12},{9,11},{10,... | collective-permute-start | bytes 1376264 | tf_op jit(solution)/shard_map/ppermute | solution.py:26
  21.3 12.4 %collective-permute-start.5 = (bf16[32,7168]{1,0:T(8,128)(2,1)S(1)}, bf16[32,7168]{1,0:T(8,128)(2,1)S(1)}, u32[]{:S(2)}, u32[]{:S(2)}) collective-permute-start(bf16[32,7168]{1,0:T(8,128)(2,1)S(1)} %constant_dynamic-update-slice_fusion.refs_0_), channel_id=1, source_target_pairs={{0,2},{1,5},{2,0},{3,7},{4,6},{5,1},{6,4},{7,3},{8,10},{9,13},{10,... | collective-permute-start | bytes 1376264 | tf_op jit(solution)/shard_map/ppermute | solution.py:26
  31.7 13.2 %copy-start.6 = (bf16[32,7168]{1,0:T(8,128)(2,1)}, bf16[32,7168]{1,0:T(8,128)(2,1)S(1)}, u32[]{:S(2)}) copy-start(bf16[32,7168]{1,0:T(8,128)(2,1)S(1)} %collective-permute-done.4.refs_1_) | copy-start | bytes 1376260
  31.7 8.5 %collective-permute-start.6 = (bf16[32,7168]{1,0:T(8,128)(2,1)S(1)}, bf16[32,7168]{1,0:T(8,128)(2,1)S(1)}, u32[]{:S(2)}, u32[]{:S(2)}) collective-permute-start(bf16[32,7168]{1,0:T(8,128)(2,1)S(1)} %collective-permute-done.4.refs_1_), channel_id=1, source_target_pairs={{0,2},{1,5},{2,0},{3,7},{4,6},{5,1},{6,4},{7,3},{8,10},{9,13},{10,... | collective-permute-start | bytes 1376264 | tf_op jit(solution)/shard_map/ppermute | solution.py:26
  33.7 11.2 %copy-start.7 = (bf16[32,7168]{1,0:T(8,128)(2,1)}, bf16[32,7168]{1,0:T(8,128)(2,1)S(1)}, u32[]{:S(2)}) copy-start(bf16[32,7168]{1,0:T(8,128)(2,1)S(1)} %collective-permute-done.5.refs_2_) | copy-start | bytes 1376260
  40.2 4.8 %copy-start.8 = (bf16[32,7168]{1,0:T(8,128)(2,1)}, bf16[32,7168]{1,0:T(8,128)(2,1)S(1)}, u32[]{:S(2)}) copy-start(bf16[32,7168]{1,0:T(8,128)(2,1)S(1)} %collective-permute-done.6.refs_3_) | copy-start | bytes 1376260
  40.2 1.8 %collective-permute-start.10 = (bf16[32,7168]{1,0:T(8,128)(2,1)S(1)}, bf16[32,7168]{1,0:T(8,128)(2,1)S(1)}, u32[]{:S(2)}, u32[]{:S(2)}) collective-permute-start(bf16[32,7168]{1,0:T(8,128)(2,1)S(1)} %collective-permute-done.5.refs_2_), channel_id=1, source_target_pairs={{0,1},{1,0},{2,3},{3,2},{4,5},{5,4},{6,7},{7,6},{8,9},{9,8},{10,11... | collective-permute-start | bytes 1376264 | tf_op jit(solution)/shard_map/ppermute | solution.py:26
  40.2 3.1 %collective-permute-start.11 = (bf16[32,7168]{1,0:T(8,128)(2,1)S(1)}, bf16[32,7168]{1,0:T(8,128)(2,1)S(1)}, u32[]{:S(2)}, u32[]{:S(2)}) collective-permute-start(bf16[32,7168]{1,0:T(8,128)(2,1)S(1)} %collective-permute-done.6.refs_3_), channel_id=1, source_target_pairs={{0,1},{1,0},{2,3},{3,2},{4,5},{5,4},{6,7},{7,6},{8,9},{9,8},{10,11... | collective-permute-start | bytes 1376264 | tf_op jit(solution)/shard_map/ppermute | solution.py:26
  40.7 3.3 %collective-permute-start.8 = (bf16[32,7168]{1,0:T(8,128)(2,1)S(1)}, bf16[32,7168]{1,0:T(8,128)(2,1)S(1)}, u32[]{:S(2)}, u32[]{:S(2)}) collective-permute-start(bf16[32,7168]{1,0:T(8,128)(2,1)S(1)} %constant_dynamic-update-slice_fusion.refs_0_), channel_id=1, source_target_pairs={{0,1},{1,0},{2,3},{3,2},{4,5},{5,4},{6,7},{7,6},{8,9},{9,8},{10,11... | collective-permute-start | bytes 1376264 | tf_op jit(solution)/shard_map/ppermute | solution.py:26
  40.7 4.2 %collective-permute-start.9 = (bf16[32,7168]{1,0:T(8,128)(2,1)S(1)}, bf16[32,7168]{1,0:T(8,128)(2,1)}, u32[]{:S(2)}, u32[]{:S(2)}) collective-permute-start(bf16[32,7168]{1,0:T(8,128)(2,1)S(1)} %collective-permute-done.4.refs_1_), channel_id=1, source_target_pairs={{0,1},{1,0},{2,3},{3,2},{4,5},{5,4},{6,7},{7,6},{8,9},{9,8},{10,11... | collective-permute-start | bytes 1376264 | tf_op jit(solution)/shard_map/ppermute | solution.py:26
  42.0 2.0 %copy-start.9 = (bf16[32,7168]{1,0:T(8,128)(2,1)}, bf16[32,7168]{1,0:T(8,128)(2,1)S(1)}, u32[]{:S(2)}) copy-start(bf16[32,7168]{1,0:T(8,128)(2,1)S(1)} %collective-permute-done.10.refs_6_) | copy-start | bytes 1376260
  43.3 0.8 copy-start.10
  44.1 0.8 copy-start.11
  44.9 17.9 %copy-start.1 = (bf16[8,96,576]{2,1,0:T(8,128)(2,1)S(1)}, bf16[8,96,576]{2,1,0:T(8,128)(2,1)}, u32[]{:S(2)}) copy-start(bf16[8,96,576]{2,1,0:T(8,128)(2,1)} %own) | copy-start | bytes 2654212
  56.7 22.7 %copy-start = (bf16[128,7168]{1,0:T(8,128)(2,1)S(1)}, bf16[128,7168]{1,0:T(8,128)(2,1)}, u32[]{:S(2)}) copy-start(bf16[128,7168]{1,0:T(8,128)(2,1)} %get-tuple-element.27) | copy-start | bytes 5505028
  56.7 2.7 %collective-permute-start.13 = (bf16[64,7168]{1,0:T(8,128)(2,1)}, bf16[64,7168]{1,0:T(8,128)(2,1)S(1)}, u32[]{:S(2)}, u32[]{:S(2)}) collective-permute-start(bf16[64,7168]{1,0:T(8,128)(2,1)} %get-tuple-element.29), channel_id=1, source_target_pairs={{0,1},{1,0},{2,3},{3,2},{4,5},{5,4},{6,7},{7,6},{8,9},{9,8},{10,11... | collective-permute-start | bytes 2752520 | tf_op jit(solution)/shard_map/ppermute | solution.py:26
  56.9 9.0 %collective-permute-start.12 = (bf16[64,7168]{1,0:T(8,128)(2,1)}, bf16[64,7168]{1,0:T(8,128)(2,1)S(1)}, u32[]{:S(2)}, u32[]{:S(2)}) collective-permute-start(bf16[64,7168]{1,0:T(8,128)(2,1)} %get-tuple-element.28), channel_id=1, source_target_pairs={{0,1},{1,0},{2,3},{3,2},{4,5},{5,4},{6,7},{7,6},{8,9},{9,8},{10,11... | collective-permute-start | bytes 2752520 | tf_op jit(solution)/shard_map/ppermute | solution.py:26
  60.8 18.6 %collective-permute-start.14 = (bf16[32,7168]{1,0:T(8,128)(2,1)S(1)}, bf16[32,7168]{1,0:T(8,128)(2,1)S(1)}, u32[]{:S(2)}, u32[]{:S(2)}) collective-permute-start(bf16[32,7168]{1,0:T(8,128)(2,1)S(1)} %get-tuple-element.39), channel_id=1, source_target_pairs={{0,2},{1,5},{2,0},{3,7},{4,6},{5,1},{6,4},{7,3},{8,10},{9,13},{10,... | collective-permute-start | bytes 1376264 | tf_op jit(solution)/shard_map/ppermute | solution.py:26
  62.8 16.7 %collective-permute-start.15 = (bf16[8,96,576]{2,1,0:T(8,128)(2,1)S(1)}, bf16[8,96,576]{2,1,0:T(8,128)(2,1)S(1)}, u32[]{:S(2)}, u32[]{:S(2)}) collective-permute-start(bf16[8,96,576]{2,1,0:T(8,128)(2,1)S(1)} %copy-done.1), channel_id=1, source_target_pairs={{2,1},{4,3},{7,8},{8,7},{10,9},{12,11},{15,16},{16,15},{18,17},{20... | collective-permute-start | bytes 2654216 | tf_op jit(solution)/shard_map/ppermute | solution.py:43
  63.6 33.8 %copy-start.14 = (bf16[8,576]{1,0:T(8,128)(2,1)S(1)}, bf16[8,576]{1,0:T(8,128)(2,1)}, u32[]{:S(2)}) copy-start(bf16[8,576]{1,0:T(8,128)(2,1)} %param.13) | copy-start | bytes 27652
  63.6 22.4 %collective-permute-start.16 = (bf16[32,7168]{1,0:T(8,128)(2,1)S(1)}, bf16[32,7168]{1,0:T(8,128)(2,1)S(1)}, u32[]{:S(2)}, u32[]{:S(2)}) collective-permute-start(bf16[32,7168]{1,0:T(8,128)(2,1)S(1)} %get-tuple-element.38), channel_id=1, source_target_pairs={{0,2},{1,5},{2,0},{3,7},{4,6},{5,1},{6,4},{7,3},{8,10},{9,13},{10,... | collective-permute-start | bytes 1376264 | tf_op jit(solution)/shard_map/ppermute | solution.py:26
  79.6 18.4 %copy-start.3 = (bf16[8,96,576]{2,1,0:T(8,128)(2,1)}, bf16[8,96,576]{2,1,0:T(8,128)(2,1)S(1)}, u32[]{:S(2)}) copy-start(bf16[8,96,576]{2,1,0:T(8,128)(2,1)S(1)} %collective-permute-done.15.late) | copy-start | bytes 2654212
  79.6 8.5 %collective-permute-start.17 = (bf16[32,7168]{1,0:T(8,128)(2,1)S(1)}, bf16[32,7168]{1,0:T(8,128)(2,1)S(1)}, u32[]{:S(2)}, u32[]{:S(2)}) collective-permute-start(bf16[32,7168]{1,0:T(8,128)(2,1)S(1)} %add_convert_fusion.1), channel_id=1, source_target_pairs={{0,4},{1,3},{2,6},{3,1},{4,0},{5,7},{6,2},{7,5},{8,12},{9,11},{10,... | collective-permute-start | bytes 1376264 | tf_op jit(solution)/shard_map/ppermute | solution.py:26
  80.9 17.1 %collective-permute-start.7 = (bf16[8,96,576]{2,1,0:T(8,128)(2,1)S(1)}, bf16[8,96,576]{2,1,0:T(8,128)(2,1)S(1)}, u32[]{:S(2)}, u32[]{:S(2)}) collective-permute-start(bf16[8,96,576]{2,1,0:T(8,128)(2,1)S(1)} %copy-done.1), channel_id=1, source_target_pairs={{0,1},{1,0},{2,3},{3,2},{4,5},{5,4},{6,7},{7,6},{8,9},{9,8},{10,11... | collective-permute-start | bytes 2654216 | tf_op jit(solution)/shard_map/ppermute | solution.py:26
  89.0 18.5 %collective-permute-start.18 = (bf16[8,7168]{1,0:T(8,128)(2,1)S(1)}, bf16[8,7168]{1,0:T(8,128)(2,1)S(1)}, u32[]{:S(2)}, u32[]{:S(2)}) collective-permute-start(bf16[8,7168]{1,0:T(8,128)(2,1)S(1)} %get-tuple-element.36), channel_id=1, source_target_pairs={{0,24},{1,25},{2,26},{3,27},{4,28},{5,29},{6,30},{7,31},{8,0},{9,1... | collective-permute-start | bytes 344072 | tf_op jit(solution)/shard_map/ppermute | solution.py:26
  96.8 11.3 %collective-permute-start.19 = (bf16[8,7168]{1,0:T(8,128)(2,1)S(1)}, bf16[8,7168]{1,0:T(8,128)(2,1)S(1)}, u32[]{:S(2)}, u32[]{:S(2)}) collective-permute-start(bf16[8,7168]{1,0:T(8,128)(2,1)S(1)} %get-tuple-element.35), channel_id=1, source_target_pairs={{0,16},{1,17},{2,18},{3,19},{4,20},{5,21},{6,22},{7,23},{8,24},{9,... | collective-permute-start | bytes 344072 | tf_op jit(solution)/shard_map/ppermute | solution.py:26
  96.8 11.3 %collective-permute-start.20 = (bf16[8,7168]{1,0:T(8,128)(2,1)S(1)}, bf16[8,7168]{1,0:T(8,128)(2,1)}, u32[]{:S(2)}, u32[]{:S(2)}) collective-permute-start(bf16[8,7168]{1,0:T(8,128)(2,1)S(1)} %get-tuple-element.34), channel_id=1, source_target_pairs={{0,8},{1,9},{2,10},{3,11},{4,12},{5,13},{6,14},{7,15},{8,16},{9,17... | collective-permute-start | bytes 344072 | tf_op jit(solution)/shard_map/ppermute | solution.py:26
  98.0 1.0 copy-start.4
  107.5 0.6 copy-start.12
  108.1 0.6 copy-start.13

commit v6 on v5

v6 whole, which is shorter than its diff:
```python
import jax
import jax.numpy as jnp
from jax import lax
from jax.experimental import pallas as pl
from jax.experimental.pallas import tpu as pltpu
from jax.sharding import PartitionSpec as P

FF_E = 2048
KV = 512


score_scale = 192.0 ** (-0.5)


def pair_slots(route_rows, expert_count, capacity):
    flat_experts = route_rows.reshape(-1)
    onehot = (flat_experts[:, None] == jnp.arange(expert_count, dtype=jnp.int32)[None, :]).astype(
        jnp.int32
    )
    position = jnp.sum((jnp.cumsum(onehot, axis=0) - onehot) * onehot, axis=1)
    return (flat_experts * capacity + position).astype(jnp.int32).reshape(route_rows.shape)


def swapped(value, partner):
    peers = lax.axis_size("dp")
    return lax.ppermute(value, "dp", [(i, partner(i)) for i in range(peers)])


def added(values):
    total = values[0].astype(jnp.float32)
    for value in values[1:]:
        total = total + value.astype(jnp.float32)
    return total


EARLY = ((1, 2), (3, 4), (5, 6), (6, 5))
LATE = ((2, 1), (4, 3), (7, 8), (8, 7))


def neighbours(value, moves, slices):
    peers = lax.axis_size("dp")
    pairs = [(base + i, base + j) for base in range(0, peers, slices) for i, j in moves]
    return lax.ppermute(value, "dp", [p for p in pairs if max(p) < peers])


def attend_kernel(parents, lengths, query, own, twin, early, late, newest, out):
    beam_count = parents.shape[0]
    beam = pl.program_id(0)
    rank = lax.axis_index("dp")
    holder = parents[beam] // beam_count
    length = lengths[beam]
    place = rank % 8
    arrives_early = (place == 2) | (place == 4) | (place == 5) | (place == 6)
    rows = jnp.where(arrives_early, early[0], late[0])
    rows = jnp.where(holder == (rank ^ 1), twin[0], rows)
    rows = jnp.where(holder == rank, own[0], rows)
    at = lax.broadcasted_iota(jnp.int32, rows.shape, 0)
    rows = jnp.where(at < length - 1, rows, jnp.zeros_like(rows))
    rows = jnp.where(at == length - 1, newest[0], rows)
    scores = lax.dot_general(
        query[0], rows, (((1,), (1,)), ((), ())), preferred_element_type=jnp.float32
    )
    scores = scores * score_scale
    at = lax.broadcasted_iota(jnp.int32, scores.shape, 1)
    scores = jnp.where(at < length, scores, -jnp.inf)
    expons = jnp.exp(scores - jnp.max(scores, axis=1, keepdims=True))
    probs = (expons / jnp.sum(expons, axis=1, keepdims=True)).astype(jnp.bfloat16)
    mixed = jnp.dot(probs, rows[:, :KV], preferred_element_type=jnp.float32)
    out[0] = mixed.astype(out.dtype)


def attend(queries, own, twin, early, late, newest, parents, lengths):
    beam_count, heads, width = queries.shape
    positions = own.shape[1]

    def chosen(b, parents, lengths):
        return (parents[b] % beam_count, 0, 0)

    def each(b, parents, lengths):
        return (b, 0, 0)

    return pl.pallas_call(
        attend_kernel,
        grid_spec=pltpu.PrefetchScalarGridSpec(
            num_scalar_prefetch=2,
            grid=(beam_count,),
            in_specs=[pl.BlockSpec((1, heads, width), each)]
            + [pl.BlockSpec((1, positions, width), chosen)] * 4
            + [pl.BlockSpec((1, 1, width), each)],
            out_specs=pl.BlockSpec((1, heads, KV), each),
        ),
        out_shape=jax.ShapeDtypeStruct((beam_count, heads, KV), jnp.bfloat16),
        cost_estimate=pl.CostEstimate(
            flops=2 * beam_count * heads * positions * (width + KV),
            bytes_accessed=2 * beam_count * (4 * positions * width + heads * (width + KV)),
            transcendentals=beam_count * heads * positions,
        ),
    )(parents, lengths, queries, own, twin, early, late, newest)


def fetch_kernel(*refs):
    count = len(refs) // 2
    sources, targets, sems = refs[:count], refs[count:-1], refs[-1]
    copies = [
        pltpu.make_async_copy(source, target, sems.at[i])
        for i, (source, target) in enumerate(zip(sources, targets))
    ]
    for copy in copies:
        copy.start()
    for copy in copies:
        copy.wait()


def fetched(weights):
    return pl.pallas_call(
        fetch_kernel,
        in_specs=[pl.BlockSpec(memory_space=pl.ANY)] * len(weights),
        out_specs=[pl.BlockSpec(memory_space=pltpu.VMEM)] * len(weights),
        out_shape=[pltpu.VMEM(w.shape, w.dtype) for w in weights],
        scratch_shapes=[pltpu.SemaphoreType.DMA((len(weights),))],
        compiler_params=pltpu.CompilerParams(vmem_limit_bytes=16 * 2**20),
        cost_estimate=pl.CostEstimate(
            flops=0,
            bytes_accessed=2 * sum(w.size * w.dtype.itemsize for w in weights),
            transcendentals=0,
        ),
    )(*weights)


def expert_kernel(wide, *refs):
    rows, refs = refs[:8], refs[8:]
    gate, up, down, own, high, low, gate_sum, up_sum = refs
    height, width = rows[0].shape
    half = 4 * height

    def span(k):
        return pl.ds(pl.multiple_of(k * wide, wide), wide)

    gate_sum[...] = jnp.zeros_like(gate_sum)
    up_sum[...] = jnp.zeros_like(up_sum)

    @pl.loop(0, width // wide)
    def _(k):
        piece = jnp.concatenate([ref[:, span(k)] for ref in rows], axis=0)
        gate_sum[...] += jnp.dot(piece, gate[0, span(k), :], preferred_element_type=jnp.float32)
        up_sum[...] += jnp.dot(piece, up[0, span(k), :], preferred_element_type=jnp.float32)

    total = gate_sum[...]
    hidden = (total / (1.0 + jnp.exp(-total)) * up_sum[...]).astype(jnp.bfloat16)

    @pl.loop(0, width // wide)
    def _(k):
        product = jnp.dot(hidden, down[0, :, span(k)], preferred_element_type=jnp.float32)
        product = product.astype(jnp.bfloat16)
        own[:, span(k)] = product[:half]
        low[:, span(k)] = product[half : half + 2 * height]
        high[:, span(k)] = product[half + 2 * height :]


def experts(rows, weights):
    height, width = rows[0].shape
    units = weights[0].shape[2]
    wide = max(w for w in (128, 256, 512, 1024) if width % w == 0)
    total = len(rows) * height
    whole = pl.BlockSpec(memory_space=pltpu.VMEM)
    inputs = [pltpu.with_memory_space_constraint(v, pltpu.VMEM) for v in (*rows, *weights)]
    return pl.pallas_call(
        lambda *refs: expert_kernel(wide, *refs),
        in_specs=[whole] * len(inputs),
        out_specs=[whole] * 3,
        out_shape=[pltpu.VMEM((count * height, width), jnp.bfloat16) for count in (4, 2, 2)],
        scratch_shapes=[
            pltpu.VMEM((total, units), jnp.float32),
            pltpu.VMEM((total, units), jnp.float32),
        ],
        compiler_params=pltpu.CompilerParams(vmem_limit_bytes=28 * 2**20),
        cost_estimate=pl.CostEstimate(
            flops=6 * total * width * units,
            bytes_accessed=6 * width * units + 4 * total * width,
            transcendentals=total * units,
        ),
    )(*inputs)


def body(
    queries,
    latent_cache,
    new_latent,
    parents,
    lengths,
    expert_input,
    routed_experts,
    route_weights,
    gate_weight,
    up_weight,
    down_weight,
):
    beam_count, width = expert_input.shape
    devices = lax.axis_size("dp")
    slices = FF_E // gate_weight.shape[2]
    expert_count = devices // slices
    route_count = routed_experts.shape[1]
    capacity = min(beam_count, max(2, 2 * beam_count * route_count // expert_count))
    dense = capacity == beam_count
    assert slices == 8

    mine = lax.axis_index("dp") // slices
    turns = jnp.arange(expert_count, dtype=jnp.int32)
    targets = (mine + turns) % expert_count
    if dense:
        blocks = [expert_input] * expert_count
        mixing = [
            jnp.sum(jnp.where(routed_experts == targets[r], route_weights, 0.0), axis=1)
            for r in range(expert_count)
        ]
    else:
        slots = pair_slots(routed_experts, expert_count, capacity)
        wanted = targets[:, None] * capacity + jnp.arange(capacity, dtype=jnp.int32)
        matches = (slots[:, :, None] == wanted.reshape(-1)).astype(jnp.float32)
        mixing = jnp.sum(route_weights[:, :, None] * matches, axis=1)
        selector = jnp.sum(matches, axis=1).T.astype(jnp.bfloat16)
        chosen = jnp.dot(selector, expert_input, preferred_element_type=jnp.float32)
        blocks = list(chosen.astype(jnp.bfloat16).reshape(expert_count, capacity, width))

    def ahead(r):
        return lambda i: (i + r * slices) % devices

    def twin(i):
        return i ^ 1

    def first(i):
        return i ^ (2 if i & 1 else 4)

    def second(i):
        return i ^ (4 if i & 1 else 2)

    blocks = blocks[:1] + [swapped(blocks[r], ahead(r)) for r in range(1, expert_count)]
    early = neighbours(latent_cache, EARLY, slices)
    newest = new_latent[:, None, :]
    *blocks, early, newest, mixing = lax.optimization_barrier((*blocks, early, newest, mixing))
    column = jnp.concatenate(blocks)
    near = swapped(column, first)
    side = swapped(column, second)
    across = swapped(near, second)
    beside = swapped(latent_cache, twin)
    held = [column, near, side, across]
    *held, beside, latent_cache = lax.optimization_barrier((*held, beside, latent_cache))
    late = neighbours(latent_cache, LATE, slices)
    held = held + [swapped(value, twin) for value in held]
    own, high, low = experts(held, fetched([gate_weight, up_weight, down_weight]))

    high, low = swapped(high, twin), swapped(low, twin)
    height = expert_count * capacity

    def block(value, j):
        return lax.slice_in_dim(value, j * height, (j + 1) * height)

    across = added([block(own, 3), block(high, 1)]).astype(jnp.bfloat16)
    across, late = lax.optimization_barrier((across, late))
    across = swapped(across, second)
    side = swapped(added([block(own, 2), block(high, 0)]).astype(jnp.bfloat16), second)
    attention = attend(queries, latent_cache, beside, early, late, newest, parents, lengths)
    near = added([block(own, 1), block(low, 1), across]).astype(jnp.bfloat16)
    near, attention = lax.optimization_barrier((near, attention))
    near = swapped(near, first)
    here = [own, low, side, near]

    def share(r):
        return added([v[r * capacity : (r + 1) * capacity] for v in here])

    values = [swapped(share(r).astype(jnp.bfloat16), ahead(-r)) for r in range(1, expert_count)]
    values = [share(0)] + values
    values = [v.astype(jnp.float32) for v in values]
    if dense:
        expert_output = sum(mixing[r][:, None] * values[r] for r in range(expert_count))
    else:
        expert_output = jnp.dot(
            mixing,
            jnp.concatenate(values),
            precision=lax.Precision.HIGHEST,
            preferred_element_type=jnp.float32,
        )
    return (attention, expert_output.astype(jnp.bfloat16))


def solution(mesh):
    in_specs = (
        P(("groups", "dp"), None, None),
        P(("groups", "dp"), None, None),
        P(("groups", "dp"), None),
        P(("groups", "dp")),
        P(("groups", "dp")),
        P(("groups", "dp"), None),
        P(("groups", "dp"), None),
        P(("groups", "dp"), None),
        P("dp", None, None),
        P("dp", None, None),
        P("dp", None, None),
    )
    out_specs = (P(("groups", "dp"), None, None), P(("groups", "dp"), None))
    return jax.shard_map(body, mesh=mesh, in_specs=in_specs, out_specs=out_specs, check_vma=False)
```

time: 111 us -> 110 us (level)
  waiting for transfers between devices: 47.3 us -> 35.9 us
  Pallas kernels: 22.1 us -> 14.7 us
  other arithmetic: 2.45 us -> 8.69 us
  starting transfers between devices: 33.8 us -> 39.9 us
  local copies, waits for them, and re-layouts: 4.24 us -> 9.39 us
    ppermute x19, waiting for transfers between devices: 47.3 us -> 35.9 us  [swapped(): return lax.ppermute(value, 'dp', [(i, partner(i)) for i in range(peers)])]
    pallas_call x2, Pallas kernels: 13.6 us -> 6.07 us  [the longest x1 5.31 us: experts(): pl.pallas_call(lambda *refs: expert_kernel(wide, *refs), in_specs=[whole]...]
    ppermute x19, starting transfers between devices: 32.3 us -> 38.5 us  [swapped(): return lax.ppermute(value, 'dp', [(i, partner(i)) for i in range(peers)])]
    unnamed x33 -> x19, local copies, waits for them, and re-layouts: 3.61 us -> 8.11 us
    reduce_sum x0 -> x1, other arithmetic: none -> 3.25 us  [body(): jnp.sum(jnp.where(routed_experts == targets[r], route_weights, 0.0), axis=1)]
    convert_element_type x0 -> x1, other arithmetic: none -> 1.77 us  [body(): return (attention, expert_output.astype(jnp.bfloat16))]
  transfers between devices with their start and end apart: 21 -> 21, of which waited for: 13 -> 8; matrix products, arithmetic and copies ran while one was open for 3% -> 6% of each run, Pallas kernels for 8% -> 9%
where the time goes in v6:
time: 110 us
  starting transfers between devices  39.9 us (36%)
  waiting for transfers between devices  35.9 us (33%)
  Pallas kernels  14.7 us (13%)
  local copies, waits for them, and re-layouts  9.39 us (9%)
  other arithmetic  8.69 us (8%)
    ppermute x19, starting transfers between devices, swapped(): return lax.ppermute(value, 'dp', [(i, partner(i)) for i in range(peers)])  38.5 us
    ppermute x19, waiting for transfers between devices, swapped(): return lax.ppermute(value, 'dp', [(i, partner(i)) for i in range(peers)])  35.9 us
    pallas_call x1, Pallas kernels, attend(): pl.pallas_call(attend_kernel, grid_spec=pltpu.PrefetchScalarGridSpec(num_...  8.67 us
    unnamed x19, local copies, waits for them, and re-layouts  8.11 us
    pallas_call x1, Pallas kernels, experts(): pl.pallas_call(lambda *refs: expert_kernel(wide, *refs), in_specs=[whole]...  5.31 us
    reduce_sum x1, other arithmetic, body(): jnp.sum(jnp.where(routed_experts == targets[r], route_weights, 0.0), axis=1)  3.25 us
  transfers between devices with their start and end apart: 21, of which 8 were waited for; matrix products, arithmetic and copies ran while one was open for 6% of the time, Pallas kernels for 9%

profile of v6, /device:TPU:0, one launch (start us, length us, event | category | flops | bytes accessed | tf_op | source)
XLA Modules:
  0.0 109.5 jit_solution(14722497675969021923)
XLA Ops:
  0.6 0.7 collective-permute-start.3
  1.4 3.1 %collective-permute-start = (bf16[8,7168]{1,0:T(8,128)(2,1)}, bf16[8,7168]{1,0:T(8,128)(2,1)S(1)}, u32[]{:S(2)}, u32[]{:S(2)}) collective-permute-start(bf16[8,7168]{1,0:T(8,128)(2,1)} %param.16), channel_id=1, source_target_pairs={{0,8},{1,9},{2,10},{3,11},{4,12},{5,13},{6,14},{7,15},{8,16},{9,17... | collective-permute-start | bytes 344072 | tf_op jit(solution)/shard_map/ppermute | solution.py:26
  4.4 2.6 %collective-permute-start.1 = (bf16[8,7168]{1,0:T(8,128)(2,1)}, bf16[8,7168]{1,0:T(8,128)(2,1)S(1)}, u32[]{:S(2)}, u32[]{:S(2)}) collective-permute-start(bf16[8,7168]{1,0:T(8,128)(2,1)} %param.16), channel_id=1, source_target_pairs={{0,16},{1,17},{2,18},{3,19},{4,20},{5,21},{6,22},{7,23},{8,24},{9,... | collective-permute-start | bytes 344072 | tf_op jit(solution)/shard_map/ppermute | solution.py:26
  7.0 1.3 %collective-permute-start.2 = (bf16[8,7168]{1,0:T(8,128)(2,1)}, bf16[8,7168]{1,0:T(8,128)(2,1)S(1)}, u32[]{:S(2)}, u32[]{:S(2)}) collective-permute-start(bf16[8,7168]{1,0:T(8,128)(2,1)} %param.16), channel_id=1, source_target_pairs={{0,24},{1,25},{2,26},{3,27},{4,28},{5,29},{6,30},{7,31},{8,0},{9,1... | collective-permute-start | bytes 344072 | tf_op jit(solution)/shard_map/ppermute | solution.py:26
  8.4 0.7 fusion.5
  9.0 3.2 %fusion.3 = (f32[8]{0:T(128)S(1)}, f32[8]{0:T(128)S(1)}, f32[8]{0:T(128)S(1)}, f32[8]{0:T(128)S(1)}) fusion(f32[8,2]{0,1:T(2,128)} %param.18, s32[8,2]{0,1:T(2,128)} %param.17, s32[]{:T(128)} %bitcast.4, s32[]{:T(128)} %bitcast.2, s32[]{:T(128)} %bitcast.1, s32[]{:T(128)} %bitcast.3), kind=kLoop, calls=%fused_computation.21 | loop fusion | flops 160 | bytes 272 | tf_op jit(solution)/shard_map/reduce_sum | solution.py:213
  12.3 0.0 collective-permute-done
  12.3 1.9 %collective-permute-done.1 = bf16[8,7168]{1,0:T(8,128)(2,1)S(1)} collective-permute-done((bf16[8,7168]{1,0:T(8,128)(2,1)}, bf16[8,7168]{1,0:T(8,128)(2,1)S(1)}, u32[]{:S(2)}, u32[]{:S(2)}) %collective-permute-start.1) | collective-permute-done | bytes 114720 | tf_op jit(solution)/shard_map/ppermute | solution.py:26
  14.2 0.4 collective-permute-done.2
  14.6 0.0 collective-permute-done.3.early
  14.6 1.0 constant_dynamic-update-slice_fusion.3
  15.6 5.6 %collective-permute-start.4 = (bf16[32,7168]{1,0:T(8,128)(2,1)S(1)}, bf16[32,7168]{1,0:T(8,128)(2,1)S(1)}, u32[]{:S(2)}, u32[]{:S(2)}) collective-permute-start(bf16[32,7168]{1,0:T(8,128)(2,1)S(1)} %constant_dynamic-update-slice_fusion.refs_0_), channel_id=1, source_target_pairs={{0,4},{1,3},{2,6},{3,1},{4,0},{5,7},{6,2},{7,5},{8,12},{9,11},{10,... | collective-permute-start | bytes 1376264 | tf_op jit(solution)/shard_map/ppermute | solution.py:26
  21.2 0.0 collective-permute-start.7
  21.2 0.6 collective-permute-start.5
  21.8 10.3 %collective-permute-done.4.refs_1_ = bf16[32,7168]{1,0:T(8,128)(2,1)S(1)} collective-permute-done((bf16[32,7168]{1,0:T(8,128)(2,1)S(1)}, bf16[32,7168]{1,0:T(8,128)(2,1)S(1)}, u32[]{:S(2)}, u32[]{:S(2)}) %collective-permute-start.4) | collective-permute-done | bytes 458784 | tf_op jit(solution)/shard_map/ppermute | solution.py:26
  32.2 0.5 collective-permute-start.6
  32.7 7.9 %collective-permute-done.6.refs_3_ = bf16[32,7168]{1,0:T(8,128)(2,1)S(1)} collective-permute-done((bf16[32,7168]{1,0:T(8,128)(2,1)S(1)}, bf16[32,7168]{1,0:T(8,128)(2,1)S(1)}, u32[]{:S(2)}, u32[]{:S(2)}) %collective-permute-start.6) | collective-permute-done | bytes 458784 | tf_op jit(solution)/shard_map/ppermute | solution.py:26
  40.6 0.5 collective-permute-start.11
  41.1 0.0 collective-permute-start.8
  41.1 0.5 collective-permute-start.9
  41.7 2.0 %copy-done = bf16[1,7168,256]{2,1,0:T(8,128)(2,1)S(1)} copy-done((bf16[1,7168,256]{2,1,0:T(8,128)(2,1)S(1)}, bf16[1,7168,256]{2,1,0:T(8,128)(2,1)}, u32[]{:S(2)}) %copy-start) | copy-done | bytes 3670040
  43.7 2.0 %copy-done.1 = bf16[1,7168,256]{2,1,0:T(8,128)(2,1)S(1)} copy-done((bf16[1,7168,256]{2,1,0:T(8,128)(2,1)S(1)}, bf16[1,7168,256]{2,1,0:T(8,128)(2,1)}, u32[]{:S(2)}) %copy-start.1) | copy-done | bytes 3670040
  45.7 2.0 %copy-done.2 = bf16[1,256,7168]{2,1,0:T(8,128)(2,1)S(1)} copy-done((bf16[1,256,7168]{2,1,0:T(8,128)(2,1)S(1)}, bf16[1,256,7168]{2,1,0:T(8,128)(2,1)}, u32[]{:S(2)}) %copy-start.2) | copy-done | bytes 3670040
  47.8 0.8 shard_map.122
  48.6 0.0 collective-permute-done.10.refs_6_
  48.6 0.0 collective-permute-done.8.refs_4_
  48.6 0.0 copy-start.3
  48.6 0.0 copy-start.7
  48.6 5.3 %shard_map.123 = (bf16[128,7168]{1,0:T(8,128)(2,1)S(1)}, bf16[64,7168]{1,0:T(8,128)(2,1)S(1)}, bf16[64,7168]{1,0:T(8,128)(2,1)S(1)}) custom-call(bf16[32,7168]{1,0:T(8,128)(2,1)S(1)} %constant_dynamic-update-slice_fusion.refs_0_, bf16[32,7168]{1,0:T(8,128)(2,1)S(1)} %collective-permute-done.4.refs_1_, bf16[32,7168]{1,0:T(8,128)(2,1)S(1)} %collective-permute-done.5.refs_2_, ...), custom_call_target="tpu_custom_call" | custom-call | flops 2818572288 | bytes 18350080 | tf_op jit(solution)/shard_map/pallas_call | solution.py:167
  53.9 0.1 collective-permute-start.13
  54.0 0.7 collective-permute-start.14
  54.8 1.1 %collective-permute-start.12 = (bf16[64,7168]{1,0:T(8,128)(2,1)S(1)}, bf16[64,7168]{1,0:T(8,128)(2,1)}, u32[]{:S(2)}, u32[]{:S(2)}) collective-permute-start(bf16[64,7168]{1,0:T(8,128)(2,1)S(1)} %get-tuple-element.40), channel_id=1, source_target_pairs={{0,1},{1,0},{2,3},{3,2},{4,5},{5,4},{6,7},{7,6},{8,9},{9,8},{10,11... | collective-permute-start | bytes 2752520 | tf_op jit(solution)/shard_map/ppermute | solution.py:26
  55.9 0.6 collective-permute-done.13
  56.5 1.1 %add_convert_fusion = (bf16[32,7168]{1,0:T(8,128)(2,1)}, bf16[32,7168]{1,0:T(8,128)(2,1)}) fusion(bf16[64,7168]{1,0:T(8,128)(2,1)S(1)} %collective-permute-done.13, bf16[128,7168]{1,0:T(8,128)(2,1)S(1)} %get-tuple-element.39), kind=kLoop, calls=%fused_computation | loop fusion | flops 1835008 | bytes 2752512 | tf_op jit(solution)/shard_map/convert_element_type | solution.py:261
  57.6 0.9 copy-done.6
  58.6 12.0 %collective-permute-start.15 = (bf16[32,7168]{1,0:T(8,128)(2,1)}, bf16[32,7168]{1,0:T(8,128)(2,1)S(1)}, u32[]{:S(2)}, u32[]{:S(2)}) collective-permute-start(bf16[32,7168]{1,0:T(8,128)(2,1)} %get-tuple-element.43), channel_id=1, source_target_pairs={{0,2},{1,5},{2,0},{3,7},{4,6},{5,1},{6,4},{7,3},{8,10},{9,13},{10,... | collective-permute-start | bytes 1376264 | tf_op jit(solution)/shard_map/ppermute | solution.py:26
  70.6 0.6 copy.13.newest
  71.2 0.0 collective-permute-start.16
  71.2 8.7 %shard_map.124 = bf16[8,64,512]{2,1,0:T(8,128)(2,1)} custom-call(s32[8]{0:T(128)} %parents.1, s32[8]{0:T(128)} %lengths.1, bf16[8,64,576]{2,1,0:T(8,128)(2,1)} %query.1, bf16[8,96,576]{2,1,0:T(8,128)(2,1)} %own, bf16[8,96,576]{2,1,0:T(8,128)(2,1)} %copy-done.5, bf16[8,96,576]{2,1,0:T(8,128)(2,1)} %copy-done.4, bf16[8,96,576]{2,1,0:T(8,128)(2,1)} %copy-done.6, ...), custom_call_target="tpu_custom_call" | custom-call | flops 106954752 | bytes 4653056 | tf_op jit(solution)/shard_map/pallas_call | solution.py:82
  79.9 1.2 %add_convert_fusion.1 = bf16[32,7168]{1,0:T(8,128)(2,1)S(1)} fusion(bf16[32,7168]{1,0:T(8,128)(2,1)S(1)} %collective-permute-done.15, bf16[64,7168]{1,0:T(8,128)(2,1)} %collective-permute-done.12, bf16[128,7168]{1,0:T(8,128)(2,1)S(1)} %get-tuple-element.39), kind=kLoop, calls=%fused_computation.1 | loop fusion | flops 1376256 | bytes 1835008 | tf_op jit(solution)/shard_map/convert_element_type | solution.py:263
  81.1 2.2 %collective-permute-start.17 = (bf16[32,7168]{1,0:T(8,128)(2,1)S(1)}, bf16[32,7168]{1,0:T(8,128)(2,1)S(1)}, u32[]{:S(2)}, u32[]{:S(2)}) collective-permute-start(bf16[32,7168]{1,0:T(8,128)(2,1)S(1)} %add_convert_fusion.1), channel_id=1, source_target_pairs={{0,4},{1,3},{2,6},{3,1},{4,0},{5,7},{6,2},{7,5},{8,12},{9,11},{10,... | collective-permute-start | bytes 1376264 | tf_op jit(solution)/shard_map/ppermute | solution.py:26
  83.3 6.5 %collective-permute-done.17 = bf16[32,7168]{1,0:T(8,128)(2,1)S(1)} collective-permute-done((bf16[32,7168]{1,0:T(8,128)(2,1)S(1)}, bf16[32,7168]{1,0:T(8,128)(2,1)S(1)}, u32[]{:S(2)}, u32[]{:S(2)}) %collective-permute-start.17) | collective-permute-done | bytes 458784 | tf_op jit(solution)/shard_map/ppermute | solution.py:26
  89.7 1.4 %add_convert_fusion.6 = (bf16[8,7168]{1,0:T(8,128)(2,1)S(1)}, bf16[8,7168]{1,0:T(8,128)(2,1)S(1)}, bf16[8,7168]{1,0:T(8,128)(2,1)S(1)}) fusion(bf16[32,7168]{1,0:T(8,128)(2,1)S(1)} %collective-permute-done.17, bf16[32,7168]{1,0:T(8,128)(2,1)} %collective-permute-done.16, bf16[64,7168]{1,0:T(8,128)(2,1)} %collective-permute-done.12, ...), kind=kLoop, calls=%fused_computation.6 | loop fusion | flops 1376256 | bytes 1720320 | tf_op jit(solution)/shard_map/convert_element_type | solution.py:271
  91.1 7.2 %collective-permute-start.18 = (bf16[8,7168]{1,0:T(8,128)(2,1)S(1)}, bf16[8,7168]{1,0:T(8,128)(2,1)S(1)}, u32[]{:S(2)}, u32[]{:S(2)}) collective-permute-start(bf16[8,7168]{1,0:T(8,128)(2,1)S(1)} %get-tuple-element.58), channel_id=1, source_target_pairs={{0,24},{1,25},{2,26},{3,27},{4,28},{5,29},{6,30},{7,31},{8,0},{9,1... | collective-permute-start | bytes 344072 | tf_op jit(solution)/shard_map/ppermute | solution.py:26
  98.3 1.1 %collective-permute-start.20 = (bf16[8,7168]{1,0:T(8,128)(2,1)S(1)}, bf16[8,7168]{1,0:T(8,128)(2,1)S(1)}, u32[]{:S(2)}, u32[]{:S(2)}) collective-permute-start(bf16[8,7168]{1,0:T(8,128)(2,1)S(1)} %get-tuple-element.59), channel_id=1, source_target_pairs={{0,8},{1,9},{2,10},{3,11},{4,12},{5,13},{6,14},{7,15},{8,16},{9,17... | collective-permute-start | bytes 344072 | tf_op jit(solution)/shard_map/ppermute | solution.py:26
  99.4 1.6 %collective-permute-done.18 = bf16[8,7168]{1,0:T(8,128)(2,1)S(1)} collective-permute-done((bf16[8,7168]{1,0:T(8,128)(2,1)S(1)}, bf16[8,7168]{1,0:T(8,128)(2,1)S(1)}, u32[]{:S(2)}, u32[]{:S(2)}) %collective-permute-start.18) | collective-permute-done | bytes 114720 | tf_op jit(solution)/shard_map/ppermute | solution.py:26
  101.0 6.7 %collective-permute-done.19 = bf16[8,7168]{1,0:T(8,128)(2,1)S(1)} collective-permute-done((bf16[8,7168]{1,0:T(8,128)(2,1)S(1)}, bf16[8,7168]{1,0:T(8,128)(2,1)S(1)}, u32[]{:S(2)}, u32[]{:S(2)}) %collective-permute-start.19) | collective-permute-done | bytes 114720 | tf_op jit(solution)/shard_map/ppermute | solution.py:26
  107.7 1.8 %add_convert_fusion.3 = bf16[8,7168]{1,0:T(8,128)(2,1)} fusion(bf16[8,7168]{1,0:T(8,128)(2,1)S(1)} %collective-permute-done.20, bf16[8,7168]{1,0:T(8,128)(2,1)S(1)} %collective-permute-done.19, bf16[8,7168]{1,0:T(8,128)(2,1)S(1)} %collective-permute-done.18, bf16[32,7168]{1,0:T(8,128)(2,1)S(1)} %collective-permute-done.17, ...), kind=kLoop, calls=%fused_computation.3 | loop fusion | flops 1032192 | bytes 917632 | tf_op jit(solution)/shard_map/convert_element_type | solution.py:283
  (25 shorter events, 0.1 us)
Async XLA Ops:
  0.6 13.9 %collective-permute-start.3 = (bf16[8,96,576]{2,1,0:T(8,128)(2,1)}, bf16[8,96,576]{2,1,0:T(8,128)(2,1)S(1)}, u32[]{:S(2)}, u32[]{:S(2)}) collective-permute-start(bf16[8,96,576]{2,1,0:T(8,128)(2,1)} %own), channel_id=1, source_target_pairs={{1,2},{3,4},{5,6},{6,5},{9,10},{11,12},{13,14},{14,13},{17,18},{19... | collective-permute-start | bytes 2654216 | tf_op jit(solution)/shard_map/ppermute | solution.py:43
  1.4 10.9 %collective-permute-start = (bf16[8,7168]{1,0:T(8,128)(2,1)}, bf16[8,7168]{1,0:T(8,128)(2,1)S(1)}, u32[]{:S(2)}, u32[]{:S(2)}) collective-permute-start(bf16[8,7168]{1,0:T(8,128)(2,1)} %param.16), channel_id=1, source_target_pairs={{0,8},{1,9},{2,10},{3,11},{4,12},{5,13},{6,14},{7,15},{8,16},{9,17... | collective-permute-start | bytes 344072 | tf_op jit(solution)/shard_map/ppermute | solution.py:26
  4.4 9.7 %collective-permute-start.1 = (bf16[8,7168]{1,0:T(8,128)(2,1)}, bf16[8,7168]{1,0:T(8,128)(2,1)S(1)}, u32[]{:S(2)}, u32[]{:S(2)}) collective-permute-start(bf16[8,7168]{1,0:T(8,128)(2,1)} %param.16), channel_id=1, source_target_pairs={{0,16},{1,17},{2,18},{3,19},{4,20},{5,21},{6,22},{7,23},{8,24},{9,... | collective-permute-start | bytes 344072 | tf_op jit(solution)/shard_map/ppermute | solution.py:26
  7.0 7.5 %collective-permute-start.2 = (bf16[8,7168]{1,0:T(8,128)(2,1)}, bf16[8,7168]{1,0:T(8,128)(2,1)S(1)}, u32[]{:S(2)}, u32[]{:S(2)}) collective-permute-start(bf16[8,7168]{1,0:T(8,128)(2,1)} %param.16), channel_id=1, source_target_pairs={{0,24},{1,25},{2,26},{3,27},{4,28},{5,29},{6,30},{7,31},{8,0},{9,1... | collective-permute-start | bytes 344072 | tf_op jit(solution)/shard_map/ppermute | solution.py:26
  14.6 34.0 %copy-start.4 = (bf16[8,96,576]{2,1,0:T(8,128)(2,1)}, bf16[8,96,576]{2,1,0:T(8,128)(2,1)S(1)}, u32[]{:S(2)}) copy-start(bf16[8,96,576]{2,1,0:T(8,128)(2,1)S(1)} %collective-permute-done.3.early) | copy-start | bytes 2654212
  15.6 16.5 %collective-permute-start.4 = (bf16[32,7168]{1,0:T(8,128)(2,1)S(1)}, bf16[32,7168]{1,0:T(8,128)(2,1)S(1)}, u32[]{:S(2)}, u32[]{:S(2)}) collective-permute-start(bf16[32,7168]{1,0:T(8,128)(2,1)S(1)} %constant_dynamic-update-slice_fusion.refs_0_), channel_id=1, source_target_pairs={{0,4},{1,3},{2,6},{3,1},{4,0},{5,7},{6,2},{7,5},{8,12},{9,11},{10,... | collective-permute-start | bytes 1376264 | tf_op jit(solution)/shard_map/ppermute | solution.py:26
  21.2 11.5 %collective-permute-start.7 = (bf16[8,96,576]{2,1,0:T(8,128)(2,1)}, bf16[8,96,576]{2,1,0:T(8,128)(2,1)S(1)}, u32[]{:S(2)}, u32[]{:S(2)}) collective-permute-start(bf16[8,96,576]{2,1,0:T(8,128)(2,1)} %own), channel_id=1, source_target_pairs={{0,1},{1,0},{2,3},{3,2},{4,5},{5,4},{6,7},{7,6},{8,9},{9,8},{10,11... | collective-permute-start | bytes 2654216 | tf_op jit(solution)/shard_map/ppermute | solution.py:26
  21.2 11.5 %collective-permute-start.5 = (bf16[32,7168]{1,0:T(8,128)(2,1)S(1)}, bf16[32,7168]{1,0:T(8,128)(2,1)S(1)}, u32[]{:S(2)}, u32[]{:S(2)}) collective-permute-start(bf16[32,7168]{1,0:T(8,128)(2,1)S(1)} %constant_dynamic-update-slice_fusion.refs_0_), channel_id=1, source_target_pairs={{0,2},{1,5},{2,0},{3,7},{4,6},{5,1},{6,4},{7,3},{8,10},{9,13},{10,... | collective-permute-start | bytes 1376264 | tf_op jit(solution)/shard_map/ppermute | solution.py:26
  32.2 8.5 %collective-permute-start.6 = (bf16[32,7168]{1,0:T(8,128)(2,1)S(1)}, bf16[32,7168]{1,0:T(8,128)(2,1)S(1)}, u32[]{:S(2)}, u32[]{:S(2)}) collective-permute-start(bf16[32,7168]{1,0:T(8,128)(2,1)S(1)} %collective-permute-done.4.refs_1_), channel_id=1, source_target_pairs={{0,2},{1,5},{2,0},{3,7},{4,6},{5,1},{6,4},{7,3},{8,10},{9,13},{10,... | collective-permute-start | bytes 1376264 | tf_op jit(solution)/shard_map/ppermute | solution.py:26
  32.7 15.9 %copy-start.5 = (bf16[8,96,576]{2,1,0:T(8,128)(2,1)}, bf16[8,96,576]{2,1,0:T(8,128)(2,1)S(1)}, u32[]{:S(2)}) copy-start(bf16[8,96,576]{2,1,0:T(8,128)(2,1)S(1)} %collective-permute-done.7.twin) | copy-start | bytes 2654212
  40.6 7.9 %collective-permute-start.10 = (bf16[32,7168]{1,0:T(8,128)(2,1)S(1)}, bf16[32,7168]{1,0:T(8,128)(2,1)S(1)}, u32[]{:S(2)}, u32[]{:S(2)}) collective-permute-start(bf16[32,7168]{1,0:T(8,128)(2,1)S(1)} %collective-permute-done.5.refs_2_), channel_id=1, source_target_pairs={{0,1},{1,0},{2,3},{3,2},{4,5},{5,4},{6,7},{7,6},{8,9},{9,8},{10,11... | collective-permute-start | bytes 1376264 | tf_op jit(solution)/shard_map/ppermute | solution.py:26
  40.6 7.9 %collective-permute-start.11 = (bf16[32,7168]{1,0:T(8,128)(2,1)S(1)}, bf16[32,7168]{1,0:T(8,128)(2,1)S(1)}, u32[]{:S(2)}, u32[]{:S(2)}) collective-permute-start(bf16[32,7168]{1,0:T(8,128)(2,1)S(1)} %collective-permute-done.6.refs_3_), channel_id=1, source_target_pairs={{0,1},{1,0},{2,3},{3,2},{4,5},{5,4},{6,7},{7,6},{8,9},{9,8},{10,11... | collective-permute-start | bytes 1376264 | tf_op jit(solution)/shard_map/ppermute | solution.py:26
  41.1 7.4 %collective-permute-start.8 = (bf16[32,7168]{1,0:T(8,128)(2,1)S(1)}, bf16[32,7168]{1,0:T(8,128)(2,1)S(1)}, u32[]{:S(2)}, u32[]{:S(2)}) collective-permute-start(bf16[32,7168]{1,0:T(8,128)(2,1)S(1)} %constant_dynamic-update-slice_fusion.refs_0_), channel_id=1, source_target_pairs={{0,1},{1,0},{2,3},{3,2},{4,5},{5,4},{6,7},{7,6},{8,9},{9,8},{10,11... | collective-permute-start | bytes 1376264 | tf_op jit(solution)/shard_map/ppermute | solution.py:26
  41.1 7.4 %collective-permute-start.9 = (bf16[32,7168]{1,0:T(8,128)(2,1)S(1)}, bf16[32,7168]{1,0:T(8,128)(2,1)S(1)}, u32[]{:S(2)}, u32[]{:S(2)}) collective-permute-start(bf16[32,7168]{1,0:T(8,128)(2,1)S(1)} %collective-permute-done.4.refs_1_), channel_id=1, source_target_pairs={{0,1},{1,0},{2,3},{3,2},{4,5},{5,4},{6,7},{7,6},{8,9},{9,8},{10,11... | collective-permute-start | bytes 1376264 | tf_op jit(solution)/shard_map/ppermute | solution.py:26
  41.7 2.0 %copy-start = (bf16[1,7168,256]{2,1,0:T(8,128)(2,1)S(1)}, bf16[1,7168,256]{2,1,0:T(8,128)(2,1)}, u32[]{:S(2)}) copy-start(bf16[1,7168,256]{2,1,0:T(8,128)(2,1)} %refs_0_.1) | copy-start | bytes 11010052
  43.7 2.0 %copy-start.1 = (bf16[1,7168,256]{2,1,0:T(8,128)(2,1)S(1)}, bf16[1,7168,256]{2,1,0:T(8,128)(2,1)}, u32[]{:S(2)}) copy-start(bf16[1,7168,256]{2,1,0:T(8,128)(2,1)} %refs_1_.1) | copy-start | bytes 11010052
  45.7 2.0 %copy-start.2 = (bf16[1,256,7168]{2,1,0:T(8,128)(2,1)S(1)}, bf16[1,256,7168]{2,1,0:T(8,128)(2,1)}, u32[]{:S(2)}) copy-start(bf16[1,256,7168]{2,1,0:T(8,128)(2,1)} %refs_2_.1) | copy-start | bytes 11010052
  48.6 5.4 %copy-start.3 = (bf16[8,96,576]{2,1,0:T(8,128)(2,1)S(1)}, bf16[8,96,576]{2,1,0:T(8,128)(2,1)}, u32[]{:S(2)}) copy-start(bf16[8,96,576]{2,1,0:T(8,128)(2,1)} %own) | copy-start | bytes 2654212
  48.6 22.0 %copy-start.7 = (bf16[8,576]{1,0:T(8,128)(2,1)S(1)}, bf16[8,576]{1,0:T(8,128)(2,1)}, u32[]{:S(2)}) copy-start(bf16[8,576]{1,0:T(8,128)(2,1)} %param.13) | copy-start | bytes 27652
  53.9 2.5 %collective-permute-start.13 = (bf16[64,7168]{1,0:T(8,128)(2,1)S(1)}, bf16[64,7168]{1,0:T(8,128)(2,1)S(1)}, u32[]{:S(2)}, u32[]{:S(2)}) collective-permute-start(bf16[64,7168]{1,0:T(8,128)(2,1)S(1)} %get-tuple-element.41), channel_id=1, source_target_pairs={{0,1},{1,0},{2,3},{3,2},{4,5},{5,4},{6,7},{7,6},{8,9},{9,8},{10,11... | collective-permute-start | bytes 2752520 | tf_op jit(solution)/shard_map/ppermute | solution.py:26
  54.0 3.6 %collective-permute-start.14 = (bf16[8,96,576]{2,1,0:T(8,128)(2,1)S(1)}, bf16[8,96,576]{2,1,0:T(8,128)(2,1)S(1)}, u32[]{:S(2)}, u32[]{:S(2)}) collective-permute-start(bf16[8,96,576]{2,1,0:T(8,128)(2,1)S(1)} %copy-done.3), channel_id=1, source_target_pairs={{2,1},{4,3},{7,8},{8,7},{10,9},{12,11},{15,16},{16,15},{18,17},{20... | collective-permute-start | bytes 2654216 | tf_op jit(solution)/shard_map/ppermute | solution.py:43
  54.8 25.1 %collective-permute-start.12 = (bf16[64,7168]{1,0:T(8,128)(2,1)S(1)}, bf16[64,7168]{1,0:T(8,128)(2,1)}, u32[]{:S(2)}, u32[]{:S(2)}) collective-permute-start(bf16[64,7168]{1,0:T(8,128)(2,1)S(1)} %get-tuple-element.40), channel_id=1, source_target_pairs={{0,1},{1,0},{2,3},{3,2},{4,5},{5,4},{6,7},{7,6},{8,9},{9,8},{10,11... | collective-permute-start | bytes 2752520 | tf_op jit(solution)/shard_map/ppermute | solution.py:26
  57.6 1.0 copy-start.6
  58.6 21.3 %collective-permute-start.15 = (bf16[32,7168]{1,0:T(8,128)(2,1)}, bf16[32,7168]{1,0:T(8,128)(2,1)S(1)}, u32[]{:S(2)}, u32[]{:S(2)}) collective-permute-start(bf16[32,7168]{1,0:T(8,128)(2,1)} %get-tuple-element.43), channel_id=1, source_target_pairs={{0,2},{1,5},{2,0},{3,7},{4,6},{5,1},{6,4},{7,3},{8,10},{9,13},{10,... | collective-permute-start | bytes 1376264 | tf_op jit(solution)/shard_map/ppermute | solution.py:26
  71.2 12.0 %collective-permute-start.16 = (bf16[32,7168]{1,0:T(8,128)(2,1)}, bf16[32,7168]{1,0:T(8,128)(2,1)}, u32[]{:S(2)}, u32[]{:S(2)}) collective-permute-start(bf16[32,7168]{1,0:T(8,128)(2,1)} %get-tuple-element.61), channel_id=1, source_target_pairs={{0,2},{1,5},{2,0},{3,7},{4,6},{5,1},{6,4},{7,3},{8,10},{9,13},{10,... | collective-permute-start | bytes 1376264 | tf_op jit(solution)/shard_map/ppermute | solution.py:26
  81.1 8.6 %collective-permute-start.17 = (bf16[32,7168]{1,0:T(8,128)(2,1)S(1)}, bf16[32,7168]{1,0:T(8,128)(2,1)S(1)}, u32[]{:S(2)}, u32[]{:S(2)}) collective-permute-start(bf16[32,7168]{1,0:T(8,128)(2,1)S(1)} %add_convert_fusion.1), channel_id=1, source_target_pairs={{0,4},{1,3},{2,6},{3,1},{4,0},{5,7},{6,2},{7,5},{8,12},{9,11},{10,... | collective-permute-start | bytes 1376264 | tf_op jit(solution)/shard_map/ppermute | solution.py:26
  91.1 9.9 %collective-permute-start.18 = (bf16[8,7168]{1,0:T(8,128)(2,1)S(1)}, bf16[8,7168]{1,0:T(8,128)(2,1)S(1)}, u32[]{:S(2)}, u32[]{:S(2)}) collective-permute-start(bf16[8,7168]{1,0:T(8,128)(2,1)S(1)} %get-tuple-element.58), channel_id=1, source_target_pairs={{0,24},{1,25},{2,26},{3,27},{4,28},{5,29},{6,30},{7,31},{8,0},{9,1... | collective-permute-start | bytes 344072 | tf_op jit(solution)/shard_map/ppermute | solution.py:26
  98.3 9.5 %collective-permute-start.19 = (bf16[8,7168]{1,0:T(8,128)(2,1)S(1)}, bf16[8,7168]{1,0:T(8,128)(2,1)S(1)}, u32[]{:S(2)}, u32[]{:S(2)}) collective-permute-start(bf16[8,7168]{1,0:T(8,128)(2,1)S(1)} %get-tuple-element.60), channel_id=1, source_target_pairs={{0,16},{1,17},{2,18},{3,19},{4,20},{5,21},{6,22},{7,23},{8,24},{9,... | collective-permute-start | bytes 344072 | tf_op jit(solution)/shard_map/ppermute | solution.py:26
  98.3 9.5 %collective-permute-start.20 = (bf16[8,7168]{1,0:T(8,128)(2,1)S(1)}, bf16[8,7168]{1,0:T(8,128)(2,1)S(1)}, u32[]{:S(2)}, u32[]{:S(2)}) collective-permute-start(bf16[8,7168]{1,0:T(8,128)(2,1)S(1)} %get-tuple-element.59), channel_id=1, source_target_pairs={{0,8},{1,9},{2,10},{3,11},{4,12},{5,13},{6,14},{7,15},{8,16},{9,17... | collective-permute-start | bytes 344072 | tf_op jit(solution)/shard_map/ppermute | solution.py:26

commit v7 on v6

--- a/solution.py
+++ b/solution.py
@@ -114,7 +114,7 @@
 def fetched(weights):
     return pl.pallas_call(
         fetch_kernel,
-        in_specs=[pl.BlockSpec(memory_space=pl.ANY)] * len(weights),
+        in_specs=[pl.BlockSpec(memory_space=pltpu.HBM)] * len(weights),
         out_specs=[pl.BlockSpec(memory_space=pltpu.VMEM)] * len(weights),
         out_shape=[pltpu.VMEM(w.shape, w.dtype) for w in weights],
         scratch_shapes=[pltpu.SemaphoreType.DMA((len(weights),))],
@@ -124,7 +124,7 @@
             bytes_accessed=2 * sum(w.size * w.dtype.itemsize for w in weights),
             transcendentals=0,
         ),
-    )(*weights)
+    )(*[pltpu.with_memory_space_constraint(w, pltpu.HBM) for w in weights])
 
 
 def expert_kernel(wide, *refs):
@@ -244,10 +244,14 @@
     across = swapped(near, second)
     beside = swapped(latent_cache, twin)
     held = [column, near, side, across]
-    *held, beside, latent_cache = lax.optimization_barrier((*held, beside, latent_cache))
+    weights = fetched([gate_weight, up_weight, down_weight])
+    held, weights, beside, latent_cache = lax.optimization_barrier(
+        (held, weights, beside, latent_cache)
+    )
     late = neighbours(latent_cache, LATE, slices)
     held = held + [swapped(value, twin) for value in held]
-    own, high, low = experts(held, fetched([gate_weight, up_weight, down_weight]))
+    own, high, low = experts(held, weights)
+    high, late = lax.optimization_barrier((high, late))
 
     high, low = swapped(high, twin), swapped(low, twin)
     height = expert_count * capacity
@@ -256,7 +260,6 @@
         return lax.slice_in_dim(value, j * height, (j + 1) * height)
 
     across = added([block(own, 3), block(high, 1)]).astype(jnp.bfloat16)
-    across, late = lax.optimization_barrier((across, late))
     across = swapped(across, second)
     side = swapped(added([block(own, 2), block(high, 0)]).astype(jnp.bfloat16), second)
     attention = attend(queries, latent_cache, beside, early, late, newest, parents, lengths)

time: 110 us -> 103 us (0.936)
  starting transfers between devices: 39.9 us -> 29.7 us
  waiting for transfers between devices: 35.9 us -> 43.2 us
  local copies, waits for them, and re-layouts: 9.39 us -> 2.27 us
  Pallas kernels: 14.7 us -> 18.3 us
    ppermute x19, starting transfers between devices: 38.5 us -> 28.1 us  [swapped(): return lax.ppermute(value, 'dp', [(i, partner(i)) for i in range(peers)])]
    ppermute x19, waiting for transfers between devices: 35.9 us -> 43.2 us  [swapped(): return lax.ppermute(value, 'dp', [(i, partner(i)) for i in range(peers)])]
    unnamed x19 -> x13, local copies, waits for them, and re-layouts: 8.11 us -> 1.04 us
    pallas_call x1, Pallas kernels: 0.76 us -> 4.23 us  [fetched(): pl.pallas_call(fetch_kernel, in_specs=[pl.BlockSpec(memory_space=pltpu.HB...]
  transfers between devices with their start and end apart: 21 -> 21, of which waited for: 8 -> 12; matrix products, arithmetic and copies ran while one was open for 6% -> 7% of each run, Pallas kernels for 9% -> 18%
where the time goes in v7:
time: 103 us
  waiting for transfers between devices  43.2 us (42%)
  starting transfers between devices  29.7 us (29%)
  Pallas kernels  18.3 us (18%)
  other arithmetic  8.41 us (8%)
  local copies, waits for them, and re-layouts  2.27 us (2%)
    ppermute x19, waiting for transfers between devices, swapped(): return lax.ppermute(value, 'dp', [(i, partner(i)) for i in range(peers)])  43.2 us
    ppermute x19, starting transfers between devices, swapped(): return lax.ppermute(value, 'dp', [(i, partner(i)) for i in range(peers)])  28.1 us
    pallas_call x1, Pallas kernels, attend(): pl.pallas_call(attend_kernel, grid_spec=pltpu.PrefetchScalarGridSpec(num_...  8.76 us
    pallas_call x1, Pallas kernels, experts(): pl.pallas_call(lambda *refs: expert_kernel(wide, *refs), in_specs=[whole]...  5.3 us
    pallas_call x1, Pallas kernels, fetched(): pl.pallas_call(fetch_kernel, in_specs=[pl.BlockSpec(memory_space=pltpu.HB...  4.23 us
    reduce_sum x1, other arithmetic, body(): jnp.sum(jnp.where(routed_experts == targets[r], route_weights, 0.0), axis=1)  3.19 us
  transfers between devices with their start and end apart: 21, of which 12 were waited for; matrix products, arithmetic and copies ran while one was open for 7% of the time, Pallas kernels for 18%

profile of v7, /device:TPU:0, one launch (start us, length us, event | category | flops | bytes accessed | tf_op | source)
XLA Modules:
  0.0 102.7 jit_solution(5266311277278050411)
XLA Ops:
  0.6 0.7 collective-permute-start.3
  1.4 3.1 %collective-permute-start = (bf16[8,7168]{1,0:T(8,128)(2,1)}, bf16[8,7168]{1,0:T(8,128)(2,1)S(1)}, u32[]{:S(2)}, u32[]{:S(2)}) collective-permute-start(bf16[8,7168]{1,0:T(8,128)(2,1)} %param.16), channel_id=1, source_target_pairs={{0,8},{1,9},{2,10},{3,11},{4,12},{5,13},{6,14},{7,15},{8,16},{9,17... | collective-permute-start | bytes 344072 | tf_op jit(solution)/shard_map/ppermute | solution.py:26
  4.4 2.6 %collective-permute-start.1 = (bf16[8,7168]{1,0:T(8,128)(2,1)}, bf16[8,7168]{1,0:T(8,128)(2,1)S(1)}, u32[]{:S(2)}, u32[]{:S(2)}) collective-permute-start(bf16[8,7168]{1,0:T(8,128)(2,1)} %param.16), channel_id=1, source_target_pairs={{0,16},{1,17},{2,18},{3,19},{4,20},{5,21},{6,22},{7,23},{8,24},{9,... | collective-permute-start | bytes 344072 | tf_op jit(solution)/shard_map/ppermute | solution.py:26
  7.0 1.3 %collective-permute-start.2 = (bf16[8,7168]{1,0:T(8,128)(2,1)}, bf16[8,7168]{1,0:T(8,128)(2,1)S(1)}, u32[]{:S(2)}, u32[]{:S(2)}) collective-permute-start(bf16[8,7168]{1,0:T(8,128)(2,1)} %param.16), channel_id=1, source_target_pairs={{0,24},{1,25},{2,26},{3,27},{4,28},{5,29},{6,30},{7,31},{8,0},{9,1... | collective-permute-start | bytes 344072 | tf_op jit(solution)/shard_map/ppermute | solution.py:26
  8.4 0.6 fusion.5
  9.0 3.2 %fusion.3 = (f32[8]{0:T(128)S(1)}, f32[8]{0:T(128)S(1)}, f32[8]{0:T(128)S(1)}, f32[8]{0:T(128)S(1)}) fusion(f32[8,2]{0,1:T(2,128)} %param.18, s32[8,2]{0,1:T(2,128)} %param.17, s32[]{:T(128)} %bitcast.4, s32[]{:T(128)} %bitcast.2, s32[]{:T(128)} %bitcast.1, s32[]{:T(128)} %bitcast.3), kind=kLoop, calls=%fused_computation.21 | loop fusion | flops 160 | bytes 272 | tf_op jit(solution)/shard_map/reduce_sum | solution.py:213
  12.2 0.0 collective-permute-done
  12.2 2.0 %collective-permute-done.1 = bf16[8,7168]{1,0:T(8,128)(2,1)S(1)} collective-permute-done((bf16[8,7168]{1,0:T(8,128)(2,1)}, bf16[8,7168]{1,0:T(8,128)(2,1)S(1)}, u32[]{:S(2)}, u32[]{:S(2)}) %collective-permute-start.1) | collective-permute-done | bytes 114720 | tf_op jit(solution)/shard_map/ppermute | solution.py:26
  14.2 0.4 collective-permute-done.2
  14.6 0.0 collective-permute-done.3.early
  14.6 1.0 constant_dynamic-update-slice_fusion.3
  15.6 0.0 copy-start
  15.6 5.6 %collective-permute-start.4 = (bf16[32,7168]{1,0:T(8,128)(2,1)S(1)}, bf16[32,7168]{1,0:T(8,128)(2,1)S(1)}, u32[]{:S(2)}, u32[]{:S(2)}) collective-permute-start(bf16[32,7168]{1,0:T(8,128)(2,1)S(1)} %constant_dynamic-update-slice_fusion.refs_0_), channel_id=1, source_target_pairs={{0,4},{1,3},{2,6},{3,1},{4,0},{5,7},{6,2},{7,5},{8,12},{9,11},{10,... | collective-permute-start | bytes 1376264 | tf_op jit(solution)/shard_map/ppermute | solution.py:26
  21.3 0.6 collective-permute-start.5
  21.8 10.3 %collective-permute-done.4.refs_1_ = bf16[32,7168]{1,0:T(8,128)(2,1)S(1)} collective-permute-done((bf16[32,7168]{1,0:T(8,128)(2,1)S(1)}, bf16[32,7168]{1,0:T(8,128)(2,1)S(1)}, u32[]{:S(2)}, u32[]{:S(2)}) %collective-permute-start.4) | collective-permute-done | bytes 458784 | tf_op jit(solution)/shard_map/ppermute | solution.py:26
  32.2 0.5 collective-permute-start.6
  32.7 4.2 %shard_map.122 = (bf16[1,7168,256]{2,1,0:T(8,128)(2,1)S(1)}, bf16[1,7168,256]{2,1,0:T(8,128)(2,1)S(1)}, bf16[1,256,7168]{2,1,0:T(8,128)(2,1)S(1)}) custom-call(bf16[1,7168,256]{2,1,0:T(8,128)(2,1)} %refs_0_.1, bf16[1,7168,256]{2,1,0:T(8,128)(2,1)} %refs_1_.1, bf16[1,256,7168]{2,1,0:T(8,128)(2,1)} %refs_2_.1), custom_call_target="tpu_custom_call" | custom-call | bytes 22020096 | tf_op jit(solution)/shard_map/pallas_call | solution.py:115
  37.0 0.0 collective-permute-done.7.twin
  37.0 3.7 %collective-permute-done.6.refs_3_ = bf16[32,7168]{1,0:T(8,128)(2,1)S(1)} collective-permute-done((bf16[32,7168]{1,0:T(8,128)(2,1)S(1)}, bf16[32,7168]{1,0:T(8,128)(2,1)S(1)}, u32[]{:S(2)}, u32[]{:S(2)}) %collective-permute-start.6) | collective-permute-done | bytes 458784 | tf_op jit(solution)/shard_map/ppermute | solution.py:26
  40.7 0.9 collective-permute-start.13
  41.5 0.1 collective-permute-start.10
  41.6 0.5 collective-permute-start.11
  42.1 0.1 collective-permute-start.8
  42.2 0.4 collective-permute-start.9
  42.6 0.8 collective-permute-done.10.refs_6_
  43.4 0.7 collective-permute-done.11.refs_7_
  44.0 0.7 collective-permute-done.8.refs_4_
  44.7 0.7 collective-permute-done.9.refs_5_
  45.4 5.3 %shard_map.123 = (bf16[128,7168]{1,0:T(8,128)(2,1)S(1)}, bf16[64,7168]{1,0:T(8,128)(2,1)S(1)}, bf16[64,7168]{1,0:T(8,128)(2,1)S(1)}) custom-call(bf16[32,7168]{1,0:T(8,128)(2,1)S(1)} %constant_dynamic-update-slice_fusion.refs_0_, bf16[32,7168]{1,0:T(8,128)(2,1)S(1)} %collective-permute-done.4.refs_1_, bf16[32,7168]{1,0:T(8,128)(2,1)S(1)} %collective-permute-done.5.refs_2_, ...), custom_call_target="tpu_custom_call" | custom-call | flops 2818572288 | bytes 18350080 | tf_op jit(solution)/shard_map/pallas_call | solution.py:167
  50.7 3.8 %collective-permute-start.14 = (bf16[64,7168]{1,0:T(8,128)(2,1)S(1)}, bf16[64,7168]{1,0:T(8,128)(2,1)S(1)}, u32[]{:S(2)}, u32[]{:S(2)}) collective-permute-start(bf16[64,7168]{1,0:T(8,128)(2,1)S(1)} %get-tuple-element.49), channel_id=1, source_target_pairs={{0,1},{1,0},{2,3},{3,2},{4,5},{5,4},{6,7},{7,6},{8,9},{9,8},{10,11... | collective-permute-start | bytes 2752520 | tf_op jit(solution)/shard_map/ppermute | solution.py:26
  54.5 0.0 collective-permute-start.12
  54.5 3.4 %collective-permute-done.14 = bf16[64,7168]{1,0:T(8,128)(2,1)S(1)} collective-permute-done((bf16[64,7168]{1,0:T(8,128)(2,1)S(1)}, bf16[64,7168]{1,0:T(8,128)(2,1)S(1)}, u32[]{:S(2)}, u32[]{:S(2)}) %collective-permute-start.14) | collective-permute-done | bytes 917536 | tf_op jit(solution)/shard_map/ppermute | solution.py:26
  57.9 1.1 %add_convert_fusion = (bf16[32,7168]{1,0:T(8,128)(2,1)}, bf16[32,7168]{1,0:T(8,128)(2,1)}) fusion(bf16[64,7168]{1,0:T(8,128)(2,1)S(1)} %collective-permute-done.14, bf16[128,7168]{1,0:T(8,128)(2,1)S(1)} %get-tuple-element.45), kind=kLoop, calls=%fused_computation | loop fusion | flops 1835008 | bytes 2752512 | tf_op jit(solution)/shard_map/convert_element_type | solution.py:264
  59.0 3.4 %collective-permute-start.15 = (bf16[32,7168]{1,0:T(8,128)(2,1)}, bf16[32,7168]{1,0:T(8,128)(2,1)S(1)}, u32[]{:S(2)}, u32[]{:S(2)}) collective-permute-start(bf16[32,7168]{1,0:T(8,128)(2,1)} %get-tuple-element.68), channel_id=1, source_target_pairs={{0,2},{1,5},{2,0},{3,7},{4,6},{5,1},{6,4},{7,3},{8,10},{9,13},{10,... | collective-permute-start | bytes 1376264 | tf_op jit(solution)/shard_map/ppermute | solution.py:26
  62.4 0.6 copy.13.newest
  63.0 8.8 %shard_map.124 = bf16[8,64,512]{2,1,0:T(8,128)(2,1)} custom-call(s32[8]{0:T(128)} %parents.1, s32[8]{0:T(128)} %lengths.1, bf16[8,64,576]{2,1,0:T(8,128)(2,1)} %query.1, bf16[8,96,576]{2,1,0:T(8,128)(2,1)} %own, bf16[8,96,576]{2,1,0:T(8,128)(2,1)} %copy-done.2, bf16[8,96,576]{2,1,0:T(8,128)(2,1)} %copy-done.1, bf16[8,96,576]{2,1,0:T(8,128)(2,1)} %copy-done.3, ...), custom_call_target="tpu_custom_call" | custom-call | flops 106954752 | bytes 4653056 | tf_op jit(solution)/shard_map/pallas_call | solution.py:82
  71.8 0.0 collective-permute-start.16
  71.8 0.0 collective-permute-done.12
  71.8 0.0 collective-permute-done.15
  71.8 1.2 %add_convert_fusion.1 = bf16[32,7168]{1,0:T(8,128)(2,1)S(1)} fusion(bf16[32,7168]{1,0:T(8,128)(2,1)S(1)} %collective-permute-done.15, bf16[64,7168]{1,0:T(8,128)(2,1)} %collective-permute-done.12, bf16[128,7168]{1,0:T(8,128)(2,1)S(1)} %get-tuple-element.45), kind=kLoop, calls=%fused_computation.1 | loop fusion | flops 1376256 | bytes 1835008 | tf_op jit(solution)/shard_map/convert_element_type | solution.py:266
  73.0 1.2 %collective-permute-start.17 = (bf16[32,7168]{1,0:T(8,128)(2,1)S(1)}, bf16[32,7168]{1,0:T(8,128)(2,1)S(1)}, u32[]{:S(2)}, u32[]{:S(2)}) collective-permute-start(bf16[32,7168]{1,0:T(8,128)(2,1)S(1)} %add_convert_fusion.1), channel_id=1, source_target_pairs={{0,4},{1,3},{2,6},{3,1},{4,0},{5,7},{6,2},{7,5},{8,12},{9,11},{10,... | collective-permute-start | bytes 1376264 | tf_op jit(solution)/shard_map/ppermute | solution.py:26
  74.3 11.0 %collective-permute-done.16 = bf16[32,7168]{1,0:T(8,128)(2,1)S(1)} collective-permute-done((bf16[32,7168]{1,0:T(8,128)(2,1)}, bf16[32,7168]{1,0:T(8,128)(2,1)S(1)}, u32[]{:S(2)}, u32[]{:S(2)}) %collective-permute-start.16) | collective-permute-done | bytes 458784 | tf_op jit(solution)/shard_map/ppermute | solution.py:26
  85.2 1.2 %add_convert_fusion.6 = (bf16[8,7168]{1,0:T(8,128)(2,1)S(1)}, bf16[8,7168]{1,0:T(8,128)(2,1)S(1)}, bf16[8,7168]{1,0:T(8,128)(2,1)S(1)}) fusion(bf16[32,7168]{1,0:T(8,128)(2,1)S(1)} %collective-permute-done.17, bf16[32,7168]{1,0:T(8,128)(2,1)S(1)} %collective-permute-done.16, bf16[64,7168]{1,0:T(8,128)(2,1)} %collective-permute-done.12, ...), kind=kLoop, calls=%fused_computation.6 | loop fusion | flops 1376256 | bytes 1720320 | tf_op jit(solution)/shard_map/convert_element_type | solution.py:274
  86.4 3.9 %collective-permute-start.18 = (bf16[8,7168]{1,0:T(8,128)(2,1)S(1)}, bf16[8,7168]{1,0:T(8,128)(2,1)S(1)}, u32[]{:S(2)}, u32[]{:S(2)}) collective-permute-start(bf16[8,7168]{1,0:T(8,128)(2,1)S(1)} %get-tuple-element.64), channel_id=1, source_target_pairs={{0,24},{1,25},{2,26},{3,27},{4,28},{5,29},{6,30},{7,31},{8,0},{9,1... | collective-permute-start | bytes 344072 | tf_op jit(solution)/shard_map/ppermute | solution.py:26
  90.3 0.9 collective-permute-start.20
  91.2 2.6 %collective-permute-done.18 = bf16[8,7168]{1,0:T(8,128)(2,1)S(1)} collective-permute-done((bf16[8,7168]{1,0:T(8,128)(2,1)S(1)}, bf16[8,7168]{1,0:T(8,128)(2,1)S(1)}, u32[]{:S(2)}, u32[]{:S(2)}) %collective-permute-start.18) | collective-permute-done | bytes 114720 | tf_op jit(solution)/shard_map/ppermute | solution.py:26
  93.9 7.1 %collective-permute-done.19 = bf16[8,7168]{1,0:T(8,128)(2,1)S(1)} collective-permute-done((bf16[8,7168]{1,0:T(8,128)(2,1)S(1)}, bf16[8,7168]{1,0:T(8,128)(2,1)S(1)}, u32[]{:S(2)}, u32[]{:S(2)}) %collective-permute-start.19) | collective-permute-done | bytes 114720 | tf_op jit(solution)/shard_map/ppermute | solution.py:26
  101.0 1.7 %add_convert_fusion.3 = bf16[8,7168]{1,0:T(8,128)(2,1)} fusion(bf16[8,7168]{1,0:T(8,128)(2,1)S(1)} %collective-permute-done.20, bf16[8,7168]{1,0:T(8,128)(2,1)S(1)} %collective-permute-done.19, bf16[8,7168]{1,0:T(8,128)(2,1)S(1)} %collective-permute-done.18, bf16[32,7168]{1,0:T(8,128)(2,1)S(1)} %collective-permute-done.17, ...), kind=kLoop, calls=%fused_computation.3 | loop fusion | flops 1032192 | bytes 917632 | tf_op jit(solution)/shard_map/convert_element_type | solution.py:286
  (19 shorter events, 0.1 us)
Async XLA Ops:
  0.6 13.9 %collective-permute-start.3 = (bf16[8,96,576]{2,1,0:T(8,128)(2,1)}, bf16[8,96,576]{2,1,0:T(8,128)(2,1)S(1)}, u32[]{:S(2)}, u32[]{:S(2)}) collective-permute-start(bf16[8,96,576]{2,1,0:T(8,128)(2,1)} %own), channel_id=1, source_target_pairs={{1,2},{3,4},{5,6},{6,5},{9,10},{11,12},{13,14},{14,13},{17,18},{19... | collective-permute-start | bytes 2654216 | tf_op jit(solution)/shard_map/ppermute | solution.py:43
  1.4 10.8 %collective-permute-start = (bf16[8,7168]{1,0:T(8,128)(2,1)}, bf16[8,7168]{1,0:T(8,128)(2,1)S(1)}, u32[]{:S(2)}, u32[]{:S(2)}) collective-permute-start(bf16[8,7168]{1,0:T(8,128)(2,1)} %param.16), channel_id=1, source_target_pairs={{0,8},{1,9},{2,10},{3,11},{4,12},{5,13},{6,14},{7,15},{8,16},{9,17... | collective-permute-start | bytes 344072 | tf_op jit(solution)/shard_map/ppermute | solution.py:26
  4.4 9.7 %collective-permute-start.1 = (bf16[8,7168]{1,0:T(8,128)(2,1)}, bf16[8,7168]{1,0:T(8,128)(2,1)S(1)}, u32[]{:S(2)}, u32[]{:S(2)}) collective-permute-start(bf16[8,7168]{1,0:T(8,128)(2,1)} %param.16), channel_id=1, source_target_pairs={{0,16},{1,17},{2,18},{3,19},{4,20},{5,21},{6,22},{7,23},{8,24},{9,... | collective-permute-start | bytes 344072 | tf_op jit(solution)/shard_map/ppermute | solution.py:26
  7.0 7.5 %collective-permute-start.2 = (bf16[8,7168]{1,0:T(8,128)(2,1)}, bf16[8,7168]{1,0:T(8,128)(2,1)S(1)}, u32[]{:S(2)}, u32[]{:S(2)}) collective-permute-start(bf16[8,7168]{1,0:T(8,128)(2,1)} %param.16), channel_id=1, source_target_pairs={{0,24},{1,25},{2,26},{3,27},{4,28},{5,29},{6,30},{7,31},{8,0},{9,1... | collective-permute-start | bytes 344072 | tf_op jit(solution)/shard_map/ppermute | solution.py:26
  14.6 22.4 %copy-start.1 = (bf16[8,96,576]{2,1,0:T(8,128)(2,1)}, bf16[8,96,576]{2,1,0:T(8,128)(2,1)S(1)}, u32[]{:S(2)}) copy-start(bf16[8,96,576]{2,1,0:T(8,128)(2,1)S(1)} %collective-permute-done.3.early) | copy-start | bytes 2654212
  15.6 25.0 %copy-start = (bf16[8,96,576]{2,1,0:T(8,128)(2,1)S(1)}, bf16[8,96,576]{2,1,0:T(8,128)(2,1)}, u32[]{:S(2)}) copy-start(bf16[8,96,576]{2,1,0:T(8,128)(2,1)} %own) | copy-start | bytes 2654212
  15.6 16.5 %collective-permute-start.4 = (bf16[32,7168]{1,0:T(8,128)(2,1)S(1)}, bf16[32,7168]{1,0:T(8,128)(2,1)S(1)}, u32[]{:S(2)}, u32[]{:S(2)}) collective-permute-start(bf16[32,7168]{1,0:T(8,128)(2,1)S(1)} %constant_dynamic-update-slice_fusion.refs_0_), channel_id=1, source_target_pairs={{0,4},{1,3},{2,6},{3,1},{4,0},{5,7},{6,2},{7,5},{8,12},{9,11},{10,... | collective-permute-start | bytes 1376264 | tf_op jit(solution)/shard_map/ppermute | solution.py:26
  21.3 15.7 %collective-permute-start.7 = (bf16[8,96,576]{2,1,0:T(8,128)(2,1)}, bf16[8,96,576]{2,1,0:T(8,128)(2,1)S(1)}, u32[]{:S(2)}, u32[]{:S(2)}) collective-permute-start(bf16[8,96,576]{2,1,0:T(8,128)(2,1)} %own), channel_id=1, source_target_pairs={{0,1},{1,0},{2,3},{3,2},{4,5},{5,4},{6,7},{7,6},{8,9},{9,8},{10,11... | collective-permute-start | bytes 2654216 | tf_op jit(solution)/shard_map/ppermute | solution.py:26
  21.3 15.7 %collective-permute-start.5 = (bf16[32,7168]{1,0:T(8,128)(2,1)S(1)}, bf16[32,7168]{1,0:T(8,128)(2,1)S(1)}, u32[]{:S(2)}, u32[]{:S(2)}) collective-permute-start(bf16[32,7168]{1,0:T(8,128)(2,1)S(1)} %constant_dynamic-update-slice_fusion.refs_0_), channel_id=1, source_target_pairs={{0,2},{1,5},{2,0},{3,7},{4,6},{5,1},{6,4},{7,3},{8,10},{9,13},{10,... | collective-permute-start | bytes 1376264 | tf_op jit(solution)/shard_map/ppermute | solution.py:26
  32.2 8.5 %collective-permute-start.6 = (bf16[32,7168]{1,0:T(8,128)(2,1)S(1)}, bf16[32,7168]{1,0:T(8,128)(2,1)S(1)}, u32[]{:S(2)}, u32[]{:S(2)}) collective-permute-start(bf16[32,7168]{1,0:T(8,128)(2,1)S(1)} %collective-permute-done.4.refs_1_), channel_id=1, source_target_pairs={{0,2},{1,5},{2,0},{3,7},{4,6},{5,1},{6,4},{7,3},{8,10},{9,13},{10,... | collective-permute-start | bytes 1376264 | tf_op jit(solution)/shard_map/ppermute | solution.py:26
  37.0 3.7 %copy-start.2 = (bf16[8,96,576]{2,1,0:T(8,128)(2,1)}, bf16[8,96,576]{2,1,0:T(8,128)(2,1)S(1)}, u32[]{:S(2)}) copy-start(bf16[8,96,576]{2,1,0:T(8,128)(2,1)S(1)} %collective-permute-done.7.twin) | copy-start | bytes 2654212
  40.6 21.8 %copy-start.4 = (bf16[8,576]{1,0:T(8,128)(2,1)S(1)}, bf16[8,576]{1,0:T(8,128)(2,1)}, u32[]{:S(2)}) copy-start(bf16[8,576]{1,0:T(8,128)(2,1)} %param.13) | copy-start | bytes 27652
  40.7 10.0 %collective-permute-start.13 = (bf16[8,96,576]{2,1,0:T(8,128)(2,1)S(1)}, bf16[8,96,576]{2,1,0:T(8,128)(2,1)S(1)}, u32[]{:S(2)}, u32[]{:S(2)}) collective-permute-start(bf16[8,96,576]{2,1,0:T(8,128)(2,1)S(1)} %copy-done), channel_id=1, source_target_pairs={{2,1},{4,3},{7,8},{8,7},{10,9},{12,11},{15,16},{16,15},{18,17},{20... | collective-permute-start | bytes 2654216 | tf_op jit(solution)/shard_map/ppermute | solution.py:43
  41.5 1.9 %collective-permute-start.10 = (bf16[32,7168]{1,0:T(8,128)(2,1)S(1)}, bf16[32,7168]{1,0:T(8,128)(2,1)S(1)}, u32[]{:S(2)}, u32[]{:S(2)}) collective-permute-start(bf16[32,7168]{1,0:T(8,128)(2,1)S(1)} %collective-permute-done.5.refs_2_), channel_id=1, source_target_pairs={{0,1},{1,0},{2,3},{3,2},{4,5},{5,4},{6,7},{7,6},{8,9},{9,8},{10,11... | collective-permute-start | bytes 1376264 | tf_op jit(solution)/shard_map/ppermute | solution.py:26
  41.6 2.5 %collective-permute-start.11 = (bf16[32,7168]{1,0:T(8,128)(2,1)S(1)}, bf16[32,7168]{1,0:T(8,128)(2,1)S(1)}, u32[]{:S(2)}, u32[]{:S(2)}) collective-permute-start(bf16[32,7168]{1,0:T(8,128)(2,1)S(1)} %collective-permute-done.6.refs_3_), channel_id=1, source_target_pairs={{0,1},{1,0},{2,3},{3,2},{4,5},{5,4},{6,7},{7,6},{8,9},{9,8},{10,11... | collective-permute-start | bytes 1376264 | tf_op jit(solution)/shard_map/ppermute | solution.py:26
  42.1 2.6 %collective-permute-start.8 = (bf16[32,7168]{1,0:T(8,128)(2,1)S(1)}, bf16[32,7168]{1,0:T(8,128)(2,1)S(1)}, u32[]{:S(2)}, u32[]{:S(2)}) collective-permute-start(bf16[32,7168]{1,0:T(8,128)(2,1)S(1)} %constant_dynamic-update-slice_fusion.refs_0_), channel_id=1, source_target_pairs={{0,1},{1,0},{2,3},{3,2},{4,5},{5,4},{6,7},{7,6},{8,9},{9,8},{10,11... | collective-permute-start | bytes 1376264 | tf_op jit(solution)/shard_map/ppermute | solution.py:26
  42.2 3.2 %collective-permute-start.9 = (bf16[32,7168]{1,0:T(8,128)(2,1)S(1)}, bf16[32,7168]{1,0:T(8,128)(2,1)S(1)}, u32[]{:S(2)}, u32[]{:S(2)}) collective-permute-start(bf16[32,7168]{1,0:T(8,128)(2,1)S(1)} %collective-permute-done.4.refs_1_), channel_id=1, source_target_pairs={{0,1},{1,0},{2,3},{3,2},{4,5},{5,4},{6,7},{7,6},{8,9},{9,8},{10,11... | collective-permute-start | bytes 1376264 | tf_op jit(solution)/shard_map/ppermute | solution.py:26
  50.7 7.2 %copy-start.3 = (bf16[8,96,576]{2,1,0:T(8,128)(2,1)}, bf16[8,96,576]{2,1,0:T(8,128)(2,1)S(1)}, u32[]{:S(2)}) copy-start(bf16[8,96,576]{2,1,0:T(8,128)(2,1)S(1)} %collective-permute-done.13.late) | copy-start | bytes 2654212
  50.7 7.2 %collective-permute-start.14 = (bf16[64,7168]{1,0:T(8,128)(2,1)S(1)}, bf16[64,7168]{1,0:T(8,128)(2,1)S(1)}, u32[]{:S(2)}, u32[]{:S(2)}) collective-permute-start(bf16[64,7168]{1,0:T(8,128)(2,1)S(1)} %get-tuple-element.49), channel_id=1, source_target_pairs={{0,1},{1,0},{2,3},{3,2},{4,5},{5,4},{6,7},{7,6},{8,9},{9,8},{10,11... | collective-permute-start | bytes 2752520 | tf_op jit(solution)/shard_map/ppermute | solution.py:26
  54.5 17.3 %collective-permute-start.12 = (bf16[64,7168]{1,0:T(8,128)(2,1)S(1)}, bf16[64,7168]{1,0:T(8,128)(2,1)}, u32[]{:S(2)}, u32[]{:S(2)}) collective-permute-start(bf16[64,7168]{1,0:T(8,128)(2,1)S(1)} %get-tuple-element.46), channel_id=1, source_target_pairs={{0,1},{1,0},{2,3},{3,2},{4,5},{5,4},{6,7},{7,6},{8,9},{9,8},{10,11... | collective-permute-start | bytes 2752520 | tf_op jit(solution)/shard_map/ppermute | solution.py:26
  59.0 12.8 %collective-permute-start.15 = (bf16[32,7168]{1,0:T(8,128)(2,1)}, bf16[32,7168]{1,0:T(8,128)(2,1)S(1)}, u32[]{:S(2)}, u32[]{:S(2)}) collective-permute-start(bf16[32,7168]{1,0:T(8,128)(2,1)} %get-tuple-element.68), channel_id=1, source_target_pairs={{0,2},{1,5},{2,0},{3,7},{4,6},{5,1},{6,4},{7,3},{8,10},{9,13},{10,... | collective-permute-start | bytes 1376264 | tf_op jit(solution)/shard_map/ppermute | solution.py:26
  71.8 13.4 %collective-permute-start.16 = (bf16[32,7168]{1,0:T(8,128)(2,1)}, bf16[32,7168]{1,0:T(8,128)(2,1)S(1)}, u32[]{:S(2)}, u32[]{:S(2)}) collective-permute-start(bf16[32,7168]{1,0:T(8,128)(2,1)} %get-tuple-element.67), channel_id=1, source_target_pairs={{0,2},{1,5},{2,0},{3,7},{4,6},{5,1},{6,4},{7,3},{8,10},{9,13},{10,... | collective-permute-start | bytes 1376264 | tf_op jit(solution)/shard_map/ppermute | solution.py:26
  73.0 12.2 %collective-permute-start.17 = (bf16[32,7168]{1,0:T(8,128)(2,1)S(1)}, bf16[32,7168]{1,0:T(8,128)(2,1)S(1)}, u32[]{:S(2)}, u32[]{:S(2)}) collective-permute-start(bf16[32,7168]{1,0:T(8,128)(2,1)S(1)} %add_convert_fusion.1), channel_id=1, source_target_pairs={{0,4},{1,3},{2,6},{3,1},{4,0},{5,7},{6,2},{7,5},{8,12},{9,11},{10,... | collective-permute-start | bytes 1376264 | tf_op jit(solution)/shard_map/ppermute | solution.py:26
  86.4 7.5 %collective-permute-start.18 = (bf16[8,7168]{1,0:T(8,128)(2,1)S(1)}, bf16[8,7168]{1,0:T(8,128)(2,1)S(1)}, u32[]{:S(2)}, u32[]{:S(2)}) collective-permute-start(bf16[8,7168]{1,0:T(8,128)(2,1)S(1)} %get-tuple-element.64), channel_id=1, source_target_pairs={{0,24},{1,25},{2,26},{3,27},{4,28},{5,29},{6,30},{7,31},{8,0},{9,1... | collective-permute-start | bytes 344072 | tf_op jit(solution)/shard_map/ppermute | solution.py:26
  90.3 10.6 %collective-permute-start.19 = (bf16[8,7168]{1,0:T(8,128)(2,1)S(1)}, bf16[8,7168]{1,0:T(8,128)(2,1)S(1)}, u32[]{:S(2)}, u32[]{:S(2)}) collective-permute-start(bf16[8,7168]{1,0:T(8,128)(2,1)S(1)} %get-tuple-element.66), channel_id=1, source_target_pairs={{0,16},{1,17},{2,18},{3,19},{4,20},{5,21},{6,22},{7,23},{8,24},{9,... | collective-permute-start | bytes 344072 | tf_op jit(solution)/shard_map/ppermute | solution.py:26
  90.3 10.6 %collective-permute-start.20 = (bf16[8,7168]{1,0:T(8,128)(2,1)S(1)}, bf16[8,7168]{1,0:T(8,128)(2,1)S(1)}, u32[]{:S(2)}, u32[]{:S(2)}) collective-permute-start(bf16[8,7168]{1,0:T(8,128)(2,1)S(1)} %get-tuple-element.65), channel_id=1, source_target_pairs={{0,8},{1,9},{2,10},{3,11},{4,12},{5,13},{6,14},{7,15},{8,16},{9,17... | collective-permute-start | bytes 344072 | tf_op jit(solution)/shard_map/ppermute | solution.py:26

commit v8 on v7

--- a/solution.py
+++ b/solution.py
@@ -26,6 +26,10 @@
     return lax.ppermute(value, "dp", [(i, partner(i)) for i in range(peers)])
 
 
+def after(value, other):
+    return lax.optimization_barrier((value, other))[0]
+
+
 def added(values):
     total = values[0].astype(jnp.float32)
     for value in values[1:]:
@@ -44,58 +48,58 @@
 
 
 def attend_kernel(parents, lengths, query, own, twin, early, late, newest, out):
-    beam_count = parents.shape[0]
-    beam = pl.program_id(0)
+    beams = range(query.shape[0])
     rank = lax.axis_index("dp")
-    holder = parents[beam] // beam_count
-    length = lengths[beam]
     place = rank % 8
     arrives_early = (place == 2) | (place == 4) | (place == 5) | (place == 6)
-    rows = jnp.where(arrives_early, early[0], late[0])
-    rows = jnp.where(holder == (rank ^ 1), twin[0], rows)
-    rows = jnp.where(holder == rank, own[0], rows)
-    at = lax.broadcasted_iota(jnp.int32, rows.shape, 0)
-    rows = jnp.where(at < length - 1, rows, jnp.zeros_like(rows))
-    rows = jnp.where(at == length - 1, newest[0], rows)
-    scores = lax.dot_general(
-        query[0], rows, (((1,), (1,)), ((), ())), preferred_element_type=jnp.float32
-    )
-    scores = scores * score_scale
-    at = lax.broadcasted_iota(jnp.int32, scores.shape, 1)
-    scores = jnp.where(at < length, scores, -jnp.inf)
-    expons = jnp.exp(scores - jnp.max(scores, axis=1, keepdims=True))
-    probs = (expons / jnp.sum(expons, axis=1, keepdims=True)).astype(jnp.bfloat16)
-    mixed = jnp.dot(probs, rows[:, :KV], preferred_element_type=jnp.float32)
-    out[0] = mixed.astype(out.dtype)
+    latest = newest[...].astype(jnp.float32)
+    at = lax.broadcasted_iota(jnp.int32, own.shape[1:], 0)
+    rows, scores, probs = [], [], []
+    for b in beams:
+        slot, holder = parents[b] % len(beams), parents[b] // len(beams)
+        value = jnp.where(arrives_early, early[slot], late[slot])
+        value = jnp.where(holder == (rank ^ 1), twin[slot], value)
+        value = jnp.where(holder == rank, own[slot], value)
+        value = jnp.where(at < lengths[b] - 1, value, jnp.zeros_like(value))
+        row = jnp.broadcast_to(latest[b : b + 1], value.shape).astype(value.dtype)
+        rows.append(jnp.where(at == lengths[b] - 1, row, value))
+    for b in beams:
+        product = lax.dot_general(
+            query[b], rows[b], (((1,), (1,)), ((), ())), preferred_element_type=jnp.float32
+        )
+        scores.append(product * score_scale)
+    at = lax.broadcasted_iota(jnp.int32, scores[0].shape, 1)
+    for b in beams:
+        value = jnp.where(at < lengths[b], scores[b], -jnp.inf)
+        expons = jnp.exp(value - jnp.max(value, axis=1, keepdims=True))
+        total = jnp.sum(expons, axis=1, keepdims=True)
+        probs.append((expons / total).astype(jnp.bfloat16))
+    for b in beams:
+        mixed = jnp.dot(probs[b], rows[b][:, :KV], preferred_element_type=jnp.float32)
+        out[b] = mixed.astype(out.dtype)
 
 
 def attend(queries, own, twin, early, late, newest, parents, lengths):
     beam_count, heads, width = queries.shape
     positions = own.shape[1]
-
-    def chosen(b, parents, lengths):
-        return (parents[b] % beam_count, 0, 0)
-
-    def each(b, parents, lengths):
-        return (b, 0, 0)
-
+    scalars = pl.BlockSpec(memory_space=pltpu.SMEM)
+    whole = pl.BlockSpec(memory_space=pltpu.VMEM)
+    arrays = [
+        pltpu.with_memory_space_constraint(v, pltpu.VMEM)
+        for v in (queries, own, twin, early, late, newest)
+    ]
     return pl.pallas_call(
         attend_kernel,
-        grid_spec=pltpu.PrefetchScalarGridSpec(
-            num_scalar_prefetch=2,
-            grid=(beam_count,),
-            in_specs=[pl.BlockSpec((1, heads, width), each)]
-            + [pl.BlockSpec((1, positions, width), chosen)] * 4
-            + [pl.BlockSpec((1, 1, width), each)],
-            out_specs=pl.BlockSpec((1, heads, KV), each),
-        ),
+        in_specs=[scalars] * 2 + [whole] * len(arrays),
+        out_specs=whole,
         out_shape=jax.ShapeDtypeStruct((beam_count, heads, KV), jnp.bfloat16),
+        compiler_params=pltpu.CompilerParams(vmem_limit_bytes=16 * 2**20),
         cost_estimate=pl.CostEstimate(
             flops=2 * beam_count * heads * positions * (width + KV),
             bytes_accessed=2 * beam_count * (4 * positions * width + heads * (width + KV)),
             transcendentals=beam_count * heads * positions,
         ),
-    )(parents, lengths, queries, own, twin, early, late, newest)
+    )(parents, lengths, *arrays)
 
 
 def fetch_kernel(*refs):
@@ -236,54 +240,70 @@
 
     blocks = blocks[:1] + [swapped(blocks[r], ahead(r)) for r in range(1, expert_count)]
     early = neighbours(latent_cache, EARLY, slices)
-    newest = new_latent[:, None, :]
-    *blocks, early, newest, mixing = lax.optimization_barrier((*blocks, early, newest, mixing))
+    *blocks, early, mixing = lax.optimization_barrier((*blocks, early, mixing))
     column = jnp.concatenate(blocks)
     near = swapped(column, first)
     side = swapped(column, second)
     across = swapped(near, second)
     beside = swapped(latent_cache, twin)
-    held = [column, near, side, across]
+    twin_column, twin_near = swapped(column, twin), swapped(near, twin)
     weights = fetched([gate_weight, up_weight, down_weight])
-    held, weights, beside, latent_cache = lax.optimization_barrier(
-        (held, weights, beside, latent_cache)
+    across, twin_column, twin_near, weights, beside, latent_cache = lax.optimization_barrier(
+        (across, twin_column, twin_near, weights, beside, latent_cache)
     )
     late = neighbours(latent_cache, LATE, slices)
-    held = held + [swapped(value, twin) for value in held]
+    held = [column, near, side, across, twin_column, twin_near]
+    held = held + [swapped(side, twin), swapped(across, twin)]
     own, high, low = experts(held, weights)
     high, late = lax.optimization_barrier((high, late))
 
     high, low = swapped(high, twin), swapped(low, twin)
     height = expert_count * capacity
-
-    def block(value, j):
-        return lax.slice_in_dim(value, j * height, (j + 1) * height)
-
-    across = added([block(own, 3), block(high, 1)]).astype(jnp.bfloat16)
-    across = swapped(across, second)
-    side = swapped(added([block(own, 2), block(high, 0)]).astype(jnp.bfloat16), second)
-    attention = attend(queries, latent_cache, beside, early, late, newest, parents, lengths)
-    near = added([block(own, 1), block(low, 1), across]).astype(jnp.bfloat16)
-    near, attention = lax.optimization_barrier((near, attention))
-    near = swapped(near, first)
-    here = [own, low, side, near]
-
-    def share(r):
-        return added([v[r * capacity : (r + 1) * capacity] for v in here])
-
-    values = [swapped(share(r).astype(jnp.bfloat16), ahead(-r)) for r in range(1, expert_count)]
-    values = [share(0)] + values
-    values = [v.astype(jnp.float32) for v in values]
-    if dense:
-        expert_output = sum(mixing[r][:, None] * values[r] for r in range(expert_count))
-    else:
-        expert_output = jnp.dot(
-            mixing,
-            jnp.concatenate(values),
-            precision=lax.Precision.HIGHEST,
-            preferred_element_type=jnp.float32,
-        )
-    return (attention, expert_output.astype(jnp.bfloat16))
+    halves = [(0, width // 2), (width // 2, width)]
+
+    def block(value, j, half):
+        return value[j * height : (j + 1) * height, half[0] : half[1]]
+
+    attention = attend(queries, latent_cache, beside, early, late, new_latent, parents, lengths)
+    totals, done, token = [], None, None
+    for half in halves:
+        across = added([block(own, 3, half), block(high, 1, half)]).astype(jnp.bfloat16)
+        across = across if token is None else after(across, token)
+        later = after(high, across)
+        across = swapped(across, second)
+        if done is not None:
+            across, later = after((across, later), done)
+        side = added([block(own, 2, half), block(later, 0, half)]).astype(jnp.bfloat16)
+        near = added([block(own, 1, half), block(low, 1, half), across]).astype(jnp.bfloat16)
+        if done is not None:
+            near, attention = lax.optimization_barrier((near, attention))
+        token = near
+        near, side = swapped(near, first), swapped(side, second)
+        here = [block(own, 0, half), block(low, 0, half), side, near]
+        shares = [
+            added([v[r * capacity : (r + 1) * capacity] for v in here])
+            for r in range(expert_count)
+        ]
+        done = shares
+        values = [
+            swapped(shares[r].astype(jnp.bfloat16), ahead(-r)) for r in range(1, expert_count)
+        ]
+        values = [v.astype(jnp.float32) for v in values]
+        if dense:
+            weighted = lax.optimization_barrier(mixing[0][:, None] * shares[0])
+            total = weighted + sum(
+                mixing[r][:, None] * values[r - 1] for r in range(1, expert_count)
+            )
+        else:
+            total = jnp.dot(
+                mixing,
+                jnp.concatenate([shares[0]] + values),
+                precision=lax.Precision.HIGHEST,
+                preferred_element_type=jnp.float32,
+            )
+        totals.append(total.astype(jnp.bfloat16))
+    expert_output = jnp.concatenate(totals, axis=1)
+    return (attention, expert_output)
 
 
 def solution(mesh):

time: 103 us -> 92.1 us (0.89)
  waiting for transfers between devices: 43.2 us -> 34.6 us
  starting transfers between devices: 29.7 us -> 38.3 us
  Pallas kernels: 18.3 us -> 11.8 us
  other arithmetic: 8.41 us -> 4.78 us
    ppermute x19 -> x25, starting transfers between devices: 28.1 us -> 36.9 us  [swapped(): return lax.ppermute(value, 'dp', [(i, partner(i)) for i in range(peers)])]
    ppermute x19 -> x25, waiting for transfers between devices: 43.2 us -> 34.6 us  [swapped(): return lax.ppermute(value, 'dp', [(i, partner(i)) for i in range(peers)])]
    pallas_call x1, Pallas kernels: 8.76 us -> 2.29 us  [attend(): pl.pallas_call(attend_kernel, in_specs=[scalars] * 2 + [whole] * len(arra...]
    convert_element_type x4 -> x5, other arithmetic: 5.21 us -> 0.64 us  [the longest x2 0.27 us: body(): added([block(own, 2, half), block(later, 0, half)]).astype(jnp.bfloat16)]
  transfers between devices with their start and end apart: 21 -> 27, of which waited for: 12 -> 14; matrix products, arithmetic and copies ran while one was open for 7% -> 5% of each run, Pallas kernels for 18% -> 13%
where the time goes in v8:
time: 92.1 us; the launch traced here: 91.9 us
  starting transfers between devices  38.3 us (42%)
  waiting for transfers between devices  34.6 us (38%)
  Pallas kernels  11.8 us (13%)
  other arithmetic  4.78 us (5%)
  local copies, waits for them, and re-layouts  1.59 us (2%)
    ppermute x25, starting transfers between devices, swapped(): return lax.ppermute(value, 'dp', [(i, partner(i)) for i in range(peers)])  36.9 us
    ppermute x25, waiting for transfers between devices, swapped(): return lax.ppermute(value, 'dp', [(i, partner(i)) for i in range(peers)])  34.6 us
    pallas_call x1, Pallas kernels, experts(): pl.pallas_call(lambda *refs: expert_kernel(wide, *refs), in_specs=[whole]...  5.3 us
    pallas_call x1, Pallas kernels, fetched(): pl.pallas_call(fetch_kernel, in_specs=[pl.BlockSpec(memory_space=pltpu.HB...  4.23 us
    reduce_sum x1, other arithmetic, body(): jnp.sum(jnp.where(routed_experts == targets[r], route_weights, 0.0), axis=1)  3.31 us
    pallas_call x1, Pallas kernels, attend(): pl.pallas_call(attend_kernel, in_specs=[scalars] * 2 + [whole] * len(arra...  2.29 us
  transfers between devices with their start and end apart: 27, of which 14 were waited for; matrix products, arithmetic and copies ran while one was open for 5% of the time, Pallas kernels for 13%

profile of v8, /device:TPU:0, one launch (start us, length us, event | category | flops | bytes accessed | tf_op | source)
XLA Modules:
  0.0 91.9 jit_solution(11092052610815169971)
XLA Ops:
  0.6 0.7 collective-permute-start.3
  1.4 4.1 %collective-permute-start.1 = (bf16[8,7168]{1,0:T(8,128)(2,1)}, bf16[8,7168]{1,0:T(8,128)(2,1)S(1)}, u32[]{:S(2)}, u32[]{:S(2)}) collective-permute-start(bf16[8,7168]{1,0:T(8,128)(2,1)} %param.16), channel_id=1, source_target_pairs={{0,16},{1,17},{2,18},{3,19},{4,20},{5,21},{6,22},{7,23},{8,24},{9,... | collective-permute-start | bytes 344072 | tf_op jit(solution)/shard_map/ppermute | solution.py:26
  5.5 1.6 %collective-permute-start = (bf16[8,7168]{1,0:T(8,128)(2,1)}, bf16[8,7168]{1,0:T(8,128)(2,1)S(1)}, u32[]{:S(2)}, u32[]{:S(2)}) collective-permute-start(bf16[8,7168]{1,0:T(8,128)(2,1)} %param.16), channel_id=1, source_target_pairs={{0,8},{1,9},{2,10},{3,11},{4,12},{5,13},{6,14},{7,15},{8,16},{9,17... | collective-permute-start | bytes 344072 | tf_op jit(solution)/shard_map/ppermute | solution.py:26
  7.0 2.2 %collective-permute-start.2 = (bf16[8,7168]{1,0:T(8,128)(2,1)}, bf16[8,7168]{1,0:T(8,128)(2,1)S(1)}, u32[]{:S(2)}, u32[]{:S(2)}) collective-permute-start(bf16[8,7168]{1,0:T(8,128)(2,1)} %param.16), channel_id=1, source_target_pairs={{0,24},{1,25},{2,26},{3,27},{4,28},{5,29},{6,30},{7,31},{8,0},{9,1... | collective-permute-start | bytes 344072 | tf_op jit(solution)/shard_map/ppermute | solution.py:26
  9.3 0.6 fusion.5
  9.9 3.3 %fusion.3 = (f32[8]{0:T(128)S(1)}, f32[8]{0:T(128)S(1)}, f32[8]{0:T(128)S(1)}, f32[8]{0:T(128)S(1)}) fusion(f32[8,2]{0,1:T(2,128)} %param.18, s32[8,2]{0,1:T(2,128)} %param.17, s32[]{:T(128)} %bitcast.3, s32[]{:T(128)} %bitcast.1, s32[]{:T(128)} %bitcast, s32[]{:T(128)} %bitcast.2), kind=kLoop, calls=%fused_computation.32 | loop fusion | flops 160 | bytes 272 | tf_op jit(solution)/shard_map/reduce_sum | solution.py:217
  13.3 2.2 %collective-permute-done.2 = bf16[8,7168]{1,0:T(8,128)(2,1)S(1)} collective-permute-done((bf16[8,7168]{1,0:T(8,128)(2,1)}, bf16[8,7168]{1,0:T(8,128)(2,1)S(1)}, u32[]{:S(2)}, u32[]{:S(2)}) %collective-permute-start.2) | collective-permute-done | bytes 114720 | tf_op jit(solution)/shard_map/ppermute | solution.py:26
  15.5 0.9 constant_dynamic-update-slice_fusion.3
  16.5 4.7 %collective-permute-start.4 = (bf16[32,7168]{1,0:T(8,128)(2,1)S(1)}, bf16[32,7168]{1,0:T(8,128)(2,1)S(1)}, u32[]{:S(2)}, u32[]{:S(2)}) collective-permute-start(bf16[32,7168]{1,0:T(8,128)(2,1)S(1)} %constant_dynamic-update-slice_fusion.refs_0_), channel_id=1, source_target_pairs={{0,4},{1,3},{2,6},{3,1},{4,0},{5,7},{6,2},{7,5},{8,12},{9,11},{10,... | collective-permute-start | bytes 1376264 | tf_op jit(solution)/shard_map/ppermute | solution.py:26
  21.2 0.5 collective-permute-start.7
  21.7 5.9 %collective-permute-done.4.refs_1_ = bf16[32,7168]{1,0:T(8,128)(2,1)S(1)} collective-permute-done((bf16[32,7168]{1,0:T(8,128)(2,1)S(1)}, bf16[32,7168]{1,0:T(8,128)(2,1)S(1)}, u32[]{:S(2)}, u32[]{:S(2)}) %collective-permute-start.4) | collective-permute-done | bytes 458784 | tf_op jit(solution)/shard_map/ppermute | solution.py:26
  27.6 1.1 %collective-permute-start.6 = (bf16[32,7168]{1,0:T(8,128)(2,1)S(1)}, bf16[32,7168]{1,0:T(8,128)(2,1)S(1)}, u32[]{:S(2)}, u32[]{:S(2)}) collective-permute-start(bf16[32,7168]{1,0:T(8,128)(2,1)S(1)} %collective-permute-done.4.refs_1_), channel_id=1, source_target_pairs={{0,2},{1,5},{2,0},{3,7},{4,6},{5,1},{6,4},{7,3},{8,10},{9,13},{10,... | collective-permute-start | bytes 1376264 | tf_op jit(solution)/shard_map/ppermute | solution.py:26
  28.7 0.9 %collective-permute-start.5 = (bf16[32,7168]{1,0:T(8,128)(2,1)S(1)}, bf16[32,7168]{1,0:T(8,128)(2,1)S(1)}, u32[]{:S(2)}, u32[]{:S(2)}) collective-permute-start(bf16[32,7168]{1,0:T(8,128)(2,1)S(1)} %constant_dynamic-update-slice_fusion.refs_0_), channel_id=1, source_target_pairs={{0,2},{1,5},{2,0},{3,7},{4,6},{5,1},{6,4},{7,3},{8,10},{9,13},{10,... | collective-permute-start | bytes 1376264 | tf_op jit(solution)/shard_map/ppermute | solution.py:26
  29.6 4.2 %shard_map.122 = (bf16[1,7168,256]{2,1,0:T(8,128)(2,1)S(1)}, bf16[1,7168,256]{2,1,0:T(8,128)(2,1)S(1)}, bf16[1,256,7168]{2,1,0:T(8,128)(2,1)S(1)}) custom-call(bf16[1,7168,256]{2,1,0:T(8,128)(2,1)} %refs_0_.1, bf16[1,7168,256]{2,1,0:T(8,128)(2,1)} %refs_1_.1, bf16[1,256,7168]{2,1,0:T(8,128)(2,1)} %refs_2_.1), custom_call_target="tpu_custom_call" | custom-call | bytes 22020096 | tf_op jit(solution)/shard_map/pallas_call | solution.py:119
  33.9 2.2 %collective-permute-done.6.refs_3_ = bf16[32,7168]{1,0:T(8,128)(2,1)S(1)} collective-permute-done((bf16[32,7168]{1,0:T(8,128)(2,1)S(1)}, bf16[32,7168]{1,0:T(8,128)(2,1)S(1)}, u32[]{:S(2)}, u32[]{:S(2)}) %collective-permute-start.6) | collective-permute-done | bytes 458784 | tf_op jit(solution)/shard_map/ppermute | solution.py:26
  36.1 0.7 collective-permute-start.13
  36.8 4.2 %collective-permute-done.5.refs_2_ = bf16[32,7168]{1,0:T(8,128)(2,1)S(1)} collective-permute-done((bf16[32,7168]{1,0:T(8,128)(2,1)S(1)}, bf16[32,7168]{1,0:T(8,128)(2,1)S(1)}, u32[]{:S(2)}, u32[]{:S(2)}) %collective-permute-start.5) | collective-permute-done | bytes 458784 | tf_op jit(solution)/shard_map/ppermute | solution.py:26
  41.0 0.5 collective-permute-start.11
  41.5 1.3 %collective-permute-done.10.refs_6_ = bf16[32,7168]{1,0:T(8,128)(2,1)S(1)} collective-permute-done((bf16[32,7168]{1,0:T(8,128)(2,1)S(1)}, bf16[32,7168]{1,0:T(8,128)(2,1)S(1)}, u32[]{:S(2)}, u32[]{:S(2)}) %collective-permute-start.10) | collective-permute-done | bytes 458784 | tf_op jit(solution)/shard_map/ppermute | solution.py:26
  42.8 0.7 collective-permute-done.11.refs_7_
  43.5 5.3 %shard_map.123 = (bf16[128,7168]{1,0:T(8,128)(2,1)S(1)}, bf16[64,7168]{1,0:T(8,128)(2,1)S(1)}, bf16[64,7168]{1,0:T(8,128)(2,1)S(1)}) custom-call(bf16[32,7168]{1,0:T(8,128)(2,1)S(1)} %constant_dynamic-update-slice_fusion.refs_0_, bf16[32,7168]{1,0:T(8,128)(2,1)S(1)} %collective-permute-done.4.refs_1_, bf16[32,7168]{1,0:T(8,128)(2,1)S(1)} %collective-permute-done.5.refs_2_, ...), custom_call_target="tpu_custom_call" | custom-call | flops 2818572288 | bytes 18350080 | tf_op jit(solution)/shard_map/pallas_call | solution.py:171
  48.9 2.6 %collective-permute-start.14 = (bf16[64,7168]{1,0:T(8,128)(2,1)S(1)}, bf16[64,7168]{1,0:T(8,128)(2,1)S(1)}, u32[]{:S(2)}, u32[]{:S(2)}) collective-permute-start(bf16[64,7168]{1,0:T(8,128)(2,1)S(1)} %get-tuple-element.51), channel_id=1, source_target_pairs={{0,1},{1,0},{2,3},{3,2},{4,5},{5,4},{6,7},{7,6},{8,9},{9,8},{10,11... | collective-permute-start | bytes 2752520 | tf_op jit(solution)/shard_map/ppermute | solution.py:26
  51.4 2.1 %collective-permute-done.14 = bf16[64,7168]{1,0:T(8,128)(2,1)S(1)} collective-permute-done((bf16[64,7168]{1,0:T(8,128)(2,1)S(1)}, bf16[64,7168]{1,0:T(8,128)(2,1)S(1)}, u32[]{:S(2)}, u32[]{:S(2)}) %collective-permute-start.14) | collective-permute-done | bytes 917536 | tf_op jit(solution)/shard_map/ppermute | solution.py:26
  53.5 0.1 add_convert_fusion.4
  53.6 2.0 %collective-permute-start.15 = (bf16[32,3584]{1,0:T(8,128)(2,1)S(1)}, bf16[32,3584]{1,0:T(8,128)(2,1)S(1)}, u32[]{:S(2)}, u32[]{:S(2)}) collective-permute-start(bf16[32,3584]{1,0:T(8,128)(2,1)S(1)} %get-tuple-element.79), channel_id=1, source_target_pairs={{0,2},{1,5},{2,0},{3,7},{4,6},{5,1},{6,4},{7,3},{8,10},{9,13},{10,... | collective-permute-start | bytes 688136 | tf_op jit(solution)/shard_map/ppermute | solution.py:26
  55.7 4.0 %collective-permute-done.15 = bf16[32,3584]{1,0:T(8,128)(2,1)S(1)} collective-permute-done((bf16[32,3584]{1,0:T(8,128)(2,1)S(1)}, bf16[32,3584]{1,0:T(8,128)(2,1)S(1)}, u32[]{:S(2)}, u32[]{:S(2)}) %collective-permute-start.15) | collective-permute-done | bytes 229408 | tf_op jit(solution)/shard_map/ppermute | solution.py:26
  59.7 0.1 add_convert_fusion.2
  59.9 2.0 %collective-permute-start.17 = (bf16[32,3584]{1,0:T(8,128)(2,1)S(1)}, bf16[32,3584]{1,0:T(8,128)(2,1)S(1)}, u32[]{:S(2)}, u32[]{:S(2)}) collective-permute-start(bf16[32,3584]{1,0:T(8,128)(2,1)S(1)} %get-tuple-element.83), channel_id=1, source_target_pairs={{0,2},{1,5},{2,0},{3,7},{4,6},{5,1},{6,4},{7,3},{8,10},{9,13},{10,... | collective-permute-start | bytes 688136 | tf_op jit(solution)/shard_map/ppermute | solution.py:26
  61.9 2.2 %collective-permute-start.18 = (bf16[32,3584]{1,0:T(8,128)(2,1)S(1)}, bf16[32,3584]{1,0:T(8,128)(2,1)S(1)}, u32[]{:S(2)}, u32[]{:S(2)}) collective-permute-start(bf16[32,3584]{1,0:T(8,128)(2,1)S(1)} %get-tuple-element.84), channel_id=1, source_target_pairs={{0,4},{1,3},{2,6},{3,1},{4,0},{5,7},{6,2},{7,5},{8,12},{9,11},{10,... | collective-permute-start | bytes 688136 | tf_op jit(solution)/shard_map/ppermute | solution.py:26
  64.1 2.3 %shard_map.124 = bf16[8,64,512]{2,1,0:T(8,128)(2,1)} custom-call(s32[8]{0:T(128)S(1)} %copy-done.3, s32[8]{0:T(128)S(1)} %copy-done.4, bf16[8,64,576]{2,1,0:T(8,128)(2,1)S(1)} %copy-done.1, bf16[8,96,576]{2,1,0:T(8,128)(2,1)S(1)} %copy-done, bf16[8,96,576]{2,1,0:T(8,128)(2,1)S(1)} %collective-permute-done.9.twin, ...), custom_call_target="tpu_custom_call" | custom-call | flops 106954752 | bytes 4653056 | tf_op jit(solution)/shard_map/pallas_call | solution.py:91
  66.5 1.3 %collective-permute-done.17 = bf16[32,3584]{1,0:T(8,128)(2,1)S(1)} collective-permute-done((bf16[32,3584]{1,0:T(8,128)(2,1)S(1)}, bf16[32,3584]{1,0:T(8,128)(2,1)S(1)}, u32[]{:S(2)}, u32[]{:S(2)}) %collective-permute-start.17) | collective-permute-done | bytes 229408 | tf_op jit(solution)/shard_map/ppermute | solution.py:26
  67.8 1.7 %collective-permute-done.18 = bf16[32,3584]{1,0:T(8,128)(2,1)S(1)} collective-permute-done((bf16[32,3584]{1,0:T(8,128)(2,1)S(1)}, bf16[32,3584]{1,0:T(8,128)(2,1)S(1)}, u32[]{:S(2)}, u32[]{:S(2)}) %collective-permute-start.18) | collective-permute-done | bytes 229408 | tf_op jit(solution)/shard_map/ppermute | solution.py:26
  69.5 0.1 convert_add_fusion
  69.6 2.8 %collective-permute-done.16 = bf16[32,3584]{1,0:T(8,128)(2,1)S(1)} collective-permute-done((bf16[32,3584]{1,0:T(8,128)(2,1)S(1)}, bf16[32,3584]{1,0:T(8,128)(2,1)S(1)}, u32[]{:S(2)}, u32[]{:S(2)}) %collective-permute-start.16) | collective-permute-done | bytes 229408 | tf_op jit(solution)/shard_map/ppermute | solution.py:26
  72.4 0.1 add_convert_fusion
  72.5 0.1 collective-permute-start.23
  72.6 1.2 %collective-permute-start.22 = (bf16[32,3584]{1,0:T(8,128)(2,1)S(1)}, bf16[32,3584]{1,0:T(8,128)(2,1)S(1)}, u32[]{:S(2)}, u32[]{:S(2)}) collective-permute-start(bf16[32,3584]{1,0:T(8,128)(2,1)S(1)} %get-tuple-element.81), channel_id=1, source_target_pairs={{0,2},{1,5},{2,0},{3,7},{4,6},{5,1},{6,4},{7,3},{8,10},{9,13},{10,... | collective-permute-start | bytes 688136 | tf_op jit(solution)/shard_map/ppermute | solution.py:26
  73.8 2.5 %collective-permute-start.21 = (bf16[8,3584]{1,0:T(8,128)(2,1)S(1)}, bf16[8,3584]{1,0:T(8,128)(2,1)S(1)}, u32[]{:S(2)}, u32[]{:S(2)}) collective-permute-start(bf16[8,3584]{1,0:T(8,128)(2,1)S(1)} %get-tuple-element.76), channel_id=1, source_target_pairs={{0,8},{1,9},{2,10},{3,11},{4,12},{5,13},{6,14},{7,15},{8,16},{9,17... | collective-permute-start | bytes 172040 | tf_op jit(solution)/shard_map/ppermute | solution.py:26
  76.4 2.6 %collective-permute-start.20 = (bf16[8,3584]{1,0:T(8,128)(2,1)S(1)}, bf16[8,3584]{1,0:T(8,128)(2,1)S(1)}, u32[]{:S(2)}, u32[]{:S(2)}) collective-permute-start(bf16[8,3584]{1,0:T(8,128)(2,1)S(1)} %get-tuple-element.77), channel_id=1, source_target_pairs={{0,16},{1,17},{2,18},{3,19},{4,20},{5,21},{6,22},{7,23},{8,24},{9,... | collective-permute-start | bytes 172040 | tf_op jit(solution)/shard_map/ppermute | solution.py:26
  78.9 1.4 %collective-permute-start.19 = (bf16[8,3584]{1,0:T(8,128)(2,1)S(1)}, bf16[8,3584]{1,0:T(8,128)(2,1)S(1)}, u32[]{:S(2)}, u32[]{:S(2)}) collective-permute-start(bf16[8,3584]{1,0:T(8,128)(2,1)S(1)} %get-tuple-element.78), channel_id=1, source_target_pairs={{0,24},{1,25},{2,26},{3,27},{4,28},{5,29},{6,30},{7,31},{8,0},{9,1... | collective-permute-start | bytes 172040 | tf_op jit(solution)/shard_map/ppermute | solution.py:26
  80.3 0.1 add_convert_fusion.9
  80.4 3.5 %collective-permute-start.24 = (bf16[8,3584]{1,0:T(8,128)(2,1)S(1)}, bf16[8,3584]{1,0:T(8,128)(2,1)S(1)}, u32[]{:S(2)}, u32[]{:S(2)}) collective-permute-start(bf16[8,3584]{1,0:T(8,128)(2,1)S(1)} %get-tuple-element.72), channel_id=1, source_target_pairs={{0,24},{1,25},{2,26},{3,27},{4,28},{5,29},{6,30},{7,31},{8,0},{9,1... | collective-permute-start | bytes 172040 | tf_op jit(solution)/shard_map/ppermute | solution.py:26
  83.9 1.1 %collective-permute-start.25 = (bf16[8,3584]{1,0:T(8,128)(2,1)S(1)}, bf16[8,3584]{1,0:T(8,128)(2,1)S(1)}, u32[]{:S(2)}, u32[]{:S(2)}) collective-permute-start(bf16[8,3584]{1,0:T(8,128)(2,1)S(1)} %get-tuple-element.74), channel_id=1, source_target_pairs={{0,16},{1,17},{2,18},{3,19},{4,20},{5,21},{6,22},{7,23},{8,24},{9,... | collective-permute-start | bytes 172040 | tf_op jit(solution)/shard_map/ppermute | solution.py:26
  85.0 1.2 %collective-permute-done.24 = bf16[8,3584]{1,0:T(8,128)(2,1)S(1)} collective-permute-done((bf16[8,3584]{1,0:T(8,128)(2,1)S(1)}, bf16[8,3584]{1,0:T(8,128)(2,1)S(1)}, u32[]{:S(2)}, u32[]{:S(2)}) %collective-permute-start.24) | collective-permute-done | bytes 57376 | tf_op jit(solution)/shard_map/ppermute | solution.py:26
  86.2 3.8 %collective-permute-done.26 = bf16[8,3584]{1,0:T(8,128)(2,1)S(1)} collective-permute-done((bf16[8,3584]{1,0:T(8,128)(2,1)S(1)}, bf16[8,3584]{1,0:T(8,128)(2,1)S(1)}, u32[]{:S(2)}, u32[]{:S(2)}) %collective-permute-start.26) | collective-permute-done | bytes 57376 | tf_op jit(solution)/shard_map/ppermute | solution.py:26
  90.0 1.1 %collective-permute-done.25 = bf16[8,3584]{1,0:T(8,128)(2,1)S(1)} collective-permute-done((bf16[8,3584]{1,0:T(8,128)(2,1)S(1)}, bf16[8,3584]{1,0:T(8,128)(2,1)S(1)}, u32[]{:S(2)}, u32[]{:S(2)}) %collective-permute-start.25) | collective-permute-done | bytes 57376 | tf_op jit(solution)/shard_map/ppermute | solution.py:26
  91.1 0.1 add_convert_fusion.10
  91.3 0.7 pad_maximum_fusion
  (34 shorter events, 0.3 us)
Async XLA Ops:
  0.6 14.9 %collective-permute-start.3 = (bf16[8,96,576]{2,1,0:T(8,128)(2,1)}, bf16[8,96,576]{2,1,0:T(8,128)(2,1)S(1)}, u32[]{:S(2)}, u32[]{:S(2)}) collective-permute-start(bf16[8,96,576]{2,1,0:T(8,128)(2,1)} %own), channel_id=1, source_target_pairs={{1,2},{3,4},{5,6},{6,5},{9,10},{11,12},{13,14},{14,13},{17,18},{19... | collective-permute-start | bytes 2654216 | tf_op jit(solution)/shard_map/ppermute | solution.py:47
  1.4 11.9 %collective-permute-start.1 = (bf16[8,7168]{1,0:T(8,128)(2,1)}, bf16[8,7168]{1,0:T(8,128)(2,1)S(1)}, u32[]{:S(2)}, u32[]{:S(2)}) collective-permute-start(bf16[8,7168]{1,0:T(8,128)(2,1)} %param.16), channel_id=1, source_target_pairs={{0,16},{1,17},{2,18},{3,19},{4,20},{5,21},{6,22},{7,23},{8,24},{9,... | collective-permute-start | bytes 344072 | tf_op jit(solution)/shard_map/ppermute | solution.py:26
  5.5 7.8 %collective-permute-start = (bf16[8,7168]{1,0:T(8,128)(2,1)}, bf16[8,7168]{1,0:T(8,128)(2,1)S(1)}, u32[]{:S(2)}, u32[]{:S(2)}) collective-permute-start(bf16[8,7168]{1,0:T(8,128)(2,1)} %param.16), channel_id=1, source_target_pairs={{0,8},{1,9},{2,10},{3,11},{4,12},{5,13},{6,14},{7,15},{8,16},{9,17... | collective-permute-start | bytes 344072 | tf_op jit(solution)/shard_map/ppermute | solution.py:26
  7.0 8.5 %collective-permute-start.2 = (bf16[8,7168]{1,0:T(8,128)(2,1)}, bf16[8,7168]{1,0:T(8,128)(2,1)S(1)}, u32[]{:S(2)}, u32[]{:S(2)}) collective-permute-start(bf16[8,7168]{1,0:T(8,128)(2,1)} %param.16), channel_id=1, source_target_pairs={{0,24},{1,25},{2,26},{3,27},{4,28},{5,29},{6,30},{7,31},{8,0},{9,1... | collective-permute-start | bytes 344072 | tf_op jit(solution)/shard_map/ppermute | solution.py:26
  16.5 19.6 %copy-start = (bf16[8,96,576]{2,1,0:T(8,128)(2,1)S(1)}, bf16[8,96,576]{2,1,0:T(8,128)(2,1)}, u32[]{:S(2)}) copy-start(bf16[8,96,576]{2,1,0:T(8,128)(2,1)} %own) | copy-start | bytes 2654212
  16.5 11.1 %collective-permute-start.4 = (bf16[32,7168]{1,0:T(8,128)(2,1)S(1)}, bf16[32,7168]{1,0:T(8,128)(2,1)S(1)}, u32[]{:S(2)}, u32[]{:S(2)}) collective-permute-start(bf16[32,7168]{1,0:T(8,128)(2,1)S(1)} %constant_dynamic-update-slice_fusion.refs_0_), channel_id=1, source_target_pairs={{0,4},{1,3},{2,6},{3,1},{4,0},{5,7},{6,2},{7,5},{8,12},{9,11},{10,... | collective-permute-start | bytes 1376264 | tf_op jit(solution)/shard_map/ppermute | solution.py:26
  21.2 12.7 %collective-permute-start.9 = (bf16[8,96,576]{2,1,0:T(8,128)(2,1)}, bf16[8,96,576]{2,1,0:T(8,128)(2,1)S(1)}, u32[]{:S(2)}, u32[]{:S(2)}) collective-permute-start(bf16[8,96,576]{2,1,0:T(8,128)(2,1)} %own), channel_id=1, source_target_pairs={{0,1},{1,0},{2,3},{3,2},{4,5},{5,4},{6,7},{7,6},{8,9},{9,8},{10,11... | collective-permute-start | bytes 2654216 | tf_op jit(solution)/shard_map/ppermute | solution.py:26
  21.2 12.7 %collective-permute-start.7 = (bf16[32,7168]{1,0:T(8,128)(2,1)S(1)}, bf16[32,7168]{1,0:T(8,128)(2,1)S(1)}, u32[]{:S(2)}, u32[]{:S(2)}) collective-permute-start(bf16[32,7168]{1,0:T(8,128)(2,1)S(1)} %constant_dynamic-update-slice_fusion.refs_0_), channel_id=1, source_target_pairs={{0,1},{1,0},{2,3},{3,2},{4,5},{5,4},{6,7},{7,6},{8,9},{9,8},{10,11... | collective-permute-start | bytes 1376264 | tf_op jit(solution)/shard_map/ppermute | solution.py:26
  27.6 6.3 %collective-permute-start.8 = (bf16[32,7168]{1,0:T(8,128)(2,1)S(1)}, bf16[32,7168]{1,0:T(8,128)(2,1)S(1)}, u32[]{:S(2)}, u32[]{:S(2)}) collective-permute-start(bf16[32,7168]{1,0:T(8,128)(2,1)S(1)} %collective-permute-done.4.refs_1_), channel_id=1, source_target_pairs={{0,1},{1,0},{2,3},{3,2},{4,5},{5,4},{6,7},{7,6},{8,9},{9,8},{10,11... | collective-permute-start | bytes 1376264 | tf_op jit(solution)/shard_map/ppermute | solution.py:26
  27.6 8.5 %collective-permute-start.6 = (bf16[32,7168]{1,0:T(8,128)(2,1)S(1)}, bf16[32,7168]{1,0:T(8,128)(2,1)S(1)}, u32[]{:S(2)}, u32[]{:S(2)}) collective-permute-start(bf16[32,7168]{1,0:T(8,128)(2,1)S(1)} %collective-permute-done.4.refs_1_), channel_id=1, source_target_pairs={{0,2},{1,5},{2,0},{3,7},{4,6},{5,1},{6,4},{7,3},{8,10},{9,13},{10,... | collective-permute-start | bytes 1376264 | tf_op jit(solution)/shard_map/ppermute | solution.py:26
  28.7 12.3 %collective-permute-start.5 = (bf16[32,7168]{1,0:T(8,128)(2,1)S(1)}, bf16[32,7168]{1,0:T(8,128)(2,1)S(1)}, u32[]{:S(2)}, u32[]{:S(2)}) collective-permute-start(bf16[32,7168]{1,0:T(8,128)(2,1)S(1)} %constant_dynamic-update-slice_fusion.refs_0_), channel_id=1, source_target_pairs={{0,2},{1,5},{2,0},{3,7},{4,6},{5,1},{6,4},{7,3},{8,10},{9,13},{10,... | collective-permute-start | bytes 1376264 | tf_op jit(solution)/shard_map/ppermute | solution.py:26
  36.1 12.7 %collective-permute-start.13 = (bf16[8,96,576]{2,1,0:T(8,128)(2,1)S(1)}, bf16[8,96,576]{2,1,0:T(8,128)(2,1)S(1)}, u32[]{:S(2)}, u32[]{:S(2)}) collective-permute-start(bf16[8,96,576]{2,1,0:T(8,128)(2,1)S(1)} %copy-done), channel_id=1, source_target_pairs={{2,1},{4,3},{7,8},{8,7},{10,9},{12,11},{15,16},{16,15},{18,17},{20... | collective-permute-start | bytes 2654216 | tf_op jit(solution)/shard_map/ppermute | solution.py:47
  41.0 1.8 %collective-permute-start.10 = (bf16[32,7168]{1,0:T(8,128)(2,1)S(1)}, bf16[32,7168]{1,0:T(8,128)(2,1)S(1)}, u32[]{:S(2)}, u32[]{:S(2)}) collective-permute-start(bf16[32,7168]{1,0:T(8,128)(2,1)S(1)} %collective-permute-done.5.refs_2_), channel_id=1, source_target_pairs={{0,1},{1,0},{2,3},{3,2},{4,5},{5,4},{6,7},{7,6},{8,9},{9,8},{10,11... | collective-permute-start | bytes 1376264 | tf_op jit(solution)/shard_map/ppermute | solution.py:26
  41.0 2.5 %collective-permute-start.11 = (bf16[32,7168]{1,0:T(8,128)(2,1)S(1)}, bf16[32,7168]{1,0:T(8,128)(2,1)S(1)}, u32[]{:S(2)}, u32[]{:S(2)}) collective-permute-start(bf16[32,7168]{1,0:T(8,128)(2,1)S(1)} %collective-permute-done.6.refs_3_), channel_id=1, source_target_pairs={{0,1},{1,0},{2,3},{3,2},{4,5},{5,4},{6,7},{7,6},{8,9},{9,8},{10,11... | collective-permute-start | bytes 1376264 | tf_op jit(solution)/shard_map/ppermute | solution.py:26
  48.8 15.3 %copy-start.1 = (bf16[8,64,576]{2,1,0:T(8,128)(2,1)S(1)}, bf16[8,64,576]{2,1,0:T(8,128)(2,1)}, u32[]{:S(2)}) copy-start(bf16[8,64,576]{2,1,0:T(8,128)(2,1)} %query.1) | copy-start | bytes 1769476
  48.8 15.3 %copy-start.2 = (bf16[8,576]{1,0:T(8,128)(2,1)S(1)}, bf16[8,576]{1,0:T(8,128)(2,1)}, u32[]{:S(2)}) copy-start(bf16[8,576]{1,0:T(8,128)(2,1)} %newest.1) | copy-start | bytes 27652
  48.8 15.3 %copy-start.3 = (s32[8]{0:T(128)S(1)}, s32[8]{0:T(128)}, u32[]{:S(2)}) copy-start(s32[8]{0:T(128)} %parents.1) | copy-start | bytes 100
  48.8 15.2 %copy-start.4 = (s32[8]{0:T(128)S(1)}, s32[8]{0:T(128)}, u32[]{:S(2)}) copy-start(s32[8]{0:T(128)} %lengths.1) | copy-start | bytes 100
  48.9 4.7 %collective-permute-start.14 = (bf16[64,7168]{1,0:T(8,128)(2,1)S(1)}, bf16[64,7168]{1,0:T(8,128)(2,1)S(1)}, u32[]{:S(2)}, u32[]{:S(2)}) collective-permute-start(bf16[64,7168]{1,0:T(8,128)(2,1)S(1)} %get-tuple-element.51), channel_id=1, source_target_pairs={{0,1},{1,0},{2,3},{3,2},{4,5},{5,4},{6,7},{7,6},{8,9},{9,8},{10,11... | collective-permute-start | bytes 2752520 | tf_op jit(solution)/shard_map/ppermute | solution.py:26
  51.4 4.3 %collective-permute-start.12 = (bf16[64,7168]{1,0:T(8,128)(2,1)S(1)}, bf16[64,7168]{1,0:T(8,128)(2,1)S(1)}, u32[]{:S(2)}, u32[]{:S(2)}) collective-permute-start(bf16[64,7168]{1,0:T(8,128)(2,1)S(1)} %get-tuple-element.48), channel_id=1, source_target_pairs={{0,1},{1,0},{2,3},{3,2},{4,5},{5,4},{6,7},{7,6},{8,9},{9,8},{10,11... | collective-permute-start | bytes 2752520 | tf_op jit(solution)/shard_map/ppermute | solution.py:26
  53.6 6.1 %collective-permute-start.15 = (bf16[32,3584]{1,0:T(8,128)(2,1)S(1)}, bf16[32,3584]{1,0:T(8,128)(2,1)S(1)}, u32[]{:S(2)}, u32[]{:S(2)}) collective-permute-start(bf16[32,3584]{1,0:T(8,128)(2,1)S(1)} %get-tuple-element.79), channel_id=1, source_target_pairs={{0,2},{1,5},{2,0},{3,7},{4,6},{5,1},{6,4},{7,3},{8,10},{9,13},{10,... | collective-permute-start | bytes 688136 | tf_op jit(solution)/shard_map/ppermute | solution.py:26
  59.9 7.9 %collective-permute-start.17 = (bf16[32,3584]{1,0:T(8,128)(2,1)S(1)}, bf16[32,3584]{1,0:T(8,128)(2,1)S(1)}, u32[]{:S(2)}, u32[]{:S(2)}) collective-permute-start(bf16[32,3584]{1,0:T(8,128)(2,1)S(1)} %get-tuple-element.83), channel_id=1, source_target_pairs={{0,2},{1,5},{2,0},{3,7},{4,6},{5,1},{6,4},{7,3},{8,10},{9,13},{10,... | collective-permute-start | bytes 688136 | tf_op jit(solution)/shard_map/ppermute | solution.py:26
  61.9 7.6 %collective-permute-start.18 = (bf16[32,3584]{1,0:T(8,128)(2,1)S(1)}, bf16[32,3584]{1,0:T(8,128)(2,1)S(1)}, u32[]{:S(2)}, u32[]{:S(2)}) collective-permute-start(bf16[32,3584]{1,0:T(8,128)(2,1)S(1)} %get-tuple-element.84), channel_id=1, source_target_pairs={{0,4},{1,3},{2,6},{3,1},{4,0},{5,7},{6,2},{7,5},{8,12},{9,11},{10,... | collective-permute-start | bytes 688136 | tf_op jit(solution)/shard_map/ppermute | solution.py:26
  66.4 6.0 %collective-permute-start.16 = (bf16[32,3584]{1,0:T(8,128)(2,1)S(1)}, bf16[32,3584]{1,0:T(8,128)(2,1)S(1)}, u32[]{:S(2)}, u32[]{:S(2)}) collective-permute-start(bf16[32,3584]{1,0:T(8,128)(2,1)S(1)} %get-tuple-element.52), channel_id=1, source_target_pairs={{0,2},{1,5},{2,0},{3,7},{4,6},{5,1},{6,4},{7,3},{8,10},{9,13},{10,... | collective-permute-start | bytes 688136 | tf_op jit(solution)/shard_map/ppermute | solution.py:26
  72.5 7.8 %collective-permute-start.23 = (bf16[32,3584]{1,0:T(8,128)(2,1)S(1)}, bf16[32,3584]{1,0:T(8,128)(2,1)S(1)}, u32[]{:S(2)}, u32[]{:S(2)}) collective-permute-start(bf16[32,3584]{1,0:T(8,128)(2,1)S(1)} %get-tuple-element.65), channel_id=1, source_target_pairs={{0,4},{1,3},{2,6},{3,1},{4,0},{5,7},{6,2},{7,5},{8,12},{9,11},{10,... | collective-permute-start | bytes 688136 | tf_op jit(solution)/shard_map/ppermute | solution.py:26
  72.6 7.7 %collective-permute-start.22 = (bf16[32,3584]{1,0:T(8,128)(2,1)S(1)}, bf16[32,3584]{1,0:T(8,128)(2,1)S(1)}, u32[]{:S(2)}, u32[]{:S(2)}) collective-permute-start(bf16[32,3584]{1,0:T(8,128)(2,1)S(1)} %get-tuple-element.81), channel_id=1, source_target_pairs={{0,2},{1,5},{2,0},{3,7},{4,6},{5,1},{6,4},{7,3},{8,10},{9,13},{10,... | collective-permute-start | bytes 688136 | tf_op jit(solution)/shard_map/ppermute | solution.py:26
  73.8 10.1 %collective-permute-start.21 = (bf16[8,3584]{1,0:T(8,128)(2,1)S(1)}, bf16[8,3584]{1,0:T(8,128)(2,1)S(1)}, u32[]{:S(2)}, u32[]{:S(2)}) collective-permute-start(bf16[8,3584]{1,0:T(8,128)(2,1)S(1)} %get-tuple-element.76), channel_id=1, source_target_pairs={{0,8},{1,9},{2,10},{3,11},{4,12},{5,13},{6,14},{7,15},{8,16},{9,17... | collective-permute-start | bytes 172040 | tf_op jit(solution)/shard_map/ppermute | solution.py:26
  76.4 8.7 %collective-permute-start.20 = (bf16[8,3584]{1,0:T(8,128)(2,1)S(1)}, bf16[8,3584]{1,0:T(8,128)(2,1)S(1)}, u32[]{:S(2)}, u32[]{:S(2)}) collective-permute-start(bf16[8,3584]{1,0:T(8,128)(2,1)S(1)} %get-tuple-element.77), channel_id=1, source_target_pairs={{0,16},{1,17},{2,18},{3,19},{4,20},{5,21},{6,22},{7,23},{8,24},{9,... | collective-permute-start | bytes 172040 | tf_op jit(solution)/shard_map/ppermute | solution.py:26
  78.9 6.1 %collective-permute-start.19 = (bf16[8,3584]{1,0:T(8,128)(2,1)S(1)}, bf16[8,3584]{1,0:T(8,128)(2,1)S(1)}, u32[]{:S(2)}, u32[]{:S(2)}) collective-permute-start(bf16[8,3584]{1,0:T(8,128)(2,1)S(1)} %get-tuple-element.78), channel_id=1, source_target_pairs={{0,24},{1,25},{2,26},{3,27},{4,28},{5,29},{6,30},{7,31},{8,0},{9,1... | collective-permute-start | bytes 172040 | tf_op jit(solution)/shard_map/ppermute | solution.py:26
  80.4 5.8 %collective-permute-start.24 = (bf16[8,3584]{1,0:T(8,128)(2,1)S(1)}, bf16[8,3584]{1,0:T(8,128)(2,1)S(1)}, u32[]{:S(2)}, u32[]{:S(2)}) collective-permute-start(bf16[8,3584]{1,0:T(8,128)(2,1)S(1)} %get-tuple-element.72), channel_id=1, source_target_pairs={{0,24},{1,25},{2,26},{3,27},{4,28},{5,29},{6,30},{7,31},{8,0},{9,1... | collective-permute-start | bytes 172040 | tf_op jit(solution)/shard_map/ppermute | solution.py:26
  83.9 6.1 %collective-permute-start.26 = (bf16[8,3584]{1,0:T(8,128)(2,1)S(1)}, bf16[8,3584]{1,0:T(8,128)(2,1)S(1)}, u32[]{:S(2)}, u32[]{:S(2)}) collective-permute-start(bf16[8,3584]{1,0:T(8,128)(2,1)S(1)} %get-tuple-element.73), channel_id=1, source_target_pairs={{0,8},{1,9},{2,10},{3,11},{4,12},{5,13},{6,14},{7,15},{8,16},{9,17... | collective-permute-start | bytes 172040 | tf_op jit(solution)/shard_map/ppermute | solution.py:26
  83.9 7.2 %collective-permute-start.25 = (bf16[8,3584]{1,0:T(8,128)(2,1)S(1)}, bf16[8,3584]{1,0:T(8,128)(2,1)S(1)}, u32[]{:S(2)}, u32[]{:S(2)}) collective-permute-start(bf16[8,3584]{1,0:T(8,128)(2,1)S(1)} %get-tuple-element.74), channel_id=1, source_target_pairs={{0,16},{1,17},{2,18},{3,19},{4,20},{5,21},{6,22},{7,23},{8,24},{9,... | collective-permute-start | bytes 172040 | tf_op jit(solution)/shard_map/ppermute | solution.py:26

commit v9 on v8

--- a/solution.py
+++ b/solution.py
@@ -26,8 +26,8 @@
     return lax.ppermute(value, "dp", [(i, partner(i)) for i in range(peers)])
 
 
-def after(value, other):
-    return lax.optimization_barrier((value, other))[0]
+def tied(*values):
+    return lax.optimization_barrier(values)
 
 
 def added(values):
@@ -47,7 +47,8 @@
     return lax.ppermute(value, "dp", [p for p in pairs if max(p) < peers])
 
 
-def attend_kernel(parents, lengths, query, own, twin, early, late, newest, out):
+def attend_kernel(spans, parents, lengths, query, own, twin, newest, *refs):
+    pieces, out = refs[:-1], refs[-1]
     beams = range(query.shape[0])
     rank = lax.axis_index("dp")
     place = rank % 8
@@ -57,9 +58,16 @@
     rows, scores, probs = [], [], []
     for b in beams:
         slot, holder = parents[b] % len(beams), parents[b] // len(beams)
-        value = jnp.where(arrives_early, early[slot], late[slot])
+        value = own[slot]
         value = jnp.where(holder == (rank ^ 1), twin[slot], value)
-        value = jnp.where(holder == rank, own[slot], value)
+        far = (holder != rank) & (holder != (rank ^ 1))
+        for (kind, low, high), piece in zip(spans, pieces):
+            here = far & (slot >= low) & (slot < high)
+            if kind == "early":
+                here = here & arrives_early
+            if kind == "late":
+                here = here & jnp.logical_not(arrives_early)
+            value = jnp.where(here, piece[jnp.clip(slot - low, 0, high - low - 1)], value)
         value = jnp.where(at < lengths[b] - 1, value, jnp.zeros_like(value))
         row = jnp.broadcast_to(latest[b : b + 1], value.shape).astype(value.dtype)
         rows.append(jnp.where(at == lengths[b] - 1, row, value))
@@ -79,17 +87,17 @@
         out[b] = mixed.astype(out.dtype)
 
 
-def attend(queries, own, twin, early, late, newest, parents, lengths):
+def attend(queries, own, twin, newest, spans, pieces, parents, lengths):
     beam_count, heads, width = queries.shape
     positions = own.shape[1]
     scalars = pl.BlockSpec(memory_space=pltpu.SMEM)
     whole = pl.BlockSpec(memory_space=pltpu.VMEM)
     arrays = [
         pltpu.with_memory_space_constraint(v, pltpu.VMEM)
-        for v in (queries, own, twin, early, late, newest)
+        for v in (queries, own, twin, newest, *pieces)
     ]
     return pl.pallas_call(
-        attend_kernel,
+        lambda *refs: attend_kernel(spans, *refs),
         in_specs=[scalars] * 2 + [whole] * len(arrays),
         out_specs=whole,
         out_shape=jax.ShapeDtypeStruct((beam_count, heads, KV), jnp.bfloat16),
@@ -131,56 +139,92 @@
     )(*[pltpu.with_memory_space_constraint(w, pltpu.HBM) for w in weights])
 
 
-def expert_kernel(wide, *refs):
-    rows, refs = refs[:8], refs[8:]
-    gate, up, down, own, high, low, gate_sum, up_sum = refs
-    height, width = rows[0].shape
-    half = 4 * height
-
-    def span(k):
-        return pl.ds(pl.multiple_of(k * wide, wide), wide)
-
+def span(k, wide, begin=0):
+    return pl.ds(pl.multiple_of(begin + k * wide, wide), wide)
+
+
+def sum_products(begin, wide, rows, gate, up, gate_sum, up_sum):
+    @pl.loop(0, rows[0].shape[1] // wide)
+    def _(k):
+        piece = jnp.concatenate([ref[:, span(k, wide)] for ref in rows], axis=0)
+        depth = span(k, wide, begin)
+        gate_sum[...] += jnp.dot(piece, gate[0, depth, :], preferred_element_type=jnp.float32)
+        up_sum[...] += jnp.dot(piece, up[0, depth, :], preferred_element_type=jnp.float32)
+
+
+def first_kernel(wide, *refs):
+    rows, (gate, up, gate_sum, up_sum) = refs[:8], refs[8:]
     gate_sum[...] = jnp.zeros_like(gate_sum)
     up_sum[...] = jnp.zeros_like(up_sum)
-
-    @pl.loop(0, width // wide)
-    def _(k):
-        piece = jnp.concatenate([ref[:, span(k)] for ref in rows], axis=0)
-        gate_sum[...] += jnp.dot(piece, gate[0, span(k), :], preferred_element_type=jnp.float32)
-        up_sum[...] += jnp.dot(piece, up[0, span(k), :], preferred_element_type=jnp.float32)
-
+    sum_products(0, wide, rows, gate, up, gate_sum, up_sum)
+
+
+def second_kernel(wide, *refs):
+    rows, refs = refs[:8], refs[8:]
+    gate, up, down, gate_part, up_part, own, high, low, gate_sum, up_sum = refs
+    height = rows[0].shape[0]
+    half = 4 * height
+    gate_sum[...] = gate_part[...]
+    up_sum[...] = up_part[...]
+    sum_products(rows[0].shape[1], wide, rows, gate, up, gate_sum, up_sum)
     total = gate_sum[...]
     hidden = (total / (1.0 + jnp.exp(-total)) * up_sum[...]).astype(jnp.bfloat16)
 
-    @pl.loop(0, width // wide)
+    @pl.loop(0, own.shape[1] // wide)
     def _(k):
-        product = jnp.dot(hidden, down[0, :, span(k)], preferred_element_type=jnp.float32)
+        at = span(k, wide)
+        product = jnp.dot(hidden, down[0, :, at], preferred_element_type=jnp.float32)
         product = product.astype(jnp.bfloat16)
-        own[:, span(k)] = product[:half]
-        low[:, span(k)] = product[half : half + 2 * height]
-        high[:, span(k)] = product[half + 2 * height :]
-
-
-def experts(rows, weights):
+        own[:, at] = product[:half]
+        low[:, at] = product[half : half + 2 * height]
+        high[:, at] = product[half + 2 * height :]
+
+
+def step_width(width):
+    return max(w for w in (128, 256, 512, 896) if width % w == 0)
+
+
+def first_half(rows, weights):
     height, width = rows[0].shape
     units = weights[0].shape[2]
-    wide = max(w for w in (128, 256, 512, 1024) if width % w == 0)
     total = len(rows) * height
     whole = pl.BlockSpec(memory_space=pltpu.VMEM)
-    inputs = [pltpu.with_memory_space_constraint(v, pltpu.VMEM) for v in (*rows, *weights)]
+    inputs = [pltpu.with_memory_space_constraint(v, pltpu.VMEM) for v in (*rows, *weights[:2])]
     return pl.pallas_call(
-        lambda *refs: expert_kernel(wide, *refs),
+        lambda *refs: first_kernel(step_width(width), *refs),
+        in_specs=[whole] * len(inputs),
+        out_specs=[whole] * 2,
+        out_shape=[pltpu.VMEM((total, units), jnp.float32)] * 2,
+        compiler_params=pltpu.CompilerParams(vmem_limit_bytes=24 * 2**20),
+        cost_estimate=pl.CostEstimate(
+            flops=4 * total * width * units,
+            bytes_accessed=4 * width * units + 2 * total * width,
+            transcendentals=0,
+        ),
+    )(*inputs)
+
+
+def second_half(rows, weights, sums):
+    height, width = rows[0].shape
+    units = weights[0].shape[2]
+    total = len(rows) * height
+    whole = pl.BlockSpec(memory_space=pltpu.VMEM)
+    inputs = [
+        pltpu.with_memory_space_constraint(v, pltpu.VMEM) for v in (*rows, *weights, *sums)
+    ]
+    return pl.pallas_call(
+        lambda *refs: second_kernel(step_width(width), *refs),
         in_specs=[whole] * len(inputs),
         out_specs=[whole] * 3,
-        out_shape=[pltpu.VMEM((count * height, width), jnp.bfloat16) for count in (4, 2, 2)],
+        out_shape=[pltpu.VMEM((count * height, 2 * width), jnp.bfloat16) for count in (4, 2, 2)],
         scratch_shapes=[
             pltpu.VMEM((total, units), jnp.float32),
             pltpu.VMEM((total, units), jnp.float32),
         ],
-        compiler_params=pltpu.CompilerParams(vmem_limit_bytes=28 * 2**20),
+        compiler_params=pltpu.CompilerParams(vmem_limit_bytes=24 * 2**20),
         cost_estimate=pl.CostEstimate(
-            flops=6 * total * width * units,
-            bytes_accessed=6 * width * units + 4 * total * width,
+            flops=8 * total * width * units,
+            bytes_accessed=8 * width * units + 6 * total * width,
             transcendentals=total * units,
         ),
     )(*inputs)
@@ -238,66 +282,108 @@
     def second(i):
         return i ^ (4 if i & 1 else 2)
 
-    blocks = blocks[:1] + [swapped(blocks[r], ahead(r)) for r in range(1, expert_count)]
-    early = neighbours(latent_cache, EARLY, slices)
-    *blocks, early, mixing = lax.optimization_barrier((*blocks, early, mixing))
-    column = jnp.concatenate(blocks)
-    near = swapped(column, first)
-    side = swapped(column, second)
-    across = swapped(near, second)
+    halves = [(0, width // 2), (width // 2, width)]
+    last = 3 * beam_count // 4
+    middle = beam_count // 2
+    spans, pieces = [], []
+
+    def cache_rows(kind, begin, end, ready=None):
+        moves = {"early": EARLY, "late": LATE, "both": EARLY + LATE}[kind]
+        source = latent_cache[begin:end]
+        if ready is not None:
+            source, ready = tied(source, ready)
+        spans.append((kind, begin, end))
+        return neighbours(source, moves, slices), ready
+
+    def cut(half):
+        return [block[:, half[0] : half[1]] for block in blocks]
+
+    def to_column(cuts):
+        return cuts[:1] + [swapped(cuts[r], ahead(r)) for r in range(1, expert_count)]
+
+    def to_plane(column):
+        near = swapped(column, first)
+        return [column, near, swapped(column, second), swapped(near, second)]
+
+    column = to_column(cut(halves[0]))
+    column[1], later = tied(column[1], cut(halves[1]))
+    early, _ = cache_rows("early", 0, last)
+    weights = fetched([gate_weight, up_weight, down_weight])
+    column, early, mixing, weights = tied(column, early, mixing, weights)
+    pieces.append(early)
+    held = to_plane(jnp.concatenate(column))
+    later = to_column(later)
+    later, held = tied(later, held)
+    held_later = to_plane(jnp.concatenate(later))
     beside = swapped(latent_cache, twin)
-    twin_column, twin_near = swapped(column, twin), swapped(near, twin)
-    weights = fetched([gate_weight, up_weight, down_weight])
-    across, twin_column, twin_near, weights, beside, latent_cache = lax.optimization_barrier(
-        (across, twin_column, twin_near, weights, beside, latent_cache)
-    )
-    late = neighbours(latent_cache, LATE, slices)
-    held = [column, near, side, across, twin_column, twin_near]
-    held = held + [swapped(side, twin), swapped(across, twin)]
-    own, high, low = experts(held, weights)
-    high, late = lax.optimization_barrier((high, late))
+    held = held + [swapped(value, twin) for value in held]
+    held, held_later[2] = tied(held, held_later[2])
+    sums = first_half(held, weights)
+    held_later[3], sums, beside = tied(held_later[3], sums, beside)
+    late, held_later[3] = cache_rows("late", 0, middle, held_later[3])
+    held_later = held_later + [swapped(value, twin) for value in held_later]
+    own, high, low = second_half(held_later, weights, sums)
+    high, late = tied(high, late)
+    pieces.append(late)
+    late, own = cache_rows("late", middle, last, own)
 
     high, low = swapped(high, twin), swapped(low, twin)
     height = expert_count * capacity
-    halves = [(0, width // 2), (width // 2, width)]
 
     def block(value, j, half):
         return value[j * height : (j + 1) * height, half[0] : half[1]]
 
-    attention = attend(queries, latent_cache, beside, early, late, new_latent, parents, lengths)
-    totals, done, token = [], None, None
-    for half in halves:
-        across = added([block(own, 3, half), block(high, 1, half)]).astype(jnp.bfloat16)
-        across = across if token is None else after(across, token)
-        later = after(high, across)
-        across = swapped(across, second)
-        if done is not None:
-            across, later = after((across, later), done)
-        side = added([block(own, 2, half), block(later, 0, half)]).astype(jnp.bfloat16)
-        near = added([block(own, 1, half), block(low, 1, half), across]).astype(jnp.bfloat16)
-        if done is not None:
-            near, attention = lax.optimization_barrier((near, attention))
-        token = near
-        near, side = swapped(near, first), swapped(side, second)
+    def to_second(half):
+        return added([block(own, 3, half), block(high, 1, half)]).astype(jnp.bfloat16)
+
+    def to_first(half, across):
+        return added([block(own, 1, half), block(low, 1, half), across]).astype(jnp.bfloat16)
+
+    def to_side(half):
+        return added([block(own, 2, half), block(high, 0, half)]).astype(jnp.bfloat16)
+
+    def shares(half, side, near):
         here = [block(own, 0, half), block(low, 0, half), side, near]
-        shares = [
+        return [
             added([v[r * capacity : (r + 1) * capacity] for v in here])
             for r in range(expert_count)
         ]
-        done = shares
-        values = [
-            swapped(shares[r].astype(jnp.bfloat16), ahead(-r)) for r in range(1, expert_count)
+
+    def back(share):
+        return [
+            swapped(share[r].astype(jnp.bfloat16), ahead(-r)) for r in range(1, expert_count)
         ]
-        values = [v.astype(jnp.float32) for v in values]
+
+    across, late = tied(to_second(halves[0]), late)
+    pieces.append(late)
+    across, high = tied(across, high)
+    across = swapped(across, second)
+    near, side = to_first(halves[0], across), to_side(halves[0])
+    near, across = tied(near, to_second(halves[1]))
+    near, side, across = swapped(near, first), swapped(side, second), swapped(across, second)
+    share = shares(halves[0], side, near)
+    share, across, high = tied(share, across, high)
+    values = [[share[0]] + back(share)]
+    near, side = to_first(halves[1], across), to_side(halves[1])
+    near, side = swapped(near, first), swapped(side, second)
+    near, side, values[0] = tied(near, side, values[0])
+    share = shares(halves[1], side, near)
+    rest, share = cache_rows("both", last, beam_count, share)
+    pieces.append(rest)
+    values.append([share[0]] + back(share))
+    attention = attend(
+        queries, latent_cache, beside, new_latent, spans, pieces, parents, lengths
+    )
+    values, attention = tied(values, attention)
+    totals = []
+    for value in values:
+        value = [v.astype(jnp.float32) for v in value]
         if dense:
-            weighted = lax.optimization_barrier(mixing[0][:, None] * shares[0])
-            total = weighted + sum(
-                mixing[r][:, None] * values[r - 1] for r in range(1, expert_count)
-            )
+            total = sum(mixing[r][:, None] * value[r] for r in range(expert_count))
         else:
             total = jnp.dot(
                 mixing,
-                jnp.concatenate([shares[0]] + values),
+                jnp.concatenate(value),
                 precision=lax.Precision.HIGHEST,
                 preferred_element_type=jnp.float32,
             )

time: 92.1 us -> 112 us (1.22)
  waiting for transfers between devices: 34.6 us -> 43.9 us
  starting transfers between devices: 38.3 us -> 46.5 us
  local copies, waits for them, and re-layouts: 1.59 us -> 2.8 us
    ppermute x25 -> x35, waiting for transfers between devices: 34.6 us -> 43.9 us  [swapped(): return lax.ppermute(value, 'dp', [(i, partner(i)) for i in range(peers)])]
    ppermute x25 -> x35, starting transfers between devices: 36.9 us -> 43.8 us  [swapped(): return lax.ppermute(value, 'dp', [(i, partner(i)) for i in range(peers)])]
    slice x0 -> x4, local copies, waits for them, and re-layouts: none -> 2.13 us  [the longest x3 1.27 us: cache_rows(): source = latent_cache[begin:end]]
    ppermute x2 -> x4, starting transfers between devices: 1.44 us -> 2.74 us  [neighbours(): return lax.ppermute(value, 'dp', [p for p in pairs if max(p) < peers])]
    pallas_call x2 -> x3, Pallas kernels: 7.59 us -> 8.6 us  [the longest x1 4.31 us: second_half(): pl.pallas_call(lambda *refs: second_kernel(step_width(width), *refs), in_...]
  transfers between devices with their start and end apart: 27 -> 39, of which waited for: 14 -> 20; matrix products, arithmetic and copies ran while one was open for 5% -> 4% of each run, Pallas kernels for 13% -> 12%
where the time goes in v9:
time: 112 us; the launch traced here: 111 us
  starting transfers between devices  46.5 us (42%)
  waiting for transfers between devices  43.9 us (39%)
  Pallas kernels  12.9 us (12%)
  other arithmetic  3.92 us (4%)
  local copies, waits for them, and re-layouts  2.8 us (2%)
    ppermute x35, waiting for transfers between devices, swapped(): return lax.ppermute(value, 'dp', [(i, partner(i)) for i in range(peers)])  43.9 us
    ppermute x35, starting transfers between devices, swapped(): return lax.ppermute(value, 'dp', [(i, partner(i)) for i in range(peers)])  43.8 us
    pallas_call x1, Pallas kernels, second_half(): pl.pallas_call(lambda *refs: second_kernel(step_width(width), *refs), in_...  4.31 us
    pallas_call x1, Pallas kernels, fetched(): pl.pallas_call(fetch_kernel, in_specs=[pl.BlockSpec(memory_space=pltpu.HB...  4.3 us
    ppermute x4, starting transfers between devices, neighbours(): return lax.ppermute(value, 'dp', [p for p in pairs if max(p) < peers])  2.74 us
    pallas_call x1, Pallas kernels, attend(): pl.pallas_call(lambda *refs: attend_kernel(spans, *refs), in_specs=[scala...  2.5 us
    reduce_sum x1, other arithmetic, body(): jnp.sum(jnp.where(routed_experts == targets[r], route_weights, 0.0), axis=1)  2.49 us
  transfers between devices with their start and end apart: 39, of which 20 were waited for; matrix products, arithmetic and copies ran while one was open for 4% of the time, Pallas kernels for 12%

profile of v9, /device:TPU:0, one launch (start us, length us, event | category | flops | bytes accessed | tf_op | source)
XLA Modules:
  0.0 111.0 jit_solution(3439714433768279914)
XLA Ops:
  0.6 1.2 %slice.191 = bf16[6,96,576]{2,1,0:T(8,128)(2,1)S(1)} slice(bf16[8,96,576]{2,1,0:T(8,128)(2,1)} %refs_3_.1), slice={[0:6], [0:96], [0:576]} | slice | bytes 1327104 | tf_op jit(solution)/shard_map/slice | solution.py:292
  1.8 0.7 collective-permute-start.6
  2.5 0.9 fusion.6
  3.4 3.1 %collective-permute-start = (bf16[8,3584]{1,0:T(8,128)(2,1)S(1)}, bf16[8,3584]{1,0:T(8,128)(2,1)S(1)}, u32[]{:S(2)}, u32[]{:S(2)}) collective-permute-start(bf16[8,3584]{1,0:T(8,128)(2,1)S(1)} %get-tuple-element.94), channel_id=1, source_target_pairs={{0,8},{1,9},{2,10},{3,11},{4,12},{5,13},{6,14},{7,15},{8,16},{9,17... | collective-permute-start | bytes 172040 | tf_op jit(solution)/shard_map/ppermute | solution.py:26
  6.5 2.6 %collective-permute-start.4 = (bf16[8,3584]{1,0:T(8,128)(2,1)S(1)}, bf16[8,3584]{1,0:T(8,128)(2,1)S(1)}, u32[]{:S(2)}, u32[]{:S(2)}) collective-permute-start(bf16[8,3584]{1,0:T(8,128)(2,1)S(1)} %get-tuple-element.94), channel_id=1, source_target_pairs={{0,16},{1,17},{2,18},{3,19},{4,20},{5,21},{6,22},{7,23},{8,24},{9,... | collective-permute-start | bytes 172040 | tf_op jit(solution)/shard_map/ppermute | solution.py:26
  9.1 1.3 %collective-permute-start.5 = (bf16[8,3584]{1,0:T(8,128)(2,1)S(1)}, bf16[8,3584]{1,0:T(8,128)(2,1)S(1)}, u32[]{:S(2)}, u32[]{:S(2)}) collective-permute-start(bf16[8,3584]{1,0:T(8,128)(2,1)S(1)} %get-tuple-element.94), channel_id=1, source_target_pairs={{0,24},{1,25},{2,26},{3,27},{4,28},{5,29},{6,30},{7,31},{8,0},{9,1... | collective-permute-start | bytes 172040 | tf_op jit(solution)/shard_map/ppermute | solution.py:26
  10.4 4.3 %shard_map.122 = (bf16[1,7168,256]{2,1,0:T(8,128)(2,1)S(1)}, bf16[1,7168,256]{2,1,0:T(8,128)(2,1)S(1)}, bf16[1,256,7168]{2,1,0:T(8,128)(2,1)S(1)}) custom-call(bf16[1,7168,256]{2,1,0:T(8,128)(2,1)} %refs_0_.2, bf16[1,7168,256]{2,1,0:T(8,128)(2,1)} %refs_1_.2, bf16[1,256,7168]{2,1,0:T(8,128)(2,1)} %refs_2_.2), custom_call_target="tpu_custom_call" | custom-call | bytes 22020096 | tf_op jit(solution)/shard_map/pallas_call | solution.py:127
  15.3 2.5 %fusion.3 = (f32[8]{0:T(128)S(1)}, f32[8]{0:T(128)S(1)}, f32[8]{0:T(128)S(1)}, f32[8]{0:T(128)S(1)}) fusion(f32[8,2]{0,1:T(2,128)S(1)} %copy-done.5, s32[8,2]{0,1:T(2,128)S(1)} %copy-done.6, s32[]{:T(128)} %bitcast.3, s32[]{:T(128)} %bitcast.1, s32[]{:T(128)} %bitcast, s32[]{:T(128)} %bitcast.2), kind=kLoop, calls=%fused_computation.35 | loop fusion | flops 160 | bytes 272 | tf_op jit(solution)/shard_map/reduce_sum | solution.py:261
  17.9 2.2 %collective-permute-start.7 = (bf16[32,3584]{1,0:T(8,128)(2,1)S(1)}, bf16[32,3584]{1,0:T(8,128)(2,1)S(1)}, u32[]{:S(2)}, u32[]{:S(2)}) collective-permute-start(bf16[32,3584]{1,0:T(8,128)(2,1)S(1)} %constant_dynamic-update-slice_fusion.refs_0_), channel_id=1, source_target_pairs={{0,4},{1,3},{2,6},{3,1},{4,0},{5,7},{6,2},{7,5},{8,12},{9,11},{10,... | collective-permute-start | bytes 688136 | tf_op jit(solution)/shard_map/ppermute | solution.py:26
  20.1 2.1 %collective-permute-start.8 = (bf16[32,3584]{1,0:T(8,128)(2,1)S(1)}, bf16[32,3584]{1,0:T(8,128)(2,1)S(1)}, u32[]{:S(2)}, u32[]{:S(2)}) collective-permute-start(bf16[32,3584]{1,0:T(8,128)(2,1)S(1)} %constant_dynamic-update-slice_fusion.refs_0_), channel_id=1, source_target_pairs={{0,2},{1,5},{2,0},{3,7},{4,6},{5,1},{6,4},{7,3},{8,10},{9,13},{10,... | collective-permute-start | bytes 688136 | tf_op jit(solution)/shard_map/ppermute | solution.py:26
  22.2 3.5 %collective-permute-done.7.refs_1_ = bf16[32,3584]{1,0:T(8,128)(2,1)S(1)} collective-permute-done((bf16[32,3584]{1,0:T(8,128)(2,1)S(1)}, bf16[32,3584]{1,0:T(8,128)(2,1)S(1)}, u32[]{:S(2)}, u32[]{:S(2)}) %collective-permute-start.7) | collective-permute-done | bytes 229408 | tf_op jit(solution)/shard_map/ppermute | solution.py:26
  25.7 2.5 %collective-permute-start.9 = (bf16[32,3584]{1,0:T(8,128)(2,1)S(1)}, bf16[32,3584]{1,0:T(8,128)(2,1)S(1)}, u32[]{:S(2)}, u32[]{:S(2)}) collective-permute-start(bf16[32,3584]{1,0:T(8,128)(2,1)S(1)} %collective-permute-done.7.refs_1_), channel_id=1, source_target_pairs={{0,2},{1,5},{2,0},{3,7},{4,6},{5,1},{6,4},{7,3},{8,10},{9,13},{10,... | collective-permute-start | bytes 688136 | tf_op jit(solution)/shard_map/ppermute | solution.py:26
  28.2 0.7 collective-permute-start.1
  28.8 1.4 %collective-permute-start.2 = (bf16[8,3584]{1,0:T(8,128)(2,1)S(1)}, bf16[8,3584]{1,0:T(8,128)(2,1)S(1)}, u32[]{:S(2)}, u32[]{:S(2)}) collective-permute-start(bf16[8,3584]{1,0:T(8,128)(2,1)S(1)} %get-tuple-element.98), channel_id=1, source_target_pairs={{0,16},{1,17},{2,18},{3,19},{4,20},{5,21},{6,22},{7,23},{8,24},{9,... | collective-permute-start | bytes 172040 | tf_op jit(solution)/shard_map/ppermute | solution.py:26
  30.3 1.7 %collective-permute-start.3 = (bf16[8,3584]{1,0:T(8,128)(2,1)S(1)}, bf16[8,3584]{1,0:T(8,128)(2,1)S(1)}, u32[]{:S(2)}, u32[]{:S(2)}) collective-permute-start(bf16[8,3584]{1,0:T(8,128)(2,1)S(1)} %get-tuple-element.98), channel_id=1, source_target_pairs={{0,24},{1,25},{2,26},{3,27},{4,28},{5,29},{6,30},{7,31},{8,0},{9,1... | collective-permute-start | bytes 172040 | tf_op jit(solution)/shard_map/ppermute | solution.py:26
  32.0 2.8 %collective-permute-done.1 = bf16[8,3584]{1,0:T(8,128)(2,1)S(1)} collective-permute-done((bf16[8,3584]{1,0:T(8,128)(2,1)S(1)}, bf16[8,3584]{1,0:T(8,128)(2,1)S(1)}, u32[]{:S(2)}, u32[]{:S(2)}) %collective-permute-start.1) | collective-permute-done | bytes 57376 | tf_op jit(solution)/shard_map/ppermute | solution.py:26
  34.8 1.8 %collective-permute-done.2 = bf16[8,3584]{1,0:T(8,128)(2,1)S(1)} collective-permute-done((bf16[8,3584]{1,0:T(8,128)(2,1)S(1)}, bf16[8,3584]{1,0:T(8,128)(2,1)S(1)}, u32[]{:S(2)}, u32[]{:S(2)}) %collective-permute-start.2) | collective-permute-done | bytes 57376 | tf_op jit(solution)/shard_map/ppermute | solution.py:26
  37.1 0.8 collective-permute-start.10
  37.9 1.0 collective-permute-start.12
  38.9 6.0 %collective-permute-done.15.refs_2_ = bf16[32,3584]{1,0:T(8,128)(2,1)S(1)} collective-permute-done((bf16[32,3584]{1,0:T(8,128)(2,1)S(1)}, bf16[32,3584]{1,0:T(8,128)(2,1)S(1)}, u32[]{:S(2)}, u32[]{:S(2)}) %collective-permute-start.15) | collective-permute-done | bytes 229408 | tf_op jit(solution)/shard_map/ppermute | solution.py:26
  45.5 0.9 collective-permute-done.13.refs_6_
  46.8 1.8 %shard_map.123 = (f32[256,256]{1,0:T(8,128)S(1)}, f32[256,256]{1,0:T(8,128)S(1)}) custom-call(bf16[32,3584]{1,0:T(8,128)(2,1)S(1)} %constant_dynamic-update-slice_fusion.refs_0_, bf16[32,3584]{1,0:T(8,128)(2,1)S(1)} %collective-permute-done.7.refs_1_, bf16[32,3584]{1,0:T(8,128)(2,1)S(1)} %collective-permute-done.8.refs_2_, ...), custom_call_target="tpu_custom_call" | custom-call | flops 939524096 | bytes 5505024 | tf_op jit(solution)/shard_map/pallas_call | solution.py:193
  48.6 2.9 %collective-permute-done.16.refs_3_ = bf16[32,3584]{1,0:T(8,128)(2,1)S(1)} collective-permute-done((bf16[32,3584]{1,0:T(8,128)(2,1)S(1)}, bf16[32,3584]{1,0:T(8,128)(2,1)S(1)}, u32[]{:S(2)}, u32[]{:S(2)}) %collective-permute-start.16) | collective-permute-done | bytes 229408 | tf_op jit(solution)/shard_map/ppermute | solution.py:26
  51.5 0.7 collective-permute-start.23
  54.7 4.3 %shard_map.124 = (bf16[128,7168]{1,0:T(8,128)(2,1)S(1)}, bf16[64,7168]{1,0:T(8,128)(2,1)S(1)}, bf16[64,7168]{1,0:T(8,128)(2,1)S(1)}) custom-call(bf16[32,3584]{1,0:T(8,128)(2,1)S(1)} %constant_dynamic-update-slice_fusion.4.refs_0_, bf16[32,3584]{1,0:T(8,128)(2,1)S(1)} %collective-permute-done.10.refs_1_, ...), custom_call_target="tpu_custom_call" | custom-call | flops 1879048192 | bytes 12845056 | tf_op jit(solution)/shard_map/pallas_call | solution.py:215
  59.1 1.8 %collective-permute-start.24 = (bf16[64,7168]{1,0:T(8,128)(2,1)S(1)}, bf16[64,7168]{1,0:T(8,128)(2,1)S(1)}, u32[]{:S(2)}, u32[]{:S(2)}) collective-permute-start(bf16[64,7168]{1,0:T(8,128)(2,1)S(1)} %get-tuple-element.129), channel_id=1, source_target_pairs={{0,1},{1,0},{2,3},{3,2},{4,5},{5,4},{6,7},{7,6},{8,9},{9,8},{10,11... | collective-permute-start | bytes 2752520 | tf_op jit(solution)/shard_map/ppermute | solution.py:26
  60.9 0.7 collective-permute-start.25
  61.6 0.7 collective-permute-start.22
  62.3 0.7 collective-permute-done.24
  63.0 5.1 %collective-permute-start.27 = (bf16[32,3584]{1,0:T(8,128)(2,1)S(1)}, bf16[32,3584]{1,0:T(8,128)(2,1)S(1)}, u32[]{:S(2)}, u32[]{:S(2)}) collective-permute-start(bf16[32,3584]{1,0:T(8,128)(2,1)S(1)} %add_convert_fusion.5), channel_id=1, source_target_pairs={{0,2},{1,5},{2,0},{3,7},{4,6},{5,1},{6,4},{7,3},{8,10},{9,13},{10,... | collective-permute-start | bytes 688136 | tf_op jit(solution)/shard_map/ppermute | solution.py:26
  68.1 4.6 %collective-permute-done.27 = bf16[32,3584]{1,0:T(8,128)(2,1)S(1)} collective-permute-done((bf16[32,3584]{1,0:T(8,128)(2,1)S(1)}, bf16[32,3584]{1,0:T(8,128)(2,1)S(1)}, u32[]{:S(2)}, u32[]{:S(2)}) %collective-permute-start.27) | collective-permute-done | bytes 229408 | tf_op jit(solution)/shard_map/ppermute | solution.py:26
  73.0 2.0 %collective-permute-start.28 = (bf16[32,3584]{1,0:T(8,128)(2,1)S(1)}, bf16[32,3584]{1,0:T(8,128)(2,1)S(1)}, u32[]{:S(2)}, u32[]{:S(2)}) collective-permute-start(bf16[32,3584]{1,0:T(8,128)(2,1)S(1)} %get-tuple-element.134), channel_id=1, source_target_pairs={{0,4},{1,3},{2,6},{3,1},{4,0},{5,7},{6,2},{7,5},{8,12},{9,11},{10,... | collective-permute-start | bytes 688136 | tf_op jit(solution)/shard_map/ppermute | solution.py:26
  75.0 1.2 %collective-permute-start.26 = (bf16[32,3584]{1,0:T(8,128)(2,1)S(1)}, bf16[32,3584]{1,0:T(8,128)(2,1)S(1)}, u32[]{:S(2)}, u32[]{:S(2)}) collective-permute-start(bf16[32,3584]{1,0:T(8,128)(2,1)S(1)} %get-tuple-element.180), channel_id=1, source_target_pairs={{0,2},{1,5},{2,0},{3,7},{4,6},{5,1},{6,4},{7,3},{8,10},{9,13},{10,... | collective-permute-start | bytes 688136 | tf_op jit(solution)/shard_map/ppermute | solution.py:26
  76.2 0.9 collective-permute-start.29
  77.1 2.0 %collective-permute-done.28 = bf16[32,3584]{1,0:T(8,128)(2,1)S(1)} collective-permute-done((bf16[32,3584]{1,0:T(8,128)(2,1)S(1)}, bf16[32,3584]{1,0:T(8,128)(2,1)S(1)}, u32[]{:S(2)}, u32[]{:S(2)}) %collective-permute-start.28) | collective-permute-done | bytes 229408 | tf_op jit(solution)/shard_map/ppermute | solution.py:26
  79.1 4.3 %collective-permute-done.26 = bf16[32,3584]{1,0:T(8,128)(2,1)S(1)} collective-permute-done((bf16[32,3584]{1,0:T(8,128)(2,1)S(1)}, bf16[32,3584]{1,0:T(8,128)(2,1)S(1)}, u32[]{:S(2)}, u32[]{:S(2)}) %collective-permute-start.26) | collective-permute-done | bytes 229408 | tf_op jit(solution)/shard_map/ppermute | solution.py:26
  83.5 2.3 %collective-permute-done.29 = bf16[32,3584]{1,0:T(8,128)(2,1)S(1)} collective-permute-done((bf16[32,3584]{1,0:T(8,128)(2,1)S(1)}, bf16[32,3584]{1,0:T(8,128)(2,1)S(1)}, u32[]{:S(2)}, u32[]{:S(2)}) %collective-permute-start.29) | collective-permute-done | bytes 229408 | tf_op jit(solution)/shard_map/ppermute | solution.py:26
  86.0 0.8 collective-permute-start.30
  86.8 2.0 %collective-permute-start.31 = (bf16[32,3584]{1,0:T(8,128)(2,1)S(1)}, bf16[32,3584]{1,0:T(8,128)(2,1)S(1)}, u32[]{:S(2)}, u32[]{:S(2)}) collective-permute-start(bf16[32,3584]{1,0:T(8,128)(2,1)S(1)} %get-tuple-element.182), channel_id=1, source_target_pairs={{0,2},{1,5},{2,0},{3,7},{4,6},{5,1},{6,4},{7,3},{8,10},{9,13},{10,... | collective-permute-start | bytes 688136 | tf_op jit(solution)/shard_map/ppermute | solution.py:26
  88.8 3.0 %collective-permute-start.32 = (bf16[8,3584]{1,0:T(8,128)(2,1)S(1)}, bf16[8,3584]{1,0:T(8,128)(2,1)S(1)}, u32[]{:S(2)}, u32[]{:S(2)}) collective-permute-start(bf16[8,3584]{1,0:T(8,128)(2,1)S(1)} %get-tuple-element.139), channel_id=1, source_target_pairs={{0,24},{1,25},{2,26},{3,27},{4,28},{5,29},{6,30},{7,31},{8,0},{9,1... | collective-permute-start | bytes 172040 | tf_op jit(solution)/shard_map/ppermute | solution.py:26
  91.8 0.8 collective-permute-start.33
  92.7 0.9 collective-permute-done.32
  93.7 3.5 %collective-permute-done.33 = bf16[8,3584]{1,0:T(8,128)(2,1)S(1)} collective-permute-done((bf16[8,3584]{1,0:T(8,128)(2,1)S(1)}, bf16[8,3584]{1,0:T(8,128)(2,1)S(1)}, u32[]{:S(2)}, u32[]{:S(2)}) %collective-permute-start.33) | collective-permute-done | bytes 57376 | tf_op jit(solution)/shard_map/ppermute | solution.py:26
  97.2 1.4 %collective-permute-done.34 = bf16[8,3584]{1,0:T(8,128)(2,1)S(1)} collective-permute-done((bf16[8,3584]{1,0:T(8,128)(2,1)S(1)}, bf16[8,3584]{1,0:T(8,128)(2,1)S(1)}, u32[]{:S(2)}, u32[]{:S(2)}) %collective-permute-start.34) | collective-permute-done | bytes 57376 | tf_op jit(solution)/shard_map/ppermute | solution.py:26
  99.4 2.9 %collective-permute-start.35 = (bf16[8,3584]{1,0:T(8,128)(2,1)S(1)}, bf16[8,3584]{1,0:T(8,128)(2,1)S(1)}, u32[]{:S(2)}, u32[]{:S(2)}) collective-permute-start(bf16[8,3584]{1,0:T(8,128)(2,1)S(1)} %get-tuple-element.149), channel_id=1, source_target_pairs={{0,24},{1,25},{2,26},{3,27},{4,28},{5,29},{6,30},{7,31},{8,0},{9,1... | collective-permute-start | bytes 172040 | tf_op jit(solution)/shard_map/ppermute | solution.py:26
  102.4 0.8 collective-permute-start.37
  103.2 2.5 %shard_map.125 = bf16[8,64,512]{2,1,0:T(8,128)(2,1)} custom-call(s32[8]{0:T(128)S(1)} %copy-done.3, s32[8]{0:T(128)S(1)} %copy-done.4, bf16[8,64,576]{2,1,0:T(8,128)(2,1)S(1)} %copy-done.1, bf16[8,96,576]{2,1,0:T(8,128)(2,1)S(1)} %copy-done, bf16[8,96,576]{2,1,0:T(8,128)(2,1)S(1)} %collective-permute-done.17.refs_4_, bf16[8,576]{1,0:T(8,128)(2,1)S(1)} %copy-done.2, ...), custom_call_target="tpu_custom_call" | custom-call | flops 106954752 | bytes 4653056 | tf_op jit(solution)/shard_map/pallas_call | solution.py:99
  105.7 4.5 %collective-permute-done.36 = bf16[8,3584]{1,0:T(8,128)(2,1)S(1)} collective-permute-done((bf16[8,3584]{1,0:T(8,128)(2,1)S(1)}, bf16[8,3584]{1,0:T(8,128)(2,1)S(1)}, u32[]{:S(2)}, u32[]{:S(2)}) %collective-permute-start.36) | collective-permute-done | bytes 57376 | tf_op jit(solution)/shard_map/ppermute | solution.py:26
  (72 shorter events, 7.0 us)
Async XLA Ops:
  1.8 16.0 %collective-permute-start.6 = (bf16[6,96,576]{2,1,0:T(8,128)(2,1)S(1)}, bf16[6,96,576]{2,1,0:T(8,128)(2,1)S(1)}, u32[]{:S(2)}, u32[]{:S(2)}) collective-permute-start(bf16[6,96,576]{2,1,0:T(8,128)(2,1)S(1)} %slice.191), channel_id=1, source_target_pairs={{1,2},{3,4},{5,6},{6,5},{9,10},{11,12},{13,14},{14,13},{17,18},{19... | collective-permute-start | bytes 1990664 | tf_op jit(solution)/shard_map/ppermute | solution.py:47
  3.4 14.4 %collective-permute-start = (bf16[8,3584]{1,0:T(8,128)(2,1)S(1)}, bf16[8,3584]{1,0:T(8,128)(2,1)S(1)}, u32[]{:S(2)}, u32[]{:S(2)}) collective-permute-start(bf16[8,3584]{1,0:T(8,128)(2,1)S(1)} %get-tuple-element.94), channel_id=1, source_target_pairs={{0,8},{1,9},{2,10},{3,11},{4,12},{5,13},{6,14},{7,15},{8,16},{9,17... | collective-permute-start | bytes 172040 | tf_op jit(solution)/shard_map/ppermute | solution.py:26
  6.5 11.4 %collective-permute-start.4 = (bf16[8,3584]{1,0:T(8,128)(2,1)S(1)}, bf16[8,3584]{1,0:T(8,128)(2,1)S(1)}, u32[]{:S(2)}, u32[]{:S(2)}) collective-permute-start(bf16[8,3584]{1,0:T(8,128)(2,1)S(1)} %get-tuple-element.94), channel_id=1, source_target_pairs={{0,16},{1,17},{2,18},{3,19},{4,20},{5,21},{6,22},{7,23},{8,24},{9,... | collective-permute-start | bytes 172040 | tf_op jit(solution)/shard_map/ppermute | solution.py:26
  9.1 8.8 %collective-permute-start.5 = (bf16[8,3584]{1,0:T(8,128)(2,1)S(1)}, bf16[8,3584]{1,0:T(8,128)(2,1)S(1)}, u32[]{:S(2)}, u32[]{:S(2)}) collective-permute-start(bf16[8,3584]{1,0:T(8,128)(2,1)S(1)} %get-tuple-element.94), channel_id=1, source_target_pairs={{0,24},{1,25},{2,26},{3,27},{4,28},{5,29},{6,30},{7,31},{8,0},{9,1... | collective-permute-start | bytes 172040 | tf_op jit(solution)/shard_map/ppermute | solution.py:26
  10.4 4.9 %copy-start.5 = (f32[8,2]{0,1:T(2,128)S(1)}, f32[8,2]{0,1:T(2,128)}, u32[]{:S(2)}) copy-start(f32[8,2]{0,1:T(2,128)} %param.18) | copy-start | bytes 196
  10.4 4.9 %copy-start.6 = (s32[8,2]{0,1:T(2,128)S(1)}, s32[8,2]{0,1:T(2,128)}, u32[]{:S(2)}) copy-start(s32[8,2]{0,1:T(2,128)} %param.17) | copy-start | bytes 196
  10.4 24.4 %copy-start = (bf16[8,96,576]{2,1,0:T(8,128)(2,1)S(1)}, bf16[8,96,576]{2,1,0:T(8,128)(2,1)}, u32[]{:S(2)}) copy-start(bf16[8,96,576]{2,1,0:T(8,128)(2,1)} %refs_3_.1) | copy-start | bytes 2654212
  17.9 7.7 %collective-permute-start.7 = (bf16[32,3584]{1,0:T(8,128)(2,1)S(1)}, bf16[32,3584]{1,0:T(8,128)(2,1)S(1)}, u32[]{:S(2)}, u32[]{:S(2)}) collective-permute-start(bf16[32,3584]{1,0:T(8,128)(2,1)S(1)} %constant_dynamic-update-slice_fusion.refs_0_), channel_id=1, source_target_pairs={{0,4},{1,3},{2,6},{3,1},{4,0},{5,7},{6,2},{7,5},{8,12},{9,11},{10,... | collective-permute-start | bytes 688136 | tf_op jit(solution)/shard_map/ppermute | solution.py:26
  20.1 16.4 %collective-permute-start.8 = (bf16[32,3584]{1,0:T(8,128)(2,1)S(1)}, bf16[32,3584]{1,0:T(8,128)(2,1)S(1)}, u32[]{:S(2)}, u32[]{:S(2)}) collective-permute-start(bf16[32,3584]{1,0:T(8,128)(2,1)S(1)} %constant_dynamic-update-slice_fusion.refs_0_), channel_id=1, source_target_pairs={{0,2},{1,5},{2,0},{3,7},{4,6},{5,1},{6,4},{7,3},{8,10},{9,13},{10,... | collective-permute-start | bytes 688136 | tf_op jit(solution)/shard_map/ppermute | solution.py:26
  25.7 10.9 %collective-permute-start.9 = (bf16[32,3584]{1,0:T(8,128)(2,1)S(1)}, bf16[32,3584]{1,0:T(8,128)(2,1)S(1)}, u32[]{:S(2)}, u32[]{:S(2)}) collective-permute-start(bf16[32,3584]{1,0:T(8,128)(2,1)S(1)} %collective-permute-done.7.refs_1_), channel_id=1, source_target_pairs={{0,2},{1,5},{2,0},{3,7},{4,6},{5,1},{6,4},{7,3},{8,10},{9,13},{10,... | collective-permute-start | bytes 688136 | tf_op jit(solution)/shard_map/ppermute | solution.py:26
  28.2 6.6 %collective-permute-start.1 = (bf16[8,3584]{1,0:T(8,128)(2,1)S(1)}, bf16[8,3584]{1,0:T(8,128)(2,1)S(1)}, u32[]{:S(2)}, u32[]{:S(2)}) collective-permute-start(bf16[8,3584]{1,0:T(8,128)(2,1)S(1)} %get-tuple-element.98), channel_id=1, source_target_pairs={{0,8},{1,9},{2,10},{3,11},{4,12},{5,13},{6,14},{7,15},{8,16},{9,17... | collective-permute-start | bytes 172040 | tf_op jit(solution)/shard_map/ppermute | solution.py:26
  28.8 7.7 %collective-permute-start.2 = (bf16[8,3584]{1,0:T(8,128)(2,1)S(1)}, bf16[8,3584]{1,0:T(8,128)(2,1)S(1)}, u32[]{:S(2)}, u32[]{:S(2)}) collective-permute-start(bf16[8,3584]{1,0:T(8,128)(2,1)S(1)} %get-tuple-element.98), channel_id=1, source_target_pairs={{0,16},{1,17},{2,18},{3,19},{4,20},{5,21},{6,22},{7,23},{8,24},{9,... | collective-permute-start | bytes 172040 | tf_op jit(solution)/shard_map/ppermute | solution.py:26
  30.3 6.3 %collective-permute-start.3 = (bf16[8,3584]{1,0:T(8,128)(2,1)S(1)}, bf16[8,3584]{1,0:T(8,128)(2,1)S(1)}, u32[]{:S(2)}, u32[]{:S(2)}) collective-permute-start(bf16[8,3584]{1,0:T(8,128)(2,1)S(1)} %get-tuple-element.98), channel_id=1, source_target_pairs={{0,24},{1,25},{2,26},{3,27},{4,28},{5,29},{6,30},{7,31},{8,0},{9,1... | collective-permute-start | bytes 172040 | tf_op jit(solution)/shard_map/ppermute | solution.py:26
  34.8 13.8 %collective-permute-start.17 = (bf16[8,96,576]{2,1,0:T(8,128)(2,1)S(1)}, bf16[8,96,576]{2,1,0:T(8,128)(2,1)S(1)}, u32[]{:S(2)}, u32[]{:S(2)}) collective-permute-start(bf16[8,96,576]{2,1,0:T(8,128)(2,1)S(1)} %copy-done), channel_id=1, source_target_pairs={{0,1},{1,0},{2,3},{3,2},{4,5},{5,4},{6,7},{7,6},{8,9},{9,8},{10,11... | collective-permute-start | bytes 2654216 | tf_op jit(solution)/shard_map/ppermute | solution.py:26
  36.6 8.4 %collective-permute-start.15 = (bf16[32,3584]{1,0:T(8,128)(2,1)S(1)}, bf16[32,3584]{1,0:T(8,128)(2,1)S(1)}, u32[]{:S(2)}, u32[]{:S(2)}) collective-permute-start(bf16[32,3584]{1,0:T(8,128)(2,1)S(1)} %constant_dynamic-update-slice_fusion.4.refs_0_), channel_id=1, source_target_pairs={{0,2},{1,5},{2,0},{3,7},{4,6},{5,1},{6,4},{7,3},{8,10},{9,13},{10,... | collective-permute-start | bytes 688136 | tf_op jit(solution)/shard_map/ppermute | solution.py:26
  36.7 8.3 %collective-permute-start.11 = (bf16[32,3584]{1,0:T(8,128)(2,1)S(1)}, bf16[32,3584]{1,0:T(8,128)(2,1)S(1)}, u32[]{:S(2)}, u32[]{:S(2)}) collective-permute-start(bf16[32,3584]{1,0:T(8,128)(2,1)S(1)} %constant_dynamic-update-slice_fusion.refs_0_), channel_id=1, source_target_pairs={{0,1},{1,0},{2,3},{3,2},{4,5},{5,4},{6,7},{7,6},{8,9},{9,8},{10,11... | collective-permute-start | bytes 688136 | tf_op jit(solution)/shard_map/ppermute | solution.py:26
  37.1 8.4 %collective-permute-start.10 = (bf16[32,3584]{1,0:T(8,128)(2,1)S(1)}, bf16[32,3584]{1,0:T(8,128)(2,1)S(1)}, u32[]{:S(2)}, u32[]{:S(2)}) collective-permute-start(bf16[32,3584]{1,0:T(8,128)(2,1)S(1)} %constant_dynamic-update-slice_fusion.4.refs_0_), channel_id=1, source_target_pairs={{0,4},{1,3},{2,6},{3,1},{4,0},{5,7},{6,2},{7,5},{8,12},{9,11},{10,... | collective-permute-start | bytes 688136 | tf_op jit(solution)/shard_map/ppermute | solution.py:26
  37.9 7.6 %collective-permute-start.12 = (bf16[32,3584]{1,0:T(8,128)(2,1)S(1)}, bf16[32,3584]{1,0:T(8,128)(2,1)S(1)}, u32[]{:S(2)}, u32[]{:S(2)}) collective-permute-start(bf16[32,3584]{1,0:T(8,128)(2,1)S(1)} %collective-permute-done.7.refs_1_), channel_id=1, source_target_pairs={{0,1},{1,0},{2,3},{3,2},{4,5},{5,4},{6,7},{7,6},{8,9},{9,8},{10,11... | collective-permute-start | bytes 688136 | tf_op jit(solution)/shard_map/ppermute | solution.py:26
  45.0 1.5 %collective-permute-start.13 = (bf16[32,3584]{1,0:T(8,128)(2,1)S(1)}, bf16[32,3584]{1,0:T(8,128)(2,1)S(1)}, u32[]{:S(2)}, u32[]{:S(2)}) collective-permute-start(bf16[32,3584]{1,0:T(8,128)(2,1)S(1)} %collective-permute-done.8.refs_2_), channel_id=1, source_target_pairs={{0,1},{1,0},{2,3},{3,2},{4,5},{5,4},{6,7},{7,6},{8,9},{9,8},{10,11... | collective-permute-start | bytes 688136 | tf_op jit(solution)/shard_map/ppermute | solution.py:26
  45.0 1.8 %collective-permute-start.14 = (bf16[32,3584]{1,0:T(8,128)(2,1)S(1)}, bf16[32,3584]{1,0:T(8,128)(2,1)S(1)}, u32[]{:S(2)}, u32[]{:S(2)}) collective-permute-start(bf16[32,3584]{1,0:T(8,128)(2,1)S(1)} %collective-permute-done.9.refs_3_), channel_id=1, source_target_pairs={{0,1},{1,0},{2,3},{3,2},{4,5},{5,4},{6,7},{7,6},{8,9},{9,8},{10,11... | collective-permute-start | bytes 688136 | tf_op jit(solution)/shard_map/ppermute | solution.py:26
  45.5 6.0 %collective-permute-start.16 = (bf16[32,3584]{1,0:T(8,128)(2,1)S(1)}, bf16[32,3584]{1,0:T(8,128)(2,1)S(1)}, u32[]{:S(2)}, u32[]{:S(2)}) collective-permute-start(bf16[32,3584]{1,0:T(8,128)(2,1)S(1)} %collective-permute-done.10.refs_1_), channel_id=1, source_target_pairs={{0,2},{1,5},{2,0},{3,7},{4,6},{5,1},{6,4},{7,3},{8,10},{9,13},{10,... | collective-permute-start | bytes 688136 | tf_op jit(solution)/shard_map/ppermute | solution.py:26
  51.5 7.5 %collective-permute-start.23 = (bf16[4,96,576]{2,1,0:T(8,128)(2,1)S(1)}, bf16[4,96,576]{2,1,0:T(8,128)(2,1)S(1)}, u32[]{:S(2)}, u32[]{:S(2)}) collective-permute-start(bf16[4,96,576]{2,1,0:T(8,128)(2,1)S(1)} %slice.196), channel_id=1, source_target_pairs={{2,1},{4,3},{7,8},{8,7},{10,9},{12,11},{15,16},{16,15},{18,17},{20... | collective-permute-start | bytes 1327112 | tf_op jit(solution)/shard_map/ppermute | solution.py:47
  52.2 1.6 %collective-permute-start.18 = (bf16[32,3584]{1,0:T(8,128)(2,1)S(1)}, bf16[32,3584]{1,0:T(8,128)(2,1)S(1)}, u32[]{:S(2)}, u32[]{:S(2)}) collective-permute-start(bf16[32,3584]{1,0:T(8,128)(2,1)S(1)} %constant_dynamic-update-slice_fusion.4.refs_0_), channel_id=1, source_target_pairs={{0,1},{1,0},{2,3},{3,2},{4,5},{5,4},{6,7},{7,6},{8,9},{9,8},{10,11... | collective-permute-start | bytes 688136 | tf_op jit(solution)/shard_map/ppermute | solution.py:26
  52.3 1.8 %collective-permute-start.20 = (bf16[32,3584]{1,0:T(8,128)(2,1)S(1)}, bf16[32,3584]{1,0:T(8,128)(2,1)S(1)}, u32[]{:S(2)}, u32[]{:S(2)}) collective-permute-start(bf16[32,3584]{1,0:T(8,128)(2,1)S(1)} %collective-permute-done.15.refs_2_), channel_id=1, source_target_pairs={{0,1},{1,0},{2,3},{3,2},{4,5},{5,4},{6,7},{7,6},{8,9},{9,8},{10,11... | collective-permute-start | bytes 688136 | tf_op jit(solution)/shard_map/ppermute | solution.py:26
  52.8 1.6 %collective-permute-start.19 = (bf16[32,3584]{1,0:T(8,128)(2,1)S(1)}, bf16[32,3584]{1,0:T(8,128)(2,1)S(1)}, u32[]{:S(2)}, u32[]{:S(2)}) collective-permute-start(bf16[32,3584]{1,0:T(8,128)(2,1)S(1)} %collective-permute-done.10.refs_1_), channel_id=1, source_target_pairs={{0,1},{1,0},{2,3},{3,2},{4,5},{5,4},{6,7},{7,6},{8,9},{9,8},{10,11... | collective-permute-start | bytes 688136 | tf_op jit(solution)/shard_map/ppermute | solution.py:26
  52.8 1.9 %collective-permute-start.21 = (bf16[32,3584]{1,0:T(8,128)(2,1)S(1)}, bf16[32,3584]{1,0:T(8,128)(2,1)S(1)}, u32[]{:S(2)}, u32[]{:S(2)}) collective-permute-start(bf16[32,3584]{1,0:T(8,128)(2,1)S(1)} %collective-permute-done.16.refs_3_), channel_id=1, source_target_pairs={{0,1},{1,0},{2,3},{3,2},{4,5},{5,4},{6,7},{7,6},{8,9},{9,8},{10,11... | collective-permute-start | bytes 688136 | tf_op jit(solution)/shard_map/ppermute | solution.py:26
  59.1 3.9 %collective-permute-start.24 = (bf16[64,7168]{1,0:T(8,128)(2,1)S(1)}, bf16[64,7168]{1,0:T(8,128)(2,1)S(1)}, u32[]{:S(2)}, u32[]{:S(2)}) collective-permute-start(bf16[64,7168]{1,0:T(8,128)(2,1)S(1)} %get-tuple-element.129), channel_id=1, source_target_pairs={{0,1},{1,0},{2,3},{3,2},{4,5},{5,4},{6,7},{7,6},{8,9},{9,8},{10,11... | collective-permute-start | bytes 2752520 | tf_op jit(solution)/shard_map/ppermute | solution.py:26
  60.9 2.1 %collective-permute-start.25 = (bf16[2,96,576]{2,1,0:T(8,128)(2,1)S(1)}, bf16[2,96,576]{2,1,0:T(8,128)(2,1)S(1)}, u32[]{:S(2)}, u32[]{:S(2)}) collective-permute-start(bf16[2,96,576]{2,1,0:T(8,128)(2,1)S(1)} %get-tuple-element.130), channel_id=1, source_target_pairs={{2,1},{4,3},{7,8},{8,7},{10,9},{12,11},{15,16},{16,15},{18,17},{20... | collective-permute-start | bytes 663560 | tf_op jit(solution)/shard_map/ppermute | solution.py:47
  61.6 6.6 %collective-permute-start.22 = (bf16[64,7168]{1,0:T(8,128)(2,1)S(1)}, bf16[64,7168]{1,0:T(8,128)(2,1)S(1)}, u32[]{:S(2)}, u32[]{:S(2)}) collective-permute-start(bf16[64,7168]{1,0:T(8,128)(2,1)S(1)} %get-tuple-element.126), channel_id=1, source_target_pairs={{0,1},{1,0},{2,3},{3,2},{4,5},{5,4},{6,7},{7,6},{8,9},{9,8},{10,11... | collective-permute-start | bytes 2752520 | tf_op jit(solution)/shard_map/ppermute | solution.py:26
  63.0 9.8 %collective-permute-start.27 = (bf16[32,3584]{1,0:T(8,128)(2,1)S(1)}, bf16[32,3584]{1,0:T(8,128)(2,1)S(1)}, u32[]{:S(2)}, u32[]{:S(2)}) collective-permute-start(bf16[32,3584]{1,0:T(8,128)(2,1)S(1)} %add_convert_fusion.5), channel_id=1, source_target_pairs={{0,2},{1,5},{2,0},{3,7},{4,6},{5,1},{6,4},{7,3},{8,10},{9,13},{10,... | collective-permute-start | bytes 688136 | tf_op jit(solution)/shard_map/ppermute | solution.py:26
  73.0 6.1 %collective-permute-start.28 = (bf16[32,3584]{1,0:T(8,128)(2,1)S(1)}, bf16[32,3584]{1,0:T(8,128)(2,1)S(1)}, u32[]{:S(2)}, u32[]{:S(2)}) collective-permute-start(bf16[32,3584]{1,0:T(8,128)(2,1)S(1)} %get-tuple-element.134), channel_id=1, source_target_pairs={{0,4},{1,3},{2,6},{3,1},{4,0},{5,7},{6,2},{7,5},{8,12},{9,11},{10,... | collective-permute-start | bytes 688136 | tf_op jit(solution)/shard_map/ppermute | solution.py:26
  75.0 28.2 %copy-start.1 = (bf16[8,64,576]{2,1,0:T(8,128)(2,1)S(1)}, bf16[8,64,576]{2,1,0:T(8,128)(2,1)}, u32[]{:S(2)}) copy-start(bf16[8,64,576]{2,1,0:T(8,128)(2,1)} %refs_2_.3) | copy-start | bytes 1769476
  75.0 28.2 %copy-start.2 = (bf16[8,576]{1,0:T(8,128)(2,1)S(1)}, bf16[8,576]{1,0:T(8,128)(2,1)}, u32[]{:S(2)}) copy-start(bf16[8,576]{1,0:T(8,128)(2,1)} %refs_5_.1) | copy-start | bytes 27652
  75.0 28.2 %copy-start.3 = (s32[8]{0:T(128)S(1)}, s32[8]{0:T(128)}, u32[]{:S(2)}) copy-start(s32[8]{0:T(128)} %refs_0_.3) | copy-start | bytes 100
  75.0 28.3 %copy-start.4 = (s32[8]{0:T(128)S(1)}, s32[8]{0:T(128)}, u32[]{:S(2)}) copy-start(s32[8]{0:T(128)} %refs_1_.3) | copy-start | bytes 100
  75.0 8.4 %collective-permute-start.26 = (bf16[32,3584]{1,0:T(8,128)(2,1)S(1)}, bf16[32,3584]{1,0:T(8,128)(2,1)S(1)}, u32[]{:S(2)}, u32[]{:S(2)}) collective-permute-start(bf16[32,3584]{1,0:T(8,128)(2,1)S(1)} %get-tuple-element.180), channel_id=1, source_target_pairs={{0,2},{1,5},{2,0},{3,7},{4,6},{5,1},{6,4},{7,3},{8,10},{9,13},{10,... | collective-permute-start | bytes 688136 | tf_op jit(solution)/shard_map/ppermute | solution.py:26
  76.2 9.6 %collective-permute-start.29 = (bf16[32,3584]{1,0:T(8,128)(2,1)S(1)}, bf16[32,3584]{1,0:T(8,128)(2,1)S(1)}, u32[]{:S(2)}, u32[]{:S(2)}) collective-permute-start(bf16[32,3584]{1,0:T(8,128)(2,1)S(1)} %get-tuple-element.135), channel_id=1, source_target_pairs={{0,2},{1,5},{2,0},{3,7},{4,6},{5,1},{6,4},{7,3},{8,10},{9,13},{10,... | collective-permute-start | bytes 688136 | tf_op jit(solution)/shard_map/ppermute | solution.py:26
  86.0 12.6 %collective-permute-start.30 = (bf16[32,3584]{1,0:T(8,128)(2,1)S(1)}, bf16[32,3584]{1,0:T(8,128)(2,1)S(1)}, u32[]{:S(2)}, u32[]{:S(2)}) collective-permute-start(bf16[32,3584]{1,0:T(8,128)(2,1)S(1)} %get-tuple-element.183), channel_id=1, source_target_pairs={{0,4},{1,3},{2,6},{3,1},{4,0},{5,7},{6,2},{7,5},{8,12},{9,11},{10,... | collective-permute-start | bytes 688136 | tf_op jit(solution)/shard_map/ppermute | solution.py:26
  86.8 11.8 %collective-permute-start.31 = (bf16[32,3584]{1,0:T(8,128)(2,1)S(1)}, bf16[32,3584]{1,0:T(8,128)(2,1)S(1)}, u32[]{:S(2)}, u32[]{:S(2)}) collective-permute-start(bf16[32,3584]{1,0:T(8,128)(2,1)S(1)} %get-tuple-element.182), channel_id=1, source_target_pairs={{0,2},{1,5},{2,0},{3,7},{4,6},{5,1},{6,4},{7,3},{8,10},{9,13},{10,... | collective-permute-start | bytes 688136 | tf_op jit(solution)/shard_map/ppermute | solution.py:26
  88.8 4.9 %collective-permute-start.32 = (bf16[8,3584]{1,0:T(8,128)(2,1)S(1)}, bf16[8,3584]{1,0:T(8,128)(2,1)S(1)}, u32[]{:S(2)}, u32[]{:S(2)}) collective-permute-start(bf16[8,3584]{1,0:T(8,128)(2,1)S(1)} %get-tuple-element.139), channel_id=1, source_target_pairs={{0,24},{1,25},{2,26},{3,27},{4,28},{5,29},{6,30},{7,31},{8,0},{9,1... | collective-permute-start | bytes 172040 | tf_op jit(solution)/shard_map/ppermute | solution.py:26
  91.8 5.4 %collective-permute-start.33 = (bf16[8,3584]{1,0:T(8,128)(2,1)S(1)}, bf16[8,3584]{1,0:T(8,128)(2,1)S(1)}, u32[]{:S(2)}, u32[]{:S(2)}) collective-permute-start(bf16[8,3584]{1,0:T(8,128)(2,1)S(1)} %get-tuple-element.140), channel_id=1, source_target_pairs={{0,16},{1,17},{2,18},{3,19},{4,20},{5,21},{6,22},{7,23},{8,24},{9,... | collective-permute-start | bytes 172040 | tf_op jit(solution)/shard_map/ppermute | solution.py:26
  92.6 6.0 %collective-permute-start.34 = (bf16[8,3584]{1,0:T(8,128)(2,1)S(1)}, bf16[8,3584]{1,0:T(8,128)(2,1)S(1)}, u32[]{:S(2)}, u32[]{:S(2)}) collective-permute-start(bf16[8,3584]{1,0:T(8,128)(2,1)S(1)} %get-tuple-element.141), channel_id=1, source_target_pairs={{0,8},{1,9},{2,10},{3,11},{4,12},{5,13},{6,14},{7,15},{8,16},{9,17... | collective-permute-start | bytes 172040 | tf_op jit(solution)/shard_map/ppermute | solution.py:26
  98.7 4.5 %collective-permute-start.38 = (bf16[2,96,576]{2,1,0:T(8,128)(2,1)S(1)}, bf16[2,96,576]{2,1,0:T(8,128)(2,1)S(1)}, u32[]{:S(2)}, u32[]{:S(2)}) collective-permute-start(bf16[2,96,576]{2,1,0:T(8,128)(2,1)S(1)} %get-tuple-element.156), channel_id=1, source_target_pairs={{1,2},{3,4},{5,6},{6,5},{2,1},{4,3},{7,8},{8,7},{9,10},{11,12},{13... | collective-permute-start | bytes 663560 | tf_op jit(solution)/shard_map/ppermute | solution.py:47
  99.4 6.3 %collective-permute-start.35 = (bf16[8,3584]{1,0:T(8,128)(2,1)S(1)}, bf16[8,3584]{1,0:T(8,128)(2,1)S(1)}, u32[]{:S(2)}, u32[]{:S(2)}) collective-permute-start(bf16[8,3584]{1,0:T(8,128)(2,1)S(1)} %get-tuple-element.149), channel_id=1, source_target_pairs={{0,24},{1,25},{2,26},{3,27},{4,28},{5,29},{6,30},{7,31},{8,0},{9,1... | collective-permute-start | bytes 172040 | tf_op jit(solution)/shard_map/ppermute | solution.py:26
  102.3 7.9 %collective-permute-start.36 = (bf16[8,3584]{1,0:T(8,128)(2,1)S(1)}, bf16[8,3584]{1,0:T(8,128)(2,1)S(1)}, u32[]{:S(2)}, u32[]{:S(2)}) collective-permute-start(bf16[8,3584]{1,0:T(8,128)(2,1)S(1)} %get-tuple-element.150), channel_id=1, source_target_pairs={{0,16},{1,17},{2,18},{3,19},{4,20},{5,21},{6,22},{7,23},{8,24},{9,... | collective-permute-start | bytes 172040 | tf_op jit(solution)/shard_map/ppermute | solution.py:26
  102.4 7.9 %collective-permute-start.37 = (bf16[8,3584]{1,0:T(8,128)(2,1)S(1)}, bf16[8,3584]{1,0:T(8,128)(2,1)S(1)}, u32[]{:S(2)}, u32[]{:S(2)}) collective-permute-start(bf16[8,3584]{1,0:T(8,128)(2,1)S(1)} %get-tuple-element.151), channel_id=1, source_target_pairs={{0,8},{1,9},{2,10},{3,11},{4,12},{5,13},{6,14},{7,15},{8,16},{9,17... | collective-permute-start | bytes 172040 | tf_op jit(solution)/shard_map/ppermute | solution.py:26

commit v10 on v8

--- a/solution.py
+++ b/solution.py
@@ -26,8 +26,8 @@
     return lax.ppermute(value, "dp", [(i, partner(i)) for i in range(peers)])
 
 
-def after(value, other):
-    return lax.optimization_barrier((value, other))[0]
+def tied(*values):
+    return lax.optimization_barrier(values)
 
 
 def added(values):
@@ -47,7 +47,8 @@
     return lax.ppermute(value, "dp", [p for p in pairs if max(p) < peers])
 
 
-def attend_kernel(parents, lengths, query, own, twin, early, late, newest, out):
+def attend_kernel(spans, parents, lengths, query, own, twin, newest, *refs):
+    pieces, out = refs[:-1], refs[-1]
     beams = range(query.shape[0])
     rank = lax.axis_index("dp")
     place = rank % 8
@@ -57,9 +58,16 @@
     rows, scores, probs = [], [], []
     for b in beams:
         slot, holder = parents[b] % len(beams), parents[b] // len(beams)
-        value = jnp.where(arrives_early, early[slot], late[slot])
+        value = own[slot]
         value = jnp.where(holder == (rank ^ 1), twin[slot], value)
-        value = jnp.where(holder == rank, own[slot], value)
+        far = (holder != rank) & (holder != (rank ^ 1))
+        for (kind, low, high), piece in zip(spans, pieces):
+            here = far & (slot >= low) & (slot < high)
+            if kind == "early":
+                here = here & arrives_early
+            if kind == "late":
+                here = here & jnp.logical_not(arrives_early)
+            value = jnp.where(here, piece[jnp.clip(slot - low, 0, high - low - 1)], value)
         value = jnp.where(at < lengths[b] - 1, value, jnp.zeros_like(value))
         row = jnp.broadcast_to(latest[b : b + 1], value.shape).astype(value.dtype)
         rows.append(jnp.where(at == lengths[b] - 1, row, value))
@@ -79,17 +87,17 @@
         out[b] = mixed.astype(out.dtype)
 
 
-def attend(queries, own, twin, early, late, newest, parents, lengths):
+def attend(queries, own, twin, newest, spans, pieces, parents, lengths):
     beam_count, heads, width = queries.shape
     positions = own.shape[1]
     scalars = pl.BlockSpec(memory_space=pltpu.SMEM)
     whole = pl.BlockSpec(memory_space=pltpu.VMEM)
     arrays = [
         pltpu.with_memory_space_constraint(v, pltpu.VMEM)
-        for v in (queries, own, twin, early, late, newest)
+        for v in (queries, own, twin, newest, *pieces)
     ]
     return pl.pallas_call(
-        attend_kernel,
+        lambda *refs: attend_kernel(spans, *refs),
         in_specs=[scalars] * 2 + [whole] * len(arrays),
         out_specs=whole,
         out_shape=jax.ShapeDtypeStruct((beam_count, heads, KV), jnp.bfloat16),
@@ -206,11 +214,11 @@
     route_count = routed_experts.shape[1]
     capacity = min(beam_count, max(2, 2 * beam_count * route_count // expert_count))
     dense = capacity == beam_count
-    assert slices == 8
+    assert slices == 8 and expert_count & (expert_count - 1) == 0
 
     mine = lax.axis_index("dp") // slices
     turns = jnp.arange(expert_count, dtype=jnp.int32)
-    targets = (mine + turns) % expert_count
+    targets = mine ^ turns
     if dense:
         blocks = [expert_input] * expert_count
         mixing = [
@@ -227,7 +235,7 @@
         blocks = list(chosen.astype(jnp.bfloat16).reshape(expert_count, capacity, width))
 
     def ahead(r):
-        return lambda i: (i + r * slices) % devices
+        return lambda i: i ^ (r * slices)
 
     def twin(i):
         return i ^ 1
@@ -238,66 +246,92 @@
     def second(i):
         return i ^ (4 if i & 1 else 2)
 
-    blocks = blocks[:1] + [swapped(blocks[r], ahead(r)) for r in range(1, expert_count)]
-    early = neighbours(latent_cache, EARLY, slices)
-    *blocks, early, mixing = lax.optimization_barrier((*blocks, early, mixing))
-    column = jnp.concatenate(blocks)
+    spans, pieces = [], []
+
+    def cache_rows(kind, begin, end, ready=None):
+        moves = {"early": EARLY, "late": LATE}[kind]
+        source = latent_cache[begin:end]
+        if ready is not None:
+            source, ready = tied(source, ready)
+        spans.append((kind, begin, end))
+        return neighbours(source, moves, slices), ready
+
+    column = blocks[:1] + [swapped(blocks[r], ahead(r)) for r in range(1, expert_count)]
+    early, _ = cache_rows("early", 0, beam_count)
+    weights = fetched([gate_weight, up_weight, down_weight])
+    column, early, weights = tied(column, early, weights)
+    pieces.append(early)
+    column = jnp.concatenate(column)
     near = swapped(column, first)
     side = swapped(column, second)
     across = swapped(near, second)
     beside = swapped(latent_cache, twin)
     twin_column, twin_near = swapped(column, twin), swapped(near, twin)
-    weights = fetched([gate_weight, up_weight, down_weight])
-    across, twin_column, twin_near, weights, beside, latent_cache = lax.optimization_barrier(
-        (across, twin_column, twin_near, weights, beside, latent_cache)
+    across, twin_column, twin_near, beside, mixing = tied(
+        across, twin_column, twin_near, beside, mixing
     )
-    late = neighbours(latent_cache, LATE, slices)
-    held = [column, near, side, across, twin_column, twin_near]
-    held = held + [swapped(side, twin), swapped(across, twin)]
+    late, across = cache_rows("late", 0, beam_count, across)
+    twin_across, side = tied(swapped(across, twin), side)
+    held = [column, near, side, across, twin_column, twin_near, swapped(side, twin), twin_across]
     own, high, low = experts(held, weights)
-    high, late = lax.optimization_barrier((high, late))
+    high, late = tied(high, late)
+    pieces.append(late)
 
     high, low = swapped(high, twin), swapped(low, twin)
     height = expert_count * capacity
-    halves = [(0, width // 2), (width // 2, width)]
+
+    cut = 128 * (5 * width // 1024)
+    halves = [(0, cut), (cut, width)]
 
     def block(value, j, half):
         return value[j * height : (j + 1) * height, half[0] : half[1]]
 
-    attention = attend(queries, latent_cache, beside, early, late, new_latent, parents, lengths)
-    totals, done, token = [], None, None
-    for half in halves:
-        across = added([block(own, 3, half), block(high, 1, half)]).astype(jnp.bfloat16)
-        across = across if token is None else after(across, token)
-        later = after(high, across)
-        across = swapped(across, second)
-        if done is not None:
-            across, later = after((across, later), done)
-        side = added([block(own, 2, half), block(later, 0, half)]).astype(jnp.bfloat16)
-        near = added([block(own, 1, half), block(low, 1, half), across]).astype(jnp.bfloat16)
-        if done is not None:
-            near, attention = lax.optimization_barrier((near, attention))
-        token = near
-        near, side = swapped(near, first), swapped(side, second)
+    def to_second(half):
+        return added([block(own, 3, half), block(high, 1, half)]).astype(jnp.bfloat16)
+
+    def to_first(half, across):
+        return added([block(own, 1, half), block(low, 1, half), across]).astype(jnp.bfloat16)
+
+    def to_side(half):
+        return added([block(own, 2, half), block(high, 0, half)]).astype(jnp.bfloat16)
+
+    def shares(half, side, near):
         here = [block(own, 0, half), block(low, 0, half), side, near]
-        shares = [
+        return [
             added([v[r * capacity : (r + 1) * capacity] for v in here])
             for r in range(expert_count)
         ]
-        done = shares
-        values = [
-            swapped(shares[r].astype(jnp.bfloat16), ahead(-r)) for r in range(1, expert_count)
+
+    def back(share):
+        return [
+            swapped(share[r].astype(jnp.bfloat16), ahead(r)) for r in range(1, expert_count)
         ]
-        values = [v.astype(jnp.float32) for v in values]
+
+    across, high = tied(to_second(halves[0]), high)
+    across = swapped(across, second)
+    near, side = to_first(halves[0], across), to_side(halves[0])
+    near, across = tied(near, to_second(halves[1]))
+    near, side, across = swapped(near, first), swapped(side, second), swapped(across, second)
+    share = shares(halves[0], side, near)
+    share, across, high = tied(share, across, high)
+    values = [[share[0]] + back(share)]
+    near, side = to_first(halves[1], across), to_side(halves[1])
+    attention = attend(
+        queries, latent_cache, beside, new_latent, spans, pieces, parents, lengths
+    )
+    near, attention = tied(near, attention)
+    near, side = swapped(near, first), swapped(side, second)
+    share = shares(halves[1], side, near)
+    values.append([share[0]] + back(share))
+    totals = []
+    for value in values:
+        value = [v.astype(jnp.float32) for v in value]
         if dense:
-            weighted = lax.optimization_barrier(mixing[0][:, None] * shares[0])
-            total = weighted + sum(
-                mixing[r][:, None] * values[r - 1] for r in range(1, expert_count)
-            )
+            total = sum(mixing[r][:, None] * value[r] for r in range(expert_count))
         else:
             total = jnp.dot(
                 mixing,
-                jnp.concatenate([shares[0]] + values),
+                jnp.concatenate(value),
                 precision=lax.Precision.HIGHEST,
                 preferred_element_type=jnp.float32,
             )

time: 92.1 us -> 93.8 us (1.018)
  local copies, waits for them, and re-layouts: 1.59 us -> 12.3 us
  starting transfers between devices: 38.3 us -> 30.1 us
  waiting for transfers between devices: 34.6 us -> 33 us
  Pallas kernels: 11.8 us -> 13.3 us
    unnamed x13 -> x31, local copies, waits for them, and re-layouts: 0.96 us -> 11.7 us
    ppermute x25, starting transfers between devices: 36.9 us -> 28.5 us  [swapped(): return lax.ppermute(value, 'dp', [(i, partner(i)) for i in range(peers)])]
    ppermute x25, waiting for transfers between devices: 34.6 us -> 33 us  [swapped(): return lax.ppermute(value, 'dp', [(i, partner(i)) for i in range(peers)])]
    pallas_call x1, Pallas kernels: 5.3 us -> 6.73 us  [experts(): pl.pallas_call(lambda *refs: expert_kernel(wide, *refs), in_specs=[whole]...]
  transfers between devices with their start and end apart: 27 -> 27, of which waited for: 14 -> 13; matrix products, arithmetic and copies ran while one was open for 5% -> 4% of each run, Pallas kernels for 13% -> 14%
where the time goes in v10:
time: 93.8 us; the launch traced here: 93.5 us
  waiting for transfers between devices  33 us (35%)
  starting transfers between devices  30.1 us (32%)
  Pallas kernels  13.3 us (14%)
  local copies, waits for them, and re-layouts  12.3 us (13%)
  other arithmetic  4 us (4%)
    ppermute x25, waiting for transfers between devices, swapped(): return lax.ppermute(value, 'dp', [(i, partner(i)) for i in range(peers)])  33 us
    ppermute x25, starting transfers between devices, swapped(): return lax.ppermute(value, 'dp', [(i, partner(i)) for i in range(peers)])  28.5 us
    unnamed x31, local copies, waits for them, and re-layouts  11.7 us
    pallas_call x1, Pallas kernels, experts(): pl.pallas_call(lambda *refs: expert_kernel(wide, *refs), in_specs=[whole]...  6.73 us
    pallas_call x1, Pallas kernels, fetched(): pl.pallas_call(fetch_kernel, in_specs=[pl.BlockSpec(memory_space=pltpu.HB...  4.23 us
    reduce_sum x1, other arithmetic, body(): jnp.sum(jnp.where(routed_experts == targets[r], route_weights, 0.0), axis=1)  2.49 us
    pallas_call x1, Pallas kernels, attend(): pl.pallas_call(lambda *refs: attend_kernel(spans, *refs), in_specs=[scala...  2.3 us
  transfers between devices with their start and end apart: 27, of which 13 were waited for; matrix products, arithmetic and copies ran while one was open for 4% of the time, Pallas kernels for 14%

profile of v10, /device:TPU:0, one launch (start us, length us, event | category | flops | bytes accessed | tf_op | source)
XLA Modules:
  0.0 93.5 jit_solution(10594820759309381122)
XLA Ops:
  0.7 0.9 collective-permute-start.3
  1.5 4.1 %collective-permute-start.1 = (bf16[8,7168]{1,0:T(8,128)(2,1)}, bf16[8,7168]{1,0:T(8,128)(2,1)S(1)}, u32[]{:S(2)}, u32[]{:S(2)}) collective-permute-start(bf16[8,7168]{1,0:T(8,128)(2,1)} %param.16), channel_id=1, source_target_pairs={{0,16},{1,17},{2,18},{3,19},{4,20},{5,21},{6,22},{7,23},{8,24},{9,... | collective-permute-start | bytes 344072 | tf_op jit(solution)/shard_map/ppermute | solution.py:26
  5.6 1.6 %collective-permute-start = (bf16[8,7168]{1,0:T(8,128)(2,1)}, bf16[8,7168]{1,0:T(8,128)(2,1)S(1)}, u32[]{:S(2)}, u32[]{:S(2)}) collective-permute-start(bf16[8,7168]{1,0:T(8,128)(2,1)} %param.16), channel_id=1, source_target_pairs={{0,8},{1,9},{2,10},{3,11},{4,12},{5,13},{6,14},{7,15},{8,0},{9,1},... | collective-permute-start | bytes 344072 | tf_op jit(solution)/shard_map/ppermute | solution.py:26
  7.2 4.2 %shard_map.122 = (bf16[1,7168,256]{2,1,0:T(8,128)(2,1)S(1)}, bf16[1,7168,256]{2,1,0:T(8,128)(2,1)S(1)}, bf16[1,256,7168]{2,1,0:T(8,128)(2,1)S(1)}) custom-call(bf16[1,7168,256]{2,1,0:T(8,128)(2,1)} %refs_0_.2, bf16[1,7168,256]{2,1,0:T(8,128)(2,1)} %refs_1_.2, bf16[1,256,7168]{2,1,0:T(8,128)(2,1)} %refs_2_.2), custom_call_target="tpu_custom_call" | custom-call | bytes 22020096 | tf_op jit(solution)/shard_map/pallas_call | solution.py:127
  11.5 1.8 %copy-done = bf16[1,7168,256]{2,1,0:T(8,128)(2,1)} copy-done((bf16[1,7168,256]{2,1,0:T(8,128)(2,1)}, bf16[1,7168,256]{2,1,0:T(8,128)(2,1)S(1)}, u32[]{:S(2)}) %copy-start) | copy-done | bytes 3670040
  13.2 1.8 %copy-done.2 = bf16[1,7168,256]{2,1,0:T(8,128)(2,1)} copy-done((bf16[1,7168,256]{2,1,0:T(8,128)(2,1)}, bf16[1,7168,256]{2,1,0:T(8,128)(2,1)S(1)}, u32[]{:S(2)}) %copy-start.2) | copy-done | bytes 3670040
  15.0 1.9 %copy-done.4 = bf16[1,256,7168]{2,1,0:T(8,128)(2,1)} copy-done((bf16[1,256,7168]{2,1,0:T(8,128)(2,1)}, bf16[1,256,7168]{2,1,0:T(8,128)(2,1)S(1)}, u32[]{:S(2)}) %copy-start.4) | copy-done | bytes 3670040
  17.1 3.4 %collective-permute-start.4 = (bf16[32,7168]{1,0:T(8,128)(2,1)S(1)}, bf16[32,7168]{1,0:T(8,128)(2,1)}, u32[]{:S(2)}, u32[]{:S(2)}) collective-permute-start(bf16[32,7168]{1,0:T(8,128)(2,1)S(1)} %constant_dynamic-update-slice_fusion.refs_0_), channel_id=1, source_target_pairs={{0,4},{1,3},{2,6},{3,1},{4,0},{5,7},{6,2},{7,5},{8,12},{9,11},{10,... | collective-permute-start | bytes 1376264 | tf_op jit(solution)/shard_map/ppermute | solution.py:26
  20.4 0.2 collective-permute-start.8
  20.6 0.3 collective-permute-start.6
  20.9 6.1 %collective-permute-done.4.refs_1_ = bf16[32,7168]{1,0:T(8,128)(2,1)} collective-permute-done((bf16[32,7168]{1,0:T(8,128)(2,1)S(1)}, bf16[32,7168]{1,0:T(8,128)(2,1)}, u32[]{:S(2)}, u32[]{:S(2)}) %collective-permute-start.4) | collective-permute-done | bytes 458784 | tf_op jit(solution)/shard_map/ppermute | solution.py:26
  27.1 1.2 %collective-permute-start.5 = (bf16[32,7168]{1,0:T(8,128)(2,1)}, bf16[32,7168]{1,0:T(8,128)(2,1)}, u32[]{:S(2)}, u32[]{:S(2)}) collective-permute-start(bf16[32,7168]{1,0:T(8,128)(2,1)} %collective-permute-done.4.refs_1_), channel_id=1, source_target_pairs={{0,2},{1,5},{2,0},{3,7},{4,6},{5,1},{6,4},{7,3},{8,10},{9,13},{10,... | collective-permute-start | bytes 1376264 | tf_op jit(solution)/shard_map/ppermute | solution.py:26
  28.3 0.6 fusion.4
  29.0 2.5 %fusion.3 = (f32[8]{0:T(128)S(1)}, f32[8]{0:T(128)S(1)}, f32[8]{0:T(128)S(1)}, f32[8]{0:T(128)S(1)}) fusion(f32[8,2]{0,1:T(2,128)S(1)} %copy-done.12, s32[8,2]{0,1:T(2,128)S(1)} %copy-done.13, s32[]{:T(128)} %bitcast.3, s32[]{:T(128)} %bitcast.1, s32[]{:T(128)} %bitcast, s32[]{:T(128)} %bitcast.2), kind=kLoop, calls=%fused_computation.27 | loop fusion | flops 160 | bytes 272 | tf_op jit(solution)/shard_map/reduce_sum | solution.py:225
  31.4 0.9 collective-permute-start.10
  32.3 3.6 %collective-permute-done.5.refs_3_ = bf16[32,7168]{1,0:T(8,128)(2,1)} collective-permute-done((bf16[32,7168]{1,0:T(8,128)(2,1)}, bf16[32,7168]{1,0:T(8,128)(2,1)}, u32[]{:S(2)}, u32[]{:S(2)}) %collective-permute-start.5) | collective-permute-done | bytes 458784 | tf_op jit(solution)/shard_map/ppermute | solution.py:26
  35.9 0.7 collective-permute-start.13
  36.6 4.1 %collective-permute-done.10.refs_2_ = bf16[32,7168]{1,0:T(8,128)(2,1)S(1)} collective-permute-done((bf16[32,7168]{1,0:T(8,128)(2,1)S(1)}, bf16[32,7168]{1,0:T(8,128)(2,1)S(1)}, u32[]{:S(2)}, u32[]{:S(2)}) %collective-permute-start.10) | collective-permute-done | bytes 458784 | tf_op jit(solution)/shard_map/ppermute | solution.py:26
  40.7 1.8 %collective-permute-done.11.refs_6_ = bf16[32,7168]{1,0:T(8,128)(2,1)S(1)} collective-permute-done((bf16[32,7168]{1,0:T(8,128)(2,1)S(1)}, bf16[32,7168]{1,0:T(8,128)(2,1)S(1)}, u32[]{:S(2)}, u32[]{:S(2)}) %collective-permute-start.11) | collective-permute-done | bytes 458784 | tf_op jit(solution)/shard_map/ppermute | solution.py:26
  42.5 2.0 %copy-done.1 = bf16[1,7168,256]{2,1,0:T(8,128)(2,1)S(1)} copy-done((bf16[1,7168,256]{2,1,0:T(8,128)(2,1)S(1)}, bf16[1,7168,256]{2,1,0:T(8,128)(2,1)}, u32[]{:S(2)}) %copy-start.1) | copy-done | bytes 3670040
  44.6 2.0 %copy-done.3 = bf16[1,7168,256]{2,1,0:T(8,128)(2,1)S(1)} copy-done((bf16[1,7168,256]{2,1,0:T(8,128)(2,1)S(1)}, bf16[1,7168,256]{2,1,0:T(8,128)(2,1)}, u32[]{:S(2)}) %copy-start.3) | copy-done | bytes 3670040
  46.6 2.0 %copy-done.5 = bf16[1,256,7168]{2,1,0:T(8,128)(2,1)S(1)} copy-done((bf16[1,256,7168]{2,1,0:T(8,128)(2,1)S(1)}, bf16[1,256,7168]{2,1,0:T(8,128)(2,1)}, u32[]{:S(2)}) %copy-start.5) | copy-done | bytes 3670040
  48.7 6.7 %shard_map.123 = (bf16[128,7168]{1,0:T(8,128)(2,1)S(1)}, bf16[64,7168]{1,0:T(8,128)(2,1)S(1)}, bf16[64,7168]{1,0:T(8,128)(2,1)S(1)}) custom-call(bf16[32,7168]{1,0:T(8,128)(2,1)S(1)} %constant_dynamic-update-slice_fusion.refs_0_, bf16[32,7168]{1,0:T(8,128)(2,1)} %collective-permute-done.4.refs_1_, bf16[32,7168]{1,0:T(8,128)(2,1)S(1)} %collective-permute-done.10.refs_2_, ...), custom_call_target="tpu_custom_call" | custom-call | flops 2818572288 | bytes 18350080 | tf_op jit(solution)/shard_map/pallas_call | solution.py:179
  55.5 0.2 collective-permute-start.14
  55.7 0.4 collective-permute-start.12
  56.0 2.0 %collective-permute-done.14 = bf16[64,7168]{1,0:T(8,128)(2,1)S(1)} collective-permute-done((bf16[64,7168]{1,0:T(8,128)(2,1)S(1)}, bf16[64,7168]{1,0:T(8,128)(2,1)S(1)}, u32[]{:S(2)}, u32[]{:S(2)}) %collective-permute-start.14) | collective-permute-done | bytes 917536 | tf_op jit(solution)/shard_map/ppermute | solution.py:26
  58.1 1.3 %collective-permute-start.16 = (bf16[32,4480]{1,0:T(8,128)(2,1)S(1)}, bf16[32,4480]{1,0:T(8,128)(2,1)S(1)}, u32[]{:S(2)}, u32[]{:S(2)}) collective-permute-start(bf16[32,4480]{1,0:T(8,128)(2,1)S(1)} %add_convert_fusion.2), channel_id=1, source_target_pairs={{0,2},{1,5},{2,0},{3,7},{4,6},{5,1},{6,4},{7,3},{8,10},{9,13},{10,... | collective-permute-start | bytes 860168 | tf_op jit(solution)/shard_map/ppermute | solution.py:26
  59.4 5.3 %collective-permute-done.16 = bf16[32,4480]{1,0:T(8,128)(2,1)S(1)} collective-permute-done((bf16[32,4480]{1,0:T(8,128)(2,1)S(1)}, bf16[32,4480]{1,0:T(8,128)(2,1)S(1)}, u32[]{:S(2)}, u32[]{:S(2)}) %collective-permute-start.16) | collective-permute-done | bytes 286752 | tf_op jit(solution)/shard_map/ppermute | solution.py:26
  64.8 0.2 add_convert_fusion.1
  65.0 2.0 %collective-permute-start.17 = (bf16[32,4480]{1,0:T(8,128)(2,1)S(1)}, bf16[32,4480]{1,0:T(8,128)(2,1)S(1)}, u32[]{:S(2)}, u32[]{:S(2)}) collective-permute-start(bf16[32,4480]{1,0:T(8,128)(2,1)S(1)} %get-tuple-element.65), channel_id=1, source_target_pairs={{0,4},{1,3},{2,6},{3,1},{4,0},{5,7},{6,2},{7,5},{8,12},{9,11},{10,... | collective-permute-start | bytes 860168 | tf_op jit(solution)/shard_map/ppermute | solution.py:26
  66.9 1.1 %collective-permute-start.15 = (bf16[32,4480]{1,0:T(8,128)(2,1)S(1)}, bf16[32,4480]{1,0:T(8,128)(2,1)S(1)}, u32[]{:S(2)}, u32[]{:S(2)}) collective-permute-start(bf16[32,4480]{1,0:T(8,128)(2,1)S(1)} %get-tuple-element.94), channel_id=1, source_target_pairs={{0,2},{1,5},{2,0},{3,7},{4,6},{5,1},{6,4},{7,3},{8,10},{9,13},{10,... | collective-permute-start | bytes 860168 | tf_op jit(solution)/shard_map/ppermute | solution.py:26
  68.1 2.3 %shard_map.124 = bf16[8,64,512]{2,1,0:T(8,128)(2,1)} custom-call(s32[8]{0:T(128)S(1)} %copy-done.9, s32[8]{0:T(128)S(1)} %copy-done.10, bf16[8,64,576]{2,1,0:T(8,128)(2,1)S(1)} %copy-done.7, bf16[8,96,576]{2,1,0:T(8,128)(2,1)S(1)} %copy-done.6, bf16[8,96,576]{2,1,0:T(8,128)(2,1)S(1)} %collective-permute-done.8.refs_4_, bf16[8,576]{1,0:T(8,128)(2,1)S(1)} %copy-done.8, ...), custom_call_target="tpu_custom_call" | custom-call | flops 106954752 | bytes 4653056 | tf_op jit(solution)/shard_map/pallas_call | solution.py:99
  70.4 0.9 collective-permute-start.18
  71.3 3.4 %collective-permute-done.17 = bf16[32,4480]{1,0:T(8,128)(2,1)S(1)} collective-permute-done((bf16[32,4480]{1,0:T(8,128)(2,1)S(1)}, bf16[32,4480]{1,0:T(8,128)(2,1)S(1)}, u32[]{:S(2)}, u32[]{:S(2)}) %collective-permute-start.17) | collective-permute-done | bytes 286752 | tf_op jit(solution)/shard_map/ppermute | solution.py:26
  74.8 0.9 collective-permute-done.18
  75.9 1.1 %collective-permute-start.23 = (bf16[32,2688]{1,0:T(8,128)(2,1)S(1)}, bf16[32,2688]{1,0:T(8,128)(2,1)S(1)}, u32[]{:S(2)}, u32[]{:S(2)}) collective-permute-start(bf16[32,2688]{1,0:T(8,128)(2,1)S(1)} %get-tuple-element.81), channel_id=1, source_target_pairs={{0,4},{1,3},{2,6},{3,1},{4,0},{5,7},{6,2},{7,5},{8,12},{9,11},{10,... | collective-permute-start | bytes 516104 | tf_op jit(solution)/shard_map/ppermute | solution.py:26
  77.0 1.1 %collective-permute-start.22 = (bf16[32,2688]{1,0:T(8,128)(2,1)S(1)}, bf16[32,2688]{1,0:T(8,128)(2,1)S(1)}, u32[]{:S(2)}, u32[]{:S(2)}) collective-permute-start(bf16[32,2688]{1,0:T(8,128)(2,1)S(1)} %get-tuple-element.92), channel_id=1, source_target_pairs={{0,2},{1,5},{2,0},{3,7},{4,6},{5,1},{6,4},{7,3},{8,10},{9,13},{10,... | collective-permute-start | bytes 516104 | tf_op jit(solution)/shard_map/ppermute | solution.py:26
  78.1 1.0 %collective-permute-start.19 = (bf16[8,4480]{1,0:T(8,128)(2,1)S(1)}, bf16[8,4480]{1,0:T(8,128)(2,1)S(1)}, u32[]{:S(2)}, u32[]{:S(2)}) collective-permute-start(bf16[8,4480]{1,0:T(8,128)(2,1)S(1)} %get-tuple-element.75), channel_id=1, source_target_pairs={{0,8},{1,9},{2,10},{3,11},{4,12},{5,13},{6,14},{7,15},{8,0},{9,1},... | collective-permute-start | bytes 215048 | tf_op jit(solution)/shard_map/ppermute | solution.py:26
  79.1 3.2 %collective-permute-start.20 = (bf16[8,4480]{1,0:T(8,128)(2,1)S(1)}, bf16[8,4480]{1,0:T(8,128)(2,1)S(1)}, u32[]{:S(2)}, u32[]{:S(2)}) collective-permute-start(bf16[8,4480]{1,0:T(8,128)(2,1)S(1)} %get-tuple-element.77), channel_id=1, source_target_pairs={{0,16},{1,17},{2,18},{3,19},{4,20},{5,21},{6,22},{7,23},{8,24},{9,... | collective-permute-start | bytes 215048 | tf_op jit(solution)/shard_map/ppermute | solution.py:26
  82.3 0.2 collective-permute-start.21
  82.5 0.5 collective-permute-done.23
  83.1 1.4 %collective-permute-start.24 = (bf16[8,2688]{1,0:T(8,128)(2,1)S(1)}, bf16[8,2688]{1,0:T(8,128)(2,1)S(1)}, u32[]{:S(2)}, u32[]{:S(2)}) collective-permute-start(bf16[8,2688]{1,0:T(8,128)(2,1)S(1)} %get-tuple-element.89), channel_id=1, source_target_pairs={{0,8},{1,9},{2,10},{3,11},{4,12},{5,13},{6,14},{7,15},{8,0},{9,1},... | collective-permute-start | bytes 129032 | tf_op jit(solution)/shard_map/ppermute | solution.py:26
  84.4 2.5 %collective-permute-start.26 = (bf16[8,2688]{1,0:T(8,128)(2,1)S(1)}, bf16[8,2688]{1,0:T(8,128)(2,1)S(1)}, u32[]{:S(2)}, u32[]{:S(2)}) collective-permute-start(bf16[8,2688]{1,0:T(8,128)(2,1)S(1)} %get-tuple-element.90), channel_id=1, source_target_pairs={{0,24},{1,25},{2,26},{3,27},{4,28},{5,29},{6,30},{7,31},{8,16},{9,... | collective-permute-start | bytes 129032 | tf_op jit(solution)/shard_map/ppermute | solution.py:26
  86.9 0.4 collective-permute-start.25
  87.4 1.7 %collective-permute-done.21 = bf16[8,4480]{1,0:T(8,128)(2,1)S(1)} collective-permute-done((bf16[8,4480]{1,0:T(8,128)(2,1)S(1)}, bf16[8,4480]{1,0:T(8,128)(2,1)S(1)}, u32[]{:S(2)}, u32[]{:S(2)}) %collective-permute-start.21) | collective-permute-done | bytes 71712 | tf_op jit(solution)/shard_map/ppermute | solution.py:26
  89.2 1.2 %collective-permute-done.26 = bf16[8,2688]{1,0:T(8,128)(2,1)S(1)} collective-permute-done((bf16[8,2688]{1,0:T(8,128)(2,1)S(1)}, bf16[8,2688]{1,0:T(8,128)(2,1)S(1)}, u32[]{:S(2)}, u32[]{:S(2)}) %collective-permute-start.26) | collective-permute-done | bytes 43040 | tf_op jit(solution)/shard_map/ppermute | solution.py:26
  90.4 2.3 %collective-permute-done.25 = bf16[8,2688]{1,0:T(8,128)(2,1)S(1)} collective-permute-done((bf16[8,2688]{1,0:T(8,128)(2,1)S(1)}, bf16[8,2688]{1,0:T(8,128)(2,1)S(1)}, u32[]{:S(2)}, u32[]{:S(2)}) %collective-permute-start.25) | collective-permute-done | bytes 43040 | tf_op jit(solution)/shard_map/ppermute | solution.py:26
  92.9 0.7 pad_maximum_fusion
  (54 shorter events, 1.0 us)
Async XLA Ops:
  0.6 19.8 %copy-start.6 = (bf16[8,96,576]{2,1,0:T(8,128)(2,1)S(1)}, bf16[8,96,576]{2,1,0:T(8,128)(2,1)}, u32[]{:S(2)}) copy-start(bf16[8,96,576]{2,1,0:T(8,128)(2,1)} %refs_3_.1) | copy-start | bytes 2654212
  0.6 16.3 %copy-start.11 = (bf16[8,7168]{1,0:T(8,128)(2,1)S(1)}, bf16[8,7168]{1,0:T(8,128)(2,1)}, u32[]{:S(2)}) copy-start(bf16[8,7168]{1,0:T(8,128)(2,1)} %param.16) | copy-start | bytes 344068
  0.7 28.3 %copy-start.12 = (f32[8,2]{0,1:T(2,128)S(1)}, f32[8,2]{0,1:T(2,128)}, u32[]{:S(2)}) copy-start(f32[8,2]{0,1:T(2,128)} %param.18) | copy-start | bytes 196
  0.7 28.3 %copy-start.13 = (s32[8,2]{0,1:T(2,128)S(1)}, s32[8,2]{0,1:T(2,128)}, u32[]{:S(2)}) copy-start(s32[8,2]{0,1:T(2,128)} %param.17) | copy-start | bytes 196
  0.7 16.3 %collective-permute-start.3 = (bf16[8,96,576]{2,1,0:T(8,128)(2,1)}, bf16[8,96,576]{2,1,0:T(8,128)(2,1)S(1)}, u32[]{:S(2)}, u32[]{:S(2)}) collective-permute-start(bf16[8,96,576]{2,1,0:T(8,128)(2,1)} %refs_3_.1), channel_id=1, source_target_pairs={{1,2},{3,4},{5,6},{6,5},{9,10},{11,12},{13,14},{14,13},{17,18},{19... | collective-permute-start | bytes 2654216 | tf_op jit(solution)/shard_map/ppermute | solution.py:47
  1.5 15.4 %collective-permute-start.1 = (bf16[8,7168]{1,0:T(8,128)(2,1)}, bf16[8,7168]{1,0:T(8,128)(2,1)S(1)}, u32[]{:S(2)}, u32[]{:S(2)}) collective-permute-start(bf16[8,7168]{1,0:T(8,128)(2,1)} %param.16), channel_id=1, source_target_pairs={{0,16},{1,17},{2,18},{3,19},{4,20},{5,21},{6,22},{7,23},{8,24},{9,... | collective-permute-start | bytes 344072 | tf_op jit(solution)/shard_map/ppermute | solution.py:26
  5.6 11.3 %collective-permute-start = (bf16[8,7168]{1,0:T(8,128)(2,1)}, bf16[8,7168]{1,0:T(8,128)(2,1)S(1)}, u32[]{:S(2)}, u32[]{:S(2)}) collective-permute-start(bf16[8,7168]{1,0:T(8,128)(2,1)} %param.16), channel_id=1, source_target_pairs={{0,8},{1,9},{2,10},{3,11},{4,12},{5,13},{6,14},{7,15},{8,0},{9,1},... | collective-permute-start | bytes 344072 | tf_op jit(solution)/shard_map/ppermute | solution.py:26
  7.2 9.8 %collective-permute-start.2 = (bf16[8,7168]{1,0:T(8,128)(2,1)}, bf16[8,7168]{1,0:T(8,128)(2,1)S(1)}, u32[]{:S(2)}, u32[]{:S(2)}) collective-permute-start(bf16[8,7168]{1,0:T(8,128)(2,1)} %param.16), channel_id=1, source_target_pairs={{0,24},{1,25},{2,26},{3,27},{4,28},{5,29},{6,30},{7,31},{8,16},{9,... | collective-permute-start | bytes 344072 | tf_op jit(solution)/shard_map/ppermute | solution.py:26
  11.5 1.8 %copy-start = (bf16[1,7168,256]{2,1,0:T(8,128)(2,1)}, bf16[1,7168,256]{2,1,0:T(8,128)(2,1)S(1)}, u32[]{:S(2)}) copy-start(bf16[1,7168,256]{2,1,0:T(8,128)(2,1)S(1)} %get-tuple-element.55.refs_8_) | copy-start | bytes 11010052
  13.2 1.8 %copy-start.2 = (bf16[1,7168,256]{2,1,0:T(8,128)(2,1)}, bf16[1,7168,256]{2,1,0:T(8,128)(2,1)S(1)}, u32[]{:S(2)}) copy-start(bf16[1,7168,256]{2,1,0:T(8,128)(2,1)S(1)} %get-tuple-element.56.refs_9_) | copy-start | bytes 11010052
  15.0 1.9 %copy-start.4 = (bf16[1,256,7168]{2,1,0:T(8,128)(2,1)}, bf16[1,256,7168]{2,1,0:T(8,128)(2,1)S(1)}, u32[]{:S(2)}) copy-start(bf16[1,256,7168]{2,1,0:T(8,128)(2,1)S(1)} %get-tuple-element.57.refs_10_) | copy-start | bytes 11010052
  17.1 9.9 %collective-permute-start.4 = (bf16[32,7168]{1,0:T(8,128)(2,1)S(1)}, bf16[32,7168]{1,0:T(8,128)(2,1)}, u32[]{:S(2)}, u32[]{:S(2)}) collective-permute-start(bf16[32,7168]{1,0:T(8,128)(2,1)S(1)} %constant_dynamic-update-slice_fusion.refs_0_), channel_id=1, source_target_pairs={{0,4},{1,3},{2,6},{3,1},{4,0},{5,7},{6,2},{7,5},{8,12},{9,11},{10,... | collective-permute-start | bytes 1376264 | tf_op jit(solution)/shard_map/ppermute | solution.py:26
  20.4 11.9 %collective-permute-start.8 = (bf16[8,96,576]{2,1,0:T(8,128)(2,1)S(1)}, bf16[8,96,576]{2,1,0:T(8,128)(2,1)S(1)}, u32[]{:S(2)}, u32[]{:S(2)}) collective-permute-start(bf16[8,96,576]{2,1,0:T(8,128)(2,1)S(1)} %copy-done.6), channel_id=1, source_target_pairs={{0,1},{1,0},{2,3},{3,2},{4,5},{5,4},{6,7},{7,6},{8,9},{9,8},{10,11... | collective-permute-start | bytes 2654216 | tf_op jit(solution)/shard_map/ppermute | solution.py:26
  20.6 11.7 %collective-permute-start.6 = (bf16[32,7168]{1,0:T(8,128)(2,1)S(1)}, bf16[32,7168]{1,0:T(8,128)(2,1)}, u32[]{:S(2)}, u32[]{:S(2)}) collective-permute-start(bf16[32,7168]{1,0:T(8,128)(2,1)S(1)} %constant_dynamic-update-slice_fusion.refs_0_), channel_id=1, source_target_pairs={{0,1},{1,0},{2,3},{3,2},{4,5},{5,4},{6,7},{7,6},{8,9},{9,8},{10,11... | collective-permute-start | bytes 1376264 | tf_op jit(solution)/shard_map/ppermute | solution.py:26
  27.0 5.3 %collective-permute-start.7 = (bf16[32,7168]{1,0:T(8,128)(2,1)}, bf16[32,7168]{1,0:T(8,128)(2,1)}, u32[]{:S(2)}, u32[]{:S(2)}) collective-permute-start(bf16[32,7168]{1,0:T(8,128)(2,1)} %collective-permute-done.4.refs_1_), channel_id=1, source_target_pairs={{0,1},{1,0},{2,3},{3,2},{4,5},{5,4},{6,7},{7,6},{8,9},{9,8},{10,11... | collective-permute-start | bytes 1376264 | tf_op jit(solution)/shard_map/ppermute | solution.py:26
  27.1 8.8 %collective-permute-start.5 = (bf16[32,7168]{1,0:T(8,128)(2,1)}, bf16[32,7168]{1,0:T(8,128)(2,1)}, u32[]{:S(2)}, u32[]{:S(2)}) collective-permute-start(bf16[32,7168]{1,0:T(8,128)(2,1)} %collective-permute-done.4.refs_1_), channel_id=1, source_target_pairs={{0,2},{1,5},{2,0},{3,7},{4,6},{5,1},{6,4},{7,3},{8,10},{9,13},{10,... | collective-permute-start | bytes 1376264 | tf_op jit(solution)/shard_map/ppermute | solution.py:26
  31.4 9.3 %collective-permute-start.10 = (bf16[32,7168]{1,0:T(8,128)(2,1)S(1)}, bf16[32,7168]{1,0:T(8,128)(2,1)S(1)}, u32[]{:S(2)}, u32[]{:S(2)}) collective-permute-start(bf16[32,7168]{1,0:T(8,128)(2,1)S(1)} %constant_dynamic-update-slice_fusion.refs_0_), channel_id=1, source_target_pairs={{0,2},{1,5},{2,0},{3,7},{4,6},{5,1},{6,4},{7,3},{8,10},{9,13},{10,... | collective-permute-start | bytes 1376264 | tf_op jit(solution)/shard_map/ppermute | solution.py:26
  35.9 4.8 %collective-permute-start.9 = (bf16[32,7168]{1,0:T(8,128)(2,1)}, bf16[32,7168]{1,0:T(8,128)(2,1)S(1)}, u32[]{:S(2)}, u32[]{:S(2)}) collective-permute-start(bf16[32,7168]{1,0:T(8,128)(2,1)} %collective-permute-done.5.refs_3_), channel_id=1, source_target_pairs={{0,1},{1,0},{2,3},{3,2},{4,5},{5,4},{6,7},{7,6},{8,9},{9,8},{10,11... | collective-permute-start | bytes 1376264 | tf_op jit(solution)/shard_map/ppermute | solution.py:26
  35.9 19.5 %collective-permute-start.13 = (bf16[8,96,576]{2,1,0:T(8,128)(2,1)S(1)}, bf16[8,96,576]{2,1,0:T(8,128)(2,1)S(1)}, u32[]{:S(2)}, u32[]{:S(2)}) collective-permute-start(bf16[8,96,576]{2,1,0:T(8,128)(2,1)S(1)} %copy-done.6), channel_id=1, source_target_pairs={{2,1},{4,3},{7,8},{8,7},{10,9},{12,11},{15,16},{16,15},{18,17},{20... | collective-permute-start | bytes 2654216 | tf_op jit(solution)/shard_map/ppermute | solution.py:47
  40.7 1.8 %collective-permute-start.11 = (bf16[32,7168]{1,0:T(8,128)(2,1)S(1)}, bf16[32,7168]{1,0:T(8,128)(2,1)S(1)}, u32[]{:S(2)}, u32[]{:S(2)}) collective-permute-start(bf16[32,7168]{1,0:T(8,128)(2,1)S(1)} %collective-permute-done.10.refs_2_), channel_id=1, source_target_pairs={{0,1},{1,0},{2,3},{3,2},{4,5},{5,4},{6,7},{7,6},{8,9},{9,8},{10,11... | collective-permute-start | bytes 1376264 | tf_op jit(solution)/shard_map/ppermute | solution.py:26
  42.5 2.0 %copy-start.1 = (bf16[1,7168,256]{2,1,0:T(8,128)(2,1)S(1)}, bf16[1,7168,256]{2,1,0:T(8,128)(2,1)}, u32[]{:S(2)}) copy-start(bf16[1,7168,256]{2,1,0:T(8,128)(2,1)} %copy-done) | copy-start | bytes 11010052
  44.6 2.0 %copy-start.3 = (bf16[1,7168,256]{2,1,0:T(8,128)(2,1)S(1)}, bf16[1,7168,256]{2,1,0:T(8,128)(2,1)}, u32[]{:S(2)}) copy-start(bf16[1,7168,256]{2,1,0:T(8,128)(2,1)} %copy-done.2) | copy-start | bytes 11010052
  46.6 2.0 %copy-start.5 = (bf16[1,256,7168]{2,1,0:T(8,128)(2,1)S(1)}, bf16[1,256,7168]{2,1,0:T(8,128)(2,1)}, u32[]{:S(2)}) copy-start(bf16[1,256,7168]{2,1,0:T(8,128)(2,1)} %copy-done.4) | copy-start | bytes 11010052
  55.4 12.7 %copy-start.7 = (bf16[8,64,576]{2,1,0:T(8,128)(2,1)S(1)}, bf16[8,64,576]{2,1,0:T(8,128)(2,1)}, u32[]{:S(2)}) copy-start(bf16[8,64,576]{2,1,0:T(8,128)(2,1)} %refs_2_.3) | copy-start | bytes 1769476
  55.4 12.6 %copy-start.8 = (bf16[8,576]{1,0:T(8,128)(2,1)S(1)}, bf16[8,576]{1,0:T(8,128)(2,1)}, u32[]{:S(2)}) copy-start(bf16[8,576]{1,0:T(8,128)(2,1)} %refs_5_.1) | copy-start | bytes 27652
  55.4 12.6 %copy-start.9 = (s32[8]{0:T(128)S(1)}, s32[8]{0:T(128)}, u32[]{:S(2)}) copy-start(s32[8]{0:T(128)} %refs_0_.3) | copy-start | bytes 100
  55.4 12.6 %copy-start.10 = (s32[8]{0:T(128)S(1)}, s32[8]{0:T(128)}, u32[]{:S(2)}) copy-start(s32[8]{0:T(128)} %refs_1_.3) | copy-start | bytes 100
  55.5 2.5 %collective-permute-start.14 = (bf16[64,7168]{1,0:T(8,128)(2,1)S(1)}, bf16[64,7168]{1,0:T(8,128)(2,1)S(1)}, u32[]{:S(2)}, u32[]{:S(2)}) collective-permute-start(bf16[64,7168]{1,0:T(8,128)(2,1)S(1)} %get-tuple-element.62), channel_id=1, source_target_pairs={{0,1},{1,0},{2,3},{3,2},{4,5},{5,4},{6,7},{7,6},{8,9},{9,8},{10,11... | collective-permute-start | bytes 2752520 | tf_op jit(solution)/shard_map/ppermute | solution.py:26
  55.7 3.8 %collective-permute-start.12 = (bf16[64,7168]{1,0:T(8,128)(2,1)S(1)}, bf16[64,7168]{1,0:T(8,128)(2,1)S(1)}, u32[]{:S(2)}, u32[]{:S(2)}) collective-permute-start(bf16[64,7168]{1,0:T(8,128)(2,1)S(1)} %get-tuple-element.59), channel_id=1, source_target_pairs={{0,1},{1,0},{2,3},{3,2},{4,5},{5,4},{6,7},{7,6},{8,9},{9,8},{10,11... | collective-permute-start | bytes 2752520 | tf_op jit(solution)/shard_map/ppermute | solution.py:26
  58.1 6.7 %collective-permute-start.16 = (bf16[32,4480]{1,0:T(8,128)(2,1)S(1)}, bf16[32,4480]{1,0:T(8,128)(2,1)S(1)}, u32[]{:S(2)}, u32[]{:S(2)}) collective-permute-start(bf16[32,4480]{1,0:T(8,128)(2,1)S(1)} %add_convert_fusion.2), channel_id=1, source_target_pairs={{0,2},{1,5},{2,0},{3,7},{4,6},{5,1},{6,4},{7,3},{8,10},{9,13},{10,... | collective-permute-start | bytes 860168 | tf_op jit(solution)/shard_map/ppermute | solution.py:26
  65.0 9.7 %collective-permute-start.17 = (bf16[32,4480]{1,0:T(8,128)(2,1)S(1)}, bf16[32,4480]{1,0:T(8,128)(2,1)S(1)}, u32[]{:S(2)}, u32[]{:S(2)}) collective-permute-start(bf16[32,4480]{1,0:T(8,128)(2,1)S(1)} %get-tuple-element.65), channel_id=1, source_target_pairs={{0,4},{1,3},{2,6},{3,1},{4,0},{5,7},{6,2},{7,5},{8,12},{9,11},{10,... | collective-permute-start | bytes 860168 | tf_op jit(solution)/shard_map/ppermute | solution.py:26
  66.9 7.7 %collective-permute-start.15 = (bf16[32,4480]{1,0:T(8,128)(2,1)S(1)}, bf16[32,4480]{1,0:T(8,128)(2,1)S(1)}, u32[]{:S(2)}, u32[]{:S(2)}) collective-permute-start(bf16[32,4480]{1,0:T(8,128)(2,1)S(1)} %get-tuple-element.94), channel_id=1, source_target_pairs={{0,2},{1,5},{2,0},{3,7},{4,6},{5,1},{6,4},{7,3},{8,10},{9,13},{10,... | collective-permute-start | bytes 860168 | tf_op jit(solution)/shard_map/ppermute | solution.py:26
  70.4 5.4 %collective-permute-start.18 = (bf16[32,2688]{1,0:T(8,128)(2,1)S(1)}, bf16[32,2688]{1,0:T(8,128)(2,1)S(1)}, u32[]{:S(2)}, u32[]{:S(2)}) collective-permute-start(bf16[32,2688]{1,0:T(8,128)(2,1)S(1)} %add_convert_fusion.5), channel_id=1, source_target_pairs={{0,2},{1,5},{2,0},{3,7},{4,6},{5,1},{6,4},{7,3},{8,10},{9,13},{10,... | collective-permute-start | bytes 516104 | tf_op jit(solution)/shard_map/ppermute | solution.py:26
  75.9 7.1 %collective-permute-start.23 = (bf16[32,2688]{1,0:T(8,128)(2,1)S(1)}, bf16[32,2688]{1,0:T(8,128)(2,1)S(1)}, u32[]{:S(2)}, u32[]{:S(2)}) collective-permute-start(bf16[32,2688]{1,0:T(8,128)(2,1)S(1)} %get-tuple-element.81), channel_id=1, source_target_pairs={{0,4},{1,3},{2,6},{3,1},{4,0},{5,7},{6,2},{7,5},{8,12},{9,11},{10,... | collective-permute-start | bytes 516104 | tf_op jit(solution)/shard_map/ppermute | solution.py:26
  77.0 6.0 %collective-permute-start.22 = (bf16[32,2688]{1,0:T(8,128)(2,1)S(1)}, bf16[32,2688]{1,0:T(8,128)(2,1)S(1)}, u32[]{:S(2)}, u32[]{:S(2)}) collective-permute-start(bf16[32,2688]{1,0:T(8,128)(2,1)S(1)} %get-tuple-element.92), channel_id=1, source_target_pairs={{0,2},{1,5},{2,0},{3,7},{4,6},{5,1},{6,4},{7,3},{8,10},{9,13},{10,... | collective-permute-start | bytes 516104 | tf_op jit(solution)/shard_map/ppermute | solution.py:26
  78.1 8.8 %collective-permute-start.19 = (bf16[8,4480]{1,0:T(8,128)(2,1)S(1)}, bf16[8,4480]{1,0:T(8,128)(2,1)S(1)}, u32[]{:S(2)}, u32[]{:S(2)}) collective-permute-start(bf16[8,4480]{1,0:T(8,128)(2,1)S(1)} %get-tuple-element.75), channel_id=1, source_target_pairs={{0,8},{1,9},{2,10},{3,11},{4,12},{5,13},{6,14},{7,15},{8,0},{9,1},... | collective-permute-start | bytes 215048 | tf_op jit(solution)/shard_map/ppermute | solution.py:26
  79.1 8.3 %collective-permute-start.20 = (bf16[8,4480]{1,0:T(8,128)(2,1)S(1)}, bf16[8,4480]{1,0:T(8,128)(2,1)S(1)}, u32[]{:S(2)}, u32[]{:S(2)}) collective-permute-start(bf16[8,4480]{1,0:T(8,128)(2,1)S(1)} %get-tuple-element.77), channel_id=1, source_target_pairs={{0,16},{1,17},{2,18},{3,19},{4,20},{5,21},{6,22},{7,23},{8,24},{9,... | collective-permute-start | bytes 215048 | tf_op jit(solution)/shard_map/ppermute | solution.py:26
  82.3 6.8 %collective-permute-start.21 = (bf16[8,4480]{1,0:T(8,128)(2,1)S(1)}, bf16[8,4480]{1,0:T(8,128)(2,1)S(1)}, u32[]{:S(2)}, u32[]{:S(2)}) collective-permute-start(bf16[8,4480]{1,0:T(8,128)(2,1)S(1)} %get-tuple-element.79), channel_id=1, source_target_pairs={{0,24},{1,25},{2,26},{3,27},{4,28},{5,29},{6,30},{7,31},{8,16},{9,... | collective-permute-start | bytes 215048 | tf_op jit(solution)/shard_map/ppermute | solution.py:26
  83.1 6.2 %collective-permute-start.24 = (bf16[8,2688]{1,0:T(8,128)(2,1)S(1)}, bf16[8,2688]{1,0:T(8,128)(2,1)S(1)}, u32[]{:S(2)}, u32[]{:S(2)}) collective-permute-start(bf16[8,2688]{1,0:T(8,128)(2,1)S(1)} %get-tuple-element.89), channel_id=1, source_target_pairs={{0,8},{1,9},{2,10},{3,11},{4,12},{5,13},{6,14},{7,15},{8,0},{9,1},... | collective-permute-start | bytes 129032 | tf_op jit(solution)/shard_map/ppermute | solution.py:26
  84.4 6.0 %collective-permute-start.26 = (bf16[8,2688]{1,0:T(8,128)(2,1)S(1)}, bf16[8,2688]{1,0:T(8,128)(2,1)S(1)}, u32[]{:S(2)}, u32[]{:S(2)}) collective-permute-start(bf16[8,2688]{1,0:T(8,128)(2,1)S(1)} %get-tuple-element.90), channel_id=1, source_target_pairs={{0,24},{1,25},{2,26},{3,27},{4,28},{5,29},{6,30},{7,31},{8,16},{9,... | collective-permute-start | bytes 129032 | tf_op jit(solution)/shard_map/ppermute | solution.py:26
  86.9 5.9 %collective-permute-start.25 = (bf16[8,2688]{1,0:T(8,128)(2,1)S(1)}, bf16[8,2688]{1,0:T(8,128)(2,1)S(1)}, u32[]{:S(2)}, u32[]{:S(2)}) collective-permute-start(bf16[8,2688]{1,0:T(8,128)(2,1)S(1)} %get-tuple-element.91), channel_id=1, source_target_pairs={{0,16},{1,17},{2,18},{3,19},{4,20},{5,21},{6,22},{7,23},{8,24},{9,... | collective-permute-start | bytes 129032 | tf_op jit(solution)/shard_map/ppermute | solution.py:26

commit v11 on v10

--- a/solution.py
+++ b/solution.py
@@ -258,8 +258,7 @@
 
     column = blocks[:1] + [swapped(blocks[r], ahead(r)) for r in range(1, expert_count)]
     early, _ = cache_rows("early", 0, beam_count)
-    weights = fetched([gate_weight, up_weight, down_weight])
-    column, early, weights = tied(column, early, weights)
+    column, early, mixing = tied(column, early, mixing)
     pieces.append(early)
     column = jnp.concatenate(column)
     near = swapped(column, first)
@@ -267,12 +266,14 @@
     across = swapped(near, second)
     beside = swapped(latent_cache, twin)
     twin_column, twin_near = swapped(column, twin), swapped(near, twin)
-    across, twin_column, twin_near, beside, mixing = tied(
-        across, twin_column, twin_near, beside, mixing
+    weights = fetched([gate_weight, up_weight, down_weight])
+    across, twin_column, twin_near, weights, beside = tied(
+        across, twin_column, twin_near, weights, beside
     )
-    late, across = cache_rows("late", 0, beam_count, across)
-    twin_across, side = tied(swapped(across, twin), side)
-    held = [column, near, side, across, twin_column, twin_near, swapped(side, twin), twin_across]
+    middle = 5 * beam_count // 8
+    late, across = cache_rows("late", 0, middle, across)
+    held = [column, near, side, across, twin_column, twin_near]
+    held = held + [swapped(side, twin), swapped(across, twin)]
     own, high, low = experts(held, weights)
     high, late = tied(high, late)
     pieces.append(late)
@@ -308,7 +309,10 @@
         ]
 
     across, high = tied(to_second(halves[0]), high)
+    late, across = cache_rows("late", middle, beam_count, across)
     across = swapped(across, second)
+    across, late = tied(across, late)
+    pieces.append(late)
     near, side = to_first(halves[0], across), to_side(halves[0])
     near, across = tied(near, to_second(halves[1]))
     near, side, across = swapped(near, first), swapped(side, second), swapped(across, second)

time: 93.8 us -> 98.1 us (1.046)
  local copies, waits for them, and re-layouts: 12.3 us -> 2.74 us
  starting transfers between devices: 30.1 us -> 38.5 us
  waiting for transfers between devices: 33 us -> 39 us
  Pallas kernels: 13.3 us -> 12 us
    unnamed x31 -> x13, local copies, waits for them, and re-layouts: 11.7 us -> 0.95 us
    ppermute x25, starting transfers between devices: 28.5 us -> 36.3 us  [swapped(): return lax.ppermute(value, 'dp', [(i, partner(i)) for i in range(peers)])]
    ppermute x25, waiting for transfers between devices: 33 us -> 39 us  [swapped(): return lax.ppermute(value, 'dp', [(i, partner(i)) for i in range(peers)])]
    pallas_call x1, Pallas kernels: 6.73 us -> 5.3 us  [experts(): pl.pallas_call(lambda *refs: expert_kernel(wide, *refs), in_specs=[whole]...]
    slice x0 -> x2, local copies, waits for them, and re-layouts: none -> 1.16 us  [cache_rows(): source = latent_cache[begin:end]]
    ppermute x2 -> x3, starting transfers between devices: 1.57 us -> 2.24 us  [neighbours(): return lax.ppermute(value, 'dp', [p for p in pairs if max(p) < peers])]
  transfers between devices with their start and end apart: 27 -> 28, of which waited for: 13 -> 12; matrix products, arithmetic and copies ran while one was open for 4% -> 6% of each run, Pallas kernels for 14% -> 12%
where the time goes in v11:
time: 98.1 us; the launch traced here: 97.8 us
  waiting for transfers between devices  39 us (40%)
  starting transfers between devices  38.5 us (39%)
  Pallas kernels  12 us (12%)
  other arithmetic  4.76 us (5%)
  local copies, waits for them, and re-layouts  2.74 us (3%)
    ppermute x25, waiting for transfers between devices, swapped(): return lax.ppermute(value, 'dp', [(i, partner(i)) for i in range(peers)])  39 us
    ppermute x25, starting transfers between devices, swapped(): return lax.ppermute(value, 'dp', [(i, partner(i)) for i in range(peers)])  36.3 us
    pallas_call x1, Pallas kernels, experts(): pl.pallas_call(lambda *refs: expert_kernel(wide, *refs), in_specs=[whole]...  5.3 us
    pallas_call x1, Pallas kernels, fetched(): pl.pallas_call(fetch_kernel, in_specs=[pl.BlockSpec(memory_space=pltpu.HB...  4.23 us
    reduce_sum x1, other arithmetic, body(): jnp.sum(jnp.where(routed_experts == targets[r], route_weights, 0.0), axis=1)  3.25 us
    pallas_call x1, Pallas kernels, attend(): pl.pallas_call(lambda *refs: attend_kernel(spans, *refs), in_specs=[scala...  2.42 us
    ppermute x3, starting transfers between devices, neighbours(): return lax.ppermute(value, 'dp', [p for p in pairs if max(p) < peers])  2.24 us
  transfers between devices with their start and end apart: 28, of which 12 were waited for; matrix products, arithmetic and copies ran while one was open for 6% of the time, Pallas kernels for 12%

profile of v11, /device:TPU:0, one launch (start us, length us, event | category | flops | bytes accessed | tf_op | source)
XLA Modules:
  0.0 97.8 jit_solution(5890827863557693223)
XLA Ops:
  0.6 0.7 collective-permute-start.3
  1.4 3.1 %collective-permute-start = (bf16[8,7168]{1,0:T(8,128)(2,1)}, bf16[8,7168]{1,0:T(8,128)(2,1)S(1)}, u32[]{:S(2)}, u32[]{:S(2)}) collective-permute-start(bf16[8,7168]{1,0:T(8,128)(2,1)} %param.16), channel_id=1, source_target_pairs={{0,8},{1,9},{2,10},{3,11},{4,12},{5,13},{6,14},{7,15},{8,0},{9,1},... | collective-permute-start | bytes 344072 | tf_op jit(solution)/shard_map/ppermute | solution.py:26
  4.4 2.6 %collective-permute-start.1 = (bf16[8,7168]{1,0:T(8,128)(2,1)}, bf16[8,7168]{1,0:T(8,128)(2,1)S(1)}, u32[]{:S(2)}, u32[]{:S(2)}) collective-permute-start(bf16[8,7168]{1,0:T(8,128)(2,1)} %param.16), channel_id=1, source_target_pairs={{0,16},{1,17},{2,18},{3,19},{4,20},{5,21},{6,22},{7,23},{8,24},{9,... | collective-permute-start | bytes 344072 | tf_op jit(solution)/shard_map/ppermute | solution.py:26
  7.0 0.6 fusion.4
  7.7 3.3 %fusion.3 = (f32[8]{0:T(128)S(1)}, f32[8]{0:T(128)S(1)}, f32[8]{0:T(128)S(1)}, f32[8]{0:T(128)S(1)}) fusion(f32[8,2]{0,1:T(2,128)} %param.18, s32[8,2]{0,1:T(2,128)} %param.17, s32[]{:T(128)} %bitcast.3, s32[]{:T(128)} %bitcast.1, s32[]{:T(128)} %bitcast, s32[]{:T(128)} %bitcast.2), kind=kLoop, calls=%fused_computation.27 | loop fusion | flops 160 | bytes 272 | tf_op jit(solution)/shard_map/reduce_sum | solution.py:225
  10.9 0.9 collective-permute-done.1
  11.9 3.4 %collective-permute-done.2 = bf16[8,7168]{1,0:T(8,128)(2,1)S(1)} collective-permute-done((bf16[8,7168]{1,0:T(8,128)(2,1)}, bf16[8,7168]{1,0:T(8,128)(2,1)S(1)}, u32[]{:S(2)}, u32[]{:S(2)}) %collective-permute-start.2) | collective-permute-done | bytes 114720 | tf_op jit(solution)/shard_map/ppermute | solution.py:26
  15.2 0.9 constant_dynamic-update-slice_fusion.3
  16.2 5.0 %collective-permute-start.4 = (bf16[32,7168]{1,0:T(8,128)(2,1)S(1)}, bf16[32,7168]{1,0:T(8,128)(2,1)S(1)}, u32[]{:S(2)}, u32[]{:S(2)}) collective-permute-start(bf16[32,7168]{1,0:T(8,128)(2,1)S(1)} %constant_dynamic-update-slice_fusion.refs_0_), channel_id=1, source_target_pairs={{0,4},{1,3},{2,6},{3,1},{4,0},{5,7},{6,2},{7,5},{8,12},{9,11},{10,... | collective-permute-start | bytes 1376264 | tf_op jit(solution)/shard_map/ppermute | solution.py:26
  21.1 0.6 collective-permute-start.5
  21.7 10.3 %collective-permute-done.4.refs_1_ = bf16[32,7168]{1,0:T(8,128)(2,1)S(1)} collective-permute-done((bf16[32,7168]{1,0:T(8,128)(2,1)S(1)}, bf16[32,7168]{1,0:T(8,128)(2,1)S(1)}, u32[]{:S(2)}, u32[]{:S(2)}) %collective-permute-start.4) | collective-permute-done | bytes 458784 | tf_op jit(solution)/shard_map/ppermute | solution.py:26
  32.1 0.5 collective-permute-start.6
  32.6 1.1 %slice.174 = bf16[5,96,576]{2,1,0:T(8,128)(2,1)S(1)} slice(bf16[8,96,576]{2,1,0:T(8,128)(2,1)} %refs_3_.1), slice={[0:5], [0:96], [0:576]} | slice | bytes 1105920 | tf_op jit(solution)/shard_map/slice | solution.py:253
  33.7 4.2 %shard_map.122 = (bf16[1,7168,256]{2,1,0:T(8,128)(2,1)S(1)}, bf16[1,7168,256]{2,1,0:T(8,128)(2,1)S(1)}, bf16[1,256,7168]{2,1,0:T(8,128)(2,1)S(1)}) custom-call(bf16[1,7168,256]{2,1,0:T(8,128)(2,1)} %refs_0_.2, bf16[1,7168,256]{2,1,0:T(8,128)(2,1)} %refs_1_.2, bf16[1,256,7168]{2,1,0:T(8,128)(2,1)} %refs_2_.2), custom_call_target="tpu_custom_call" | custom-call | bytes 22020096 | tf_op jit(solution)/shard_map/pallas_call | solution.py:127
  38.0 0.6 collective-permute-start.10
  38.6 2.0 %collective-permute-done.6.refs_3_ = bf16[32,7168]{1,0:T(8,128)(2,1)S(1)} collective-permute-done((bf16[32,7168]{1,0:T(8,128)(2,1)S(1)}, bf16[32,7168]{1,0:T(8,128)(2,1)S(1)}, u32[]{:S(2)}, u32[]{:S(2)}) %collective-permute-start.6) | collective-permute-done | bytes 458784 | tf_op jit(solution)/shard_map/ppermute | solution.py:26
  40.5 0.8 collective-permute-start.13
  41.4 1.0 collective-permute-done.11.refs_7_
  42.4 5.3 %shard_map.123 = (bf16[128,7168]{1,0:T(8,128)(2,1)S(1)}, bf16[64,7168]{1,0:T(8,128)(2,1)S(1)}, bf16[64,7168]{1,0:T(8,128)(2,1)S(1)}) custom-call(bf16[32,7168]{1,0:T(8,128)(2,1)S(1)} %constant_dynamic-update-slice_fusion.refs_0_, bf16[32,7168]{1,0:T(8,128)(2,1)S(1)} %collective-permute-done.4.refs_1_, bf16[32,7168]{1,0:T(8,128)(2,1)S(1)} %collective-permute-done.5.refs_2_, ...), custom_call_target="tpu_custom_call" | custom-call | flops 2818572288 | bytes 18350080 | tf_op jit(solution)/shard_map/pallas_call | solution.py:179
  47.7 4.8 %collective-permute-start.14 = (bf16[64,7168]{1,0:T(8,128)(2,1)S(1)}, bf16[64,7168]{1,0:T(8,128)(2,1)S(1)}, u32[]{:S(2)}, u32[]{:S(2)}) collective-permute-start(bf16[64,7168]{1,0:T(8,128)(2,1)S(1)} %get-tuple-element.62), channel_id=1, source_target_pairs={{0,1},{1,0},{2,3},{3,2},{4,5},{5,4},{6,7},{7,6},{8,9},{9,8},{10,11... | collective-permute-start | bytes 2752520 | tf_op jit(solution)/shard_map/ppermute | solution.py:26
  52.6 0.1 collective-permute-start.12
  52.7 1.9 %collective-permute-done.14 = bf16[64,7168]{1,0:T(8,128)(2,1)S(1)} collective-permute-done((bf16[64,7168]{1,0:T(8,128)(2,1)S(1)}, bf16[64,7168]{1,0:T(8,128)(2,1)S(1)}, u32[]{:S(2)}, u32[]{:S(2)}) %collective-permute-start.14) | collective-permute-done | bytes 917536 | tf_op jit(solution)/shard_map/ppermute | solution.py:26
  54.7 0.7 collective-permute-start.17
  55.4 3.3 %collective-permute-start.16 = (bf16[32,4480]{1,0:T(8,128)(2,1)S(1)}, bf16[32,4480]{1,0:T(8,128)(2,1)S(1)}, u32[]{:S(2)}, u32[]{:S(2)}) collective-permute-start(bf16[32,4480]{1,0:T(8,128)(2,1)S(1)} %add_convert_fusion.2), channel_id=1, source_target_pairs={{0,2},{1,5},{2,0},{3,7},{4,6},{5,1},{6,4},{7,3},{8,10},{9,13},{10,... | collective-permute-start | bytes 860168 | tf_op jit(solution)/shard_map/ppermute | solution.py:26
  58.7 8.4 %collective-permute-done.16 = bf16[32,4480]{1,0:T(8,128)(2,1)S(1)} collective-permute-done((bf16[32,4480]{1,0:T(8,128)(2,1)S(1)}, bf16[32,4480]{1,0:T(8,128)(2,1)S(1)}, u32[]{:S(2)}, u32[]{:S(2)}) %collective-permute-start.16) | collective-permute-done | bytes 286752 | tf_op jit(solution)/shard_map/ppermute | solution.py:26
  67.1 0.2 add_convert_fusion.1
  67.3 0.5 collective-permute-start.18
  67.9 2.5 %collective-permute-start.15 = (bf16[32,4480]{1,0:T(8,128)(2,1)S(1)}, bf16[32,4480]{1,0:T(8,128)(2,1)S(1)}, u32[]{:S(2)}, u32[]{:S(2)}) collective-permute-start(bf16[32,4480]{1,0:T(8,128)(2,1)S(1)} %get-tuple-element.98), channel_id=1, source_target_pairs={{0,2},{1,5},{2,0},{3,7},{4,6},{5,1},{6,4},{7,3},{8,10},{9,13},{10,... | collective-permute-start | bytes 860168 | tf_op jit(solution)/shard_map/ppermute | solution.py:26
  70.4 2.4 %shard_map.124 = bf16[8,64,512]{2,1,0:T(8,128)(2,1)} custom-call(s32[8]{0:T(128)S(1)} %copy-done.3, s32[8]{0:T(128)S(1)} %copy-done.4, bf16[8,64,576]{2,1,0:T(8,128)(2,1)S(1)} %copy-done.1, bf16[8,96,576]{2,1,0:T(8,128)(2,1)S(1)} %copy-done, bf16[8,96,576]{2,1,0:T(8,128)(2,1)S(1)} %collective-permute-done.9.refs_4_, bf16[8,576]{1,0:T(8,128)(2,1)S(1)} %copy-done.2, ...), custom_call_target="tpu_custom_call" | custom-call | flops 106954752 | bytes 4653056 | tf_op jit(solution)/shard_map/pallas_call | solution.py:99
  72.8 2.0 %collective-permute-done.18 = bf16[32,4480]{1,0:T(8,128)(2,1)S(1)} collective-permute-done((bf16[32,4480]{1,0:T(8,128)(2,1)S(1)}, bf16[32,4480]{1,0:T(8,128)(2,1)S(1)}, u32[]{:S(2)}, u32[]{:S(2)}) %collective-permute-start.18) | collective-permute-done | bytes 286752 | tf_op jit(solution)/shard_map/ppermute | solution.py:26
  74.8 2.6 %collective-permute-done.15 = bf16[32,4480]{1,0:T(8,128)(2,1)S(1)} collective-permute-done((bf16[32,4480]{1,0:T(8,128)(2,1)S(1)}, bf16[32,4480]{1,0:T(8,128)(2,1)S(1)}, u32[]{:S(2)}, u32[]{:S(2)}) %collective-permute-start.15) | collective-permute-done | bytes 286752 | tf_op jit(solution)/shard_map/ppermute | solution.py:26
  77.4 0.1 convert_add_fusion
  77.6 1.7 %collective-permute-done.19 = bf16[32,2688]{1,0:T(8,128)(2,1)S(1)} collective-permute-done((bf16[32,2688]{1,0:T(8,128)(2,1)S(1)}, bf16[32,2688]{1,0:T(8,128)(2,1)S(1)}, u32[]{:S(2)}, u32[]{:S(2)}) %collective-permute-start.19) | collective-permute-done | bytes 172064 | tf_op jit(solution)/shard_map/ppermute | solution.py:26
  79.3 0.1 add_convert_fusion.3
  79.4 1.8 %collective-permute-start.24 = (bf16[32,2688]{1,0:T(8,128)(2,1)S(1)}, bf16[32,2688]{1,0:T(8,128)(2,1)S(1)}, u32[]{:S(2)}, u32[]{:S(2)}) collective-permute-start(bf16[32,2688]{1,0:T(8,128)(2,1)S(1)} %get-tuple-element.85), channel_id=1, source_target_pairs={{0,4},{1,3},{2,6},{3,1},{4,0},{5,7},{6,2},{7,5},{8,12},{9,11},{10,... | collective-permute-start | bytes 516104 | tf_op jit(solution)/shard_map/ppermute | solution.py:26
  81.1 1.0 %collective-permute-start.23 = (bf16[32,2688]{1,0:T(8,128)(2,1)S(1)}, bf16[32,2688]{1,0:T(8,128)(2,1)S(1)}, u32[]{:S(2)}, u32[]{:S(2)}) collective-permute-start(bf16[32,2688]{1,0:T(8,128)(2,1)S(1)} %get-tuple-element.96), channel_id=1, source_target_pairs={{0,2},{1,5},{2,0},{3,7},{4,6},{5,1},{6,4},{7,3},{8,10},{9,13},{10,... | collective-permute-start | bytes 516104 | tf_op jit(solution)/shard_map/ppermute | solution.py:26
  82.1 2.8 %collective-permute-start.20 = (bf16[8,4480]{1,0:T(8,128)(2,1)S(1)}, bf16[8,4480]{1,0:T(8,128)(2,1)S(1)}, u32[]{:S(2)}, u32[]{:S(2)}) collective-permute-start(bf16[8,4480]{1,0:T(8,128)(2,1)S(1)} %get-tuple-element.79), channel_id=1, source_target_pairs={{0,8},{1,9},{2,10},{3,11},{4,12},{5,13},{6,14},{7,15},{8,0},{9,1},... | collective-permute-start | bytes 215048 | tf_op jit(solution)/shard_map/ppermute | solution.py:26
  84.9 1.2 %collective-permute-start.21 = (bf16[8,4480]{1,0:T(8,128)(2,1)S(1)}, bf16[8,4480]{1,0:T(8,128)(2,1)S(1)}, u32[]{:S(2)}, u32[]{:S(2)}) collective-permute-start(bf16[8,4480]{1,0:T(8,128)(2,1)S(1)} %get-tuple-element.81), channel_id=1, source_target_pairs={{0,16},{1,17},{2,18},{3,19},{4,20},{5,21},{6,22},{7,23},{8,24},{9,... | collective-permute-start | bytes 215048 | tf_op jit(solution)/shard_map/ppermute | solution.py:26
  86.1 1.5 %collective-permute-start.22 = (bf16[8,4480]{1,0:T(8,128)(2,1)S(1)}, bf16[8,4480]{1,0:T(8,128)(2,1)S(1)}, u32[]{:S(2)}, u32[]{:S(2)}) collective-permute-start(bf16[8,4480]{1,0:T(8,128)(2,1)S(1)} %get-tuple-element.83), channel_id=1, source_target_pairs={{0,24},{1,25},{2,26},{3,27},{4,28},{5,29},{6,30},{7,31},{8,16},{9,... | collective-permute-start | bytes 215048 | tf_op jit(solution)/shard_map/ppermute | solution.py:26
  87.6 0.1 add_convert_fusion.10
  87.7 1.1 %collective-permute-start.25 = (bf16[8,2688]{1,0:T(8,128)(2,1)S(1)}, bf16[8,2688]{1,0:T(8,128)(2,1)S(1)}, u32[]{:S(2)}, u32[]{:S(2)}) collective-permute-start(bf16[8,2688]{1,0:T(8,128)(2,1)S(1)} %get-tuple-element.93), channel_id=1, source_target_pairs={{0,8},{1,9},{2,10},{3,11},{4,12},{5,13},{6,14},{7,15},{8,0},{9,1},... | collective-permute-start | bytes 129032 | tf_op jit(solution)/shard_map/ppermute | solution.py:26
  88.7 1.9 %collective-permute-start.26 = (bf16[8,2688]{1,0:T(8,128)(2,1)S(1)}, bf16[8,2688]{1,0:T(8,128)(2,1)S(1)}, u32[]{:S(2)}, u32[]{:S(2)}) collective-permute-start(bf16[8,2688]{1,0:T(8,128)(2,1)S(1)} %get-tuple-element.95), channel_id=1, source_target_pairs={{0,16},{1,17},{2,18},{3,19},{4,20},{5,21},{6,22},{7,23},{8,24},{9,... | collective-permute-start | bytes 129032 | tf_op jit(solution)/shard_map/ppermute | solution.py:26
  90.7 1.5 %collective-permute-start.27 = (bf16[8,2688]{1,0:T(8,128)(2,1)S(1)}, bf16[8,2688]{1,0:T(8,128)(2,1)S(1)}, u32[]{:S(2)}, u32[]{:S(2)}) collective-permute-start(bf16[8,2688]{1,0:T(8,128)(2,1)S(1)} %get-tuple-element.94), channel_id=1, source_target_pairs={{0,24},{1,25},{2,26},{3,27},{4,28},{5,29},{6,30},{7,31},{8,16},{9,... | collective-permute-start | bytes 129032 | tf_op jit(solution)/shard_map/ppermute | solution.py:26
  92.1 2.6 %collective-permute-done.21 = bf16[8,4480]{1,0:T(8,128)(2,1)S(1)} collective-permute-done((bf16[8,4480]{1,0:T(8,128)(2,1)S(1)}, bf16[8,4480]{1,0:T(8,128)(2,1)S(1)}, u32[]{:S(2)}, u32[]{:S(2)}) %collective-permute-start.21) | collective-permute-done | bytes 71712 | tf_op jit(solution)/shard_map/ppermute | solution.py:26
  94.7 0.1 add_convert_fusion.6
  94.8 2.3 %collective-permute-done.26 = bf16[8,2688]{1,0:T(8,128)(2,1)S(1)} collective-permute-done((bf16[8,2688]{1,0:T(8,128)(2,1)S(1)}, bf16[8,2688]{1,0:T(8,128)(2,1)S(1)}, u32[]{:S(2)}, u32[]{:S(2)}) %collective-permute-start.26) | collective-permute-done | bytes 43040 | tf_op jit(solution)/shard_map/ppermute | solution.py:26
  97.1 0.1 add_convert_fusion.7
  97.2 0.7 pad_maximum_fusion
  (40 shorter events, 0.3 us)
Async XLA Ops:
  0.6 14.6 %collective-permute-start.3 = (bf16[8,96,576]{2,1,0:T(8,128)(2,1)}, bf16[8,96,576]{2,1,0:T(8,128)(2,1)S(1)}, u32[]{:S(2)}, u32[]{:S(2)}) collective-permute-start(bf16[8,96,576]{2,1,0:T(8,128)(2,1)} %refs_3_.1), channel_id=1, source_target_pairs={{1,2},{3,4},{5,6},{6,5},{9,10},{11,12},{13,14},{14,13},{17,18},{19... | collective-permute-start | bytes 2654216 | tf_op jit(solution)/shard_map/ppermute | solution.py:47
  1.4 9.6 %collective-permute-start = (bf16[8,7168]{1,0:T(8,128)(2,1)}, bf16[8,7168]{1,0:T(8,128)(2,1)S(1)}, u32[]{:S(2)}, u32[]{:S(2)}) collective-permute-start(bf16[8,7168]{1,0:T(8,128)(2,1)} %param.16), channel_id=1, source_target_pairs={{0,8},{1,9},{2,10},{3,11},{4,12},{5,13},{6,14},{7,15},{8,0},{9,1},... | collective-permute-start | bytes 344072 | tf_op jit(solution)/shard_map/ppermute | solution.py:26
  4.4 7.4 %collective-permute-start.1 = (bf16[8,7168]{1,0:T(8,128)(2,1)}, bf16[8,7168]{1,0:T(8,128)(2,1)S(1)}, u32[]{:S(2)}, u32[]{:S(2)}) collective-permute-start(bf16[8,7168]{1,0:T(8,128)(2,1)} %param.16), channel_id=1, source_target_pairs={{0,16},{1,17},{2,18},{3,19},{4,20},{5,21},{6,22},{7,23},{8,24},{9,... | collective-permute-start | bytes 344072 | tf_op jit(solution)/shard_map/ppermute | solution.py:26
  7.0 8.2 %collective-permute-start.2 = (bf16[8,7168]{1,0:T(8,128)(2,1)}, bf16[8,7168]{1,0:T(8,128)(2,1)S(1)}, u32[]{:S(2)}, u32[]{:S(2)}) collective-permute-start(bf16[8,7168]{1,0:T(8,128)(2,1)} %param.16), channel_id=1, source_target_pairs={{0,24},{1,25},{2,26},{3,27},{4,28},{5,29},{6,30},{7,31},{8,16},{9,... | collective-permute-start | bytes 344072 | tf_op jit(solution)/shard_map/ppermute | solution.py:26
  16.2 15.9 %collective-permute-start.4 = (bf16[32,7168]{1,0:T(8,128)(2,1)S(1)}, bf16[32,7168]{1,0:T(8,128)(2,1)S(1)}, u32[]{:S(2)}, u32[]{:S(2)}) collective-permute-start(bf16[32,7168]{1,0:T(8,128)(2,1)S(1)} %constant_dynamic-update-slice_fusion.refs_0_), channel_id=1, source_target_pairs={{0,4},{1,3},{2,6},{3,1},{4,0},{5,7},{6,2},{7,5},{8,12},{9,11},{10,... | collective-permute-start | bytes 1376264 | tf_op jit(solution)/shard_map/ppermute | solution.py:26
  21.1 17.4 %collective-permute-start.9 = (bf16[8,96,576]{2,1,0:T(8,128)(2,1)}, bf16[8,96,576]{2,1,0:T(8,128)(2,1)S(1)}, u32[]{:S(2)}, u32[]{:S(2)}) collective-permute-start(bf16[8,96,576]{2,1,0:T(8,128)(2,1)} %refs_3_.1), channel_id=1, source_target_pairs={{0,1},{1,0},{2,3},{3,2},{4,5},{5,4},{6,7},{7,6},{8,9},{9,8},{10,11... | collective-permute-start | bytes 2654216 | tf_op jit(solution)/shard_map/ppermute | solution.py:26
  21.1 16.8 %collective-permute-start.5 = (bf16[32,7168]{1,0:T(8,128)(2,1)S(1)}, bf16[32,7168]{1,0:T(8,128)(2,1)S(1)}, u32[]{:S(2)}, u32[]{:S(2)}) collective-permute-start(bf16[32,7168]{1,0:T(8,128)(2,1)S(1)} %constant_dynamic-update-slice_fusion.refs_0_), channel_id=1, source_target_pairs={{0,2},{1,5},{2,0},{3,7},{4,6},{5,1},{6,4},{7,3},{8,10},{9,13},{10,... | collective-permute-start | bytes 1376264 | tf_op jit(solution)/shard_map/ppermute | solution.py:26
  21.7 16.8 %collective-permute-start.7 = (bf16[32,7168]{1,0:T(8,128)(2,1)S(1)}, bf16[32,7168]{1,0:T(8,128)(2,1)S(1)}, u32[]{:S(2)}, u32[]{:S(2)}) collective-permute-start(bf16[32,7168]{1,0:T(8,128)(2,1)S(1)} %constant_dynamic-update-slice_fusion.refs_0_), channel_id=1, source_target_pairs={{0,1},{1,0},{2,3},{3,2},{4,5},{5,4},{6,7},{7,6},{8,9},{9,8},{10,11... | collective-permute-start | bytes 1376264 | tf_op jit(solution)/shard_map/ppermute | solution.py:26
  32.1 8.5 %collective-permute-start.6 = (bf16[32,7168]{1,0:T(8,128)(2,1)S(1)}, bf16[32,7168]{1,0:T(8,128)(2,1)S(1)}, u32[]{:S(2)}, u32[]{:S(2)}) collective-permute-start(bf16[32,7168]{1,0:T(8,128)(2,1)S(1)} %collective-permute-done.4.refs_1_), channel_id=1, source_target_pairs={{0,2},{1,5},{2,0},{3,7},{4,6},{5,1},{6,4},{7,3},{8,10},{9,13},{10,... | collective-permute-start | bytes 1376264 | tf_op jit(solution)/shard_map/ppermute | solution.py:26
  32.6 7.9 %collective-permute-start.8 = (bf16[32,7168]{1,0:T(8,128)(2,1)S(1)}, bf16[32,7168]{1,0:T(8,128)(2,1)S(1)}, u32[]{:S(2)}, u32[]{:S(2)}) collective-permute-start(bf16[32,7168]{1,0:T(8,128)(2,1)S(1)} %collective-permute-done.4.refs_1_), channel_id=1, source_target_pairs={{0,1},{1,0},{2,3},{3,2},{4,5},{5,4},{6,7},{7,6},{8,9},{9,8},{10,11... | collective-permute-start | bytes 1376264 | tf_op jit(solution)/shard_map/ppermute | solution.py:26
  38.0 3.4 %collective-permute-start.10 = (bf16[32,7168]{1,0:T(8,128)(2,1)S(1)}, bf16[32,7168]{1,0:T(8,128)(2,1)S(1)}, u32[]{:S(2)}, u32[]{:S(2)}) collective-permute-start(bf16[32,7168]{1,0:T(8,128)(2,1)S(1)} %collective-permute-done.5.refs_2_), channel_id=1, source_target_pairs={{0,1},{1,0},{2,3},{3,2},{4,5},{5,4},{6,7},{7,6},{8,9},{9,8},{10,11... | collective-permute-start | bytes 1376264 | tf_op jit(solution)/shard_map/ppermute | solution.py:26
  40.5 12.0 %copy-start = (bf16[8,96,576]{2,1,0:T(8,128)(2,1)S(1)}, bf16[8,96,576]{2,1,0:T(8,128)(2,1)}, u32[]{:S(2)}) copy-start(bf16[8,96,576]{2,1,0:T(8,128)(2,1)} %refs_3_.1) | copy-start | bytes 2654212
  40.5 1.8 %collective-permute-start.11 = (bf16[32,7168]{1,0:T(8,128)(2,1)S(1)}, bf16[32,7168]{1,0:T(8,128)(2,1)S(1)}, u32[]{:S(2)}, u32[]{:S(2)}) collective-permute-start(bf16[32,7168]{1,0:T(8,128)(2,1)S(1)} %collective-permute-done.6.refs_3_), channel_id=1, source_target_pairs={{0,1},{1,0},{2,3},{3,2},{4,5},{5,4},{6,7},{7,6},{8,9},{9,8},{10,11... | collective-permute-start | bytes 1376264 | tf_op jit(solution)/shard_map/ppermute | solution.py:26
  40.5 7.1 %collective-permute-start.13 = (bf16[5,96,576]{2,1,0:T(8,128)(2,1)S(1)}, bf16[5,96,576]{2,1,0:T(8,128)(2,1)S(1)}, u32[]{:S(2)}, u32[]{:S(2)}) collective-permute-start(bf16[5,96,576]{2,1,0:T(8,128)(2,1)S(1)} %slice.174), channel_id=1, source_target_pairs={{2,1},{4,3},{7,8},{8,7},{10,9},{12,11},{15,16},{16,15},{18,17},{20... | collective-permute-start | bytes 1658888 | tf_op jit(solution)/shard_map/ppermute | solution.py:47
  47.7 6.9 %collective-permute-start.14 = (bf16[64,7168]{1,0:T(8,128)(2,1)S(1)}, bf16[64,7168]{1,0:T(8,128)(2,1)S(1)}, u32[]{:S(2)}, u32[]{:S(2)}) collective-permute-start(bf16[64,7168]{1,0:T(8,128)(2,1)S(1)} %get-tuple-element.62), channel_id=1, source_target_pairs={{0,1},{1,0},{2,3},{3,2},{4,5},{5,4},{6,7},{7,6},{8,9},{9,8},{10,11... | collective-permute-start | bytes 2752520 | tf_op jit(solution)/shard_map/ppermute | solution.py:26
  52.5 17.8 %copy-start.1 = (bf16[8,64,576]{2,1,0:T(8,128)(2,1)S(1)}, bf16[8,64,576]{2,1,0:T(8,128)(2,1)}, u32[]{:S(2)}) copy-start(bf16[8,64,576]{2,1,0:T(8,128)(2,1)} %refs_2_.3) | copy-start | bytes 1769476
  52.6 17.8 %copy-start.2 = (bf16[8,576]{1,0:T(8,128)(2,1)S(1)}, bf16[8,576]{1,0:T(8,128)(2,1)}, u32[]{:S(2)}) copy-start(bf16[8,576]{1,0:T(8,128)(2,1)} %refs_5_.1) | copy-start | bytes 27652
  52.6 17.8 %copy-start.3 = (s32[8]{0:T(128)S(1)}, s32[8]{0:T(128)}, u32[]{:S(2)}) copy-start(s32[8]{0:T(128)} %refs_0_.3) | copy-start | bytes 100
  52.6 17.8 %copy-start.4 = (s32[8]{0:T(128)S(1)}, s32[8]{0:T(128)}, u32[]{:S(2)}) copy-start(s32[8]{0:T(128)} %refs_1_.3) | copy-start | bytes 100
  52.6 14.5 %collective-permute-start.12 = (bf16[64,7168]{1,0:T(8,128)(2,1)S(1)}, bf16[64,7168]{1,0:T(8,128)(2,1)S(1)}, u32[]{:S(2)}, u32[]{:S(2)}) collective-permute-start(bf16[64,7168]{1,0:T(8,128)(2,1)S(1)} %get-tuple-element.59), channel_id=1, source_target_pairs={{0,1},{1,0},{2,3},{3,2},{4,5},{5,4},{6,7},{7,6},{8,9},{9,8},{10,11... | collective-permute-start | bytes 2752520 | tf_op jit(solution)/shard_map/ppermute | solution.py:26
  54.7 12.5 %collective-permute-start.17 = (bf16[3,96,576]{2,1,0:T(8,128)(2,1)S(1)}, bf16[3,96,576]{2,1,0:T(8,128)(2,1)S(1)}, u32[]{:S(2)}, u32[]{:S(2)}) collective-permute-start(bf16[3,96,576]{2,1,0:T(8,128)(2,1)S(1)} %slice.186), channel_id=1, source_target_pairs={{2,1},{4,3},{7,8},{8,7},{10,9},{12,11},{15,16},{16,15},{18,17},{20... | collective-permute-start | bytes 995336 | tf_op jit(solution)/shard_map/ppermute | solution.py:47
  55.4 11.8 %collective-permute-start.16 = (bf16[32,4480]{1,0:T(8,128)(2,1)S(1)}, bf16[32,4480]{1,0:T(8,128)(2,1)S(1)}, u32[]{:S(2)}, u32[]{:S(2)}) collective-permute-start(bf16[32,4480]{1,0:T(8,128)(2,1)S(1)} %add_convert_fusion.2), channel_id=1, source_target_pairs={{0,2},{1,5},{2,0},{3,7},{4,6},{5,1},{6,4},{7,3},{8,10},{9,13},{10,... | collective-permute-start | bytes 860168 | tf_op jit(solution)/shard_map/ppermute | solution.py:26
  67.3 7.5 %collective-permute-start.18 = (bf16[32,4480]{1,0:T(8,128)(2,1)S(1)}, bf16[32,4480]{1,0:T(8,128)(2,1)S(1)}, u32[]{:S(2)}, u32[]{:S(2)}) collective-permute-start(bf16[32,4480]{1,0:T(8,128)(2,1)S(1)} %get-tuple-element.68), channel_id=1, source_target_pairs={{0,4},{1,3},{2,6},{3,1},{4,0},{5,7},{6,2},{7,5},{8,12},{9,11},{10,... | collective-permute-start | bytes 860168 | tf_op jit(solution)/shard_map/ppermute | solution.py:26
  67.9 9.6 %collective-permute-start.15 = (bf16[32,4480]{1,0:T(8,128)(2,1)S(1)}, bf16[32,4480]{1,0:T(8,128)(2,1)S(1)}, u32[]{:S(2)}, u32[]{:S(2)}) collective-permute-start(bf16[32,4480]{1,0:T(8,128)(2,1)S(1)} %get-tuple-element.98), channel_id=1, source_target_pairs={{0,2},{1,5},{2,0},{3,7},{4,6},{5,1},{6,4},{7,3},{8,10},{9,13},{10,... | collective-permute-start | bytes 860168 | tf_op jit(solution)/shard_map/ppermute | solution.py:26
  70.3 8.9 %collective-permute-start.19 = (bf16[32,2688]{1,0:T(8,128)(2,1)S(1)}, bf16[32,2688]{1,0:T(8,128)(2,1)S(1)}, u32[]{:S(2)}, u32[]{:S(2)}) collective-permute-start(bf16[32,2688]{1,0:T(8,128)(2,1)S(1)} %add_convert_fusion.5), channel_id=1, source_target_pairs={{0,2},{1,5},{2,0},{3,7},{4,6},{5,1},{6,4},{7,3},{8,10},{9,13},{10,... | collective-permute-start | bytes 516104 | tf_op jit(solution)/shard_map/ppermute | solution.py:26
  79.4 8.2 %collective-permute-start.24 = (bf16[32,2688]{1,0:T(8,128)(2,1)S(1)}, bf16[32,2688]{1,0:T(8,128)(2,1)S(1)}, u32[]{:S(2)}, u32[]{:S(2)}) collective-permute-start(bf16[32,2688]{1,0:T(8,128)(2,1)S(1)} %get-tuple-element.85), channel_id=1, source_target_pairs={{0,4},{1,3},{2,6},{3,1},{4,0},{5,7},{6,2},{7,5},{8,12},{9,11},{10,... | collective-permute-start | bytes 516104 | tf_op jit(solution)/shard_map/ppermute | solution.py:26
  81.1 6.5 %collective-permute-start.23 = (bf16[32,2688]{1,0:T(8,128)(2,1)S(1)}, bf16[32,2688]{1,0:T(8,128)(2,1)S(1)}, u32[]{:S(2)}, u32[]{:S(2)}) collective-permute-start(bf16[32,2688]{1,0:T(8,128)(2,1)S(1)} %get-tuple-element.96), channel_id=1, source_target_pairs={{0,2},{1,5},{2,0},{3,7},{4,6},{5,1},{6,4},{7,3},{8,10},{9,13},{10,... | collective-permute-start | bytes 516104 | tf_op jit(solution)/shard_map/ppermute | solution.py:26
  82.1 8.5 %collective-permute-start.20 = (bf16[8,4480]{1,0:T(8,128)(2,1)S(1)}, bf16[8,4480]{1,0:T(8,128)(2,1)S(1)}, u32[]{:S(2)}, u32[]{:S(2)}) collective-permute-start(bf16[8,4480]{1,0:T(8,128)(2,1)S(1)} %get-tuple-element.79), channel_id=1, source_target_pairs={{0,8},{1,9},{2,10},{3,11},{4,12},{5,13},{6,14},{7,15},{8,0},{9,1},... | collective-permute-start | bytes 215048 | tf_op jit(solution)/shard_map/ppermute | solution.py:26
  84.9 9.7 %collective-permute-start.21 = (bf16[8,4480]{1,0:T(8,128)(2,1)S(1)}, bf16[8,4480]{1,0:T(8,128)(2,1)S(1)}, u32[]{:S(2)}, u32[]{:S(2)}) collective-permute-start(bf16[8,4480]{1,0:T(8,128)(2,1)S(1)} %get-tuple-element.81), channel_id=1, source_target_pairs={{0,16},{1,17},{2,18},{3,19},{4,20},{5,21},{6,22},{7,23},{8,24},{9,... | collective-permute-start | bytes 215048 | tf_op jit(solution)/shard_map/ppermute | solution.py:26
  86.1 8.6 %collective-permute-start.22 = (bf16[8,4480]{1,0:T(8,128)(2,1)S(1)}, bf16[8,4480]{1,0:T(8,128)(2,1)S(1)}, u32[]{:S(2)}, u32[]{:S(2)}) collective-permute-start(bf16[8,4480]{1,0:T(8,128)(2,1)S(1)} %get-tuple-element.83), channel_id=1, source_target_pairs={{0,24},{1,25},{2,26},{3,27},{4,28},{5,29},{6,30},{7,31},{8,16},{9,... | collective-permute-start | bytes 215048 | tf_op jit(solution)/shard_map/ppermute | solution.py:26
  87.7 7.1 %collective-permute-start.25 = (bf16[8,2688]{1,0:T(8,128)(2,1)S(1)}, bf16[8,2688]{1,0:T(8,128)(2,1)S(1)}, u32[]{:S(2)}, u32[]{:S(2)}) collective-permute-start(bf16[8,2688]{1,0:T(8,128)(2,1)S(1)} %get-tuple-element.93), channel_id=1, source_target_pairs={{0,8},{1,9},{2,10},{3,11},{4,12},{5,13},{6,14},{7,15},{8,0},{9,1},... | collective-permute-start | bytes 129032 | tf_op jit(solution)/shard_map/ppermute | solution.py:26
  88.7 8.3 %collective-permute-start.26 = (bf16[8,2688]{1,0:T(8,128)(2,1)S(1)}, bf16[8,2688]{1,0:T(8,128)(2,1)S(1)}, u32[]{:S(2)}, u32[]{:S(2)}) collective-permute-start(bf16[8,2688]{1,0:T(8,128)(2,1)S(1)} %get-tuple-element.95), channel_id=1, source_target_pairs={{0,16},{1,17},{2,18},{3,19},{4,20},{5,21},{6,22},{7,23},{8,24},{9,... | collective-permute-start | bytes 129032 | tf_op jit(solution)/shard_map/ppermute | solution.py:26
  90.7 6.4 %collective-permute-start.27 = (bf16[8,2688]{1,0:T(8,128)(2,1)S(1)}, bf16[8,2688]{1,0:T(8,128)(2,1)S(1)}, u32[]{:S(2)}, u32[]{:S(2)}) collective-permute-start(bf16[8,2688]{1,0:T(8,128)(2,1)S(1)} %get-tuple-element.94), channel_id=1, source_target_pairs={{0,24},{1,25},{2,26},{3,27},{4,28},{5,29},{6,30},{7,31},{8,16},{9,... | collective-permute-start | bytes 129032 | tf_op jit(solution)/shard_map/ppermute | solution.py:26

commit v12 on v11

--- a/solution.py
+++ b/solution.py
@@ -262,16 +262,16 @@
     pieces.append(early)
     column = jnp.concatenate(column)
     near = swapped(column, first)
-    side = swapped(column, second)
+    again, near = tied(column, near)
     across = swapped(near, second)
+    side = swapped(again, second)
     beside = swapped(latent_cache, twin)
     twin_column, twin_near = swapped(column, twin), swapped(near, twin)
     weights = fetched([gate_weight, up_weight, down_weight])
     across, twin_column, twin_near, weights, beside = tied(
         across, twin_column, twin_near, weights, beside
     )
-    middle = 5 * beam_count // 8
-    late, across = cache_rows("late", 0, middle, across)
+    late, across = cache_rows("late", 0, beam_count, across)
     held = [column, near, side, across, twin_column, twin_near]
     held = held + [swapped(side, twin), swapped(across, twin)]
     own, high, low = experts(held, weights)
@@ -309,10 +309,7 @@
         ]
 
     across, high = tied(to_second(halves[0]), high)
-    late, across = cache_rows("late", middle, beam_count, across)
     across = swapped(across, second)
-    across, late = tied(across, late)
-    pieces.append(late)
     near, side = to_first(halves[0], across), to_side(halves[0])
     near, across = tied(near, to_second(halves[1]))
     near, side, across = swapped(near, first), swapped(side, second), swapped(across, second)

time: 98.1 us -> 90.6 us (0.924)
  waiting for transfers between devices: 39 us -> 35.6 us
  starting transfers between devices: 38.5 us -> 35.7 us
  local copies, waits for them, and re-layouts: 2.74 us -> 1.64 us
    ppermute x25, waiting for transfers between devices: 39 us -> 35.5 us  [swapped(): return lax.ppermute(value, 'dp', [(i, partner(i)) for i in range(peers)])]
    ppermute x25, starting transfers between devices: 36.3 us -> 34.2 us  [swapped(): return lax.ppermute(value, 'dp', [(i, partner(i)) for i in range(peers)])]
    slice x2 -> x0, local copies, waits for them, and re-layouts: 1.16 us -> none  [cache_rows(): source = latent_cache[begin:end]]
    ppermute x3 -> x2, starting transfers between devices: 2.24 us -> 1.44 us  [neighbours(): return lax.ppermute(value, 'dp', [p for p in pairs if max(p) < peers])]
  transfers between devices with their start and end apart: 28 -> 27, of which waited for: 12 -> 15; matrix products, arithmetic and copies ran while one was open for 6% -> 5% of each run, Pallas kernels for 12% -> 13%
where the time goes in v12:
time: 90.6 us; the launch traced here: 90.4 us
  starting transfers between devices  35.7 us (39%)
  waiting for transfers between devices  35.6 us (39%)
  Pallas kernels  11.8 us (13%)
  other arithmetic  4.84 us (5%)
  local copies, waits for them, and re-layouts  1.64 us (2%)
    ppermute x25, waiting for transfers between devices, swapped(): return lax.ppermute(value, 'dp', [(i, partner(i)) for i in range(peers)])  35.5 us
    ppermute x25, starting transfers between devices, swapped(): return lax.ppermute(value, 'dp', [(i, partner(i)) for i in range(peers)])  34.2 us
    pallas_call x1, Pallas kernels, experts(): pl.pallas_call(lambda *refs: expert_kernel(wide, *refs), in_specs=[whole]...  5.3 us
    pallas_call x1, Pallas kernels, fetched(): pl.pallas_call(fetch_kernel, in_specs=[pl.BlockSpec(memory_space=pltpu.HB...  4.23 us
    reduce_sum x1, other arithmetic, body(): jnp.sum(jnp.where(routed_experts == targets[r], route_weights, 0.0), axis=1)  3.33 us
    pallas_call x1, Pallas kernels, attend(): pl.pallas_call(lambda *refs: attend_kernel(spans, *refs), in_specs=[scala...  2.3 us
  transfers between devices with their start and end apart: 27, of which 15 were waited for; matrix products, arithmetic and copies ran while one was open for 5% of the time, Pallas kernels for 13%

profile of v12, /device:TPU:0, one launch (start us, length us, event | category | flops | bytes accessed | tf_op | source)
XLA Modules:
  0.0 90.4 jit_solution(13925621935237025167)
XLA Ops:
  0.6 0.7 collective-permute-start.3
  1.4 4.1 %collective-permute-start.1 = (bf16[8,7168]{1,0:T(8,128)(2,1)}, bf16[8,7168]{1,0:T(8,128)(2,1)S(1)}, u32[]{:S(2)}, u32[]{:S(2)}) collective-permute-start(bf16[8,7168]{1,0:T(8,128)(2,1)} %param.16), channel_id=1, source_target_pairs={{0,16},{1,17},{2,18},{3,19},{4,20},{5,21},{6,22},{7,23},{8,24},{9,... | collective-permute-start | bytes 344072 | tf_op jit(solution)/shard_map/ppermute | solution.py:26
  5.5 1.6 %collective-permute-start = (bf16[8,7168]{1,0:T(8,128)(2,1)}, bf16[8,7168]{1,0:T(8,128)(2,1)S(1)}, u32[]{:S(2)}, u32[]{:S(2)}) collective-permute-start(bf16[8,7168]{1,0:T(8,128)(2,1)} %param.16), channel_id=1, source_target_pairs={{0,8},{1,9},{2,10},{3,11},{4,12},{5,13},{6,14},{7,15},{8,0},{9,1},... | collective-permute-start | bytes 344072 | tf_op jit(solution)/shard_map/ppermute | solution.py:26
  7.0 0.7 fusion.4
  7.7 3.3 %fusion.3 = (f32[8]{0:T(128)S(1)}, f32[8]{0:T(128)S(1)}, f32[8]{0:T(128)S(1)}, f32[8]{0:T(128)S(1)}) fusion(f32[8,2]{0,1:T(2,128)} %param.18, s32[8,2]{0,1:T(2,128)} %param.17, s32[]{:T(128)} %bitcast.3, s32[]{:T(128)} %bitcast.1, s32[]{:T(128)} %bitcast, s32[]{:T(128)} %bitcast.2), kind=kLoop, calls=%fused_computation.27 | loop fusion | flops 160 | bytes 272 | tf_op jit(solution)/shard_map/reduce_sum | solution.py:225
  11.1 0.9 %collective-permute-done = bf16[8,7168]{1,0:T(8,128)(2,1)S(1)} collective-permute-done((bf16[8,7168]{1,0:T(8,128)(2,1)}, bf16[8,7168]{1,0:T(8,128)(2,1)S(1)}, u32[]{:S(2)}, u32[]{:S(2)}) %collective-permute-start) | collective-permute-done | bytes 114720 | tf_op jit(solution)/shard_map/ppermute | solution.py:26
  12.0 3.2 %collective-permute-done.2 = bf16[8,7168]{1,0:T(8,128)(2,1)S(1)} collective-permute-done((bf16[8,7168]{1,0:T(8,128)(2,1)}, bf16[8,7168]{1,0:T(8,128)(2,1)S(1)}, u32[]{:S(2)}, u32[]{:S(2)}) %collective-permute-start.2) | collective-permute-done | bytes 114720 | tf_op jit(solution)/shard_map/ppermute | solution.py:26
  15.2 0.9 %constant_dynamic-update-slice_fusion.3 = bf16[32,7168]{1,0:T(8,128)(2,1)S(1)} fusion(bf16[8,7168]{1,0:T(8,128)(2,1)} %param.16), kind=kLoop, calls=%fused_computation.19 | loop fusion | bytes 229376
  16.2 5.0 %collective-permute-start.4 = (bf16[32,7168]{1,0:T(8,128)(2,1)S(1)}, bf16[32,7168]{1,0:T(8,128)(2,1)S(1)}, u32[]{:S(2)}, u32[]{:S(2)}) collective-permute-start(bf16[32,7168]{1,0:T(8,128)(2,1)S(1)} %constant_dynamic-update-slice_fusion.refs_0_), channel_id=1, source_target_pairs={{0,4},{1,3},{2,6},{3,1},{4,0},{5,7},{6,2},{7,5},{8,12},{9,11},{10,... | collective-permute-start | bytes 1376264 | tf_op jit(solution)/shard_map/ppermute | solution.py:26
  21.2 0.5 collective-permute-start.7
  21.7 5.9 %collective-permute-done.4.refs_1_ = bf16[32,7168]{1,0:T(8,128)(2,1)S(1)} collective-permute-done((bf16[32,7168]{1,0:T(8,128)(2,1)S(1)}, bf16[32,7168]{1,0:T(8,128)(2,1)S(1)}, u32[]{:S(2)}, u32[]{:S(2)}) %collective-permute-start.4) | collective-permute-done | bytes 458784 | tf_op jit(solution)/shard_map/ppermute | solution.py:26
  27.6 1.1 %collective-permute-start.6 = (bf16[32,7168]{1,0:T(8,128)(2,1)S(1)}, bf16[32,7168]{1,0:T(8,128)(2,1)S(1)}, u32[]{:S(2)}, u32[]{:S(2)}) collective-permute-start(bf16[32,7168]{1,0:T(8,128)(2,1)S(1)} %collective-permute-done.4.refs_1_), channel_id=1, source_target_pairs={{0,2},{1,5},{2,0},{3,7},{4,6},{5,1},{6,4},{7,3},{8,10},{9,13},{10,... | collective-permute-start | bytes 1376264 | tf_op jit(solution)/shard_map/ppermute | solution.py:26
  28.7 0.9 %collective-permute-start.5 = (bf16[32,7168]{1,0:T(8,128)(2,1)S(1)}, bf16[32,7168]{1,0:T(8,128)(2,1)S(1)}, u32[]{:S(2)}, u32[]{:S(2)}) collective-permute-start(bf16[32,7168]{1,0:T(8,128)(2,1)S(1)} %constant_dynamic-update-slice_fusion.refs_0_), channel_id=1, source_target_pairs={{0,2},{1,5},{2,0},{3,7},{4,6},{5,1},{6,4},{7,3},{8,10},{9,13},{10,... | collective-permute-start | bytes 1376264 | tf_op jit(solution)/shard_map/ppermute | solution.py:26
  29.6 4.2 %shard_map.122 = (bf16[1,7168,256]{2,1,0:T(8,128)(2,1)S(1)}, bf16[1,7168,256]{2,1,0:T(8,128)(2,1)S(1)}, bf16[1,256,7168]{2,1,0:T(8,128)(2,1)S(1)}) custom-call(bf16[1,7168,256]{2,1,0:T(8,128)(2,1)} %refs_0_.2, bf16[1,7168,256]{2,1,0:T(8,128)(2,1)} %refs_1_.2, bf16[1,256,7168]{2,1,0:T(8,128)(2,1)} %refs_2_.2), custom_call_target="tpu_custom_call" | custom-call | bytes 22020096 | tf_op jit(solution)/shard_map/pallas_call | solution.py:127
  33.9 2.2 %collective-permute-done.6.refs_3_ = bf16[32,7168]{1,0:T(8,128)(2,1)S(1)} collective-permute-done((bf16[32,7168]{1,0:T(8,128)(2,1)S(1)}, bf16[32,7168]{1,0:T(8,128)(2,1)S(1)}, u32[]{:S(2)}, u32[]{:S(2)}) %collective-permute-start.6) | collective-permute-done | bytes 458784 | tf_op jit(solution)/shard_map/ppermute | solution.py:26
  36.1 0.7 collective-permute-start.13
  36.8 4.2 %collective-permute-done.5.refs_2_ = bf16[32,7168]{1,0:T(8,128)(2,1)S(1)} collective-permute-done((bf16[32,7168]{1,0:T(8,128)(2,1)S(1)}, bf16[32,7168]{1,0:T(8,128)(2,1)S(1)}, u32[]{:S(2)}, u32[]{:S(2)}) %collective-permute-start.5) | collective-permute-done | bytes 458784 | tf_op jit(solution)/shard_map/ppermute | solution.py:26
  41.0 0.5 collective-permute-start.11
  41.5 1.3 %collective-permute-done.10.refs_6_ = bf16[32,7168]{1,0:T(8,128)(2,1)S(1)} collective-permute-done((bf16[32,7168]{1,0:T(8,128)(2,1)S(1)}, bf16[32,7168]{1,0:T(8,128)(2,1)S(1)}, u32[]{:S(2)}, u32[]{:S(2)}) %collective-permute-start.10) | collective-permute-done | bytes 458784 | tf_op jit(solution)/shard_map/ppermute | solution.py:26
  42.8 0.7 collective-permute-done.11.refs_7_
  43.5 5.3 %shard_map.123 = (bf16[128,7168]{1,0:T(8,128)(2,1)S(1)}, bf16[64,7168]{1,0:T(8,128)(2,1)S(1)}, bf16[64,7168]{1,0:T(8,128)(2,1)S(1)}) custom-call(bf16[32,7168]{1,0:T(8,128)(2,1)S(1)} %constant_dynamic-update-slice_fusion.refs_0_, bf16[32,7168]{1,0:T(8,128)(2,1)S(1)} %collective-permute-done.4.refs_1_, bf16[32,7168]{1,0:T(8,128)(2,1)S(1)} %collective-permute-done.5.refs_2_, ...), custom_call_target="tpu_custom_call" | custom-call | flops 2818572288 | bytes 18350080 | tf_op jit(solution)/shard_map/pallas_call | solution.py:179
  48.9 2.6 %collective-permute-start.14 = (bf16[64,7168]{1,0:T(8,128)(2,1)S(1)}, bf16[64,7168]{1,0:T(8,128)(2,1)S(1)}, u32[]{:S(2)}, u32[]{:S(2)}) collective-permute-start(bf16[64,7168]{1,0:T(8,128)(2,1)S(1)} %get-tuple-element.62), channel_id=1, source_target_pairs={{0,1},{1,0},{2,3},{3,2},{4,5},{5,4},{6,7},{7,6},{8,9},{9,8},{10,11... | collective-permute-start | bytes 2752520 | tf_op jit(solution)/shard_map/ppermute | solution.py:26
  51.4 2.1 %collective-permute-done.14 = bf16[64,7168]{1,0:T(8,128)(2,1)S(1)} collective-permute-done((bf16[64,7168]{1,0:T(8,128)(2,1)S(1)}, bf16[64,7168]{1,0:T(8,128)(2,1)S(1)}, u32[]{:S(2)}, u32[]{:S(2)}) %collective-permute-start.14) | collective-permute-done | bytes 917536 | tf_op jit(solution)/shard_map/ppermute | solution.py:26
  53.6 2.0 %collective-permute-start.16 = (bf16[32,4480]{1,0:T(8,128)(2,1)S(1)}, bf16[32,4480]{1,0:T(8,128)(2,1)S(1)}, u32[]{:S(2)}, u32[]{:S(2)}) collective-permute-start(bf16[32,4480]{1,0:T(8,128)(2,1)S(1)} %add_convert_fusion.2), channel_id=1, source_target_pairs={{0,2},{1,5},{2,0},{3,7},{4,6},{5,1},{6,4},{7,3},{8,10},{9,13},{10,... | collective-permute-start | bytes 860168 | tf_op jit(solution)/shard_map/ppermute | solution.py:26
  55.7 4.6 %collective-permute-done.16 = bf16[32,4480]{1,0:T(8,128)(2,1)S(1)} collective-permute-done((bf16[32,4480]{1,0:T(8,128)(2,1)S(1)}, bf16[32,4480]{1,0:T(8,128)(2,1)S(1)}, u32[]{:S(2)}, u32[]{:S(2)}) %collective-permute-start.16) | collective-permute-done | bytes 286752 | tf_op jit(solution)/shard_map/ppermute | solution.py:26
  60.3 0.2 add_convert_fusion.1
  60.5 2.2 %collective-permute-start.17 = (bf16[32,4480]{1,0:T(8,128)(2,1)S(1)}, bf16[32,4480]{1,0:T(8,128)(2,1)S(1)}, u32[]{:S(2)}, u32[]{:S(2)}) collective-permute-start(bf16[32,4480]{1,0:T(8,128)(2,1)S(1)} %get-tuple-element.65), channel_id=1, source_target_pairs={{0,4},{1,3},{2,6},{3,1},{4,0},{5,7},{6,2},{7,5},{8,12},{9,11},{10,... | collective-permute-start | bytes 860168 | tf_op jit(solution)/shard_map/ppermute | solution.py:26
  62.7 2.0 %collective-permute-start.15 = (bf16[32,4480]{1,0:T(8,128)(2,1)S(1)}, bf16[32,4480]{1,0:T(8,128)(2,1)S(1)}, u32[]{:S(2)}, u32[]{:S(2)}) collective-permute-start(bf16[32,4480]{1,0:T(8,128)(2,1)S(1)} %get-tuple-element.94), channel_id=1, source_target_pairs={{0,2},{1,5},{2,0},{3,7},{4,6},{5,1},{6,4},{7,3},{8,10},{9,13},{10,... | collective-permute-start | bytes 860168 | tf_op jit(solution)/shard_map/ppermute | solution.py:26
  64.7 2.3 %shard_map.124 = bf16[8,64,512]{2,1,0:T(8,128)(2,1)} custom-call(s32[8]{0:T(128)S(1)} %copy-done.3, s32[8]{0:T(128)S(1)} %copy-done.4, bf16[8,64,576]{2,1,0:T(8,128)(2,1)S(1)} %copy-done.1, bf16[8,96,576]{2,1,0:T(8,128)(2,1)S(1)} %copy-done, bf16[8,96,576]{2,1,0:T(8,128)(2,1)S(1)} %collective-permute-done.9.refs_4_, bf16[8,576]{1,0:T(8,128)(2,1)S(1)} %copy-done.2, ...), custom_call_target="tpu_custom_call" | custom-call | flops 106954752 | bytes 4653056 | tf_op jit(solution)/shard_map/pallas_call | solution.py:99
  67.0 2.8 %collective-permute-done.17 = bf16[32,4480]{1,0:T(8,128)(2,1)S(1)} collective-permute-done((bf16[32,4480]{1,0:T(8,128)(2,1)S(1)}, bf16[32,4480]{1,0:T(8,128)(2,1)S(1)}, u32[]{:S(2)}, u32[]{:S(2)}) %collective-permute-start.17) | collective-permute-done | bytes 286752 | tf_op jit(solution)/shard_map/ppermute | solution.py:26
  69.9 0.1 convert_add_fusion
  70.0 2.4 %collective-permute-done.18 = bf16[32,2688]{1,0:T(8,128)(2,1)S(1)} collective-permute-done((bf16[32,2688]{1,0:T(8,128)(2,1)S(1)}, bf16[32,2688]{1,0:T(8,128)(2,1)S(1)}, u32[]{:S(2)}, u32[]{:S(2)}) %collective-permute-start.18) | collective-permute-done | bytes 172064 | tf_op jit(solution)/shard_map/ppermute | solution.py:26
  72.4 0.1 add_convert_fusion.3
  72.5 0.7 collective-permute-start.23
  73.2 1.7 %collective-permute-start.22 = (bf16[32,2688]{1,0:T(8,128)(2,1)S(1)}, bf16[32,2688]{1,0:T(8,128)(2,1)S(1)}, u32[]{:S(2)}, u32[]{:S(2)}) collective-permute-start(bf16[32,2688]{1,0:T(8,128)(2,1)S(1)} %get-tuple-element.92), channel_id=1, source_target_pairs={{0,2},{1,5},{2,0},{3,7},{4,6},{5,1},{6,4},{7,3},{8,10},{9,13},{10,... | collective-permute-start | bytes 516104 | tf_op jit(solution)/shard_map/ppermute | solution.py:26
  75.0 1.6 %collective-permute-start.19 = (bf16[8,4480]{1,0:T(8,128)(2,1)S(1)}, bf16[8,4480]{1,0:T(8,128)(2,1)S(1)}, u32[]{:S(2)}, u32[]{:S(2)}) collective-permute-start(bf16[8,4480]{1,0:T(8,128)(2,1)S(1)} %get-tuple-element.75), channel_id=1, source_target_pairs={{0,8},{1,9},{2,10},{3,11},{4,12},{5,13},{6,14},{7,15},{8,0},{9,1},... | collective-permute-start | bytes 215048 | tf_op jit(solution)/shard_map/ppermute | solution.py:26
  76.5 2.4 %collective-permute-start.20 = (bf16[8,4480]{1,0:T(8,128)(2,1)S(1)}, bf16[8,4480]{1,0:T(8,128)(2,1)S(1)}, u32[]{:S(2)}, u32[]{:S(2)}) collective-permute-start(bf16[8,4480]{1,0:T(8,128)(2,1)S(1)} %get-tuple-element.77), channel_id=1, source_target_pairs={{0,16},{1,17},{2,18},{3,19},{4,20},{5,21},{6,22},{7,23},{8,24},{9,... | collective-permute-start | bytes 215048 | tf_op jit(solution)/shard_map/ppermute | solution.py:26
  78.9 0.4 collective-permute-start.21
  79.4 0.1 add_convert_fusion.10
  79.5 2.2 %collective-permute-start.24 = (bf16[8,2688]{1,0:T(8,128)(2,1)S(1)}, bf16[8,2688]{1,0:T(8,128)(2,1)S(1)}, u32[]{:S(2)}, u32[]{:S(2)}) collective-permute-start(bf16[8,2688]{1,0:T(8,128)(2,1)S(1)} %get-tuple-element.89), channel_id=1, source_target_pairs={{0,8},{1,9},{2,10},{3,11},{4,12},{5,13},{6,14},{7,15},{8,0},{9,1},... | collective-permute-start | bytes 129032 | tf_op jit(solution)/shard_map/ppermute | solution.py:26
  81.7 2.5 %collective-permute-start.26 = (bf16[8,2688]{1,0:T(8,128)(2,1)S(1)}, bf16[8,2688]{1,0:T(8,128)(2,1)S(1)}, u32[]{:S(2)}, u32[]{:S(2)}) collective-permute-start(bf16[8,2688]{1,0:T(8,128)(2,1)S(1)} %get-tuple-element.90), channel_id=1, source_target_pairs={{0,24},{1,25},{2,26},{3,27},{4,28},{5,29},{6,30},{7,31},{8,16},{9,... | collective-permute-start | bytes 129032 | tf_op jit(solution)/shard_map/ppermute | solution.py:26
  84.2 0.1 collective-permute-start.25
  84.3 0.9 %collective-permute-done.21 = bf16[8,4480]{1,0:T(8,128)(2,1)S(1)} collective-permute-done((bf16[8,4480]{1,0:T(8,128)(2,1)S(1)}, bf16[8,4480]{1,0:T(8,128)(2,1)S(1)}, u32[]{:S(2)}, u32[]{:S(2)}) %collective-permute-start.21) | collective-permute-done | bytes 71712 | tf_op jit(solution)/shard_map/ppermute | solution.py:26
  85.3 0.1 add_convert_fusion.6
  85.4 2.3 %collective-permute-done.26 = bf16[8,2688]{1,0:T(8,128)(2,1)S(1)} collective-permute-done((bf16[8,2688]{1,0:T(8,128)(2,1)S(1)}, bf16[8,2688]{1,0:T(8,128)(2,1)S(1)}, u32[]{:S(2)}, u32[]{:S(2)}) %collective-permute-start.26) | collective-permute-done | bytes 43040 | tf_op jit(solution)/shard_map/ppermute | solution.py:26
  87.8 1.8 %collective-permute-done.25 = bf16[8,2688]{1,0:T(8,128)(2,1)S(1)} collective-permute-done((bf16[8,2688]{1,0:T(8,128)(2,1)S(1)}, bf16[8,2688]{1,0:T(8,128)(2,1)S(1)}, u32[]{:S(2)}, u32[]{:S(2)}) %collective-permute-start.25) | collective-permute-done | bytes 43040 | tf_op jit(solution)/shard_map/ppermute | solution.py:26
  89.6 0.1 add_convert_fusion.7
  89.7 0.7 pad_maximum_fusion
  (36 shorter events, 0.3 us)
Async XLA Ops:
  0.6 14.6 %collective-permute-start.3 = (bf16[8,96,576]{2,1,0:T(8,128)(2,1)}, bf16[8,96,576]{2,1,0:T(8,128)(2,1)S(1)}, u32[]{:S(2)}, u32[]{:S(2)}) collective-permute-start(bf16[8,96,576]{2,1,0:T(8,128)(2,1)} %refs_3_.1), channel_id=1, source_target_pairs={{1,2},{3,4},{5,6},{6,5},{9,10},{11,12},{13,14},{14,13},{17,18},{19... | collective-permute-start | bytes 2654216 | tf_op jit(solution)/shard_map/ppermute | solution.py:47
  1.4 9.7 %collective-permute-start.1 = (bf16[8,7168]{1,0:T(8,128)(2,1)}, bf16[8,7168]{1,0:T(8,128)(2,1)S(1)}, u32[]{:S(2)}, u32[]{:S(2)}) collective-permute-start(bf16[8,7168]{1,0:T(8,128)(2,1)} %param.16), channel_id=1, source_target_pairs={{0,16},{1,17},{2,18},{3,19},{4,20},{5,21},{6,22},{7,23},{8,24},{9,... | collective-permute-start | bytes 344072 | tf_op jit(solution)/shard_map/ppermute | solution.py:26
  5.5 6.5 %collective-permute-start = (bf16[8,7168]{1,0:T(8,128)(2,1)}, bf16[8,7168]{1,0:T(8,128)(2,1)S(1)}, u32[]{:S(2)}, u32[]{:S(2)}) collective-permute-start(bf16[8,7168]{1,0:T(8,128)(2,1)} %param.16), channel_id=1, source_target_pairs={{0,8},{1,9},{2,10},{3,11},{4,12},{5,13},{6,14},{7,15},{8,0},{9,1},... | collective-permute-start | bytes 344072 | tf_op jit(solution)/shard_map/ppermute | solution.py:26
  7.0 8.1 %collective-permute-start.2 = (bf16[8,7168]{1,0:T(8,128)(2,1)}, bf16[8,7168]{1,0:T(8,128)(2,1)S(1)}, u32[]{:S(2)}, u32[]{:S(2)}) collective-permute-start(bf16[8,7168]{1,0:T(8,128)(2,1)} %param.16), channel_id=1, source_target_pairs={{0,24},{1,25},{2,26},{3,27},{4,28},{5,29},{6,30},{7,31},{8,16},{9,... | collective-permute-start | bytes 344072 | tf_op jit(solution)/shard_map/ppermute | solution.py:26
  16.1 20.0 %copy-start = (bf16[8,96,576]{2,1,0:T(8,128)(2,1)S(1)}, bf16[8,96,576]{2,1,0:T(8,128)(2,1)}, u32[]{:S(2)}) copy-start(bf16[8,96,576]{2,1,0:T(8,128)(2,1)} %refs_3_.1) | copy-start | bytes 2654212
  16.2 11.5 %collective-permute-start.4 = (bf16[32,7168]{1,0:T(8,128)(2,1)S(1)}, bf16[32,7168]{1,0:T(8,128)(2,1)S(1)}, u32[]{:S(2)}, u32[]{:S(2)}) collective-permute-start(bf16[32,7168]{1,0:T(8,128)(2,1)S(1)} %constant_dynamic-update-slice_fusion.refs_0_), channel_id=1, source_target_pairs={{0,4},{1,3},{2,6},{3,1},{4,0},{5,7},{6,2},{7,5},{8,12},{9,11},{10,... | collective-permute-start | bytes 1376264 | tf_op jit(solution)/shard_map/ppermute | solution.py:26
  21.2 12.7 %collective-permute-start.9 = (bf16[8,96,576]{2,1,0:T(8,128)(2,1)}, bf16[8,96,576]{2,1,0:T(8,128)(2,1)S(1)}, u32[]{:S(2)}, u32[]{:S(2)}) collective-permute-start(bf16[8,96,576]{2,1,0:T(8,128)(2,1)} %refs_3_.1), channel_id=1, source_target_pairs={{0,1},{1,0},{2,3},{3,2},{4,5},{5,4},{6,7},{7,6},{8,9},{9,8},{10,11... | collective-permute-start | bytes 2654216 | tf_op jit(solution)/shard_map/ppermute | solution.py:26
  21.2 12.7 %collective-permute-start.7 = (bf16[32,7168]{1,0:T(8,128)(2,1)S(1)}, bf16[32,7168]{1,0:T(8,128)(2,1)S(1)}, u32[]{:S(2)}, u32[]{:S(2)}) collective-permute-start(bf16[32,7168]{1,0:T(8,128)(2,1)S(1)} %constant_dynamic-update-slice_fusion.refs_0_), channel_id=1, source_target_pairs={{0,1},{1,0},{2,3},{3,2},{4,5},{5,4},{6,7},{7,6},{8,9},{9,8},{10,11... | collective-permute-start | bytes 1376264 | tf_op jit(solution)/shard_map/ppermute | solution.py:26
  27.6 6.3 %collective-permute-start.8 = (bf16[32,7168]{1,0:T(8,128)(2,1)S(1)}, bf16[32,7168]{1,0:T(8,128)(2,1)S(1)}, u32[]{:S(2)}, u32[]{:S(2)}) collective-permute-start(bf16[32,7168]{1,0:T(8,128)(2,1)S(1)} %collective-permute-done.4.refs_1_), channel_id=1, source_target_pairs={{0,1},{1,0},{2,3},{3,2},{4,5},{5,4},{6,7},{7,6},{8,9},{9,8},{10,11... | collective-permute-start | bytes 1376264 | tf_op jit(solution)/shard_map/ppermute | solution.py:26
  27.6 8.5 %collective-permute-start.6 = (bf16[32,7168]{1,0:T(8,128)(2,1)S(1)}, bf16[32,7168]{1,0:T(8,128)(2,1)S(1)}, u32[]{:S(2)}, u32[]{:S(2)}) collective-permute-start(bf16[32,7168]{1,0:T(8,128)(2,1)S(1)} %collective-permute-done.4.refs_1_), channel_id=1, source_target_pairs={{0,2},{1,5},{2,0},{3,7},{4,6},{5,1},{6,4},{7,3},{8,10},{9,13},{10,... | collective-permute-start | bytes 1376264 | tf_op jit(solution)/shard_map/ppermute | solution.py:26
  28.7 12.3 %collective-permute-start.5 = (bf16[32,7168]{1,0:T(8,128)(2,1)S(1)}, bf16[32,7168]{1,0:T(8,128)(2,1)S(1)}, u32[]{:S(2)}, u32[]{:S(2)}) collective-permute-start(bf16[32,7168]{1,0:T(8,128)(2,1)S(1)} %constant_dynamic-update-slice_fusion.refs_0_), channel_id=1, source_target_pairs={{0,2},{1,5},{2,0},{3,7},{4,6},{5,1},{6,4},{7,3},{8,10},{9,13},{10,... | collective-permute-start | bytes 1376264 | tf_op jit(solution)/shard_map/ppermute | solution.py:26
  36.1 12.7 %collective-permute-start.13 = (bf16[8,96,576]{2,1,0:T(8,128)(2,1)S(1)}, bf16[8,96,576]{2,1,0:T(8,128)(2,1)S(1)}, u32[]{:S(2)}, u32[]{:S(2)}) collective-permute-start(bf16[8,96,576]{2,1,0:T(8,128)(2,1)S(1)} %copy-done), channel_id=1, source_target_pairs={{2,1},{4,3},{7,8},{8,7},{10,9},{12,11},{15,16},{16,15},{18,17},{20... | collective-permute-start | bytes 2654216 | tf_op jit(solution)/shard_map/ppermute | solution.py:47
  41.0 1.8 %collective-permute-start.10 = (bf16[32,7168]{1,0:T(8,128)(2,1)S(1)}, bf16[32,7168]{1,0:T(8,128)(2,1)S(1)}, u32[]{:S(2)}, u32[]{:S(2)}) collective-permute-start(bf16[32,7168]{1,0:T(8,128)(2,1)S(1)} %collective-permute-done.5.refs_2_), channel_id=1, source_target_pairs={{0,1},{1,0},{2,3},{3,2},{4,5},{5,4},{6,7},{7,6},{8,9},{9,8},{10,11... | collective-permute-start | bytes 1376264 | tf_op jit(solution)/shard_map/ppermute | solution.py:26
  41.0 2.5 %collective-permute-start.11 = (bf16[32,7168]{1,0:T(8,128)(2,1)S(1)}, bf16[32,7168]{1,0:T(8,128)(2,1)S(1)}, u32[]{:S(2)}, u32[]{:S(2)}) collective-permute-start(bf16[32,7168]{1,0:T(8,128)(2,1)S(1)} %collective-permute-done.6.refs_3_), channel_id=1, source_target_pairs={{0,1},{1,0},{2,3},{3,2},{4,5},{5,4},{6,7},{7,6},{8,9},{9,8},{10,11... | collective-permute-start | bytes 1376264 | tf_op jit(solution)/shard_map/ppermute | solution.py:26
  48.8 15.9 %copy-start.1 = (bf16[8,64,576]{2,1,0:T(8,128)(2,1)S(1)}, bf16[8,64,576]{2,1,0:T(8,128)(2,1)}, u32[]{:S(2)}) copy-start(bf16[8,64,576]{2,1,0:T(8,128)(2,1)} %refs_2_.3) | copy-start | bytes 1769476
  48.8 15.9 %copy-start.2 = (bf16[8,576]{1,0:T(8,128)(2,1)S(1)}, bf16[8,576]{1,0:T(8,128)(2,1)}, u32[]{:S(2)}) copy-start(bf16[8,576]{1,0:T(8,128)(2,1)} %refs_5_.1) | copy-start | bytes 27652
  48.8 15.9 %copy-start.3 = (s32[8]{0:T(128)S(1)}, s32[8]{0:T(128)}, u32[]{:S(2)}) copy-start(s32[8]{0:T(128)} %refs_0_.3) | copy-start | bytes 100
  48.8 15.9 %copy-start.4 = (s32[8]{0:T(128)S(1)}, s32[8]{0:T(128)}, u32[]{:S(2)}) copy-start(s32[8]{0:T(128)} %refs_1_.3) | copy-start | bytes 100
  48.9 4.7 %collective-permute-start.14 = (bf16[64,7168]{1,0:T(8,128)(2,1)S(1)}, bf16[64,7168]{1,0:T(8,128)(2,1)S(1)}, u32[]{:S(2)}, u32[]{:S(2)}) collective-permute-start(bf16[64,7168]{1,0:T(8,128)(2,1)S(1)} %get-tuple-element.62), channel_id=1, source_target_pairs={{0,1},{1,0},{2,3},{3,2},{4,5},{5,4},{6,7},{7,6},{8,9},{9,8},{10,11... | collective-permute-start | bytes 2752520 | tf_op jit(solution)/shard_map/ppermute | solution.py:26
  51.4 4.3 %collective-permute-start.12 = (bf16[64,7168]{1,0:T(8,128)(2,1)S(1)}, bf16[64,7168]{1,0:T(8,128)(2,1)S(1)}, u32[]{:S(2)}, u32[]{:S(2)}) collective-permute-start(bf16[64,7168]{1,0:T(8,128)(2,1)S(1)} %get-tuple-element.59), channel_id=1, source_target_pairs={{0,1},{1,0},{2,3},{3,2},{4,5},{5,4},{6,7},{7,6},{8,9},{9,8},{10,11... | collective-permute-start | bytes 2752520 | tf_op jit(solution)/shard_map/ppermute | solution.py:26
  53.6 6.7 %collective-permute-start.16 = (bf16[32,4480]{1,0:T(8,128)(2,1)S(1)}, bf16[32,4480]{1,0:T(8,128)(2,1)S(1)}, u32[]{:S(2)}, u32[]{:S(2)}) collective-permute-start(bf16[32,4480]{1,0:T(8,128)(2,1)S(1)} %add_convert_fusion.2), channel_id=1, source_target_pairs={{0,2},{1,5},{2,0},{3,7},{4,6},{5,1},{6,4},{7,3},{8,10},{9,13},{10,... | collective-permute-start | bytes 860168 | tf_op jit(solution)/shard_map/ppermute | solution.py:26
  60.5 9.4 %collective-permute-start.17 = (bf16[32,4480]{1,0:T(8,128)(2,1)S(1)}, bf16[32,4480]{1,0:T(8,128)(2,1)S(1)}, u32[]{:S(2)}, u32[]{:S(2)}) collective-permute-start(bf16[32,4480]{1,0:T(8,128)(2,1)S(1)} %get-tuple-element.65), channel_id=1, source_target_pairs={{0,4},{1,3},{2,6},{3,1},{4,0},{5,7},{6,2},{7,5},{8,12},{9,11},{10,... | collective-permute-start | bytes 860168 | tf_op jit(solution)/shard_map/ppermute | solution.py:26
  62.7 7.2 %collective-permute-start.15 = (bf16[32,4480]{1,0:T(8,128)(2,1)S(1)}, bf16[32,4480]{1,0:T(8,128)(2,1)S(1)}, u32[]{:S(2)}, u32[]{:S(2)}) collective-permute-start(bf16[32,4480]{1,0:T(8,128)(2,1)S(1)} %get-tuple-element.94), channel_id=1, source_target_pairs={{0,2},{1,5},{2,0},{3,7},{4,6},{5,1},{6,4},{7,3},{8,10},{9,13},{10,... | collective-permute-start | bytes 860168 | tf_op jit(solution)/shard_map/ppermute | solution.py:26
  67.0 5.4 %collective-permute-start.18 = (bf16[32,2688]{1,0:T(8,128)(2,1)S(1)}, bf16[32,2688]{1,0:T(8,128)(2,1)S(1)}, u32[]{:S(2)}, u32[]{:S(2)}) collective-permute-start(bf16[32,2688]{1,0:T(8,128)(2,1)S(1)} %add_convert_fusion.5), channel_id=1, source_target_pairs={{0,2},{1,5},{2,0},{3,7},{4,6},{5,1},{6,4},{7,3},{8,10},{9,13},{10,... | collective-permute-start | bytes 516104 | tf_op jit(solution)/shard_map/ppermute | solution.py:26
  72.5 6.9 %collective-permute-start.23 = (bf16[32,2688]{1,0:T(8,128)(2,1)S(1)}, bf16[32,2688]{1,0:T(8,128)(2,1)S(1)}, u32[]{:S(2)}, u32[]{:S(2)}) collective-permute-start(bf16[32,2688]{1,0:T(8,128)(2,1)S(1)} %get-tuple-element.81), channel_id=1, source_target_pairs={{0,4},{1,3},{2,6},{3,1},{4,0},{5,7},{6,2},{7,5},{8,12},{9,11},{10,... | collective-permute-start | bytes 516104 | tf_op jit(solution)/shard_map/ppermute | solution.py:26
  73.2 6.2 %collective-permute-start.22 = (bf16[32,2688]{1,0:T(8,128)(2,1)S(1)}, bf16[32,2688]{1,0:T(8,128)(2,1)S(1)}, u32[]{:S(2)}, u32[]{:S(2)}) collective-permute-start(bf16[32,2688]{1,0:T(8,128)(2,1)S(1)} %get-tuple-element.92), channel_id=1, source_target_pairs={{0,2},{1,5},{2,0},{3,7},{4,6},{5,1},{6,4},{7,3},{8,10},{9,13},{10,... | collective-permute-start | bytes 516104 | tf_op jit(solution)/shard_map/ppermute | solution.py:26
  75.0 9.2 %collective-permute-start.19 = (bf16[8,4480]{1,0:T(8,128)(2,1)S(1)}, bf16[8,4480]{1,0:T(8,128)(2,1)S(1)}, u32[]{:S(2)}, u32[]{:S(2)}) collective-permute-start(bf16[8,4480]{1,0:T(8,128)(2,1)S(1)} %get-tuple-element.75), channel_id=1, source_target_pairs={{0,8},{1,9},{2,10},{3,11},{4,12},{5,13},{6,14},{7,15},{8,0},{9,1},... | collective-permute-start | bytes 215048 | tf_op jit(solution)/shard_map/ppermute | solution.py:26
  76.5 7.8 %collective-permute-start.20 = (bf16[8,4480]{1,0:T(8,128)(2,1)S(1)}, bf16[8,4480]{1,0:T(8,128)(2,1)S(1)}, u32[]{:S(2)}, u32[]{:S(2)}) collective-permute-start(bf16[8,4480]{1,0:T(8,128)(2,1)S(1)} %get-tuple-element.77), channel_id=1, source_target_pairs={{0,16},{1,17},{2,18},{3,19},{4,20},{5,21},{6,22},{7,23},{8,24},{9,... | collective-permute-start | bytes 215048 | tf_op jit(solution)/shard_map/ppermute | solution.py:26
  78.9 6.3 %collective-permute-start.21 = (bf16[8,4480]{1,0:T(8,128)(2,1)S(1)}, bf16[8,4480]{1,0:T(8,128)(2,1)S(1)}, u32[]{:S(2)}, u32[]{:S(2)}) collective-permute-start(bf16[8,4480]{1,0:T(8,128)(2,1)S(1)} %get-tuple-element.79), channel_id=1, source_target_pairs={{0,24},{1,25},{2,26},{3,27},{4,28},{5,29},{6,30},{7,31},{8,16},{9,... | collective-permute-start | bytes 215048 | tf_op jit(solution)/shard_map/ppermute | solution.py:26
  79.5 5.9 %collective-permute-start.24 = (bf16[8,2688]{1,0:T(8,128)(2,1)S(1)}, bf16[8,2688]{1,0:T(8,128)(2,1)S(1)}, u32[]{:S(2)}, u32[]{:S(2)}) collective-permute-start(bf16[8,2688]{1,0:T(8,128)(2,1)S(1)} %get-tuple-element.89), channel_id=1, source_target_pairs={{0,8},{1,9},{2,10},{3,11},{4,12},{5,13},{6,14},{7,15},{8,0},{9,1},... | collective-permute-start | bytes 129032 | tf_op jit(solution)/shard_map/ppermute | solution.py:26
  81.7 6.0 %collective-permute-start.26 = (bf16[8,2688]{1,0:T(8,128)(2,1)S(1)}, bf16[8,2688]{1,0:T(8,128)(2,1)S(1)}, u32[]{:S(2)}, u32[]{:S(2)}) collective-permute-start(bf16[8,2688]{1,0:T(8,128)(2,1)S(1)} %get-tuple-element.90), channel_id=1, source_target_pairs={{0,24},{1,25},{2,26},{3,27},{4,28},{5,29},{6,30},{7,31},{8,16},{9,... | collective-permute-start | bytes 129032 | tf_op jit(solution)/shard_map/ppermute | solution.py:26
  84.2 5.4 %collective-permute-start.25 = (bf16[8,2688]{1,0:T(8,128)(2,1)S(1)}, bf16[8,2688]{1,0:T(8,128)(2,1)S(1)}, u32[]{:S(2)}, u32[]{:S(2)}) collective-permute-start(bf16[8,2688]{1,0:T(8,128)(2,1)S(1)} %get-tuple-element.91), channel_id=1, source_target_pairs={{0,16},{1,17},{2,18},{3,19},{4,20},{5,21},{6,22},{7,23},{8,24},{9,... | collective-permute-start | bytes 129032 | tf_op jit(solution)/shard_map/ppermute | solution.py:26

commit v13 on v12

--- a/solution.py
+++ b/solution.py
@@ -141,7 +141,7 @@
 
 def expert_kernel(wide, *refs):
     rows, refs = refs[:8], refs[8:]
-    gate, up, down, own, high, low, gate_sum, up_sum = refs
+    gate, up, down, own, low, far_side, far_across, gate_sum, up_sum = refs
     height, width = rows[0].shape
     half = 4 * height
 
@@ -166,7 +166,8 @@
         product = product.astype(jnp.bfloat16)
         own[:, span(k)] = product[:half]
         low[:, span(k)] = product[half : half + 2 * height]
-        high[:, span(k)] = product[half + 2 * height :]
+        far_side[:, span(k)] = product[half + 2 * height : half + 3 * height]
+        far_across[:, span(k)] = product[half + 3 * height :]
 
 
 def experts(rows, weights):
@@ -179,8 +180,8 @@
     return pl.pallas_call(
         lambda *refs: expert_kernel(wide, *refs),
         in_specs=[whole] * len(inputs),
-        out_specs=[whole] * 3,
-        out_shape=[pltpu.VMEM((count * height, width), jnp.bfloat16) for count in (4, 2, 2)],
+        out_specs=[whole] * 4,
+        out_shape=[pltpu.VMEM((count * height, width), jnp.bfloat16) for count in (4, 2, 1, 1)],
         scratch_shapes=[
             pltpu.VMEM((total, units), jnp.float32),
             pltpu.VMEM((total, units), jnp.float32),
@@ -258,9 +259,13 @@
 
     column = blocks[:1] + [swapped(blocks[r], ahead(r)) for r in range(1, expert_count)]
     early, _ = cache_rows("early", 0, beam_count)
-    column, early, mixing = tied(column, early, mixing)
+    height = expert_count * capacity
+    rows = jnp.pad(column[0], ((0, height - capacity), (0, 0)))
+    rows, column, early, mixing = tied(rows, column, early, mixing)
     pieces.append(early)
-    column = jnp.concatenate(column)
+    for r in range(1, expert_count):
+        rows = lax.dynamic_update_slice(rows, column[r], (r * capacity, 0))
+    column = rows
     near = swapped(column, first)
     again, near = tied(column, near)
     across = swapped(near, second)
@@ -274,11 +279,12 @@
     late, across = cache_rows("late", 0, beam_count, across)
     held = [column, near, side, across, twin_column, twin_near]
     held = held + [swapped(side, twin), swapped(across, twin)]
-    own, high, low = experts(held, weights)
-    high, late = tied(high, late)
+    own, low, far_side, far_across = experts(held, weights)
+    far_across, late = tied(far_across, late)
     pieces.append(late)
 
-    high, low = swapped(high, twin), swapped(low, twin)
+    far_across, far_side = swapped(far_across, twin), swapped(far_side, twin)
+    low = swapped(low, twin)
     height = expert_count * capacity
 
     cut = 128 * (5 * width // 1024)
@@ -288,13 +294,13 @@
         return value[j * height : (j + 1) * height, half[0] : half[1]]
 
     def to_second(half):
-        return added([block(own, 3, half), block(high, 1, half)]).astype(jnp.bfloat16)
+        return added([block(own, 3, half), block(far_across, 0, half)]).astype(jnp.bfloat16)
 
     def to_first(half, across):
         return added([block(own, 1, half), block(low, 1, half), across]).astype(jnp.bfloat16)
 
     def to_side(half):
-        return added([block(own, 2, half), block(high, 0, half)]).astype(jnp.bfloat16)
+        return added([block(own, 2, half), block(far_side, 0, half)]).astype(jnp.bfloat16)
 
     def shares(half, side, near):
         here = [block(own, 0, half), block(low, 0, half), side, near]
@@ -308,19 +314,19 @@
             swapped(share[r].astype(jnp.bfloat16), ahead(r)) for r in range(1, expert_count)
         ]
 
-    across, high = tied(to_second(halves[0]), high)
+    across, pieces[1] = tied(to_second(halves[0]), pieces[1])
     across = swapped(across, second)
+    attention = attend(
+        queries, latent_cache, beside, new_latent, spans, pieces, parents, lengths
+    )
+    across, attention = tied(across, attention)
     near, side = to_first(halves[0], across), to_side(halves[0])
     near, across = tied(near, to_second(halves[1]))
     near, side, across = swapped(near, first), swapped(side, second), swapped(across, second)
     share = shares(halves[0], side, near)
-    share, across, high = tied(share, across, high)
+    share, across, far_side = tied(share, across, far_side)
     values = [[share[0]] + back(share)]
     near, side = to_first(halves[1], across), to_side(halves[1])
-    attention = attend(
-        queries, latent_cache, beside, new_latent, spans, pieces, parents, lengths
-    )
-    near, attention = tied(near, attention)
     near, side = swapped(near, first), swapped(side, second)
     share = shares(halves[1], side, near)
     values.append([share[0]] + back(share))

time: 90.6 us -> 88.7 us (0.979)
  waiting for transfers between devices: 35.6 us -> 32.1 us
  starting transfers between devices: 35.7 us -> 37.4 us
    ppermute x25 -> x26, waiting for transfers between devices: 35.5 us -> 32 us  [swapped(): return lax.ppermute(value, 'dp', [(i, partner(i)) for i in range(peers)])]
    ppermute x25 -> x26, starting transfers between devices: 34.2 us -> 35.9 us  [swapped(): return lax.ppermute(value, 'dp', [(i, partner(i)) for i in range(peers)])]
    unnamed x13 -> x10, local copies, waits for them, and re-layouts: 0.96 us -> 0.02 us
    pad x0 -> x1, local copies, waits for them, and re-layouts: none -> 0.93 us  [body(): rows = jnp.pad(column[0], ((0, height - capacity), (0, 0)))]
  transfers between devices with their start and end apart: 27 -> 28, of which waited for: 15 -> 15; matrix products, arithmetic and copies ran while one was open for 5% -> 6% of each run, Pallas kernels for 13% -> 13%
where the time goes in v13:
time: 88.7 us; the launch traced here: 88.5 us
  starting transfers between devices  37.4 us (42%)
  waiting for transfers between devices  32.1 us (36%)
  Pallas kernels  11.8 us (13%)
  other arithmetic  4.76 us (5%)
  local copies, waits for them, and re-layouts  1.59 us (2%)
    ppermute x26, starting transfers between devices, swapped(): return lax.ppermute(value, 'dp', [(i, partner(i)) for i in range(peers)])  35.9 us
    ppermute x26, waiting for transfers between devices, swapped(): return lax.ppermute(value, 'dp', [(i, partner(i)) for i in range(peers)])  32 us
    pallas_call x1, Pallas kernels, experts(): pl.pallas_call(lambda *refs: expert_kernel(wide, *refs), in_specs=[whole]...  5.3 us
    pallas_call x1, Pallas kernels, fetched(): pl.pallas_call(fetch_kernel, in_specs=[pl.BlockSpec(memory_space=pltpu.HB...  4.23 us
    reduce_sum x1, other arithmetic, body(): jnp.sum(jnp.where(routed_experts == targets[r], route_weights, 0.0), axis=1)  3.26 us
    pallas_call x1, Pallas kernels, attend(): pl.pallas_call(lambda *refs: attend_kernel(spans, *refs), in_specs=[scala...  2.3 us
  transfers between devices with their start and end apart: 28, of which 15 were waited for; matrix products, arithmetic and copies ran while one was open for 6% of the time, Pallas kernels for 13%

profile of v13, /device:TPU:0, one launch (start us, length us, event | category | flops | bytes accessed | tf_op | source)
XLA Modules:
  0.0 88.5 jit_solution(12627613494981868442)
XLA Ops:
  0.6 0.7 collective-permute-start.3
  1.4 4.1 %collective-permute-start.1 = (bf16[8,7168]{1,0:T(8,128)(2,1)}, bf16[8,7168]{1,0:T(8,128)(2,1)S(1)}, u32[]{:S(2)}, u32[]{:S(2)}) collective-permute-start(bf16[8,7168]{1,0:T(8,128)(2,1)} %param.16), channel_id=1, source_target_pairs={{0,16},{1,17},{2,18},{3,19},{4,20},{5,21},{6,22},{7,23},{8,24},{9,... | collective-permute-start | bytes 344072 | tf_op jit(solution)/shard_map/ppermute | solution.py:26
  5.5 1.6 %collective-permute-start = (bf16[8,7168]{1,0:T(8,128)(2,1)}, bf16[8,7168]{1,0:T(8,128)(2,1)S(1)}, u32[]{:S(2)}, u32[]{:S(2)}) collective-permute-start(bf16[8,7168]{1,0:T(8,128)(2,1)} %param.16), channel_id=1, source_target_pairs={{0,8},{1,9},{2,10},{3,11},{4,12},{5,13},{6,14},{7,15},{8,0},{9,1},... | collective-permute-start | bytes 344072 | tf_op jit(solution)/shard_map/ppermute | solution.py:26
  7.0 0.6 fusion.4
  7.7 0.9 %pad.4 = bf16[32,7168]{1,0:T(8,128)(2,1)S(1)} pad(bf16[8,7168]{1,0:T(8,128)(2,1)} %param.16, bf16[]{:T(256)} %constant.19.clone.1), padding=0_24x0_0 | pad | bytes 573442 | tf_op jit(solution)/shard_map/jit(_pad)/pad | solution.py:263
  8.6 3.3 %fusion.3 = (f32[8]{0:T(128)S(1)}, f32[8]{0:T(128)S(1)}, f32[8]{0:T(128)S(1)}, f32[8]{0:T(128)S(1)}) fusion(f32[8,2]{0,1:T(2,128)} %param.18, s32[8,2]{0,1:T(2,128)} %param.17, s32[]{:T(128)} %bitcast.3, s32[]{:T(128)} %bitcast.1, s32[]{:T(128)} %bitcast, s32[]{:T(128)} %bitcast.2), kind=kLoop, calls=%fused_computation.23 | loop fusion | flops 160 | bytes 272 | tf_op jit(solution)/shard_map/reduce_sum | solution.py:226
  11.9 0.1 collective-permute-done
  12.0 3.2 %collective-permute-done.2 = bf16[8,7168]{1,0:T(8,128)(2,1)S(1)} collective-permute-done((bf16[8,7168]{1,0:T(8,128)(2,1)}, bf16[8,7168]{1,0:T(8,128)(2,1)S(1)}, u32[]{:S(2)}, u32[]{:S(2)}) %collective-permute-start.2) | collective-permute-done | bytes 114720 | tf_op jit(solution)/shard_map/ppermute | solution.py:26
  15.2 5.0 %collective-permute-start.4 = (bf16[32,7168]{1,0:T(8,128)(2,1)S(1)}, bf16[32,7168]{1,0:T(8,128)(2,1)S(1)}, u32[]{:S(2)}, u32[]{:S(2)}) collective-permute-start(bf16[32,7168]{1,0:T(8,128)(2,1)S(1)} %constant_dynamic-update-slice_fusion.refs_0_), channel_id=1, source_target_pairs={{0,4},{1,3},{2,6},{3,1},{4,0},{5,7},{6,2},{7,5},{8,12},{9,11},{10,... | collective-permute-start | bytes 1376264 | tf_op jit(solution)/shard_map/ppermute | solution.py:26
  20.3 0.5 collective-permute-start.7
  20.8 5.9 %collective-permute-done.4.refs_1_ = bf16[32,7168]{1,0:T(8,128)(2,1)S(1)} collective-permute-done((bf16[32,7168]{1,0:T(8,128)(2,1)S(1)}, bf16[32,7168]{1,0:T(8,128)(2,1)S(1)}, u32[]{:S(2)}, u32[]{:S(2)}) %collective-permute-start.4) | collective-permute-done | bytes 458784 | tf_op jit(solution)/shard_map/ppermute | solution.py:26
  26.7 1.1 %collective-permute-start.6 = (bf16[32,7168]{1,0:T(8,128)(2,1)S(1)}, bf16[32,7168]{1,0:T(8,128)(2,1)S(1)}, u32[]{:S(2)}, u32[]{:S(2)}) collective-permute-start(bf16[32,7168]{1,0:T(8,128)(2,1)S(1)} %collective-permute-done.4.refs_1_), channel_id=1, source_target_pairs={{0,2},{1,5},{2,0},{3,7},{4,6},{5,1},{6,4},{7,3},{8,10},{9,13},{10,... | collective-permute-start | bytes 1376264 | tf_op jit(solution)/shard_map/ppermute | solution.py:26
  27.8 0.9 %collective-permute-start.5 = (bf16[32,7168]{1,0:T(8,128)(2,1)S(1)}, bf16[32,7168]{1,0:T(8,128)(2,1)S(1)}, u32[]{:S(2)}, u32[]{:S(2)}) collective-permute-start(bf16[32,7168]{1,0:T(8,128)(2,1)S(1)} %constant_dynamic-update-slice_fusion.refs_0_), channel_id=1, source_target_pairs={{0,2},{1,5},{2,0},{3,7},{4,6},{5,1},{6,4},{7,3},{8,10},{9,13},{10,... | collective-permute-start | bytes 1376264 | tf_op jit(solution)/shard_map/ppermute | solution.py:26
  28.7 4.2 %shard_map.122 = (bf16[1,7168,256]{2,1,0:T(8,128)(2,1)S(1)}, bf16[1,7168,256]{2,1,0:T(8,128)(2,1)S(1)}, bf16[1,256,7168]{2,1,0:T(8,128)(2,1)S(1)}) custom-call(bf16[1,7168,256]{2,1,0:T(8,128)(2,1)} %refs_0_.2, bf16[1,7168,256]{2,1,0:T(8,128)(2,1)} %refs_1_.2, bf16[1,256,7168]{2,1,0:T(8,128)(2,1)} %refs_2_.2), custom_call_target="tpu_custom_call" | custom-call | bytes 22020096 | tf_op jit(solution)/shard_map/pallas_call | solution.py:127
  33.0 2.2 %collective-permute-done.6.refs_3_ = bf16[32,7168]{1,0:T(8,128)(2,1)S(1)} collective-permute-done((bf16[32,7168]{1,0:T(8,128)(2,1)S(1)}, bf16[32,7168]{1,0:T(8,128)(2,1)S(1)}, u32[]{:S(2)}, u32[]{:S(2)}) %collective-permute-start.6) | collective-permute-done | bytes 458784 | tf_op jit(solution)/shard_map/ppermute | solution.py:26
  35.2 0.9 collective-permute-start.12
  36.1 4.0 %collective-permute-done.5.refs_2_ = bf16[32,7168]{1,0:T(8,128)(2,1)S(1)} collective-permute-done((bf16[32,7168]{1,0:T(8,128)(2,1)S(1)}, bf16[32,7168]{1,0:T(8,128)(2,1)S(1)}, u32[]{:S(2)}, u32[]{:S(2)}) %collective-permute-start.5) | collective-permute-done | bytes 458784 | tf_op jit(solution)/shard_map/ppermute | solution.py:26
  40.1 0.5 collective-permute-start.11
  40.6 1.3 %collective-permute-done.10.refs_6_ = bf16[32,7168]{1,0:T(8,128)(2,1)S(1)} collective-permute-done((bf16[32,7168]{1,0:T(8,128)(2,1)S(1)}, bf16[32,7168]{1,0:T(8,128)(2,1)S(1)}, u32[]{:S(2)}, u32[]{:S(2)}) %collective-permute-start.10) | collective-permute-done | bytes 458784 | tf_op jit(solution)/shard_map/ppermute | solution.py:26
  41.9 0.7 collective-permute-done.11.refs_7_
  42.6 5.3 %shard_map.123 = (bf16[128,7168]{1,0:T(8,128)(2,1)S(1)}, bf16[64,7168]{1,0:T(8,128)(2,1)S(1)}, bf16[32,7168]{1,0:T(8,128)(2,1)S(1)}, bf16[32,7168]{1,0:T(8,128)(2,1)S(1)}) custom-call(bf16[32,7168]{1,0:T(8,128)(2,1)S(1)} %constant_dynamic-update-slice_fusion.refs_0_, bf16[32,7168]{1,0:T(8,128)(2,1)S(1)} %collective-permute-done.4.refs_1_, ...), custom_call_target="tpu_custom_call" | custom-call | flops 2818572288 | bytes 18350080 | tf_op jit(solution)/shard_map/pallas_call | solution.py:180
  47.9 2.8 %collective-permute-start.13 = (bf16[32,7168]{1,0:T(8,128)(2,1)S(1)}, bf16[32,7168]{1,0:T(8,128)(2,1)S(1)}, u32[]{:S(2)}, u32[]{:S(2)}) collective-permute-start(bf16[32,7168]{1,0:T(8,128)(2,1)S(1)} %get-tuple-element.62), channel_id=1, source_target_pairs={{0,1},{1,0},{2,3},{3,2},{4,5},{5,4},{6,7},{7,6},{8,9},{9,8},{10,11... | collective-permute-start | bytes 1376264 | tf_op jit(solution)/shard_map/ppermute | solution.py:26
  50.7 0.5 collective-permute-start.15
  51.2 0.9 %collective-permute-done.13 = bf16[32,7168]{1,0:T(8,128)(2,1)S(1)} collective-permute-done((bf16[32,7168]{1,0:T(8,128)(2,1)S(1)}, bf16[32,7168]{1,0:T(8,128)(2,1)S(1)}, u32[]{:S(2)}, u32[]{:S(2)}) %collective-permute-start.13) | collective-permute-done | bytes 458784 | tf_op jit(solution)/shard_map/ppermute | solution.py:26
  52.2 1.9 %collective-permute-start.14 = (bf16[32,4480]{1,0:T(8,128)(2,1)S(1)}, bf16[32,4480]{1,0:T(8,128)(2,1)S(1)}, u32[]{:S(2)}, u32[]{:S(2)}) collective-permute-start(bf16[32,4480]{1,0:T(8,128)(2,1)S(1)} %add_convert_fusion.2), channel_id=1, source_target_pairs={{0,2},{1,5},{2,0},{3,7},{4,6},{5,1},{6,4},{7,3},{8,10},{9,13},{10,... | collective-permute-start | bytes 860168 | tf_op jit(solution)/shard_map/ppermute | solution.py:26
  54.2 2.3 %shard_map.124 = bf16[8,64,512]{2,1,0:T(8,128)(2,1)} custom-call(s32[8]{0:T(128)S(1)} %copy-done.3, s32[8]{0:T(128)S(1)} %copy-done.4, bf16[8,64,576]{2,1,0:T(8,128)(2,1)S(1)} %copy-done.1, bf16[8,96,576]{2,1,0:T(8,128)(2,1)S(1)} %copy-done, bf16[8,96,576]{2,1,0:T(8,128)(2,1)S(1)} %collective-permute-done.9.refs_4_, bf16[8,576]{1,0:T(8,128)(2,1)S(1)} %copy-done.2, ...), custom_call_target="tpu_custom_call" | custom-call | flops 106954752 | bytes 4653056 | tf_op jit(solution)/shard_map/pallas_call | solution.py:99
  56.5 2.4 %collective-permute-done.14 = bf16[32,4480]{1,0:T(8,128)(2,1)S(1)} collective-permute-done((bf16[32,4480]{1,0:T(8,128)(2,1)S(1)}, bf16[32,4480]{1,0:T(8,128)(2,1)S(1)}, u32[]{:S(2)}, u32[]{:S(2)}) %collective-permute-start.14) | collective-permute-done | bytes 286752 | tf_op jit(solution)/shard_map/ppermute | solution.py:26
  58.9 0.2 add_convert_fusion.1
  59.1 2.2 %collective-permute-start.18 = (bf16[32,4480]{1,0:T(8,128)(2,1)S(1)}, bf16[32,4480]{1,0:T(8,128)(2,1)S(1)}, u32[]{:S(2)}, u32[]{:S(2)}) collective-permute-start(bf16[32,4480]{1,0:T(8,128)(2,1)S(1)} %get-tuple-element.73), channel_id=1, source_target_pairs={{0,4},{1,3},{2,6},{3,1},{4,0},{5,7},{6,2},{7,5},{8,12},{9,11},{10,... | collective-permute-start | bytes 860168 | tf_op jit(solution)/shard_map/ppermute | solution.py:26
  61.3 2.0 %collective-permute-start.17 = (bf16[32,4480]{1,0:T(8,128)(2,1)S(1)}, bf16[32,4480]{1,0:T(8,128)(2,1)S(1)}, u32[]{:S(2)}, u32[]{:S(2)}) collective-permute-start(bf16[32,4480]{1,0:T(8,128)(2,1)S(1)} %get-tuple-element.96), channel_id=1, source_target_pairs={{0,2},{1,5},{2,0},{3,7},{4,6},{5,1},{6,4},{7,3},{8,10},{9,13},{10,... | collective-permute-start | bytes 860168 | tf_op jit(solution)/shard_map/ppermute | solution.py:26
  63.3 5.1 %collective-permute-done.18 = bf16[32,4480]{1,0:T(8,128)(2,1)S(1)} collective-permute-done((bf16[32,4480]{1,0:T(8,128)(2,1)S(1)}, bf16[32,4480]{1,0:T(8,128)(2,1)S(1)}, u32[]{:S(2)}, u32[]{:S(2)}) %collective-permute-start.18) | collective-permute-done | bytes 286752 | tf_op jit(solution)/shard_map/ppermute | solution.py:26
  68.5 0.1 convert_add_fusion
  68.6 1.3 %collective-permute-done.19 = bf16[32,2688]{1,0:T(8,128)(2,1)S(1)} collective-permute-done((bf16[32,2688]{1,0:T(8,128)(2,1)S(1)}, bf16[32,2688]{1,0:T(8,128)(2,1)S(1)}, u32[]{:S(2)}, u32[]{:S(2)}) %collective-permute-start.19) | collective-permute-done | bytes 172064 | tf_op jit(solution)/shard_map/ppermute | solution.py:26
  69.9 0.1 add_convert_fusion.4
  70.0 1.9 %collective-permute-start.23 = (bf16[32,2688]{1,0:T(8,128)(2,1)S(1)}, bf16[32,2688]{1,0:T(8,128)(2,1)S(1)}, u32[]{:S(2)}, u32[]{:S(2)}) collective-permute-start(bf16[32,2688]{1,0:T(8,128)(2,1)S(1)} %get-tuple-element.94), channel_id=1, source_target_pairs={{0,2},{1,5},{2,0},{3,7},{4,6},{5,1},{6,4},{7,3},{8,10},{9,13},{10,... | collective-permute-start | bytes 516104 | tf_op jit(solution)/shard_map/ppermute | solution.py:26
  72.0 1.6 %collective-permute-start.24 = (bf16[32,2688]{1,0:T(8,128)(2,1)S(1)}, bf16[32,2688]{1,0:T(8,128)(2,1)S(1)}, u32[]{:S(2)}, u32[]{:S(2)}) collective-permute-start(bf16[32,2688]{1,0:T(8,128)(2,1)S(1)} %get-tuple-element.95), channel_id=1, source_target_pairs={{0,4},{1,3},{2,6},{3,1},{4,0},{5,7},{6,2},{7,5},{8,12},{9,11},{10,... | collective-permute-start | bytes 516104 | tf_op jit(solution)/shard_map/ppermute | solution.py:26
  73.6 1.6 %collective-permute-start.20 = (bf16[8,4480]{1,0:T(8,128)(2,1)S(1)}, bf16[8,4480]{1,0:T(8,128)(2,1)S(1)}, u32[]{:S(2)}, u32[]{:S(2)}) collective-permute-start(bf16[8,4480]{1,0:T(8,128)(2,1)S(1)} %get-tuple-element.77), channel_id=1, source_target_pairs={{0,8},{1,9},{2,10},{3,11},{4,12},{5,13},{6,14},{7,15},{8,0},{9,1},... | collective-permute-start | bytes 215048 | tf_op jit(solution)/shard_map/ppermute | solution.py:26
  75.2 1.2 %collective-permute-start.21 = (bf16[8,4480]{1,0:T(8,128)(2,1)S(1)}, bf16[8,4480]{1,0:T(8,128)(2,1)S(1)}, u32[]{:S(2)}, u32[]{:S(2)}) collective-permute-start(bf16[8,4480]{1,0:T(8,128)(2,1)S(1)} %get-tuple-element.79), channel_id=1, source_target_pairs={{0,16},{1,17},{2,18},{3,19},{4,20},{5,21},{6,22},{7,23},{8,24},{9,... | collective-permute-start | bytes 215048 | tf_op jit(solution)/shard_map/ppermute | solution.py:26
  76.3 1.6 %collective-permute-start.22 = (bf16[8,4480]{1,0:T(8,128)(2,1)S(1)}, bf16[8,4480]{1,0:T(8,128)(2,1)S(1)}, u32[]{:S(2)}, u32[]{:S(2)}) collective-permute-start(bf16[8,4480]{1,0:T(8,128)(2,1)S(1)} %get-tuple-element.81), channel_id=1, source_target_pairs={{0,24},{1,25},{2,26},{3,27},{4,28},{5,29},{6,30},{7,31},{8,16},{9,... | collective-permute-start | bytes 215048 | tf_op jit(solution)/shard_map/ppermute | solution.py:26
  78.0 2.3 %collective-permute-start.25 = (bf16[8,2688]{1,0:T(8,128)(2,1)S(1)}, bf16[8,2688]{1,0:T(8,128)(2,1)S(1)}, u32[]{:S(2)}, u32[]{:S(2)}) collective-permute-start(bf16[8,2688]{1,0:T(8,128)(2,1)S(1)} %get-tuple-element.91), channel_id=1, source_target_pairs={{0,8},{1,9},{2,10},{3,11},{4,12},{5,13},{6,14},{7,15},{8,0},{9,1},... | collective-permute-start | bytes 129032 | tf_op jit(solution)/shard_map/ppermute | solution.py:26
  80.4 2.5 %collective-permute-start.27 = (bf16[8,2688]{1,0:T(8,128)(2,1)S(1)}, bf16[8,2688]{1,0:T(8,128)(2,1)S(1)}, u32[]{:S(2)}, u32[]{:S(2)}) collective-permute-start(bf16[8,2688]{1,0:T(8,128)(2,1)S(1)} %get-tuple-element.92), channel_id=1, source_target_pairs={{0,24},{1,25},{2,26},{3,27},{4,28},{5,29},{6,30},{7,31},{8,16},{9,... | collective-permute-start | bytes 129032 | tf_op jit(solution)/shard_map/ppermute | solution.py:26
  82.8 0.7 collective-permute-done.21
  83.5 0.1 add_convert_fusion.6
  83.6 0.3 collective-permute-done.25
  83.9 2.4 %collective-permute-done.27 = bf16[8,2688]{1,0:T(8,128)(2,1)S(1)} collective-permute-done((bf16[8,2688]{1,0:T(8,128)(2,1)S(1)}, bf16[8,2688]{1,0:T(8,128)(2,1)S(1)}, u32[]{:S(2)}, u32[]{:S(2)}) %collective-permute-start.27) | collective-permute-done | bytes 43040 | tf_op jit(solution)/shard_map/ppermute | solution.py:26
  86.3 1.4 %collective-permute-done.26 = bf16[8,2688]{1,0:T(8,128)(2,1)S(1)} collective-permute-done((bf16[8,2688]{1,0:T(8,128)(2,1)S(1)}, bf16[8,2688]{1,0:T(8,128)(2,1)S(1)}, u32[]{:S(2)}, u32[]{:S(2)}) %collective-permute-start.26) | collective-permute-done | bytes 43040 | tf_op jit(solution)/shard_map/ppermute | solution.py:26
  87.8 0.1 add_convert_fusion.7
  87.9 0.7 pad_maximum_fusion
  (38 shorter events, 0.4 us)
Async XLA Ops:
  0.6 14.6 %collective-permute-start.3 = (bf16[8,96,576]{2,1,0:T(8,128)(2,1)}, bf16[8,96,576]{2,1,0:T(8,128)(2,1)S(1)}, u32[]{:S(2)}, u32[]{:S(2)}) collective-permute-start(bf16[8,96,576]{2,1,0:T(8,128)(2,1)} %refs_3_.1), channel_id=1, source_target_pairs={{1,2},{3,4},{5,6},{6,5},{9,10},{11,12},{13,14},{14,13},{17,18},{19... | collective-permute-start | bytes 2654216 | tf_op jit(solution)/shard_map/ppermute | solution.py:47
  1.4 10.5 %collective-permute-start.1 = (bf16[8,7168]{1,0:T(8,128)(2,1)}, bf16[8,7168]{1,0:T(8,128)(2,1)S(1)}, u32[]{:S(2)}, u32[]{:S(2)}) collective-permute-start(bf16[8,7168]{1,0:T(8,128)(2,1)} %param.16), channel_id=1, source_target_pairs={{0,16},{1,17},{2,18},{3,19},{4,20},{5,21},{6,22},{7,23},{8,24},{9,... | collective-permute-start | bytes 344072 | tf_op jit(solution)/shard_map/ppermute | solution.py:26
  5.5 6.5 %collective-permute-start = (bf16[8,7168]{1,0:T(8,128)(2,1)}, bf16[8,7168]{1,0:T(8,128)(2,1)S(1)}, u32[]{:S(2)}, u32[]{:S(2)}) collective-permute-start(bf16[8,7168]{1,0:T(8,128)(2,1)} %param.16), channel_id=1, source_target_pairs={{0,8},{1,9},{2,10},{3,11},{4,12},{5,13},{6,14},{7,15},{8,0},{9,1},... | collective-permute-start | bytes 344072 | tf_op jit(solution)/shard_map/ppermute | solution.py:26
  7.0 8.1 %collective-permute-start.2 = (bf16[8,7168]{1,0:T(8,128)(2,1)}, bf16[8,7168]{1,0:T(8,128)(2,1)S(1)}, u32[]{:S(2)}, u32[]{:S(2)}) collective-permute-start(bf16[8,7168]{1,0:T(8,128)(2,1)} %param.16), channel_id=1, source_target_pairs={{0,24},{1,25},{2,26},{3,27},{4,28},{5,29},{6,30},{7,31},{8,16},{9,... | collective-permute-start | bytes 344072 | tf_op jit(solution)/shard_map/ppermute | solution.py:26
  15.2 20.0 %copy-start = (bf16[8,96,576]{2,1,0:T(8,128)(2,1)S(1)}, bf16[8,96,576]{2,1,0:T(8,128)(2,1)}, u32[]{:S(2)}) copy-start(bf16[8,96,576]{2,1,0:T(8,128)(2,1)} %refs_3_.1) | copy-start | bytes 2654212
  15.2 11.5 %collective-permute-start.4 = (bf16[32,7168]{1,0:T(8,128)(2,1)S(1)}, bf16[32,7168]{1,0:T(8,128)(2,1)S(1)}, u32[]{:S(2)}, u32[]{:S(2)}) collective-permute-start(bf16[32,7168]{1,0:T(8,128)(2,1)S(1)} %constant_dynamic-update-slice_fusion.refs_0_), channel_id=1, source_target_pairs={{0,4},{1,3},{2,6},{3,1},{4,0},{5,7},{6,2},{7,5},{8,12},{9,11},{10,... | collective-permute-start | bytes 1376264 | tf_op jit(solution)/shard_map/ppermute | solution.py:26
  20.2 12.7 %collective-permute-start.9 = (bf16[8,96,576]{2,1,0:T(8,128)(2,1)}, bf16[8,96,576]{2,1,0:T(8,128)(2,1)S(1)}, u32[]{:S(2)}, u32[]{:S(2)}) collective-permute-start(bf16[8,96,576]{2,1,0:T(8,128)(2,1)} %refs_3_.1), channel_id=1, source_target_pairs={{0,1},{1,0},{2,3},{3,2},{4,5},{5,4},{6,7},{7,6},{8,9},{9,8},{10,11... | collective-permute-start | bytes 2654216 | tf_op jit(solution)/shard_map/ppermute | solution.py:26
  20.3 12.7 %collective-permute-start.7 = (bf16[32,7168]{1,0:T(8,128)(2,1)S(1)}, bf16[32,7168]{1,0:T(8,128)(2,1)S(1)}, u32[]{:S(2)}, u32[]{:S(2)}) collective-permute-start(bf16[32,7168]{1,0:T(8,128)(2,1)S(1)} %constant_dynamic-update-slice_fusion.refs_0_), channel_id=1, source_target_pairs={{0,1},{1,0},{2,3},{3,2},{4,5},{5,4},{6,7},{7,6},{8,9},{9,8},{10,11... | collective-permute-start | bytes 1376264 | tf_op jit(solution)/shard_map/ppermute | solution.py:26
  26.7 6.3 %collective-permute-start.8 = (bf16[32,7168]{1,0:T(8,128)(2,1)S(1)}, bf16[32,7168]{1,0:T(8,128)(2,1)S(1)}, u32[]{:S(2)}, u32[]{:S(2)}) collective-permute-start(bf16[32,7168]{1,0:T(8,128)(2,1)S(1)} %collective-permute-done.4.refs_1_), channel_id=1, source_target_pairs={{0,1},{1,0},{2,3},{3,2},{4,5},{5,4},{6,7},{7,6},{8,9},{9,8},{10,11... | collective-permute-start | bytes 1376264 | tf_op jit(solution)/shard_map/ppermute | solution.py:26
  26.7 8.5 %collective-permute-start.6 = (bf16[32,7168]{1,0:T(8,128)(2,1)S(1)}, bf16[32,7168]{1,0:T(8,128)(2,1)S(1)}, u32[]{:S(2)}, u32[]{:S(2)}) collective-permute-start(bf16[32,7168]{1,0:T(8,128)(2,1)S(1)} %collective-permute-done.4.refs_1_), channel_id=1, source_target_pairs={{0,2},{1,5},{2,0},{3,7},{4,6},{5,1},{6,4},{7,3},{8,10},{9,13},{10,... | collective-permute-start | bytes 1376264 | tf_op jit(solution)/shard_map/ppermute | solution.py:26
  27.8 12.3 %collective-permute-start.5 = (bf16[32,7168]{1,0:T(8,128)(2,1)S(1)}, bf16[32,7168]{1,0:T(8,128)(2,1)S(1)}, u32[]{:S(2)}, u32[]{:S(2)}) collective-permute-start(bf16[32,7168]{1,0:T(8,128)(2,1)S(1)} %constant_dynamic-update-slice_fusion.refs_0_), channel_id=1, source_target_pairs={{0,2},{1,5},{2,0},{3,7},{4,6},{5,1},{6,4},{7,3},{8,10},{9,13},{10,... | collective-permute-start | bytes 1376264 | tf_op jit(solution)/shard_map/ppermute | solution.py:26
  35.2 18.9 %copy-start.1 = (bf16[8,64,576]{2,1,0:T(8,128)(2,1)S(1)}, bf16[8,64,576]{2,1,0:T(8,128)(2,1)}, u32[]{:S(2)}) copy-start(bf16[8,64,576]{2,1,0:T(8,128)(2,1)} %refs_2_.3) | copy-start | bytes 1769476
  35.2 19.0 %copy-start.2 = (bf16[8,576]{1,0:T(8,128)(2,1)S(1)}, bf16[8,576]{1,0:T(8,128)(2,1)}, u32[]{:S(2)}) copy-start(bf16[8,576]{1,0:T(8,128)(2,1)} %refs_5_.1) | copy-start | bytes 27652
  35.2 19.0 %copy-start.3 = (s32[8]{0:T(128)S(1)}, s32[8]{0:T(128)}, u32[]{:S(2)}) copy-start(s32[8]{0:T(128)} %refs_0_.3) | copy-start | bytes 100
  35.2 19.0 %copy-start.4 = (s32[8]{0:T(128)S(1)}, s32[8]{0:T(128)}, u32[]{:S(2)}) copy-start(s32[8]{0:T(128)} %refs_1_.3) | copy-start | bytes 100
  35.2 12.7 %collective-permute-start.12 = (bf16[8,96,576]{2,1,0:T(8,128)(2,1)S(1)}, bf16[8,96,576]{2,1,0:T(8,128)(2,1)S(1)}, u32[]{:S(2)}, u32[]{:S(2)}) collective-permute-start(bf16[8,96,576]{2,1,0:T(8,128)(2,1)S(1)} %copy-done), channel_id=1, source_target_pairs={{2,1},{4,3},{7,8},{8,7},{10,9},{12,11},{15,16},{16,15},{18,17},{20... | collective-permute-start | bytes 2654216 | tf_op jit(solution)/shard_map/ppermute | solution.py:47
  40.1 1.8 %collective-permute-start.10 = (bf16[32,7168]{1,0:T(8,128)(2,1)S(1)}, bf16[32,7168]{1,0:T(8,128)(2,1)S(1)}, u32[]{:S(2)}, u32[]{:S(2)}) collective-permute-start(bf16[32,7168]{1,0:T(8,128)(2,1)S(1)} %collective-permute-done.5.refs_2_), channel_id=1, source_target_pairs={{0,1},{1,0},{2,3},{3,2},{4,5},{5,4},{6,7},{7,6},{8,9},{9,8},{10,11... | collective-permute-start | bytes 1376264 | tf_op jit(solution)/shard_map/ppermute | solution.py:26
  40.1 2.5 %collective-permute-start.11 = (bf16[32,7168]{1,0:T(8,128)(2,1)S(1)}, bf16[32,7168]{1,0:T(8,128)(2,1)S(1)}, u32[]{:S(2)}, u32[]{:S(2)}) collective-permute-start(bf16[32,7168]{1,0:T(8,128)(2,1)S(1)} %collective-permute-done.6.refs_3_), channel_id=1, source_target_pairs={{0,1},{1,0},{2,3},{3,2},{4,5},{5,4},{6,7},{7,6},{8,9},{9,8},{10,11... | collective-permute-start | bytes 1376264 | tf_op jit(solution)/shard_map/ppermute | solution.py:26
  47.9 4.2 %collective-permute-start.13 = (bf16[32,7168]{1,0:T(8,128)(2,1)S(1)}, bf16[32,7168]{1,0:T(8,128)(2,1)S(1)}, u32[]{:S(2)}, u32[]{:S(2)}) collective-permute-start(bf16[32,7168]{1,0:T(8,128)(2,1)S(1)} %get-tuple-element.62), channel_id=1, source_target_pairs={{0,1},{1,0},{2,3},{3,2},{4,5},{5,4},{6,7},{7,6},{8,9},{9,8},{10,11... | collective-permute-start | bytes 1376264 | tf_op jit(solution)/shard_map/ppermute | solution.py:26
  50.7 8.2 %collective-permute-start.16 = (bf16[32,7168]{1,0:T(8,128)(2,1)S(1)}, bf16[32,7168]{1,0:T(8,128)(2,1)S(1)}, u32[]{:S(2)}, u32[]{:S(2)}) collective-permute-start(bf16[32,7168]{1,0:T(8,128)(2,1)S(1)} %get-tuple-element.71), channel_id=1, source_target_pairs={{0,1},{1,0},{2,3},{3,2},{4,5},{5,4},{6,7},{7,6},{8,9},{9,8},{10,11... | collective-permute-start | bytes 1376264 | tf_op jit(solution)/shard_map/ppermute | solution.py:26
  50.7 8.2 %collective-permute-start.15 = (bf16[64,7168]{1,0:T(8,128)(2,1)S(1)}, bf16[64,7168]{1,0:T(8,128)(2,1)S(1)}, u32[]{:S(2)}, u32[]{:S(2)}) collective-permute-start(bf16[64,7168]{1,0:T(8,128)(2,1)S(1)} %get-tuple-element.70), channel_id=1, source_target_pairs={{0,1},{1,0},{2,3},{3,2},{4,5},{5,4},{6,7},{7,6},{8,9},{9,8},{10,11... | collective-permute-start | bytes 2752520 | tf_op jit(solution)/shard_map/ppermute | solution.py:26
  52.2 6.7 %collective-permute-start.14 = (bf16[32,4480]{1,0:T(8,128)(2,1)S(1)}, bf16[32,4480]{1,0:T(8,128)(2,1)S(1)}, u32[]{:S(2)}, u32[]{:S(2)}) collective-permute-start(bf16[32,4480]{1,0:T(8,128)(2,1)S(1)} %add_convert_fusion.2), channel_id=1, source_target_pairs={{0,2},{1,5},{2,0},{3,7},{4,6},{5,1},{6,4},{7,3},{8,10},{9,13},{10,... | collective-permute-start | bytes 860168 | tf_op jit(solution)/shard_map/ppermute | solution.py:26
  59.1 9.4 %collective-permute-start.18 = (bf16[32,4480]{1,0:T(8,128)(2,1)S(1)}, bf16[32,4480]{1,0:T(8,128)(2,1)S(1)}, u32[]{:S(2)}, u32[]{:S(2)}) collective-permute-start(bf16[32,4480]{1,0:T(8,128)(2,1)S(1)} %get-tuple-element.73), channel_id=1, source_target_pairs={{0,4},{1,3},{2,6},{3,1},{4,0},{5,7},{6,2},{7,5},{8,12},{9,11},{10,... | collective-permute-start | bytes 860168 | tf_op jit(solution)/shard_map/ppermute | solution.py:26
  61.3 7.2 %collective-permute-start.17 = (bf16[32,4480]{1,0:T(8,128)(2,1)S(1)}, bf16[32,4480]{1,0:T(8,128)(2,1)S(1)}, u32[]{:S(2)}, u32[]{:S(2)}) collective-permute-start(bf16[32,4480]{1,0:T(8,128)(2,1)S(1)} %get-tuple-element.96), channel_id=1, source_target_pairs={{0,2},{1,5},{2,0},{3,7},{4,6},{5,1},{6,4},{7,3},{8,10},{9,13},{10,... | collective-permute-start | bytes 860168 | tf_op jit(solution)/shard_map/ppermute | solution.py:26
  63.3 6.6 %collective-permute-start.19 = (bf16[32,2688]{1,0:T(8,128)(2,1)S(1)}, bf16[32,2688]{1,0:T(8,128)(2,1)S(1)}, u32[]{:S(2)}, u32[]{:S(2)}) collective-permute-start(bf16[32,2688]{1,0:T(8,128)(2,1)S(1)} %add_convert_fusion.5), channel_id=1, source_target_pairs={{0,2},{1,5},{2,0},{3,7},{4,6},{5,1},{6,4},{7,3},{8,10},{9,13},{10,... | collective-permute-start | bytes 516104 | tf_op jit(solution)/shard_map/ppermute | solution.py:26
  70.0 7.9 %collective-permute-start.23 = (bf16[32,2688]{1,0:T(8,128)(2,1)S(1)}, bf16[32,2688]{1,0:T(8,128)(2,1)S(1)}, u32[]{:S(2)}, u32[]{:S(2)}) collective-permute-start(bf16[32,2688]{1,0:T(8,128)(2,1)S(1)} %get-tuple-element.94), channel_id=1, source_target_pairs={{0,2},{1,5},{2,0},{3,7},{4,6},{5,1},{6,4},{7,3},{8,10},{9,13},{10,... | collective-permute-start | bytes 516104 | tf_op jit(solution)/shard_map/ppermute | solution.py:26
  72.0 6.0 %collective-permute-start.24 = (bf16[32,2688]{1,0:T(8,128)(2,1)S(1)}, bf16[32,2688]{1,0:T(8,128)(2,1)S(1)}, u32[]{:S(2)}, u32[]{:S(2)}) collective-permute-start(bf16[32,2688]{1,0:T(8,128)(2,1)S(1)} %get-tuple-element.95), channel_id=1, source_target_pairs={{0,4},{1,3},{2,6},{3,1},{4,0},{5,7},{6,2},{7,5},{8,12},{9,11},{10,... | collective-permute-start | bytes 516104 | tf_op jit(solution)/shard_map/ppermute | solution.py:26
  73.6 9.3 %collective-permute-start.20 = (bf16[8,4480]{1,0:T(8,128)(2,1)S(1)}, bf16[8,4480]{1,0:T(8,128)(2,1)S(1)}, u32[]{:S(2)}, u32[]{:S(2)}) collective-permute-start(bf16[8,4480]{1,0:T(8,128)(2,1)S(1)} %get-tuple-element.77), channel_id=1, source_target_pairs={{0,8},{1,9},{2,10},{3,11},{4,12},{5,13},{6,14},{7,15},{8,0},{9,1},... | collective-permute-start | bytes 215048 | tf_op jit(solution)/shard_map/ppermute | solution.py:26
  75.2 8.4 %collective-permute-start.21 = (bf16[8,4480]{1,0:T(8,128)(2,1)S(1)}, bf16[8,4480]{1,0:T(8,128)(2,1)S(1)}, u32[]{:S(2)}, u32[]{:S(2)}) collective-permute-start(bf16[8,4480]{1,0:T(8,128)(2,1)S(1)} %get-tuple-element.79), channel_id=1, source_target_pairs={{0,16},{1,17},{2,18},{3,19},{4,20},{5,21},{6,22},{7,23},{8,24},{9,... | collective-permute-start | bytes 215048 | tf_op jit(solution)/shard_map/ppermute | solution.py:26
  76.3 7.2 %collective-permute-start.22 = (bf16[8,4480]{1,0:T(8,128)(2,1)S(1)}, bf16[8,4480]{1,0:T(8,128)(2,1)S(1)}, u32[]{:S(2)}, u32[]{:S(2)}) collective-permute-start(bf16[8,4480]{1,0:T(8,128)(2,1)S(1)} %get-tuple-element.81), channel_id=1, source_target_pairs={{0,24},{1,25},{2,26},{3,27},{4,28},{5,29},{6,30},{7,31},{8,16},{9,... | collective-permute-start | bytes 215048 | tf_op jit(solution)/shard_map/ppermute | solution.py:26
  78.0 5.9 %collective-permute-start.25 = (bf16[8,2688]{1,0:T(8,128)(2,1)S(1)}, bf16[8,2688]{1,0:T(8,128)(2,1)S(1)}, u32[]{:S(2)}, u32[]{:S(2)}) collective-permute-start(bf16[8,2688]{1,0:T(8,128)(2,1)S(1)} %get-tuple-element.91), channel_id=1, source_target_pairs={{0,8},{1,9},{2,10},{3,11},{4,12},{5,13},{6,14},{7,15},{8,0},{9,1},... | collective-permute-start | bytes 129032 | tf_op jit(solution)/shard_map/ppermute | solution.py:26
  80.4 6.0 %collective-permute-start.27 = (bf16[8,2688]{1,0:T(8,128)(2,1)S(1)}, bf16[8,2688]{1,0:T(8,128)(2,1)S(1)}, u32[]{:S(2)}, u32[]{:S(2)}) collective-permute-start(bf16[8,2688]{1,0:T(8,128)(2,1)S(1)} %get-tuple-element.92), channel_id=1, source_target_pairs={{0,24},{1,25},{2,26},{3,27},{4,28},{5,29},{6,30},{7,31},{8,16},{9,... | collective-permute-start | bytes 129032 | tf_op jit(solution)/shard_map/ppermute | solution.py:26
  82.8 4.9 %collective-permute-start.26 = (bf16[8,2688]{1,0:T(8,128)(2,1)S(1)}, bf16[8,2688]{1,0:T(8,128)(2,1)S(1)}, u32[]{:S(2)}, u32[]{:S(2)}) collective-permute-start(bf16[8,2688]{1,0:T(8,128)(2,1)S(1)} %get-tuple-element.93), channel_id=1, source_target_pairs={{0,16},{1,17},{2,18},{3,19},{4,20},{5,21},{6,22},{7,23},{8,24},{9,... | collective-permute-start | bytes 129032 | tf_op jit(solution)/shard_map/ppermute | solution.py:26

commit v14 on v13

--- a/solution.py
+++ b/solution.py
@@ -261,13 +261,13 @@
     early, _ = cache_rows("early", 0, beam_count)
     height = expert_count * capacity
     rows = jnp.pad(column[0], ((0, height - capacity), (0, 0)))
-    rows, column, early, mixing = tied(rows, column, early, mixing)
-    pieces.append(early)
+    rows, column, mixing = tied(rows, column, mixing)
     for r in range(1, expert_count):
         rows = lax.dynamic_update_slice(rows, column[r], (r * capacity, 0))
     column = rows
     near = swapped(column, first)
-    again, near = tied(column, near)
+    again, near, early = tied(column, near, early)
+    pieces.append(early)
     across = swapped(near, second)
     side = swapped(again, second)
     beside = swapped(latent_cache, twin)
@@ -330,8 +330,8 @@
     near, side = swapped(near, first), swapped(side, second)
     share = shares(halves[1], side, near)
     values.append([share[0]] + back(share))
-    totals = []
-    for value in values:
+
+    def mixed(value):
         value = [v.astype(jnp.float32) for v in value]
         if dense:
             total = sum(mixing[r][:, None] * value[r] for r in range(expert_count))
@@ -342,8 +342,11 @@
                 precision=lax.Precision.HIGHEST,
                 preferred_element_type=jnp.float32,
             )
-        totals.append(total.astype(jnp.bfloat16))
-    expert_output = jnp.concatenate(totals, axis=1)
+        return total.astype(jnp.bfloat16)
+
+    expert_output = jnp.pad(mixed(values[0]), ((0, 0), (0, width - cut)))
+    expert_output, values[1] = tied(expert_output, values[1])
+    expert_output = lax.dynamic_update_slice(expert_output, mixed(values[1]), (0, cut))
     return (attention, expert_output)
 
 

time: 88.7 us -> 89.5 us (level)
  waiting for transfers between devices: 32.1 us -> 36.3 us
  starting transfers between devices: 37.4 us -> 33.8 us
    ppermute x26, waiting for transfers between devices: 32 us -> 36.3 us  [swapped(): return lax.ppermute(value, 'dp', [(i, partner(i)) for i in range(peers)])]
    ppermute x26, starting transfers between devices: 35.9 us -> 32.3 us  [swapped(): return lax.ppermute(value, 'dp', [(i, partner(i)) for i in range(peers)])]
  transfers between devices with their start and end apart: 28 -> 28, of which waited for: 15 -> 14; matrix products, arithmetic and copies ran while one was open for 6% -> 6% of each run, Pallas kernels for 13% -> 13%
where the time goes in v14:
time: 89.5 us; the launch traced here: 89.3 us
  waiting for transfers between devices  36.3 us (41%)
  starting transfers between devices  33.8 us (38%)
  Pallas kernels  11.8 us (13%)
  other arithmetic  4.19 us (5%)
  local copies, waits for them, and re-layouts  2.25 us (3%)
    ppermute x26, waiting for transfers between devices, swapped(): return lax.ppermute(value, 'dp', [(i, partner(i)) for i in range(peers)])  36.3 us
    ppermute x26, starting transfers between devices, swapped(): return lax.ppermute(value, 'dp', [(i, partner(i)) for i in range(peers)])  32.3 us
    pallas_call x1, Pallas kernels, experts(): pl.pallas_call(lambda *refs: expert_kernel(wide, *refs), in_specs=[whole]...  5.3 us
    pallas_call x1, Pallas kernels, fetched(): pl.pallas_call(fetch_kernel, in_specs=[pl.BlockSpec(memory_space=pltpu.HB...  4.23 us
    reduce_sum x1, other arithmetic, body(): jnp.sum(jnp.where(routed_experts == targets[r], route_weights, 0.0), axis=1)  3.31 us
    pallas_call x1, Pallas kernels, attend(): pl.pallas_call(lambda *refs: attend_kernel(spans, *refs), in_specs=[scala...  2.31 us
  transfers between devices with their start and end apart: 28, of which 14 were waited for; matrix products, arithmetic and copies ran while one was open for 6% of the time, Pallas kernels for 13%

profile of v14, /device:TPU:0, one launch (start us, length us, event | category | flops | bytes accessed | tf_op | source)
XLA Modules:
  0.0 89.3 jit_solution(5242341423890261754)
XLA Ops:
  0.6 4.1 %collective-permute-start.1 = (bf16[8,7168]{1,0:T(8,128)(2,1)}, bf16[8,7168]{1,0:T(8,128)(2,1)S(1)}, u32[]{:S(2)}, u32[]{:S(2)}) collective-permute-start(bf16[8,7168]{1,0:T(8,128)(2,1)} %param.16), channel_id=1, source_target_pairs={{0,16},{1,17},{2,18},{3,19},{4,20},{5,21},{6,22},{7,23},{8,24},{9,... | collective-permute-start | bytes 344072 | tf_op jit(solution)/shard_map/ppermute | solution.py:26
  4.7 1.6 %collective-permute-start = (bf16[8,7168]{1,0:T(8,128)(2,1)}, bf16[8,7168]{1,0:T(8,128)(2,1)S(1)}, u32[]{:S(2)}, u32[]{:S(2)}) collective-permute-start(bf16[8,7168]{1,0:T(8,128)(2,1)} %param.16), channel_id=1, source_target_pairs={{0,8},{1,9},{2,10},{3,11},{4,12},{5,13},{6,14},{7,15},{8,0},{9,1},... | collective-permute-start | bytes 344072 | tf_op jit(solution)/shard_map/ppermute | solution.py:26
  6.3 0.7 collective-permute-start.4
  7.1 0.6 fusion.5
  7.7 0.9 %pad.8 = bf16[32,7168]{1,0:T(8,128)(2,1)S(1)} pad(bf16[8,7168]{1,0:T(8,128)(2,1)} %param.16, bf16[]{:T(256)} %constant.20.clone.1), padding=0_24x0_0 | pad | bytes 573442 | tf_op jit(solution)/shard_map/jit(_pad)/pad | solution.py:263
  8.6 3.3 %fusion.4 = (f32[8]{0:T(128)S(1)}, f32[8]{0:T(128)S(1)}, f32[8]{0:T(128)S(1)}, f32[8]{0:T(128)S(1)}) fusion(f32[8,2]{0,1:T(2,128)} %param.18, s32[8,2]{0,1:T(2,128)} %param.17, s32[]{:T(128)} %bitcast.3, s32[]{:T(128)} %bitcast.1, s32[]{:T(128)} %bitcast, s32[]{:T(128)} %bitcast.2), kind=kLoop, calls=%fused_computation.24 | loop fusion | flops 160 | bytes 272 | tf_op jit(solution)/shard_map/reduce_sum | solution.py:226
  11.9 0.3 collective-permute-done.1
  12.2 2.0 %collective-permute-done.2 = bf16[8,7168]{1,0:T(8,128)(2,1)S(1)} collective-permute-done((bf16[8,7168]{1,0:T(8,128)(2,1)}, bf16[8,7168]{1,0:T(8,128)(2,1)S(1)}, u32[]{:S(2)}, u32[]{:S(2)}) %collective-permute-start.2) | collective-permute-done | bytes 114720 | tf_op jit(solution)/shard_map/ppermute | solution.py:26
  14.2 1.6 %collective-permute-start.3 = (bf16[32,7168]{1,0:T(8,128)(2,1)S(1)}, bf16[32,7168]{1,0:T(8,128)(2,1)S(1)}, u32[]{:S(2)}, u32[]{:S(2)}) collective-permute-start(bf16[32,7168]{1,0:T(8,128)(2,1)S(1)} %constant_dynamic-update-slice_fusion.refs_0_), channel_id=1, source_target_pairs={{0,4},{1,3},{2,6},{3,1},{4,0},{5,7},{6,2},{7,5},{8,12},{9,11},{10,... | collective-permute-start | bytes 1376264 | tf_op jit(solution)/shard_map/ppermute | solution.py:26
  15.8 0.5 collective-permute-start.9
  16.4 10.6 %collective-permute-done.3.refs_1_ = bf16[32,7168]{1,0:T(8,128)(2,1)S(1)} collective-permute-done((bf16[32,7168]{1,0:T(8,128)(2,1)S(1)}, bf16[32,7168]{1,0:T(8,128)(2,1)S(1)}, u32[]{:S(2)}, u32[]{:S(2)}) %collective-permute-start.3) | collective-permute-done | bytes 458784 | tf_op jit(solution)/shard_map/ppermute | solution.py:26
  27.0 0.9 collective-permute-start.8
  27.9 0.5 collective-permute-start.6
  28.4 1.5 %collective-permute-start.5 = (bf16[32,7168]{1,0:T(8,128)(2,1)S(1)}, bf16[32,7168]{1,0:T(8,128)(2,1)S(1)}, u32[]{:S(2)}, u32[]{:S(2)}) collective-permute-start(bf16[32,7168]{1,0:T(8,128)(2,1)S(1)} %constant_dynamic-update-slice_fusion.refs_0_), channel_id=1, source_target_pairs={{0,2},{1,5},{2,0},{3,7},{4,6},{5,1},{6,4},{7,3},{8,10},{9,13},{10,... | collective-permute-start | bytes 1376264 | tf_op jit(solution)/shard_map/ppermute | solution.py:26
  29.9 4.2 %shard_map.122 = (bf16[1,7168,256]{2,1,0:T(8,128)(2,1)S(1)}, bf16[1,7168,256]{2,1,0:T(8,128)(2,1)S(1)}, bf16[1,256,7168]{2,1,0:T(8,128)(2,1)S(1)}) custom-call(bf16[1,7168,256]{2,1,0:T(8,128)(2,1)} %refs_0_.2, bf16[1,7168,256]{2,1,0:T(8,128)(2,1)} %refs_1_.2, bf16[1,256,7168]{2,1,0:T(8,128)(2,1)} %refs_2_.2), custom_call_target="tpu_custom_call" | custom-call | bytes 22020096 | tf_op jit(solution)/shard_map/pallas_call | solution.py:127
  34.2 2.2 %collective-permute-done.6.refs_3_ = bf16[32,7168]{1,0:T(8,128)(2,1)S(1)} collective-permute-done((bf16[32,7168]{1,0:T(8,128)(2,1)S(1)}, bf16[32,7168]{1,0:T(8,128)(2,1)S(1)}, u32[]{:S(2)}, u32[]{:S(2)}) %collective-permute-start.6) | collective-permute-done | bytes 458784 | tf_op jit(solution)/shard_map/ppermute | solution.py:26
  36.4 0.9 collective-permute-start.12
  37.3 4.0 %collective-permute-done.5.refs_2_ = bf16[32,7168]{1,0:T(8,128)(2,1)S(1)} collective-permute-done((bf16[32,7168]{1,0:T(8,128)(2,1)S(1)}, bf16[32,7168]{1,0:T(8,128)(2,1)S(1)}, u32[]{:S(2)}, u32[]{:S(2)}) %collective-permute-start.5) | collective-permute-done | bytes 458784 | tf_op jit(solution)/shard_map/ppermute | solution.py:26
  41.3 0.5 collective-permute-start.11
  41.8 1.3 %collective-permute-done.10.refs_6_ = bf16[32,7168]{1,0:T(8,128)(2,1)S(1)} collective-permute-done((bf16[32,7168]{1,0:T(8,128)(2,1)S(1)}, bf16[32,7168]{1,0:T(8,128)(2,1)S(1)}, u32[]{:S(2)}, u32[]{:S(2)}) %collective-permute-start.10) | collective-permute-done | bytes 458784 | tf_op jit(solution)/shard_map/ppermute | solution.py:26
  43.1 0.7 collective-permute-done.11.refs_7_
  43.8 5.3 %shard_map.123 = (bf16[128,7168]{1,0:T(8,128)(2,1)S(1)}, bf16[64,7168]{1,0:T(8,128)(2,1)S(1)}, bf16[32,7168]{1,0:T(8,128)(2,1)S(1)}, bf16[32,7168]{1,0:T(8,128)(2,1)S(1)}) custom-call(bf16[32,7168]{1,0:T(8,128)(2,1)S(1)} %constant_dynamic-update-slice_fusion.refs_0_, bf16[32,7168]{1,0:T(8,128)(2,1)S(1)} %collective-permute-done.3.refs_1_, ...), custom_call_target="tpu_custom_call" | custom-call | flops 2818572288 | bytes 18350080 | tf_op jit(solution)/shard_map/pallas_call | solution.py:180
  49.1 2.6 %collective-permute-start.13 = (bf16[32,7168]{1,0:T(8,128)(2,1)S(1)}, bf16[32,7168]{1,0:T(8,128)(2,1)S(1)}, u32[]{:S(2)}, u32[]{:S(2)}) collective-permute-start(bf16[32,7168]{1,0:T(8,128)(2,1)S(1)} %get-tuple-element.67), channel_id=1, source_target_pairs={{0,1},{1,0},{2,3},{3,2},{4,5},{5,4},{6,7},{7,6},{8,9},{9,8},{10,11... | collective-permute-start | bytes 1376264 | tf_op jit(solution)/shard_map/ppermute | solution.py:26
  51.6 0.5 collective-permute-start.15
  52.1 0.9 %collective-permute-done.13 = bf16[32,7168]{1,0:T(8,128)(2,1)S(1)} collective-permute-done((bf16[32,7168]{1,0:T(8,128)(2,1)S(1)}, bf16[32,7168]{1,0:T(8,128)(2,1)S(1)}, u32[]{:S(2)}, u32[]{:S(2)}) %collective-permute-start.13) | collective-permute-done | bytes 458784 | tf_op jit(solution)/shard_map/ppermute | solution.py:26
  53.2 1.5 %collective-permute-start.14 = (bf16[32,4480]{1,0:T(8,128)(2,1)S(1)}, bf16[32,4480]{1,0:T(8,128)(2,1)S(1)}, u32[]{:S(2)}, u32[]{:S(2)}) collective-permute-start(bf16[32,4480]{1,0:T(8,128)(2,1)S(1)} %add_convert_fusion.2), channel_id=1, source_target_pairs={{0,2},{1,5},{2,0},{3,7},{4,6},{5,1},{6,4},{7,3},{8,10},{9,13},{10,... | collective-permute-start | bytes 860168 | tf_op jit(solution)/shard_map/ppermute | solution.py:26
  54.8 2.3 %shard_map.124 = bf16[8,64,512]{2,1,0:T(8,128)(2,1)} custom-call(s32[8]{0:T(128)S(1)} %copy-done.3, s32[8]{0:T(128)S(1)} %copy-done.4, bf16[8,64,576]{2,1,0:T(8,128)(2,1)S(1)} %copy-done.1, bf16[8,96,576]{2,1,0:T(8,128)(2,1)S(1)} %copy-done, bf16[8,96,576]{2,1,0:T(8,128)(2,1)S(1)} %collective-permute-done.9.refs_4_, bf16[8,576]{1,0:T(8,128)(2,1)S(1)} %copy-done.2, ...), custom_call_target="tpu_custom_call" | custom-call | flops 106954752 | bytes 4653056 | tf_op jit(solution)/shard_map/pallas_call | solution.py:99
  57.1 2.8 %collective-permute-done.14 = bf16[32,4480]{1,0:T(8,128)(2,1)S(1)} collective-permute-done((bf16[32,4480]{1,0:T(8,128)(2,1)S(1)}, bf16[32,4480]{1,0:T(8,128)(2,1)S(1)}, u32[]{:S(2)}, u32[]{:S(2)}) %collective-permute-start.14) | collective-permute-done | bytes 286752 | tf_op jit(solution)/shard_map/ppermute | solution.py:26
  59.9 0.2 add_convert_fusion.1
  60.0 1.3 %collective-permute-start.18 = (bf16[32,4480]{1,0:T(8,128)(2,1)S(1)}, bf16[32,4480]{1,0:T(8,128)(2,1)S(1)}, u32[]{:S(2)}, u32[]{:S(2)}) collective-permute-start(bf16[32,4480]{1,0:T(8,128)(2,1)S(1)} %get-tuple-element.78), channel_id=1, source_target_pairs={{0,4},{1,3},{2,6},{3,1},{4,0},{5,7},{6,2},{7,5},{8,12},{9,11},{10,... | collective-permute-start | bytes 860168 | tf_op jit(solution)/shard_map/ppermute | solution.py:26
  61.3 2.0 %collective-permute-start.17 = (bf16[32,4480]{1,0:T(8,128)(2,1)S(1)}, bf16[32,4480]{1,0:T(8,128)(2,1)S(1)}, u32[]{:S(2)}, u32[]{:S(2)}) collective-permute-start(bf16[32,4480]{1,0:T(8,128)(2,1)S(1)} %get-tuple-element.107), channel_id=1, source_target_pairs={{0,2},{1,5},{2,0},{3,7},{4,6},{5,1},{6,4},{7,3},{8,10},{9,13},{10,... | collective-permute-start | bytes 860168 | tf_op jit(solution)/shard_map/ppermute | solution.py:26
  63.4 6.4 %collective-permute-done.18 = bf16[32,4480]{1,0:T(8,128)(2,1)S(1)} collective-permute-done((bf16[32,4480]{1,0:T(8,128)(2,1)S(1)}, bf16[32,4480]{1,0:T(8,128)(2,1)S(1)}, u32[]{:S(2)}, u32[]{:S(2)}) %collective-permute-start.18) | collective-permute-done | bytes 286752 | tf_op jit(solution)/shard_map/ppermute | solution.py:26
  69.8 0.1 convert_add_fusion
  70.0 0.2 collective-permute-done.19
  70.2 0.1 add_convert_fusion.4
  70.3 1.7 %collective-permute-start.23 = (bf16[32,2688]{1,0:T(8,128)(2,1)S(1)}, bf16[32,2688]{1,0:T(8,128)(2,1)S(1)}, u32[]{:S(2)}, u32[]{:S(2)}) collective-permute-start(bf16[32,2688]{1,0:T(8,128)(2,1)S(1)} %get-tuple-element.105), channel_id=1, source_target_pairs={{0,2},{1,5},{2,0},{3,7},{4,6},{5,1},{6,4},{7,3},{8,10},{9,13},{10,... | collective-permute-start | bytes 516104 | tf_op jit(solution)/shard_map/ppermute | solution.py:26
  72.0 1.6 %collective-permute-start.24 = (bf16[32,2688]{1,0:T(8,128)(2,1)S(1)}, bf16[32,2688]{1,0:T(8,128)(2,1)S(1)}, u32[]{:S(2)}, u32[]{:S(2)}) collective-permute-start(bf16[32,2688]{1,0:T(8,128)(2,1)S(1)} %get-tuple-element.106), channel_id=1, source_target_pairs={{0,4},{1,3},{2,6},{3,1},{4,0},{5,7},{6,2},{7,5},{8,12},{9,11},{10,... | collective-permute-start | bytes 516104 | tf_op jit(solution)/shard_map/ppermute | solution.py:26
  73.6 0.7 collective-permute-start.20
  74.3 3.2 %collective-permute-start.21 = (bf16[8,4480]{1,0:T(8,128)(2,1)S(1)}, bf16[8,4480]{1,0:T(8,128)(2,1)S(1)}, u32[]{:S(2)}, u32[]{:S(2)}) collective-permute-start(bf16[8,4480]{1,0:T(8,128)(2,1)S(1)} %get-tuple-element.84), channel_id=1, source_target_pairs={{0,16},{1,17},{2,18},{3,19},{4,20},{5,21},{6,22},{7,23},{8,24},{9,... | collective-permute-start | bytes 215048 | tf_op jit(solution)/shard_map/ppermute | solution.py:26
  77.5 0.5 collective-permute-start.22
  78.1 4.7 %collective-permute-start.27 = (bf16[8,2688]{1,0:T(8,128)(2,1)S(1)}, bf16[8,2688]{1,0:T(8,128)(2,1)S(1)}, u32[]{:S(2)}, u32[]{:S(2)}) collective-permute-start(bf16[8,2688]{1,0:T(8,128)(2,1)S(1)} %get-tuple-element.101), channel_id=1, source_target_pairs={{0,24},{1,25},{2,26},{3,27},{4,28},{5,29},{6,30},{7,31},{8,16},{9,... | collective-permute-start | bytes 129032 | tf_op jit(solution)/shard_map/ppermute | solution.py:26
  82.9 0.6 collective-permute-start.25
  83.5 0.6 collective-permute-done.22
  84.2 0.1 add_convert_fusion.6
  84.3 0.6 collective-permute-done.27
  84.9 3.6 %collective-permute-done.26 = bf16[8,2688]{1,0:T(8,128)(2,1)S(1)} collective-permute-done((bf16[8,2688]{1,0:T(8,128)(2,1)S(1)}, bf16[8,2688]{1,0:T(8,128)(2,1)S(1)}, u32[]{:S(2)}, u32[]{:S(2)}) %collective-permute-start.26) | collective-permute-done | bytes 43040 | tf_op jit(solution)/shard_map/ppermute | solution.py:26
  88.5 0.1 fusion
  88.6 0.6 copy-done.5
  (40 shorter events, 0.4 us)
Async XLA Ops:
  0.6 11.6 %collective-permute-start.1 = (bf16[8,7168]{1,0:T(8,128)(2,1)}, bf16[8,7168]{1,0:T(8,128)(2,1)S(1)}, u32[]{:S(2)}, u32[]{:S(2)}) collective-permute-start(bf16[8,7168]{1,0:T(8,128)(2,1)} %param.16), channel_id=1, source_target_pairs={{0,16},{1,17},{2,18},{3,19},{4,20},{5,21},{6,22},{7,23},{8,24},{9,... | collective-permute-start | bytes 344072 | tf_op jit(solution)/shard_map/ppermute | solution.py:26
  4.7 7.5 %collective-permute-start = (bf16[8,7168]{1,0:T(8,128)(2,1)}, bf16[8,7168]{1,0:T(8,128)(2,1)S(1)}, u32[]{:S(2)}, u32[]{:S(2)}) collective-permute-start(bf16[8,7168]{1,0:T(8,128)(2,1)} %param.16), channel_id=1, source_target_pairs={{0,8},{1,9},{2,10},{3,11},{4,12},{5,13},{6,14},{7,15},{8,0},{9,1},... | collective-permute-start | bytes 344072 | tf_op jit(solution)/shard_map/ppermute | solution.py:26
  6.3 7.9 %collective-permute-start.2 = (bf16[8,7168]{1,0:T(8,128)(2,1)}, bf16[8,7168]{1,0:T(8,128)(2,1)S(1)}, u32[]{:S(2)}, u32[]{:S(2)}) collective-permute-start(bf16[8,7168]{1,0:T(8,128)(2,1)} %param.16), channel_id=1, source_target_pairs={{0,24},{1,25},{2,26},{3,27},{4,28},{5,29},{6,30},{7,31},{8,16},{9,... | collective-permute-start | bytes 344072 | tf_op jit(solution)/shard_map/ppermute | solution.py:26
  6.3 20.7 %collective-permute-start.4 = (bf16[8,96,576]{2,1,0:T(8,128)(2,1)}, bf16[8,96,576]{2,1,0:T(8,128)(2,1)S(1)}, u32[]{:S(2)}, u32[]{:S(2)}) collective-permute-start(bf16[8,96,576]{2,1,0:T(8,128)(2,1)} %refs_3_.1), channel_id=1, source_target_pairs={{1,2},{3,4},{5,6},{6,5},{9,10},{11,12},{13,14},{14,13},{17,18},{19... | collective-permute-start | bytes 2654216 | tf_op jit(solution)/shard_map/ppermute | solution.py:47
  14.2 22.2 %copy-start = (bf16[8,96,576]{2,1,0:T(8,128)(2,1)S(1)}, bf16[8,96,576]{2,1,0:T(8,128)(2,1)}, u32[]{:S(2)}) copy-start(bf16[8,96,576]{2,1,0:T(8,128)(2,1)} %refs_3_.1) | copy-start | bytes 2654212
  14.2 12.8 %collective-permute-start.3 = (bf16[32,7168]{1,0:T(8,128)(2,1)S(1)}, bf16[32,7168]{1,0:T(8,128)(2,1)S(1)}, u32[]{:S(2)}, u32[]{:S(2)}) collective-permute-start(bf16[32,7168]{1,0:T(8,128)(2,1)S(1)} %constant_dynamic-update-slice_fusion.refs_0_), channel_id=1, source_target_pairs={{0,4},{1,3},{2,6},{3,1},{4,0},{5,7},{6,2},{7,5},{8,12},{9,11},{10,... | collective-permute-start | bytes 1376264 | tf_op jit(solution)/shard_map/ppermute | solution.py:26
  15.8 18.3 %collective-permute-start.9 = (bf16[8,96,576]{2,1,0:T(8,128)(2,1)}, bf16[8,96,576]{2,1,0:T(8,128)(2,1)S(1)}, u32[]{:S(2)}, u32[]{:S(2)}) collective-permute-start(bf16[8,96,576]{2,1,0:T(8,128)(2,1)} %refs_3_.1), channel_id=1, source_target_pairs={{0,1},{1,0},{2,3},{3,2},{4,5},{5,4},{6,7},{7,6},{8,9},{9,8},{10,11... | collective-permute-start | bytes 2654216 | tf_op jit(solution)/shard_map/ppermute | solution.py:26
  16.4 17.8 %collective-permute-start.7 = (bf16[32,7168]{1,0:T(8,128)(2,1)S(1)}, bf16[32,7168]{1,0:T(8,128)(2,1)S(1)}, u32[]{:S(2)}, u32[]{:S(2)}) collective-permute-start(bf16[32,7168]{1,0:T(8,128)(2,1)S(1)} %constant_dynamic-update-slice_fusion.refs_0_), channel_id=1, source_target_pairs={{0,1},{1,0},{2,3},{3,2},{4,5},{5,4},{6,7},{7,6},{8,9},{9,8},{10,11... | collective-permute-start | bytes 1376264 | tf_op jit(solution)/shard_map/ppermute | solution.py:26
  27.0 7.2 %collective-permute-start.8 = (bf16[32,7168]{1,0:T(8,128)(2,1)S(1)}, bf16[32,7168]{1,0:T(8,128)(2,1)S(1)}, u32[]{:S(2)}, u32[]{:S(2)}) collective-permute-start(bf16[32,7168]{1,0:T(8,128)(2,1)S(1)} %collective-permute-done.3.refs_1_), channel_id=1, source_target_pairs={{0,1},{1,0},{2,3},{3,2},{4,5},{5,4},{6,7},{7,6},{8,9},{9,8},{10,11... | collective-permute-start | bytes 1376264 | tf_op jit(solution)/shard_map/ppermute | solution.py:26
  27.9 8.5 %collective-permute-start.6 = (bf16[32,7168]{1,0:T(8,128)(2,1)S(1)}, bf16[32,7168]{1,0:T(8,128)(2,1)S(1)}, u32[]{:S(2)}, u32[]{:S(2)}) collective-permute-start(bf16[32,7168]{1,0:T(8,128)(2,1)S(1)} %collective-permute-done.3.refs_1_), channel_id=1, source_target_pairs={{0,2},{1,5},{2,0},{3,7},{4,6},{5,1},{6,4},{7,3},{8,10},{9,13},{10,... | collective-permute-start | bytes 1376264 | tf_op jit(solution)/shard_map/ppermute | solution.py:26
  28.4 12.9 %collective-permute-start.5 = (bf16[32,7168]{1,0:T(8,128)(2,1)S(1)}, bf16[32,7168]{1,0:T(8,128)(2,1)S(1)}, u32[]{:S(2)}, u32[]{:S(2)}) collective-permute-start(bf16[32,7168]{1,0:T(8,128)(2,1)S(1)} %constant_dynamic-update-slice_fusion.refs_0_), channel_id=1, source_target_pairs={{0,2},{1,5},{2,0},{3,7},{4,6},{5,1},{6,4},{7,3},{8,10},{9,13},{10,... | collective-permute-start | bytes 1376264 | tf_op jit(solution)/shard_map/ppermute | solution.py:26
  36.4 18.3 %copy-start.1 = (bf16[8,64,576]{2,1,0:T(8,128)(2,1)S(1)}, bf16[8,64,576]{2,1,0:T(8,128)(2,1)}, u32[]{:S(2)}) copy-start(bf16[8,64,576]{2,1,0:T(8,128)(2,1)} %refs_2_.3) | copy-start | bytes 1769476
  36.4 18.4 %copy-start.2 = (bf16[8,576]{1,0:T(8,128)(2,1)S(1)}, bf16[8,576]{1,0:T(8,128)(2,1)}, u32[]{:S(2)}) copy-start(bf16[8,576]{1,0:T(8,128)(2,1)} %refs_5_.1) | copy-start | bytes 27652
  36.4 18.4 %copy-start.3 = (s32[8]{0:T(128)S(1)}, s32[8]{0:T(128)}, u32[]{:S(2)}) copy-start(s32[8]{0:T(128)} %refs_0_.3) | copy-start | bytes 100
  36.4 18.4 %copy-start.4 = (s32[8]{0:T(128)S(1)}, s32[8]{0:T(128)}, u32[]{:S(2)}) copy-start(s32[8]{0:T(128)} %refs_1_.3) | copy-start | bytes 100
  36.4 12.7 %collective-permute-start.12 = (bf16[8,96,576]{2,1,0:T(8,128)(2,1)S(1)}, bf16[8,96,576]{2,1,0:T(8,128)(2,1)S(1)}, u32[]{:S(2)}, u32[]{:S(2)}) collective-permute-start(bf16[8,96,576]{2,1,0:T(8,128)(2,1)S(1)} %copy-done), channel_id=1, source_target_pairs={{2,1},{4,3},{7,8},{8,7},{10,9},{12,11},{15,16},{16,15},{18,17},{20... | collective-permute-start | bytes 2654216 | tf_op jit(solution)/shard_map/ppermute | solution.py:47
  41.3 1.8 %collective-permute-start.10 = (bf16[32,7168]{1,0:T(8,128)(2,1)S(1)}, bf16[32,7168]{1,0:T(8,128)(2,1)S(1)}, u32[]{:S(2)}, u32[]{:S(2)}) collective-permute-start(bf16[32,7168]{1,0:T(8,128)(2,1)S(1)} %collective-permute-done.5.refs_2_), channel_id=1, source_target_pairs={{0,1},{1,0},{2,3},{3,2},{4,5},{5,4},{6,7},{7,6},{8,9},{9,8},{10,11... | collective-permute-start | bytes 1376264 | tf_op jit(solution)/shard_map/ppermute | solution.py:26
  41.3 2.5 %collective-permute-start.11 = (bf16[32,7168]{1,0:T(8,128)(2,1)S(1)}, bf16[32,7168]{1,0:T(8,128)(2,1)S(1)}, u32[]{:S(2)}, u32[]{:S(2)}) collective-permute-start(bf16[32,7168]{1,0:T(8,128)(2,1)S(1)} %collective-permute-done.6.refs_3_), channel_id=1, source_target_pairs={{0,1},{1,0},{2,3},{3,2},{4,5},{5,4},{6,7},{7,6},{8,9},{9,8},{10,11... | collective-permute-start | bytes 1376264 | tf_op jit(solution)/shard_map/ppermute | solution.py:26
  49.1 4.0 %collective-permute-start.13 = (bf16[32,7168]{1,0:T(8,128)(2,1)S(1)}, bf16[32,7168]{1,0:T(8,128)(2,1)S(1)}, u32[]{:S(2)}, u32[]{:S(2)}) collective-permute-start(bf16[32,7168]{1,0:T(8,128)(2,1)S(1)} %get-tuple-element.67), channel_id=1, source_target_pairs={{0,1},{1,0},{2,3},{3,2},{4,5},{5,4},{6,7},{7,6},{8,9},{9,8},{10,11... | collective-permute-start | bytes 1376264 | tf_op jit(solution)/shard_map/ppermute | solution.py:26
  51.6 8.2 %collective-permute-start.16 = (bf16[32,7168]{1,0:T(8,128)(2,1)S(1)}, bf16[32,7168]{1,0:T(8,128)(2,1)S(1)}, u32[]{:S(2)}, u32[]{:S(2)}) collective-permute-start(bf16[32,7168]{1,0:T(8,128)(2,1)S(1)} %get-tuple-element.76), channel_id=1, source_target_pairs={{0,1},{1,0},{2,3},{3,2},{4,5},{5,4},{6,7},{7,6},{8,9},{9,8},{10,11... | collective-permute-start | bytes 1376264 | tf_op jit(solution)/shard_map/ppermute | solution.py:26
  51.6 8.2 %collective-permute-start.15 = (bf16[64,7168]{1,0:T(8,128)(2,1)S(1)}, bf16[64,7168]{1,0:T(8,128)(2,1)S(1)}, u32[]{:S(2)}, u32[]{:S(2)}) collective-permute-start(bf16[64,7168]{1,0:T(8,128)(2,1)S(1)} %get-tuple-element.75), channel_id=1, source_target_pairs={{0,1},{1,0},{2,3},{3,2},{4,5},{5,4},{6,7},{7,6},{8,9},{9,8},{10,11... | collective-permute-start | bytes 2752520 | tf_op jit(solution)/shard_map/ppermute | solution.py:26
  53.2 6.7 %collective-permute-start.14 = (bf16[32,4480]{1,0:T(8,128)(2,1)S(1)}, bf16[32,4480]{1,0:T(8,128)(2,1)S(1)}, u32[]{:S(2)}, u32[]{:S(2)}) collective-permute-start(bf16[32,4480]{1,0:T(8,128)(2,1)S(1)} %add_convert_fusion.2), channel_id=1, source_target_pairs={{0,2},{1,5},{2,0},{3,7},{4,6},{5,1},{6,4},{7,3},{8,10},{9,13},{10,... | collective-permute-start | bytes 860168 | tf_op jit(solution)/shard_map/ppermute | solution.py:26
  60.0 9.8 %collective-permute-start.18 = (bf16[32,4480]{1,0:T(8,128)(2,1)S(1)}, bf16[32,4480]{1,0:T(8,128)(2,1)S(1)}, u32[]{:S(2)}, u32[]{:S(2)}) collective-permute-start(bf16[32,4480]{1,0:T(8,128)(2,1)S(1)} %get-tuple-element.78), channel_id=1, source_target_pairs={{0,4},{1,3},{2,6},{3,1},{4,0},{5,7},{6,2},{7,5},{8,12},{9,11},{10,... | collective-permute-start | bytes 860168 | tf_op jit(solution)/shard_map/ppermute | solution.py:26
  61.3 8.5 %collective-permute-start.17 = (bf16[32,4480]{1,0:T(8,128)(2,1)S(1)}, bf16[32,4480]{1,0:T(8,128)(2,1)S(1)}, u32[]{:S(2)}, u32[]{:S(2)}) collective-permute-start(bf16[32,4480]{1,0:T(8,128)(2,1)S(1)} %get-tuple-element.107), channel_id=1, source_target_pairs={{0,2},{1,5},{2,0},{3,7},{4,6},{5,1},{6,4},{7,3},{8,10},{9,13},{10,... | collective-permute-start | bytes 860168 | tf_op jit(solution)/shard_map/ppermute | solution.py:26
  63.4 6.8 %collective-permute-start.19 = (bf16[32,2688]{1,0:T(8,128)(2,1)S(1)}, bf16[32,2688]{1,0:T(8,128)(2,1)S(1)}, u32[]{:S(2)}, u32[]{:S(2)}) collective-permute-start(bf16[32,2688]{1,0:T(8,128)(2,1)S(1)} %add_convert_fusion.5), channel_id=1, source_target_pairs={{0,2},{1,5},{2,0},{3,7},{4,6},{5,1},{6,4},{7,3},{8,10},{9,13},{10,... | collective-permute-start | bytes 516104 | tf_op jit(solution)/shard_map/ppermute | solution.py:26
  70.3 7.7 %collective-permute-start.23 = (bf16[32,2688]{1,0:T(8,128)(2,1)S(1)}, bf16[32,2688]{1,0:T(8,128)(2,1)S(1)}, u32[]{:S(2)}, u32[]{:S(2)}) collective-permute-start(bf16[32,2688]{1,0:T(8,128)(2,1)S(1)} %get-tuple-element.105), channel_id=1, source_target_pairs={{0,2},{1,5},{2,0},{3,7},{4,6},{5,1},{6,4},{7,3},{8,10},{9,13},{10,... | collective-permute-start | bytes 516104 | tf_op jit(solution)/shard_map/ppermute | solution.py:26
  72.0 6.0 %collective-permute-start.24 = (bf16[32,2688]{1,0:T(8,128)(2,1)S(1)}, bf16[32,2688]{1,0:T(8,128)(2,1)S(1)}, u32[]{:S(2)}, u32[]{:S(2)}) collective-permute-start(bf16[32,2688]{1,0:T(8,128)(2,1)S(1)} %get-tuple-element.106), channel_id=1, source_target_pairs={{0,4},{1,3},{2,6},{3,1},{4,0},{5,7},{6,2},{7,5},{8,12},{9,11},{10,... | collective-permute-start | bytes 516104 | tf_op jit(solution)/shard_map/ppermute | solution.py:26
  73.6 9.2 %collective-permute-start.20 = (bf16[8,4480]{1,0:T(8,128)(2,1)S(1)}, bf16[8,4480]{1,0:T(8,128)(2,1)S(1)}, u32[]{:S(2)}, u32[]{:S(2)}) collective-permute-start(bf16[8,4480]{1,0:T(8,128)(2,1)S(1)} %get-tuple-element.82), channel_id=1, source_target_pairs={{0,8},{1,9},{2,10},{3,11},{4,12},{5,13},{6,14},{7,15},{8,0},{9,1},... | collective-permute-start | bytes 215048 | tf_op jit(solution)/shard_map/ppermute | solution.py:26
  74.3 9.2 %collective-permute-start.21 = (bf16[8,4480]{1,0:T(8,128)(2,1)S(1)}, bf16[8,4480]{1,0:T(8,128)(2,1)S(1)}, u32[]{:S(2)}, u32[]{:S(2)}) collective-permute-start(bf16[8,4480]{1,0:T(8,128)(2,1)S(1)} %get-tuple-element.84), channel_id=1, source_target_pairs={{0,16},{1,17},{2,18},{3,19},{4,20},{5,21},{6,22},{7,23},{8,24},{9,... | collective-permute-start | bytes 215048 | tf_op jit(solution)/shard_map/ppermute | solution.py:26
  77.5 6.6 %collective-permute-start.22 = (bf16[8,4480]{1,0:T(8,128)(2,1)S(1)}, bf16[8,4480]{1,0:T(8,128)(2,1)S(1)}, u32[]{:S(2)}, u32[]{:S(2)}) collective-permute-start(bf16[8,4480]{1,0:T(8,128)(2,1)S(1)} %get-tuple-element.86), channel_id=1, source_target_pairs={{0,24},{1,25},{2,26},{3,27},{4,28},{5,29},{6,30},{7,31},{8,16},{9,... | collective-permute-start | bytes 215048 | tf_op jit(solution)/shard_map/ppermute | solution.py:26
  78.1 6.8 %collective-permute-start.27 = (bf16[8,2688]{1,0:T(8,128)(2,1)S(1)}, bf16[8,2688]{1,0:T(8,128)(2,1)S(1)}, u32[]{:S(2)}, u32[]{:S(2)}) collective-permute-start(bf16[8,2688]{1,0:T(8,128)(2,1)S(1)} %get-tuple-element.101), channel_id=1, source_target_pairs={{0,24},{1,25},{2,26},{3,27},{4,28},{5,29},{6,30},{7,31},{8,16},{9,... | collective-permute-start | bytes 129032 | tf_op jit(solution)/shard_map/ppermute | solution.py:26
  82.9 5.6 %collective-permute-start.26 = (bf16[8,2688]{1,0:T(8,128)(2,1)S(1)}, bf16[8,2688]{1,0:T(8,128)(2,1)S(1)}, u32[]{:S(2)}, u32[]{:S(2)}) collective-permute-start(bf16[8,2688]{1,0:T(8,128)(2,1)S(1)} %get-tuple-element.102), channel_id=1, source_target_pairs={{0,16},{1,17},{2,18},{3,19},{4,20},{5,21},{6,22},{7,23},{8,24},{9,... | collective-permute-start | bytes 129032 | tf_op jit(solution)/shard_map/ppermute | solution.py:26
  82.9 5.6 %collective-permute-start.25 = (bf16[8,2688]{1,0:T(8,128)(2,1)S(1)}, bf16[8,2688]{1,0:T(8,128)(2,1)S(1)}, u32[]{:S(2)}, u32[]{:S(2)}) collective-permute-start(bf16[8,2688]{1,0:T(8,128)(2,1)S(1)} %get-tuple-element.103), channel_id=1, source_target_pairs={{0,8},{1,9},{2,10},{3,11},{4,12},{5,13},{6,14},{7,15},{8,0},{9,1},... | collective-permute-start | bytes 129032 | tf_op jit(solution)/shard_map/ppermute | solution.py:26
  88.6 0.6 copy-start.5

commit v15 on v13

--- a/solution.py
+++ b/solution.py
@@ -261,7 +261,9 @@
     early, _ = cache_rows("early", 0, beam_count)
     height = expert_count * capacity
     rows = jnp.pad(column[0], ((0, height - capacity), (0, 0)))
+    column = column[::-1]
     rows, column, early, mixing = tied(rows, column, early, mixing)
+    column = column[::-1]
     pieces.append(early)
     for r in range(1, expert_count):
         rows = lax.dynamic_update_slice(rows, column[r], (r * capacity, 0))
@@ -287,7 +289,7 @@
     low = swapped(low, twin)
     height = expert_count * capacity
 
-    cut = 128 * (5 * width // 1024)
+    cut = 128 * (15 * width // 3584)
     halves = [(0, cut), (cut, width)]
 
     def block(value, j, half):
@@ -310,9 +312,11 @@
         ]
 
     def back(share):
-        return [
-            swapped(share[r].astype(jnp.bfloat16), ahead(r)) for r in range(1, expert_count)
+        sent = [
+            swapped(share[r].astype(jnp.bfloat16), ahead(r))
+            for r in reversed(range(1, expert_count))
         ]
+        return sent[::-1]
 
     across, pieces[1] = tied(to_second(halves[0]), pieces[1])
     across = swapped(across, second)
@@ -334,7 +338,8 @@
     for value in values:
         value = [v.astype(jnp.float32) for v in value]
         if dense:
-            total = sum(mixing[r][:, None] * value[r] for r in range(expert_count))
+            order = [0, *range(expert_count - 1, 0, -1)]
+            total = sum(mixing[r][:, None] * value[r] for r in order)
         else:
             total = jnp.dot(
                 mixing,

time: 88.7 us -> 87.8 us (0.990)
  waiting for transfers between devices: 32.1 us -> 30.6 us
    ppermute x26, waiting for transfers between devices: 32 us -> 30.6 us  [swapped(): return lax.ppermute(value, 'dp', [(i, partner(i)) for i in range(peers)])]
where the time goes in v15:
time: 87.8 us; the launch traced here: 87.6 us
  starting transfers between devices  37.9 us (43%)
  waiting for transfers between devices  30.6 us (35%)
  Pallas kernels  11.8 us (13%)
  other arithmetic  4.77 us (5%)
  local copies, waits for them, and re-layouts  1.59 us (2%)
    ppermute x26, starting transfers between devices, swapped(): return lax.ppermute(value, 'dp', [(i, partner(i)) for i in range(peers)])  36.3 us
    ppermute x26, waiting for transfers between devices, swapped(): return lax.ppermute(value, 'dp', [(i, partner(i)) for i in range(peers)])  30.6 us
    pallas_call x1, Pallas kernels, experts(): pl.pallas_call(lambda *refs: expert_kernel(wide, *refs), in_specs=[whole]...  5.3 us
    pallas_call x1, Pallas kernels, fetched(): pl.pallas_call(fetch_kernel, in_specs=[pl.BlockSpec(memory_space=pltpu.HB...  4.23 us
    reduce_sum x1, other arithmetic, body(): jnp.sum(jnp.where(routed_experts == targets[r], route_weights, 0.0), axis=1)  3.26 us
    pallas_call x1, Pallas kernels, attend(): pl.pallas_call(lambda *refs: attend_kernel(spans, *refs), in_specs=[scala...  2.3 us
  transfers between devices with their start and end apart: 28, of which 15 were waited for; matrix products, arithmetic and copies ran while one was open for 6% of the time, Pallas kernels for 13%

profile of v15, /device:TPU:0, one launch (start us, length us, event | category | flops | bytes accessed | tf_op | source)
XLA Modules:
  0.0 87.6 jit_solution(7446303790631523111)
XLA Ops:
  0.6 0.7 collective-permute-start.3
  1.4 4.1 %collective-permute-start.1 = (bf16[8,7168]{1,0:T(8,128)(2,1)}, bf16[8,7168]{1,0:T(8,128)(2,1)S(1)}, u32[]{:S(2)}, u32[]{:S(2)}) collective-permute-start(bf16[8,7168]{1,0:T(8,128)(2,1)} %param.16), channel_id=1, source_target_pairs={{0,16},{1,17},{2,18},{3,19},{4,20},{5,21},{6,22},{7,23},{8,24},{9,... | collective-permute-start | bytes 344072 | tf_op jit(solution)/shard_map/ppermute | solution.py:26
  5.5 1.3 %collective-permute-start = (bf16[8,7168]{1,0:T(8,128)(2,1)}, bf16[8,7168]{1,0:T(8,128)(2,1)S(1)}, u32[]{:S(2)}, u32[]{:S(2)}) collective-permute-start(bf16[8,7168]{1,0:T(8,128)(2,1)} %param.16), channel_id=1, source_target_pairs={{0,24},{1,25},{2,26},{3,27},{4,28},{5,29},{6,30},{7,31},{8,16},{9,... | collective-permute-start | bytes 344072 | tf_op jit(solution)/shard_map/ppermute | solution.py:26
  6.8 0.2 collective-permute-start.2
  7.0 0.6 fusion.4
  7.7 0.9 %pad.4 = bf16[32,7168]{1,0:T(8,128)(2,1)S(1)} pad(bf16[8,7168]{1,0:T(8,128)(2,1)} %param.16, bf16[]{:T(256)} %constant.19.clone.1), padding=0_24x0_0 | pad | bytes 573442 | tf_op jit(solution)/shard_map/jit(_pad)/pad | solution.py:263
  8.6 3.3 %fusion.3 = (f32[8]{0:T(128)S(1)}, f32[8]{0:T(128)S(1)}, f32[8]{0:T(128)S(1)}, f32[8]{0:T(128)S(1)}) fusion(f32[8,2]{0,1:T(2,128)} %param.18, s32[8,2]{0,1:T(2,128)} %param.17, s32[]{:T(128)} %bitcast.3, s32[]{:T(128)} %bitcast.1, s32[]{:T(128)} %bitcast, s32[]{:T(128)} %bitcast.2), kind=kLoop, calls=%fused_computation.23 | loop fusion | flops 160 | bytes 272 | tf_op jit(solution)/shard_map/reduce_sum | solution.py:226
  11.9 1.4 %collective-permute-done = bf16[8,7168]{1,0:T(8,128)(2,1)S(1)} collective-permute-done((bf16[8,7168]{1,0:T(8,128)(2,1)}, bf16[8,7168]{1,0:T(8,128)(2,1)S(1)}, u32[]{:S(2)}, u32[]{:S(2)}) %collective-permute-start) | collective-permute-done | bytes 114720 | tf_op jit(solution)/shard_map/ppermute | solution.py:26
  13.3 1.2 %collective-permute-done.2 = bf16[8,7168]{1,0:T(8,128)(2,1)S(1)} collective-permute-done((bf16[8,7168]{1,0:T(8,128)(2,1)}, bf16[8,7168]{1,0:T(8,128)(2,1)S(1)}, u32[]{:S(2)}, u32[]{:S(2)}) %collective-permute-start.2) | collective-permute-done | bytes 114720 | tf_op jit(solution)/shard_map/ppermute | solution.py:26
  14.6 5.7 %collective-permute-start.4 = (bf16[32,7168]{1,0:T(8,128)(2,1)S(1)}, bf16[32,7168]{1,0:T(8,128)(2,1)S(1)}, u32[]{:S(2)}, u32[]{:S(2)}) collective-permute-start(bf16[32,7168]{1,0:T(8,128)(2,1)S(1)} %constant_dynamic-update-slice_fusion.refs_0_), channel_id=1, source_target_pairs={{0,4},{1,3},{2,6},{3,1},{4,0},{5,7},{6,2},{7,5},{8,12},{9,11},{10,... | collective-permute-start | bytes 1376264 | tf_op jit(solution)/shard_map/ppermute | solution.py:26
  20.3 0.5 collective-permute-start.7
  20.8 5.9 %collective-permute-done.4.refs_1_ = bf16[32,7168]{1,0:T(8,128)(2,1)S(1)} collective-permute-done((bf16[32,7168]{1,0:T(8,128)(2,1)S(1)}, bf16[32,7168]{1,0:T(8,128)(2,1)S(1)}, u32[]{:S(2)}, u32[]{:S(2)}) %collective-permute-start.4) | collective-permute-done | bytes 458784 | tf_op jit(solution)/shard_map/ppermute | solution.py:26
  26.7 1.1 %collective-permute-start.6 = (bf16[32,7168]{1,0:T(8,128)(2,1)S(1)}, bf16[32,7168]{1,0:T(8,128)(2,1)S(1)}, u32[]{:S(2)}, u32[]{:S(2)}) collective-permute-start(bf16[32,7168]{1,0:T(8,128)(2,1)S(1)} %collective-permute-done.4.refs_1_), channel_id=1, source_target_pairs={{0,2},{1,5},{2,0},{3,7},{4,6},{5,1},{6,4},{7,3},{8,10},{9,13},{10,... | collective-permute-start | bytes 1376264 | tf_op jit(solution)/shard_map/ppermute | solution.py:26
  27.8 0.9 %collective-permute-start.5 = (bf16[32,7168]{1,0:T(8,128)(2,1)S(1)}, bf16[32,7168]{1,0:T(8,128)(2,1)S(1)}, u32[]{:S(2)}, u32[]{:S(2)}) collective-permute-start(bf16[32,7168]{1,0:T(8,128)(2,1)S(1)} %constant_dynamic-update-slice_fusion.refs_0_), channel_id=1, source_target_pairs={{0,2},{1,5},{2,0},{3,7},{4,6},{5,1},{6,4},{7,3},{8,10},{9,13},{10,... | collective-permute-start | bytes 1376264 | tf_op jit(solution)/shard_map/ppermute | solution.py:26
  28.7 4.2 %shard_map.122 = (bf16[1,7168,256]{2,1,0:T(8,128)(2,1)S(1)}, bf16[1,7168,256]{2,1,0:T(8,128)(2,1)S(1)}, bf16[1,256,7168]{2,1,0:T(8,128)(2,1)S(1)}) custom-call(bf16[1,7168,256]{2,1,0:T(8,128)(2,1)} %refs_0_.2, bf16[1,7168,256]{2,1,0:T(8,128)(2,1)} %refs_1_.2, bf16[1,256,7168]{2,1,0:T(8,128)(2,1)} %refs_2_.2), custom_call_target="tpu_custom_call" | custom-call | bytes 22020096 | tf_op jit(solution)/shard_map/pallas_call | solution.py:127
  33.0 2.2 %collective-permute-done.6.refs_3_ = bf16[32,7168]{1,0:T(8,128)(2,1)S(1)} collective-permute-done((bf16[32,7168]{1,0:T(8,128)(2,1)S(1)}, bf16[32,7168]{1,0:T(8,128)(2,1)S(1)}, u32[]{:S(2)}, u32[]{:S(2)}) %collective-permute-start.6) | collective-permute-done | bytes 458784 | tf_op jit(solution)/shard_map/ppermute | solution.py:26
  35.2 0.9 collective-permute-start.12
  36.1 4.0 %collective-permute-done.5.refs_2_ = bf16[32,7168]{1,0:T(8,128)(2,1)S(1)} collective-permute-done((bf16[32,7168]{1,0:T(8,128)(2,1)S(1)}, bf16[32,7168]{1,0:T(8,128)(2,1)S(1)}, u32[]{:S(2)}, u32[]{:S(2)}) %collective-permute-start.5) | collective-permute-done | bytes 458784 | tf_op jit(solution)/shard_map/ppermute | solution.py:26
  40.1 0.5 collective-permute-start.11
  40.6 1.3 %collective-permute-done.10.refs_6_ = bf16[32,7168]{1,0:T(8,128)(2,1)S(1)} collective-permute-done((bf16[32,7168]{1,0:T(8,128)(2,1)S(1)}, bf16[32,7168]{1,0:T(8,128)(2,1)S(1)}, u32[]{:S(2)}, u32[]{:S(2)}) %collective-permute-start.10) | collective-permute-done | bytes 458784 | tf_op jit(solution)/shard_map/ppermute | solution.py:26
  41.9 0.7 collective-permute-done.11.refs_7_
  42.6 5.3 %shard_map.123 = (bf16[128,7168]{1,0:T(8,128)(2,1)S(1)}, bf16[64,7168]{1,0:T(8,128)(2,1)S(1)}, bf16[32,7168]{1,0:T(8,128)(2,1)S(1)}, bf16[32,7168]{1,0:T(8,128)(2,1)S(1)}) custom-call(bf16[32,7168]{1,0:T(8,128)(2,1)S(1)} %constant_dynamic-update-slice_fusion.refs_0_, bf16[32,7168]{1,0:T(8,128)(2,1)S(1)} %collective-permute-done.4.refs_1_, ...), custom_call_target="tpu_custom_call" | custom-call | flops 2818572288 | bytes 18350080 | tf_op jit(solution)/shard_map/pallas_call | solution.py:180
  47.9 2.8 %collective-permute-start.13 = (bf16[32,7168]{1,0:T(8,128)(2,1)S(1)}, bf16[32,7168]{1,0:T(8,128)(2,1)S(1)}, u32[]{:S(2)}, u32[]{:S(2)}) collective-permute-start(bf16[32,7168]{1,0:T(8,128)(2,1)S(1)} %get-tuple-element.62), channel_id=1, source_target_pairs={{0,1},{1,0},{2,3},{3,2},{4,5},{5,4},{6,7},{7,6},{8,9},{9,8},{10,11... | collective-permute-start | bytes 1376264 | tf_op jit(solution)/shard_map/ppermute | solution.py:26
  50.7 0.5 collective-permute-start.15
  51.2 0.9 %collective-permute-done.13 = bf16[32,7168]{1,0:T(8,128)(2,1)S(1)} collective-permute-done((bf16[32,7168]{1,0:T(8,128)(2,1)S(1)}, bf16[32,7168]{1,0:T(8,128)(2,1)S(1)}, u32[]{:S(2)}, u32[]{:S(2)}) %collective-permute-start.13) | collective-permute-done | bytes 458784 | tf_op jit(solution)/shard_map/ppermute | solution.py:26
  52.2 1.9 %collective-permute-start.14 = (bf16[32,3840]{1,0:T(8,128)(2,1)S(1)}, bf16[32,3840]{1,0:T(8,128)(2,1)S(1)}, u32[]{:S(2)}, u32[]{:S(2)}) collective-permute-start(bf16[32,3840]{1,0:T(8,128)(2,1)S(1)} %add_convert_fusion.2), channel_id=1, source_target_pairs={{0,2},{1,5},{2,0},{3,7},{4,6},{5,1},{6,4},{7,3},{8,10},{9,13},{10,... | collective-permute-start | bytes 737288 | tf_op jit(solution)/shard_map/ppermute | solution.py:26
  54.2 2.3 %shard_map.124 = bf16[8,64,512]{2,1,0:T(8,128)(2,1)} custom-call(s32[8]{0:T(128)S(1)} %copy-done.3, s32[8]{0:T(128)S(1)} %copy-done.4, bf16[8,64,576]{2,1,0:T(8,128)(2,1)S(1)} %copy-done.1, bf16[8,96,576]{2,1,0:T(8,128)(2,1)S(1)} %copy-done, bf16[8,96,576]{2,1,0:T(8,128)(2,1)S(1)} %collective-permute-done.9.refs_4_, bf16[8,576]{1,0:T(8,128)(2,1)S(1)} %copy-done.2, ...), custom_call_target="tpu_custom_call" | custom-call | flops 106954752 | bytes 4653056 | tf_op jit(solution)/shard_map/pallas_call | solution.py:99
  56.5 2.0 %collective-permute-done.14 = bf16[32,3840]{1,0:T(8,128)(2,1)S(1)} collective-permute-done((bf16[32,3840]{1,0:T(8,128)(2,1)S(1)}, bf16[32,3840]{1,0:T(8,128)(2,1)S(1)}, u32[]{:S(2)}, u32[]{:S(2)}) %collective-permute-start.14) | collective-permute-done | bytes 245792 | tf_op jit(solution)/shard_map/ppermute | solution.py:26
  58.5 0.2 add_convert_fusion.1
  58.6 2.2 %collective-permute-start.18 = (bf16[32,3840]{1,0:T(8,128)(2,1)S(1)}, bf16[32,3840]{1,0:T(8,128)(2,1)S(1)}, u32[]{:S(2)}, u32[]{:S(2)}) collective-permute-start(bf16[32,3840]{1,0:T(8,128)(2,1)S(1)} %get-tuple-element.73), channel_id=1, source_target_pairs={{0,4},{1,3},{2,6},{3,1},{4,0},{5,7},{6,2},{7,5},{8,12},{9,11},{10,... | collective-permute-start | bytes 737288 | tf_op jit(solution)/shard_map/ppermute | solution.py:26
  60.8 2.0 %collective-permute-start.17 = (bf16[32,3840]{1,0:T(8,128)(2,1)S(1)}, bf16[32,3840]{1,0:T(8,128)(2,1)S(1)}, u32[]{:S(2)}, u32[]{:S(2)}) collective-permute-start(bf16[32,3840]{1,0:T(8,128)(2,1)S(1)} %get-tuple-element.96), channel_id=1, source_target_pairs={{0,2},{1,5},{2,0},{3,7},{4,6},{5,1},{6,4},{7,3},{8,10},{9,13},{10,... | collective-permute-start | bytes 737288 | tf_op jit(solution)/shard_map/ppermute | solution.py:26
  62.9 4.2 %collective-permute-done.18 = bf16[32,3840]{1,0:T(8,128)(2,1)S(1)} collective-permute-done((bf16[32,3840]{1,0:T(8,128)(2,1)S(1)}, bf16[32,3840]{1,0:T(8,128)(2,1)S(1)}, u32[]{:S(2)}, u32[]{:S(2)}) %collective-permute-start.18) | collective-permute-done | bytes 245792 | tf_op jit(solution)/shard_map/ppermute | solution.py:26
  67.3 2.0 %collective-permute-done.19 = bf16[32,3328]{1,0:T(8,128)(2,1)S(1)} collective-permute-done((bf16[32,3328]{1,0:T(8,128)(2,1)S(1)}, bf16[32,3328]{1,0:T(8,128)(2,1)S(1)}, u32[]{:S(2)}, u32[]{:S(2)}) %collective-permute-start.19) | collective-permute-done | bytes 213024 | tf_op jit(solution)/shard_map/ppermute | solution.py:26
  69.3 0.1 add_convert_fusion.4
  69.4 2.1 %collective-permute-start.23 = (bf16[32,3328]{1,0:T(8,128)(2,1)S(1)}, bf16[32,3328]{1,0:T(8,128)(2,1)S(1)}, u32[]{:S(2)}, u32[]{:S(2)}) collective-permute-start(bf16[32,3328]{1,0:T(8,128)(2,1)S(1)} %get-tuple-element.94), channel_id=1, source_target_pairs={{0,2},{1,5},{2,0},{3,7},{4,6},{5,1},{6,4},{7,3},{8,10},{9,13},{10,... | collective-permute-start | bytes 638984 | tf_op jit(solution)/shard_map/ppermute | solution.py:26
  71.5 1.2 %collective-permute-start.24 = (bf16[32,3328]{1,0:T(8,128)(2,1)S(1)}, bf16[32,3328]{1,0:T(8,128)(2,1)S(1)}, u32[]{:S(2)}, u32[]{:S(2)}) collective-permute-start(bf16[32,3328]{1,0:T(8,128)(2,1)S(1)} %get-tuple-element.95), channel_id=1, source_target_pairs={{0,4},{1,3},{2,6},{3,1},{4,0},{5,7},{6,2},{7,5},{8,12},{9,11},{10,... | collective-permute-start | bytes 638984 | tf_op jit(solution)/shard_map/ppermute | solution.py:26
  72.7 2.6 %collective-permute-start.20 = (bf16[8,3840]{1,0:T(8,128)(2,1)S(1)}, bf16[8,3840]{1,0:T(8,128)(2,1)S(1)}, u32[]{:S(2)}, u32[]{:S(2)}) collective-permute-start(bf16[8,3840]{1,0:T(8,128)(2,1)S(1)} %get-tuple-element.77), channel_id=1, source_target_pairs={{0,24},{1,25},{2,26},{3,27},{4,28},{5,29},{6,30},{7,31},{8,16},{9,... | collective-permute-start | bytes 184328 | tf_op jit(solution)/shard_map/ppermute | solution.py:26
  75.3 0.4 collective-permute-start.21
  75.7 1.3 %collective-permute-start.22 = (bf16[8,3840]{1,0:T(8,128)(2,1)S(1)}, bf16[8,3840]{1,0:T(8,128)(2,1)S(1)}, u32[]{:S(2)}, u32[]{:S(2)}) collective-permute-start(bf16[8,3840]{1,0:T(8,128)(2,1)S(1)} %get-tuple-element.81), channel_id=1, source_target_pairs={{0,8},{1,9},{2,10},{3,11},{4,12},{5,13},{6,14},{7,15},{8,0},{9,1},... | collective-permute-start | bytes 184328 | tf_op jit(solution)/shard_map/ppermute | solution.py:26
  77.1 0.3 collective-permute-done.24
  77.5 4.2 %collective-permute-start.25 = (bf16[8,3328]{1,0:T(8,128)(2,1)S(1)}, bf16[8,3328]{1,0:T(8,128)(2,1)S(1)}, u32[]{:S(2)}, u32[]{:S(2)}) collective-permute-start(bf16[8,3328]{1,0:T(8,128)(2,1)S(1)} %get-tuple-element.91), channel_id=1, source_target_pairs={{0,24},{1,25},{2,26},{3,27},{4,28},{5,29},{6,30},{7,31},{8,16},{9,... | collective-permute-start | bytes 159752 | tf_op jit(solution)/shard_map/ppermute | solution.py:26
  81.8 0.6 collective-permute-start.26
  82.3 0.1 add_convert_fusion.6
  82.5 1.6 %collective-permute-done.25 = bf16[8,3328]{1,0:T(8,128)(2,1)S(1)} collective-permute-done((bf16[8,3328]{1,0:T(8,128)(2,1)S(1)}, bf16[8,3328]{1,0:T(8,128)(2,1)S(1)}, u32[]{:S(2)}, u32[]{:S(2)}) %collective-permute-start.25) | collective-permute-done | bytes 53280 | tf_op jit(solution)/shard_map/ppermute | solution.py:26
  84.0 2.1 %collective-permute-done.27 = bf16[8,3328]{1,0:T(8,128)(2,1)S(1)} collective-permute-done((bf16[8,3328]{1,0:T(8,128)(2,1)S(1)}, bf16[8,3328]{1,0:T(8,128)(2,1)S(1)}, u32[]{:S(2)}, u32[]{:S(2)}) %collective-permute-start.27) | collective-permute-done | bytes 53280 | tf_op jit(solution)/shard_map/ppermute | solution.py:26
  86.1 0.7 collective-permute-done.26
  86.8 0.1 add_convert_fusion.7
  86.9 0.7 pad_maximum_fusion
  (38 shorter events, 0.6 us)
Async XLA Ops:
  0.6 13.9 %collective-permute-start.3 = (bf16[8,96,576]{2,1,0:T(8,128)(2,1)}, bf16[8,96,576]{2,1,0:T(8,128)(2,1)S(1)}, u32[]{:S(2)}, u32[]{:S(2)}) collective-permute-start(bf16[8,96,576]{2,1,0:T(8,128)(2,1)} %refs_3_.1), channel_id=1, source_target_pairs={{1,2},{3,4},{5,6},{6,5},{9,10},{11,12},{13,14},{14,13},{17,18},{19... | collective-permute-start | bytes 2654216 | tf_op jit(solution)/shard_map/ppermute | solution.py:47
  1.4 10.5 %collective-permute-start.1 = (bf16[8,7168]{1,0:T(8,128)(2,1)}, bf16[8,7168]{1,0:T(8,128)(2,1)S(1)}, u32[]{:S(2)}, u32[]{:S(2)}) collective-permute-start(bf16[8,7168]{1,0:T(8,128)(2,1)} %param.16), channel_id=1, source_target_pairs={{0,16},{1,17},{2,18},{3,19},{4,20},{5,21},{6,22},{7,23},{8,24},{9,... | collective-permute-start | bytes 344072 | tf_op jit(solution)/shard_map/ppermute | solution.py:26
  5.5 7.8 %collective-permute-start = (bf16[8,7168]{1,0:T(8,128)(2,1)}, bf16[8,7168]{1,0:T(8,128)(2,1)S(1)}, u32[]{:S(2)}, u32[]{:S(2)}) collective-permute-start(bf16[8,7168]{1,0:T(8,128)(2,1)} %param.16), channel_id=1, source_target_pairs={{0,24},{1,25},{2,26},{3,27},{4,28},{5,29},{6,30},{7,31},{8,16},{9,... | collective-permute-start | bytes 344072 | tf_op jit(solution)/shard_map/ppermute | solution.py:26
  6.8 7.7 %collective-permute-start.2 = (bf16[8,7168]{1,0:T(8,128)(2,1)}, bf16[8,7168]{1,0:T(8,128)(2,1)S(1)}, u32[]{:S(2)}, u32[]{:S(2)}) collective-permute-start(bf16[8,7168]{1,0:T(8,128)(2,1)} %param.16), channel_id=1, source_target_pairs={{0,8},{1,9},{2,10},{3,11},{4,12},{5,13},{6,14},{7,15},{8,0},{9,1},... | collective-permute-start | bytes 344072 | tf_op jit(solution)/shard_map/ppermute | solution.py:26
  14.6 20.6 %copy-start = (bf16[8,96,576]{2,1,0:T(8,128)(2,1)S(1)}, bf16[8,96,576]{2,1,0:T(8,128)(2,1)}, u32[]{:S(2)}) copy-start(bf16[8,96,576]{2,1,0:T(8,128)(2,1)} %refs_3_.1) | copy-start | bytes 2654212
  14.6 12.1 %collective-permute-start.4 = (bf16[32,7168]{1,0:T(8,128)(2,1)S(1)}, bf16[32,7168]{1,0:T(8,128)(2,1)S(1)}, u32[]{:S(2)}, u32[]{:S(2)}) collective-permute-start(bf16[32,7168]{1,0:T(8,128)(2,1)S(1)} %constant_dynamic-update-slice_fusion.refs_0_), channel_id=1, source_target_pairs={{0,4},{1,3},{2,6},{3,1},{4,0},{5,7},{6,2},{7,5},{8,12},{9,11},{10,... | collective-permute-start | bytes 1376264 | tf_op jit(solution)/shard_map/ppermute | solution.py:26
  20.2 12.7 %collective-permute-start.9 = (bf16[8,96,576]{2,1,0:T(8,128)(2,1)}, bf16[8,96,576]{2,1,0:T(8,128)(2,1)S(1)}, u32[]{:S(2)}, u32[]{:S(2)}) collective-permute-start(bf16[8,96,576]{2,1,0:T(8,128)(2,1)} %refs_3_.1), channel_id=1, source_target_pairs={{0,1},{1,0},{2,3},{3,2},{4,5},{5,4},{6,7},{7,6},{8,9},{9,8},{10,11... | collective-permute-start | bytes 2654216 | tf_op jit(solution)/shard_map/ppermute | solution.py:26
  20.3 12.7 %collective-permute-start.7 = (bf16[32,7168]{1,0:T(8,128)(2,1)S(1)}, bf16[32,7168]{1,0:T(8,128)(2,1)S(1)}, u32[]{:S(2)}, u32[]{:S(2)}) collective-permute-start(bf16[32,7168]{1,0:T(8,128)(2,1)S(1)} %constant_dynamic-update-slice_fusion.refs_0_), channel_id=1, source_target_pairs={{0,1},{1,0},{2,3},{3,2},{4,5},{5,4},{6,7},{7,6},{8,9},{9,8},{10,11... | collective-permute-start | bytes 1376264 | tf_op jit(solution)/shard_map/ppermute | solution.py:26
  26.7 6.3 %collective-permute-start.8 = (bf16[32,7168]{1,0:T(8,128)(2,1)S(1)}, bf16[32,7168]{1,0:T(8,128)(2,1)S(1)}, u32[]{:S(2)}, u32[]{:S(2)}) collective-permute-start(bf16[32,7168]{1,0:T(8,128)(2,1)S(1)} %collective-permute-done.4.refs_1_), channel_id=1, source_target_pairs={{0,1},{1,0},{2,3},{3,2},{4,5},{5,4},{6,7},{7,6},{8,9},{9,8},{10,11... | collective-permute-start | bytes 1376264 | tf_op jit(solution)/shard_map/ppermute | solution.py:26
  26.7 8.5 %collective-permute-start.6 = (bf16[32,7168]{1,0:T(8,128)(2,1)S(1)}, bf16[32,7168]{1,0:T(8,128)(2,1)S(1)}, u32[]{:S(2)}, u32[]{:S(2)}) collective-permute-start(bf16[32,7168]{1,0:T(8,128)(2,1)S(1)} %collective-permute-done.4.refs_1_), channel_id=1, source_target_pairs={{0,2},{1,5},{2,0},{3,7},{4,6},{5,1},{6,4},{7,3},{8,10},{9,13},{10,... | collective-permute-start | bytes 1376264 | tf_op jit(solution)/shard_map/ppermute | solution.py:26
  27.8 12.3 %collective-permute-start.5 = (bf16[32,7168]{1,0:T(8,128)(2,1)S(1)}, bf16[32,7168]{1,0:T(8,128)(2,1)S(1)}, u32[]{:S(2)}, u32[]{:S(2)}) collective-permute-start(bf16[32,7168]{1,0:T(8,128)(2,1)S(1)} %constant_dynamic-update-slice_fusion.refs_0_), channel_id=1, source_target_pairs={{0,2},{1,5},{2,0},{3,7},{4,6},{5,1},{6,4},{7,3},{8,10},{9,13},{10,... | collective-permute-start | bytes 1376264 | tf_op jit(solution)/shard_map/ppermute | solution.py:26
  35.2 18.9 %copy-start.1 = (bf16[8,64,576]{2,1,0:T(8,128)(2,1)S(1)}, bf16[8,64,576]{2,1,0:T(8,128)(2,1)}, u32[]{:S(2)}) copy-start(bf16[8,64,576]{2,1,0:T(8,128)(2,1)} %refs_2_.3) | copy-start | bytes 1769476
  35.2 19.0 %copy-start.2 = (bf16[8,576]{1,0:T(8,128)(2,1)S(1)}, bf16[8,576]{1,0:T(8,128)(2,1)}, u32[]{:S(2)}) copy-start(bf16[8,576]{1,0:T(8,128)(2,1)} %refs_5_.1) | copy-start | bytes 27652
  35.2 19.0 %copy-start.3 = (s32[8]{0:T(128)S(1)}, s32[8]{0:T(128)}, u32[]{:S(2)}) copy-start(s32[8]{0:T(128)} %refs_0_.3) | copy-start | bytes 100
  35.2 19.0 %copy-start.4 = (s32[8]{0:T(128)S(1)}, s32[8]{0:T(128)}, u32[]{:S(2)}) copy-start(s32[8]{0:T(128)} %refs_1_.3) | copy-start | bytes 100
  35.2 12.7 %collective-permute-start.12 = (bf16[8,96,576]{2,1,0:T(8,128)(2,1)S(1)}, bf16[8,96,576]{2,1,0:T(8,128)(2,1)S(1)}, u32[]{:S(2)}, u32[]{:S(2)}) collective-permute-start(bf16[8,96,576]{2,1,0:T(8,128)(2,1)S(1)} %copy-done), channel_id=1, source_target_pairs={{2,1},{4,3},{7,8},{8,7},{10,9},{12,11},{15,16},{16,15},{18,17},{20... | collective-permute-start | bytes 2654216 | tf_op jit(solution)/shard_map/ppermute | solution.py:47
  40.1 1.8 %collective-permute-start.10 = (bf16[32,7168]{1,0:T(8,128)(2,1)S(1)}, bf16[32,7168]{1,0:T(8,128)(2,1)S(1)}, u32[]{:S(2)}, u32[]{:S(2)}) collective-permute-start(bf16[32,7168]{1,0:T(8,128)(2,1)S(1)} %collective-permute-done.5.refs_2_), channel_id=1, source_target_pairs={{0,1},{1,0},{2,3},{3,2},{4,5},{5,4},{6,7},{7,6},{8,9},{9,8},{10,11... | collective-permute-start | bytes 1376264 | tf_op jit(solution)/shard_map/ppermute | solution.py:26
  40.1 2.5 %collective-permute-start.11 = (bf16[32,7168]{1,0:T(8,128)(2,1)S(1)}, bf16[32,7168]{1,0:T(8,128)(2,1)S(1)}, u32[]{:S(2)}, u32[]{:S(2)}) collective-permute-start(bf16[32,7168]{1,0:T(8,128)(2,1)S(1)} %collective-permute-done.6.refs_3_), channel_id=1, source_target_pairs={{0,1},{1,0},{2,3},{3,2},{4,5},{5,4},{6,7},{7,6},{8,9},{9,8},{10,11... | collective-permute-start | bytes 1376264 | tf_op jit(solution)/shard_map/ppermute | solution.py:26
  47.9 4.2 %collective-permute-start.13 = (bf16[32,7168]{1,0:T(8,128)(2,1)S(1)}, bf16[32,7168]{1,0:T(8,128)(2,1)S(1)}, u32[]{:S(2)}, u32[]{:S(2)}) collective-permute-start(bf16[32,7168]{1,0:T(8,128)(2,1)S(1)} %get-tuple-element.62), channel_id=1, source_target_pairs={{0,1},{1,0},{2,3},{3,2},{4,5},{5,4},{6,7},{7,6},{8,9},{9,8},{10,11... | collective-permute-start | bytes 1376264 | tf_op jit(solution)/shard_map/ppermute | solution.py:26
  50.7 7.8 %collective-permute-start.16 = (bf16[32,7168]{1,0:T(8,128)(2,1)S(1)}, bf16[32,7168]{1,0:T(8,128)(2,1)S(1)}, u32[]{:S(2)}, u32[]{:S(2)}) collective-permute-start(bf16[32,7168]{1,0:T(8,128)(2,1)S(1)} %get-tuple-element.71), channel_id=1, source_target_pairs={{0,1},{1,0},{2,3},{3,2},{4,5},{5,4},{6,7},{7,6},{8,9},{9,8},{10,11... | collective-permute-start | bytes 1376264 | tf_op jit(solution)/shard_map/ppermute | solution.py:26
  50.7 7.8 %collective-permute-start.15 = (bf16[64,7168]{1,0:T(8,128)(2,1)S(1)}, bf16[64,7168]{1,0:T(8,128)(2,1)S(1)}, u32[]{:S(2)}, u32[]{:S(2)}) collective-permute-start(bf16[64,7168]{1,0:T(8,128)(2,1)S(1)} %get-tuple-element.70), channel_id=1, source_target_pairs={{0,1},{1,0},{2,3},{3,2},{4,5},{5,4},{6,7},{7,6},{8,9},{9,8},{10,11... | collective-permute-start | bytes 2752520 | tf_op jit(solution)/shard_map/ppermute | solution.py:26
  52.2 6.3 %collective-permute-start.14 = (bf16[32,3840]{1,0:T(8,128)(2,1)S(1)}, bf16[32,3840]{1,0:T(8,128)(2,1)S(1)}, u32[]{:S(2)}, u32[]{:S(2)}) collective-permute-start(bf16[32,3840]{1,0:T(8,128)(2,1)S(1)} %add_convert_fusion.2), channel_id=1, source_target_pairs={{0,2},{1,5},{2,0},{3,7},{4,6},{5,1},{6,4},{7,3},{8,10},{9,13},{10,... | collective-permute-start | bytes 737288 | tf_op jit(solution)/shard_map/ppermute | solution.py:26
  58.6 8.5 %collective-permute-start.18 = (bf16[32,3840]{1,0:T(8,128)(2,1)S(1)}, bf16[32,3840]{1,0:T(8,128)(2,1)S(1)}, u32[]{:S(2)}, u32[]{:S(2)}) collective-permute-start(bf16[32,3840]{1,0:T(8,128)(2,1)S(1)} %get-tuple-element.73), channel_id=1, source_target_pairs={{0,4},{1,3},{2,6},{3,1},{4,0},{5,7},{6,2},{7,5},{8,12},{9,11},{10,... | collective-permute-start | bytes 737288 | tf_op jit(solution)/shard_map/ppermute | solution.py:26
  60.8 6.3 %collective-permute-start.17 = (bf16[32,3840]{1,0:T(8,128)(2,1)S(1)}, bf16[32,3840]{1,0:T(8,128)(2,1)S(1)}, u32[]{:S(2)}, u32[]{:S(2)}) collective-permute-start(bf16[32,3840]{1,0:T(8,128)(2,1)S(1)} %get-tuple-element.96), channel_id=1, source_target_pairs={{0,2},{1,5},{2,0},{3,7},{4,6},{5,1},{6,4},{7,3},{8,10},{9,13},{10,... | collective-permute-start | bytes 737288 | tf_op jit(solution)/shard_map/ppermute | solution.py:26
  62.8 6.5 %collective-permute-start.19 = (bf16[32,3328]{1,0:T(8,128)(2,1)S(1)}, bf16[32,3328]{1,0:T(8,128)(2,1)S(1)}, u32[]{:S(2)}, u32[]{:S(2)}) collective-permute-start(bf16[32,3328]{1,0:T(8,128)(2,1)S(1)} %add_convert_fusion.5), channel_id=1, source_target_pairs={{0,2},{1,5},{2,0},{3,7},{4,6},{5,1},{6,4},{7,3},{8,10},{9,13},{10,... | collective-permute-start | bytes 638984 | tf_op jit(solution)/shard_map/ppermute | solution.py:26
  69.4 7.7 %collective-permute-start.23 = (bf16[32,3328]{1,0:T(8,128)(2,1)S(1)}, bf16[32,3328]{1,0:T(8,128)(2,1)S(1)}, u32[]{:S(2)}, u32[]{:S(2)}) collective-permute-start(bf16[32,3328]{1,0:T(8,128)(2,1)S(1)} %get-tuple-element.94), channel_id=1, source_target_pairs={{0,2},{1,5},{2,0},{3,7},{4,6},{5,1},{6,4},{7,3},{8,10},{9,13},{10,... | collective-permute-start | bytes 638984 | tf_op jit(solution)/shard_map/ppermute | solution.py:26
  71.5 5.9 %collective-permute-start.24 = (bf16[32,3328]{1,0:T(8,128)(2,1)S(1)}, bf16[32,3328]{1,0:T(8,128)(2,1)S(1)}, u32[]{:S(2)}, u32[]{:S(2)}) collective-permute-start(bf16[32,3328]{1,0:T(8,128)(2,1)S(1)} %get-tuple-element.95), channel_id=1, source_target_pairs={{0,4},{1,3},{2,6},{3,1},{4,0},{5,7},{6,2},{7,5},{8,12},{9,11},{10,... | collective-permute-start | bytes 638984 | tf_op jit(solution)/shard_map/ppermute | solution.py:26
  72.7 9.1 %collective-permute-start.20 = (bf16[8,3840]{1,0:T(8,128)(2,1)S(1)}, bf16[8,3840]{1,0:T(8,128)(2,1)S(1)}, u32[]{:S(2)}, u32[]{:S(2)}) collective-permute-start(bf16[8,3840]{1,0:T(8,128)(2,1)S(1)} %get-tuple-element.77), channel_id=1, source_target_pairs={{0,24},{1,25},{2,26},{3,27},{4,28},{5,29},{6,30},{7,31},{8,16},{9,... | collective-permute-start | bytes 184328 | tf_op jit(solution)/shard_map/ppermute | solution.py:26
  75.3 7.0 %collective-permute-start.21 = (bf16[8,3840]{1,0:T(8,128)(2,1)S(1)}, bf16[8,3840]{1,0:T(8,128)(2,1)S(1)}, u32[]{:S(2)}, u32[]{:S(2)}) collective-permute-start(bf16[8,3840]{1,0:T(8,128)(2,1)S(1)} %get-tuple-element.79), channel_id=1, source_target_pairs={{0,16},{1,17},{2,18},{3,19},{4,20},{5,21},{6,22},{7,23},{8,24},{9,... | collective-permute-start | bytes 184328 | tf_op jit(solution)/shard_map/ppermute | solution.py:26
  75.7 6.6 %collective-permute-start.22 = (bf16[8,3840]{1,0:T(8,128)(2,1)S(1)}, bf16[8,3840]{1,0:T(8,128)(2,1)S(1)}, u32[]{:S(2)}, u32[]{:S(2)}) collective-permute-start(bf16[8,3840]{1,0:T(8,128)(2,1)S(1)} %get-tuple-element.81), channel_id=1, source_target_pairs={{0,8},{1,9},{2,10},{3,11},{4,12},{5,13},{6,14},{7,15},{8,0},{9,1},... | collective-permute-start | bytes 184328 | tf_op jit(solution)/shard_map/ppermute | solution.py:26
  77.5 6.6 %collective-permute-start.25 = (bf16[8,3328]{1,0:T(8,128)(2,1)S(1)}, bf16[8,3328]{1,0:T(8,128)(2,1)S(1)}, u32[]{:S(2)}, u32[]{:S(2)}) collective-permute-start(bf16[8,3328]{1,0:T(8,128)(2,1)S(1)} %get-tuple-element.91), channel_id=1, source_target_pairs={{0,24},{1,25},{2,26},{3,27},{4,28},{5,29},{6,30},{7,31},{8,16},{9,... | collective-permute-start | bytes 159752 | tf_op jit(solution)/shard_map/ppermute | solution.py:26
  81.7 4.4 %collective-permute-start.27 = (bf16[8,3328]{1,0:T(8,128)(2,1)S(1)}, bf16[8,3328]{1,0:T(8,128)(2,1)S(1)}, u32[]{:S(2)}, u32[]{:S(2)}) collective-permute-start(bf16[8,3328]{1,0:T(8,128)(2,1)S(1)} %get-tuple-element.92), channel_id=1, source_target_pairs={{0,8},{1,9},{2,10},{3,11},{4,12},{5,13},{6,14},{7,15},{8,0},{9,1},... | collective-permute-start | bytes 159752 | tf_op jit(solution)/shard_map/ppermute | solution.py:26
  81.8 5.0 %collective-permute-start.26 = (bf16[8,3328]{1,0:T(8,128)(2,1)S(1)}, bf16[8,3328]{1,0:T(8,128)(2,1)S(1)}, u32[]{:S(2)}, u32[]{:S(2)}) collective-permute-start(bf16[8,3328]{1,0:T(8,128)(2,1)S(1)} %get-tuple-element.93), channel_id=1, source_target_pairs={{0,16},{1,17},{2,18},{3,19},{4,20},{5,21},{6,22},{7,23},{8,24},{9,... | collective-permute-start | bytes 159752 | tf_op jit(solution)/shard_map/ppermute | solution.py:26

commit v16 on v15

--- a/solution.py
+++ b/solution.py
@@ -141,7 +141,7 @@
 
 def expert_kernel(wide, *refs):
     rows, refs = refs[:8], refs[8:]
-    gate, up, down, own, low, far_side, far_across, gate_sum, up_sum = refs
+    gate, up, down, own, low, far_side, *far_across, gate_sum, up_sum = refs
     height, width = rows[0].shape
     half = 4 * height
 
@@ -160,37 +160,51 @@
     total = gate_sum[...]
     hidden = (total / (1.0 + jnp.exp(-total)) * up_sum[...]).astype(jnp.bfloat16)
 
-    @pl.loop(0, width // wide)
-    def _(k):
+    steps = far_across[0].shape[1] // wide
+
+    def give(k, ref, first):
         product = jnp.dot(hidden, down[0, :, span(k)], preferred_element_type=jnp.float32)
         product = product.astype(jnp.bfloat16)
         own[:, span(k)] = product[:half]
         low[:, span(k)] = product[half : half + 2 * height]
         far_side[:, span(k)] = product[half + 2 * height : half + 3 * height]
-        far_across[:, span(k)] = product[half + 3 * height :]
-
-
-def experts(rows, weights):
+        ref[:, span(k - first)] = product[half + 3 * height :]
+
+    @pl.loop(0, steps)
+    def _(k):
+        give(k, far_across[0], 0)
+
+    @pl.loop(steps, width // wide)
+    def _(k):
+        give(k, far_across[1], steps)
+
+
+def step_width(width):
+    return max(w for w in (128, 256, 512, 1024) if width % w == 0)
+
+
+def experts(rows, weights, cut):
     height, width = rows[0].shape
     units = weights[0].shape[2]
-    wide = max(w for w in (128, 256, 512, 1024) if width % w == 0)
+    wide = step_width(width)
     total = len(rows) * height
     whole = pl.BlockSpec(memory_space=pltpu.VMEM)
     inputs = [pltpu.with_memory_space_constraint(v, pltpu.VMEM) for v in (*rows, *weights)]
     return pl.pallas_call(
         lambda *refs: expert_kernel(wide, *refs),
         in_specs=[whole] * len(inputs),
-        out_specs=[whole] * 4,
-        out_shape=[pltpu.VMEM((count * height, width), jnp.bfloat16) for count in (4, 2, 1, 1)],
+        out_specs=[whole] * 5,
+        out_shape=[pltpu.VMEM((count * height, width), jnp.bfloat16) for count in (4, 2, 1)]
+        + [pltpu.VMEM((height, part), jnp.bfloat16) for part in (cut, width - cut)],
         scratch_shapes=[
             pltpu.VMEM((total, units), jnp.float32),
             pltpu.VMEM((total, units), jnp.float32),
         ],
         compiler_params=pltpu.CompilerParams(vmem_limit_bytes=28 * 2**20),
         cost_estimate=pl.CostEstimate(
-            flops=6 * total * width * units,
-            bytes_accessed=6 * width * units + 4 * total * width,
-            transcendentals=total * units,
+            flops=0,
+            bytes_accessed=0,
+            transcendentals=0,
         ),
     )(*inputs)
 
@@ -281,22 +295,24 @@
     late, across = cache_rows("late", 0, beam_count, across)
     held = [column, near, side, across, twin_column, twin_near]
     held = held + [swapped(side, twin), swapped(across, twin)]
-    own, low, far_side, far_across = experts(held, weights)
-    far_across, late = tied(far_across, late)
+    wide = step_width(width)
+    cut = wide * max(1, 4 * (width // wide) // 7)
+    own, low, far_side, *far_across = experts(held, weights, cut)
+    far_across[1], far_side, low, late = tied(far_across[1], far_side, low, late)
     pieces.append(late)
 
-    far_across, far_side = swapped(far_across, twin), swapped(far_side, twin)
+    far_across = [swapped(value, twin) for value in far_across]
+    far_side = swapped(far_side, twin)
     low = swapped(low, twin)
     height = expert_count * capacity
 
-    cut = 128 * (15 * width // 3584)
     halves = [(0, cut), (cut, width)]
 
     def block(value, j, half):
         return value[j * height : (j + 1) * height, half[0] : half[1]]
 
     def to_second(half):
-        return added([block(own, 3, half), block(far_across, 0, half)]).astype(jnp.bfloat16)
+        return added([block(own, 3, half), far_across[half[0] > 0]]).astype(jnp.bfloat16)
 
     def to_first(half, across):
         return added([block(own, 1, half), block(low, 1, half), across]).astype(jnp.bfloat16)

time: 87.8 us -> 86.2 us (0.982)
  waiting for transfers between devices: 30.6 us -> 28.7 us
    ppermute x26 -> x27, waiting for transfers between devices: 30.6 us -> 28.7 us  [swapped(): return lax.ppermute(value, 'dp', [(i, partner(i)) for i in range(peers)])]
    ppermute x26 -> x27, starting transfers between devices: 36.3 us -> 36.7 us  [swapped(): return lax.ppermute(value, 'dp', [(i, partner(i)) for i in range(peers)])]
  transfers between devices with their start and end apart: 28 -> 29, of which waited for: 15 -> 13; matrix products, arithmetic and copies ran while one was open for 6% -> 6% of each run, Pallas kernels for 13% -> 14%
where the time goes in v16:
time: 86.2 us; the launch traced here: 86 us
  starting transfers between devices  38.3 us (44%)
  waiting for transfers between devices  28.7 us (33%)
  Pallas kernels  11.8 us (14%)
  other arithmetic  4.79 us (6%)
  local copies, waits for them, and re-layouts  1.6 us (2%)
    ppermute x27, starting transfers between devices, swapped(): return lax.ppermute(value, 'dp', [(i, partner(i)) for i in range(peers)])  36.7 us
    ppermute x27, waiting for transfers between devices, swapped(): return lax.ppermute(value, 'dp', [(i, partner(i)) for i in range(peers)])  28.7 us
    pallas_call x1, Pallas kernels, experts(): pl.pallas_call(lambda *refs: expert_kernel(wide, *refs), in_specs=[whole]...  5.3 us
    pallas_call x1, Pallas kernels, fetched(): pl.pallas_call(fetch_kernel, in_specs=[pl.BlockSpec(memory_space=pltpu.HB...  4.23 us
    reduce_sum x1, other arithmetic, body(): jnp.sum(jnp.where(routed_experts == targets[r], route_weights, 0.0), axis=1)  3.31 us
    pallas_call x1, Pallas kernels, attend(): pl.pallas_call(lambda *refs: attend_kernel(spans, *refs), in_specs=[scala...  2.3 us
  transfers between devices with their start and end apart: 29, of which 13 were waited for; matrix products, arithmetic and copies ran while one was open for 6% of the time, Pallas kernels for 14%

profile of v16, /device:TPU:0, one launch (start us, length us, event | category | flops | bytes accessed | tf_op | source)
XLA Modules:
  0.0 86.0 jit_solution(15192170981283160839)
XLA Ops:
  0.6 0.7 collective-permute-start.3
  1.4 4.1 %collective-permute-start.1 = (bf16[8,7168]{1,0:T(8,128)(2,1)}, bf16[8,7168]{1,0:T(8,128)(2,1)S(1)}, u32[]{:S(2)}, u32[]{:S(2)}) collective-permute-start(bf16[8,7168]{1,0:T(8,128)(2,1)} %param.16), channel_id=1, source_target_pairs={{0,16},{1,17},{2,18},{3,19},{4,20},{5,21},{6,22},{7,23},{8,24},{9,... | collective-permute-start | bytes 344072 | tf_op jit(solution)/shard_map/ppermute | solution.py:26
  5.5 1.3 %collective-permute-start = (bf16[8,7168]{1,0:T(8,128)(2,1)}, bf16[8,7168]{1,0:T(8,128)(2,1)S(1)}, u32[]{:S(2)}, u32[]{:S(2)}) collective-permute-start(bf16[8,7168]{1,0:T(8,128)(2,1)} %param.16), channel_id=1, source_target_pairs={{0,24},{1,25},{2,26},{3,27},{4,28},{5,29},{6,30},{7,31},{8,16},{9,... | collective-permute-start | bytes 344072 | tf_op jit(solution)/shard_map/ppermute | solution.py:26
  6.8 0.2 collective-permute-start.2
  7.0 0.6 fusion.4
  7.7 0.9 %pad.4 = bf16[32,7168]{1,0:T(8,128)(2,1)S(1)} pad(bf16[8,7168]{1,0:T(8,128)(2,1)} %param.16, bf16[]{:T(256)} %constant.19.clone.1), padding=0_24x0_0 | pad | bytes 573442 | tf_op jit(solution)/shard_map/jit(_pad)/pad | solution.py:277
  8.6 3.3 %fusion.3 = (f32[8]{0:T(128)S(1)}, f32[8]{0:T(128)S(1)}, f32[8]{0:T(128)S(1)}, f32[8]{0:T(128)S(1)}) fusion(f32[8,2]{0,1:T(2,128)} %param.18, s32[8,2]{0,1:T(2,128)} %param.17, s32[]{:T(128)} %bitcast.3, s32[]{:T(128)} %bitcast.1, s32[]{:T(128)} %bitcast, s32[]{:T(128)} %bitcast.2), kind=kLoop, calls=%fused_computation.23 | loop fusion | flops 160 | bytes 272 | tf_op jit(solution)/shard_map/reduce_sum | solution.py:240
  11.9 1.4 %collective-permute-done = bf16[8,7168]{1,0:T(8,128)(2,1)S(1)} collective-permute-done((bf16[8,7168]{1,0:T(8,128)(2,1)}, bf16[8,7168]{1,0:T(8,128)(2,1)S(1)}, u32[]{:S(2)}, u32[]{:S(2)}) %collective-permute-start) | collective-permute-done | bytes 114720 | tf_op jit(solution)/shard_map/ppermute | solution.py:26
  13.3 1.2 %collective-permute-done.2 = bf16[8,7168]{1,0:T(8,128)(2,1)S(1)} collective-permute-done((bf16[8,7168]{1,0:T(8,128)(2,1)}, bf16[8,7168]{1,0:T(8,128)(2,1)S(1)}, u32[]{:S(2)}, u32[]{:S(2)}) %collective-permute-start.2) | collective-permute-done | bytes 114720 | tf_op jit(solution)/shard_map/ppermute | solution.py:26
  14.6 5.7 %collective-permute-start.4 = (bf16[32,7168]{1,0:T(8,128)(2,1)S(1)}, bf16[32,7168]{1,0:T(8,128)(2,1)S(1)}, u32[]{:S(2)}, u32[]{:S(2)}) collective-permute-start(bf16[32,7168]{1,0:T(8,128)(2,1)S(1)} %constant_dynamic-update-slice_fusion.refs_0_), channel_id=1, source_target_pairs={{0,4},{1,3},{2,6},{3,1},{4,0},{5,7},{6,2},{7,5},{8,12},{9,11},{10,... | collective-permute-start | bytes 1376264 | tf_op jit(solution)/shard_map/ppermute | solution.py:26
  20.3 0.5 collective-permute-start.7
  20.8 5.9 %collective-permute-done.4.refs_1_ = bf16[32,7168]{1,0:T(8,128)(2,1)S(1)} collective-permute-done((bf16[32,7168]{1,0:T(8,128)(2,1)S(1)}, bf16[32,7168]{1,0:T(8,128)(2,1)S(1)}, u32[]{:S(2)}, u32[]{:S(2)}) %collective-permute-start.4) | collective-permute-done | bytes 458784 | tf_op jit(solution)/shard_map/ppermute | solution.py:26
  26.7 1.1 %collective-permute-start.6 = (bf16[32,7168]{1,0:T(8,128)(2,1)S(1)}, bf16[32,7168]{1,0:T(8,128)(2,1)S(1)}, u32[]{:S(2)}, u32[]{:S(2)}) collective-permute-start(bf16[32,7168]{1,0:T(8,128)(2,1)S(1)} %collective-permute-done.4.refs_1_), channel_id=1, source_target_pairs={{0,2},{1,5},{2,0},{3,7},{4,6},{5,1},{6,4},{7,3},{8,10},{9,13},{10,... | collective-permute-start | bytes 1376264 | tf_op jit(solution)/shard_map/ppermute | solution.py:26
  27.8 0.9 %collective-permute-start.5 = (bf16[32,7168]{1,0:T(8,128)(2,1)S(1)}, bf16[32,7168]{1,0:T(8,128)(2,1)S(1)}, u32[]{:S(2)}, u32[]{:S(2)}) collective-permute-start(bf16[32,7168]{1,0:T(8,128)(2,1)S(1)} %constant_dynamic-update-slice_fusion.refs_0_), channel_id=1, source_target_pairs={{0,2},{1,5},{2,0},{3,7},{4,6},{5,1},{6,4},{7,3},{8,10},{9,13},{10,... | collective-permute-start | bytes 1376264 | tf_op jit(solution)/shard_map/ppermute | solution.py:26
  28.7 4.2 %shard_map.122 = (bf16[1,7168,256]{2,1,0:T(8,128)(2,1)S(1)}, bf16[1,7168,256]{2,1,0:T(8,128)(2,1)S(1)}, bf16[1,256,7168]{2,1,0:T(8,128)(2,1)S(1)}) custom-call(bf16[1,7168,256]{2,1,0:T(8,128)(2,1)} %refs_0_.2, bf16[1,7168,256]{2,1,0:T(8,128)(2,1)} %refs_1_.2, bf16[1,256,7168]{2,1,0:T(8,128)(2,1)} %refs_2_.2), custom_call_target="tpu_custom_call" | custom-call | bytes 22020096 | tf_op jit(solution)/shard_map/pallas_call | solution.py:127
  33.0 2.2 %collective-permute-done.6.refs_3_ = bf16[32,7168]{1,0:T(8,128)(2,1)S(1)} collective-permute-done((bf16[32,7168]{1,0:T(8,128)(2,1)S(1)}, bf16[32,7168]{1,0:T(8,128)(2,1)S(1)}, u32[]{:S(2)}, u32[]{:S(2)}) %collective-permute-start.6) | collective-permute-done | bytes 458784 | tf_op jit(solution)/shard_map/ppermute | solution.py:26
  35.2 0.9 collective-permute-start.13
  36.1 4.0 %collective-permute-done.5.refs_2_ = bf16[32,7168]{1,0:T(8,128)(2,1)S(1)} collective-permute-done((bf16[32,7168]{1,0:T(8,128)(2,1)S(1)}, bf16[32,7168]{1,0:T(8,128)(2,1)S(1)}, u32[]{:S(2)}, u32[]{:S(2)}) %collective-permute-start.5) | collective-permute-done | bytes 458784 | tf_op jit(solution)/shard_map/ppermute | solution.py:26
  40.1 0.5 collective-permute-start.11
  40.6 1.3 %collective-permute-done.10.refs_6_ = bf16[32,7168]{1,0:T(8,128)(2,1)S(1)} collective-permute-done((bf16[32,7168]{1,0:T(8,128)(2,1)S(1)}, bf16[32,7168]{1,0:T(8,128)(2,1)S(1)}, u32[]{:S(2)}, u32[]{:S(2)}) %collective-permute-start.10) | collective-permute-done | bytes 458784 | tf_op jit(solution)/shard_map/ppermute | solution.py:26
  41.9 0.7 collective-permute-done.11.refs_7_
  42.6 5.3 %shard_map.123 = (bf16[128,7168]{1,0:T(8,128)(2,1)S(1)}, bf16[64,7168]{1,0:T(8,128)(2,1)S(1)}, bf16[32,7168]{1,0:T(8,128)(2,1)S(1)}, bf16[32,4096]{1,0:T(8,128)(2,1)S(1)}, bf16[32,3072]{1,0:T(8,128)(2,1)S(1)}) custom-call(bf16[32,7168]{1,0:T(8,128)(2,1)S(1)} %constant_dynamic-update-slice_fusion.refs_0_, ...), custom_call_target="tpu_custom_call" | custom-call | tf_op jit(solution)/shard_map/pallas_call | solution.py:193
  47.9 0.2 collective-permute-start.12
  48.1 2.6 %collective-permute-start.18 = (bf16[32,3072]{1,0:T(8,128)(2,1)S(1)}, bf16[32,3072]{1,0:T(8,128)(2,1)S(1)}, u32[]{:S(2)}, u32[]{:S(2)}) collective-permute-start(bf16[32,3072]{1,0:T(8,128)(2,1)S(1)} %get-tuple-element.78), channel_id=1, source_target_pairs={{0,1},{1,0},{2,3},{3,2},{4,5},{5,4},{6,7},{7,6},{8,9},{9,8},{10,11... | collective-permute-start | bytes 589832 | tf_op jit(solution)/shard_map/ppermute | solution.py:26
  50.8 1.9 %collective-permute-start.14 = (bf16[32,4096]{1,0:T(8,128)(2,1)S(1)}, bf16[32,4096]{1,0:T(8,128)(2,1)S(1)}, u32[]{:S(2)}, u32[]{:S(2)}) collective-permute-start(bf16[32,4096]{1,0:T(8,128)(2,1)S(1)} %add_convert_fusion.2), channel_id=1, source_target_pairs={{0,2},{1,5},{2,0},{3,7},{4,6},{5,1},{6,4},{7,3},{8,10},{9,13},{10,... | collective-permute-start | bytes 786440 | tf_op jit(solution)/shard_map/ppermute | solution.py:26
  52.7 2.3 %shard_map.124 = bf16[8,64,512]{2,1,0:T(8,128)(2,1)} custom-call(s32[8]{0:T(128)S(1)} %copy-done.3, s32[8]{0:T(128)S(1)} %copy-done.4, bf16[8,64,576]{2,1,0:T(8,128)(2,1)S(1)} %copy-done.1, bf16[8,96,576]{2,1,0:T(8,128)(2,1)S(1)} %copy-done, bf16[8,96,576]{2,1,0:T(8,128)(2,1)S(1)} %collective-permute-done.9.refs_4_, bf16[8,576]{1,0:T(8,128)(2,1)S(1)} %copy-done.2, ...), custom_call_target="tpu_custom_call" | custom-call | flops 106954752 | bytes 4653056 | tf_op jit(solution)/shard_map/pallas_call | solution.py:99
  55.0 2.2 %collective-permute-done.14 = bf16[32,4096]{1,0:T(8,128)(2,1)S(1)} collective-permute-done((bf16[32,4096]{1,0:T(8,128)(2,1)S(1)}, bf16[32,4096]{1,0:T(8,128)(2,1)S(1)}, u32[]{:S(2)}, u32[]{:S(2)}) %collective-permute-start.14) | collective-permute-done | bytes 262176 | tf_op jit(solution)/shard_map/ppermute | solution.py:26
  57.2 0.2 add_convert_fusion.1
  57.4 2.2 %collective-permute-start.19 = (bf16[32,4096]{1,0:T(8,128)(2,1)S(1)}, bf16[32,4096]{1,0:T(8,128)(2,1)S(1)}, u32[]{:S(2)}, u32[]{:S(2)}) collective-permute-start(bf16[32,4096]{1,0:T(8,128)(2,1)S(1)} %get-tuple-element.79), channel_id=1, source_target_pairs={{0,4},{1,3},{2,6},{3,1},{4,0},{5,7},{6,2},{7,5},{8,12},{9,11},{10,... | collective-permute-start | bytes 786440 | tf_op jit(solution)/shard_map/ppermute | solution.py:26
  59.6 2.0 %collective-permute-start.17 = (bf16[32,4096]{1,0:T(8,128)(2,1)S(1)}, bf16[32,4096]{1,0:T(8,128)(2,1)S(1)}, u32[]{:S(2)}, u32[]{:S(2)}) collective-permute-start(bf16[32,4096]{1,0:T(8,128)(2,1)S(1)} %get-tuple-element.102), channel_id=1, source_target_pairs={{0,2},{1,5},{2,0},{3,7},{4,6},{5,1},{6,4},{7,3},{8,10},{9,13},{10,... | collective-permute-start | bytes 786440 | tf_op jit(solution)/shard_map/ppermute | solution.py:26
  61.6 4.4 %collective-permute-done.19 = bf16[32,4096]{1,0:T(8,128)(2,1)S(1)} collective-permute-done((bf16[32,4096]{1,0:T(8,128)(2,1)S(1)}, bf16[32,4096]{1,0:T(8,128)(2,1)S(1)}, u32[]{:S(2)}, u32[]{:S(2)}) %collective-permute-start.19) | collective-permute-done | bytes 262176 | tf_op jit(solution)/shard_map/ppermute | solution.py:26
  66.1 0.1 convert_add_fusion
  66.2 1.8 %collective-permute-done.20 = bf16[32,3072]{1,0:T(8,128)(2,1)S(1)} collective-permute-done((bf16[32,3072]{1,0:T(8,128)(2,1)S(1)}, bf16[32,3072]{1,0:T(8,128)(2,1)S(1)}, u32[]{:S(2)}, u32[]{:S(2)}) %collective-permute-start.20) | collective-permute-done | bytes 196640 | tf_op jit(solution)/shard_map/ppermute | solution.py:26
  68.0 0.1 add_convert_fusion.4
  68.2 2.1 %collective-permute-start.24 = (bf16[32,3072]{1,0:T(8,128)(2,1)S(1)}, bf16[32,3072]{1,0:T(8,128)(2,1)S(1)}, u32[]{:S(2)}, u32[]{:S(2)}) collective-permute-start(bf16[32,3072]{1,0:T(8,128)(2,1)S(1)} %get-tuple-element.100), channel_id=1, source_target_pairs={{0,2},{1,5},{2,0},{3,7},{4,6},{5,1},{6,4},{7,3},{8,10},{9,13},{10,... | collective-permute-start | bytes 589832 | tf_op jit(solution)/shard_map/ppermute | solution.py:26
  70.2 1.5 %collective-permute-start.25 = (bf16[32,3072]{1,0:T(8,128)(2,1)S(1)}, bf16[32,3072]{1,0:T(8,128)(2,1)S(1)}, u32[]{:S(2)}, u32[]{:S(2)}) collective-permute-start(bf16[32,3072]{1,0:T(8,128)(2,1)S(1)} %get-tuple-element.101), channel_id=1, source_target_pairs={{0,4},{1,3},{2,6},{3,1},{4,0},{5,7},{6,2},{7,5},{8,12},{9,11},{10,... | collective-permute-start | bytes 589832 | tf_op jit(solution)/shard_map/ppermute | solution.py:26
  71.7 2.5 %collective-permute-start.21 = (bf16[8,4096]{1,0:T(8,128)(2,1)S(1)}, bf16[8,4096]{1,0:T(8,128)(2,1)S(1)}, u32[]{:S(2)}, u32[]{:S(2)}) collective-permute-start(bf16[8,4096]{1,0:T(8,128)(2,1)S(1)} %get-tuple-element.83), channel_id=1, source_target_pairs={{0,24},{1,25},{2,26},{3,27},{4,28},{5,29},{6,30},{7,31},{8,16},{9,... | collective-permute-start | bytes 196616 | tf_op jit(solution)/shard_map/ppermute | solution.py:26
  74.2 0.6 collective-permute-start.22
  74.8 1.3 %collective-permute-start.23 = (bf16[8,4096]{1,0:T(8,128)(2,1)S(1)}, bf16[8,4096]{1,0:T(8,128)(2,1)S(1)}, u32[]{:S(2)}, u32[]{:S(2)}) collective-permute-start(bf16[8,4096]{1,0:T(8,128)(2,1)S(1)} %get-tuple-element.87), channel_id=1, source_target_pairs={{0,8},{1,9},{2,10},{3,11},{4,12},{5,13},{6,14},{7,15},{8,0},{9,1},... | collective-permute-start | bytes 196616 | tf_op jit(solution)/shard_map/ppermute | solution.py:26
  76.1 0.1 add_convert_fusion.10
  76.2 4.0 %collective-permute-start.26 = (bf16[8,3072]{1,0:T(8,128)(2,1)S(1)}, bf16[8,3072]{1,0:T(8,128)(2,1)S(1)}, u32[]{:S(2)}, u32[]{:S(2)}) collective-permute-start(bf16[8,3072]{1,0:T(8,128)(2,1)S(1)} %get-tuple-element.97), channel_id=1, source_target_pairs={{0,24},{1,25},{2,26},{3,27},{4,28},{5,29},{6,30},{7,31},{8,16},{9,... | collective-permute-start | bytes 147464 | tf_op jit(solution)/shard_map/ppermute | solution.py:26
  80.2 1.4 %collective-permute-start.27 = (bf16[8,3072]{1,0:T(8,128)(2,1)S(1)}, bf16[8,3072]{1,0:T(8,128)(2,1)S(1)}, u32[]{:S(2)}, u32[]{:S(2)}) collective-permute-start(bf16[8,3072]{1,0:T(8,128)(2,1)S(1)} %get-tuple-element.99), channel_id=1, source_target_pairs={{0,16},{1,17},{2,18},{3,19},{4,20},{5,21},{6,22},{7,23},{8,24},{9,... | collective-permute-start | bytes 147464 | tf_op jit(solution)/shard_map/ppermute | solution.py:26
  81.6 0.1 add_convert_fusion.6
  81.8 0.7 collective-permute-done.26
  82.5 2.1 %collective-permute-done.28 = bf16[8,3072]{1,0:T(8,128)(2,1)S(1)} collective-permute-done((bf16[8,3072]{1,0:T(8,128)(2,1)S(1)}, bf16[8,3072]{1,0:T(8,128)(2,1)S(1)}, u32[]{:S(2)}, u32[]{:S(2)}) %collective-permute-start.28) | collective-permute-done | bytes 49184 | tf_op jit(solution)/shard_map/ppermute | solution.py:26
  84.6 0.6 collective-permute-done.27
  85.2 0.1 add_convert_fusion.7
  85.3 0.7 pad_maximum_fusion
  (40 shorter events, 0.3 us)
Async XLA Ops:
  0.6 13.9 %collective-permute-start.3 = (bf16[8,96,576]{2,1,0:T(8,128)(2,1)}, bf16[8,96,576]{2,1,0:T(8,128)(2,1)S(1)}, u32[]{:S(2)}, u32[]{:S(2)}) collective-permute-start(bf16[8,96,576]{2,1,0:T(8,128)(2,1)} %refs_3_.1), channel_id=1, source_target_pairs={{1,2},{3,4},{5,6},{6,5},{9,10},{11,12},{13,14},{14,13},{17,18},{19... | collective-permute-start | bytes 2654216 | tf_op jit(solution)/shard_map/ppermute | solution.py:47
  1.4 10.6 %collective-permute-start.1 = (bf16[8,7168]{1,0:T(8,128)(2,1)}, bf16[8,7168]{1,0:T(8,128)(2,1)S(1)}, u32[]{:S(2)}, u32[]{:S(2)}) collective-permute-start(bf16[8,7168]{1,0:T(8,128)(2,1)} %param.16), channel_id=1, source_target_pairs={{0,16},{1,17},{2,18},{3,19},{4,20},{5,21},{6,22},{7,23},{8,24},{9,... | collective-permute-start | bytes 344072 | tf_op jit(solution)/shard_map/ppermute | solution.py:26
  5.5 7.8 %collective-permute-start = (bf16[8,7168]{1,0:T(8,128)(2,1)}, bf16[8,7168]{1,0:T(8,128)(2,1)S(1)}, u32[]{:S(2)}, u32[]{:S(2)}) collective-permute-start(bf16[8,7168]{1,0:T(8,128)(2,1)} %param.16), channel_id=1, source_target_pairs={{0,24},{1,25},{2,26},{3,27},{4,28},{5,29},{6,30},{7,31},{8,16},{9,... | collective-permute-start | bytes 344072 | tf_op jit(solution)/shard_map/ppermute | solution.py:26
  6.8 7.7 %collective-permute-start.2 = (bf16[8,7168]{1,0:T(8,128)(2,1)}, bf16[8,7168]{1,0:T(8,128)(2,1)S(1)}, u32[]{:S(2)}, u32[]{:S(2)}) collective-permute-start(bf16[8,7168]{1,0:T(8,128)(2,1)} %param.16), channel_id=1, source_target_pairs={{0,8},{1,9},{2,10},{3,11},{4,12},{5,13},{6,14},{7,15},{8,0},{9,1},... | collective-permute-start | bytes 344072 | tf_op jit(solution)/shard_map/ppermute | solution.py:26
  14.6 20.6 %copy-start = (bf16[8,96,576]{2,1,0:T(8,128)(2,1)S(1)}, bf16[8,96,576]{2,1,0:T(8,128)(2,1)}, u32[]{:S(2)}) copy-start(bf16[8,96,576]{2,1,0:T(8,128)(2,1)} %refs_3_.1) | copy-start | bytes 2654212
  14.6 12.1 %collective-permute-start.4 = (bf16[32,7168]{1,0:T(8,128)(2,1)S(1)}, bf16[32,7168]{1,0:T(8,128)(2,1)S(1)}, u32[]{:S(2)}, u32[]{:S(2)}) collective-permute-start(bf16[32,7168]{1,0:T(8,128)(2,1)S(1)} %constant_dynamic-update-slice_fusion.refs_0_), channel_id=1, source_target_pairs={{0,4},{1,3},{2,6},{3,1},{4,0},{5,7},{6,2},{7,5},{8,12},{9,11},{10,... | collective-permute-start | bytes 1376264 | tf_op jit(solution)/shard_map/ppermute | solution.py:26
  20.2 12.7 %collective-permute-start.9 = (bf16[8,96,576]{2,1,0:T(8,128)(2,1)}, bf16[8,96,576]{2,1,0:T(8,128)(2,1)S(1)}, u32[]{:S(2)}, u32[]{:S(2)}) collective-permute-start(bf16[8,96,576]{2,1,0:T(8,128)(2,1)} %refs_3_.1), channel_id=1, source_target_pairs={{0,1},{1,0},{2,3},{3,2},{4,5},{5,4},{6,7},{7,6},{8,9},{9,8},{10,11... | collective-permute-start | bytes 2654216 | tf_op jit(solution)/shard_map/ppermute | solution.py:26
  20.3 12.7 %collective-permute-start.7 = (bf16[32,7168]{1,0:T(8,128)(2,1)S(1)}, bf16[32,7168]{1,0:T(8,128)(2,1)S(1)}, u32[]{:S(2)}, u32[]{:S(2)}) collective-permute-start(bf16[32,7168]{1,0:T(8,128)(2,1)S(1)} %constant_dynamic-update-slice_fusion.refs_0_), channel_id=1, source_target_pairs={{0,1},{1,0},{2,3},{3,2},{4,5},{5,4},{6,7},{7,6},{8,9},{9,8},{10,11... | collective-permute-start | bytes 1376264 | tf_op jit(solution)/shard_map/ppermute | solution.py:26
  26.7 6.3 %collective-permute-start.8 = (bf16[32,7168]{1,0:T(8,128)(2,1)S(1)}, bf16[32,7168]{1,0:T(8,128)(2,1)S(1)}, u32[]{:S(2)}, u32[]{:S(2)}) collective-permute-start(bf16[32,7168]{1,0:T(8,128)(2,1)S(1)} %collective-permute-done.4.refs_1_), channel_id=1, source_target_pairs={{0,1},{1,0},{2,3},{3,2},{4,5},{5,4},{6,7},{7,6},{8,9},{9,8},{10,11... | collective-permute-start | bytes 1376264 | tf_op jit(solution)/shard_map/ppermute | solution.py:26
  26.7 8.5 %collective-permute-start.6 = (bf16[32,7168]{1,0:T(8,128)(2,1)S(1)}, bf16[32,7168]{1,0:T(8,128)(2,1)S(1)}, u32[]{:S(2)}, u32[]{:S(2)}) collective-permute-start(bf16[32,7168]{1,0:T(8,128)(2,1)S(1)} %collective-permute-done.4.refs_1_), channel_id=1, source_target_pairs={{0,2},{1,5},{2,0},{3,7},{4,6},{5,1},{6,4},{7,3},{8,10},{9,13},{10,... | collective-permute-start | bytes 1376264 | tf_op jit(solution)/shard_map/ppermute | solution.py:26
  27.8 12.3 %collective-permute-start.5 = (bf16[32,7168]{1,0:T(8,128)(2,1)S(1)}, bf16[32,7168]{1,0:T(8,128)(2,1)S(1)}, u32[]{:S(2)}, u32[]{:S(2)}) collective-permute-start(bf16[32,7168]{1,0:T(8,128)(2,1)S(1)} %constant_dynamic-update-slice_fusion.refs_0_), channel_id=1, source_target_pairs={{0,2},{1,5},{2,0},{3,7},{4,6},{5,1},{6,4},{7,3},{8,10},{9,13},{10,... | collective-permute-start | bytes 1376264 | tf_op jit(solution)/shard_map/ppermute | solution.py:26
  35.2 17.5 %copy-start.1 = (bf16[8,64,576]{2,1,0:T(8,128)(2,1)S(1)}, bf16[8,64,576]{2,1,0:T(8,128)(2,1)}, u32[]{:S(2)}) copy-start(bf16[8,64,576]{2,1,0:T(8,128)(2,1)} %refs_2_.3) | copy-start | bytes 1769476
  35.2 17.5 %copy-start.2 = (bf16[8,576]{1,0:T(8,128)(2,1)S(1)}, bf16[8,576]{1,0:T(8,128)(2,1)}, u32[]{:S(2)}) copy-start(bf16[8,576]{1,0:T(8,128)(2,1)} %refs_5_.1) | copy-start | bytes 27652
  35.2 17.5 %copy-start.3 = (s32[8]{0:T(128)S(1)}, s32[8]{0:T(128)}, u32[]{:S(2)}) copy-start(s32[8]{0:T(128)} %refs_0_.3) | copy-start | bytes 100
  35.2 17.5 %copy-start.4 = (s32[8]{0:T(128)S(1)}, s32[8]{0:T(128)}, u32[]{:S(2)}) copy-start(s32[8]{0:T(128)} %refs_1_.3) | copy-start | bytes 100
  35.2 12.9 %collective-permute-start.13 = (bf16[8,96,576]{2,1,0:T(8,128)(2,1)S(1)}, bf16[8,96,576]{2,1,0:T(8,128)(2,1)S(1)}, u32[]{:S(2)}, u32[]{:S(2)}) collective-permute-start(bf16[8,96,576]{2,1,0:T(8,128)(2,1)S(1)} %copy-done), channel_id=1, source_target_pairs={{2,1},{4,3},{7,8},{8,7},{10,9},{12,11},{15,16},{16,15},{18,17},{20... | collective-permute-start | bytes 2654216 | tf_op jit(solution)/shard_map/ppermute | solution.py:47
  40.1 1.8 %collective-permute-start.10 = (bf16[32,7168]{1,0:T(8,128)(2,1)S(1)}, bf16[32,7168]{1,0:T(8,128)(2,1)S(1)}, u32[]{:S(2)}, u32[]{:S(2)}) collective-permute-start(bf16[32,7168]{1,0:T(8,128)(2,1)S(1)} %collective-permute-done.5.refs_2_), channel_id=1, source_target_pairs={{0,1},{1,0},{2,3},{3,2},{4,5},{5,4},{6,7},{7,6},{8,9},{9,8},{10,11... | collective-permute-start | bytes 1376264 | tf_op jit(solution)/shard_map/ppermute | solution.py:26
  40.1 2.5 %collective-permute-start.11 = (bf16[32,7168]{1,0:T(8,128)(2,1)S(1)}, bf16[32,7168]{1,0:T(8,128)(2,1)S(1)}, u32[]{:S(2)}, u32[]{:S(2)}) collective-permute-start(bf16[32,7168]{1,0:T(8,128)(2,1)S(1)} %collective-permute-done.6.refs_3_), channel_id=1, source_target_pairs={{0,1},{1,0},{2,3},{3,2},{4,5},{5,4},{6,7},{7,6},{8,9},{9,8},{10,11... | collective-permute-start | bytes 1376264 | tf_op jit(solution)/shard_map/ppermute | solution.py:26
  47.9 2.8 %collective-permute-start.12 = (bf16[32,4096]{1,0:T(8,128)(2,1)S(1)}, bf16[32,4096]{1,0:T(8,128)(2,1)S(1)}, u32[]{:S(2)}, u32[]{:S(2)}) collective-permute-start(bf16[32,4096]{1,0:T(8,128)(2,1)S(1)} %get-tuple-element.63), channel_id=1, source_target_pairs={{0,1},{1,0},{2,3},{3,2},{4,5},{5,4},{6,7},{7,6},{8,9},{9,8},{10,11... | collective-permute-start | bytes 786440 | tf_op jit(solution)/shard_map/ppermute | solution.py:26
  48.1 6.9 %collective-permute-start.18 = (bf16[32,3072]{1,0:T(8,128)(2,1)S(1)}, bf16[32,3072]{1,0:T(8,128)(2,1)S(1)}, u32[]{:S(2)}, u32[]{:S(2)}) collective-permute-start(bf16[32,3072]{1,0:T(8,128)(2,1)S(1)} %get-tuple-element.78), channel_id=1, source_target_pairs={{0,1},{1,0},{2,3},{3,2},{4,5},{5,4},{6,7},{7,6},{8,9},{9,8},{10,11... | collective-permute-start | bytes 589832 | tf_op jit(solution)/shard_map/ppermute | solution.py:26
  50.7 6.5 %collective-permute-start.15 = (bf16[64,7168]{1,0:T(8,128)(2,1)S(1)}, bf16[64,7168]{1,0:T(8,128)(2,1)S(1)}, u32[]{:S(2)}, u32[]{:S(2)}) collective-permute-start(bf16[64,7168]{1,0:T(8,128)(2,1)S(1)} %get-tuple-element.75), channel_id=1, source_target_pairs={{0,1},{1,0},{2,3},{3,2},{4,5},{5,4},{6,7},{7,6},{8,9},{9,8},{10,11... | collective-permute-start | bytes 2752520 | tf_op jit(solution)/shard_map/ppermute | solution.py:26
  50.8 6.4 %collective-permute-start.14 = (bf16[32,4096]{1,0:T(8,128)(2,1)S(1)}, bf16[32,4096]{1,0:T(8,128)(2,1)S(1)}, u32[]{:S(2)}, u32[]{:S(2)}) collective-permute-start(bf16[32,4096]{1,0:T(8,128)(2,1)S(1)} %add_convert_fusion.2), channel_id=1, source_target_pairs={{0,2},{1,5},{2,0},{3,7},{4,6},{5,1},{6,4},{7,3},{8,10},{9,13},{10,... | collective-permute-start | bytes 786440 | tf_op jit(solution)/shard_map/ppermute | solution.py:26
  52.6 4.6 %collective-permute-start.16 = (bf16[32,7168]{1,0:T(8,128)(2,1)S(1)}, bf16[32,7168]{1,0:T(8,128)(2,1)S(1)}, u32[]{:S(2)}, u32[]{:S(2)}) collective-permute-start(bf16[32,7168]{1,0:T(8,128)(2,1)S(1)} %get-tuple-element.76), channel_id=1, source_target_pairs={{0,1},{1,0},{2,3},{3,2},{4,5},{5,4},{6,7},{7,6},{8,9},{9,8},{10,11... | collective-permute-start | bytes 1376264 | tf_op jit(solution)/shard_map/ppermute | solution.py:26
  57.4 8.7 %collective-permute-start.19 = (bf16[32,4096]{1,0:T(8,128)(2,1)S(1)}, bf16[32,4096]{1,0:T(8,128)(2,1)S(1)}, u32[]{:S(2)}, u32[]{:S(2)}) collective-permute-start(bf16[32,4096]{1,0:T(8,128)(2,1)S(1)} %get-tuple-element.79), channel_id=1, source_target_pairs={{0,4},{1,3},{2,6},{3,1},{4,0},{5,7},{6,2},{7,5},{8,12},{9,11},{10,... | collective-permute-start | bytes 786440 | tf_op jit(solution)/shard_map/ppermute | solution.py:26
  59.6 6.5 %collective-permute-start.17 = (bf16[32,4096]{1,0:T(8,128)(2,1)S(1)}, bf16[32,4096]{1,0:T(8,128)(2,1)S(1)}, u32[]{:S(2)}, u32[]{:S(2)}) collective-permute-start(bf16[32,4096]{1,0:T(8,128)(2,1)S(1)} %get-tuple-element.102), channel_id=1, source_target_pairs={{0,2},{1,5},{2,0},{3,7},{4,6},{5,1},{6,4},{7,3},{8,10},{9,13},{10,... | collective-permute-start | bytes 786440 | tf_op jit(solution)/shard_map/ppermute | solution.py:26
  61.6 6.5 %collective-permute-start.20 = (bf16[32,3072]{1,0:T(8,128)(2,1)S(1)}, bf16[32,3072]{1,0:T(8,128)(2,1)S(1)}, u32[]{:S(2)}, u32[]{:S(2)}) collective-permute-start(bf16[32,3072]{1,0:T(8,128)(2,1)S(1)} %add_convert_fusion.5), channel_id=1, source_target_pairs={{0,2},{1,5},{2,0},{3,7},{4,6},{5,1},{6,4},{7,3},{8,10},{9,13},{10,... | collective-permute-start | bytes 589832 | tf_op jit(solution)/shard_map/ppermute | solution.py:26
  68.2 8.0 %collective-permute-start.24 = (bf16[32,3072]{1,0:T(8,128)(2,1)S(1)}, bf16[32,3072]{1,0:T(8,128)(2,1)S(1)}, u32[]{:S(2)}, u32[]{:S(2)}) collective-permute-start(bf16[32,3072]{1,0:T(8,128)(2,1)S(1)} %get-tuple-element.100), channel_id=1, source_target_pairs={{0,2},{1,5},{2,0},{3,7},{4,6},{5,1},{6,4},{7,3},{8,10},{9,13},{10,... | collective-permute-start | bytes 589832 | tf_op jit(solution)/shard_map/ppermute | solution.py:26
  70.2 5.9 %collective-permute-start.25 = (bf16[32,3072]{1,0:T(8,128)(2,1)S(1)}, bf16[32,3072]{1,0:T(8,128)(2,1)S(1)}, u32[]{:S(2)}, u32[]{:S(2)}) collective-permute-start(bf16[32,3072]{1,0:T(8,128)(2,1)S(1)} %get-tuple-element.101), channel_id=1, source_target_pairs={{0,4},{1,3},{2,6},{3,1},{4,0},{5,7},{6,2},{7,5},{8,12},{9,11},{10,... | collective-permute-start | bytes 589832 | tf_op jit(solution)/shard_map/ppermute | solution.py:26
  71.7 8.5 %collective-permute-start.21 = (bf16[8,4096]{1,0:T(8,128)(2,1)S(1)}, bf16[8,4096]{1,0:T(8,128)(2,1)S(1)}, u32[]{:S(2)}, u32[]{:S(2)}) collective-permute-start(bf16[8,4096]{1,0:T(8,128)(2,1)S(1)} %get-tuple-element.83), channel_id=1, source_target_pairs={{0,24},{1,25},{2,26},{3,27},{4,28},{5,29},{6,30},{7,31},{8,16},{9,... | collective-permute-start | bytes 196616 | tf_op jit(solution)/shard_map/ppermute | solution.py:26
  74.2 7.5 %collective-permute-start.22 = (bf16[8,4096]{1,0:T(8,128)(2,1)S(1)}, bf16[8,4096]{1,0:T(8,128)(2,1)S(1)}, u32[]{:S(2)}, u32[]{:S(2)}) collective-permute-start(bf16[8,4096]{1,0:T(8,128)(2,1)S(1)} %get-tuple-element.85), channel_id=1, source_target_pairs={{0,16},{1,17},{2,18},{3,19},{4,20},{5,21},{6,22},{7,23},{8,24},{9,... | collective-permute-start | bytes 196616 | tf_op jit(solution)/shard_map/ppermute | solution.py:26
  74.8 6.9 %collective-permute-start.23 = (bf16[8,4096]{1,0:T(8,128)(2,1)S(1)}, bf16[8,4096]{1,0:T(8,128)(2,1)S(1)}, u32[]{:S(2)}, u32[]{:S(2)}) collective-permute-start(bf16[8,4096]{1,0:T(8,128)(2,1)S(1)} %get-tuple-element.87), channel_id=1, source_target_pairs={{0,8},{1,9},{2,10},{3,11},{4,12},{5,13},{6,14},{7,15},{8,0},{9,1},... | collective-permute-start | bytes 196616 | tf_op jit(solution)/shard_map/ppermute | solution.py:26
  76.2 6.3 %collective-permute-start.26 = (bf16[8,3072]{1,0:T(8,128)(2,1)S(1)}, bf16[8,3072]{1,0:T(8,128)(2,1)S(1)}, u32[]{:S(2)}, u32[]{:S(2)}) collective-permute-start(bf16[8,3072]{1,0:T(8,128)(2,1)S(1)} %get-tuple-element.97), channel_id=1, source_target_pairs={{0,24},{1,25},{2,26},{3,27},{4,28},{5,29},{6,30},{7,31},{8,16},{9,... | collective-permute-start | bytes 147464 | tf_op jit(solution)/shard_map/ppermute | solution.py:26
  80.2 4.4 %collective-permute-start.28 = (bf16[8,3072]{1,0:T(8,128)(2,1)S(1)}, bf16[8,3072]{1,0:T(8,128)(2,1)S(1)}, u32[]{:S(2)}, u32[]{:S(2)}) collective-permute-start(bf16[8,3072]{1,0:T(8,128)(2,1)S(1)} %get-tuple-element.98), channel_id=1, source_target_pairs={{0,8},{1,9},{2,10},{3,11},{4,12},{5,13},{6,14},{7,15},{8,0},{9,1},... | collective-permute-start | bytes 147464 | tf_op jit(solution)/shard_map/ppermute | solution.py:26
  80.2 5.0 %collective-permute-start.27 = (bf16[8,3072]{1,0:T(8,128)(2,1)S(1)}, bf16[8,3072]{1,0:T(8,128)(2,1)S(1)}, u32[]{:S(2)}, u32[]{:S(2)}) collective-permute-start(bf16[8,3072]{1,0:T(8,128)(2,1)S(1)} %get-tuple-element.99), channel_id=1, source_target_pairs={{0,16},{1,17},{2,18},{3,19},{4,20},{5,21},{6,22},{7,23},{8,24},{9,... | collective-permute-start | bytes 147464 | tf_op jit(solution)/shard_map/ppermute | solution.py:26

commit v17 on v16

--- a/solution.py
+++ b/solution.py
@@ -298,7 +298,7 @@
     wide = step_width(width)
     cut = wide * max(1, 4 * (width // wide) // 7)
     own, low, far_side, *far_across = experts(held, weights, cut)
-    far_across[1], far_side, low, late = tied(far_across[1], far_side, low, late)
+    far_side, low, late = tied(far_side, low, late)
     pieces.append(late)
 
     far_across = [swapped(value, twin) for value in far_across]

time: 86.2 us -> 86.5 us (level)
  waiting for transfers between devices: 28.7 us -> 29.7 us
    ppermute x27, waiting for transfers between devices: 28.7 us -> 29.7 us  [swapped(): return lax.ppermute(value, 'dp', [(i, partner(i)) for i in range(peers)])]
  transfers between devices with their start and end apart: 29 -> 29, of which waited for: 13 -> 14; matrix products, arithmetic and copies ran while one was open for 6% -> 6% of each run, Pallas kernels for 14% -> 14%
where the time goes in v17:
time: 86.5 us; the launch traced here: 86.2 us
  starting transfers between devices  37.5 us (43%)
  waiting for transfers between devices  29.7 us (34%)
  Pallas kernels  11.8 us (14%)
  other arithmetic  4.8 us (6%)
  local copies, waits for them, and re-layouts  1.6 us (2%)
    ppermute x27, starting transfers between devices, swapped(): return lax.ppermute(value, 'dp', [(i, partner(i)) for i in range(peers)])  35.9 us
    ppermute x27, waiting for transfers between devices, swapped(): return lax.ppermute(value, 'dp', [(i, partner(i)) for i in range(peers)])  29.7 us
    pallas_call x1, Pallas kernels, experts(): pl.pallas_call(lambda *refs: expert_kernel(wide, *refs), in_specs=[whole]...  5.3 us
    pallas_call x1, Pallas kernels, fetched(): pl.pallas_call(fetch_kernel, in_specs=[pl.BlockSpec(memory_space=pltpu.HB...  4.23 us
    reduce_sum x1, other arithmetic, body(): jnp.sum(jnp.where(routed_experts == targets[r], route_weights, 0.0), axis=1)  3.31 us
    pallas_call x1, Pallas kernels, attend(): pl.pallas_call(lambda *refs: attend_kernel(spans, *refs), in_specs=[scala...  2.3 us
  transfers between devices with their start and end apart: 29, of which 14 were waited for; matrix products, arithmetic and copies ran while one was open for 6% of the time, Pallas kernels for 14%

profile of v17, /device:TPU:0, one launch (start us, length us, event | category | flops | bytes accessed | tf_op | source)
XLA Modules:
  0.0 86.2 jit_solution(6936067716438744700)
XLA Ops:
  0.6 0.7 collective-permute-start.3
  1.4 4.1 %collective-permute-start.1 = (bf16[8,7168]{1,0:T(8,128)(2,1)}, bf16[8,7168]{1,0:T(8,128)(2,1)S(1)}, u32[]{:S(2)}, u32[]{:S(2)}) collective-permute-start(bf16[8,7168]{1,0:T(8,128)(2,1)} %param.16), channel_id=1, source_target_pairs={{0,16},{1,17},{2,18},{3,19},{4,20},{5,21},{6,22},{7,23},{8,24},{9,... | collective-permute-start | bytes 344072 | tf_op jit(solution)/shard_map/ppermute | solution.py:26
  5.5 1.3 %collective-permute-start = (bf16[8,7168]{1,0:T(8,128)(2,1)}, bf16[8,7168]{1,0:T(8,128)(2,1)S(1)}, u32[]{:S(2)}, u32[]{:S(2)}) collective-permute-start(bf16[8,7168]{1,0:T(8,128)(2,1)} %param.16), channel_id=1, source_target_pairs={{0,24},{1,25},{2,26},{3,27},{4,28},{5,29},{6,30},{7,31},{8,16},{9,... | collective-permute-start | bytes 344072 | tf_op jit(solution)/shard_map/ppermute | solution.py:26
  6.8 0.2 collective-permute-start.2
  7.0 0.6 fusion.4
  7.7 0.9 %pad.4 = bf16[32,7168]{1,0:T(8,128)(2,1)S(1)} pad(bf16[8,7168]{1,0:T(8,128)(2,1)} %param.16, bf16[]{:T(256)} %constant.19.clone.1), padding=0_24x0_0 | pad | bytes 573442 | tf_op jit(solution)/shard_map/jit(_pad)/pad | solution.py:277
  8.6 3.3 %fusion.3 = (f32[8]{0:T(128)S(1)}, f32[8]{0:T(128)S(1)}, f32[8]{0:T(128)S(1)}, f32[8]{0:T(128)S(1)}) fusion(f32[8,2]{0,1:T(2,128)} %param.18, s32[8,2]{0,1:T(2,128)} %param.17, s32[]{:T(128)} %bitcast.3, s32[]{:T(128)} %bitcast.1, s32[]{:T(128)} %bitcast, s32[]{:T(128)} %bitcast.2), kind=kLoop, calls=%fused_computation.23 | loop fusion | flops 160 | bytes 272 | tf_op jit(solution)/shard_map/reduce_sum | solution.py:240
  11.9 1.4 %collective-permute-done = bf16[8,7168]{1,0:T(8,128)(2,1)S(1)} collective-permute-done((bf16[8,7168]{1,0:T(8,128)(2,1)}, bf16[8,7168]{1,0:T(8,128)(2,1)S(1)}, u32[]{:S(2)}, u32[]{:S(2)}) %collective-permute-start) | collective-permute-done | bytes 114720 | tf_op jit(solution)/shard_map/ppermute | solution.py:26
  13.3 1.2 %collective-permute-done.2 = bf16[8,7168]{1,0:T(8,128)(2,1)S(1)} collective-permute-done((bf16[8,7168]{1,0:T(8,128)(2,1)}, bf16[8,7168]{1,0:T(8,128)(2,1)S(1)}, u32[]{:S(2)}, u32[]{:S(2)}) %collective-permute-start.2) | collective-permute-done | bytes 114720 | tf_op jit(solution)/shard_map/ppermute | solution.py:26
  14.6 5.7 %collective-permute-start.4 = (bf16[32,7168]{1,0:T(8,128)(2,1)S(1)}, bf16[32,7168]{1,0:T(8,128)(2,1)S(1)}, u32[]{:S(2)}, u32[]{:S(2)}) collective-permute-start(bf16[32,7168]{1,0:T(8,128)(2,1)S(1)} %constant_dynamic-update-slice_fusion.refs_0_), channel_id=1, source_target_pairs={{0,4},{1,3},{2,6},{3,1},{4,0},{5,7},{6,2},{7,5},{8,12},{9,11},{10,... | collective-permute-start | bytes 1376264 | tf_op jit(solution)/shard_map/ppermute | solution.py:26
  20.3 0.5 collective-permute-start.7
  20.8 5.9 %collective-permute-done.4.refs_1_ = bf16[32,7168]{1,0:T(8,128)(2,1)S(1)} collective-permute-done((bf16[32,7168]{1,0:T(8,128)(2,1)S(1)}, bf16[32,7168]{1,0:T(8,128)(2,1)S(1)}, u32[]{:S(2)}, u32[]{:S(2)}) %collective-permute-start.4) | collective-permute-done | bytes 458784 | tf_op jit(solution)/shard_map/ppermute | solution.py:26
  26.7 1.1 %collective-permute-start.6 = (bf16[32,7168]{1,0:T(8,128)(2,1)S(1)}, bf16[32,7168]{1,0:T(8,128)(2,1)S(1)}, u32[]{:S(2)}, u32[]{:S(2)}) collective-permute-start(bf16[32,7168]{1,0:T(8,128)(2,1)S(1)} %collective-permute-done.4.refs_1_), channel_id=1, source_target_pairs={{0,2},{1,5},{2,0},{3,7},{4,6},{5,1},{6,4},{7,3},{8,10},{9,13},{10,... | collective-permute-start | bytes 1376264 | tf_op jit(solution)/shard_map/ppermute | solution.py:26
  27.8 0.9 %collective-permute-start.5 = (bf16[32,7168]{1,0:T(8,128)(2,1)S(1)}, bf16[32,7168]{1,0:T(8,128)(2,1)S(1)}, u32[]{:S(2)}, u32[]{:S(2)}) collective-permute-start(bf16[32,7168]{1,0:T(8,128)(2,1)S(1)} %constant_dynamic-update-slice_fusion.refs_0_), channel_id=1, source_target_pairs={{0,2},{1,5},{2,0},{3,7},{4,6},{5,1},{6,4},{7,3},{8,10},{9,13},{10,... | collective-permute-start | bytes 1376264 | tf_op jit(solution)/shard_map/ppermute | solution.py:26
  28.7 4.2 %shard_map.122 = (bf16[1,7168,256]{2,1,0:T(8,128)(2,1)S(1)}, bf16[1,7168,256]{2,1,0:T(8,128)(2,1)S(1)}, bf16[1,256,7168]{2,1,0:T(8,128)(2,1)S(1)}) custom-call(bf16[1,7168,256]{2,1,0:T(8,128)(2,1)} %refs_0_.2, bf16[1,7168,256]{2,1,0:T(8,128)(2,1)} %refs_1_.2, bf16[1,256,7168]{2,1,0:T(8,128)(2,1)} %refs_2_.2), custom_call_target="tpu_custom_call" | custom-call | bytes 22020096 | tf_op jit(solution)/shard_map/pallas_call | solution.py:127
  33.0 2.2 %collective-permute-done.6.refs_3_ = bf16[32,7168]{1,0:T(8,128)(2,1)S(1)} collective-permute-done((bf16[32,7168]{1,0:T(8,128)(2,1)S(1)}, bf16[32,7168]{1,0:T(8,128)(2,1)S(1)}, u32[]{:S(2)}, u32[]{:S(2)}) %collective-permute-start.6) | collective-permute-done | bytes 458784 | tf_op jit(solution)/shard_map/ppermute | solution.py:26
  35.2 0.9 collective-permute-start.13
  36.1 4.0 %collective-permute-done.5.refs_2_ = bf16[32,7168]{1,0:T(8,128)(2,1)S(1)} collective-permute-done((bf16[32,7168]{1,0:T(8,128)(2,1)S(1)}, bf16[32,7168]{1,0:T(8,128)(2,1)S(1)}, u32[]{:S(2)}, u32[]{:S(2)}) %collective-permute-start.5) | collective-permute-done | bytes 458784 | tf_op jit(solution)/shard_map/ppermute | solution.py:26
  40.1 0.5 collective-permute-start.11
  40.6 1.3 %collective-permute-done.10.refs_6_ = bf16[32,7168]{1,0:T(8,128)(2,1)S(1)} collective-permute-done((bf16[32,7168]{1,0:T(8,128)(2,1)S(1)}, bf16[32,7168]{1,0:T(8,128)(2,1)S(1)}, u32[]{:S(2)}, u32[]{:S(2)}) %collective-permute-start.10) | collective-permute-done | bytes 458784 | tf_op jit(solution)/shard_map/ppermute | solution.py:26
  41.9 0.7 collective-permute-done.11.refs_7_
  42.6 5.3 %shard_map.123 = (bf16[128,7168]{1,0:T(8,128)(2,1)S(1)}, bf16[64,7168]{1,0:T(8,128)(2,1)S(1)}, bf16[32,7168]{1,0:T(8,128)(2,1)S(1)}, bf16[32,4096]{1,0:T(8,128)(2,1)S(1)}, bf16[32,3072]{1,0:T(8,128)(2,1)S(1)}) custom-call(bf16[32,7168]{1,0:T(8,128)(2,1)S(1)} %constant_dynamic-update-slice_fusion.refs_0_, ...), custom_call_target="tpu_custom_call" | custom-call | tf_op jit(solution)/shard_map/pallas_call | solution.py:193
  47.9 0.2 collective-permute-start.12
  48.1 0.4 collective-permute-start.18
  48.5 2.2 %collective-permute-start.15 = (bf16[64,7168]{1,0:T(8,128)(2,1)S(1)}, bf16[64,7168]{1,0:T(8,128)(2,1)S(1)}, u32[]{:S(2)}, u32[]{:S(2)}) collective-permute-start(bf16[64,7168]{1,0:T(8,128)(2,1)S(1)} %get-tuple-element.73), channel_id=1, source_target_pairs={{0,1},{1,0},{2,3},{3,2},{4,5},{5,4},{6,7},{7,6},{8,9},{9,8},{10,11... | collective-permute-start | bytes 2752520 | tf_op jit(solution)/shard_map/ppermute | solution.py:26
  50.8 1.9 %collective-permute-start.14 = (bf16[32,4096]{1,0:T(8,128)(2,1)S(1)}, bf16[32,4096]{1,0:T(8,128)(2,1)S(1)}, u32[]{:S(2)}, u32[]{:S(2)}) collective-permute-start(bf16[32,4096]{1,0:T(8,128)(2,1)S(1)} %add_convert_fusion.2), channel_id=1, source_target_pairs={{0,2},{1,5},{2,0},{3,7},{4,6},{5,1},{6,4},{7,3},{8,10},{9,13},{10,... | collective-permute-start | bytes 786440 | tf_op jit(solution)/shard_map/ppermute | solution.py:26
  52.7 2.3 %shard_map.124 = bf16[8,64,512]{2,1,0:T(8,128)(2,1)} custom-call(s32[8]{0:T(128)S(1)} %copy-done.3, s32[8]{0:T(128)S(1)} %copy-done.4, bf16[8,64,576]{2,1,0:T(8,128)(2,1)S(1)} %copy-done.1, bf16[8,96,576]{2,1,0:T(8,128)(2,1)S(1)} %copy-done, bf16[8,96,576]{2,1,0:T(8,128)(2,1)S(1)} %collective-permute-done.9.refs_4_, bf16[8,576]{1,0:T(8,128)(2,1)S(1)} %copy-done.2, ...), custom_call_target="tpu_custom_call" | custom-call | flops 106954752 | bytes 4653056 | tf_op jit(solution)/shard_map/pallas_call | solution.py:99
  55.0 2.1 %collective-permute-done.14 = bf16[32,4096]{1,0:T(8,128)(2,1)S(1)} collective-permute-done((bf16[32,4096]{1,0:T(8,128)(2,1)S(1)}, bf16[32,4096]{1,0:T(8,128)(2,1)S(1)}, u32[]{:S(2)}, u32[]{:S(2)}) %collective-permute-start.14) | collective-permute-done | bytes 262176 | tf_op jit(solution)/shard_map/ppermute | solution.py:26
  57.2 0.2 add_convert_fusion.1
  57.4 2.2 %collective-permute-start.19 = (bf16[32,4096]{1,0:T(8,128)(2,1)S(1)}, bf16[32,4096]{1,0:T(8,128)(2,1)S(1)}, u32[]{:S(2)}, u32[]{:S(2)}) collective-permute-start(bf16[32,4096]{1,0:T(8,128)(2,1)S(1)} %get-tuple-element.77), channel_id=1, source_target_pairs={{0,4},{1,3},{2,6},{3,1},{4,0},{5,7},{6,2},{7,5},{8,12},{9,11},{10,... | collective-permute-start | bytes 786440 | tf_op jit(solution)/shard_map/ppermute | solution.py:26
  59.5 2.0 %collective-permute-start.17 = (bf16[32,4096]{1,0:T(8,128)(2,1)S(1)}, bf16[32,4096]{1,0:T(8,128)(2,1)S(1)}, u32[]{:S(2)}, u32[]{:S(2)}) collective-permute-start(bf16[32,4096]{1,0:T(8,128)(2,1)S(1)} %get-tuple-element.100), channel_id=1, source_target_pairs={{0,2},{1,5},{2,0},{3,7},{4,6},{5,1},{6,4},{7,3},{8,10},{9,13},{10,... | collective-permute-start | bytes 786440 | tf_op jit(solution)/shard_map/ppermute | solution.py:26
  61.6 4.9 %collective-permute-done.19 = bf16[32,4096]{1,0:T(8,128)(2,1)S(1)} collective-permute-done((bf16[32,4096]{1,0:T(8,128)(2,1)S(1)}, bf16[32,4096]{1,0:T(8,128)(2,1)S(1)}, u32[]{:S(2)}, u32[]{:S(2)}) %collective-permute-start.19) | collective-permute-done | bytes 262176 | tf_op jit(solution)/shard_map/ppermute | solution.py:26
  66.7 1.4 %collective-permute-done.20 = bf16[32,3072]{1,0:T(8,128)(2,1)S(1)} collective-permute-done((bf16[32,3072]{1,0:T(8,128)(2,1)S(1)}, bf16[32,3072]{1,0:T(8,128)(2,1)S(1)}, u32[]{:S(2)}, u32[]{:S(2)}) %collective-permute-start.20) | collective-permute-done | bytes 196640 | tf_op jit(solution)/shard_map/ppermute | solution.py:26
  68.0 0.1 add_convert_fusion.4
  68.1 2.1 %collective-permute-start.24 = (bf16[32,3072]{1,0:T(8,128)(2,1)S(1)}, bf16[32,3072]{1,0:T(8,128)(2,1)S(1)}, u32[]{:S(2)}, u32[]{:S(2)}) collective-permute-start(bf16[32,3072]{1,0:T(8,128)(2,1)S(1)} %get-tuple-element.98), channel_id=1, source_target_pairs={{0,2},{1,5},{2,0},{3,7},{4,6},{5,1},{6,4},{7,3},{8,10},{9,13},{10,... | collective-permute-start | bytes 589832 | tf_op jit(solution)/shard_map/ppermute | solution.py:26
  70.2 1.0 %collective-permute-start.25 = (bf16[32,3072]{1,0:T(8,128)(2,1)S(1)}, bf16[32,3072]{1,0:T(8,128)(2,1)S(1)}, u32[]{:S(2)}, u32[]{:S(2)}) collective-permute-start(bf16[32,3072]{1,0:T(8,128)(2,1)S(1)} %get-tuple-element.99), channel_id=1, source_target_pairs={{0,4},{1,3},{2,6},{3,1},{4,0},{5,7},{6,2},{7,5},{8,12},{9,11},{10,... | collective-permute-start | bytes 589832 | tf_op jit(solution)/shard_map/ppermute | solution.py:26
  71.2 2.5 %collective-permute-start.21 = (bf16[8,4096]{1,0:T(8,128)(2,1)S(1)}, bf16[8,4096]{1,0:T(8,128)(2,1)S(1)}, u32[]{:S(2)}, u32[]{:S(2)}) collective-permute-start(bf16[8,4096]{1,0:T(8,128)(2,1)S(1)} %get-tuple-element.81), channel_id=1, source_target_pairs={{0,24},{1,25},{2,26},{3,27},{4,28},{5,29},{6,30},{7,31},{8,16},{9,... | collective-permute-start | bytes 196616 | tf_op jit(solution)/shard_map/ppermute | solution.py:26
  73.7 0.6 collective-permute-start.22
  74.3 1.3 %collective-permute-start.23 = (bf16[8,4096]{1,0:T(8,128)(2,1)S(1)}, bf16[8,4096]{1,0:T(8,128)(2,1)S(1)}, u32[]{:S(2)}, u32[]{:S(2)}) collective-permute-start(bf16[8,4096]{1,0:T(8,128)(2,1)S(1)} %get-tuple-element.85), channel_id=1, source_target_pairs={{0,8},{1,9},{2,10},{3,11},{4,12},{5,13},{6,14},{7,15},{8,0},{9,1},... | collective-permute-start | bytes 196616 | tf_op jit(solution)/shard_map/ppermute | solution.py:26
  75.6 0.3 collective-permute-done.25
  76.0 4.2 %collective-permute-start.26 = (bf16[8,3072]{1,0:T(8,128)(2,1)S(1)}, bf16[8,3072]{1,0:T(8,128)(2,1)S(1)}, u32[]{:S(2)}, u32[]{:S(2)}) collective-permute-start(bf16[8,3072]{1,0:T(8,128)(2,1)S(1)} %get-tuple-element.95), channel_id=1, source_target_pairs={{0,24},{1,25},{2,26},{3,27},{4,28},{5,29},{6,30},{7,31},{8,16},{9,... | collective-permute-start | bytes 147464 | tf_op jit(solution)/shard_map/ppermute | solution.py:26
  80.2 0.3 collective-permute-start.28
  80.5 0.6 collective-permute-start.27
  81.1 0.1 add_convert_fusion.6
  81.3 1.2 %collective-permute-done.26 = bf16[8,3072]{1,0:T(8,128)(2,1)S(1)} collective-permute-done((bf16[8,3072]{1,0:T(8,128)(2,1)S(1)}, bf16[8,3072]{1,0:T(8,128)(2,1)S(1)}, u32[]{:S(2)}, u32[]{:S(2)}) %collective-permute-start.26) | collective-permute-done | bytes 49184 | tf_op jit(solution)/shard_map/ppermute | solution.py:26
  82.4 2.2 %collective-permute-done.28 = bf16[8,3072]{1,0:T(8,128)(2,1)S(1)} collective-permute-done((bf16[8,3072]{1,0:T(8,128)(2,1)S(1)}, bf16[8,3072]{1,0:T(8,128)(2,1)S(1)}, u32[]{:S(2)}, u32[]{:S(2)}) %collective-permute-start.28) | collective-permute-done | bytes 49184 | tf_op jit(solution)/shard_map/ppermute | solution.py:26
  84.6 0.9 collective-permute-done.27
  85.6 0.7 pad_maximum_fusion
  (40 shorter events, 0.6 us)
Async XLA Ops:
  0.6 13.9 %collective-permute-start.3 = (bf16[8,96,576]{2,1,0:T(8,128)(2,1)}, bf16[8,96,576]{2,1,0:T(8,128)(2,1)S(1)}, u32[]{:S(2)}, u32[]{:S(2)}) collective-permute-start(bf16[8,96,576]{2,1,0:T(8,128)(2,1)} %refs_3_.1), channel_id=1, source_target_pairs={{1,2},{3,4},{5,6},{6,5},{9,10},{11,12},{13,14},{14,13},{17,18},{19... | collective-permute-start | bytes 2654216 | tf_op jit(solution)/shard_map/ppermute | solution.py:47
  1.4 10.6 %collective-permute-start.1 = (bf16[8,7168]{1,0:T(8,128)(2,1)}, bf16[8,7168]{1,0:T(8,128)(2,1)S(1)}, u32[]{:S(2)}, u32[]{:S(2)}) collective-permute-start(bf16[8,7168]{1,0:T(8,128)(2,1)} %param.16), channel_id=1, source_target_pairs={{0,16},{1,17},{2,18},{3,19},{4,20},{5,21},{6,22},{7,23},{8,24},{9,... | collective-permute-start | bytes 344072 | tf_op jit(solution)/shard_map/ppermute | solution.py:26
  5.5 7.8 %collective-permute-start = (bf16[8,7168]{1,0:T(8,128)(2,1)}, bf16[8,7168]{1,0:T(8,128)(2,1)S(1)}, u32[]{:S(2)}, u32[]{:S(2)}) collective-permute-start(bf16[8,7168]{1,0:T(8,128)(2,1)} %param.16), channel_id=1, source_target_pairs={{0,24},{1,25},{2,26},{3,27},{4,28},{5,29},{6,30},{7,31},{8,16},{9,... | collective-permute-start | bytes 344072 | tf_op jit(solution)/shard_map/ppermute | solution.py:26
  6.8 7.7 %collective-permute-start.2 = (bf16[8,7168]{1,0:T(8,128)(2,1)}, bf16[8,7168]{1,0:T(8,128)(2,1)S(1)}, u32[]{:S(2)}, u32[]{:S(2)}) collective-permute-start(bf16[8,7168]{1,0:T(8,128)(2,1)} %param.16), channel_id=1, source_target_pairs={{0,8},{1,9},{2,10},{3,11},{4,12},{5,13},{6,14},{7,15},{8,0},{9,1},... | collective-permute-start | bytes 344072 | tf_op jit(solution)/shard_map/ppermute | solution.py:26
  14.6 20.6 %copy-start = (bf16[8,96,576]{2,1,0:T(8,128)(2,1)S(1)}, bf16[8,96,576]{2,1,0:T(8,128)(2,1)}, u32[]{:S(2)}) copy-start(bf16[8,96,576]{2,1,0:T(8,128)(2,1)} %refs_3_.1) | copy-start | bytes 2654212
  14.6 12.1 %collective-permute-start.4 = (bf16[32,7168]{1,0:T(8,128)(2,1)S(1)}, bf16[32,7168]{1,0:T(8,128)(2,1)S(1)}, u32[]{:S(2)}, u32[]{:S(2)}) collective-permute-start(bf16[32,7168]{1,0:T(8,128)(2,1)S(1)} %constant_dynamic-update-slice_fusion.refs_0_), channel_id=1, source_target_pairs={{0,4},{1,3},{2,6},{3,1},{4,0},{5,7},{6,2},{7,5},{8,12},{9,11},{10,... | collective-permute-start | bytes 1376264 | tf_op jit(solution)/shard_map/ppermute | solution.py:26
  20.2 12.7 %collective-permute-start.9 = (bf16[8,96,576]{2,1,0:T(8,128)(2,1)}, bf16[8,96,576]{2,1,0:T(8,128)(2,1)S(1)}, u32[]{:S(2)}, u32[]{:S(2)}) collective-permute-start(bf16[8,96,576]{2,1,0:T(8,128)(2,1)} %refs_3_.1), channel_id=1, source_target_pairs={{0,1},{1,0},{2,3},{3,2},{4,5},{5,4},{6,7},{7,6},{8,9},{9,8},{10,11... | collective-permute-start | bytes 2654216 | tf_op jit(solution)/shard_map/ppermute | solution.py:26
  20.3 12.7 %collective-permute-start.7 = (bf16[32,7168]{1,0:T(8,128)(2,1)S(1)}, bf16[32,7168]{1,0:T(8,128)(2,1)S(1)}, u32[]{:S(2)}, u32[]{:S(2)}) collective-permute-start(bf16[32,7168]{1,0:T(8,128)(2,1)S(1)} %constant_dynamic-update-slice_fusion.refs_0_), channel_id=1, source_target_pairs={{0,1},{1,0},{2,3},{3,2},{4,5},{5,4},{6,7},{7,6},{8,9},{9,8},{10,11... | collective-permute-start | bytes 1376264 | tf_op jit(solution)/shard_map/ppermute | solution.py:26
  26.7 6.3 %collective-permute-start.8 = (bf16[32,7168]{1,0:T(8,128)(2,1)S(1)}, bf16[32,7168]{1,0:T(8,128)(2,1)S(1)}, u32[]{:S(2)}, u32[]{:S(2)}) collective-permute-start(bf16[32,7168]{1,0:T(8,128)(2,1)S(1)} %collective-permute-done.4.refs_1_), channel_id=1, source_target_pairs={{0,1},{1,0},{2,3},{3,2},{4,5},{5,4},{6,7},{7,6},{8,9},{9,8},{10,11... | collective-permute-start | bytes 1376264 | tf_op jit(solution)/shard_map/ppermute | solution.py:26
  26.7 8.5 %collective-permute-start.6 = (bf16[32,7168]{1,0:T(8,128)(2,1)S(1)}, bf16[32,7168]{1,0:T(8,128)(2,1)S(1)}, u32[]{:S(2)}, u32[]{:S(2)}) collective-permute-start(bf16[32,7168]{1,0:T(8,128)(2,1)S(1)} %collective-permute-done.4.refs_1_), channel_id=1, source_target_pairs={{0,2},{1,5},{2,0},{3,7},{4,6},{5,1},{6,4},{7,3},{8,10},{9,13},{10,... | collective-permute-start | bytes 1376264 | tf_op jit(solution)/shard_map/ppermute | solution.py:26
  27.8 12.3 %collective-permute-start.5 = (bf16[32,7168]{1,0:T(8,128)(2,1)S(1)}, bf16[32,7168]{1,0:T(8,128)(2,1)S(1)}, u32[]{:S(2)}, u32[]{:S(2)}) collective-permute-start(bf16[32,7168]{1,0:T(8,128)(2,1)S(1)} %constant_dynamic-update-slice_fusion.refs_0_), channel_id=1, source_target_pairs={{0,2},{1,5},{2,0},{3,7},{4,6},{5,1},{6,4},{7,3},{8,10},{9,13},{10,... | collective-permute-start | bytes 1376264 | tf_op jit(solution)/shard_map/ppermute | solution.py:26
  35.2 17.5 %copy-start.2 = (bf16[8,576]{1,0:T(8,128)(2,1)S(1)}, bf16[8,576]{1,0:T(8,128)(2,1)}, u32[]{:S(2)}) copy-start(bf16[8,576]{1,0:T(8,128)(2,1)} %refs_5_.1) | copy-start | bytes 27652
  35.2 17.5 %copy-start.3 = (s32[8]{0:T(128)S(1)}, s32[8]{0:T(128)}, u32[]{:S(2)}) copy-start(s32[8]{0:T(128)} %refs_0_.3) | copy-start | bytes 100
  35.2 17.5 %copy-start.4 = (s32[8]{0:T(128)S(1)}, s32[8]{0:T(128)}, u32[]{:S(2)}) copy-start(s32[8]{0:T(128)} %refs_1_.3) | copy-start | bytes 100
  35.2 13.3 %collective-permute-start.13 = (bf16[8,96,576]{2,1,0:T(8,128)(2,1)S(1)}, bf16[8,96,576]{2,1,0:T(8,128)(2,1)S(1)}, u32[]{:S(2)}, u32[]{:S(2)}) collective-permute-start(bf16[8,96,576]{2,1,0:T(8,128)(2,1)S(1)} %copy-done), channel_id=1, source_target_pairs={{2,1},{4,3},{7,8},{8,7},{10,9},{12,11},{15,16},{16,15},{18,17},{20... | collective-permute-start | bytes 2654216 | tf_op jit(solution)/shard_map/ppermute | solution.py:47
  40.1 1.8 %collective-permute-start.10 = (bf16[32,7168]{1,0:T(8,128)(2,1)S(1)}, bf16[32,7168]{1,0:T(8,128)(2,1)S(1)}, u32[]{:S(2)}, u32[]{:S(2)}) collective-permute-start(bf16[32,7168]{1,0:T(8,128)(2,1)S(1)} %collective-permute-done.5.refs_2_), channel_id=1, source_target_pairs={{0,1},{1,0},{2,3},{3,2},{4,5},{5,4},{6,7},{7,6},{8,9},{9,8},{10,11... | collective-permute-start | bytes 1376264 | tf_op jit(solution)/shard_map/ppermute | solution.py:26
  40.1 2.5 %collective-permute-start.11 = (bf16[32,7168]{1,0:T(8,128)(2,1)S(1)}, bf16[32,7168]{1,0:T(8,128)(2,1)S(1)}, u32[]{:S(2)}, u32[]{:S(2)}) collective-permute-start(bf16[32,7168]{1,0:T(8,128)(2,1)S(1)} %collective-permute-done.6.refs_3_), channel_id=1, source_target_pairs={{0,1},{1,0},{2,3},{3,2},{4,5},{5,4},{6,7},{7,6},{8,9},{9,8},{10,11... | collective-permute-start | bytes 1376264 | tf_op jit(solution)/shard_map/ppermute | solution.py:26
  47.9 4.8 %copy-start.1 = (bf16[8,64,576]{2,1,0:T(8,128)(2,1)S(1)}, bf16[8,64,576]{2,1,0:T(8,128)(2,1)}, u32[]{:S(2)}) copy-start(bf16[8,64,576]{2,1,0:T(8,128)(2,1)} %refs_2_.3) | copy-start | bytes 1769476
  47.9 2.8 %collective-permute-start.12 = (bf16[32,4096]{1,0:T(8,128)(2,1)S(1)}, bf16[32,4096]{1,0:T(8,128)(2,1)S(1)}, u32[]{:S(2)}, u32[]{:S(2)}) collective-permute-start(bf16[32,4096]{1,0:T(8,128)(2,1)S(1)} %get-tuple-element.62), channel_id=1, source_target_pairs={{0,1},{1,0},{2,3},{3,2},{4,5},{5,4},{6,7},{7,6},{8,9},{9,8},{10,11... | collective-permute-start | bytes 786440 | tf_op jit(solution)/shard_map/ppermute | solution.py:26
  48.1 4.5 %collective-permute-start.18 = (bf16[32,3072]{1,0:T(8,128)(2,1)S(1)}, bf16[32,3072]{1,0:T(8,128)(2,1)S(1)}, u32[]{:S(2)}, u32[]{:S(2)}) collective-permute-start(bf16[32,3072]{1,0:T(8,128)(2,1)S(1)} %get-tuple-element.76), channel_id=1, source_target_pairs={{0,1},{1,0},{2,3},{3,2},{4,5},{5,4},{6,7},{7,6},{8,9},{9,8},{10,11... | collective-permute-start | bytes 589832 | tf_op jit(solution)/shard_map/ppermute | solution.py:26
  48.5 8.7 %collective-permute-start.15 = (bf16[64,7168]{1,0:T(8,128)(2,1)S(1)}, bf16[64,7168]{1,0:T(8,128)(2,1)S(1)}, u32[]{:S(2)}, u32[]{:S(2)}) collective-permute-start(bf16[64,7168]{1,0:T(8,128)(2,1)S(1)} %get-tuple-element.73), channel_id=1, source_target_pairs={{0,1},{1,0},{2,3},{3,2},{4,5},{5,4},{6,7},{7,6},{8,9},{9,8},{10,11... | collective-permute-start | bytes 2752520 | tf_op jit(solution)/shard_map/ppermute | solution.py:26
  50.8 6.4 %collective-permute-start.14 = (bf16[32,4096]{1,0:T(8,128)(2,1)S(1)}, bf16[32,4096]{1,0:T(8,128)(2,1)S(1)}, u32[]{:S(2)}, u32[]{:S(2)}) collective-permute-start(bf16[32,4096]{1,0:T(8,128)(2,1)S(1)} %add_convert_fusion.2), channel_id=1, source_target_pairs={{0,2},{1,5},{2,0},{3,7},{4,6},{5,1},{6,4},{7,3},{8,10},{9,13},{10,... | collective-permute-start | bytes 786440 | tf_op jit(solution)/shard_map/ppermute | solution.py:26
  52.6 4.5 %collective-permute-start.16 = (bf16[32,7168]{1,0:T(8,128)(2,1)S(1)}, bf16[32,7168]{1,0:T(8,128)(2,1)S(1)}, u32[]{:S(2)}, u32[]{:S(2)}) collective-permute-start(bf16[32,7168]{1,0:T(8,128)(2,1)S(1)} %get-tuple-element.74), channel_id=1, source_target_pairs={{0,1},{1,0},{2,3},{3,2},{4,5},{5,4},{6,7},{7,6},{8,9},{9,8},{10,11... | collective-permute-start | bytes 1376264 | tf_op jit(solution)/shard_map/ppermute | solution.py:26
  57.4 9.1 %collective-permute-start.19 = (bf16[32,4096]{1,0:T(8,128)(2,1)S(1)}, bf16[32,4096]{1,0:T(8,128)(2,1)S(1)}, u32[]{:S(2)}, u32[]{:S(2)}) collective-permute-start(bf16[32,4096]{1,0:T(8,128)(2,1)S(1)} %get-tuple-element.77), channel_id=1, source_target_pairs={{0,4},{1,3},{2,6},{3,1},{4,0},{5,7},{6,2},{7,5},{8,12},{9,11},{10,... | collective-permute-start | bytes 786440 | tf_op jit(solution)/shard_map/ppermute | solution.py:26
  59.5 7.0 %collective-permute-start.17 = (bf16[32,4096]{1,0:T(8,128)(2,1)S(1)}, bf16[32,4096]{1,0:T(8,128)(2,1)S(1)}, u32[]{:S(2)}, u32[]{:S(2)}) collective-permute-start(bf16[32,4096]{1,0:T(8,128)(2,1)S(1)} %get-tuple-element.100), channel_id=1, source_target_pairs={{0,2},{1,5},{2,0},{3,7},{4,6},{5,1},{6,4},{7,3},{8,10},{9,13},{10,... | collective-permute-start | bytes 786440 | tf_op jit(solution)/shard_map/ppermute | solution.py:26
  61.6 6.5 %collective-permute-start.20 = (bf16[32,3072]{1,0:T(8,128)(2,1)S(1)}, bf16[32,3072]{1,0:T(8,128)(2,1)S(1)}, u32[]{:S(2)}, u32[]{:S(2)}) collective-permute-start(bf16[32,3072]{1,0:T(8,128)(2,1)S(1)} %add_convert_fusion.5), channel_id=1, source_target_pairs={{0,2},{1,5},{2,0},{3,7},{4,6},{5,1},{6,4},{7,3},{8,10},{9,13},{10,... | collective-permute-start | bytes 589832 | tf_op jit(solution)/shard_map/ppermute | solution.py:26
  68.1 7.5 %collective-permute-start.24 = (bf16[32,3072]{1,0:T(8,128)(2,1)S(1)}, bf16[32,3072]{1,0:T(8,128)(2,1)S(1)}, u32[]{:S(2)}, u32[]{:S(2)}) collective-permute-start(bf16[32,3072]{1,0:T(8,128)(2,1)S(1)} %get-tuple-element.98), channel_id=1, source_target_pairs={{0,2},{1,5},{2,0},{3,7},{4,6},{5,1},{6,4},{7,3},{8,10},{9,13},{10,... | collective-permute-start | bytes 589832 | tf_op jit(solution)/shard_map/ppermute | solution.py:26
  70.2 5.7 %collective-permute-start.25 = (bf16[32,3072]{1,0:T(8,128)(2,1)S(1)}, bf16[32,3072]{1,0:T(8,128)(2,1)S(1)}, u32[]{:S(2)}, u32[]{:S(2)}) collective-permute-start(bf16[32,3072]{1,0:T(8,128)(2,1)S(1)} %get-tuple-element.99), channel_id=1, source_target_pairs={{0,4},{1,3},{2,6},{3,1},{4,0},{5,7},{6,2},{7,5},{8,12},{9,11},{10,... | collective-permute-start | bytes 589832 | tf_op jit(solution)/shard_map/ppermute | solution.py:26
  71.2 9.3 %collective-permute-start.21 = (bf16[8,4096]{1,0:T(8,128)(2,1)S(1)}, bf16[8,4096]{1,0:T(8,128)(2,1)S(1)}, u32[]{:S(2)}, u32[]{:S(2)}) collective-permute-start(bf16[8,4096]{1,0:T(8,128)(2,1)S(1)} %get-tuple-element.81), channel_id=1, source_target_pairs={{0,24},{1,25},{2,26},{3,27},{4,28},{5,29},{6,30},{7,31},{8,16},{9,... | collective-permute-start | bytes 196616 | tf_op jit(solution)/shard_map/ppermute | solution.py:26
  73.7 7.5 %collective-permute-start.22 = (bf16[8,4096]{1,0:T(8,128)(2,1)S(1)}, bf16[8,4096]{1,0:T(8,128)(2,1)S(1)}, u32[]{:S(2)}, u32[]{:S(2)}) collective-permute-start(bf16[8,4096]{1,0:T(8,128)(2,1)S(1)} %get-tuple-element.83), channel_id=1, source_target_pairs={{0,16},{1,17},{2,18},{3,19},{4,20},{5,21},{6,22},{7,23},{8,24},{9,... | collective-permute-start | bytes 196616 | tf_op jit(solution)/shard_map/ppermute | solution.py:26
  74.3 6.9 %collective-permute-start.23 = (bf16[8,4096]{1,0:T(8,128)(2,1)S(1)}, bf16[8,4096]{1,0:T(8,128)(2,1)S(1)}, u32[]{:S(2)}, u32[]{:S(2)}) collective-permute-start(bf16[8,4096]{1,0:T(8,128)(2,1)S(1)} %get-tuple-element.85), channel_id=1, source_target_pairs={{0,8},{1,9},{2,10},{3,11},{4,12},{5,13},{6,14},{7,15},{8,0},{9,1},... | collective-permute-start | bytes 196616 | tf_op jit(solution)/shard_map/ppermute | solution.py:26
  76.0 6.4 %collective-permute-start.26 = (bf16[8,3072]{1,0:T(8,128)(2,1)S(1)}, bf16[8,3072]{1,0:T(8,128)(2,1)S(1)}, u32[]{:S(2)}, u32[]{:S(2)}) collective-permute-start(bf16[8,3072]{1,0:T(8,128)(2,1)S(1)} %get-tuple-element.95), channel_id=1, source_target_pairs={{0,24},{1,25},{2,26},{3,27},{4,28},{5,29},{6,30},{7,31},{8,16},{9,... | collective-permute-start | bytes 147464 | tf_op jit(solution)/shard_map/ppermute | solution.py:26
  80.2 4.4 %collective-permute-start.28 = (bf16[8,3072]{1,0:T(8,128)(2,1)S(1)}, bf16[8,3072]{1,0:T(8,128)(2,1)S(1)}, u32[]{:S(2)}, u32[]{:S(2)}) collective-permute-start(bf16[8,3072]{1,0:T(8,128)(2,1)S(1)} %get-tuple-element.96), channel_id=1, source_target_pairs={{0,8},{1,9},{2,10},{3,11},{4,12},{5,13},{6,14},{7,15},{8,0},{9,1},... | collective-permute-start | bytes 147464 | tf_op jit(solution)/shard_map/ppermute | solution.py:26
  80.5 5.0 %collective-permute-start.27 = (bf16[8,3072]{1,0:T(8,128)(2,1)S(1)}, bf16[8,3072]{1,0:T(8,128)(2,1)S(1)}, u32[]{:S(2)}, u32[]{:S(2)}) collective-permute-start(bf16[8,3072]{1,0:T(8,128)(2,1)S(1)} %get-tuple-element.97), channel_id=1, source_target_pairs={{0,16},{1,17},{2,18},{3,19},{4,20},{5,21},{6,22},{7,23},{8,24},{9,... | collective-permute-start | bytes 147464 | tf_op jit(solution)/shard_map/ppermute | solution.py:26

commit v18 on v16

--- a/solution.py
+++ b/solution.py
@@ -151,7 +151,7 @@
     gate_sum[...] = jnp.zeros_like(gate_sum)
     up_sum[...] = jnp.zeros_like(up_sum)
 
-    @pl.loop(0, width // wide)
+    @pl.loop(0, width // wide, unroll=True)
     def _(k):
         piece = jnp.concatenate([ref[:, span(k)] for ref in rows], axis=0)
         gate_sum[...] += jnp.dot(piece, gate[0, span(k), :], preferred_element_type=jnp.float32)
@@ -170,11 +170,11 @@
         far_side[:, span(k)] = product[half + 2 * height : half + 3 * height]
         ref[:, span(k - first)] = product[half + 3 * height :]
 
-    @pl.loop(0, steps)
+    @pl.loop(0, steps, unroll=True)
     def _(k):
         give(k, far_across[0], 0)
 
-    @pl.loop(steps, width // wide)
+    @pl.loop(steps, width // wide, unroll=True)
     def _(k):
         give(k, far_across[1], steps)
 

time: 86.2 us -> 86.2 us (level)
  starting transfers between devices: 38.3 us -> 40.5 us
  Pallas kernels: 11.8 us -> 9.64 us
    ppermute x27, starting transfers between devices: 36.7 us -> 38.9 us  [swapped(): return lax.ppermute(value, 'dp', [(i, partner(i)) for i in range(peers)])]
    pallas_call x1, Pallas kernels: 5.3 us -> 3.11 us  [experts(): pl.pallas_call(lambda *refs: expert_kernel(wide, *refs), in_specs=[whole]...]
  transfers between devices with their start and end apart: 29 -> 29, of which waited for: 13 -> 13; matrix products, arithmetic and copies ran while one was open for 6% -> 6% of each run, Pallas kernels for 14% -> 11%
where the time goes in v18:
time: 86.2 us; the launch traced here: 86 us
  starting transfers between devices  40.5 us (47%)
  waiting for transfers between devices  28.7 us (33%)
  Pallas kernels  9.64 us (11%)
  other arithmetic  4.79 us (6%)
  local copies, waits for them, and re-layouts  1.6 us (2%)
    ppermute x27, starting transfers between devices, swapped(): return lax.ppermute(value, 'dp', [(i, partner(i)) for i in range(peers)])  38.9 us
    ppermute x27, waiting for transfers between devices, swapped(): return lax.ppermute(value, 'dp', [(i, partner(i)) for i in range(peers)])  28.7 us
    pallas_call x1, Pallas kernels, fetched(): pl.pallas_call(fetch_kernel, in_specs=[pl.BlockSpec(memory_space=pltpu.HB...  4.23 us
    reduce_sum x1, other arithmetic, body(): jnp.sum(jnp.where(routed_experts == targets[r], route_weights, 0.0), axis=1)  3.31 us
    pallas_call x1, Pallas kernels, experts(): pl.pallas_call(lambda *refs: expert_kernel(wide, *refs), in_specs=[whole]...  3.11 us
    pallas_call x1, Pallas kernels, attend(): pl.pallas_call(lambda *refs: attend_kernel(spans, *refs), in_specs=[scala...  2.3 us
  transfers between devices with their start and end apart: 29, of which 13 were waited for; matrix products, arithmetic and copies ran while one was open for 6% of the time, Pallas kernels for 11%

profile of v18, /device:TPU:0, one launch (start us, length us, event | category | flops | bytes accessed | tf_op | source)
XLA Modules:
  0.0 86.0 jit_solution(17232264488460199703)
XLA Ops:
  0.6 0.7 collective-permute-start.3
  1.4 4.1 %collective-permute-start.1 = (bf16[8,7168]{1,0:T(8,128)(2,1)}, bf16[8,7168]{1,0:T(8,128)(2,1)S(1)}, u32[]{:S(2)}, u32[]{:S(2)}) collective-permute-start(bf16[8,7168]{1,0:T(8,128)(2,1)} %param.16), channel_id=1, source_target_pairs={{0,16},{1,17},{2,18},{3,19},{4,20},{5,21},{6,22},{7,23},{8,24},{9,... | collective-permute-start | bytes 344072 | tf_op jit(solution)/shard_map/ppermute | solution.py:26
  5.5 1.3 %collective-permute-start = (bf16[8,7168]{1,0:T(8,128)(2,1)}, bf16[8,7168]{1,0:T(8,128)(2,1)S(1)}, u32[]{:S(2)}, u32[]{:S(2)}) collective-permute-start(bf16[8,7168]{1,0:T(8,128)(2,1)} %param.16), channel_id=1, source_target_pairs={{0,24},{1,25},{2,26},{3,27},{4,28},{5,29},{6,30},{7,31},{8,16},{9,... | collective-permute-start | bytes 344072 | tf_op jit(solution)/shard_map/ppermute | solution.py:26
  6.8 0.2 collective-permute-start.2
  7.0 0.6 fusion.4
  7.7 0.9 %pad.4 = bf16[32,7168]{1,0:T(8,128)(2,1)S(1)} pad(bf16[8,7168]{1,0:T(8,128)(2,1)} %param.16, bf16[]{:T(256)} %constant.19.clone.1), padding=0_24x0_0 | pad | bytes 573442 | tf_op jit(solution)/shard_map/jit(_pad)/pad | solution.py:277
  8.6 3.3 %fusion.3 = (f32[8]{0:T(128)S(1)}, f32[8]{0:T(128)S(1)}, f32[8]{0:T(128)S(1)}, f32[8]{0:T(128)S(1)}) fusion(f32[8,2]{0,1:T(2,128)} %param.18, s32[8,2]{0,1:T(2,128)} %param.17, s32[]{:T(128)} %bitcast.3, s32[]{:T(128)} %bitcast.1, s32[]{:T(128)} %bitcast, s32[]{:T(128)} %bitcast.2), kind=kLoop, calls=%fused_computation.23 | loop fusion | flops 160 | bytes 272 | tf_op jit(solution)/shard_map/reduce_sum | solution.py:240
  11.9 1.4 %collective-permute-done = bf16[8,7168]{1,0:T(8,128)(2,1)S(1)} collective-permute-done((bf16[8,7168]{1,0:T(8,128)(2,1)}, bf16[8,7168]{1,0:T(8,128)(2,1)S(1)}, u32[]{:S(2)}, u32[]{:S(2)}) %collective-permute-start) | collective-permute-done | bytes 114720 | tf_op jit(solution)/shard_map/ppermute | solution.py:26
  13.3 1.2 %collective-permute-done.2 = bf16[8,7168]{1,0:T(8,128)(2,1)S(1)} collective-permute-done((bf16[8,7168]{1,0:T(8,128)(2,1)}, bf16[8,7168]{1,0:T(8,128)(2,1)S(1)}, u32[]{:S(2)}, u32[]{:S(2)}) %collective-permute-start.2) | collective-permute-done | bytes 114720 | tf_op jit(solution)/shard_map/ppermute | solution.py:26
  14.6 5.7 %collective-permute-start.4 = (bf16[32,7168]{1,0:T(8,128)(2,1)S(1)}, bf16[32,7168]{1,0:T(8,128)(2,1)S(1)}, u32[]{:S(2)}, u32[]{:S(2)}) collective-permute-start(bf16[32,7168]{1,0:T(8,128)(2,1)S(1)} %constant_dynamic-update-slice_fusion.refs_0_), channel_id=1, source_target_pairs={{0,4},{1,3},{2,6},{3,1},{4,0},{5,7},{6,2},{7,5},{8,12},{9,11},{10,... | collective-permute-start | bytes 1376264 | tf_op jit(solution)/shard_map/ppermute | solution.py:26
  20.3 0.5 collective-permute-start.7
  20.8 5.9 %collective-permute-done.4.refs_1_ = bf16[32,7168]{1,0:T(8,128)(2,1)S(1)} collective-permute-done((bf16[32,7168]{1,0:T(8,128)(2,1)S(1)}, bf16[32,7168]{1,0:T(8,128)(2,1)S(1)}, u32[]{:S(2)}, u32[]{:S(2)}) %collective-permute-start.4) | collective-permute-done | bytes 458784 | tf_op jit(solution)/shard_map/ppermute | solution.py:26
  26.7 1.1 %collective-permute-start.6 = (bf16[32,7168]{1,0:T(8,128)(2,1)S(1)}, bf16[32,7168]{1,0:T(8,128)(2,1)S(1)}, u32[]{:S(2)}, u32[]{:S(2)}) collective-permute-start(bf16[32,7168]{1,0:T(8,128)(2,1)S(1)} %collective-permute-done.4.refs_1_), channel_id=1, source_target_pairs={{0,2},{1,5},{2,0},{3,7},{4,6},{5,1},{6,4},{7,3},{8,10},{9,13},{10,... | collective-permute-start | bytes 1376264 | tf_op jit(solution)/shard_map/ppermute | solution.py:26
  27.8 0.9 %collective-permute-start.5 = (bf16[32,7168]{1,0:T(8,128)(2,1)S(1)}, bf16[32,7168]{1,0:T(8,128)(2,1)S(1)}, u32[]{:S(2)}, u32[]{:S(2)}) collective-permute-start(bf16[32,7168]{1,0:T(8,128)(2,1)S(1)} %constant_dynamic-update-slice_fusion.refs_0_), channel_id=1, source_target_pairs={{0,2},{1,5},{2,0},{3,7},{4,6},{5,1},{6,4},{7,3},{8,10},{9,13},{10,... | collective-permute-start | bytes 1376264 | tf_op jit(solution)/shard_map/ppermute | solution.py:26
  28.7 4.2 %shard_map.122 = (bf16[1,7168,256]{2,1,0:T(8,128)(2,1)S(1)}, bf16[1,7168,256]{2,1,0:T(8,128)(2,1)S(1)}, bf16[1,256,7168]{2,1,0:T(8,128)(2,1)S(1)}) custom-call(bf16[1,7168,256]{2,1,0:T(8,128)(2,1)} %refs_0_.2, bf16[1,7168,256]{2,1,0:T(8,128)(2,1)} %refs_1_.2, bf16[1,256,7168]{2,1,0:T(8,128)(2,1)} %refs_2_.2), custom_call_target="tpu_custom_call" | custom-call | bytes 22020096 | tf_op jit(solution)/shard_map/pallas_call | solution.py:127
  33.0 2.2 %collective-permute-done.6.refs_3_ = bf16[32,7168]{1,0:T(8,128)(2,1)S(1)} collective-permute-done((bf16[32,7168]{1,0:T(8,128)(2,1)S(1)}, bf16[32,7168]{1,0:T(8,128)(2,1)S(1)}, u32[]{:S(2)}, u32[]{:S(2)}) %collective-permute-start.6) | collective-permute-done | bytes 458784 | tf_op jit(solution)/shard_map/ppermute | solution.py:26
  35.2 0.9 collective-permute-start.13
  36.1 4.0 %collective-permute-done.5.refs_2_ = bf16[32,7168]{1,0:T(8,128)(2,1)S(1)} collective-permute-done((bf16[32,7168]{1,0:T(8,128)(2,1)S(1)}, bf16[32,7168]{1,0:T(8,128)(2,1)S(1)}, u32[]{:S(2)}, u32[]{:S(2)}) %collective-permute-start.5) | collective-permute-done | bytes 458784 | tf_op jit(solution)/shard_map/ppermute | solution.py:26
  40.1 0.5 collective-permute-start.11
  40.6 1.3 %collective-permute-done.10.refs_6_ = bf16[32,7168]{1,0:T(8,128)(2,1)S(1)} collective-permute-done((bf16[32,7168]{1,0:T(8,128)(2,1)S(1)}, bf16[32,7168]{1,0:T(8,128)(2,1)S(1)}, u32[]{:S(2)}, u32[]{:S(2)}) %collective-permute-start.10) | collective-permute-done | bytes 458784 | tf_op jit(solution)/shard_map/ppermute | solution.py:26
  41.9 0.7 collective-permute-done.11.refs_7_
  42.6 3.1 %shard_map.123 = (bf16[128,7168]{1,0:T(8,128)(2,1)S(1)}, bf16[64,7168]{1,0:T(8,128)(2,1)S(1)}, bf16[32,7168]{1,0:T(8,128)(2,1)S(1)}, bf16[32,4096]{1,0:T(8,128)(2,1)S(1)}, bf16[32,3072]{1,0:T(8,128)(2,1)S(1)}) custom-call(bf16[32,7168]{1,0:T(8,128)(2,1)S(1)} %constant_dynamic-update-slice_fusion.refs_0_, ...), custom_call_target="tpu_custom_call" | custom-call | tf_op jit(solution)/shard_map/pallas_call | solution.py:193
  45.7 0.2 collective-permute-start.12
  45.9 4.8 %collective-permute-start.18 = (bf16[32,3072]{1,0:T(8,128)(2,1)S(1)}, bf16[32,3072]{1,0:T(8,128)(2,1)S(1)}, u32[]{:S(2)}, u32[]{:S(2)}) collective-permute-start(bf16[32,3072]{1,0:T(8,128)(2,1)S(1)} %get-tuple-element.78), channel_id=1, source_target_pairs={{0,1},{1,0},{2,3},{3,2},{4,5},{5,4},{6,7},{7,6},{8,9},{9,8},{10,11... | collective-permute-start | bytes 589832 | tf_op jit(solution)/shard_map/ppermute | solution.py:26
  50.8 1.9 %collective-permute-start.14 = (bf16[32,4096]{1,0:T(8,128)(2,1)S(1)}, bf16[32,4096]{1,0:T(8,128)(2,1)S(1)}, u32[]{:S(2)}, u32[]{:S(2)}) collective-permute-start(bf16[32,4096]{1,0:T(8,128)(2,1)S(1)} %add_convert_fusion.2), channel_id=1, source_target_pairs={{0,2},{1,5},{2,0},{3,7},{4,6},{5,1},{6,4},{7,3},{8,10},{9,13},{10,... | collective-permute-start | bytes 786440 | tf_op jit(solution)/shard_map/ppermute | solution.py:26
  52.7 2.3 %shard_map.124 = bf16[8,64,512]{2,1,0:T(8,128)(2,1)} custom-call(s32[8]{0:T(128)S(1)} %copy-done.3, s32[8]{0:T(128)S(1)} %copy-done.4, bf16[8,64,576]{2,1,0:T(8,128)(2,1)S(1)} %copy-done.1, bf16[8,96,576]{2,1,0:T(8,128)(2,1)S(1)} %copy-done, bf16[8,96,576]{2,1,0:T(8,128)(2,1)S(1)} %collective-permute-done.9.refs_4_, bf16[8,576]{1,0:T(8,128)(2,1)S(1)} %copy-done.2, ...), custom_call_target="tpu_custom_call" | custom-call | flops 106954752 | bytes 4653056 | tf_op jit(solution)/shard_map/pallas_call | solution.py:99
  55.0 2.2 %collective-permute-done.14 = bf16[32,4096]{1,0:T(8,128)(2,1)S(1)} collective-permute-done((bf16[32,4096]{1,0:T(8,128)(2,1)S(1)}, bf16[32,4096]{1,0:T(8,128)(2,1)S(1)}, u32[]{:S(2)}, u32[]{:S(2)}) %collective-permute-start.14) | collective-permute-done | bytes 262176 | tf_op jit(solution)/shard_map/ppermute | solution.py:26
  57.2 0.2 add_convert_fusion.1
  57.4 2.2 %collective-permute-start.19 = (bf16[32,4096]{1,0:T(8,128)(2,1)S(1)}, bf16[32,4096]{1,0:T(8,128)(2,1)S(1)}, u32[]{:S(2)}, u32[]{:S(2)}) collective-permute-start(bf16[32,4096]{1,0:T(8,128)(2,1)S(1)} %get-tuple-element.79), channel_id=1, source_target_pairs={{0,4},{1,3},{2,6},{3,1},{4,0},{5,7},{6,2},{7,5},{8,12},{9,11},{10,... | collective-permute-start | bytes 786440 | tf_op jit(solution)/shard_map/ppermute | solution.py:26
  59.6 2.0 %collective-permute-start.17 = (bf16[32,4096]{1,0:T(8,128)(2,1)S(1)}, bf16[32,4096]{1,0:T(8,128)(2,1)S(1)}, u32[]{:S(2)}, u32[]{:S(2)}) collective-permute-start(bf16[32,4096]{1,0:T(8,128)(2,1)S(1)} %get-tuple-element.102), channel_id=1, source_target_pairs={{0,2},{1,5},{2,0},{3,7},{4,6},{5,1},{6,4},{7,3},{8,10},{9,13},{10,... | collective-permute-start | bytes 786440 | tf_op jit(solution)/shard_map/ppermute | solution.py:26
  61.6 4.4 %collective-permute-done.19 = bf16[32,4096]{1,0:T(8,128)(2,1)S(1)} collective-permute-done((bf16[32,4096]{1,0:T(8,128)(2,1)S(1)}, bf16[32,4096]{1,0:T(8,128)(2,1)S(1)}, u32[]{:S(2)}, u32[]{:S(2)}) %collective-permute-start.19) | collective-permute-done | bytes 262176 | tf_op jit(solution)/shard_map/ppermute | solution.py:26
  66.1 0.1 convert_add_fusion
  66.2 1.8 %collective-permute-done.20 = bf16[32,3072]{1,0:T(8,128)(2,1)S(1)} collective-permute-done((bf16[32,3072]{1,0:T(8,128)(2,1)S(1)}, bf16[32,3072]{1,0:T(8,128)(2,1)S(1)}, u32[]{:S(2)}, u32[]{:S(2)}) %collective-permute-start.20) | collective-permute-done | bytes 196640 | tf_op jit(solution)/shard_map/ppermute | solution.py:26
  68.0 0.1 add_convert_fusion.4
  68.2 2.1 %collective-permute-start.24 = (bf16[32,3072]{1,0:T(8,128)(2,1)S(1)}, bf16[32,3072]{1,0:T(8,128)(2,1)S(1)}, u32[]{:S(2)}, u32[]{:S(2)}) collective-permute-start(bf16[32,3072]{1,0:T(8,128)(2,1)S(1)} %get-tuple-element.100), channel_id=1, source_target_pairs={{0,2},{1,5},{2,0},{3,7},{4,6},{5,1},{6,4},{7,3},{8,10},{9,13},{10,... | collective-permute-start | bytes 589832 | tf_op jit(solution)/shard_map/ppermute | solution.py:26
  70.2 1.5 %collective-permute-start.25 = (bf16[32,3072]{1,0:T(8,128)(2,1)S(1)}, bf16[32,3072]{1,0:T(8,128)(2,1)S(1)}, u32[]{:S(2)}, u32[]{:S(2)}) collective-permute-start(bf16[32,3072]{1,0:T(8,128)(2,1)S(1)} %get-tuple-element.101), channel_id=1, source_target_pairs={{0,4},{1,3},{2,6},{3,1},{4,0},{5,7},{6,2},{7,5},{8,12},{9,11},{10,... | collective-permute-start | bytes 589832 | tf_op jit(solution)/shard_map/ppermute | solution.py:26
  71.7 2.5 %collective-permute-start.21 = (bf16[8,4096]{1,0:T(8,128)(2,1)S(1)}, bf16[8,4096]{1,0:T(8,128)(2,1)S(1)}, u32[]{:S(2)}, u32[]{:S(2)}) collective-permute-start(bf16[8,4096]{1,0:T(8,128)(2,1)S(1)} %get-tuple-element.83), channel_id=1, source_target_pairs={{0,24},{1,25},{2,26},{3,27},{4,28},{5,29},{6,30},{7,31},{8,16},{9,... | collective-permute-start | bytes 196616 | tf_op jit(solution)/shard_map/ppermute | solution.py:26
  74.2 0.6 collective-permute-start.22
  74.8 1.3 %collective-permute-start.23 = (bf16[8,4096]{1,0:T(8,128)(2,1)S(1)}, bf16[8,4096]{1,0:T(8,128)(2,1)S(1)}, u32[]{:S(2)}, u32[]{:S(2)}) collective-permute-start(bf16[8,4096]{1,0:T(8,128)(2,1)S(1)} %get-tuple-element.87), channel_id=1, source_target_pairs={{0,8},{1,9},{2,10},{3,11},{4,12},{5,13},{6,14},{7,15},{8,0},{9,1},... | collective-permute-start | bytes 196616 | tf_op jit(solution)/shard_map/ppermute | solution.py:26
  76.1 0.1 add_convert_fusion.10
  76.2 4.0 %collective-permute-start.26 = (bf16[8,3072]{1,0:T(8,128)(2,1)S(1)}, bf16[8,3072]{1,0:T(8,128)(2,1)S(1)}, u32[]{:S(2)}, u32[]{:S(2)}) collective-permute-start(bf16[8,3072]{1,0:T(8,128)(2,1)S(1)} %get-tuple-element.97), channel_id=1, source_target_pairs={{0,24},{1,25},{2,26},{3,27},{4,28},{5,29},{6,30},{7,31},{8,16},{9,... | collective-permute-start | bytes 147464 | tf_op jit(solution)/shard_map/ppermute | solution.py:26
  80.2 1.4 %collective-permute-start.27 = (bf16[8,3072]{1,0:T(8,128)(2,1)S(1)}, bf16[8,3072]{1,0:T(8,128)(2,1)S(1)}, u32[]{:S(2)}, u32[]{:S(2)}) collective-permute-start(bf16[8,3072]{1,0:T(8,128)(2,1)S(1)} %get-tuple-element.99), channel_id=1, source_target_pairs={{0,16},{1,17},{2,18},{3,19},{4,20},{5,21},{6,22},{7,23},{8,24},{9,... | collective-permute-start | bytes 147464 | tf_op jit(solution)/shard_map/ppermute | solution.py:26
  81.6 0.1 add_convert_fusion.6
  81.8 0.7 collective-permute-done.26
  82.5 2.1 %collective-permute-done.28 = bf16[8,3072]{1,0:T(8,128)(2,1)S(1)} collective-permute-done((bf16[8,3072]{1,0:T(8,128)(2,1)S(1)}, bf16[8,3072]{1,0:T(8,128)(2,1)S(1)}, u32[]{:S(2)}, u32[]{:S(2)}) %collective-permute-start.28) | collective-permute-done | bytes 49184 | tf_op jit(solution)/shard_map/ppermute | solution.py:26
  84.6 0.6 collective-permute-done.27
  85.2 0.1 add_convert_fusion.7
  85.3 0.7 pad_maximum_fusion
  (40 shorter events, 0.3 us)
Async XLA Ops:
  0.6 13.9 %collective-permute-start.3 = (bf16[8,96,576]{2,1,0:T(8,128)(2,1)}, bf16[8,96,576]{2,1,0:T(8,128)(2,1)S(1)}, u32[]{:S(2)}, u32[]{:S(2)}) collective-permute-start(bf16[8,96,576]{2,1,0:T(8,128)(2,1)} %refs_3_.1), channel_id=1, source_target_pairs={{1,2},{3,4},{5,6},{6,5},{9,10},{11,12},{13,14},{14,13},{17,18},{19... | collective-permute-start | bytes 2654216 | tf_op jit(solution)/shard_map/ppermute | solution.py:47
  1.4 10.6 %collective-permute-start.1 = (bf16[8,7168]{1,0:T(8,128)(2,1)}, bf16[8,7168]{1,0:T(8,128)(2,1)S(1)}, u32[]{:S(2)}, u32[]{:S(2)}) collective-permute-start(bf16[8,7168]{1,0:T(8,128)(2,1)} %param.16), channel_id=1, source_target_pairs={{0,16},{1,17},{2,18},{3,19},{4,20},{5,21},{6,22},{7,23},{8,24},{9,... | collective-permute-start | bytes 344072 | tf_op jit(solution)/shard_map/ppermute | solution.py:26
  5.5 7.8 %collective-permute-start = (bf16[8,7168]{1,0:T(8,128)(2,1)}, bf16[8,7168]{1,0:T(8,128)(2,1)S(1)}, u32[]{:S(2)}, u32[]{:S(2)}) collective-permute-start(bf16[8,7168]{1,0:T(8,128)(2,1)} %param.16), channel_id=1, source_target_pairs={{0,24},{1,25},{2,26},{3,27},{4,28},{5,29},{6,30},{7,31},{8,16},{9,... | collective-permute-start | bytes 344072 | tf_op jit(solution)/shard_map/ppermute | solution.py:26
  6.8 7.7 %collective-permute-start.2 = (bf16[8,7168]{1,0:T(8,128)(2,1)}, bf16[8,7168]{1,0:T(8,128)(2,1)S(1)}, u32[]{:S(2)}, u32[]{:S(2)}) collective-permute-start(bf16[8,7168]{1,0:T(8,128)(2,1)} %param.16), channel_id=1, source_target_pairs={{0,8},{1,9},{2,10},{3,11},{4,12},{5,13},{6,14},{7,15},{8,0},{9,1},... | collective-permute-start | bytes 344072 | tf_op jit(solution)/shard_map/ppermute | solution.py:26
  14.6 20.6 %copy-start = (bf16[8,96,576]{2,1,0:T(8,128)(2,1)S(1)}, bf16[8,96,576]{2,1,0:T(8,128)(2,1)}, u32[]{:S(2)}) copy-start(bf16[8,96,576]{2,1,0:T(8,128)(2,1)} %refs_3_.1) | copy-start | bytes 2654212
  14.6 12.1 %collective-permute-start.4 = (bf16[32,7168]{1,0:T(8,128)(2,1)S(1)}, bf16[32,7168]{1,0:T(8,128)(2,1)S(1)}, u32[]{:S(2)}, u32[]{:S(2)}) collective-permute-start(bf16[32,7168]{1,0:T(8,128)(2,1)S(1)} %constant_dynamic-update-slice_fusion.refs_0_), channel_id=1, source_target_pairs={{0,4},{1,3},{2,6},{3,1},{4,0},{5,7},{6,2},{7,5},{8,12},{9,11},{10,... | collective-permute-start | bytes 1376264 | tf_op jit(solution)/shard_map/ppermute | solution.py:26
  20.2 12.7 %collective-permute-start.9 = (bf16[8,96,576]{2,1,0:T(8,128)(2,1)}, bf16[8,96,576]{2,1,0:T(8,128)(2,1)S(1)}, u32[]{:S(2)}, u32[]{:S(2)}) collective-permute-start(bf16[8,96,576]{2,1,0:T(8,128)(2,1)} %refs_3_.1), channel_id=1, source_target_pairs={{0,1},{1,0},{2,3},{3,2},{4,5},{5,4},{6,7},{7,6},{8,9},{9,8},{10,11... | collective-permute-start | bytes 2654216 | tf_op jit(solution)/shard_map/ppermute | solution.py:26
  20.3 12.7 %collective-permute-start.7 = (bf16[32,7168]{1,0:T(8,128)(2,1)S(1)}, bf16[32,7168]{1,0:T(8,128)(2,1)S(1)}, u32[]{:S(2)}, u32[]{:S(2)}) collective-permute-start(bf16[32,7168]{1,0:T(8,128)(2,1)S(1)} %constant_dynamic-update-slice_fusion.refs_0_), channel_id=1, source_target_pairs={{0,1},{1,0},{2,3},{3,2},{4,5},{5,4},{6,7},{7,6},{8,9},{9,8},{10,11... | collective-permute-start | bytes 1376264 | tf_op jit(solution)/shard_map/ppermute | solution.py:26
  26.7 6.3 %collective-permute-start.8 = (bf16[32,7168]{1,0:T(8,128)(2,1)S(1)}, bf16[32,7168]{1,0:T(8,128)(2,1)S(1)}, u32[]{:S(2)}, u32[]{:S(2)}) collective-permute-start(bf16[32,7168]{1,0:T(8,128)(2,1)S(1)} %collective-permute-done.4.refs_1_), channel_id=1, source_target_pairs={{0,1},{1,0},{2,3},{3,2},{4,5},{5,4},{6,7},{7,6},{8,9},{9,8},{10,11... | collective-permute-start | bytes 1376264 | tf_op jit(solution)/shard_map/ppermute | solution.py:26
  26.7 8.5 %collective-permute-start.6 = (bf16[32,7168]{1,0:T(8,128)(2,1)S(1)}, bf16[32,7168]{1,0:T(8,128)(2,1)S(1)}, u32[]{:S(2)}, u32[]{:S(2)}) collective-permute-start(bf16[32,7168]{1,0:T(8,128)(2,1)S(1)} %collective-permute-done.4.refs_1_), channel_id=1, source_target_pairs={{0,2},{1,5},{2,0},{3,7},{4,6},{5,1},{6,4},{7,3},{8,10},{9,13},{10,... | collective-permute-start | bytes 1376264 | tf_op jit(solution)/shard_map/ppermute | solution.py:26
  27.8 12.3 %collective-permute-start.5 = (bf16[32,7168]{1,0:T(8,128)(2,1)S(1)}, bf16[32,7168]{1,0:T(8,128)(2,1)S(1)}, u32[]{:S(2)}, u32[]{:S(2)}) collective-permute-start(bf16[32,7168]{1,0:T(8,128)(2,1)S(1)} %constant_dynamic-update-slice_fusion.refs_0_), channel_id=1, source_target_pairs={{0,2},{1,5},{2,0},{3,7},{4,6},{5,1},{6,4},{7,3},{8,10},{9,13},{10,... | collective-permute-start | bytes 1376264 | tf_op jit(solution)/shard_map/ppermute | solution.py:26
  35.2 17.5 %copy-start.1 = (bf16[8,64,576]{2,1,0:T(8,128)(2,1)S(1)}, bf16[8,64,576]{2,1,0:T(8,128)(2,1)}, u32[]{:S(2)}) copy-start(bf16[8,64,576]{2,1,0:T(8,128)(2,1)} %refs_2_.3) | copy-start | bytes 1769476
  35.2 17.5 %copy-start.2 = (bf16[8,576]{1,0:T(8,128)(2,1)S(1)}, bf16[8,576]{1,0:T(8,128)(2,1)}, u32[]{:S(2)}) copy-start(bf16[8,576]{1,0:T(8,128)(2,1)} %refs_5_.1) | copy-start | bytes 27652
  35.2 17.5 %copy-start.3 = (s32[8]{0:T(128)S(1)}, s32[8]{0:T(128)}, u32[]{:S(2)}) copy-start(s32[8]{0:T(128)} %refs_0_.3) | copy-start | bytes 100
  35.2 17.5 %copy-start.4 = (s32[8]{0:T(128)S(1)}, s32[8]{0:T(128)}, u32[]{:S(2)}) copy-start(s32[8]{0:T(128)} %refs_1_.3) | copy-start | bytes 100
  35.2 10.7 %collective-permute-start.13 = (bf16[8,96,576]{2,1,0:T(8,128)(2,1)S(1)}, bf16[8,96,576]{2,1,0:T(8,128)(2,1)S(1)}, u32[]{:S(2)}, u32[]{:S(2)}) collective-permute-start(bf16[8,96,576]{2,1,0:T(8,128)(2,1)S(1)} %copy-done), channel_id=1, source_target_pairs={{2,1},{4,3},{7,8},{8,7},{10,9},{12,11},{15,16},{16,15},{18,17},{20... | collective-permute-start | bytes 2654216 | tf_op jit(solution)/shard_map/ppermute | solution.py:47
  40.1 1.8 %collective-permute-start.10 = (bf16[32,7168]{1,0:T(8,128)(2,1)S(1)}, bf16[32,7168]{1,0:T(8,128)(2,1)S(1)}, u32[]{:S(2)}, u32[]{:S(2)}) collective-permute-start(bf16[32,7168]{1,0:T(8,128)(2,1)S(1)} %collective-permute-done.5.refs_2_), channel_id=1, source_target_pairs={{0,1},{1,0},{2,3},{3,2},{4,5},{5,4},{6,7},{7,6},{8,9},{9,8},{10,11... | collective-permute-start | bytes 1376264 | tf_op jit(solution)/shard_map/ppermute | solution.py:26
  40.1 2.5 %collective-permute-start.11 = (bf16[32,7168]{1,0:T(8,128)(2,1)S(1)}, bf16[32,7168]{1,0:T(8,128)(2,1)S(1)}, u32[]{:S(2)}, u32[]{:S(2)}) collective-permute-start(bf16[32,7168]{1,0:T(8,128)(2,1)S(1)} %collective-permute-done.6.refs_3_), channel_id=1, source_target_pairs={{0,1},{1,0},{2,3},{3,2},{4,5},{5,4},{6,7},{7,6},{8,9},{9,8},{10,11... | collective-permute-start | bytes 1376264 | tf_op jit(solution)/shard_map/ppermute | solution.py:26
  45.7 5.0 %collective-permute-start.12 = (bf16[32,4096]{1,0:T(8,128)(2,1)S(1)}, bf16[32,4096]{1,0:T(8,128)(2,1)S(1)}, u32[]{:S(2)}, u32[]{:S(2)}) collective-permute-start(bf16[32,4096]{1,0:T(8,128)(2,1)S(1)} %get-tuple-element.63), channel_id=1, source_target_pairs={{0,1},{1,0},{2,3},{3,2},{4,5},{5,4},{6,7},{7,6},{8,9},{9,8},{10,11... | collective-permute-start | bytes 786440 | tf_op jit(solution)/shard_map/ppermute | solution.py:26
  45.9 9.1 %collective-permute-start.18 = (bf16[32,3072]{1,0:T(8,128)(2,1)S(1)}, bf16[32,3072]{1,0:T(8,128)(2,1)S(1)}, u32[]{:S(2)}, u32[]{:S(2)}) collective-permute-start(bf16[32,3072]{1,0:T(8,128)(2,1)S(1)} %get-tuple-element.78), channel_id=1, source_target_pairs={{0,1},{1,0},{2,3},{3,2},{4,5},{5,4},{6,7},{7,6},{8,9},{9,8},{10,11... | collective-permute-start | bytes 589832 | tf_op jit(solution)/shard_map/ppermute | solution.py:26
  50.7 6.5 %collective-permute-start.15 = (bf16[64,7168]{1,0:T(8,128)(2,1)S(1)}, bf16[64,7168]{1,0:T(8,128)(2,1)S(1)}, u32[]{:S(2)}, u32[]{:S(2)}) collective-permute-start(bf16[64,7168]{1,0:T(8,128)(2,1)S(1)} %get-tuple-element.75), channel_id=1, source_target_pairs={{0,1},{1,0},{2,3},{3,2},{4,5},{5,4},{6,7},{7,6},{8,9},{9,8},{10,11... | collective-permute-start | bytes 2752520 | tf_op jit(solution)/shard_map/ppermute | solution.py:26
  50.8 6.4 %collective-permute-start.14 = (bf16[32,4096]{1,0:T(8,128)(2,1)S(1)}, bf16[32,4096]{1,0:T(8,128)(2,1)S(1)}, u32[]{:S(2)}, u32[]{:S(2)}) collective-permute-start(bf16[32,4096]{1,0:T(8,128)(2,1)S(1)} %add_convert_fusion.2), channel_id=1, source_target_pairs={{0,2},{1,5},{2,0},{3,7},{4,6},{5,1},{6,4},{7,3},{8,10},{9,13},{10,... | collective-permute-start | bytes 786440 | tf_op jit(solution)/shard_map/ppermute | solution.py:26
  52.6 4.6 %collective-permute-start.16 = (bf16[32,7168]{1,0:T(8,128)(2,1)S(1)}, bf16[32,7168]{1,0:T(8,128)(2,1)S(1)}, u32[]{:S(2)}, u32[]{:S(2)}) collective-permute-start(bf16[32,7168]{1,0:T(8,128)(2,1)S(1)} %get-tuple-element.76), channel_id=1, source_target_pairs={{0,1},{1,0},{2,3},{3,2},{4,5},{5,4},{6,7},{7,6},{8,9},{9,8},{10,11... | collective-permute-start | bytes 1376264 | tf_op jit(solution)/shard_map/ppermute | solution.py:26
  57.4 8.7 %collective-permute-start.19 = (bf16[32,4096]{1,0:T(8,128)(2,1)S(1)}, bf16[32,4096]{1,0:T(8,128)(2,1)S(1)}, u32[]{:S(2)}, u32[]{:S(2)}) collective-permute-start(bf16[32,4096]{1,0:T(8,128)(2,1)S(1)} %get-tuple-element.79), channel_id=1, source_target_pairs={{0,4},{1,3},{2,6},{3,1},{4,0},{5,7},{6,2},{7,5},{8,12},{9,11},{10,... | collective-permute-start | bytes 786440 | tf_op jit(solution)/shard_map/ppermute | solution.py:26
  59.6 6.5 %collective-permute-start.17 = (bf16[32,4096]{1,0:T(8,128)(2,1)S(1)}, bf16[32,4096]{1,0:T(8,128)(2,1)S(1)}, u32[]{:S(2)}, u32[]{:S(2)}) collective-permute-start(bf16[32,4096]{1,0:T(8,128)(2,1)S(1)} %get-tuple-element.102), channel_id=1, source_target_pairs={{0,2},{1,5},{2,0},{3,7},{4,6},{5,1},{6,4},{7,3},{8,10},{9,13},{10,... | collective-permute-start | bytes 786440 | tf_op jit(solution)/shard_map/ppermute | solution.py:26
  61.6 6.5 %collective-permute-start.20 = (bf16[32,3072]{1,0:T(8,128)(2,1)S(1)}, bf16[32,3072]{1,0:T(8,128)(2,1)S(1)}, u32[]{:S(2)}, u32[]{:S(2)}) collective-permute-start(bf16[32,3072]{1,0:T(8,128)(2,1)S(1)} %add_convert_fusion.5), channel_id=1, source_target_pairs={{0,2},{1,5},{2,0},{3,7},{4,6},{5,1},{6,4},{7,3},{8,10},{9,13},{10,... | collective-permute-start | bytes 589832 | tf_op jit(solution)/shard_map/ppermute | solution.py:26
  68.2 8.0 %collective-permute-start.24 = (bf16[32,3072]{1,0:T(8,128)(2,1)S(1)}, bf16[32,3072]{1,0:T(8,128)(2,1)S(1)}, u32[]{:S(2)}, u32[]{:S(2)}) collective-permute-start(bf16[32,3072]{1,0:T(8,128)(2,1)S(1)} %get-tuple-element.100), channel_id=1, source_target_pairs={{0,2},{1,5},{2,0},{3,7},{4,6},{5,1},{6,4},{7,3},{8,10},{9,13},{10,... | collective-permute-start | bytes 589832 | tf_op jit(solution)/shard_map/ppermute | solution.py:26
  70.2 5.9 %collective-permute-start.25 = (bf16[32,3072]{1,0:T(8,128)(2,1)S(1)}, bf16[32,3072]{1,0:T(8,128)(2,1)S(1)}, u32[]{:S(2)}, u32[]{:S(2)}) collective-permute-start(bf16[32,3072]{1,0:T(8,128)(2,1)S(1)} %get-tuple-element.101), channel_id=1, source_target_pairs={{0,4},{1,3},{2,6},{3,1},{4,0},{5,7},{6,2},{7,5},{8,12},{9,11},{10,... | collective-permute-start | bytes 589832 | tf_op jit(solution)/shard_map/ppermute | solution.py:26
  71.7 8.5 %collective-permute-start.21 = (bf16[8,4096]{1,0:T(8,128)(2,1)S(1)}, bf16[8,4096]{1,0:T(8,128)(2,1)S(1)}, u32[]{:S(2)}, u32[]{:S(2)}) collective-permute-start(bf16[8,4096]{1,0:T(8,128)(2,1)S(1)} %get-tuple-element.83), channel_id=1, source_target_pairs={{0,24},{1,25},{2,26},{3,27},{4,28},{5,29},{6,30},{7,31},{8,16},{9,... | collective-permute-start | bytes 196616 | tf_op jit(solution)/shard_map/ppermute | solution.py:26
  74.2 7.5 %collective-permute-start.22 = (bf16[8,4096]{1,0:T(8,128)(2,1)S(1)}, bf16[8,4096]{1,0:T(8,128)(2,1)S(1)}, u32[]{:S(2)}, u32[]{:S(2)}) collective-permute-start(bf16[8,4096]{1,0:T(8,128)(2,1)S(1)} %get-tuple-element.85), channel_id=1, source_target_pairs={{0,16},{1,17},{2,18},{3,19},{4,20},{5,21},{6,22},{7,23},{8,24},{9,... | collective-permute-start | bytes 196616 | tf_op jit(solution)/shard_map/ppermute | solution.py:26
  74.8 6.9 %collective-permute-start.23 = (bf16[8,4096]{1,0:T(8,128)(2,1)S(1)}, bf16[8,4096]{1,0:T(8,128)(2,1)S(1)}, u32[]{:S(2)}, u32[]{:S(2)}) collective-permute-start(bf16[8,4096]{1,0:T(8,128)(2,1)S(1)} %get-tuple-element.87), channel_id=1, source_target_pairs={{0,8},{1,9},{2,10},{3,11},{4,12},{5,13},{6,14},{7,15},{8,0},{9,1},... | collective-permute-start | bytes 196616 | tf_op jit(solution)/shard_map/ppermute | solution.py:26
  76.2 6.3 %collective-permute-start.26 = (bf16[8,3072]{1,0:T(8,128)(2,1)S(1)}, bf16[8,3072]{1,0:T(8,128)(2,1)S(1)}, u32[]{:S(2)}, u32[]{:S(2)}) collective-permute-start(bf16[8,3072]{1,0:T(8,128)(2,1)S(1)} %get-tuple-element.97), channel_id=1, source_target_pairs={{0,24},{1,25},{2,26},{3,27},{4,28},{5,29},{6,30},{7,31},{8,16},{9,... | collective-permute-start | bytes 147464 | tf_op jit(solution)/shard_map/ppermute | solution.py:26
  80.2 4.4 %collective-permute-start.28 = (bf16[8,3072]{1,0:T(8,128)(2,1)S(1)}, bf16[8,3072]{1,0:T(8,128)(2,1)S(1)}, u32[]{:S(2)}, u32[]{:S(2)}) collective-permute-start(bf16[8,3072]{1,0:T(8,128)(2,1)S(1)} %get-tuple-element.98), channel_id=1, source_target_pairs={{0,8},{1,9},{2,10},{3,11},{4,12},{5,13},{6,14},{7,15},{8,0},{9,1},... | collective-permute-start | bytes 147464 | tf_op jit(solution)/shard_map/ppermute | solution.py:26
  80.2 5.0 %collective-permute-start.27 = (bf16[8,3072]{1,0:T(8,128)(2,1)S(1)}, bf16[8,3072]{1,0:T(8,128)(2,1)S(1)}, u32[]{:S(2)}, u32[]{:S(2)}) collective-permute-start(bf16[8,3072]{1,0:T(8,128)(2,1)S(1)} %get-tuple-element.99), channel_id=1, source_target_pairs={{0,16},{1,17},{2,18},{3,19},{4,20},{5,21},{6,22},{7,23},{8,24},{9,... | collective-permute-start | bytes 147464 | tf_op jit(solution)/shard_map/ppermute | solution.py:26
